TPU v7x, 32 devices: a whole 2x2x4 slice. The times are simulated.
32 devices in a mesh: groups: 2 (over y), aux: 16 (over z, x, core).
Axes of the slice: x: 2, y: 2, z: 4, core: 2. Of those that a mesh axis runs over, the one named last changes fastest.
Arguments:
- block_values: bfloat16 [8192, 4096], P(('groups', 'aux')), parts along dimension 0
- block_pairs: int32 [8192, 2], P(('groups', 'aux')), parts along dimension 0, may hold values from 0 to 319, as said below
- live_counts: int32 [32], P(('groups', 'aux')), parts along dimension 0, may hold values from 64 to 256, as said below
- occupied: bfloat16 [40960, 256], P(('groups', 'aux')), parts along dimension 0, may hold values from -6 to 6
Outputs:
- exchange_window: float32 [40960, 128], P(('groups', 'aux')), parts along dimension 0
There are 2 independent parts, one for each index of `groups`. A program takes and returns all parts, laid end to end along the dimension named above; each array names one. Nothing has to cross between parts.
Inputs may be any that keep to these rules, and one draw needn't show every extreme that they name: `block_pairs`: row j holds the (row block, column block) of tile j; the tiles of auxiliary index p are rows p * 256 to (p + 1) * 256 - 1. The live tiles of index p are its first live_counts[p] slots; some index uses all 256 slots.
All inputs are finite; a program needn't handle non-finite values.
Results may differ from a plain program's by a relative error of at most 0.0037.
Values may be sent and summed in bfloat16 or wider, within the bound.
No kernel may reach another device: no remote copies, remote signals or barrier semaphores. Data moves between devices by JAX's collectives and lax.ppermute only.
A program may use at most 128 MiB of HBM per device.

v0:
```python
import math

import jax
import jax.numpy as jnp
from jax import lax
from jax.sharding import PartitionSpec as P

BLK = 64
WIN = 128


def local(block_values, block_pairs, live_counts, occupied):
    occ_whole = lax.all_gather(occupied, "aux", axis=0, tiled=True)
    orbital_total = occ_whole.shape[0]
    occ_width = occupied.shape[1]
    block_width = BLK
    window_width = WIN
    tile_total = block_values.shape[0]
    block_count = orbital_total // block_width
    occ_blocks = occ_whole.reshape(block_count, block_width, occ_width)
    tile_group = min(64, tile_total)
    live_total = live_counts[0]
    turn_total = (live_total + tile_group - 1) // tile_group
    block_ids = jnp.arange(block_count, dtype=jnp.int32)

    def add_group(turn_index, half_sum):
        first_slot = turn_index * tile_group
        tile_flat = lax.dynamic_slice_in_dim(block_values, first_slot, tile_group, 0)
        tile_set = tile_flat.reshape(tile_group, block_width, block_width)
        pair_set = lax.dynamic_slice_in_dim(block_pairs, first_slot, tile_group, 0)
        column_hot = (pair_set[:, 1][:, None] == block_ids[None, :]).astype(jnp.bfloat16)
        picked = jnp.einsum(
            "gc,cbk->gbk", column_hot, occ_blocks, preferred_element_type=jnp.float32
        ).astype(jnp.bfloat16)
        product = jnp.einsum("gab,gbk->gak", tile_set, picked, preferred_element_type=jnp.float32)
        slot_ids = first_slot + jnp.arange(tile_group, dtype=jnp.int32)
        live_mask = (slot_ids < live_total).astype(jnp.float32)
        row_hot = (pair_set[:, 0][:, None] == block_ids[None, :]).astype(jnp.float32) * live_mask[
            :, None
        ]
        added = jnp.einsum(
            "gr,gak->rak",
            row_hot,
            product,
            precision=lax.Precision.HIGHEST,
            preferred_element_type=jnp.float32,
        )
        return half_sum + added

    start_sum = jnp.zeros((block_count, block_width, occ_width), jnp.float32)
    half_sum = lax.fori_loop(0, turn_total, add_group, start_sum)
    half_rows = half_sum.reshape(orbital_total, occ_width).astype(jnp.bfloat16)
    window_own = half_rows[:window_width]
    owners = lax.axis_size("aux")
    factor = 1.0 / math.sqrt(owners * occ_width)
    block_sum = lax.psum_scatter(
        lax.dot_general(
            half_rows, window_own, (((1,), (1,)), ((), ())), preferred_element_type=jnp.float32
        ),
        "aux",
        scatter_dimension=0,
        tiled=True,
    )
    return block_sum * factor


def solution(mesh):
    placed = (
        P(("groups", "aux"), None),
        P(("groups", "aux"), None),
        P(("groups", "aux")),
        P(("groups", "aux"), None),
    )
    return jax.shard_map(
        local, mesh=mesh, in_specs=placed, out_specs=P(("groups", "aux"), None), check_vma=False
    )
```

profile of v0, /device:TPU:0, one launch (start us, length us, event | category | flops | bytes accessed | tf_op | source)
XLA Modules:
  0.0 418.5 jit_solution(11073263791412310371)
XLA Ops:
  6.5 0.0 all-gather.2.cloned.1.call-start
  6.5 0.7 all-gather.2.cloned.1.call-update
  7.3 0.0 reduce-scatter.2.cloned.1.call-start
  8.0 92.3 %all-gather.2.cloned.1.call-done = bf16[20480,256]{1,0:T(8,128)(2,1)} async-done(((bf16[1280,256]{1,0:T(8,128)(2,1)}), bf16[20480,256]{1,0:T(8,128)(2,1)}) %all-gather.2.cloned.1.call-update) | async-done | bytes 10485776 | tf_op jit(solution)/shard_map/all_gather | solution.py:13
  100.2 0.0 copy-start
  100.3 9.5 %broadcast_in_dim.2 = f32[320,64,256]{2,0,1:T(8,128)} broadcast(f32[]{:T(128)} %constant.28.clone.1), dimensions={} | broadcast | bytes 20971524 | tf_op jit(solution)/shard_map/broadcast_in_dim | solution.py:50
  109.8 0.0 copy-done
  109.8 78.6 %while.12 = (s32[]{:T(128)}, f32[320,64,256]{2,0,1:T(8,128)}, s32[]{:T(128)}, s32[256,2]{0,1:T(2,128)S(1)}, s32[]{:T(128)}, /*index=5*/bf16[256,4096]{1,0:T(8,12...) while((s32[]{:T(128)}, f32[320,64,256]{2,0,1:T(8,128)}, ...), condition=%wide.region_1.2_spmd.clone.clone, body=%wide.region_0.1_spmd.clone.clone.sunk | while | flops 4837142528 | bytes 67636392 | solution.py:51
  109.8 0.6 compare_convert_fusion.2
  110.4 0.1 constant_dynamic-slice_fusion.5
  110.5 1.1 constant_dynamic-slice_fusion.4
  111.6 1.1 reshape.22
  112.7 10.4 %fusion.31 = bf16[64,64,256]{2,0,1:T(8,128)(2,1)S(1)} fusion(bf16[320,64,256]{2,1,0:T(8,128)(2,1)} %get-tuple-element.182, s32[64]{0:T(128)S(1)} %get-tuple-element.152), kind=kOutput, calls=%fused_computation.1.clone.1 | convolution fusion | flops 671109120 | bytes 12583168 | tf_op jit(solution)/shard_map/while/body/gc,cbk->gbk/dot_general | solution.py:32
  123.1 1.7 fusion.32
  124.8 24.3 %convolution_add_fusion.2 = f32[320,64,256]{2,0,1:T(8,128)} fusion(f32[320,64,256]{2,0,1:T(8,128)} %get-tuple-element.166, f32[64,64,256]{2,1,0:T(8,128)S(1)} %fusion.32, f32[64]{0:T(128)S(1)} %compare_convert_fusion.2, s32[64]{0:T(128)S(1)} %get-tuple-element.153), kind=kOutput, calls=%fused_computation.3.clone.1 | convolution fusion | flops 4031815680 | bytes 46137856 | tf_op jit(solution)/shard_map/while/body/gr,gak->rak/dot_general | solution.py:41
  149.1 0.6 compare_convert_fusion.2
  149.8 0.1 constant_dynamic-slice_fusion.5
  149.8 1.1 constant_dynamic-slice_fusion.4
  150.9 1.1 reshape.22
  152.1 10.4 %fusion.31 = bf16[64,64,256]{2,0,1:T(8,128)(2,1)S(1)} fusion(bf16[320,64,256]{2,1,0:T(8,128)(2,1)} %get-tuple-element.182, s32[64]{0:T(128)S(1)} %get-tuple-element.152), kind=kOutput, calls=%fused_computation.1.clone.1 | convolution fusion | flops 671109120 | bytes 12583168 | tf_op jit(solution)/shard_map/while/body/gc,cbk->gbk/dot_general | solution.py:32
  162.4 1.7 fusion.32
  164.1 24.3 %convolution_add_fusion.2 = f32[320,64,256]{2,0,1:T(8,128)} fusion(f32[320,64,256]{2,0,1:T(8,128)} %get-tuple-element.166, f32[64,64,256]{2,1,0:T(8,128)S(1)} %fusion.32, f32[64]{0:T(128)S(1)} %compare_convert_fusion.2, s32[64]{0:T(128)S(1)} %get-tuple-element.153), kind=kOutput, calls=%fused_computation.3.clone.1 | convolution fusion | flops 4031815680 | bytes 46137856 | tf_op jit(solution)/shard_map/while/body/gr,gak->rak/dot_general | solution.py:41
  188.4 19.6 %copy.16 = bf16[320,64,256]{2,1,0:T(8,128)(2,1)S(1)} copy(f32[320,64,256]{2,0,1:T(8,128)} %get-tuple-element.51) | data formatting | bytes 31457280 | tf_op jit(solution)/shard_map/while | solution.py:51
  208.1 5.5 %fusion.15 = f32[20480,128]{1,0:T(8,128)} fusion(bf16[20480,256]{1,0:T(8,128)(2,1)S(1)} %bitcast.27, bf16[128,256]{1,0:T(8,128)(2,1)S(1)} %bitcast.28), kind=kOutput, calls=%fused_computation.24 | convolution fusion | flops 1342177280 | bytes 21037056 | tf_op jit(solution)/shard_map/dot_general | solution.py:57
  213.6 0.0 reduce-scatter.2.cloned.1.call-update
  213.6 196.0 %reduce-scatter.2.cloned.1.call-done = f32[1280,128]{1,0:T(8,128)} async-done(((f32[20480,128]{1,0:T(8,128)}), f32[1280,128]{1,0:T(8,128)}) %reduce-scatter.2.cloned.1.call-update) | async-done | bytes 655376 | tf_op jit(solution)/shard_map/reduce_scatter | solution.py:56
  409.6 2.0 broadcast_multiply_fusion
  (3 shorter events, 0.0 us)
Async XLA Ops:
  6.5 93.7 %all-gather.2.cloned.1.call-start = ((), (), s32[]{:S(2)}) async-start(), calls=%async_computation.1 | async-start | bytes 11141120 | tf_op jit(solution)/shard_map/all_gather | solution.py:13
  7.3 402.4 %reduce-scatter.2.cloned.1.call-start = ((), (), s32[]{:S(2)}) async-start(), calls=%async_computation.2 | async-start | bytes 11141120 | tf_op jit(solution)/shard_map/reduce_scatter | solution.py:56
  100.2 9.5 %copy-start = (s32[256,2]{0,1:T(2,128)S(1)}, s32[256,2]{0,1:T(2,128)}, u32[]{:S(2)}) copy-start(s32[256,2]{0,1:T(2,128)} %param.7) | copy-start | bytes 6148
Sparse Core Ops, SparseCore 0:
  9.6 90.5 all-gather.1
  213.8 195.8 reduce-scatter.1
where the time goes:
time: 419 us; the launch traced here: 418 us
  waiting for transfers between devices  289 us (69%)
  matrix products  78.2 us (19%)
  local copies, waits for them, and re-layouts  33.8 us (8%)
  between operations  14.1 us (3%)
    reduce_scatter x1, waiting for transfers between devices, local(): lax.psum_scatter(lax.dot_general(half_rows, window_own, (((1,), (1,)), ((...  196 us
    all_gather x1, waiting for transfers between devices, local(): occ_whole = lax.all_gather(occupied, 'aux', axis=0, tiled=True)  92.3 us
    dot_general x2, matrix products, add_group(): jnp.einsum('gr,gak->rak', row_hot, product, precision=lax.Precision.HIGHE...  48.6 us
    dot_general x2, matrix products, add_group(): jnp.einsum('gc,cbk->gbk', column_hot, occ_blocks, preferred_element_type=...  20.7 us
    while x1, local copies, waits for them, and re-layouts, local(): half_sum = lax.fori_loop(0, turn_total, add_group, start_sum)  19.6 us
    broadcast_in_dim x1, local copies, waits for them, and re-layouts, local(): start_sum = jnp.zeros((block_count, block_width, occ_width), jnp.float32)  9.53 us
  transfers between devices with their start and end apart: 2, of which 2 were waited for; matrix products, arithmetic and copies ran while one was open for 0% of the time, Pallas kernels for 0%

commit v1 on v0

v1 whole, which is shorter than its diff:
```python
import functools
import math

import jax
import jax.numpy as jnp
from jax import lax
from jax.experimental import pallas as pl
from jax.experimental.pallas import tpu as pltpu
from jax.sharding import PartitionSpec as P

BLK = 64
WIN = 128
LANES = 128
UNROLL = 8
VMEM_BYTES = 56 * 1024 * 1024


def gather_half(mine, theirs, occ, sem):
    rows = mine.shape[0]
    copies = [
        pltpu.make_async_copy(mine, occ.at[pl.ds(0, rows)], sem.at[0]),
        pltpu.make_async_copy(theirs, occ.at[pl.ds(rows, rows)], sem.at[1]),
    ]
    for copy in copies:
        copy.start()
    return copies


def clear(half):
    rows = half.shape[0]

    @pl.loop(0, rows // BLK)
    def _(index):
        half[pl.ds(pl.multiple_of(index * BLK, BLK), BLK), :] = jnp.zeros((BLK, LANES), jnp.float32)


def add_tiles(rows_ref, spots_ref, meta_ref, tiles, occ, half, piece):
    pieces = BLK // piece

    @pl.loop(0, meta_ref[0])
    def _(group):
        products = []
        for lane in range(UNROLL):
            slot = group * UNROLL + lane
            parts = [
                occ[pl.ds(pl.multiple_of(spots_ref[slot * pieces + cut], piece), piece), :]
                for cut in range(pieces)
            ]
            block = parts[0] if pieces == 1 else jnp.concatenate(parts, axis=0)
            products.append(jnp.dot(tiles[slot], block, preferred_element_type=jnp.float32))
        for lane in range(UNROLL):
            start = pl.multiple_of(rows_ref[group * UNROLL + lane], BLK)
            half[pl.ds(start, BLK), :] += products[lane]


def first_kernel(piece, rows_ref, spots_ref, meta_ref, mine, theirs, values, out, occ, tiles, half, sem):
    copies = gather_half(mine, theirs, occ, sem)
    load = pltpu.make_async_copy(values, tiles, sem.at[2])
    load.start()
    clear(half)
    load.wait()
    for copy in copies:
        copy.wait()
    add_tiles(rows_ref, spots_ref, meta_ref, tiles, occ, half, piece)
    total = out.shape[0]

    @pl.loop(0, total // 256)
    def _(index):
        span = pl.ds(pl.multiple_of(index * 256, 256), 256)
        out[span, :] = half[span, :].astype(jnp.bfloat16)


def last_kernel(
    piece, shard, rows_ref, spots_ref, meta_ref, mine, theirs, values, before, keep, send,
    occ, tiles, half, earlier, weights, keep_buf, send_buf, sem,
):
    copies = gather_half(mine, theirs, occ, sem)
    load = pltpu.make_async_copy(values, tiles, sem.at[2])
    load.start()
    fetch = pltpu.make_async_copy(before, earlier, sem.at[3])
    fetch.start()
    clear(half)
    load.wait()
    for copy in copies:
        copy.wait()
    add_tiles(rows_ref, spots_ref, meta_ref, tiles, occ, half, piece)
    fetch.wait()
    window = earlier[pl.ds(0, WIN), :].astype(jnp.float32)
    weights[pl.ds(0, LANES), :] = window.T.astype(jnp.bfloat16)
    weights[pl.ds(LANES, LANES), :] = half[pl.ds(0, WIN), :].T.astype(jnp.bfloat16)
    core = meta_ref[1]
    count = keep.shape[0]

    def rows_of(owner):
        span = pl.ds(pl.multiple_of(owner * shard, 32), shard)
        both = jnp.concatenate([earlier[span, :], half[span, :].astype(jnp.bfloat16)], axis=1)
        return jnp.dot(both, weights[...], preferred_element_type=jnp.float32)

    @pl.loop(0, count)
    def _(index):
        send_buf[index] = rows_of(2 * index + 1 - core).astype(jnp.bfloat16)
        pltpu.make_async_copy(send_buf.at[index], send.at[index], sem.at[0]).start()

    @pl.loop(0, count)
    def _(index):
        keep_buf[index] = rows_of(2 * index + core)
        pltpu.make_async_copy(keep_buf.at[index], keep.at[index], sem.at[1]).start()

    pltpu.make_async_copy(send_buf, send, sem.at[0]).wait()
    pltpu.make_async_copy(keep_buf, keep, sem.at[1]).wait()


def local(block_values, block_pairs, live_counts, occupied):
    owners = lax.axis_size("aux")
    core = lax.axis_index("aux") % 2
    shard, width = occupied.shape
    total = owners * shard
    slots = block_values.shape[0]
    piece = math.gcd(BLK, shard)
    same_core = [[2 * i + k for i in range(owners // 2)] for k in range(2)]
    swap = [(i, i ^ 1) for i in range(owners)]

    tiles = block_values.reshape(slots, BLK, BLK)
    live = live_counts[0]
    slot_ids = jnp.arange(slots, dtype=jnp.int32)
    row_starts = jnp.where(slot_ids < live, block_pairs[:, 0] * BLK, total)
    first = block_pairs[:, 1][:, None] * BLK + jnp.arange(BLK // piece, dtype=jnp.int32) * piece
    owner = first // shard
    other = (owner % 2) ^ core
    spots = (other * (total // 2) + owner // 2 * shard + first % shard).reshape(-1)
    meta = jnp.stack([(live + UNROLL - 1) // UNROLL, core]).astype(jnp.int32)

    smem = pl.BlockSpec(memory_space=pltpu.SMEM)
    hbm = pl.BlockSpec(memory_space=pl.ANY)
    vmem = pl.BlockSpec(memory_space=pltpu.VMEM)
    work = [
        pltpu.VMEM((total, LANES), jnp.bfloat16),
        pltpu.VMEM((slots, BLK, BLK), jnp.bfloat16),
        pltpu.VMEM((total + BLK, LANES), jnp.float32),
    ]
    params = pltpu.CompilerParams(vmem_limit_bytes=VMEM_BYTES)

    held = []
    for cut in range(width // LANES):
        mine = lax.all_gather(
            occupied[:, cut * LANES : (cut + 1) * LANES],
            "aux", axis_index_groups=same_core, axis=0, tiled=True,
        )
        held.append((mine, lax.ppermute(mine, "aux", swap)))

    before = pl.pallas_call(
        functools.partial(first_kernel, piece),
        out_shape=jax.ShapeDtypeStruct((total, LANES), jnp.bfloat16),
        in_specs=[smem] * 3 + [hbm] * 3,
        out_specs=vmem,
        scratch_shapes=work + [pltpu.SemaphoreType.DMA((3,))],
        compiler_params=params,
        cost_estimate=pl.CostEstimate(flops=2 * slots * BLK * BLK * LANES, bytes_accessed=15 << 20, transcendentals=0),
    )(row_starts, spots, meta, *held[0], tiles)

    keep, send = pl.pallas_call(
        functools.partial(last_kernel, piece, shard),
        out_shape=(
            jax.ShapeDtypeStruct((owners // 2, shard, WIN), jnp.float32),
            jax.ShapeDtypeStruct((owners // 2, shard, WIN), jnp.bfloat16),
        ),
        in_specs=[smem] * 3 + [hbm] * 4,
        out_specs=(hbm, hbm),
        scratch_shapes=work
        + [
            pltpu.VMEM((total, LANES), jnp.bfloat16),
            pltpu.VMEM((2 * LANES, WIN), jnp.bfloat16),
            pltpu.VMEM((owners // 2, shard, WIN), jnp.float32),
            pltpu.VMEM((owners // 2, shard, WIN), jnp.bfloat16),
            pltpu.SemaphoreType.DMA((4,)),
        ],
        compiler_params=params,
        cost_estimate=pl.CostEstimate(flops=2 * total * width * WIN, bytes_accessed=25 << 20, transcendentals=0),
    )(row_starts, spots, meta, *held[1], tiles, before)

    arrived = lax.ppermute(send, "aux", swap)
    pair_sum = (keep + arrived.astype(jnp.float32)).astype(jnp.bfloat16)
    block_sum = lax.psum_scatter(
        pair_sum.reshape(total // 2, WIN), "aux", axis_index_groups=same_core, scatter_dimension=0, tiled=True
    )
    factor = 1.0 / math.sqrt(owners * width)
    return block_sum.astype(jnp.float32) * factor


def solution(mesh):
    placed = (
        P(("groups", "aux"), None),
        P(("groups", "aux"), None),
        P(("groups", "aux")),
        P(("groups", "aux"), None),
    )
    return jax.shard_map(
        local, mesh=mesh, in_specs=placed, out_specs=P(("groups", "aux"), None), check_vma=False
    )
```

time: 419 us -> 253 us (0.60)
  waiting for transfers between devices: 289 us -> 195 us
  matrix products: 78.2 us -> 0 us
  Pallas kernels: 0 us -> 22.1 us
  local copies, waits for them, and re-layouts: 33.8 us -> 11.9 us
  other arithmetic: 3.26 us -> 8.27 us
    reduce_scatter x1, waiting for transfers between devices: 196 us -> 76.8 us  [local(): lax.psum_scatter(pair_sum.reshape(total // 2, WIN), 'aux', axis_index_gro...]
    dot_general x7 -> x0, matrix products: 78.2 us -> none  [the longest x2 48.6 us: add_group(): jnp.einsum('gr,gak->rak', row_hot, product, precision=lax.Precision.HIGHE...]
    pallas_call x0 -> x2, Pallas kernels: none -> 22.1 us  [the longest x1 12.6 us: local(): pl.pallas_call(functools.partial(last_kernel, piece, shard), out_shape=(j...]
    all_gather x1 -> x2, waiting for transfers between devices: 92.3 us -> 113 us  [local(): lax.all_gather(occupied[:, cut * LANES:(cut + 1) * LANES], 'aux', axis_in...]
    while x1 -> x0, local copies, waits for them, and re-layouts: 19.6 us -> none  [local(): half_sum = lax.fori_loop(0, turn_total, add_group, start_sum)]
    broadcast_in_dim x1 -> x0, local copies, waits for them, and re-layouts: 9.53 us -> none  [local(): start_sum = jnp.zeros((block_count, block_width, occ_width), jnp.float32)]
    ppermute x0 -> x3, waiting for transfers between devices: none -> 4.75 us  [the longest x1 4.75 us: local(): arrived = lax.ppermute(send, 'aux', swap)]
    reshape x2 -> x1, local copies, waits for them, and re-layouts: 2.25 us -> 6.66 us  [local(): tiles = block_values.reshape(slots, BLK, BLK)]
  transfers between devices with their start and end apart: 2 -> 6, of which waited for: 2 -> 4; matrix products, arithmetic and copies ran while one was open for 0% -> 5% of each run, Pallas kernels for 0% -> 4%
where the time goes in v1:
time: 253 us
  waiting for transfers between devices  195 us (77%)
  Pallas kernels  22.1 us (9%)
  between operations  13.8 us (5%)
  local copies, waits for them, and re-layouts  11.9 us (5%)
  other arithmetic  8.27 us (3%)
    all_gather x2, waiting for transfers between devices, local(): lax.all_gather(occupied[:, cut * LANES:(cut + 1) * LANES], 'aux', axis_in...  113 us
    reduce_scatter x1, waiting for transfers between devices, local(): lax.psum_scatter(pair_sum.reshape(total // 2, WIN), 'aux', axis_index_gro...  76.8 us
    pallas_call x1, Pallas kernels, local(): pl.pallas_call(functools.partial(last_kernel, piece, shard), out_shape=(j...  12.6 us
    pallas_call x1, Pallas kernels, local(): pl.pallas_call(functools.partial(first_kernel, piece), out_shape=jax.Shap...  9.52 us
    reshape x1, local copies, waits for them, and re-layouts, local(): tiles = block_values.reshape(slots, BLK, BLK)  6.66 us
  transfers between devices with their start and end apart: 6, of which 4 were waited for; matrix products, arithmetic and copies ran while one was open for 5% of the time, Pallas kernels for 4%

profile of v1, /device:TPU:0, one launch (start us, length us, event | category | flops | bytes accessed | tf_op | source)
XLA Modules:
  0.0 252.5 jit_solution(9816281781573009158)
XLA Ops:
  6.5 0.0 all-gather.5.cloned.1.call-start
  6.5 2.0 fusion.4
  8.5 0.0 all-gather.5.cloned.1.call-update
  8.5 0.0 all-gather.3.cloned.1.call-start
  8.6 0.7 all-gather.3.cloned.1.call-update
  9.3 0.0 reduce-scatter.2.cloned.1.call-start
  9.3 57.6 %all-gather.5.cloned.1.call-done.mine = bf16[10240,128]{1,0:T(8,128)(2,1)} async-done(((bf16[1280,128]{1,0:T(8,128)(2,1)}), bf16[10240,128]{1,0:T(8,128)(2,1)}) %all-gather.5.cloned.1.call-update) | async-done | bytes 2621456 | tf_op jit(solution)/shard_map/all_gather | solution.py:145
  66.9 0.0 collective-permute-start.1
  66.9 55.4 %all-gather.3.cloned.1.call-done.mine = bf16[10240,128]{1,0:T(8,128)(2,1)} async-done(((bf16[1280,128]{1,0:T(8,128)(2,1)}), bf16[10240,128]{1,0:T(8,128)(2,1)}) %all-gather.3.cloned.1.call-update) | async-done | bytes 2621456 | tf_op jit(solution)/shard_map/all_gather | solution.py:145
  122.4 0.0 collective-permute-start
  123.0 3.3 %copy.5 = bf16[256,4096]{0,1:T(8,128)(2,1)S(1)} copy(bf16[256,4096]{1,0:T(8,128)(2,1)} %param.4) | data formatting | bytes 4194304 | tf_op args[0]
  126.3 0.0 copy-start
  126.3 6.7 %copy.7.values = bf16[256,64,64]{2,1,0:T(8,128)(2,1)} copy(bf16[256,64,64]{0,2,1:T(8,128)(2,1)S(1)} %bitcast.10) | data formatting | bytes 4194304 | tf_op jit(solution)/shard_map/reshape | solution.py:123
  133.0 0.6 pad_add_fusion.meta_ref
  133.6 0.0 copy-done
  133.6 0.6 fusion
  134.2 0.6 compare_select_fusion.3.rows_ref
  134.8 0.0 collective-permute-done.1.theirs
  134.8 9.5 %shard_map.46.before = bf16[20480,128]{1,0:T(8,128)(2,1)} custom-call(s32[256]{0:T(256)} %compare_select_fusion.3.rows_ref, s32[256]{0:T(256)} %bitcast.11, s32[2]{0:T(128)} %pad_add_fusion.meta_ref, bf16[10240,128]{1,0:T(8,128)(2,1)} %all-gather.5.cloned.1.call-done.mine, bf16[10240,128]{1,0:T(8,128)(2,1)} %collective-permute-done.1.theirs, ...), custom_call_target="tpu_custom_call" | custom-call | flops 268435456 | bytes 15728640 | tf_op jit(solution)/shard_map/pallas_call | solution.py:151
  144.3 0.0 collective-permute-done.theirs
  144.3 12.6 %shard_map.47 = (f32[8,1280,128]{2,1,0:T(8,128)}, bf16[8,1280,128]{2,1,0:T(8,128)(2,1)}) custom-call(s32[256]{0:T(256)} %compare_select_fusion.3.rows_ref, s32[256]{0:T(256)} %bitcast.12, s32[2]{0:T(128)} %pad_add_fusion.meta_ref, bf16[10240,128]{1,0:T(8,128)(2,1)} %all-gather.3.cloned.1.call-done.mine, bf16[10240,128]{1,0:T(8,128)(2,1)} %collective-permute-done.theirs, ...), custom_call_target="tpu_custom_call" | custom-call | flops 1342177280 | bytes 26214400 | tf_op jit(solution)/shard_map/pallas_call | solution.py:161
  156.9 1.0 collective-permute-start.2
  157.9 4.7 %collective-permute-done.2 = bf16[8,1280,128]{2,1,0:T(8,128)(2,1)S(1)} collective-permute-done((bf16[8,1280,128]{2,1,0:T(8,128)(2,1)}, bf16[8,1280,128]{2,1,0:T(8,128)(2,1)S(1)}, u32[]{:S(2)}, u32[]{:S(2)}) %collective-permute-start.2) | collective-permute-done | bytes 2621472 | tf_op jit(solution)/shard_map/ppermute | solution.py:181
  162.6 4.6 %add_convert_fusion = bf16[8,1280,128]{2,1,0:T(8,128)(2,1)} fusion(f32[8,1280,128]{2,1,0:T(8,128)} %get-tuple-element.7, bf16[8,1280,128]{2,1,0:T(8,128)(2,1)S(1)} %collective-permute-done.2), kind=kLoop, calls=%fused_computation | loop fusion | flops 3932160 | bytes 10485760 | tf_op jit(solution)/shard_map/convert_element_type | solution.py:182
  167.3 0.0 reduce-scatter.2.cloned.1.call-update
  167.3 76.8 %reduce-scatter.2.cloned.1.call-done = bf16[1280,128]{1,0:T(8,128)(2,1)} async-done(((bf16[10240,128]{1,0:T(8,128)(2,1)}), bf16[1280,128]{1,0:T(8,128)(2,1)}) %reduce-scatter.2.cloned.1.call-update) | async-done | bytes 327696 | tf_op jit(solution)/shard_map/reduce_scatter | solution.py:183
  244.1 1.9 convert_multiply_fusion
Async XLA Ops:
  6.5 60.4 %all-gather.5.cloned.1.call-start = ((), (), s32[]{:S(2)}) async-start(), calls=%async_computation.2 | async-start | bytes 2949120 | tf_op jit(solution)/shard_map/all_gather | solution.py:145
  8.5 113.8 %all-gather.3.cloned.1.call-start = ((), (), s32[]{:S(2)}) async-start(), calls=%async_computation.1 | async-start | bytes 2949120 | tf_op jit(solution)/shard_map/all_gather | solution.py:145
  9.3 234.8 %reduce-scatter.2.cloned.1.call-start = ((), (), s32[]{:S(2)}) async-start(), calls=%async_computation.3 | async-start | bytes 2949120 | tf_op jit(solution)/shard_map/reduce_scatter | solution.py:183
  66.9 67.9 %collective-permute-start.1 = (bf16[10240,128]{1,0:T(8,128)(2,1)}, bf16[10240,128]{1,0:T(8,128)(2,1)}, u32[]{:S(2)}, u32[]{:S(2)}) collective-permute-start(bf16[10240,128]{1,0:T(8,128)(2,1)} %all-gather.5.cloned.1.call-done.mine), channel_id=1, source_target_pairs={{0,1},{1,0},{2,3},{3,2},{4,5},{5,4},{6,7},{7,6},{8,9},{9,8},{10,11... | collective-permute-start | bytes 7864328 | tf_op jit(solution)/shard_map/ppermute | solution.py:149
  122.4 21.9 %collective-permute-start = (bf16[10240,128]{1,0:T(8,128)(2,1)}, bf16[10240,128]{1,0:T(8,128)(2,1)}, u32[]{:S(2)}, u32[]{:S(2)}) collective-permute-start(bf16[10240,128]{1,0:T(8,128)(2,1)} %all-gather.3.cloned.1.call-done.mine), channel_id=1, source_target_pairs={{0,1},{1,0},{2,3},{3,2},{4,5},{5,4},{6,7},{7,6},{8,9},{9,8},{10,11... | collective-permute-start | bytes 7864328 | tf_op jit(solution)/shard_map/ppermute | solution.py:149
  126.3 7.3 %copy-start = (s32[256,2]{0,1:T(2,128)S(1)}, s32[256,2]{0,1:T(2,128)}, u32[]{:S(2)}) copy-start(s32[256,2]{0,1:T(2,128)} %param.5) | copy-start | bytes 6148
  156.9 5.7 %collective-permute-start.2 = (bf16[8,1280,128]{2,1,0:T(8,128)(2,1)}, bf16[8,1280,128]{2,1,0:T(8,128)(2,1)S(1)}, u32[]{:S(2)}, u32[]{:S(2)}) collective-permute-start(bf16[8,1280,128]{2,1,0:T(8,128)(2,1)} %get-tuple-element.8), channel_id=1, source_target_pairs={{0,1},{1,0},{2,3},{3,2},{4,5},{5,4},{6,7},{7,6},{8,9},{9,8},{10,11... | collective-permute-start | bytes 7864328 | tf_op jit(solution)/shard_map/ppermute | solution.py:181
Sparse Core Ops, SparseCore 0:
  9.5 57.3 all-gather.4
  69.1 53.2 all-gather.2
  167.4 76.6 reduce-scatter.1

commit v2 on v0

v2 whole, which is shorter than its diff:
```python
import functools
import math

import jax
import jax.numpy as jnp
from jax import lax
from jax.experimental import pallas as pl
from jax.experimental.pallas import tpu as pltpu
from jax.sharding import PartitionSpec as P

BLK = 64
WIN = 128
LANES = 128
UNROLL = 8
VMEM_BYTES = 60 * 1024 * 1024
LINE = 4


def place(z, x, core):
    return (z * 2 + x) * 2 + core


def pairs_of(step, levels=range(LINE)):
    found = []
    for z in levels:
        for x in range(2):
            for core in range(2):
                found.append((place(z, x, core), place(*step(z, x), core)))
    return found


def spread(own):
    ends, middles = (0, LINE - 1), (1, 2)
    near = pairs_of(lambda z, x: (z ^ 1, x))
    inner = pairs_of(lambda z, x: (3 - z, x), middles)
    outward = pairs_of(lambda z, x: (0 if z == 1 else 3, x), middles)
    across = pairs_of(lambda z, x: (z, 1 - x))
    across_ends = pairs_of(lambda z, x: (z, 1 - x), ends)
    across_middles = pairs_of(lambda z, x: (z, 1 - x), middles)

    def move(array, pairs):
        return lax.ppermute(array, "aux", pairs)

    x_own = move(own, across)
    z1 = move(own, near)
    z3_mid = move(own, inner)
    x1 = move(z1, across)
    z2_mid = move(z1, inner)
    z2_end = move(z3_mid, outward)
    x3_mid = move(z3_mid, across_middles)
    x2_end = move(z2_end, across_ends)
    z3_end = move(z2_mid, outward)
    x2_mid = move(z2_mid, across_middles)
    x3_end = move(z3_end, across_ends)
    return [own, z1, (z2_end, z2_mid), (z3_end, z3_mid), x_own, x1, (x2_end, x2_mid), (x3_end, x3_mid)]


def start_when(condition, source, target, sem):
    @pl.when(condition)
    def _():
        pltpu.make_async_copy(source, target, sem).start()


def work_kernel(
    piece, shard, kinds, rows_ref, spots_ref, meta_ref, *refs,
):
    sources = refs[: sum(kinds)]
    values, other_values, keep, send, occ, tiles, half, weights, keep_buf, send_buf, sem = refs[sum(kinds):]
    core, at_end = meta_ref[2], meta_ref[3]
    slot_rows = occ.shape[0] // len(kinds)
    first = 0
    for index, kind in enumerate(kinds):
        target = occ.at[pl.ds(index * slot_rows, slot_rows)]
        if kind == 1:
            pltpu.make_async_copy(sources[first], target, sem.at[0]).start()
        else:
            start_when(at_end == 1, sources[first], target, sem.at[0])
            start_when(at_end == 0, sources[first + 1], target, sem.at[0])
        first += kind
    loads = [
        pltpu.make_async_copy(values, tiles.at[0], sem.at[1]),
        pltpu.make_async_copy(other_values, tiles.at[1], sem.at[2]),
    ]
    for load in loads:
        load.start()

    @pl.loop(0, half.shape[1] // BLK)
    def _(index):
        span = pl.ds(pl.multiple_of(index * BLK, BLK), BLK)
        for side in range(2):
            half[side, span, :] = jnp.zeros((BLK, LANES), jnp.float32)

    pltpu.make_async_copy(occ, occ, sem.at[0]).wait()
    slots = tiles.shape[1]
    pieces = BLK // piece

    for side in range(2):
        loads[side].wait()

        @pl.loop(0, meta_ref[side])
        def _(group):
            products = []
            for lane in range(UNROLL):
                slot = group * UNROLL + lane
                table = side * slots + slot
                parts = [
                    occ[pl.ds(pl.multiple_of(spots_ref[table * pieces + cut], piece), piece), :]
                    for cut in range(pieces)
                ]
                block = parts[0] if pieces == 1 else jnp.concatenate(parts, axis=0)
                products.append(jnp.dot(tiles[side, slot], block, preferred_element_type=jnp.float32))
            for lane in range(UNROLL):
                start = pl.multiple_of(rows_ref[side * slots + group * UNROLL + lane], BLK)
                half[side, pl.ds(start, BLK), :] += products[lane]

        weights[pl.ds(side * LANES, LANES), :] = half[side, pl.ds(0, WIN), :].T.astype(jnp.bfloat16)

    count = keep.shape[0]

    def rows_of(owner):
        span = pl.ds(pl.multiple_of(owner * shard, 32), shard)
        both = jnp.concatenate([half[side, span, :].astype(jnp.bfloat16) for side in range(2)], axis=1)
        return jnp.dot(both, weights[...], preferred_element_type=jnp.float32)

    @pl.loop(0, count)
    def _(index):
        send_buf[index] = rows_of(2 * index + 1 - core).astype(jnp.bfloat16)
        pltpu.make_async_copy(send_buf.at[index], send.at[index], sem.at[3]).start()

    @pl.loop(0, count)
    def _(index):
        keep_buf[index] = rows_of(2 * index + core)
        pltpu.make_async_copy(keep_buf.at[index], keep.at[index], sem.at[4]).start()

    pltpu.make_async_copy(send_buf, send, sem.at[3]).wait()
    pltpu.make_async_copy(keep_buf, keep, sem.at[4]).wait()


def local(block_values, block_pairs, live_counts, occupied):
    owners = lax.axis_size("aux")
    me = lax.axis_index("aux")
    core, chip = me % 2, me // 2
    shard, width = occupied.shape
    total = owners * shard
    slots = block_values.shape[0]
    piece = math.gcd(BLK, shard)
    same_core = [[2 * i + k for i in range(owners // 2)] for k in range(2)]
    swap = [(i, i ^ 1) for i in range(owners)]

    mine = lax.dynamic_slice_in_dim(occupied, core * LANES, LANES, 1)
    given = lax.dynamic_slice_in_dim(occupied, (1 - core) * LANES, LANES, 1)
    own = jnp.concatenate([mine, lax.ppermute(given, "aux", swap)], axis=0)

    if owners == 4 * LINE:
        held = spread(own)
    else:
        held = [lax.all_gather(own, "aux", axis_index_groups=same_core, axis=0, tiled=True)]
    kinds = [len(entry) if isinstance(entry, tuple) else 1 for entry in held]
    sources = [array for entry in held for array in (entry if isinstance(entry, tuple) else (entry,))]

    live = live_counts[0]
    slot_ids = jnp.arange(slots, dtype=jnp.int32)
    row_starts = jnp.where(slot_ids < live, block_pairs[:, 0] * BLK, total)
    groups = jnp.full((slots,), (live + UNROLL - 1) // UNROLL, jnp.int32)
    table = jnp.stack([row_starts, block_pairs[:, 1], groups])
    other_table = lax.ppermute(table, "aux", swap)
    other_values = lax.ppermute(block_values, "aux", swap)
    tiles = block_values.reshape(slots, BLK, BLK)
    other_tiles = other_values.reshape(slots, BLK, BLK)

    rows = jnp.concatenate([table[0], other_table[0]])
    columns = jnp.concatenate([table[1], other_table[1]])
    first = columns[:, None] * BLK + jnp.arange(BLK // piece, dtype=jnp.int32) * piece
    owner = first // shard
    owner_chip = owner // 2
    slot_of = owner_chip
    if len(held) > 1:
        slot_of = ((owner_chip // 2) ^ (chip // 2)) + LINE * ((owner_chip % 2) ^ (chip % 2))
    spots = (slot_of * (2 * shard) + ((owner % 2) ^ core) * shard + first % shard).reshape(-1)
    level = chip // 2
    at_end = ((level == 0) | (level == LINE - 1)).astype(jnp.int32)
    meta = jnp.stack([table[2, 0], other_table[2, 0], core, at_end]).astype(jnp.int32)

    smem = pl.BlockSpec(memory_space=pltpu.SMEM)
    hbm = pl.BlockSpec(memory_space=pl.ANY)
    keep, send = pl.pallas_call(
        functools.partial(work_kernel, piece, shard, kinds),
        out_shape=(
            jax.ShapeDtypeStruct((owners // 2, shard, WIN), jnp.float32),
            jax.ShapeDtypeStruct((owners // 2, shard, WIN), jnp.bfloat16),
        ),
        in_specs=[smem] * 3 + [hbm] * (len(sources) + 2),
        out_specs=(hbm, hbm),
        scratch_shapes=[
            pltpu.VMEM((total, LANES), jnp.bfloat16),
            pltpu.VMEM((2, slots, BLK, BLK), jnp.bfloat16),
            pltpu.VMEM((2, total + BLK, LANES), jnp.float32),
            pltpu.VMEM((2 * LANES, WIN), jnp.bfloat16),
            pltpu.VMEM((owners // 2, shard, WIN), jnp.float32),
            pltpu.VMEM((owners // 2, shard, WIN), jnp.bfloat16),
            pltpu.SemaphoreType.DMA((5,)),
        ],
        compiler_params=pltpu.CompilerParams(vmem_limit_bytes=VMEM_BYTES),
        cost_estimate=pl.CostEstimate(
            flops=2 * total * width * (WIN + BLK), bytes_accessed=25 << 20, transcendentals=0
        ),
    )(rows, spots, meta, *sources, tiles, other_tiles)

    arrived = lax.ppermute(send, "aux", swap)
    pair_sum = (keep + arrived.astype(jnp.float32)).astype(jnp.bfloat16)
    block_sum = lax.psum_scatter(
        pair_sum.reshape(total // 2, WIN), "aux", axis_index_groups=same_core, scatter_dimension=0, tiled=True
    )
    factor = 1.0 / math.sqrt(owners * width)
    return block_sum.astype(jnp.float32) * factor


def solution(mesh):
    placed = (
        P(("groups", "aux"), None),
        P(("groups", "aux"), None),
        P(("groups", "aux")),
        P(("groups", "aux"), None),
    )
    return jax.shard_map(
        local, mesh=mesh, in_specs=placed, out_specs=P(("groups", "aux"), None), check_vma=False
    )
```

time: 419 us -> 215 us (0.51)
  waiting for transfers between devices: 289 us -> 132 us
  matrix products: 78.2 us -> 0 us
  Pallas kernels: 0 us -> 20 us
  starting transfers between devices: 0.04 us -> 19.7 us
  local copies, waits for them, and re-layouts: 33.8 us -> 20 us
  other arithmetic: 3.26 us -> 8.52 us
    reduce_scatter x1, waiting for transfers between devices: 196 us -> 83.9 us  [local(): lax.psum_scatter(pair_sum.reshape(total // 2, WIN), 'aux', axis_index_gro...]
    all_gather x1 -> x0, waiting for transfers between devices: 92.3 us -> none  [local(): occ_whole = lax.all_gather(occupied, 'aux', axis=0, tiled=True)]
    dot_general x7 -> x0, matrix products: 78.2 us -> none  [the longest x2 48.6 us: add_group(): jnp.einsum('gr,gak->rak', row_hot, product, precision=lax.Precision.HIGHE...]
    ppermute x0 -> x15, waiting for transfers between devices: none -> 48.3 us  [the longest x11 43.2 us: move(): return lax.ppermute(array, 'aux', pairs)]
    pallas_call x0 -> x1, Pallas kernels: none -> 20 us  [local(): pl.pallas_call(functools.partial(work_kernel, piece, shard, kinds), out_s...]
    ppermute x0 -> x15, starting transfers between devices: none -> 19.7 us  [the longest x11 19 us: move(): return lax.ppermute(array, 'aux', pairs)]
    while x1 -> x0, local copies, waits for them, and re-layouts: 19.6 us -> none  [local(): half_sum = lax.fori_loop(0, turn_total, add_group, start_sum)]
    reshape x2, local copies, waits for them, and re-layouts: 2.25 us -> 14.2 us  [the longest x1 7.46 us: local(): other_tiles = other_values.reshape(slots, BLK, BLK)]
  transfers between devices with their start and end apart: 2 -> 16, of which waited for: 2 -> 8; matrix products, arithmetic and copies ran while one was open for 0% -> 9% of each run, Pallas kernels for 0% -> 0%
where the time goes in v2:
time: 215 us
  waiting for transfers between devices  132 us (61%)
  local copies, waits for them, and re-layouts  20 us (9%)
  Pallas kernels  20 us (9%)
  starting transfers between devices  19.7 us (9%)
  between operations  14.3 us (7%)
  other arithmetic  8.52 us (4%)
    reduce_scatter x1, waiting for transfers between devices, local(): lax.psum_scatter(pair_sum.reshape(total // 2, WIN), 'aux', axis_index_gro...  83.9 us
    ppermute x11, waiting for transfers between devices, move(): return lax.ppermute(array, 'aux', pairs)  43.2 us
    pallas_call x1, Pallas kernels, local(): pl.pallas_call(functools.partial(work_kernel, piece, shard, kinds), out_s...  20 us
    ppermute x11, starting transfers between devices, move(): return lax.ppermute(array, 'aux', pairs)  19 us
    reshape x1, local copies, waits for them, and re-layouts, local(): other_tiles = other_values.reshape(slots, BLK, BLK)  7.46 us
    reshape x1, local copies, waits for them, and re-layouts, local(): tiles = block_values.reshape(slots, BLK, BLK)  6.71 us
    ppermute x1, waiting for transfers between devices, local(): arrived = lax.ppermute(send, 'aux', swap)  5.11 us
    convert_element_type x1, other arithmetic, local(): pair_sum = (keep + arrived.astype(jnp.float32)).astype(jnp.bfloat16)  4.62 us
  transfers between devices with their start and end apart: 16, of which 8 were waited for; matrix products, arithmetic and copies ran while one was open for 9% of the time, Pallas kernels for 0%

profile of v2, /device:TPU:0, one launch (start us, length us, event | category | flops | bytes accessed | tf_op | source)
XLA Modules:
  0.0 214.9 jit_solution(15142040799463937406)
XLA Ops:
  6.5 0.0 reduce-scatter.2.cloned.1.call-start
  6.5 1.1 constant_dynamic-slice_fusion.1
  7.7 0.0 copy-start.5
  7.7 0.5 collective-permute-start.1
  8.2 3.3 %copy.5 = bf16[256,4096]{0,1:T(8,128)(2,1)S(1)} copy(bf16[256,4096]{1,0:T(8,128)(2,1)} %param.4) | data formatting | bytes 4194304 | tf_op args[0]
  11.5 0.1 collective-permute-start.13
  11.6 0.0 collective-permute-done.1
  11.6 0.0 copy-start
  11.6 3.1 %collective-permute-start.2 = (bf16[2560,128]{1,0:T(8,128)(2,1)S(1)}, bf16[2560,128]{1,0:T(8,128)(2,1)S(1)}, u32[]{:S(2)}, u32[]{:S(2)}) collective-permute-start(bf16[2560,128]{1,0:T(8,128)(2,1)S(1)} %pad_maximum_fusion.refs_0_), channel_id=1, source_target_pairs={{0,4},{1,5},{2,6},{3,7},{4,0},{5,1},{6,2},{7,3},{8,12},{9,13},{10,... | collective-permute-start | bytes 1966088 | tf_op jit(solution)/shard_map/ppermute | solution.py:42
  14.7 1.5 collective-permute-start.3
  16.2 13.4 %collective-permute-done.2.refs_1_ = bf16[2560,128]{1,0:T(8,128)(2,1)S(1)} collective-permute-done((bf16[2560,128]{1,0:T(8,128)(2,1)S(1)}, bf16[2560,128]{1,0:T(8,128)(2,1)S(1)}, u32[]{:S(2)}, u32[]{:S(2)}) %collective-permute-start.2) | collective-permute-done | bytes 655392 | tf_op jit(solution)/shard_map/ppermute | solution.py:42
  29.7 0.0 copy-start.1
  29.7 1.5 collective-permute-start.5
  31.9 0.1 pad.12.clone
  31.9 1.7 collective-permute-start.7
  33.6 0.0 collective-permute-done.3.refs_5_
  33.6 1.3 collective-permute-start.4
  34.9 0.0 collective-permute-done.5.refs_3_
  34.9 1.3 collective-permute-start.6
  36.2 0.0 copy-done.5
  36.2 0.1 add_add_fusion
  36.3 0.0 collective-permute-start
  36.4 6.7 %copy.7.refs_12_ = bf16[256,64,64]{2,1,0:T(8,128)(2,1)} copy(bf16[256,64,64]{0,2,1:T(8,128)(2,1)S(1)} %bitcast.21) | data formatting | bytes 4194304 | tf_op jit(solution)/shard_map/reshape | solution.py:168
  43.1 0.0 copy-done
  43.1 0.0 collective-permute-done
  43.1 1.5 collective-permute-start.12
  44.6 3.6 %collective-permute-done.7.refs_6_ = bf16[2560,128]{1,0:T(8,128)(2,1)} collective-permute-done((bf16[2560,128]{1,0:T(8,128)(2,1)S(1)}, bf16[2560,128]{1,0:T(8,128)(2,1)}, u32[]{:S(2)}, u32[]{:S(2)}) %collective-permute-start.7) | collective-permute-done | bytes 655392 | tf_op jit(solution)/shard_map/ppermute | solution.py:42
  48.2 0.0 copy-done.1
  48.2 1.3 collective-permute-start.8
  49.5 4.8 %collective-permute-done.4.refs_2_ = bf16[2560,128]{1,0:T(8,128)(2,1)} collective-permute-done((bf16[2560,128]{1,0:T(8,128)(2,1)}, bf16[2560,128]{1,0:T(8,128)(2,1)}, u32[]{:S(2)}, u32[]{:S(2)}) %collective-permute-start.4) | collective-permute-done | bytes 655392 | tf_op jit(solution)/shard_map/ppermute | solution.py:42
  54.4 1.5 collective-permute-start.10
  55.9 0.0 collective-permute-done.13
  55.9 1.9 collective-permute-start.9
  57.8 8.6 %collective-permute-done.6.refs_4_ = bf16[2560,128]{1,0:T(8,128)(2,1)} collective-permute-done((bf16[2560,128]{1,0:T(8,128)(2,1)}, bf16[2560,128]{1,0:T(8,128)(2,1)}, u32[]{:S(2)}, u32[]{:S(2)}) %collective-permute-start.6) | collective-permute-done | bytes 655392 | tf_op jit(solution)/shard_map/ppermute | solution.py:42
  66.4 2.4 %collective-permute-start.11 = (bf16[2560,128]{1,0:T(8,128)(2,1)}, bf16[2560,128]{1,0:T(8,128)(2,1)S(1)}, u32[]{:S(2)}, u32[]{:S(2)}) collective-permute-start(bf16[2560,128]{1,0:T(8,128)(2,1)} %collective-permute-done.6.refs_4_), channel_id=1, source_target_pairs={{0,2},{1,3},{2,0},{3,1},{12,14},{13,15},{14,12},{15,13},{16,18},{1... | collective-permute-start | bytes 1966088 | tf_op jit(solution)/shard_map/ppermute | solution.py:42
  68.8 0.5 slice.23
  69.4 1.3 pad_add_fusion.1.meta_ref
  70.7 0.6 fusion.4
  71.3 7.5 %copy.8.refs_13_ = bf16[256,64,64]{2,1,0:T(8,128)(2,1)} copy(bf16[256,64,64]{0,2,1:T(8,128)(2,1)} %bitcast.12) | data formatting | bytes 4194304 | tf_op jit(solution)/shard_map/reshape | solution.py:169
  78.7 0.0 collective-permute-done.12.refs_11_
  78.7 0.0 collective-permute-done.8.refs_7_
  78.7 0.0 copy-start.2
  78.8 1.2 collective-permute-done.9.refs_8_
  79.9 0.0 copy-start.3
  79.9 0.0 collective-permute-done.10.refs_9_
  79.9 11.6 %collective-permute-done.11.refs_10_ = bf16[2560,128]{1,0:T(8,128)(2,1)S(1)} collective-permute-done((bf16[2560,128]{1,0:T(8,128)(2,1)}, bf16[2560,128]{1,0:T(8,128)(2,1)S(1)}, u32[]{:S(2)}, u32[]{:S(2)}) %collective-permute-start.11) | collective-permute-done | bytes 655392 | tf_op jit(solution)/shard_map/ppermute | solution.py:42
  91.5 0.0 copy-start.4
  91.5 0.0 copy-done.2
  91.5 0.0 copy-done.3
  91.5 0.8 copy-done.4
  92.3 20.0 %shard_map.46 = (f32[8,1280,128]{2,1,0:T(8,128)}, bf16[8,1280,128]{2,1,0:T(8,128)(2,1)}) custom-call(s32[512]{0:T(512)} %get-tuple-element.17.rows_ref, s32[512]{0:T(512)} %get-tuple-element.16.spots_ref, s32[4]{0:T(128)} %pad_add_fusion.1.meta_ref, bf16[2560,128]{1,0:T(8,128)(2,1)} %copy-done, bf16[2560,128]{1,0:T(8,128)(2,1)} %copy-done.1, ...), custom_call_target="tpu_custom_call" | custom-call | flops 2013265920 | bytes 26214400 | tf_op jit(solution)/shard_map/pallas_call | solution.py:186
  112.4 0.1 collective-permute-start.14
  112.5 5.1 %collective-permute-done.14 = bf16[8,1280,128]{2,1,0:T(8,128)(2,1)S(1)} collective-permute-done((bf16[8,1280,128]{2,1,0:T(8,128)(2,1)}, bf16[8,1280,128]{2,1,0:T(8,128)(2,1)S(1)}, u32[]{:S(2)}, u32[]{:S(2)}) %collective-permute-start.14) | collective-permute-done | bytes 2621472 | tf_op jit(solution)/shard_map/ppermute | solution.py:209
  117.6 4.6 %add_convert_fusion = bf16[8,1280,128]{2,1,0:T(8,128)(2,1)} fusion(f32[8,1280,128]{2,1,0:T(8,128)} %get-tuple-element.7, bf16[8,1280,128]{2,1,0:T(8,128)(2,1)S(1)} %collective-permute-done.14), kind=kLoop, calls=%fused_computation | loop fusion | flops 3932160 | bytes 10485760 | tf_op jit(solution)/shard_map/convert_element_type | solution.py:210
  122.2 0.0 reduce-scatter.2.cloned.1.call-update
  122.2 83.9 %reduce-scatter.2.cloned.1.call-done = bf16[1280,128]{1,0:T(8,128)(2,1)} async-done(((bf16[10240,128]{1,0:T(8,128)(2,1)}), bf16[1280,128]{1,0:T(8,128)(2,1)}) %reduce-scatter.2.cloned.1.call-update) | async-done | bytes 327696 | tf_op jit(solution)/shard_map/reduce_scatter | solution.py:211
  206.2 1.9 convert_multiply_fusion
  (5 shorter events, 0.1 us)
Async XLA Ops:
  6.5 199.6 %reduce-scatter.2.cloned.1.call-start = ((), (), s32[]{:S(2)}) async-start(), calls=%async_computation.1 | async-start | bytes 2949120 | tf_op jit(solution)/shard_map/reduce_scatter | solution.py:211
  7.7 28.6 %copy-start.5 = (s32[256,2]{0,1:T(2,128)S(1)}, s32[256,2]{0,1:T(2,128)}, u32[]{:S(2)}) copy-start(s32[256,2]{0,1:T(2,128)} %param.5) | copy-start | bytes 6148
  7.7 3.9 %collective-permute-start.1 = (bf16[1280,128]{1,0:T(8,128)(2,1)S(1)}, bf16[1280,128]{1,0:T(8,128)(2,1)S(1)}, u32[]{:S(2)}, u32[]{:S(2)}) collective-permute-start(bf16[1280,128]{1,0:T(8,128)(2,1)S(1)} %get-tuple-element.10), channel_id=1, source_target_pairs={{0,1},{1,0},{2,3},{3,2},{4,5},{5,4},{6,7},{7,6},{8,9},{9,8},{10,11... | collective-permute-start | bytes 983048 | tf_op jit(solution)/shard_map/ppermute | solution.py:152
  11.5 44.4 %collective-permute-start.13 = (bf16[256,4096]{0,1:T(8,128)(2,1)S(1)}, bf16[256,4096]{0,1:T(8,128)(2,1)}, u32[]{:S(2)}, u32[]{:S(2)}) collective-permute-start(bf16[256,4096]{0,1:T(8,128)(2,1)S(1)} %copy.5), channel_id=1, source_target_pairs={{0,1},{1,0},{2,3},{3,2},{4,5},{5,4},{6,7},{7,6},{8,9},{9,8},{10,11... | collective-permute-start | bytes 6291464 | tf_op jit(solution)/shard_map/ppermute | solution.py:167
  11.6 31.5 %copy-start = (bf16[2560,128]{1,0:T(8,128)(2,1)}, bf16[2560,128]{1,0:T(8,128)(2,1)S(1)}, u32[]{:S(2)}) copy-start(bf16[2560,128]{1,0:T(8,128)(2,1)S(1)} %pad_maximum_fusion.refs_0_) | copy-start | bytes 1966084
  11.6 18.0 %collective-permute-start.2 = (bf16[2560,128]{1,0:T(8,128)(2,1)S(1)}, bf16[2560,128]{1,0:T(8,128)(2,1)S(1)}, u32[]{:S(2)}, u32[]{:S(2)}) collective-permute-start(bf16[2560,128]{1,0:T(8,128)(2,1)S(1)} %pad_maximum_fusion.refs_0_), channel_id=1, source_target_pairs={{0,4},{1,5},{2,6},{3,7},{4,0},{5,1},{6,2},{7,3},{8,12},{9,13},{10,... | collective-permute-start | bytes 1966088 | tf_op jit(solution)/shard_map/ppermute | solution.py:42
  14.7 18.9 %collective-permute-start.3 = (bf16[2560,128]{1,0:T(8,128)(2,1)S(1)}, bf16[2560,128]{1,0:T(8,128)(2,1)}, u32[]{:S(2)}, u32[]{:S(2)}) collective-permute-start(bf16[2560,128]{1,0:T(8,128)(2,1)S(1)} %pad_maximum_fusion.refs_0_), channel_id=1, source_target_pairs={{4,8},{5,9},{6,10},{7,11},{8,4},{9,5},{10,6},{11,7},{20,24},{21,25... | collective-permute-start | bytes 1966088 | tf_op jit(solution)/shard_map/ppermute | solution.py:42
  29.7 18.5 %copy-start.1 = (bf16[2560,128]{1,0:T(8,128)(2,1)}, bf16[2560,128]{1,0:T(8,128)(2,1)S(1)}, u32[]{:S(2)}) copy-start(bf16[2560,128]{1,0:T(8,128)(2,1)S(1)} %collective-permute-done.2.refs_1_) | copy-start | bytes 1966084
  29.7 5.2 %collective-permute-start.5 = (bf16[2560,128]{1,0:T(8,128)(2,1)S(1)}, bf16[2560,128]{1,0:T(8,128)(2,1)}, u32[]{:S(2)}, u32[]{:S(2)}) collective-permute-start(bf16[2560,128]{1,0:T(8,128)(2,1)S(1)} %collective-permute-done.2.refs_1_), channel_id=1, source_target_pairs={{4,8},{5,9},{6,10},{7,11},{8,4},{9,5},{10,6},{11,7},{20,24},{21,25... | collective-permute-start | bytes 1966088 | tf_op jit(solution)/shard_map/ppermute | solution.py:42
  31.9 16.2 %collective-permute-start.7 = (bf16[2560,128]{1,0:T(8,128)(2,1)S(1)}, bf16[2560,128]{1,0:T(8,128)(2,1)}, u32[]{:S(2)}, u32[]{:S(2)}) collective-permute-start(bf16[2560,128]{1,0:T(8,128)(2,1)S(1)} %pad_maximum_fusion.refs_0_), channel_id=1, source_target_pairs={{0,2},{1,3},{2,0},{3,1},{4,6},{5,7},{6,4},{7,5},{8,10},{9,11},{10,... | collective-permute-start | bytes 1966088 | tf_op jit(solution)/shard_map/ppermute | solution.py:42
  33.6 20.8 %collective-permute-start.4 = (bf16[2560,128]{1,0:T(8,128)(2,1)}, bf16[2560,128]{1,0:T(8,128)(2,1)}, u32[]{:S(2)}, u32[]{:S(2)}) collective-permute-start(bf16[2560,128]{1,0:T(8,128)(2,1)} %collective-permute-done.3.refs_5_), channel_id=1, source_target_pairs={{4,0},{5,1},{6,2},{7,3},{8,12},{9,13},{10,14},{11,15},{20,16},{21,... | collective-permute-start | bytes 1966088 | tf_op jit(solution)/shard_map/ppermute | solution.py:42
  34.9 31.5 %collective-permute-start.6 = (bf16[2560,128]{1,0:T(8,128)(2,1)}, bf16[2560,128]{1,0:T(8,128)(2,1)}, u32[]{:S(2)}, u32[]{:S(2)}) collective-permute-start(bf16[2560,128]{1,0:T(8,128)(2,1)} %collective-permute-done.5.refs_3_), channel_id=1, source_target_pairs={{4,0},{5,1},{6,2},{7,3},{8,12},{9,13},{10,14},{11,15},{20,16},{21,... | collective-permute-start | bytes 1966088 | tf_op jit(solution)/shard_map/ppermute | solution.py:42
  36.3 6.8 %collective-permute-start = (s32[3,256]{1,0:T(4,128)S(1)}, s32[3,256]{1,0:T(4,128)S(1)}, u32[]{:S(2)}, u32[]{:S(2)}) collective-permute-start(s32[3,256]{1,0:T(4,128)S(1)} %add_add_fusion), channel_id=1, source_target_pairs={{0,1},{1,0},{2,3},{3,2},{4,5},{5,4},{6,7},{7,6},{8,9},{9,8},{10,11... | collective-permute-start | bytes 9224 | tf_op jit(solution)/shard_map/ppermute | solution.py:166
  43.1 35.6 %collective-permute-start.12 = (bf16[2560,128]{1,0:T(8,128)(2,1)}, bf16[2560,128]{1,0:T(8,128)(2,1)}, u32[]{:S(2)}, u32[]{:S(2)}) collective-permute-start(bf16[2560,128]{1,0:T(8,128)(2,1)} %collective-permute-done.3.refs_5_), channel_id=1, source_target_pairs={{4,6},{5,7},{6,4},{7,5},{8,10},{9,11},{10,8},{11,9},{20,22},{21,23... | collective-permute-start | bytes 1966088 | tf_op jit(solution)/shard_map/ppermute | solution.py:42
  48.2 30.6 %collective-permute-start.8 = (bf16[2560,128]{1,0:T(8,128)(2,1)S(1)}, bf16[2560,128]{1,0:T(8,128)(2,1)S(1)}, u32[]{:S(2)}, u32[]{:S(2)}) collective-permute-start(bf16[2560,128]{1,0:T(8,128)(2,1)S(1)} %collective-permute-done.2.refs_1_), channel_id=1, source_target_pairs={{0,2},{1,3},{2,0},{3,1},{4,6},{5,7},{6,4},{7,5},{8,10},{9,11},{10,... | collective-permute-start | bytes 1966088 | tf_op jit(solution)/shard_map/ppermute | solution.py:42
  54.4 25.6 %collective-permute-start.10 = (bf16[2560,128]{1,0:T(8,128)(2,1)}, bf16[2560,128]{1,0:T(8,128)(2,1)}, u32[]{:S(2)}, u32[]{:S(2)}) collective-permute-start(bf16[2560,128]{1,0:T(8,128)(2,1)} %collective-permute-done.5.refs_3_), channel_id=1, source_target_pairs={{4,6},{5,7},{6,4},{7,5},{8,10},{9,11},{10,8},{11,9},{20,22},{21,23... | collective-permute-start | bytes 1966088 | tf_op jit(solution)/shard_map/ppermute | solution.py:42
  55.9 24.0 %collective-permute-start.9 = (bf16[2560,128]{1,0:T(8,128)(2,1)}, bf16[2560,128]{1,0:T(8,128)(2,1)S(1)}, u32[]{:S(2)}, u32[]{:S(2)}) collective-permute-start(bf16[2560,128]{1,0:T(8,128)(2,1)} %collective-permute-done.4.refs_2_), channel_id=1, source_target_pairs={{0,2},{1,3},{2,0},{3,1},{12,14},{13,15},{14,12},{15,13},{16,18},{1... | collective-permute-start | bytes 1966088 | tf_op jit(solution)/shard_map/ppermute | solution.py:42
  66.4 25.1 %collective-permute-start.11 = (bf16[2560,128]{1,0:T(8,128)(2,1)}, bf16[2560,128]{1,0:T(8,128)(2,1)S(1)}, u32[]{:S(2)}, u32[]{:S(2)}) collective-permute-start(bf16[2560,128]{1,0:T(8,128)(2,1)} %collective-permute-done.6.refs_4_), channel_id=1, source_target_pairs={{0,2},{1,3},{2,0},{3,1},{12,14},{13,15},{14,12},{15,13},{16,18},{1... | collective-permute-start | bytes 1966088 | tf_op jit(solution)/shard_map/ppermute | solution.py:42
  78.7 12.8 %copy-start.2 = (bf16[2560,128]{1,0:T(8,128)(2,1)}, bf16[2560,128]{1,0:T(8,128)(2,1)S(1)}, u32[]{:S(2)}) copy-start(bf16[2560,128]{1,0:T(8,128)(2,1)S(1)} %collective-permute-done.8.refs_7_) | copy-start | bytes 1966084
  79.9 11.6 %copy-start.3 = (bf16[2560,128]{1,0:T(8,128)(2,1)}, bf16[2560,128]{1,0:T(8,128)(2,1)S(1)}, u32[]{:S(2)}) copy-start(bf16[2560,128]{1,0:T(8,128)(2,1)S(1)} %collective-permute-done.9.refs_8_) | copy-start | bytes 1966084
  91.5 0.8 copy-start.4
  112.4 5.2 %collective-permute-start.14 = (bf16[8,1280,128]{2,1,0:T(8,128)(2,1)}, bf16[8,1280,128]{2,1,0:T(8,128)(2,1)S(1)}, u32[]{:S(2)}, u32[]{:S(2)}) collective-permute-start(bf16[8,1280,128]{2,1,0:T(8,128)(2,1)} %get-tuple-element.8), channel_id=1, source_target_pairs={{0,1},{1,0},{2,3},{3,2},{4,5},{5,4},{6,7},{7,6},{8,9},{9,8},{10,11... | collective-permute-start | bytes 7864328 | tf_op jit(solution)/shard_map/ppermute | solution.py:209
Sparse Core Ops, SparseCore 0:
  122.3 83.7 reduce-scatter.1

commit v3 on v2

v3 whole, which is shorter than its diff:
```python
import functools
import math

import jax
import jax.numpy as jnp
from jax import lax
from jax.experimental import pallas as pl
from jax.experimental.pallas import tpu as pltpu
from jax.sharding import PartitionSpec as P

BLK = 64
WIN = 128
LANES = 128
UNROLL = 8
VMEM_BYTES = 60 * 1024 * 1024
LINE = 4


def place(z, x, core):
    return (z * 2 + x) * 2 + core


def pairs_of(step, levels=range(LINE)):
    found = []
    for z in levels:
        for x in range(2):
            for core in range(2):
                found.append((place(z, x, core), place(*step(z, x), core)))
    return found


def after(array, *others):
    return lax.optimization_barrier((array, *others))[0]


def move(array, pairs):
    return lax.ppermute(array, "aux", pairs)


ENDS, MIDDLES = (0, LINE - 1), (1, 2)
NEAR = pairs_of(lambda z, x: (z ^ 1, x))
INNER = pairs_of(lambda z, x: (3 - z, x), MIDDLES)
OUTWARD = pairs_of(lambda z, x: (0 if z == 1 else 3, x), MIDDLES)
INWARD = pairs_of(lambda z, x: (1 if z == 0 else 2, x), ENDS)
ACROSS = pairs_of(lambda z, x: (z, 1 - x))


def spread(own):
    x_own = move(own, ACROSS)
    z1 = move(own, NEAR)
    inner1 = move(own, INNER)
    x1 = move(after(z1, x_own), ACROSS)
    inner2 = move(z1, INNER)
    outward1 = move(inner1, OUTWARD)
    early = inner1 + outward1
    x_early = move(after(early, x1), ACROSS)
    late = inner2 + move(inner2, OUTWARD)
    x_late = move(after(late, x_early), ACROSS)
    return [own, z1, early, late, x_own, x1, x_early, x_late]


def collect(keep, send_far, send_near, swap):
    far = move(send_far, swap)
    near = move(send_near, swap)

    def narrow(array):
        return array.astype(jnp.bfloat16)

    crossed = {}
    last = None
    for step in (3, 2, 1, 0):
        part = narrow(keep[LINE + step] + far[step].astype(jnp.float32))
        if last is not None:
            part = after(part, last)
        last = crossed[step] = move(part, ACROSS)
    held = {
        step: keep[step] + near[step].astype(jnp.float32) + crossed[step].astype(jnp.float32) for step in range(LINE)
    }
    held[2] = held[2] + (from_end := move(narrow(held[3]), INWARD)).astype(jnp.float32)
    inner2 = move(narrow(held[2]), INNER)
    held[3] = held[3] + move(after(narrow(held[2]), from_end), INWARD).astype(jnp.float32)
    inner3 = move(narrow(held[3]), INNER)
    held[1] = held[1] + inner2.astype(jnp.float32)
    beside = move(narrow(held[1]), NEAR)
    return held[0] + beside.astype(jnp.float32) + inner3.astype(jnp.float32)


def work_kernel(piece, shard, chips_ref, rows_ref, spots_ref, meta_ref, *refs):
    count = len(refs) - 13
    sources = refs[:count]
    values, other_values, keep, send_far, send_near = refs[count : count + 5]
    occ, tiles, half, weights, keep_buf, far_buf, near_buf, sem = refs[count + 5 :]
    core = meta_ref[2]
    slot_rows = occ.shape[0] // count
    for index in range(count):
        pltpu.make_async_copy(sources[index], occ.at[pl.ds(index * slot_rows, slot_rows)], sem.at[0]).start()
    loads = [
        pltpu.make_async_copy(values, tiles.at[0], sem.at[1]),
        pltpu.make_async_copy(other_values, tiles.at[1], sem.at[2]),
    ]
    for load in loads:
        load.start()

    @pl.loop(0, half.shape[1] // BLK)
    def _(index):
        span = pl.ds(pl.multiple_of(index * BLK, BLK), BLK)
        for side in range(2):
            half[side, span, :] = jnp.zeros((BLK, LANES), jnp.float32)

    pltpu.make_async_copy(occ, occ, sem.at[0]).wait()
    slots = tiles.shape[1]
    pieces = BLK // piece

    for side in range(2):
        loads[side].wait()

        @pl.loop(0, meta_ref[side])
        def _(group):
            products = []
            for lane in range(UNROLL):
                slot = group * UNROLL + lane
                table = side * slots + slot
                parts = [
                    occ[pl.ds(pl.multiple_of(spots_ref[table * pieces + cut], piece), piece), :]
                    for cut in range(pieces)
                ]
                block = parts[0] if pieces == 1 else jnp.concatenate(parts, axis=0)
                products.append(jnp.dot(tiles[side, slot], block, preferred_element_type=jnp.float32))
            for lane in range(UNROLL):
                start = pl.multiple_of(rows_ref[side * slots + group * UNROLL + lane], BLK)
                half[side, pl.ds(start, BLK), :] += products[lane]

        weights[pl.ds(side * LANES, LANES), :] = half[side, pl.ds(0, WIN), :].T.astype(jnp.bfloat16)

    def rows_of(owner):
        span = pl.ds(pl.multiple_of(owner * shard, 32), shard)
        both = jnp.concatenate([half[side, span, :].astype(jnp.bfloat16) for side in range(2)], axis=1)
        return jnp.dot(both, weights[...], preferred_element_type=jnp.float32)

    near_count = near_buf.shape[0]
    for buf, out, base, copied in ((far_buf, send_far, near_count, 3), (near_buf, send_near, 0, 4)):

        @pl.loop(0, buf.shape[0])
        def _(index):
            chip = chips_ref[base + index]
            buf[index] = rows_of(2 * chip + 1 - core).astype(jnp.bfloat16)
            pltpu.make_async_copy(buf.at[index], out.at[index], sem.at[copied]).start()

    @pl.loop(0, keep.shape[0])
    def _(index):
        keep_buf[index] = rows_of(2 * chips_ref[index] + core)
        pltpu.make_async_copy(keep_buf.at[index], keep.at[index], sem.at[5]).start()

    pltpu.make_async_copy(far_buf, send_far, sem.at[3]).wait()
    pltpu.make_async_copy(near_buf, send_near, sem.at[4]).wait()
    pltpu.make_async_copy(keep_buf, keep, sem.at[5]).wait()


def local(block_values, block_pairs, live_counts, occupied):
    owners = lax.axis_size("aux")
    me = lax.axis_index("aux")
    core, chip = me % 2, me // 2
    shard, width = occupied.shape
    total = owners * shard
    slots = block_values.shape[0]
    piece = math.gcd(BLK, shard)
    same_core = [[2 * i + k for i in range(owners // 2)] for k in range(2)]
    swap = [(i, i ^ 1) for i in range(owners)]

    mine = lax.dynamic_slice_in_dim(occupied, core * LANES, LANES, 1)
    given = lax.dynamic_slice_in_dim(occupied, (1 - core) * LANES, LANES, 1)
    own = jnp.concatenate([mine, lax.ppermute(given, "aux", swap)], axis=0)

    chips = owners // 2
    slot_ids = jnp.arange(chips, dtype=jnp.int32)
    lined = chips == 2 * LINE
    if lined:
        held = spread(own)
        chip_of_slot = ((slot_ids % LINE) ^ (chip // 2)) * 2 + ((slot_ids // LINE) ^ (chip % 2))
    else:
        held = [lax.all_gather(own, "aux", axis_index_groups=same_core, axis=0, tiled=True)]
        chip_of_slot = slot_ids

    live = live_counts[0]
    tile_ids = jnp.arange(slots, dtype=jnp.int32)
    row_starts = jnp.where(tile_ids < live, block_pairs[:, 0] * BLK, total)
    groups = jnp.full((slots,), (live + UNROLL - 1) // UNROLL, jnp.int32)
    table = jnp.stack([row_starts, block_pairs[:, 1], groups])
    other_table = lax.ppermute(table, "aux", swap)
    block_values = after(block_values, own)
    tiles = block_values.reshape(slots, BLK, BLK)
    other_values = lax.ppermute(block_values, "aux", swap)
    other_tiles = other_values.reshape(slots, BLK, BLK)

    rows = jnp.concatenate([table[0], other_table[0]])
    columns = jnp.concatenate([table[1], other_table[1]])
    first = columns[:, None] * BLK + jnp.arange(BLK // piece, dtype=jnp.int32) * piece
    owner = first // shard
    owner_chip = owner // 2
    slot_of = owner_chip
    if lined:
        level = chip // 2
        apart = (owner_chip // 2) ^ level
        in_middle = ((level == 1) | (level == 2)).astype(jnp.int32)
        slot_of = (apart ^ (apart // 2 * in_middle)) + LINE * ((owner_chip % 2) ^ (chip % 2))
    spots = (slot_of * (2 * shard) + ((owner % 2) ^ core) * shard + first % shard).reshape(-1)
    meta = jnp.stack([table[2, 0], other_table[2, 0], core]).astype(jnp.int32)

    smem = pl.BlockSpec(memory_space=pltpu.SMEM)
    hbm = pl.BlockSpec(memory_space=pl.ANY)
    sizes = (chips, chips // 2, chips - chips // 2)
    keep, send_far, send_near = pl.pallas_call(
        functools.partial(work_kernel, piece, shard),
        out_shape=(
            jax.ShapeDtypeStruct((chips, shard, WIN), jnp.float32),
            jax.ShapeDtypeStruct((sizes[1], shard, WIN), jnp.bfloat16),
            jax.ShapeDtypeStruct((sizes[2], shard, WIN), jnp.bfloat16),
        ),
        in_specs=[smem] * 4 + [hbm] * (len(held) + 2),
        out_specs=(hbm, hbm, hbm),
        scratch_shapes=[
            pltpu.VMEM((total, LANES), jnp.bfloat16),
            pltpu.VMEM((2, slots, BLK, BLK), jnp.bfloat16),
            pltpu.VMEM((2, total + BLK, LANES), jnp.float32),
            pltpu.VMEM((2 * LANES, WIN), jnp.bfloat16),
            pltpu.VMEM((sizes[0], shard, WIN), jnp.float32),
            pltpu.VMEM((sizes[1], shard, WIN), jnp.bfloat16),
            pltpu.VMEM((sizes[2], shard, WIN), jnp.bfloat16),
            pltpu.SemaphoreType.DMA((6,)),
        ],
        compiler_params=pltpu.CompilerParams(vmem_limit_bytes=VMEM_BYTES),
        cost_estimate=pl.CostEstimate(
            flops=2 * total * width * (WIN + BLK), bytes_accessed=25 << 20, transcendentals=0
        ),
    )(chip_of_slot, rows, spots, meta, *held, tiles, other_tiles)

    factor = 1.0 / math.sqrt(owners * width)
    if lined:
        return collect(keep, send_far, send_near, swap) * factor
    send = jnp.concatenate([send_near, send_far], axis=0)
    pair_sum = (keep + move(send, swap).astype(jnp.float32)).astype(jnp.bfloat16)
    block_sum = lax.psum_scatter(
        pair_sum.reshape(total // 2, WIN), "aux", axis_index_groups=same_core, scatter_dimension=0, tiled=True
    )
    return block_sum.astype(jnp.float32) * factor


def solution(mesh):
    placed = (
        P(("groups", "aux"), None),
        P(("groups", "aux"), None),
        P(("groups", "aux")),
        P(("groups", "aux"), None),
    )
    return jax.shard_map(
        local, mesh=mesh, in_specs=placed, out_specs=P(("groups", "aux"), None), check_vma=False
    )
```

time: 215 us -> 150 us (0.70)
  waiting for transfers between devices: 132 us -> 71.7 us
  between operations: 14.3 us -> 0.92 us
  starting transfers between devices: 19.7 us -> 26.4 us
    reduce_scatter x1 -> x0, waiting for transfers between devices: 83.9 us -> none  [local(): lax.psum_scatter(pair_sum.reshape(total // 2, WIN), 'aux', axis_index_gro...]
    ppermute x11 -> x20, waiting for transfers between devices: 43.2 us -> 70.4 us  [move(): return lax.ppermute(array, 'aux', pairs)]
    ppermute x11 -> x20, starting transfers between devices: 19 us -> 25.7 us  [move(): return lax.ppermute(array, 'aux', pairs)]
    ppermute x1 -> x0, waiting for transfers between devices: 5.11 us -> none  [local(): arrived = lax.ppermute(send, 'aux', swap)]
    add x0 -> x3, other arithmetic: none -> 3.3 us  [the longest x1 1.46 us: spread(): early = inner1 + outward1]
    optimization_barrier x0 -> x1, local copies, waits for them, and re-layouts: none -> 3.27 us  [after(): return lax.optimization_barrier((array, *others))[0]]
    unnamed x13 -> x16, local copies, waits for them, and re-layouts: 4.12 us -> 0.9 us
    convert_element_type x1 -> x4, other arithmetic: 4.62 us -> 2.76 us  [narrow(): return array.astype(jnp.bfloat16)]
  transfers between devices with their start and end apart: 16 -> 23, of which waited for: 8 -> 11; matrix products, arithmetic and copies ran while one was open for 9% -> 18% of each run, Pallas kernels for 0% -> 0%
where the time goes in v3:
time: 150 us; the launch traced here: 148 us
  waiting for transfers between devices  71.7 us (48%)
  starting transfers between devices  26.4 us (18%)
  Pallas kernels  20.4 us (14%)
  local copies, waits for them, and re-layouts  20.1 us (13%)
  other arithmetic  9.04 us (6%)
    ppermute x20, waiting for transfers between devices, move(): return lax.ppermute(array, 'aux', pairs)  70.4 us
    ppermute x20, starting transfers between devices, move(): return lax.ppermute(array, 'aux', pairs)  25.7 us
    pallas_call x1, Pallas kernels, local(): pl.pallas_call(functools.partial(work_kernel, piece, shard), out_shape=(j...  20.4 us
    reshape x1, local copies, waits for them, and re-layouts, local(): other_tiles = other_values.reshape(slots, BLK, BLK)  7.45 us
    reshape x1, local copies, waits for them, and re-layouts, local(): tiles = block_values.reshape(slots, BLK, BLK)  6.71 us
    optimization_barrier x1, local copies, waits for them, and re-layouts, after(): return lax.optimization_barrier((array, *others))[0]  3.27 us
  transfers between devices with their start and end apart: 23, of which 11 were waited for; matrix products, arithmetic and copies ran while one was open for 18% of the time, Pallas kernels for 0%

profile of v3, /device:TPU:0, one launch (start us, length us, event | category | flops | bytes accessed | tf_op | source)
XLA Modules:
  0.0 148.5 jit_solution(2266742123473089520)
XLA Ops:
  0.0 1.1 constant_dynamic-slice_fusion.1
  1.1 0.5 collective-permute-start.1
  1.6 1.3 collective-permute-done.1
  2.9 0.0 copy-start.1
  3.0 2.9 %collective-permute-start.7 = (bf16[2560,128]{1,0:T(8,128)(2,1)S(1)}, bf16[2560,128]{1,0:T(8,128)(2,1)S(1)}, u32[]{:S(2)}, u32[]{:S(2)}) collective-permute-start(bf16[2560,128]{1,0:T(8,128)(2,1)S(1)} %pad_maximum_fusion.refs_0_), channel_id=1, source_target_pairs={{0,2},{1,3},{2,0},{3,1},{4,6},{5,7},{6,4},{7,5},{8,10},{9,11},{10,... | collective-permute-start | bytes 1966088 | tf_op jit(solution)/shard_map/ppermute | solution.py:37
  5.9 1.6 %collective-permute-start.2 = (bf16[2560,128]{1,0:T(8,128)(2,1)S(1)}, bf16[2560,128]{1,0:T(8,128)(2,1)S(1)}, u32[]{:S(2)}, u32[]{:S(2)}) collective-permute-start(bf16[2560,128]{1,0:T(8,128)(2,1)S(1)} %pad_maximum_fusion.refs_0_), channel_id=1, source_target_pairs={{0,4},{1,5},{2,6},{3,7},{4,0},{5,1},{6,2},{7,3},{8,12},{9,13},{10,... | collective-permute-start | bytes 1966088 | tf_op jit(solution)/shard_map/ppermute | solution.py:37
  7.5 1.5 %collective-permute-start.3 = (bf16[2560,128]{1,0:T(8,128)(2,1)S(1)}, bf16[2560,128]{1,0:T(8,128)(2,1)}, u32[]{:S(2)}, u32[]{:S(2)}) collective-permute-start(bf16[2560,128]{1,0:T(8,128)(2,1)S(1)} %pad_maximum_fusion.refs_0_), channel_id=1, source_target_pairs={{4,8},{5,9},{6,10},{7,11},{8,4},{9,5},{10,6},{11,7},{20,24},{21,25... | collective-permute-start | bytes 1966088 | tf_op jit(solution)/shard_map/ppermute | solution.py:37
  9.0 12.0 %collective-permute-done.7.refs_4_ = bf16[2560,128]{1,0:T(8,128)(2,1)S(1)} collective-permute-done((bf16[2560,128]{1,0:T(8,128)(2,1)S(1)}, bf16[2560,128]{1,0:T(8,128)(2,1)S(1)}, u32[]{:S(2)}, u32[]{:S(2)}) %collective-permute-start.7) | collective-permute-done | bytes 655392 | tf_op jit(solution)/shard_map/ppermute | solution.py:37
  20.9 1.5 collective-permute-done.2.refs_1_
  22.4 0.0 collective-permute-done.3
  22.4 1.3 collective-permute-start.4
  23.7 0.4 collective-permute-start.8
  24.1 1.5 %collective-permute-start.5 = (bf16[2560,128]{1,0:T(8,128)(2,1)S(1)}, bf16[2560,128]{1,0:T(8,128)(2,1)}, u32[]{:S(2)}, u32[]{:S(2)}) collective-permute-start(bf16[2560,128]{1,0:T(8,128)(2,1)S(1)} %collective-permute-done.2.refs_1_), channel_id=1, source_target_pairs={{4,8},{5,9},{6,10},{7,11},{8,4},{9,5},{10,6},{11,7},{20,24},{21,25... | collective-permute-start | bytes 1966088 | tf_op jit(solution)/shard_map/ppermute | solution.py:37
  25.6 3.3 %copy.5 = bf16[256,4096]{0,1:T(8,128)(2,1)S(1)} copy(bf16[256,4096]{1,0:T(8,128)(2,1)} %param.4) | data formatting | bytes 4194304 | tf_op jit(solution)/shard_map/optimization_barrier | solution.py:33
  28.9 0.0 copy-start.7
  28.9 0.1 collective-permute-start.11
  29.6 0.1 pad.11.clone
  29.7 12.8 %collective-permute-done.4 = bf16[2560,128]{1,0:T(8,128)(2,1)} collective-permute-done((bf16[2560,128]{1,0:T(8,128)(2,1)}, bf16[2560,128]{1,0:T(8,128)(2,1)}, u32[]{:S(2)}, u32[]{:S(2)}) %collective-permute-start.4) | collective-permute-done | bytes 655392 | tf_op jit(solution)/shard_map/ppermute | solution.py:37
  42.5 1.5 add.173.refs_2_
  44.0 0.0 collective-permute-done.8.refs_5_
  44.0 0.6 collective-permute-start.9
  44.6 0.0 collective-permute-done.5
  44.6 1.3 collective-permute-start.6
  45.9 0.1 add_add_fusion
  46.0 0.0 collective-permute-start
  46.0 15.4 %collective-permute-done.6 = bf16[2560,128]{1,0:T(8,128)(2,1)S(1)} collective-permute-done((bf16[2560,128]{1,0:T(8,128)(2,1)}, bf16[2560,128]{1,0:T(8,128)(2,1)S(1)}, u32[]{:S(2)}, u32[]{:S(2)}) %collective-permute-start.6) | collective-permute-done | bytes 655392 | tf_op jit(solution)/shard_map/ppermute | solution.py:37
  61.4 1.3 add.174.refs_3_
  62.7 0.0 collective-permute-done.9.refs_6_
  62.7 0.9 copy-done.6
  63.6 1.5 %collective-permute-start.10 = (bf16[2560,128]{1,0:T(8,128)(2,1)S(1)}, bf16[2560,128]{1,0:T(8,128)(2,1)}, u32[]{:S(2)}, u32[]{:S(2)}) collective-permute-start(bf16[2560,128]{1,0:T(8,128)(2,1)S(1)} %add.174.refs_3_), channel_id=1, source_target_pairs={{0,2},{1,3},{2,0},{3,1},{4,6},{5,7},{6,4},{7,5},{8,10},{9,11},{10,... | collective-permute-start | bytes 1966088 | tf_op jit(solution)/shard_map/ppermute | solution.py:37
  65.1 0.6 fusion.30.chips_ref
  65.7 0.0 collective-permute-done
  65.7 0.6 slice.87
  66.2 1.2 pad_add_fusion.1.meta_ref
  67.4 0.6 fusion.19
  68.1 6.7 %copy.7.refs_8_ = bf16[256,64,64]{2,1,0:T(8,128)(2,1)} copy(bf16[256,64,64]{0,2,1:T(8,128)(2,1)S(1)} %bitcast.52) | data formatting | bytes 4194304 | tf_op jit(solution)/shard_map/reshape | solution.py:191
  74.8 0.0 collective-permute-done.11
  74.8 7.5 %copy.8.refs_9_ = bf16[256,64,64]{2,1,0:T(8,128)(2,1)} copy(bf16[256,64,64]{0,2,1:T(8,128)(2,1)} %bitcast.11) | data formatting | bytes 4194304 | tf_op jit(solution)/shard_map/reshape | solution.py:193
  82.2 0.0 collective-permute-done.10.refs_7_
  82.2 20.4 %shard_map.46 = (f32[8,1280,128]{2,1,0:T(8,128)}, bf16[4,1280,128]{2,1,0:T(8,128)(2,1)}, bf16[4,1280,128]{2,1,0:T(8,128)(2,1)}) custom-call(s32[8]{0:T(128)} %fusion.30.chips_ref, s32[512]{0:T(512)} %get-tuple-element.41.rows_ref, s32[512]{0:T(512)} %get-tuple-element.40.spots_ref, s32[3]{0:T(128)} %pad_add_fusion.1.meta_ref, bf16[2560,128]{1,0:T(8,128)(2,1)} %copy-done.1, ...), custom_call_target="tpu_custom_call" | custom-call | flops 2013265920 | bytes 26214400 | tf_op jit(solution)/shard_map/pallas_call | solution.py:212
  102.6 0.1 collective-permute-start.13
  102.7 0.5 collective-permute-start.12
  103.2 2.7 %collective-permute-done.13 = bf16[4,1280,128]{2,1,0:T(8,128)(2,1)S(1)} collective-permute-done((bf16[4,1280,128]{2,1,0:T(8,128)(2,1)}, bf16[4,1280,128]{2,1,0:T(8,128)(2,1)S(1)}, u32[]{:S(2)}, u32[]{:S(2)}) %collective-permute-start.13) | collective-permute-done | bytes 1310752 | tf_op jit(solution)/shard_map/ppermute | solution.py:37
  105.9 2.1 %fusion.7 = (bf16[1280,128]{1,0:T(8,128)(2,1)S(1)}, bf16[1280,128]{1,0:T(8,128)(2,1)S(1)}, bf16[1280,128]{1,0:T(8,128)(2,1)S(1)}, bf16[1280,128]{1,0:T(8,128)(2,1)S(1)}) fusion(f32[8,1280,128]{2,1,0:T(8,128)} %get-tuple-element.20, bf16[4,1280,128]{2,1,0:T(8,128)(2,1)S(1)} %collective-permute-done.13), kind=kLoop, calls=%fused_computation.17 | loop fusion | flops 1966080 | bytes 5242880 | tf_op jit(solution)/shard_map/convert_element_type | solution.py:67
  108.1 0.1 collective-permute-start.14
  108.2 9.7 %collective-permute-done.14 = bf16[1280,128]{1,0:T(8,128)(2,1)S(1)} collective-permute-done((bf16[1280,128]{1,0:T(8,128)(2,1)S(1)}, bf16[1280,128]{1,0:T(8,128)(2,1)S(1)}, u32[]{:S(2)}, u32[]{:S(2)}) %collective-permute-start.14) | collective-permute-done | bytes 327712 | tf_op jit(solution)/shard_map/ppermute | solution.py:37
  117.9 0.3 collective-permute-start.15
  118.2 0.1 fusion.11
  118.3 1.3 collective-permute-start.18
  119.6 7.2 %collective-permute-done.15 = bf16[1280,128]{1,0:T(8,128)(2,1)S(1)} collective-permute-done((bf16[1280,128]{1,0:T(8,128)(2,1)S(1)}, bf16[1280,128]{1,0:T(8,128)(2,1)S(1)}, u32[]{:S(2)}, u32[]{:S(2)}) %collective-permute-start.15) | collective-permute-done | bytes 327712 | tf_op jit(solution)/shard_map/ppermute | solution.py:37
  126.8 0.6 collective-permute-start.16
  127.4 0.2 fusion.1
  127.6 3.3 %collective-permute-start.21 = (bf16[1280,128]{1,0:T(8,128)(2,1)S(1)}, bf16[1280,128]{1,0:T(8,128)(2,1)S(1)}, u32[]{:S(2)}, u32[]{:S(2)}) collective-permute-start(bf16[1280,128]{1,0:T(8,128)(2,1)S(1)} %fusion.1), channel_id=1, source_target_pairs={{0,4},{1,5},{2,6},{3,7},{12,8},{13,9},{14,10},{15,11},{16,20},{17,... | collective-permute-start | bytes 983048 | tf_op jit(solution)/shard_map/ppermute | solution.py:37
  131.0 0.7 collective-permute-start.19
  131.6 3.2 %collective-permute-done.16 = bf16[1280,128]{1,0:T(8,128)(2,1)S(1)} collective-permute-done((bf16[1280,128]{1,0:T(8,128)(2,1)S(1)}, bf16[1280,128]{1,0:T(8,128)(2,1)S(1)}, u32[]{:S(2)}, u32[]{:S(2)}) %collective-permute-start.16) | collective-permute-done | bytes 327712 | tf_op jit(solution)/shard_map/ppermute | solution.py:37
  134.8 0.9 collective-permute-start.17
  135.8 1.0 collective-permute-done.21
  136.8 0.0 collective-permute-done.19
  136.8 0.3 fusion.3
  137.1 4.7 %collective-permute-start.20 = (bf16[1280,128]{1,0:T(8,128)(2,1)S(1)}, bf16[1280,128]{1,0:T(8,128)(2,1)S(1)}, u32[]{:S(2)}, u32[]{:S(2)}) collective-permute-start(bf16[1280,128]{1,0:T(8,128)(2,1)S(1)} %get-tuple-element.31), channel_id=1, source_target_pairs={{0,4},{1,5},{2,6},{3,7},{4,0},{5,1},{6,2},{7,3},{8,12},{9,13},{10,... | collective-permute-start | bytes 983048 | tf_op jit(solution)/shard_map/ppermute | solution.py:37
  141.8 0.7 collective-permute-start.22
  142.5 0.0 collective-permute-done.17
  142.5 4.9 %collective-permute-done.20 = bf16[1280,128]{1,0:T(8,128)(2,1)S(1)} collective-permute-done((bf16[1280,128]{1,0:T(8,128)(2,1)S(1)}, bf16[1280,128]{1,0:T(8,128)(2,1)S(1)}, u32[]{:S(2)}, u32[]{:S(2)}) %collective-permute-start.20) | collective-permute-done | bytes 327712 | tf_op jit(solution)/shard_map/ppermute | solution.py:37
  147.4 1.0 fusion.6
  (21 shorter events, 0.1 us)
Async XLA Ops:
  1.1 1.8 %collective-permute-start.1 = (bf16[1280,128]{1,0:T(8,128)(2,1)S(1)}, bf16[1280,128]{1,0:T(8,128)(2,1)S(1)}, u32[]{:S(2)}, u32[]{:S(2)}) collective-permute-start(bf16[1280,128]{1,0:T(8,128)(2,1)S(1)} %get-tuple-element.34), channel_id=1, source_target_pairs={{0,1},{1,0},{2,3},{3,2},{4,5},{5,4},{6,7},{7,6},{8,9},{9,8},{10,11... | collective-permute-start | bytes 983048 | tf_op jit(solution)/shard_map/ppermute | solution.py:172
  2.9 25.9 %copy-start.1 = (bf16[2560,128]{1,0:T(8,128)(2,1)}, bf16[2560,128]{1,0:T(8,128)(2,1)S(1)}, u32[]{:S(2)}) copy-start(bf16[2560,128]{1,0:T(8,128)(2,1)S(1)} %pad_maximum_fusion.refs_0_) | copy-start | bytes 1966084
  3.0 18.0 %collective-permute-start.7 = (bf16[2560,128]{1,0:T(8,128)(2,1)S(1)}, bf16[2560,128]{1,0:T(8,128)(2,1)S(1)}, u32[]{:S(2)}, u32[]{:S(2)}) collective-permute-start(bf16[2560,128]{1,0:T(8,128)(2,1)S(1)} %pad_maximum_fusion.refs_0_), channel_id=1, source_target_pairs={{0,2},{1,3},{2,0},{3,1},{4,6},{5,7},{6,4},{7,5},{8,10},{9,11},{10,... | collective-permute-start | bytes 1966088 | tf_op jit(solution)/shard_map/ppermute | solution.py:37
  5.9 16.5 %collective-permute-start.2 = (bf16[2560,128]{1,0:T(8,128)(2,1)S(1)}, bf16[2560,128]{1,0:T(8,128)(2,1)S(1)}, u32[]{:S(2)}, u32[]{:S(2)}) collective-permute-start(bf16[2560,128]{1,0:T(8,128)(2,1)S(1)} %pad_maximum_fusion.refs_0_), channel_id=1, source_target_pairs={{0,4},{1,5},{2,6},{3,7},{4,0},{5,1},{6,2},{7,3},{8,12},{9,13},{10,... | collective-permute-start | bytes 1966088 | tf_op jit(solution)/shard_map/ppermute | solution.py:37
  7.5 14.9 %collective-permute-start.3 = (bf16[2560,128]{1,0:T(8,128)(2,1)S(1)}, bf16[2560,128]{1,0:T(8,128)(2,1)}, u32[]{:S(2)}, u32[]{:S(2)}) collective-permute-start(bf16[2560,128]{1,0:T(8,128)(2,1)S(1)} %pad_maximum_fusion.refs_0_), channel_id=1, source_target_pairs={{4,8},{5,9},{6,10},{7,11},{8,4},{9,5},{10,6},{11,7},{20,24},{21,25... | collective-permute-start | bytes 1966088 | tf_op jit(solution)/shard_map/ppermute | solution.py:37
  20.9 3.2 %copy-start.4 = (bf16[2560,128]{1,0:T(8,128)(2,1)}, bf16[2560,128]{1,0:T(8,128)(2,1)S(1)}, u32[]{:S(2)}) copy-start(bf16[2560,128]{1,0:T(8,128)(2,1)S(1)} %collective-permute-done.7.refs_4_) | copy-start | bytes 1966084
  22.4 6.5 %copy-start.5 = (bf16[2560,128]{1,0:T(8,128)(2,1)}, bf16[2560,128]{1,0:T(8,128)(2,1)S(1)}, u32[]{:S(2)}) copy-start(bf16[2560,128]{1,0:T(8,128)(2,1)S(1)} %collective-permute-done.2.refs_1_) | copy-start | bytes 1966084
  22.4 20.2 %collective-permute-start.4 = (bf16[2560,128]{1,0:T(8,128)(2,1)}, bf16[2560,128]{1,0:T(8,128)(2,1)}, u32[]{:S(2)}, u32[]{:S(2)}) collective-permute-start(bf16[2560,128]{1,0:T(8,128)(2,1)} %collective-permute-done.3), channel_id=1, source_target_pairs={{4,0},{5,1},{6,2},{7,3},{8,12},{9,13},{10,14},{11,15},{20,16},{21,... | collective-permute-start | bytes 1966088 | tf_op jit(solution)/shard_map/ppermute | solution.py:37
  23.7 20.3 %collective-permute-start.8 = (bf16[2560,128]{1,0:T(8,128)(2,1)S(1)}, bf16[2560,128]{1,0:T(8,128)(2,1)}, u32[]{:S(2)}, u32[]{:S(2)}) collective-permute-start(bf16[2560,128]{1,0:T(8,128)(2,1)S(1)} %collective-permute-done.2.refs_1_), channel_id=1, source_target_pairs={{0,2},{1,3},{2,0},{3,1},{4,6},{5,7},{6,4},{7,5},{8,10},{9,11},{10,... | collective-permute-start | bytes 1966088 | tf_op jit(solution)/shard_map/ppermute | solution.py:37
  24.1 20.5 %collective-permute-start.5 = (bf16[2560,128]{1,0:T(8,128)(2,1)S(1)}, bf16[2560,128]{1,0:T(8,128)(2,1)}, u32[]{:S(2)}, u32[]{:S(2)}) collective-permute-start(bf16[2560,128]{1,0:T(8,128)(2,1)S(1)} %collective-permute-done.2.refs_1_), channel_id=1, source_target_pairs={{4,8},{5,9},{6,10},{7,11},{8,4},{9,5},{10,6},{11,7},{20,24},{21,25... | collective-permute-start | bytes 1966088 | tf_op jit(solution)/shard_map/ppermute | solution.py:37
  28.9 17.0 %copy-start.7 = (s32[256,2]{0,1:T(2,128)S(1)}, s32[256,2]{0,1:T(2,128)}, u32[]{:S(2)}) copy-start(s32[256,2]{0,1:T(2,128)} %param.5) | copy-start | bytes 6148
  28.9 45.9 %collective-permute-start.11 = (bf16[256,4096]{0,1:T(8,128)(2,1)S(1)}, bf16[256,4096]{0,1:T(8,128)(2,1)}, u32[]{:S(2)}, u32[]{:S(2)}) collective-permute-start(bf16[256,4096]{0,1:T(8,128)(2,1)S(1)} %copy.5), channel_id=1, source_target_pairs={{0,1},{1,0},{2,3},{3,2},{4,5},{5,4},{6,7},{7,6},{8,9},{9,8},{10,11... | collective-permute-start | bytes 6291464 | tf_op jit(solution)/shard_map/ppermute | solution.py:192
  44.0 30.8 %copy-start.2 = (bf16[2560,128]{1,0:T(8,128)(2,1)}, bf16[2560,128]{1,0:T(8,128)(2,1)S(1)}, u32[]{:S(2)}) copy-start(bf16[2560,128]{1,0:T(8,128)(2,1)S(1)} %add.173.refs_2_) | copy-start | bytes 1966084
  44.0 18.7 %collective-permute-start.9 = (bf16[2560,128]{1,0:T(8,128)(2,1)S(1)}, bf16[2560,128]{1,0:T(8,128)(2,1)S(1)}, u32[]{:S(2)}, u32[]{:S(2)}) collective-permute-start(bf16[2560,128]{1,0:T(8,128)(2,1)S(1)} %add.173.refs_2_), channel_id=1, source_target_pairs={{0,2},{1,3},{2,0},{3,1},{4,6},{5,7},{6,4},{7,5},{8,10},{9,11},{10,... | collective-permute-start | bytes 1966088 | tf_op jit(solution)/shard_map/ppermute | solution.py:37
  44.6 16.8 %collective-permute-start.6 = (bf16[2560,128]{1,0:T(8,128)(2,1)}, bf16[2560,128]{1,0:T(8,128)(2,1)S(1)}, u32[]{:S(2)}, u32[]{:S(2)}) collective-permute-start(bf16[2560,128]{1,0:T(8,128)(2,1)} %collective-permute-done.5), channel_id=1, source_target_pairs={{4,0},{5,1},{6,2},{7,3},{8,12},{9,13},{10,14},{11,15},{20,16},{21,... | collective-permute-start | bytes 1966088 | tf_op jit(solution)/shard_map/ppermute | solution.py:37
  46.0 19.6 %collective-permute-start = (s32[3,256]{1,0:T(4,128)S(1)}, s32[3,256]{1,0:T(4,128)S(1)}, u32[]{:S(2)}, u32[]{:S(2)}) collective-permute-start(s32[3,256]{1,0:T(4,128)S(1)} %add_add_fusion), channel_id=1, source_target_pairs={{0,1},{1,0},{2,3},{3,2},{4,5},{5,4},{6,7},{7,6},{8,9},{9,8},{10,11... | collective-permute-start | bytes 9224 | tf_op jit(solution)/shard_map/ppermute | solution.py:189
  62.7 12.1 %copy-start.3 = (bf16[2560,128]{1,0:T(8,128)(2,1)}, bf16[2560,128]{1,0:T(8,128)(2,1)S(1)}, u32[]{:S(2)}) copy-start(bf16[2560,128]{1,0:T(8,128)(2,1)S(1)} %add.174.refs_3_) | copy-start | bytes 1966084
  62.7 0.9 copy-start.6
  63.6 18.6 %collective-permute-start.10 = (bf16[2560,128]{1,0:T(8,128)(2,1)S(1)}, bf16[2560,128]{1,0:T(8,128)(2,1)}, u32[]{:S(2)}, u32[]{:S(2)}) collective-permute-start(bf16[2560,128]{1,0:T(8,128)(2,1)S(1)} %add.174.refs_3_), channel_id=1, source_target_pairs={{0,2},{1,3},{2,0},{3,1},{4,6},{5,7},{6,4},{7,5},{8,10},{9,11},{10,... | collective-permute-start | bytes 1966088 | tf_op jit(solution)/shard_map/ppermute | solution.py:37
  102.6 3.3 %collective-permute-start.13 = (bf16[4,1280,128]{2,1,0:T(8,128)(2,1)}, bf16[4,1280,128]{2,1,0:T(8,128)(2,1)S(1)}, u32[]{:S(2)}, u32[]{:S(2)}) collective-permute-start(bf16[4,1280,128]{2,1,0:T(8,128)(2,1)} %get-tuple-element.22), channel_id=1, source_target_pairs={{0,1},{1,0},{2,3},{3,2},{4,5},{5,4},{6,7},{7,6},{8,9},{9,8},{10,11... | collective-permute-start | bytes 3932168 | tf_op jit(solution)/shard_map/ppermute | solution.py:37
  102.7 15.5 %collective-permute-start.12 = (bf16[4,1280,128]{2,1,0:T(8,128)(2,1)}, bf16[4,1280,128]{2,1,0:T(8,128)(2,1)S(1)}, u32[]{:S(2)}, u32[]{:S(2)}) collective-permute-start(bf16[4,1280,128]{2,1,0:T(8,128)(2,1)} %get-tuple-element.21), channel_id=1, source_target_pairs={{0,1},{1,0},{2,3},{3,2},{4,5},{5,4},{6,7},{7,6},{8,9},{9,8},{10,11... | collective-permute-start | bytes 3932168 | tf_op jit(solution)/shard_map/ppermute | solution.py:37
  105.9 12.3 %copy-start = (f32[8,1280,128]{2,1,0:T(8,128)S(1)}, f32[8,1280,128]{2,1,0:T(8,128)}, u32[]{:S(2)}) copy-start(f32[8,1280,128]{2,1,0:T(8,128)} %get-tuple-element.20) | copy-start | bytes 15728644
  108.1 9.8 %collective-permute-start.14 = (bf16[1280,128]{1,0:T(8,128)(2,1)S(1)}, bf16[1280,128]{1,0:T(8,128)(2,1)S(1)}, u32[]{:S(2)}, u32[]{:S(2)}) collective-permute-start(bf16[1280,128]{1,0:T(8,128)(2,1)S(1)} %get-tuple-element.28), channel_id=1, source_target_pairs={{0,2},{1,3},{2,0},{3,1},{4,6},{5,7},{6,4},{7,5},{8,10},{9,11},{10,... | collective-permute-start | bytes 983048 | tf_op jit(solution)/shard_map/ppermute | solution.py:37
  117.9 8.9 %collective-permute-start.15 = (bf16[1280,128]{1,0:T(8,128)(2,1)S(1)}, bf16[1280,128]{1,0:T(8,128)(2,1)S(1)}, u32[]{:S(2)}, u32[]{:S(2)}) collective-permute-start(bf16[1280,128]{1,0:T(8,128)(2,1)S(1)} %get-tuple-element.23), channel_id=1, source_target_pairs={{0,2},{1,3},{2,0},{3,1},{4,6},{5,7},{6,4},{7,5},{8,10},{9,11},{10,... | collective-permute-start | bytes 983048 | tf_op jit(solution)/shard_map/ppermute | solution.py:37
  118.3 9.1 %collective-permute-start.18 = (bf16[1280,128]{1,0:T(8,128)(2,1)S(1)}, bf16[1280,128]{1,0:T(8,128)(2,1)S(1)}, u32[]{:S(2)}, u32[]{:S(2)}) collective-permute-start(bf16[1280,128]{1,0:T(8,128)(2,1)S(1)} %fusion.11), channel_id=1, source_target_pairs={{0,4},{1,5},{2,6},{3,7},{12,8},{13,9},{14,10},{15,11},{16,20},{17,... | collective-permute-start | bytes 983048 | tf_op jit(solution)/shard_map/ppermute | solution.py:37
  126.8 8.0 %collective-permute-start.16 = (bf16[1280,128]{1,0:T(8,128)(2,1)S(1)}, bf16[1280,128]{1,0:T(8,128)(2,1)S(1)}, u32[]{:S(2)}, u32[]{:S(2)}) collective-permute-start(bf16[1280,128]{1,0:T(8,128)(2,1)S(1)} %get-tuple-element.24), channel_id=1, source_target_pairs={{0,2},{1,3},{2,0},{3,1},{4,6},{5,7},{6,4},{7,5},{8,10},{9,11},{10,... | collective-permute-start | bytes 983048 | tf_op jit(solution)/shard_map/ppermute | solution.py:37
  127.6 9.2 %collective-permute-start.21 = (bf16[1280,128]{1,0:T(8,128)(2,1)S(1)}, bf16[1280,128]{1,0:T(8,128)(2,1)S(1)}, u32[]{:S(2)}, u32[]{:S(2)}) collective-permute-start(bf16[1280,128]{1,0:T(8,128)(2,1)S(1)} %fusion.1), channel_id=1, source_target_pairs={{0,4},{1,5},{2,6},{3,7},{12,8},{13,9},{14,10},{15,11},{16,20},{17,... | collective-permute-start | bytes 983048 | tf_op jit(solution)/shard_map/ppermute | solution.py:37
  131.0 5.8 %collective-permute-start.19 = (bf16[1280,128]{1,0:T(8,128)(2,1)S(1)}, bf16[1280,128]{1,0:T(8,128)(2,1)S(1)}, u32[]{:S(2)}, u32[]{:S(2)}) collective-permute-start(bf16[1280,128]{1,0:T(8,128)(2,1)S(1)} %fusion.1), channel_id=1, source_target_pairs={{4,8},{5,9},{6,10},{7,11},{8,4},{9,5},{10,6},{11,7},{20,24},{21,25... | collective-permute-start | bytes 983048 | tf_op jit(solution)/shard_map/ppermute | solution.py:37
  134.8 7.6 %collective-permute-start.17 = (bf16[1280,128]{1,0:T(8,128)(2,1)S(1)}, bf16[1280,128]{1,0:T(8,128)(2,1)S(1)}, u32[]{:S(2)}, u32[]{:S(2)}) collective-permute-start(bf16[1280,128]{1,0:T(8,128)(2,1)S(1)} %get-tuple-element.25), channel_id=1, source_target_pairs={{0,2},{1,3},{2,0},{3,1},{4,6},{5,7},{6,4},{7,5},{8,10},{9,11},{10,... | collective-permute-start | bytes 983048 | tf_op jit(solution)/shard_map/ppermute | solution.py:37
  137.1 10.3 %collective-permute-start.20 = (bf16[1280,128]{1,0:T(8,128)(2,1)S(1)}, bf16[1280,128]{1,0:T(8,128)(2,1)S(1)}, u32[]{:S(2)}, u32[]{:S(2)}) collective-permute-start(bf16[1280,128]{1,0:T(8,128)(2,1)S(1)} %get-tuple-element.31), channel_id=1, source_target_pairs={{0,4},{1,5},{2,6},{3,7},{4,0},{5,1},{6,2},{7,3},{8,12},{9,13},{10,... | collective-permute-start | bytes 983048 | tf_op jit(solution)/shard_map/ppermute | solution.py:37
  141.8 5.6 %collective-permute-start.22 = (bf16[1280,128]{1,0:T(8,128)(2,1)S(1)}, bf16[1280,128]{1,0:T(8,128)(2,1)S(1)}, u32[]{:S(2)}, u32[]{:S(2)}) collective-permute-start(bf16[1280,128]{1,0:T(8,128)(2,1)S(1)} %get-tuple-element.32), channel_id=1, source_target_pairs={{4,8},{5,9},{6,10},{7,11},{8,4},{9,5},{10,6},{11,7},{20,24},{21,25... | collective-permute-start | bytes 983048 | tf_op jit(solution)/shard_map/ppermute | solution.py:37

commit v4 on v3

--- a/solution.py
+++ b/solution.py
@@ -45,18 +45,32 @@
 ACROSS = pairs_of(lambda z, x: (z, 1 - x))
 
 
-def spread(own):
-    x_own = move(own, ACROSS)
-    z1 = move(own, NEAR)
-    inner1 = move(own, INNER)
-    x1 = move(after(z1, x_own), ACROSS)
-    inner2 = move(z1, INNER)
-    outward1 = move(inner1, OUTWARD)
-    early = inner1 + outward1
-    x_early = move(after(early, x1), ACROSS)
-    late = inner2 + move(inner2, OUTWARD)
-    x_late = move(after(late, x_early), ACROSS)
-    return [own, z1, early, late, x_own, x1, x_early, x_late]
+class Queue:
+    def __init__(self, pairs):
+        self.pairs = pairs
+        self.done = []
+
+    def move(self, array):
+        if len(self.done) > 1:
+            array = after(array, self.done[-2])
+        self.done.append(move(array, self.pairs))
+        return self.done[-1]
+
+
+def spread(parts):
+    across = Queue(ACROSS)
+    x_own = [across.move(own) for own in parts]
+    z1 = [move(own, NEAR) for own in parts]
+    inner1 = [move(own, INNER) for own in parts]
+    x1 = [across.move(part) for part in z1]
+    outward1 = [move(part, OUTWARD) for part in inner1]
+    inner2 = [move(part, INNER) for part in z1]
+    early = [one + two for one, two in zip(inner1, outward1)]
+    x_early = [across.move(part) for part in early]
+    outward2 = [move(part, OUTWARD) for part in inner2]
+    late = [one + two for one, two in zip(inner2, outward2)]
+    x_late = [across.move(part) for part in late]
+    return [array for part in zip(parts, z1, early, late, x_own, x1, x_early, x_late) for array in part]
 
 
 def collect(keep, send_far, send_near, swap):
@@ -66,13 +80,10 @@
     def narrow(array):
         return array.astype(jnp.bfloat16)
 
+    across = Queue(ACROSS)
     crossed = {}
-    last = None
     for step in (3, 2, 1, 0):
-        part = narrow(keep[LINE + step] + far[step].astype(jnp.float32))
-        if last is not None:
-            part = after(part, last)
-        last = crossed[step] = move(part, ACROSS)
+        crossed[step] = across.move(narrow(keep[LINE + step] + far[step].astype(jnp.float32)))
     held = {
         step: keep[step] + near[step].astype(jnp.float32) + crossed[step].astype(jnp.float32) for step in range(LINE)
     }
@@ -169,16 +180,16 @@
 
     mine = lax.dynamic_slice_in_dim(occupied, core * LANES, LANES, 1)
     given = lax.dynamic_slice_in_dim(occupied, (1 - core) * LANES, LANES, 1)
-    own = jnp.concatenate([mine, lax.ppermute(given, "aux", swap)], axis=0)
+    parts = (mine, move(given, swap))
 
     chips = owners // 2
     slot_ids = jnp.arange(chips, dtype=jnp.int32)
     lined = chips == 2 * LINE
     if lined:
-        held = spread(own)
+        held = spread(parts)
         chip_of_slot = ((slot_ids % LINE) ^ (chip // 2)) * 2 + ((slot_ids // LINE) ^ (chip % 2))
     else:
-        held = [lax.all_gather(own, "aux", axis_index_groups=same_core, axis=0, tiled=True)]
+        held = [lax.all_gather(part, "aux", axis_index_groups=same_core, axis=0, tiled=True) for part in parts]
         chip_of_slot = slot_ids
 
     live = live_counts[0]
@@ -187,7 +198,7 @@
     groups = jnp.full((slots,), (live + UNROLL - 1) // UNROLL, jnp.int32)
     table = jnp.stack([row_starts, block_pairs[:, 1], groups])
     other_table = lax.ppermute(table, "aux", swap)
-    block_values = after(block_values, own)
+    block_values = after(block_values, parts[1])
     tiles = block_values.reshape(slots, BLK, BLK)
     other_values = lax.ppermute(block_values, "aux", swap)
     other_tiles = other_values.reshape(slots, BLK, BLK)
@@ -203,7 +214,7 @@
         apart = (owner_chip // 2) ^ level
         in_middle = ((level == 1) | (level == 2)).astype(jnp.int32)
         slot_of = (apart ^ (apart // 2 * in_middle)) + LINE * ((owner_chip % 2) ^ (chip % 2))
-    spots = (slot_of * (2 * shard) + ((owner % 2) ^ core) * shard + first % shard).reshape(-1)
+    spots = ((((owner % 2) ^ core) * chips + slot_of) * shard + first % shard).reshape(-1)
     meta = jnp.stack([table[2, 0], other_table[2, 0], core]).astype(jnp.int32)
 
     smem = pl.BlockSpec(memory_space=pltpu.SMEM)

time: 150 us -> 152 us (1.013)
  starting transfers between devices: 26.4 us -> 45.1 us
  waiting for transfers between devices: 71.7 us -> 53.7 us
  other arithmetic: 9.04 us -> 10.8 us
  Pallas kernels: 20.4 us -> 18.7 us
    ppermute x20 -> x30, starting transfers between devices: 25.7 us -> 44.7 us  [move(): return lax.ppermute(array, 'aux', pairs)]
    ppermute x20 -> x30, waiting for transfers between devices: 70.4 us -> 53.7 us  [move(): return lax.ppermute(array, 'aux', pairs)]
    add x3 -> x5, other arithmetic: 3.36 us -> 5.09 us  [the longest x2 2.34 us: spread(): early = [one + two for one, two in zip(inner1, outward1)]]
    pallas_call x1, Pallas kernels: 20.4 us -> 18.7 us  [local(): pl.pallas_call(functools.partial(work_kernel, piece, shard), out_shape=(j...]
  transfers between devices with their start and end apart: 23 -> 32, of which waited for: 11 -> 13; matrix products, arithmetic and copies ran while one was open for 18% -> 16% of each run, Pallas kernels for 0% -> 0%
where the time goes in v4:
time: 152 us; the launch traced here: 149 us
  waiting for transfers between devices  53.7 us (35%)
  starting transfers between devices  45.1 us (30%)
  local copies, waits for them, and re-layouts  20 us (13%)
  Pallas kernels  18.7 us (12%)
  other arithmetic  10.8 us (7%)
    ppermute x30, waiting for transfers between devices, move(): return lax.ppermute(array, 'aux', pairs)  53.7 us
    ppermute x30, starting transfers between devices, move(): return lax.ppermute(array, 'aux', pairs)  44.7 us
    pallas_call x1, Pallas kernels, local(): pl.pallas_call(functools.partial(work_kernel, piece, shard), out_shape=(j...  18.7 us
    reshape x1, local copies, waits for them, and re-layouts, local(): other_tiles = other_values.reshape(slots, BLK, BLK)  7.45 us
    reshape x1, local copies, waits for them, and re-layouts, local(): tiles = block_values.reshape(slots, BLK, BLK)  6.67 us
    optimization_barrier x1, local copies, waits for them, and re-layouts, after(): return lax.optimization_barrier((array, *others))[0]  3.38 us
  transfers between devices with their start and end apart: 32, of which 13 were waited for; matrix products, arithmetic and copies ran while one was open for 16% of the time, Pallas kernels for 0%

profile of v4, /device:TPU:0, one launch (start us, length us, event | category | flops | bytes accessed | tf_op | source)
XLA Modules:
  0.0 149.4 jit_solution(7876105629867728521)
XLA Ops:
  0.0 1.1 constant_dynamic-slice_fusion
  1.1 0.5 collective-permute-start.10
  1.7 1.3 collective-permute-done.10.refs_8_
  2.9 3.4 %copy.5 = bf16[256,4096]{0,1:T(8,128)(2,1)S(1)} copy(bf16[256,4096]{1,0:T(8,128)(2,1)} %param.4) | data formatting | bytes 4194304 | tf_op jit(solution)/shard_map/optimization_barrier | solution.py:33
  6.3 0.4 collective-permute-start.20
  6.8 2.6 %collective-permute-start.6 = (bf16[1280,128]{1,0:T(8,128)(2,1)S(1)}, bf16[1280,128]{1,0:T(8,128)(2,1)S(1)}, u32[]{:S(2)}, u32[]{:S(2)}) collective-permute-start(bf16[1280,128]{1,0:T(8,128)(2,1)S(1)} %get-tuple-element.38.refs_0_), channel_id=1, source_target_pairs={{0,2},{1,3},{2,0},{3,1},{4,6},{5,7},{6,4},{7,5},{8,10},{9,11},{10,... | collective-permute-start | bytes 983048 | tf_op jit(solution)/shard_map/ppermute | solution.py:37
  9.4 1.6 %collective-permute-start.1 = (bf16[1280,128]{1,0:T(8,128)(2,1)S(1)}, bf16[1280,128]{1,0:T(8,128)(2,1)S(1)}, u32[]{:S(2)}, u32[]{:S(2)}) collective-permute-start(bf16[1280,128]{1,0:T(8,128)(2,1)S(1)} %get-tuple-element.38.refs_0_), channel_id=1, source_target_pairs={{0,4},{1,5},{2,6},{3,7},{4,0},{5,1},{6,2},{7,3},{8,12},{9,13},{10,... | collective-permute-start | bytes 983048 | tf_op jit(solution)/shard_map/ppermute | solution.py:37
  11.0 1.4 collective-permute-start.2
  12.3 0.5 collective-permute-start.16
  12.9 5.1 %collective-permute-done.6.refs_4_ = bf16[1280,128]{1,0:T(8,128)(2,1)S(1)} collective-permute-done((bf16[1280,128]{1,0:T(8,128)(2,1)S(1)}, bf16[1280,128]{1,0:T(8,128)(2,1)S(1)}, u32[]{:S(2)}, u32[]{:S(2)}) %collective-permute-start.6) | collective-permute-done | bytes 327712 | tf_op jit(solution)/shard_map/ppermute | solution.py:37
  17.9 1.4 collective-permute-start.12
  19.3 2.0 %collective-permute-start.7 = (bf16[1280,128]{1,0:T(8,128)(2,1)S(1)}, bf16[1280,128]{1,0:T(8,128)(2,1)S(1)}, u32[]{:S(2)}, u32[]{:S(2)}) collective-permute-start(bf16[1280,128]{1,0:T(8,128)(2,1)S(1)} %collective-permute-done.1.refs_1_), channel_id=1, source_target_pairs={{0,2},{1,3},{2,0},{3,1},{4,6},{5,7},{6,4},{7,5},{8,10},{9,11},{10,... | collective-permute-start | bytes 983048 | tf_op jit(solution)/shard_map/ppermute | solution.py:37
  21.3 3.8 %collective-permute-start.11 = (bf16[1280,128]{1,0:T(8,128)(2,1)S(1)}, bf16[1280,128]{1,0:T(8,128)(2,1)}, u32[]{:S(2)}, u32[]{:S(2)}) collective-permute-start(bf16[1280,128]{1,0:T(8,128)(2,1)S(1)} %collective-permute-done.10.refs_8_), channel_id=1, source_target_pairs={{0,4},{1,5},{2,6},{3,7},{4,0},{5,1},{6,2},{7,3},{8,12},{9,13},{10,... | collective-permute-start | bytes 983048 | tf_op jit(solution)/shard_map/ppermute | solution.py:37
  25.1 0.7 copy-done.9
  25.8 1.3 collective-permute-start.3
  27.8 1.3 collective-permute-start.13
  29.1 0.1 pad.9.clone
  29.2 4.0 %collective-permute-done.11.refs_9_ = bf16[1280,128]{1,0:T(8,128)(2,1)} collective-permute-done((bf16[1280,128]{1,0:T(8,128)(2,1)S(1)}, bf16[1280,128]{1,0:T(8,128)(2,1)}, u32[]{:S(2)}, u32[]{:S(2)}) %collective-permute-start.11) | collective-permute-done | bytes 327712 | tf_op jit(solution)/shard_map/ppermute | solution.py:37
  33.2 1.4 collective-permute-start.4
  34.6 5.5 %collective-permute-done.3 = bf16[1280,128]{1,0:T(8,128)(2,1)S(1)} collective-permute-done((bf16[1280,128]{1,0:T(8,128)(2,1)}, bf16[1280,128]{1,0:T(8,128)(2,1)S(1)}, u32[]{:S(2)}, u32[]{:S(2)}) %collective-permute-start.3) | collective-permute-done | bytes 327712 | tf_op jit(solution)/shard_map/ppermute | solution.py:37
  40.1 0.3 collective-permute-start.17
  40.4 1.4 collective-permute-start.14
  41.8 0.1 add_add_fusion
  41.9 3.8 %collective-permute-done.13 = bf16[1280,128]{1,0:T(8,128)(2,1)} collective-permute-done((bf16[1280,128]{1,0:T(8,128)(2,1)}, bf16[1280,128]{1,0:T(8,128)(2,1)}, u32[]{:S(2)}, u32[]{:S(2)}) %collective-permute-start.13) | collective-permute-done | bytes 327712 | tf_op jit(solution)/shard_map/ppermute | solution.py:37
  45.6 0.6 fusion.30.chips_ref
  46.2 1.1 add.178.refs_2_
  47.3 1.3 add.181.refs_10_
  48.6 0.6 collective-permute-start.8
  49.2 1.3 collective-permute-start.5
  50.5 1.6 %collective-permute-start.18 = (bf16[1280,128]{1,0:T(8,128)(2,1)S(1)}, bf16[1280,128]{1,0:T(8,128)(2,1)S(1)}, u32[]{:S(2)}, u32[]{:S(2)}) collective-permute-start(bf16[1280,128]{1,0:T(8,128)(2,1)S(1)} %add.181.refs_10_), channel_id=1, source_target_pairs={{0,2},{1,3},{2,0},{3,1},{4,6},{5,7},{6,4},{7,5},{8,10},{9,11},{10,... | collective-permute-start | bytes 983048 | tf_op jit(solution)/shard_map/ppermute | solution.py:37
  52.1 1.3 collective-permute-start.15
  53.4 0.6 slice.87
  53.9 1.2 pad_add_fusion.1.meta_ref
  55.2 6.7 %collective-permute-done.5 = bf16[1280,128]{1,0:T(8,128)(2,1)S(1)} collective-permute-done((bf16[1280,128]{1,0:T(8,128)(2,1)}, bf16[1280,128]{1,0:T(8,128)(2,1)S(1)}, u32[]{:S(2)}, u32[]{:S(2)}) %collective-permute-start.5) | collective-permute-done | bytes 327712 | tf_op jit(solution)/shard_map/ppermute | solution.py:37
  61.8 1.1 add.179.refs_3_
  62.9 1.6 %collective-permute-start.9 = (bf16[1280,128]{1,0:T(8,128)(2,1)S(1)}, bf16[1280,128]{1,0:T(8,128)(2,1)}, u32[]{:S(2)}, u32[]{:S(2)}) collective-permute-start(bf16[1280,128]{1,0:T(8,128)(2,1)S(1)} %add.179.refs_3_), channel_id=1, source_target_pairs={{0,2},{1,3},{2,0},{3,1},{4,6},{5,7},{6,4},{7,5},{8,10},{9,11},{10,... | collective-permute-start | bytes 983048 | tf_op jit(solution)/shard_map/ppermute | solution.py:37
  64.5 3.7 %collective-permute-done.15 = bf16[1280,128]{1,0:T(8,128)(2,1)S(1)} collective-permute-done((bf16[1280,128]{1,0:T(8,128)(2,1)}, bf16[1280,128]{1,0:T(8,128)(2,1)S(1)}, u32[]{:S(2)}, u32[]{:S(2)}) %collective-permute-start.15) | collective-permute-done | bytes 327712 | tf_op jit(solution)/shard_map/ppermute | solution.py:37
  68.2 1.1 add.182.refs_11_
  69.3 1.6 %collective-permute-start.19 = (bf16[1280,128]{1,0:T(8,128)(2,1)S(1)}, bf16[1280,128]{1,0:T(8,128)(2,1)}, u32[]{:S(2)}, u32[]{:S(2)}) collective-permute-start(bf16[1280,128]{1,0:T(8,128)(2,1)S(1)} %add.182.refs_11_), channel_id=1, source_target_pairs={{0,2},{1,3},{2,0},{3,1},{4,6},{5,7},{6,4},{7,5},{8,10},{9,11},{10,... | collective-permute-start | bytes 983048 | tf_op jit(solution)/shard_map/ppermute | solution.py:37
  70.8 0.6 fusion.16
  71.5 6.7 %copy.7.refs_16_ = bf16[256,64,64]{2,1,0:T(8,128)(2,1)} copy(bf16[256,64,64]{0,2,1:T(8,128)(2,1)S(1)} %bitcast.52) | data formatting | bytes 4194304 | tf_op jit(solution)/shard_map/reshape | solution.py:202
  78.2 7.4 %copy.8.refs_17_ = bf16[256,64,64]{2,1,0:T(8,128)(2,1)} copy(bf16[256,64,64]{0,2,1:T(8,128)(2,1)} %bitcast.11) | data formatting | bytes 4194304 | tf_op jit(solution)/shard_map/reshape | solution.py:204
  85.6 18.7 %shard_map.46 = (f32[8,1280,128]{2,1,0:T(8,128)}, bf16[4,1280,128]{2,1,0:T(8,128)(2,1)}, bf16[4,1280,128]{2,1,0:T(8,128)(2,1)}) custom-call(s32[8]{0:T(128)} %fusion.30.chips_ref, s32[512]{0:T(512)} %get-tuple-element.45.rows_ref, s32[512]{0:T(512)} %get-tuple-element.44.spots_ref, s32[3]{0:T(128)} %pad_add_fusion.1.meta_ref, bf16[1280,128]{1,0:T(8,128)(2,1)} %copy-done.1, ...), custom_call_target="tpu_custom_call" | custom-call | flops 2013265920 | bytes 26214400 | tf_op jit(solution)/shard_map/pallas_call | solution.py:223
  104.4 0.5 collective-permute-start.21
  104.9 2.7 %collective-permute-done.22 = bf16[4,1280,128]{2,1,0:T(8,128)(2,1)S(1)} collective-permute-done((bf16[4,1280,128]{2,1,0:T(8,128)(2,1)}, bf16[4,1280,128]{2,1,0:T(8,128)(2,1)S(1)}, u32[]{:S(2)}, u32[]{:S(2)}) %collective-permute-start.22) | collective-permute-done | bytes 1310752 | tf_op jit(solution)/shard_map/ppermute | solution.py:37
  107.6 2.1 %fusion.7 = (bf16[1280,128]{1,0:T(8,128)(2,1)S(1)}, bf16[1280,128]{1,0:T(8,128)(2,1)S(1)}, bf16[1280,128]{1,0:T(8,128)(2,1)S(1)}, bf16[1280,128]{1,0:T(8,128)(2,1)S(1)}) fusion(f32[8,1280,128]{2,1,0:T(8,128)} %get-tuple-element.25, bf16[4,1280,128]{2,1,0:T(8,128)(2,1)S(1)} %collective-permute-done.22), kind=kLoop, calls=%fused_computation.16 | loop fusion | flops 1966080 | bytes 5242880 | tf_op jit(solution)/shard_map/convert_element_type | solution.py:81
  109.8 3.0 %collective-permute-start.25 = (bf16[1280,128]{1,0:T(8,128)(2,1)S(1)}, bf16[1280,128]{1,0:T(8,128)(2,1)S(1)}, u32[]{:S(2)}, u32[]{:S(2)}) collective-permute-start(bf16[1280,128]{1,0:T(8,128)(2,1)S(1)} %get-tuple-element.32), channel_id=1, source_target_pairs={{0,2},{1,3},{2,0},{3,1},{4,6},{5,7},{6,4},{7,5},{8,10},{9,11},{10,... | collective-permute-start | bytes 983048 | tf_op jit(solution)/shard_map/ppermute | solution.py:37
  112.7 0.1 collective-permute-start.23
  112.8 8.4 %collective-permute-done.25 = bf16[1280,128]{1,0:T(8,128)(2,1)S(1)} collective-permute-done((bf16[1280,128]{1,0:T(8,128)(2,1)S(1)}, bf16[1280,128]{1,0:T(8,128)(2,1)S(1)}, u32[]{:S(2)}, u32[]{:S(2)}) %collective-permute-start.25) | collective-permute-done | bytes 327712 | tf_op jit(solution)/shard_map/ppermute | solution.py:37
  121.2 0.1 fusion.11
  121.3 2.9 %collective-permute-start.27 = (bf16[1280,128]{1,0:T(8,128)(2,1)S(1)}, bf16[1280,128]{1,0:T(8,128)(2,1)S(1)}, u32[]{:S(2)}, u32[]{:S(2)}) collective-permute-start(bf16[1280,128]{1,0:T(8,128)(2,1)S(1)} %fusion.11), channel_id=1, source_target_pairs={{0,4},{1,5},{2,6},{3,7},{12,8},{13,9},{14,10},{15,11},{16,20},{17,... | collective-permute-start | bytes 983048 | tf_op jit(solution)/shard_map/ppermute | solution.py:37
  124.2 0.5 collective-permute-start.26
  124.8 3.5 %collective-permute-done.23 = bf16[1280,128]{1,0:T(8,128)(2,1)S(1)} collective-permute-done((bf16[1280,128]{1,0:T(8,128)(2,1)S(1)}, bf16[1280,128]{1,0:T(8,128)(2,1)S(1)}, u32[]{:S(2)}, u32[]{:S(2)}) %collective-permute-start.23) | collective-permute-done | bytes 327712 | tf_op jit(solution)/shard_map/ppermute | solution.py:37
  128.2 1.6 %collective-permute-done.27 = bf16[1280,128]{1,0:T(8,128)(2,1)S(1)} collective-permute-done((bf16[1280,128]{1,0:T(8,128)(2,1)S(1)}, bf16[1280,128]{1,0:T(8,128)(2,1)S(1)}, u32[]{:S(2)}, u32[]{:S(2)}) %collective-permute-start.27) | collective-permute-done | bytes 327712 | tf_op jit(solution)/shard_map/ppermute | solution.py:37
  129.8 0.2 fusion.1
  130.0 4.4 %collective-permute-start.30 = (bf16[1280,128]{1,0:T(8,128)(2,1)S(1)}, bf16[1280,128]{1,0:T(8,128)(2,1)S(1)}, u32[]{:S(2)}, u32[]{:S(2)}) collective-permute-start(bf16[1280,128]{1,0:T(8,128)(2,1)S(1)} %fusion.1), channel_id=1, source_target_pairs={{0,4},{1,5},{2,6},{3,7},{12,8},{13,9},{14,10},{15,11},{16,20},{17,... | collective-permute-start | bytes 983048 | tf_op jit(solution)/shard_map/ppermute | solution.py:37
  134.4 0.7 collective-permute-start.28
  135.1 0.8 collective-permute-start.24
  135.9 3.2 %collective-permute-done.30 = bf16[1280,128]{1,0:T(8,128)(2,1)S(1)} collective-permute-done((bf16[1280,128]{1,0:T(8,128)(2,1)S(1)}, bf16[1280,128]{1,0:T(8,128)(2,1)S(1)}, u32[]{:S(2)}, u32[]{:S(2)}) %collective-permute-start.30) | collective-permute-done | bytes 327712 | tf_op jit(solution)/shard_map/ppermute | solution.py:37
  139.1 0.3 fusion.3
  139.4 3.8 %collective-permute-start.29 = (bf16[1280,128]{1,0:T(8,128)(2,1)S(1)}, bf16[1280,128]{1,0:T(8,128)(2,1)S(1)}, u32[]{:S(2)}, u32[]{:S(2)}) collective-permute-start(bf16[1280,128]{1,0:T(8,128)(2,1)S(1)} %get-tuple-element.35), channel_id=1, source_target_pairs={{0,4},{1,5},{2,6},{3,7},{4,0},{5,1},{6,2},{7,3},{8,12},{9,13},{10,... | collective-permute-start | bytes 983048 | tf_op jit(solution)/shard_map/ppermute | solution.py:37
  143.3 0.7 collective-permute-start.31
  144.0 4.4 %collective-permute-done.29 = bf16[1280,128]{1,0:T(8,128)(2,1)S(1)} collective-permute-done((bf16[1280,128]{1,0:T(8,128)(2,1)S(1)}, bf16[1280,128]{1,0:T(8,128)(2,1)S(1)}, u32[]{:S(2)}, u32[]{:S(2)}) %collective-permute-start.29) | collective-permute-done | bytes 327712 | tf_op jit(solution)/shard_map/ppermute | solution.py:37
  148.3 1.0 fusion.6
  (52 shorter events, 0.2 us)
Async XLA Ops:
  1.1 9.8 %copy-start.1 = (bf16[1280,128]{1,0:T(8,128)(2,1)}, bf16[1280,128]{1,0:T(8,128)(2,1)S(1)}, u32[]{:S(2)}) copy-start(bf16[1280,128]{1,0:T(8,128)(2,1)S(1)} %get-tuple-element.38.refs_0_) | copy-start | bytes 983044
  1.1 26.0 %copy-start.13 = (s32[256,2]{0,1:T(2,128)S(1)}, s32[256,2]{0,1:T(2,128)}, u32[]{:S(2)}) copy-start(s32[256,2]{0,1:T(2,128)} %param.5) | copy-start | bytes 6148
  1.1 1.8 %collective-permute-start.10 = (bf16[1280,128]{1,0:T(8,128)(2,1)S(1)}, bf16[1280,128]{1,0:T(8,128)(2,1)S(1)}, u32[]{:S(2)}, u32[]{:S(2)}) collective-permute-start(bf16[1280,128]{1,0:T(8,128)(2,1)S(1)} %get-tuple-element.37), channel_id=1, source_target_pairs={{0,1},{1,0},{2,3},{3,2},{4,5},{5,4},{6,7},{7,6},{8,9},{9,8},{10,11... | collective-permute-start | bytes 983048 | tf_op jit(solution)/shard_map/ppermute | solution.py:37
  2.9 18.4 %copy-start.6 = (bf16[1280,128]{1,0:T(8,128)(2,1)}, bf16[1280,128]{1,0:T(8,128)(2,1)S(1)}, u32[]{:S(2)}) copy-start(bf16[1280,128]{1,0:T(8,128)(2,1)S(1)} %collective-permute-done.10.refs_8_) | copy-start | bytes 983044
  6.3 71.8 %collective-permute-start.20 = (bf16[256,4096]{0,1:T(8,128)(2,1)S(1)}, bf16[256,4096]{0,1:T(8,128)(2,1)}, u32[]{:S(2)}, u32[]{:S(2)}) collective-permute-start(bf16[256,4096]{0,1:T(8,128)(2,1)S(1)} %copy.5), channel_id=1, source_target_pairs={{0,1},{1,0},{2,3},{3,2},{4,5},{5,4},{6,7},{7,6},{8,9},{9,8},{10,11... | collective-permute-start | bytes 6291464 | tf_op jit(solution)/shard_map/ppermute | solution.py:203
  6.8 11.2 %collective-permute-start.6 = (bf16[1280,128]{1,0:T(8,128)(2,1)S(1)}, bf16[1280,128]{1,0:T(8,128)(2,1)S(1)}, u32[]{:S(2)}, u32[]{:S(2)}) collective-permute-start(bf16[1280,128]{1,0:T(8,128)(2,1)S(1)} %get-tuple-element.38.refs_0_), channel_id=1, source_target_pairs={{0,2},{1,3},{2,0},{3,1},{4,6},{5,7},{6,4},{7,5},{8,10},{9,11},{10,... | collective-permute-start | bytes 983048 | tf_op jit(solution)/shard_map/ppermute | solution.py:37
  9.4 9.9 %collective-permute-start.1 = (bf16[1280,128]{1,0:T(8,128)(2,1)S(1)}, bf16[1280,128]{1,0:T(8,128)(2,1)S(1)}, u32[]{:S(2)}, u32[]{:S(2)}) collective-permute-start(bf16[1280,128]{1,0:T(8,128)(2,1)S(1)} %get-tuple-element.38.refs_0_), channel_id=1, source_target_pairs={{0,4},{1,5},{2,6},{3,7},{4,0},{5,1},{6,2},{7,3},{8,12},{9,13},{10,... | collective-permute-start | bytes 983048 | tf_op jit(solution)/shard_map/ppermute | solution.py:37
  11.0 10.3 %collective-permute-start.2 = (bf16[1280,128]{1,0:T(8,128)(2,1)S(1)}, bf16[1280,128]{1,0:T(8,128)(2,1)}, u32[]{:S(2)}, u32[]{:S(2)}) collective-permute-start(bf16[1280,128]{1,0:T(8,128)(2,1)S(1)} %get-tuple-element.38.refs_0_), channel_id=1, source_target_pairs={{4,8},{5,9},{6,10},{7,11},{8,4},{9,5},{10,6},{11,7},{20,24},{21,25... | collective-permute-start | bytes 983048 | tf_op jit(solution)/shard_map/ppermute | solution.py:37
  12.3 12.7 %collective-permute-start.16 = (bf16[1280,128]{1,0:T(8,128)(2,1)S(1)}, bf16[1280,128]{1,0:T(8,128)(2,1)S(1)}, u32[]{:S(2)}, u32[]{:S(2)}) collective-permute-start(bf16[1280,128]{1,0:T(8,128)(2,1)S(1)} %collective-permute-done.10.refs_8_), channel_id=1, source_target_pairs={{0,2},{1,3},{2,0},{3,1},{4,6},{5,7},{6,4},{7,5},{8,10},{9,11},{10,... | collective-permute-start | bytes 983048 | tf_op jit(solution)/shard_map/ppermute | solution.py:37
  17.9 7.1 %copy-start.7 = (bf16[1280,128]{1,0:T(8,128)(2,1)}, bf16[1280,128]{1,0:T(8,128)(2,1)S(1)}, u32[]{:S(2)}) copy-start(bf16[1280,128]{1,0:T(8,128)(2,1)S(1)} %collective-permute-done.6.refs_4_) | copy-start | bytes 983044
  17.9 9.8 %collective-permute-start.12 = (bf16[1280,128]{1,0:T(8,128)(2,1)S(1)}, bf16[1280,128]{1,0:T(8,128)(2,1)}, u32[]{:S(2)}, u32[]{:S(2)}) collective-permute-start(bf16[1280,128]{1,0:T(8,128)(2,1)S(1)} %collective-permute-done.10.refs_8_), channel_id=1, source_target_pairs={{4,8},{5,9},{6,10},{7,11},{8,4},{9,5},{10,6},{11,7},{20,24},{21,25... | collective-permute-start | bytes 983048 | tf_op jit(solution)/shard_map/ppermute | solution.py:37
  19.3 35.8 %copy-start.8 = (bf16[1280,128]{1,0:T(8,128)(2,1)}, bf16[1280,128]{1,0:T(8,128)(2,1)S(1)}, u32[]{:S(2)}) copy-start(bf16[1280,128]{1,0:T(8,128)(2,1)S(1)} %collective-permute-done.1.refs_1_) | copy-start | bytes 983044
  19.3 21.1 %collective-permute-start.7 = (bf16[1280,128]{1,0:T(8,128)(2,1)S(1)}, bf16[1280,128]{1,0:T(8,128)(2,1)S(1)}, u32[]{:S(2)}, u32[]{:S(2)}) collective-permute-start(bf16[1280,128]{1,0:T(8,128)(2,1)S(1)} %collective-permute-done.1.refs_1_), channel_id=1, source_target_pairs={{0,2},{1,3},{2,0},{3,1},{4,6},{5,7},{6,4},{7,5},{8,10},{9,11},{10,... | collective-permute-start | bytes 983048 | tf_op jit(solution)/shard_map/ppermute | solution.py:37
  21.3 11.9 %collective-permute-start.11 = (bf16[1280,128]{1,0:T(8,128)(2,1)S(1)}, bf16[1280,128]{1,0:T(8,128)(2,1)}, u32[]{:S(2)}, u32[]{:S(2)}) collective-permute-start(bf16[1280,128]{1,0:T(8,128)(2,1)S(1)} %collective-permute-done.10.refs_8_), channel_id=1, source_target_pairs={{0,4},{1,5},{2,6},{3,7},{4,0},{5,1},{6,2},{7,3},{8,12},{9,13},{10,... | collective-permute-start | bytes 983048 | tf_op jit(solution)/shard_map/ppermute | solution.py:37
  25.1 0.7 copy-start.9
  25.8 14.3 %collective-permute-start.3 = (bf16[1280,128]{1,0:T(8,128)(2,1)}, bf16[1280,128]{1,0:T(8,128)(2,1)S(1)}, u32[]{:S(2)}, u32[]{:S(2)}) collective-permute-start(bf16[1280,128]{1,0:T(8,128)(2,1)} %collective-permute-done.2), channel_id=1, source_target_pairs={{4,0},{5,1},{6,2},{7,3},{8,12},{9,13},{10,14},{11,15},{20,16},{21,... | collective-permute-start | bytes 983048 | tf_op jit(solution)/shard_map/ppermute | solution.py:37
  27.8 17.9 %collective-permute-start.13 = (bf16[1280,128]{1,0:T(8,128)(2,1)}, bf16[1280,128]{1,0:T(8,128)(2,1)}, u32[]{:S(2)}, u32[]{:S(2)}) collective-permute-start(bf16[1280,128]{1,0:T(8,128)(2,1)} %collective-permute-done.12), channel_id=1, source_target_pairs={{4,0},{5,1},{6,2},{7,3},{8,12},{9,13},{10,14},{11,15},{20,16},{21,... | collective-permute-start | bytes 983048 | tf_op jit(solution)/shard_map/ppermute | solution.py:37
  33.2 15.4 %collective-permute-start.4 = (bf16[1280,128]{1,0:T(8,128)(2,1)S(1)}, bf16[1280,128]{1,0:T(8,128)(2,1)}, u32[]{:S(2)}, u32[]{:S(2)}) collective-permute-start(bf16[1280,128]{1,0:T(8,128)(2,1)S(1)} %collective-permute-done.1.refs_1_), channel_id=1, source_target_pairs={{4,8},{5,9},{6,10},{7,11},{8,4},{9,5},{10,6},{11,7},{20,24},{21,25... | collective-permute-start | bytes 983048 | tf_op jit(solution)/shard_map/ppermute | solution.py:37
  40.1 9.1 %collective-permute-start.17 = (bf16[1280,128]{1,0:T(8,128)(2,1)}, bf16[1280,128]{1,0:T(8,128)(2,1)}, u32[]{:S(2)}, u32[]{:S(2)}) collective-permute-start(bf16[1280,128]{1,0:T(8,128)(2,1)} %collective-permute-done.11.refs_9_), channel_id=1, source_target_pairs={{0,2},{1,3},{2,0},{3,1},{4,6},{5,7},{6,4},{7,5},{8,10},{9,11},{10,... | collective-permute-start | bytes 983048 | tf_op jit(solution)/shard_map/ppermute | solution.py:37
  40.4 24.1 %copy-start.10 = (bf16[1280,128]{1,0:T(8,128)(2,1)}, bf16[1280,128]{1,0:T(8,128)(2,1)S(1)}, u32[]{:S(2)}) copy-start(bf16[1280,128]{1,0:T(8,128)(2,1)S(1)} %collective-permute-done.7.refs_5_) | copy-start | bytes 983044
  40.4 11.7 %collective-permute-start.14 = (bf16[1280,128]{1,0:T(8,128)(2,1)}, bf16[1280,128]{1,0:T(8,128)(2,1)}, u32[]{:S(2)}, u32[]{:S(2)}) collective-permute-start(bf16[1280,128]{1,0:T(8,128)(2,1)} %collective-permute-done.11.refs_9_), channel_id=1, source_target_pairs={{4,8},{5,9},{6,10},{7,11},{8,4},{9,5},{10,6},{11,7},{20,24},{21,25... | collective-permute-start | bytes 983048 | tf_op jit(solution)/shard_map/ppermute | solution.py:37
  45.6 4.9 %collective-permute-start = (s32[3,256]{1,0:T(4,128)S(1)}, s32[3,256]{1,0:T(4,128)S(1)}, u32[]{:S(2)}, u32[]{:S(2)}) collective-permute-start(s32[3,256]{1,0:T(4,128)S(1)} %add_add_fusion), channel_id=1, source_target_pairs={{0,1},{1,0},{2,3},{3,2},{4,5},{5,4},{6,7},{7,6},{8,9},{9,8},{10,11... | collective-permute-start | bytes 9224 | tf_op jit(solution)/shard_map/ppermute | solution.py:200
  47.3 30.8 %copy-start.2 = (bf16[1280,128]{1,0:T(8,128)(2,1)}, bf16[1280,128]{1,0:T(8,128)(2,1)S(1)}, u32[]{:S(2)}) copy-start(bf16[1280,128]{1,0:T(8,128)(2,1)S(1)} %add.178.refs_2_) | copy-start | bytes 983044
  48.6 29.5 %copy-start.3 = (bf16[1280,128]{1,0:T(8,128)(2,1)}, bf16[1280,128]{1,0:T(8,128)(2,1)S(1)}, u32[]{:S(2)}) copy-start(bf16[1280,128]{1,0:T(8,128)(2,1)S(1)} %add.181.refs_10_) | copy-start | bytes 983044
  48.6 14.3 %collective-permute-start.8 = (bf16[1280,128]{1,0:T(8,128)(2,1)S(1)}, bf16[1280,128]{1,0:T(8,128)(2,1)S(1)}, u32[]{:S(2)}, u32[]{:S(2)}) collective-permute-start(bf16[1280,128]{1,0:T(8,128)(2,1)S(1)} %add.178.refs_2_), channel_id=1, source_target_pairs={{0,2},{1,3},{2,0},{3,1},{4,6},{5,7},{6,4},{7,5},{8,10},{9,11},{10,... | collective-permute-start | bytes 983048 | tf_op jit(solution)/shard_map/ppermute | solution.py:37
  49.2 12.6 %collective-permute-start.5 = (bf16[1280,128]{1,0:T(8,128)(2,1)}, bf16[1280,128]{1,0:T(8,128)(2,1)S(1)}, u32[]{:S(2)}, u32[]{:S(2)}) collective-permute-start(bf16[1280,128]{1,0:T(8,128)(2,1)} %collective-permute-done.4), channel_id=1, source_target_pairs={{4,0},{5,1},{6,2},{7,3},{8,12},{9,13},{10,14},{11,15},{20,16},{21,... | collective-permute-start | bytes 983048 | tf_op jit(solution)/shard_map/ppermute | solution.py:37
  50.5 18.7 %collective-permute-start.18 = (bf16[1280,128]{1,0:T(8,128)(2,1)S(1)}, bf16[1280,128]{1,0:T(8,128)(2,1)S(1)}, u32[]{:S(2)}, u32[]{:S(2)}) collective-permute-start(bf16[1280,128]{1,0:T(8,128)(2,1)S(1)} %add.181.refs_10_), channel_id=1, source_target_pairs={{0,2},{1,3},{2,0},{3,1},{4,6},{5,7},{6,4},{7,5},{8,10},{9,11},{10,... | collective-permute-start | bytes 983048 | tf_op jit(solution)/shard_map/ppermute | solution.py:37
  52.1 16.1 %collective-permute-start.15 = (bf16[1280,128]{1,0:T(8,128)(2,1)}, bf16[1280,128]{1,0:T(8,128)(2,1)S(1)}, u32[]{:S(2)}, u32[]{:S(2)}) collective-permute-start(bf16[1280,128]{1,0:T(8,128)(2,1)} %collective-permute-done.14), channel_id=1, source_target_pairs={{4,0},{5,1},{6,2},{7,3},{8,12},{9,13},{10,14},{11,15},{20,16},{21,... | collective-permute-start | bytes 983048 | tf_op jit(solution)/shard_map/ppermute | solution.py:37
  62.9 15.2 %copy-start.4 = (bf16[1280,128]{1,0:T(8,128)(2,1)}, bf16[1280,128]{1,0:T(8,128)(2,1)S(1)}, u32[]{:S(2)}) copy-start(bf16[1280,128]{1,0:T(8,128)(2,1)S(1)} %add.179.refs_3_) | copy-start | bytes 983044
  62.9 6.3 %copy-start.11 = (bf16[1280,128]{1,0:T(8,128)(2,1)}, bf16[1280,128]{1,0:T(8,128)(2,1)S(1)}, u32[]{:S(2)}) copy-start(bf16[1280,128]{1,0:T(8,128)(2,1)S(1)} %collective-permute-done.8.refs_6_) | copy-start | bytes 983044
  62.9 22.7 %collective-permute-start.9 = (bf16[1280,128]{1,0:T(8,128)(2,1)S(1)}, bf16[1280,128]{1,0:T(8,128)(2,1)}, u32[]{:S(2)}, u32[]{:S(2)}) collective-permute-start(bf16[1280,128]{1,0:T(8,128)(2,1)S(1)} %add.179.refs_3_), channel_id=1, source_target_pairs={{0,2},{1,3},{2,0},{3,1},{4,6},{5,7},{6,4},{7,5},{8,10},{9,11},{10,... | collective-permute-start | bytes 983048 | tf_op jit(solution)/shard_map/ppermute | solution.py:37
  69.2 8.9 %copy-start.5 = (bf16[1280,128]{1,0:T(8,128)(2,1)}, bf16[1280,128]{1,0:T(8,128)(2,1)S(1)}, u32[]{:S(2)}) copy-start(bf16[1280,128]{1,0:T(8,128)(2,1)S(1)} %add.182.refs_11_) | copy-start | bytes 983044
  69.3 1.6 %copy-start.12 = (bf16[1280,128]{1,0:T(8,128)(2,1)}, bf16[1280,128]{1,0:T(8,128)(2,1)S(1)}, u32[]{:S(2)}) copy-start(bf16[1280,128]{1,0:T(8,128)(2,1)S(1)} %collective-permute-done.18.refs_14_) | copy-start | bytes 983044
  69.3 16.3 %collective-permute-start.19 = (bf16[1280,128]{1,0:T(8,128)(2,1)S(1)}, bf16[1280,128]{1,0:T(8,128)(2,1)}, u32[]{:S(2)}, u32[]{:S(2)}) collective-permute-start(bf16[1280,128]{1,0:T(8,128)(2,1)S(1)} %add.182.refs_11_), channel_id=1, source_target_pairs={{0,2},{1,3},{2,0},{3,1},{4,6},{5,7},{6,4},{7,5},{8,10},{9,11},{10,... | collective-permute-start | bytes 983048 | tf_op jit(solution)/shard_map/ppermute | solution.py:37
  104.3 3.3 %collective-permute-start.22 = (bf16[4,1280,128]{2,1,0:T(8,128)(2,1)}, bf16[4,1280,128]{2,1,0:T(8,128)(2,1)S(1)}, u32[]{:S(2)}, u32[]{:S(2)}) collective-permute-start(bf16[4,1280,128]{2,1,0:T(8,128)(2,1)} %get-tuple-element.27), channel_id=1, source_target_pairs={{0,1},{1,0},{2,3},{3,2},{4,5},{5,4},{6,7},{7,6},{8,9},{9,8},{10,11... | collective-permute-start | bytes 3932168 | tf_op jit(solution)/shard_map/ppermute | solution.py:37
  104.4 8.4 %collective-permute-start.21 = (bf16[4,1280,128]{2,1,0:T(8,128)(2,1)}, bf16[4,1280,128]{2,1,0:T(8,128)(2,1)S(1)}, u32[]{:S(2)}, u32[]{:S(2)}) collective-permute-start(bf16[4,1280,128]{2,1,0:T(8,128)(2,1)} %get-tuple-element.26), channel_id=1, source_target_pairs={{0,1},{1,0},{2,3},{3,2},{4,5},{5,4},{6,7},{7,6},{8,9},{9,8},{10,11... | collective-permute-start | bytes 3932168 | tf_op jit(solution)/shard_map/ppermute | solution.py:37
  107.6 13.6 %copy-start = (f32[8,1280,128]{2,1,0:T(8,128)S(1)}, f32[8,1280,128]{2,1,0:T(8,128)}, u32[]{:S(2)}) copy-start(f32[8,1280,128]{2,1,0:T(8,128)} %get-tuple-element.25) | copy-start | bytes 15728644
  109.8 11.4 %collective-permute-start.25 = (bf16[1280,128]{1,0:T(8,128)(2,1)S(1)}, bf16[1280,128]{1,0:T(8,128)(2,1)S(1)}, u32[]{:S(2)}, u32[]{:S(2)}) collective-permute-start(bf16[1280,128]{1,0:T(8,128)(2,1)S(1)} %get-tuple-element.32), channel_id=1, source_target_pairs={{0,2},{1,3},{2,0},{3,1},{4,6},{5,7},{6,4},{7,5},{8,10},{9,11},{10,... | collective-permute-start | bytes 983048 | tf_op jit(solution)/shard_map/ppermute | solution.py:37
  112.7 15.5 %collective-permute-start.23 = (bf16[1280,128]{1,0:T(8,128)(2,1)S(1)}, bf16[1280,128]{1,0:T(8,128)(2,1)S(1)}, u32[]{:S(2)}, u32[]{:S(2)}) collective-permute-start(bf16[1280,128]{1,0:T(8,128)(2,1)S(1)} %get-tuple-element.34), channel_id=1, source_target_pairs={{0,2},{1,3},{2,0},{3,1},{4,6},{5,7},{6,4},{7,5},{8,10},{9,11},{10,... | collective-permute-start | bytes 983048 | tf_op jit(solution)/shard_map/ppermute | solution.py:37
  121.3 8.5 %collective-permute-start.27 = (bf16[1280,128]{1,0:T(8,128)(2,1)S(1)}, bf16[1280,128]{1,0:T(8,128)(2,1)S(1)}, u32[]{:S(2)}, u32[]{:S(2)}) collective-permute-start(bf16[1280,128]{1,0:T(8,128)(2,1)S(1)} %fusion.11), channel_id=1, source_target_pairs={{0,4},{1,5},{2,6},{3,7},{12,8},{13,9},{14,10},{15,11},{16,20},{17,... | collective-permute-start | bytes 983048 | tf_op jit(solution)/shard_map/ppermute | solution.py:37
  124.2 11.7 %collective-permute-start.26 = (bf16[1280,128]{1,0:T(8,128)(2,1)S(1)}, bf16[1280,128]{1,0:T(8,128)(2,1)S(1)}, u32[]{:S(2)}, u32[]{:S(2)}) collective-permute-start(bf16[1280,128]{1,0:T(8,128)(2,1)S(1)} %get-tuple-element.29), channel_id=1, source_target_pairs={{0,2},{1,3},{2,0},{3,1},{4,6},{5,7},{6,4},{7,5},{8,10},{9,11},{10,... | collective-permute-start | bytes 983048 | tf_op jit(solution)/shard_map/ppermute | solution.py:37
  130.0 9.1 %collective-permute-start.30 = (bf16[1280,128]{1,0:T(8,128)(2,1)S(1)}, bf16[1280,128]{1,0:T(8,128)(2,1)S(1)}, u32[]{:S(2)}, u32[]{:S(2)}) collective-permute-start(bf16[1280,128]{1,0:T(8,128)(2,1)S(1)} %fusion.1), channel_id=1, source_target_pairs={{0,4},{1,5},{2,6},{3,7},{12,8},{13,9},{14,10},{15,11},{16,20},{17,... | collective-permute-start | bytes 983048 | tf_op jit(solution)/shard_map/ppermute | solution.py:37
  134.4 4.7 %collective-permute-start.28 = (bf16[1280,128]{1,0:T(8,128)(2,1)S(1)}, bf16[1280,128]{1,0:T(8,128)(2,1)S(1)}, u32[]{:S(2)}, u32[]{:S(2)}) collective-permute-start(bf16[1280,128]{1,0:T(8,128)(2,1)S(1)} %fusion.1), channel_id=1, source_target_pairs={{4,8},{5,9},{6,10},{7,11},{8,4},{9,5},{10,6},{11,7},{20,24},{21,25... | collective-permute-start | bytes 983048 | tf_op jit(solution)/shard_map/ppermute | solution.py:37
  135.1 8.9 %collective-permute-start.24 = (bf16[1280,128]{1,0:T(8,128)(2,1)S(1)}, bf16[1280,128]{1,0:T(8,128)(2,1)S(1)}, u32[]{:S(2)}, u32[]{:S(2)}) collective-permute-start(bf16[1280,128]{1,0:T(8,128)(2,1)S(1)} %get-tuple-element.28), channel_id=1, source_target_pairs={{0,2},{1,3},{2,0},{3,1},{4,6},{5,7},{6,4},{7,5},{8,10},{9,11},{10,... | collective-permute-start | bytes 983048 | tf_op jit(solution)/shard_map/ppermute | solution.py:37
  139.4 8.9 %collective-permute-start.29 = (bf16[1280,128]{1,0:T(8,128)(2,1)S(1)}, bf16[1280,128]{1,0:T(8,128)(2,1)S(1)}, u32[]{:S(2)}, u32[]{:S(2)}) collective-permute-start(bf16[1280,128]{1,0:T(8,128)(2,1)S(1)} %get-tuple-element.35), channel_id=1, source_target_pairs={{0,4},{1,5},{2,6},{3,7},{4,0},{5,1},{6,2},{7,3},{8,12},{9,13},{10,... | collective-permute-start | bytes 983048 | tf_op jit(solution)/shard_map/ppermute | solution.py:37
  143.3 5.1 %collective-permute-start.31 = (bf16[1280,128]{1,0:T(8,128)(2,1)S(1)}, bf16[1280,128]{1,0:T(8,128)(2,1)S(1)}, u32[]{:S(2)}, u32[]{:S(2)}) collective-permute-start(bf16[1280,128]{1,0:T(8,128)(2,1)S(1)} %get-tuple-element.36), channel_id=1, source_target_pairs={{4,8},{5,9},{6,10},{7,11},{8,4},{9,5},{10,6},{11,7},{20,24},{21,25... | collective-permute-start | bytes 983048 | tf_op jit(solution)/shard_map/ppermute | solution.py:37

commit v5 on v3

v5 whole, which is shorter than its diff:
```python
import functools
import math

import jax
import jax.numpy as jnp
from jax import lax
from jax.experimental import pallas as pl
from jax.experimental.pallas import tpu as pltpu
from jax.sharding import PartitionSpec as P

BLK = 64
WIN = 128
LANES = 128
UNROLL = 8
VMEM_BYTES = 60 * 1024 * 1024
LINE = 4


def place(z, x, core):
    return (z * 2 + x) * 2 + core


def pairs_of(step):
    return [
        (place(z, x, core), place(*step(z, x), core)) for z in range(LINE) for x in range(2) for core in range(2)
    ]


def tie(*arrays):
    return lax.optimization_barrier(arrays)


def move(array, pairs):
    return lax.ppermute(array, "aux", pairs)


ALONG = pairs_of(lambda z, x: ((z + 1) % LINE, x))
ACROSS = pairs_of(lambda z, x: (z, 1 - x))


def spread(parts):
    lines, others = [[part] for part in parts], [[] for _ in parts]
    for step in range(LINE):
        for line, other in zip(lines, others):
            if other:
                line[-1], other[-1] = tie(line[-1], other[-1])
            now = line[-1]
            if step + 1 < LINE:
                line.append(move(now, ALONG))
            other.append(move(now, ACROSS))
    return [array for line, other in zip(lines, others) for array in line + other]


def collect(keep, send, swap):
    order = [LINE + 3, LINE + 2, 3, LINE + 1, 2, LINE, 1, 0]
    paired = {}
    for slot in order:
        paired[slot] = keep[slot] + move(send[slot], swap).astype(jnp.float32)
    crossed = []
    for step in (3, 2, 1, 0):
        part = paired[LINE + step].astype(jnp.bfloat16)
        if len(crossed) > 1:
            part, crossed[-2] = tie(part, crossed[-2])
        crossed.append(move(part, ACROSS))
    total = paired[3] + crossed[0].astype(jnp.float32)
    for step in (2, 1, 0):
        arrived = move(total.astype(jnp.bfloat16), ALONG)
        total = paired[step] + crossed[3 - step].astype(jnp.float32) + arrived.astype(jnp.float32)
    return total


def work_kernel(counts, piece, shard, chips_ref, rows_ref, spots_ref, meta_ref, *refs):
    occ, tiles, half, weights, keep_buf, send_buf, sem = refs[-7:]
    count, outs = counts
    sources = refs[:count]
    values, other_values = refs[count : count + 2]
    keep, send = refs[count + 2 : count + 2 + outs], refs[count + 2 + outs : count + 2 + 2 * outs]
    core = meta_ref[2]
    slot_rows = occ.shape[0] // count
    for index in range(count):
        pltpu.make_async_copy(sources[index], occ.at[pl.ds(index * slot_rows, slot_rows)], sem.at[0]).start()
    loads = [
        pltpu.make_async_copy(values, tiles.at[0], sem.at[1]),
        pltpu.make_async_copy(other_values, tiles.at[1], sem.at[2]),
    ]
    for load in loads:
        load.start()

    @pl.loop(0, half.shape[1] // BLK)
    def _(index):
        span = pl.ds(pl.multiple_of(index * BLK, BLK), BLK)
        for side in range(2):
            half[side, span, :] = jnp.zeros((BLK, LANES), jnp.float32)

    pltpu.make_async_copy(occ, occ, sem.at[0]).wait()
    slots = tiles.shape[1]
    pieces = BLK // piece
    low = lax.broadcasted_iota(jnp.int32, tiles.shape[2:], 1) < BLK
    zero = jnp.zeros(tiles.shape[2:], jnp.bfloat16)

    for side in range(2):
        loads[side].wait()

        @pl.loop(0, meta_ref[side])
        def _(group):
            products = []
            for lane in range(UNROLL):
                slot = group * UNROLL + lane
                table = side * slots + slot
                parts = [
                    occ[pl.ds(pl.multiple_of(spots_ref[table * pieces + cut], piece), piece), :]
                    for cut in range(pieces)
                ]
                pair = tiles[side, slot]
                rows = jnp.concatenate([jnp.where(low, pair, zero), jnp.where(low, zero, pair)], axis=0)
                block = jnp.concatenate(parts * 2, axis=0)
                products.append(jnp.dot(rows, block, preferred_element_type=jnp.float32))
            for lane in range(UNROLL):
                start = pl.multiple_of(rows_ref[side * slots + group * UNROLL + lane], BLK)
                for odd in range(2):
                    span = pl.ds(start + odd, BLK // 2, stride=2)
                    half[side, span, :] += products[lane][odd * (BLK // 2) : (odd + 1) * (BLK // 2)]

        weights[pl.ds(side * LANES, LANES), :] = half[side, pl.ds(0, WIN), :].T.astype(jnp.bfloat16)

    def rows_of(owner):
        span = pl.ds(pl.multiple_of(owner * shard, 32), shard)
        both = jnp.concatenate([half[side, span, :].astype(jnp.bfloat16) for side in range(2)], axis=1)
        return jnp.dot(both, weights[...], preferred_element_type=jnp.float32)

    chips = keep_buf.shape[0]
    each = chips // outs

    def give(buf, outputs, copied, turn, block):
        slot = chips - 1 - turn
        buf[slot] = block(chips_ref[slot])
        for index, out in enumerate(outputs):

            @pl.when(slot // each == index)
            def _():
                pltpu.make_async_copy(buf.at[slot], out.at[slot % each], sem.at[copied]).start()

    @pl.loop(0, chips)
    def _(turn):
        give(send_buf, send, 3, turn, lambda chip: rows_of(2 * chip + 1 - core).astype(jnp.bfloat16))

    @pl.loop(0, chips)
    def _(turn):
        give(keep_buf, keep, 4, turn, lambda chip: rows_of(2 * chip + core))

    pltpu.make_async_copy(send_buf, send_buf, sem.at[3]).wait()
    pltpu.make_async_copy(keep_buf, keep_buf, sem.at[4]).wait()


def local(block_values, block_pairs, live_counts, occupied):
    owners = lax.axis_size("aux")
    me = lax.axis_index("aux")
    core, chip = me % 2, me // 2
    shard, width = occupied.shape
    total = owners * shard
    slots = block_values.shape[0]
    piece = math.gcd(BLK, shard)
    same_core = [[2 * i + k for i in range(owners // 2)] for k in range(2)]
    swap = [(i, i ^ 1) for i in range(owners)]

    mine = lax.dynamic_slice_in_dim(occupied, core * LANES, LANES, 1)
    given = lax.dynamic_slice_in_dim(occupied, (1 - core) * LANES, LANES, 1)
    parts = (mine, move(given, swap))

    tile_sets = [
        values.reshape(slots, BLK * BLK // LANES, LANES) for values in (block_values, move(block_values, swap))
    ]

    chips = owners // 2
    slot_ids = jnp.arange(chips, dtype=jnp.int32)
    lined = chips == 2 * LINE
    if lined:
        held = spread(parts)
        chip_of_slot = (slot_ids + chip // 2) % LINE * 2 + ((slot_ids // LINE) ^ (chip % 2))
    else:
        held = [lax.all_gather(part, "aux", axis_index_groups=same_core, axis=0, tiled=True) for part in parts]
        chip_of_slot = slot_ids

    live = live_counts[0]
    tile_ids = jnp.arange(slots, dtype=jnp.int32)
    row_starts = jnp.where(tile_ids < live, block_pairs[:, 0] * BLK, total)
    groups = jnp.full((slots,), (live + UNROLL - 1) // UNROLL, jnp.int32)
    table = jnp.stack([row_starts, block_pairs[:, 1], groups])
    other_table = lax.ppermute(table, "aux", swap)

    rows = jnp.concatenate([table[0], other_table[0]])
    columns = jnp.concatenate([table[1], other_table[1]])
    first = columns[:, None] * BLK + jnp.arange(BLK // piece, dtype=jnp.int32) * piece
    owner = first // shard
    owner_chip = owner // 2
    slot_of = owner_chip
    if lined:
        slot_of = (chip // 2 - owner_chip // 2) % LINE + LINE * ((owner_chip % 2) ^ (chip % 2))
    spots = ((((owner % 2) ^ core) * chips + slot_of) * shard + first % shard).reshape(-1)
    meta = jnp.stack([table[2, 0], other_table[2, 0], core]).astype(jnp.int32)

    smem = pl.BlockSpec(memory_space=pltpu.SMEM)
    hbm = pl.BlockSpec(memory_space=pl.ANY)
    outs = chips if lined else 1
    block = (chips // outs, shard, WIN)
    results = pl.pallas_call(
        functools.partial(work_kernel, (len(held), outs), piece, shard),
        out_shape=[jax.ShapeDtypeStruct(block, jnp.float32)] * outs
        + [jax.ShapeDtypeStruct(block, jnp.bfloat16)] * outs,
        in_specs=[smem] * 4 + [hbm] * (len(held) + 2),
        out_specs=[hbm] * (2 * outs),
        scratch_shapes=[
            pltpu.VMEM((total, LANES), jnp.bfloat16),
            pltpu.VMEM((2, slots, BLK * BLK // LANES, LANES), jnp.bfloat16),
            pltpu.VMEM((2, total + BLK, LANES), jnp.float32),
            pltpu.VMEM((2 * LANES, WIN), jnp.bfloat16),
            pltpu.VMEM((chips, shard, WIN), jnp.float32),
            pltpu.VMEM((chips, shard, WIN), jnp.bfloat16),
            pltpu.SemaphoreType.DMA((5,)),
        ],
        compiler_params=pltpu.CompilerParams(vmem_limit_bytes=VMEM_BYTES),
        cost_estimate=pl.CostEstimate(
            flops=2 * total * width * (WIN + BLK), bytes_accessed=25 << 20, transcendentals=0
        ),
    )(chip_of_slot, rows, spots, meta, *held, *tile_sets)
    keep, send = results[:outs], results[outs:]

    factor = 1.0 / math.sqrt(owners * width)
    if lined:
        return collect([part[0] for part in keep], [part[0] for part in send], swap) * factor
    pair_sum = (keep[0] + move(send[0], swap).astype(jnp.float32)).astype(jnp.bfloat16)
    block_sum = lax.psum_scatter(
        pair_sum.reshape(total // 2, WIN), "aux", axis_index_groups=same_core, scatter_dimension=0, tiled=True
    )
    return block_sum.astype(jnp.float32) * factor


def solution(mesh):
    placed = (
        P(("groups", "aux"), None),
        P(("groups", "aux"), None),
        P(("groups", "aux")),
        P(("groups", "aux"), None),
    )
    return jax.shard_map(
        local, mesh=mesh, in_specs=placed, out_specs=P(("groups", "aux"), None), check_vma=False
    )
```

time: 150 us -> 133 us (0.89)
  local copies, waits for them, and re-layouts: 20.1 us -> 7.77 us
  waiting for transfers between devices: 71.7 us -> 67.9 us
  starting transfers between devices: 26.4 us -> 29.3 us
  Pallas kernels: 20.4 us -> 18.5 us
    reshape x2 -> x0, local copies, waits for them, and re-layouts: 14.2 us -> none  [the longest x1 7.45 us: local(): other_tiles = other_values.reshape(slots, BLK, BLK)]
    unnamed x16 -> x42, local copies, waits for them, and re-layouts: 0.9 us -> 6.06 us
    ppermute x20 -> x31, starting transfers between devices: 25.7 us -> 29.3 us  [move(): return lax.ppermute(array, 'aux', pairs)]
    optimization_barrier x1 -> x0, local copies, waits for them, and re-layouts: 3.27 us -> none  [after(): return lax.optimization_barrier((array, *others))[0]]
    add x4 -> x2, other arithmetic: 3.94 us -> 1.19 us  [the longest x1 0.64 us: local(): ((owner % 2 ^ core) * chips + slot_of) * shard + first % shard]
    ppermute x20 -> x31, waiting for transfers between devices: 70.4 us -> 67.9 us  [move(): return lax.ppermute(array, 'aux', pairs)]
    pallas_call x1, Pallas kernels: 20.4 us -> 18.5 us  [local(): pl.pallas_call(functools.partial(work_kernel, (len(held), outs), piece, s...]
  transfers between devices with their start and end apart: 23 -> 32, of which waited for: 11 -> 22; matrix products, arithmetic and copies ran while one was open for 18% -> 11% of each run, Pallas kernels for 0% -> 0%
where the time goes in v5:
time: 133 us; the launch traced here: 132 us
  waiting for transfers between devices  67.9 us (51%)
  starting transfers between devices  29.3 us (22%)
  Pallas kernels  18.5 us (14%)
  other arithmetic  7.91 us (6%)
  local copies, waits for them, and re-layouts  7.77 us (6%)
    ppermute x31, waiting for transfers between devices, move(): return lax.ppermute(array, 'aux', pairs)  67.9 us
    ppermute x31, starting transfers between devices, move(): return lax.ppermute(array, 'aux', pairs)  29.3 us
    pallas_call x1, Pallas kernels, local(): pl.pallas_call(functools.partial(work_kernel, (len(held), outs), piece, s...  18.5 us
    unnamed x42, local copies, waits for them, and re-layouts  6.06 us
  transfers between devices with their start and end apart: 32, of which 22 were waited for; matrix products, arithmetic and copies ran while one was open for 11% of the time, Pallas kernels for 0%

profile of v5, /device:TPU:0, one launch (start us, length us, event | category | flops | bytes accessed | tf_op | source)
XLA Modules:
  0.0 132.2 jit_solution(15359685185526554369)
XLA Ops:
  0.0 0.5 collective-permute-start.16
  0.5 1.1 constant_dynamic-slice_fusion
  1.6 0.1 collective-permute-start.8
  1.7 2.9 %collective-permute-start.2 = (bf16[1280,128]{1,0:T(8,128)(2,1)S(1)}, bf16[1280,128]{1,0:T(8,128)(2,1)S(1)}, u32[]{:S(2)}, u32[]{:S(2)}) collective-permute-start(bf16[1280,128]{1,0:T(8,128)(2,1)S(1)} %get-tuple-element.70.refs_0_), channel_id=1, source_target_pairs={{0,2},{1,3},{2,0},{3,1},{4,6},{5,7},{6,4},{7,5},{8,10},{9,11},{10,... | collective-permute-start | bytes 983048 | tf_op jit(solution)/shard_map/ppermute | solution.py:34
  4.6 1.6 %collective-permute-start.1 = (bf16[1280,128]{1,0:T(8,128)(2,1)S(1)}, bf16[1280,128]{1,0:T(8,128)(2,1)S(1)}, u32[]{:S(2)}, u32[]{:S(2)}) collective-permute-start(bf16[1280,128]{1,0:T(8,128)(2,1)S(1)} %get-tuple-element.70.refs_0_), channel_id=1, source_target_pairs={{0,4},{1,5},{2,6},{3,7},{4,8},{5,9},{6,10},{7,11},{8,12},{9,13},{1... | collective-permute-start | bytes 983048 | tf_op jit(solution)/shard_map/ppermute | solution.py:34
  6.2 1.3 %collective-permute-start.10 = (bf16[1280,128]{1,0:T(8,128)(2,1)S(1)}, bf16[1280,128]{1,0:T(8,128)(2,1)}, u32[]{:S(2)}, u32[]{:S(2)}) collective-permute-start(bf16[1280,128]{1,0:T(8,128)(2,1)S(1)} %collective-permute-done.8.refs_8_), channel_id=1, source_target_pairs={{0,2},{1,3},{2,0},{3,1},{4,6},{5,7},{6,4},{7,5},{8,10},{9,11},{10,... | collective-permute-start | bytes 983048 | tf_op jit(solution)/shard_map/ppermute | solution.py:34
  7.6 1.6 %collective-permute-start.9 = (bf16[1280,128]{1,0:T(8,128)(2,1)S(1)}, bf16[1280,128]{1,0:T(8,128)(2,1)}, u32[]{:S(2)}, u32[]{:S(2)}) collective-permute-start(bf16[1280,128]{1,0:T(8,128)(2,1)S(1)} %collective-permute-done.8.refs_8_), channel_id=1, source_target_pairs={{0,4},{1,5},{2,6},{3,7},{4,8},{5,9},{6,10},{7,11},{8,12},{9,13},{1... | collective-permute-start | bytes 983048 | tf_op jit(solution)/shard_map/ppermute | solution.py:34
  9.1 0.8 fusion.34
  10.6 2.6 %collective-permute-done.2.refs_4_ = bf16[1280,128]{1,0:T(8,128)(2,1)S(1)} collective-permute-done((bf16[1280,128]{1,0:T(8,128)(2,1)S(1)}, bf16[1280,128]{1,0:T(8,128)(2,1)S(1)}, u32[]{:S(2)}, u32[]{:S(2)}) %collective-permute-start.2) | collective-permute-done | bytes 327712 | tf_op jit(solution)/shard_map/ppermute | solution.py:34
  13.1 3.9 %collective-permute-done.1.refs_1_ = bf16[1280,128]{1,0:T(8,128)(2,1)S(1)} collective-permute-done((bf16[1280,128]{1,0:T(8,128)(2,1)S(1)}, bf16[1280,128]{1,0:T(8,128)(2,1)S(1)}, u32[]{:S(2)}, u32[]{:S(2)}) %collective-permute-start.1) | collective-permute-done | bytes 327712 | tf_op jit(solution)/shard_map/ppermute | solution.py:34
  17.0 0.3 collective-permute-start.4
  17.3 0.7 compare_select_fusion
  18.1 2.1 %collective-permute-done.10.refs_12_ = bf16[1280,128]{1,0:T(8,128)(2,1)} collective-permute-done((bf16[1280,128]{1,0:T(8,128)(2,1)S(1)}, bf16[1280,128]{1,0:T(8,128)(2,1)}, u32[]{:S(2)}, u32[]{:S(2)}) %collective-permute-start.10) | collective-permute-done | bytes 327712 | tf_op jit(solution)/shard_map/ppermute | solution.py:34
  20.3 3.9 %collective-permute-done.9.refs_9_ = bf16[1280,128]{1,0:T(8,128)(2,1)} collective-permute-done((bf16[1280,128]{1,0:T(8,128)(2,1)S(1)}, bf16[1280,128]{1,0:T(8,128)(2,1)}, u32[]{:S(2)}, u32[]{:S(2)}) %collective-permute-start.9) | collective-permute-done | bytes 327712 | tf_op jit(solution)/shard_map/ppermute | solution.py:34
  24.2 0.3 collective-permute-start.12
  24.6 3.2 %collective-permute-done.4.refs_5_ = bf16[1280,128]{1,0:T(8,128)(2,1)} collective-permute-done((bf16[1280,128]{1,0:T(8,128)(2,1)S(1)}, bf16[1280,128]{1,0:T(8,128)(2,1)}, u32[]{:S(2)}, u32[]{:S(2)}) %collective-permute-start.4) | collective-permute-done | bytes 327712 | tf_op jit(solution)/shard_map/ppermute | solution.py:34
  27.8 0.5 fusion.30.chips_ref
  28.3 3.4 %copy.5 = bf16[32,8,32,128]{3,2,1,0:T(8,128)(2,1)} copy(bf16[32,8,32,128]{3,1,2,0:T(8,128)(2,1)} %bitcast.76) | data formatting | bytes 4194304
  31.8 1.6 %collective-permute-start.6 = (bf16[1280,128]{1,0:T(8,128)(2,1)S(1)}, bf16[1280,128]{1,0:T(8,128)(2,1)S(1)}, u32[]{:S(2)}, u32[]{:S(2)}) collective-permute-start(bf16[1280,128]{1,0:T(8,128)(2,1)S(1)} %collective-permute-done.3.refs_2_), channel_id=1, source_target_pairs={{0,2},{1,3},{2,0},{3,1},{4,6},{5,7},{6,4},{7,5},{8,10},{9,11},{10,... | collective-permute-start | bytes 983048 | tf_op jit(solution)/shard_map/ppermute | solution.py:34
  33.4 0.2 collective-permute-done.12.refs_13_
  33.7 1.8 %collective-permute-start.5 = (bf16[1280,128]{1,0:T(8,128)(2,1)S(1)}, bf16[1280,128]{1,0:T(8,128)(2,1)S(1)}, u32[]{:S(2)}, u32[]{:S(2)}) collective-permute-start(bf16[1280,128]{1,0:T(8,128)(2,1)S(1)} %collective-permute-done.3.refs_2_), channel_id=1, source_target_pairs={{0,4},{1,5},{2,6},{3,7},{4,8},{5,9},{6,10},{7,11},{8,12},{9,13},{1... | collective-permute-start | bytes 983048 | tf_op jit(solution)/shard_map/ppermute | solution.py:34
  35.5 1.5 %collective-permute-done.11.refs_10_ = bf16[1280,128]{1,0:T(8,128)(2,1)S(1)} collective-permute-done((bf16[1280,128]{1,0:T(8,128)(2,1)}, bf16[1280,128]{1,0:T(8,128)(2,1)S(1)}, u32[]{:S(2)}, u32[]{:S(2)}) %collective-permute-start.11) | collective-permute-done | bytes 327712 | tf_op jit(solution)/shard_map/ppermute | solution.py:34
  37.0 0.5 collective-permute-start.14
  37.5 1.0 collective-permute-start.13
  38.6 0.5 slice.23
  39.1 1.3 pad_add_fusion.1.meta_ref
  40.4 2.0 %collective-permute-done.6.refs_6_ = bf16[1280,128]{1,0:T(8,128)(2,1)S(1)} collective-permute-done((bf16[1280,128]{1,0:T(8,128)(2,1)S(1)}, bf16[1280,128]{1,0:T(8,128)(2,1)S(1)}, u32[]{:S(2)}, u32[]{:S(2)}) %collective-permute-start.6) | collective-permute-done | bytes 327712 | tf_op jit(solution)/shard_map/ppermute | solution.py:34
  42.4 3.7 %collective-permute-done.5.refs_3_ = bf16[1280,128]{1,0:T(8,128)(2,1)S(1)} collective-permute-done((bf16[1280,128]{1,0:T(8,128)(2,1)S(1)}, bf16[1280,128]{1,0:T(8,128)(2,1)S(1)}, u32[]{:S(2)}, u32[]{:S(2)}) %collective-permute-start.5) | collective-permute-done | bytes 327712 | tf_op jit(solution)/shard_map/ppermute | solution.py:34
  46.1 1.8 %collective-permute-start.7 = (bf16[1280,128]{1,0:T(8,128)(2,1)S(1)}, bf16[1280,128]{1,0:T(8,128)(2,1)S(1)}, u32[]{:S(2)}, u32[]{:S(2)}) collective-permute-start(bf16[1280,128]{1,0:T(8,128)(2,1)S(1)} %collective-permute-done.5.refs_3_), channel_id=1, source_target_pairs={{0,2},{1,3},{2,0},{3,1},{4,6},{5,7},{6,4},{7,5},{8,10},{9,11},{10,... | collective-permute-start | bytes 983048 | tf_op jit(solution)/shard_map/ppermute | solution.py:34
  47.9 1.6 %collective-permute-done.14.refs_14_ = bf16[1280,128]{1,0:T(8,128)(2,1)S(1)} collective-permute-done((bf16[1280,128]{1,0:T(8,128)(2,1)S(1)}, bf16[1280,128]{1,0:T(8,128)(2,1)S(1)}, u32[]{:S(2)}, u32[]{:S(2)}) %collective-permute-start.14) | collective-permute-done | bytes 327712 | tf_op jit(solution)/shard_map/ppermute | solution.py:34
  49.4 2.8 %collective-permute-done.13.refs_11_ = bf16[1280,128]{1,0:T(8,128)(2,1)S(1)} collective-permute-done((bf16[1280,128]{1,0:T(8,128)(2,1)S(1)}, bf16[1280,128]{1,0:T(8,128)(2,1)S(1)}, u32[]{:S(2)}, u32[]{:S(2)}) %collective-permute-start.13) | collective-permute-done | bytes 327712 | tf_op jit(solution)/shard_map/ppermute | solution.py:34
  52.2 1.0 collective-permute-start.15
  53.1 0.6 fusion.19
  53.8 1.8 %copy.6 = bf16[32,8,32,128]{3,2,1,0:T(8,128)(2,1)} copy(bf16[32,8,32,128]{3,1,2,0:T(8,128)(2,1)S(1)} %bitcast.77) | data formatting | bytes 4194304
  55.7 1.0 collective-permute-done.7.refs_7_
  56.7 6.3 %collective-permute-done.15.refs_15_ = bf16[1280,128]{1,0:T(8,128)(2,1)S(1)} collective-permute-done((bf16[1280,128]{1,0:T(8,128)(2,1)S(1)}, bf16[1280,128]{1,0:T(8,128)(2,1)S(1)}, u32[]{:S(2)}, u32[]{:S(2)}) %collective-permute-start.15) | collective-permute-done | bytes 327712 | tf_op jit(solution)/shard_map/ppermute | solution.py:34
  63.1 0.7 copy-done.18
  63.8 18.5 %shard_map.46 = (f32[1,1280,128]{2,1,0:T(8,128)}, f32[1,1280,128]{2,1,0:T(8,128)}, f32[1,1280,128]{2,1,0:T(8,128)}, f32[1,1280,128]{2,1,0:T(8,128)}, f32[1,1280,...) custom-call(s32[8]{0:T(128)} %fusion.30.chips_ref, ...), custom_call_target="tpu_custom_call" | custom-call | flops 2013265920 | bytes 26214400 | tf_op jit(solution)/shard_map/pallas_call | solution.py:206
  82.4 0.5 collective-permute-start.18
  83.0 0.4 collective-permute-start.23
  83.5 0.7 collective-permute-done.19
  84.2 0.1 collective-permute-start.27
  84.4 1.2 fusion.10
  85.5 0.6 collective-permute-done.24
  86.1 0.1 collective-permute-start.28
  86.3 1.2 fusion.5
  87.5 3.8 %collective-permute-start.25 = (bf16[1280,128]{1,0:T(8,128)(2,1)S(1)}, bf16[1280,128]{1,0:T(8,128)(2,1)S(1)}, u32[]{:S(2)}, u32[]{:S(2)}) collective-permute-start(bf16[1280,128]{1,0:T(8,128)(2,1)S(1)} %fusion.5), channel_id=1, source_target_pairs={{0,2},{1,3},{2,0},{3,1},{4,6},{5,7},{6,4},{7,5},{8,10},{9,11},{10,... | collective-permute-start | bytes 983048 | tf_op jit(solution)/shard_map/ppermute | solution.py:34
  91.4 8.2 %collective-permute-done.25 = bf16[1280,128]{1,0:T(8,128)(2,1)S(1)} collective-permute-done((bf16[1280,128]{1,0:T(8,128)(2,1)S(1)}, bf16[1280,128]{1,0:T(8,128)(2,1)S(1)}, u32[]{:S(2)}, u32[]{:S(2)}) %collective-permute-start.25) | collective-permute-done | bytes 327712 | tf_op jit(solution)/shard_map/ppermute | solution.py:34
  99.5 1.7 %collective-permute-start.20 = (bf16[1280,128]{1,0:T(8,128)(2,1)S(1)}, bf16[1280,128]{1,0:T(8,128)(2,1)S(1)}, u32[]{:S(2)}, u32[]{:S(2)}) collective-permute-start(bf16[1280,128]{1,0:T(8,128)(2,1)S(1)} %fusion.10), channel_id=1, source_target_pairs={{0,2},{1,3},{2,0},{3,1},{4,6},{5,7},{6,4},{7,5},{8,10},{9,11},{10,... | collective-permute-start | bytes 983048 | tf_op jit(solution)/shard_map/ppermute | solution.py:34
  101.3 0.1 fusion.1
  101.4 2.7 %collective-permute-start.29 = (bf16[1280,128]{1,0:T(8,128)(2,1)S(1)}, bf16[1280,128]{1,0:T(8,128)(2,1)S(1)}, u32[]{:S(2)}, u32[]{:S(2)}) collective-permute-start(bf16[1280,128]{1,0:T(8,128)(2,1)S(1)} %fusion.1), channel_id=1, source_target_pairs={{0,4},{1,5},{2,6},{3,7},{4,8},{5,9},{6,10},{7,11},{8,12},{9,13},{1... | collective-permute-start | bytes 983048 | tf_op jit(solution)/shard_map/ppermute | solution.py:34
  104.2 4.8 %collective-permute-done.20 = bf16[1280,128]{1,0:T(8,128)(2,1)S(1)} collective-permute-done((bf16[1280,128]{1,0:T(8,128)(2,1)S(1)}, bf16[1280,128]{1,0:T(8,128)(2,1)S(1)}, u32[]{:S(2)}, u32[]{:S(2)}) %collective-permute-start.20) | collective-permute-done | bytes 327712 | tf_op jit(solution)/shard_map/ppermute | solution.py:34
  109.0 1.5 %collective-permute-start.26 = (bf16[1280,128]{1,0:T(8,128)(2,1)S(1)}, bf16[1280,128]{1,0:T(8,128)(2,1)S(1)}, u32[]{:S(2)}, u32[]{:S(2)}) collective-permute-start(bf16[1280,128]{1,0:T(8,128)(2,1)S(1)} %fusion.6), channel_id=1, source_target_pairs={{0,2},{1,3},{2,0},{3,1},{4,6},{5,7},{6,4},{7,5},{8,10},{9,11},{10,... | collective-permute-start | bytes 983048 | tf_op jit(solution)/shard_map/ppermute | solution.py:34
  110.5 1.7 %collective-permute-done.29 = bf16[1280,128]{1,0:T(8,128)(2,1)S(1)} collective-permute-done((bf16[1280,128]{1,0:T(8,128)(2,1)S(1)}, bf16[1280,128]{1,0:T(8,128)(2,1)S(1)}, u32[]{:S(2)}, u32[]{:S(2)}) %collective-permute-start.29) | collective-permute-done | bytes 327712 | tf_op jit(solution)/shard_map/ppermute | solution.py:34
  112.2 0.2 fusion.4
  112.3 1.0 collective-permute-start.30
  113.3 0.5 collective-permute-start.21
  113.9 4.6 %collective-permute-done.26 = bf16[1280,128]{1,0:T(8,128)(2,1)S(1)} collective-permute-done((bf16[1280,128]{1,0:T(8,128)(2,1)S(1)}, bf16[1280,128]{1,0:T(8,128)(2,1)S(1)}, u32[]{:S(2)}, u32[]{:S(2)}) %collective-permute-start.26) | collective-permute-done | bytes 327712 | tf_op jit(solution)/shard_map/ppermute | solution.py:34
  118.5 3.6 %collective-permute-done.30 = bf16[1280,128]{1,0:T(8,128)(2,1)S(1)} collective-permute-done((bf16[1280,128]{1,0:T(8,128)(2,1)S(1)}, bf16[1280,128]{1,0:T(8,128)(2,1)S(1)}, u32[]{:S(2)}, u32[]{:S(2)}) %collective-permute-start.30) | collective-permute-done | bytes 327712 | tf_op jit(solution)/shard_map/ppermute | solution.py:34
  122.1 0.2 fusion.9
  122.3 0.2 collective-permute-start.31
  122.5 2.1 %collective-permute-done.21 = bf16[1280,128]{1,0:T(8,128)(2,1)S(1)} collective-permute-done((bf16[1280,128]{1,0:T(8,128)(2,1)S(1)}, bf16[1280,128]{1,0:T(8,128)(2,1)S(1)}, u32[]{:S(2)}, u32[]{:S(2)}) %collective-permute-start.21) | collective-permute-done | bytes 327712 | tf_op jit(solution)/shard_map/ppermute | solution.py:34
  124.5 6.7 %collective-permute-done.31 = bf16[1280,128]{1,0:T(8,128)(2,1)S(1)} collective-permute-done((bf16[1280,128]{1,0:T(8,128)(2,1)S(1)}, bf16[1280,128]{1,0:T(8,128)(2,1)S(1)}, u32[]{:S(2)}, u32[]{:S(2)}) %collective-permute-start.31) | collective-permute-done | bytes 327712 | tf_op jit(solution)/shard_map/ppermute | solution.py:34
  131.2 1.0 fusion.14
  (62 shorter events, 0.7 us)
Async XLA Ops:
  0.0 53.8 %collective-permute-start.16 = (bf16[256,4096]{1,0:T(8,128)(2,1)}, bf16[256,4096]{1,0:T(8,128)(2,1)S(1)}, u32[]{:S(2)}, u32[]{:S(2)}) collective-permute-start(bf16[256,4096]{1,0:T(8,128)(2,1)} %param.4), channel_id=1, source_target_pairs={{0,1},{1,0},{2,3},{3,2},{4,5},{5,4},{6,7},{7,6},{8,9},{9,8},{10,11... | collective-permute-start | bytes 6291464 | tf_op jit(solution)/shard_map/ppermute | solution.py:34
  1.6 30.2 %copy-start = (bf16[1280,128]{1,0:T(8,128)(2,1)}, bf16[1280,128]{1,0:T(8,128)(2,1)S(1)}, u32[]{:S(2)}) copy-start(bf16[1280,128]{1,0:T(8,128)(2,1)S(1)} %get-tuple-element.70.refs_0_) | copy-start | bytes 983044
  1.6 4.6 %collective-permute-start.8 = (bf16[1280,128]{1,0:T(8,128)(2,1)S(1)}, bf16[1280,128]{1,0:T(8,128)(2,1)S(1)}, u32[]{:S(2)}, u32[]{:S(2)}) collective-permute-start(bf16[1280,128]{1,0:T(8,128)(2,1)S(1)} %get-tuple-element.69), channel_id=1, source_target_pairs={{0,1},{1,0},{2,3},{3,2},{4,5},{5,4},{6,7},{7,6},{8,9},{9,8},{10,11... | collective-permute-start | bytes 983048 | tf_op jit(solution)/shard_map/ppermute | solution.py:34
  1.7 11.4 %collective-permute-start.2 = (bf16[1280,128]{1,0:T(8,128)(2,1)S(1)}, bf16[1280,128]{1,0:T(8,128)(2,1)S(1)}, u32[]{:S(2)}, u32[]{:S(2)}) collective-permute-start(bf16[1280,128]{1,0:T(8,128)(2,1)S(1)} %get-tuple-element.70.refs_0_), channel_id=1, source_target_pairs={{0,2},{1,3},{2,0},{3,1},{4,6},{5,7},{6,4},{7,5},{8,10},{9,11},{10,... | collective-permute-start | bytes 983048 | tf_op jit(solution)/shard_map/ppermute | solution.py:34
  4.6 12.4 %collective-permute-start.1 = (bf16[1280,128]{1,0:T(8,128)(2,1)S(1)}, bf16[1280,128]{1,0:T(8,128)(2,1)S(1)}, u32[]{:S(2)}, u32[]{:S(2)}) collective-permute-start(bf16[1280,128]{1,0:T(8,128)(2,1)S(1)} %get-tuple-element.70.refs_0_), channel_id=1, source_target_pairs={{0,4},{1,5},{2,6},{3,7},{4,8},{5,9},{6,10},{7,11},{8,12},{9,13},{1... | collective-permute-start | bytes 983048 | tf_op jit(solution)/shard_map/ppermute | solution.py:34
  6.2 25.6 %copy-start.7 = (bf16[1280,128]{1,0:T(8,128)(2,1)}, bf16[1280,128]{1,0:T(8,128)(2,1)S(1)}, u32[]{:S(2)}) copy-start(bf16[1280,128]{1,0:T(8,128)(2,1)S(1)} %collective-permute-done.8.refs_8_) | copy-start | bytes 983044
  6.2 14.0 %collective-permute-start.10 = (bf16[1280,128]{1,0:T(8,128)(2,1)S(1)}, bf16[1280,128]{1,0:T(8,128)(2,1)}, u32[]{:S(2)}, u32[]{:S(2)}) collective-permute-start(bf16[1280,128]{1,0:T(8,128)(2,1)S(1)} %collective-permute-done.8.refs_8_), channel_id=1, source_target_pairs={{0,2},{1,3},{2,0},{3,1},{4,6},{5,7},{6,4},{7,5},{8,10},{9,11},{10,... | collective-permute-start | bytes 983048 | tf_op jit(solution)/shard_map/ppermute | solution.py:34
  7.6 16.6 %collective-permute-start.9 = (bf16[1280,128]{1,0:T(8,128)(2,1)S(1)}, bf16[1280,128]{1,0:T(8,128)(2,1)}, u32[]{:S(2)}, u32[]{:S(2)}) collective-permute-start(bf16[1280,128]{1,0:T(8,128)(2,1)S(1)} %collective-permute-done.8.refs_8_), channel_id=1, source_target_pairs={{0,4},{1,5},{2,6},{3,7},{4,8},{5,9},{6,10},{7,11},{8,12},{9,13},{1... | collective-permute-start | bytes 983048 | tf_op jit(solution)/shard_map/ppermute | solution.py:34
  13.1 18.6 %copy-start.8 = (bf16[1280,128]{1,0:T(8,128)(2,1)}, bf16[1280,128]{1,0:T(8,128)(2,1)S(1)}, u32[]{:S(2)}) copy-start(bf16[1280,128]{1,0:T(8,128)(2,1)S(1)} %collective-permute-done.2.refs_4_) | copy-start | bytes 983044
  17.0 14.7 %copy-start.9 = (bf16[1280,128]{1,0:T(8,128)(2,1)}, bf16[1280,128]{1,0:T(8,128)(2,1)S(1)}, u32[]{:S(2)}) copy-start(bf16[1280,128]{1,0:T(8,128)(2,1)S(1)} %collective-permute-done.1.refs_1_) | copy-start | bytes 983044
  17.0 10.8 %collective-permute-start.4 = (bf16[1280,128]{1,0:T(8,128)(2,1)S(1)}, bf16[1280,128]{1,0:T(8,128)(2,1)}, u32[]{:S(2)}, u32[]{:S(2)}) collective-permute-start(bf16[1280,128]{1,0:T(8,128)(2,1)S(1)} %collective-permute-done.1.refs_1_), channel_id=1, source_target_pairs={{0,2},{1,3},{2,0},{3,1},{4,6},{5,7},{6,4},{7,5},{8,10},{9,11},{10,... | collective-permute-start | bytes 983048 | tf_op jit(solution)/shard_map/ppermute | solution.py:34
  18.1 13.7 %collective-permute-start.3 = (bf16[1280,128]{1,0:T(8,128)(2,1)S(1)}, bf16[1280,128]{1,0:T(8,128)(2,1)S(1)}, u32[]{:S(2)}, u32[]{:S(2)}) collective-permute-start(bf16[1280,128]{1,0:T(8,128)(2,1)S(1)} %collective-permute-done.1.refs_1_), channel_id=1, source_target_pairs={{0,4},{1,5},{2,6},{3,7},{4,8},{5,9},{6,10},{7,11},{8,12},{9,13},{1... | collective-permute-start | bytes 983048 | tf_op jit(solution)/shard_map/ppermute | solution.py:34
  24.2 9.5 %collective-permute-start.12 = (bf16[1280,128]{1,0:T(8,128)(2,1)}, bf16[1280,128]{1,0:T(8,128)(2,1)S(1)}, u32[]{:S(2)}, u32[]{:S(2)}) collective-permute-start(bf16[1280,128]{1,0:T(8,128)(2,1)} %collective-permute-done.9.refs_9_), channel_id=1, source_target_pairs={{0,2},{1,3},{2,0},{3,1},{4,6},{5,7},{6,4},{7,5},{8,10},{9,11},{10,... | collective-permute-start | bytes 983048 | tf_op jit(solution)/shard_map/ppermute | solution.py:34
  24.5 12.5 %collective-permute-start.11 = (bf16[1280,128]{1,0:T(8,128)(2,1)}, bf16[1280,128]{1,0:T(8,128)(2,1)S(1)}, u32[]{:S(2)}, u32[]{:S(2)}) collective-permute-start(bf16[1280,128]{1,0:T(8,128)(2,1)} %collective-permute-done.9.refs_9_), channel_id=1, source_target_pairs={{0,4},{1,5},{2,6},{3,7},{4,8},{5,9},{6,10},{7,11},{8,12},{9,13},{1... | collective-permute-start | bytes 983048 | tf_op jit(solution)/shard_map/ppermute | solution.py:34
  27.8 9.7 %collective-permute-start = (s32[3,256]{1,0:T(4,128)S(1)}, s32[3,256]{1,0:T(4,128)S(1)}, u32[]{:S(2)}, u32[]{:S(2)}) collective-permute-start(s32[3,256]{1,0:T(4,128)S(1)} %add_add_fusion), channel_id=1, source_target_pairs={{0,1},{1,0},{2,3},{3,2},{4,5},{5,4},{6,7},{7,6},{8,9},{9,8},{10,11... | collective-permute-start | bytes 9224 | tf_op jit(solution)/shard_map/ppermute | solution.py:189
  31.8 23.8 %copy-start.10 = (bf16[1280,128]{1,0:T(8,128)(2,1)}, bf16[1280,128]{1,0:T(8,128)(2,1)S(1)}, u32[]{:S(2)}) copy-start(bf16[1280,128]{1,0:T(8,128)(2,1)S(1)} %collective-permute-done.3.refs_2_) | copy-start | bytes 983044
  31.8 10.6 %collective-permute-start.6 = (bf16[1280,128]{1,0:T(8,128)(2,1)S(1)}, bf16[1280,128]{1,0:T(8,128)(2,1)S(1)}, u32[]{:S(2)}, u32[]{:S(2)}) collective-permute-start(bf16[1280,128]{1,0:T(8,128)(2,1)S(1)} %collective-permute-done.3.refs_2_), channel_id=1, source_target_pairs={{0,2},{1,3},{2,0},{3,1},{4,6},{5,7},{6,4},{7,5},{8,10},{9,11},{10,... | collective-permute-start | bytes 983048 | tf_op jit(solution)/shard_map/ppermute | solution.py:34
  33.7 22.0 %copy-start.11 = (bf16[1280,128]{1,0:T(8,128)(2,1)}, bf16[1280,128]{1,0:T(8,128)(2,1)S(1)}, u32[]{:S(2)}) copy-start(bf16[1280,128]{1,0:T(8,128)(2,1)S(1)} %collective-permute-done.12.refs_13_) | copy-start | bytes 983044
  33.7 12.4 %collective-permute-start.5 = (bf16[1280,128]{1,0:T(8,128)(2,1)S(1)}, bf16[1280,128]{1,0:T(8,128)(2,1)S(1)}, u32[]{:S(2)}, u32[]{:S(2)}) collective-permute-start(bf16[1280,128]{1,0:T(8,128)(2,1)S(1)} %collective-permute-done.3.refs_2_), channel_id=1, source_target_pairs={{0,4},{1,5},{2,6},{3,7},{4,8},{5,9},{6,10},{7,11},{8,12},{9,13},{1... | collective-permute-start | bytes 983048 | tf_op jit(solution)/shard_map/ppermute | solution.py:34
  37.0 18.7 %copy-start.12 = (bf16[1280,128]{1,0:T(8,128)(2,1)}, bf16[1280,128]{1,0:T(8,128)(2,1)S(1)}, u32[]{:S(2)}) copy-start(bf16[1280,128]{1,0:T(8,128)(2,1)S(1)} %collective-permute-done.11.refs_10_) | copy-start | bytes 983044
  37.0 12.4 %collective-permute-start.14 = (bf16[1280,128]{1,0:T(8,128)(2,1)S(1)}, bf16[1280,128]{1,0:T(8,128)(2,1)S(1)}, u32[]{:S(2)}, u32[]{:S(2)}) collective-permute-start(bf16[1280,128]{1,0:T(8,128)(2,1)S(1)} %collective-permute-done.11.refs_10_), channel_id=1, source_target_pairs={{0,2},{1,3},{2,0},{3,1},{4,6},{5,7},{6,4},{7,5},{8,10},{9,11},{10,... | collective-permute-start | bytes 983048 | tf_op jit(solution)/shard_map/ppermute | solution.py:34
  37.5 14.6 %collective-permute-start.13 = (bf16[1280,128]{1,0:T(8,128)(2,1)S(1)}, bf16[1280,128]{1,0:T(8,128)(2,1)S(1)}, u32[]{:S(2)}, u32[]{:S(2)}) collective-permute-start(bf16[1280,128]{1,0:T(8,128)(2,1)S(1)} %collective-permute-done.11.refs_10_), channel_id=1, source_target_pairs={{0,4},{1,5},{2,6},{3,7},{4,8},{5,9},{6,10},{7,11},{8,12},{9,13},{1... | collective-permute-start | bytes 983048 | tf_op jit(solution)/shard_map/ppermute | solution.py:34
  42.4 13.3 %copy-start.13 = (bf16[1280,128]{1,0:T(8,128)(2,1)}, bf16[1280,128]{1,0:T(8,128)(2,1)S(1)}, u32[]{:S(2)}) copy-start(bf16[1280,128]{1,0:T(8,128)(2,1)S(1)} %collective-permute-done.6.refs_6_) | copy-start | bytes 983044
  46.1 9.6 %copy-start.14 = (bf16[1280,128]{1,0:T(8,128)(2,1)}, bf16[1280,128]{1,0:T(8,128)(2,1)S(1)}, u32[]{:S(2)}) copy-start(bf16[1280,128]{1,0:T(8,128)(2,1)S(1)} %collective-permute-done.5.refs_3_) | copy-start | bytes 983044
  46.1 10.7 %collective-permute-start.7 = (bf16[1280,128]{1,0:T(8,128)(2,1)S(1)}, bf16[1280,128]{1,0:T(8,128)(2,1)S(1)}, u32[]{:S(2)}, u32[]{:S(2)}) collective-permute-start(bf16[1280,128]{1,0:T(8,128)(2,1)S(1)} %collective-permute-done.5.refs_3_), channel_id=1, source_target_pairs={{0,2},{1,3},{2,0},{3,1},{4,6},{5,7},{6,4},{7,5},{8,10},{9,11},{10,... | collective-permute-start | bytes 983048 | tf_op jit(solution)/shard_map/ppermute | solution.py:34
  49.4 6.2 %copy-start.15 = (bf16[1280,128]{1,0:T(8,128)(2,1)}, bf16[1280,128]{1,0:T(8,128)(2,1)S(1)}, u32[]{:S(2)}) copy-start(bf16[1280,128]{1,0:T(8,128)(2,1)S(1)} %collective-permute-done.14.refs_14_) | copy-start | bytes 983044
  52.2 3.5 %copy-start.16 = (bf16[1280,128]{1,0:T(8,128)(2,1)}, bf16[1280,128]{1,0:T(8,128)(2,1)S(1)}, u32[]{:S(2)}) copy-start(bf16[1280,128]{1,0:T(8,128)(2,1)S(1)} %collective-permute-done.13.refs_11_) | copy-start | bytes 983044
  52.2 10.9 %collective-permute-start.15 = (bf16[1280,128]{1,0:T(8,128)(2,1)S(1)}, bf16[1280,128]{1,0:T(8,128)(2,1)S(1)}, u32[]{:S(2)}, u32[]{:S(2)}) collective-permute-start(bf16[1280,128]{1,0:T(8,128)(2,1)S(1)} %collective-permute-done.13.refs_11_), channel_id=1, source_target_pairs={{0,2},{1,3},{2,0},{3,1},{4,6},{5,7},{6,4},{7,5},{8,10},{9,11},{10,... | collective-permute-start | bytes 983048 | tf_op jit(solution)/shard_map/ppermute | solution.py:34
  56.7 6.3 %copy-start.17 = (bf16[1280,128]{1,0:T(8,128)(2,1)}, bf16[1280,128]{1,0:T(8,128)(2,1)S(1)}, u32[]{:S(2)}) copy-start(bf16[1280,128]{1,0:T(8,128)(2,1)S(1)} %collective-permute-done.7.refs_7_) | copy-start | bytes 983044
  63.1 0.7 copy-start.18
  82.3 9.0 %copy-start.3 = (f32[1,1280,128]{2,1,0:T(8,128)S(1)}, f32[1,1280,128]{2,1,0:T(8,128)}, u32[]{:S(2)}) copy-start(f32[1,1280,128]{2,1,0:T(8,128)} %get-tuple-element.58) | copy-start | bytes 1966084
  82.3 19.0 %copy-start.1 = (f32[1,1280,128]{2,1,0:T(8,128)S(1)}, f32[1,1280,128]{2,1,0:T(8,128)}, u32[]{:S(2)}) copy-start(f32[1,1280,128]{2,1,0:T(8,128)} %get-tuple-element.66) | copy-start | bytes 1966084
  82.3 1.9 %collective-permute-start.19 = (bf16[1280,128]{1,0:T(8,128)(2,1)}, bf16[1280,128]{1,0:T(8,128)(2,1)S(1)}, u32[]{:S(2)}, u32[]{:S(2)}) collective-permute-start(bf16[1280,128]{1,0:T(8,128)(2,1)} %bitcast.89), channel_id=1, source_target_pairs={{0,1},{1,0},{2,3},{3,2},{4,5},{5,4},{6,7},{7,6},{8,9},{9,8},{10,11... | collective-permute-start | bytes 983048 | tf_op jit(solution)/shard_map/ppermute | solution.py:34
  82.4 21.7 %collective-permute-start.18 = (bf16[1280,128]{1,0:T(8,128)(2,1)}, bf16[1280,128]{1,0:T(8,128)(2,1)S(1)}, u32[]{:S(2)}, u32[]{:S(2)}) collective-permute-start(bf16[1280,128]{1,0:T(8,128)(2,1)} %bitcast.85), channel_id=1, source_target_pairs={{0,1},{1,0},{2,3},{3,2},{4,5},{5,4},{6,7},{7,6},{8,9},{9,8},{10,11... | collective-permute-start | bytes 983048 | tf_op jit(solution)/shard_map/ppermute | solution.py:34
  82.9 30.9 %collective-permute-start.22 = (bf16[1280,128]{1,0:T(8,128)(2,1)}, bf16[1280,128]{1,0:T(8,128)(2,1)S(1)}, u32[]{:S(2)}, u32[]{:S(2)}) collective-permute-start(bf16[1280,128]{1,0:T(8,128)(2,1)} %bitcast.83), channel_id=1, source_target_pairs={{0,1},{1,0},{2,3},{3,2},{4,5},{5,4},{6,7},{7,6},{8,9},{9,8},{10,11... | collective-permute-start | bytes 983048 | tf_op jit(solution)/shard_map/ppermute | solution.py:34
  83.0 4.5 %collective-permute-start.23 = (bf16[1280,128]{1,0:T(8,128)(2,1)}, bf16[1280,128]{1,0:T(8,128)(2,1)S(1)}, u32[]{:S(2)}, u32[]{:S(2)}) collective-permute-start(bf16[1280,128]{1,0:T(8,128)(2,1)} %bitcast.87), channel_id=1, source_target_pairs={{0,1},{1,0},{2,3},{3,2},{4,5},{5,4},{6,7},{7,6},{8,9},{9,8},{10,11... | collective-permute-start | bytes 983048 | tf_op jit(solution)/shard_map/ppermute | solution.py:34
  83.4 2.7 %collective-permute-start.24 = (bf16[1280,128]{1,0:T(8,128)(2,1)}, bf16[1280,128]{1,0:T(8,128)(2,1)S(1)}, u32[]{:S(2)}, u32[]{:S(2)}) collective-permute-start(bf16[1280,128]{1,0:T(8,128)(2,1)} %bitcast.88), channel_id=1, source_target_pairs={{0,1},{1,0},{2,3},{3,2},{4,5},{5,4},{6,7},{7,6},{8,9},{9,8},{10,11... | collective-permute-start | bytes 983048 | tf_op jit(solution)/shard_map/ppermute | solution.py:34
  84.2 26.2 %collective-permute-start.27 = (bf16[1280,128]{1,0:T(8,128)(2,1)}, bf16[1280,128]{1,0:T(8,128)(2,1)S(1)}, u32[]{:S(2)}, u32[]{:S(2)}) collective-permute-start(bf16[1280,128]{1,0:T(8,128)(2,1)} %bitcast.84), channel_id=1, source_target_pairs={{0,1},{1,0},{2,3},{3,2},{4,5},{5,4},{6,7},{7,6},{8,9},{9,8},{10,11... | collective-permute-start | bytes 983048 | tf_op jit(solution)/shard_map/ppermute | solution.py:34
  86.1 15.2 %collective-permute-start.28 = (bf16[1280,128]{1,0:T(8,128)(2,1)}, bf16[1280,128]{1,0:T(8,128)(2,1)S(1)}, u32[]{:S(2)}, u32[]{:S(2)}) collective-permute-start(bf16[1280,128]{1,0:T(8,128)(2,1)} %bitcast.86), channel_id=1, source_target_pairs={{0,1},{1,0},{2,3},{3,2},{4,5},{5,4},{6,7},{7,6},{8,9},{9,8},{10,11... | collective-permute-start | bytes 983048 | tf_op jit(solution)/shard_map/ppermute | solution.py:34
  86.3 17.8 %copy-start.2 = (f32[1,1280,128]{2,1,0:T(8,128)S(1)}, f32[1,1280,128]{2,1,0:T(8,128)}, u32[]{:S(2)}) copy-start(f32[1,1280,128]{2,1,0:T(8,128)} %get-tuple-element.51) | copy-start | bytes 1966084
  87.5 12.0 %collective-permute-start.25 = (bf16[1280,128]{1,0:T(8,128)(2,1)S(1)}, bf16[1280,128]{1,0:T(8,128)(2,1)S(1)}, u32[]{:S(2)}, u32[]{:S(2)}) collective-permute-start(bf16[1280,128]{1,0:T(8,128)(2,1)S(1)} %fusion.5), channel_id=1, source_target_pairs={{0,2},{1,3},{2,0},{3,1},{4,6},{5,7},{6,4},{7,5},{8,10},{9,11},{10,... | collective-permute-start | bytes 983048 | tf_op jit(solution)/shard_map/ppermute | solution.py:34
  91.3 20.8 %copy-start.6 = (f32[1,1280,128]{2,1,0:T(8,128)S(1)}, f32[1,1280,128]{2,1,0:T(8,128)}, u32[]{:S(2)}) copy-start(f32[1,1280,128]{2,1,0:T(8,128)} %get-tuple-element.63) | copy-start | bytes 1966084
  99.5 9.4 %collective-permute-start.20 = (bf16[1280,128]{1,0:T(8,128)(2,1)S(1)}, bf16[1280,128]{1,0:T(8,128)(2,1)S(1)}, u32[]{:S(2)}, u32[]{:S(2)}) collective-permute-start(bf16[1280,128]{1,0:T(8,128)(2,1)S(1)} %fusion.10), channel_id=1, source_target_pairs={{0,2},{1,3},{2,0},{3,1},{4,6},{5,7},{6,4},{7,5},{8,10},{9,11},{10,... | collective-permute-start | bytes 983048 | tf_op jit(solution)/shard_map/ppermute | solution.py:34
  101.3 12.0 %copy-start.19 = (bf16[1,1280,128]{2,1,0:T(8,128)(2,1)S(1)}, bf16[1,1280,128]{2,1,0:T(8,128)(2,1)}, u32[]{:S(2)}) copy-start(bf16[1,1280,128]{2,1,0:T(8,128)(2,1)} %get-tuple-element.50) | copy-start | bytes 983044
  101.3 20.8 %copy-start.5 = (f32[1,1280,128]{2,1,0:T(8,128)S(1)}, f32[1,1280,128]{2,1,0:T(8,128)}, u32[]{:S(2)}) copy-start(f32[1,1280,128]{2,1,0:T(8,128)} %get-tuple-element.56) | copy-start | bytes 1966084
  101.4 10.7 %collective-permute-start.29 = (bf16[1280,128]{1,0:T(8,128)(2,1)S(1)}, bf16[1280,128]{1,0:T(8,128)(2,1)S(1)}, u32[]{:S(2)}, u32[]{:S(2)}) collective-permute-start(bf16[1280,128]{1,0:T(8,128)(2,1)S(1)} %fusion.1), channel_id=1, source_target_pairs={{0,4},{1,5},{2,6},{3,7},{4,8},{5,9},{6,10},{7,11},{8,12},{9,13},{1... | collective-permute-start | bytes 983048 | tf_op jit(solution)/shard_map/ppermute | solution.py:34
  104.2 27.0 %copy-start.4 = (f32[1,1280,128]{2,1,0:T(8,128)S(1)}, f32[1,1280,128]{2,1,0:T(8,128)}, u32[]{:S(2)}) copy-start(f32[1,1280,128]{2,1,0:T(8,128)} %get-tuple-element.49) | copy-start | bytes 1966084
  109.0 9.5 %collective-permute-start.26 = (bf16[1280,128]{1,0:T(8,128)(2,1)S(1)}, bf16[1280,128]{1,0:T(8,128)(2,1)S(1)}, u32[]{:S(2)}, u32[]{:S(2)}) collective-permute-start(bf16[1280,128]{1,0:T(8,128)(2,1)S(1)} %fusion.6), channel_id=1, source_target_pairs={{0,2},{1,3},{2,0},{3,1},{4,6},{5,7},{6,4},{7,5},{8,10},{9,11},{10,... | collective-permute-start | bytes 983048 | tf_op jit(solution)/shard_map/ppermute | solution.py:34
  112.3 9.8 %collective-permute-start.30 = (bf16[1280,128]{1,0:T(8,128)(2,1)S(1)}, bf16[1280,128]{1,0:T(8,128)(2,1)S(1)}, u32[]{:S(2)}, u32[]{:S(2)}) collective-permute-start(bf16[1280,128]{1,0:T(8,128)(2,1)S(1)} %fusion.4), channel_id=1, source_target_pairs={{0,4},{1,5},{2,6},{3,7},{4,8},{5,9},{6,10},{7,11},{8,12},{9,13},{1... | collective-permute-start | bytes 983048 | tf_op jit(solution)/shard_map/ppermute | solution.py:34
  113.3 9.1 %collective-permute-start.17 = (bf16[1280,128]{1,0:T(8,128)(2,1)S(1)}, bf16[1280,128]{1,0:T(8,128)(2,1)S(1)}, u32[]{:S(2)}, u32[]{:S(2)}) collective-permute-start(bf16[1280,128]{1,0:T(8,128)(2,1)S(1)} %bitcast.82), channel_id=1, source_target_pairs={{0,1},{1,0},{2,3},{3,2},{4,5},{5,4},{6,7},{7,6},{8,9},{9,8},{10,11... | collective-permute-start | bytes 983048 | tf_op jit(solution)/shard_map/ppermute | solution.py:34
  113.3 11.2 %collective-permute-start.21 = (bf16[1280,128]{1,0:T(8,128)(2,1)S(1)}, bf16[1280,128]{1,0:T(8,128)(2,1)S(1)}, u32[]{:S(2)}, u32[]{:S(2)}) collective-permute-start(bf16[1280,128]{1,0:T(8,128)(2,1)S(1)} %fusion.11), channel_id=1, source_target_pairs={{0,2},{1,3},{2,0},{3,1},{4,6},{5,7},{6,4},{7,5},{8,10},{9,11},{10,... | collective-permute-start | bytes 983048 | tf_op jit(solution)/shard_map/ppermute | solution.py:34
  122.3 8.9 %collective-permute-start.31 = (bf16[1280,128]{1,0:T(8,128)(2,1)S(1)}, bf16[1280,128]{1,0:T(8,128)(2,1)S(1)}, u32[]{:S(2)}, u32[]{:S(2)}) collective-permute-start(bf16[1280,128]{1,0:T(8,128)(2,1)S(1)} %fusion.9), channel_id=1, source_target_pairs={{0,4},{1,5},{2,6},{3,7},{4,8},{5,9},{6,10},{7,11},{8,12},{9,13},{1... | collective-permute-start | bytes 983048 | tf_op jit(solution)/shard_map/ppermute | solution.py:34

commit v6 on v0

v6 whole, which is shorter than its diff:
```python
import functools
import math

import jax
import jax.numpy as jnp
from jax import lax
from jax.experimental import pallas as pl
from jax.experimental.pallas import tpu as pltpu
from jax.sharding import PartitionSpec as P

BLK = 64
WIN = 128
LANES = 128
UNROLL = 8
LINE = 4
SCOPED_BYTES = 16 * 1024 * 1024


def place(z, x, core):
    return (z * 2 + x) * 2 + core


def pairs_of(step):
    return [
        (place(z, x, core), place(*step(z, x), core)) for z in range(LINE) for x in range(2) for core in range(2)
    ]


def tie(*arrays):
    return lax.optimization_barrier(arrays)


def move(array, pairs):
    return lax.ppermute(array, "aux", pairs)


ALONG = pairs_of(lambda z, x: ((z + 1) % LINE, x))
ACROSS = pairs_of(lambda z, x: (z, 1 - x))
ADD_AT = {}
LAY_AT = {}


def spread(parts, meanwhile):
    lines, others = [[part] for part in parts], [[] for _ in parts]

    def arrived(stage):
        held = [line[stage] for line in lines] if stage < LINE else []
        return held + ([other[stage - 1] for other in others] if stage else [])

    for step in range(LINE):
        for index, (line, other) in enumerate(zip(lines, others)):
            if other:
                line[-1], other[-1] = tie(line[-1], other[-1])
            line[-1] = meanwhile(step, index, arrived, line[-1])
            now = line[-1]
            if step + 1 < LINE:
                line.append(move(now, ALONG))
            other.append(move(now, ACROSS))
    return [arrived(stage) for stage in range(LINE + 1)]


def collect(keep, send, swap):
    order = [LINE + 3, LINE + 2, 3, LINE + 1, 2, LINE, 1, 0]
    paired = {}
    for slot in order:
        paired[slot] = keep[slot] + move(send[slot], swap).astype(jnp.float32)
    crossed = []
    for step in (3, 2, 1, 0):
        part = paired[LINE + step].astype(jnp.bfloat16)
        if len(crossed) > 1:
            part, crossed[-2] = tie(part, crossed[-2])
        crossed.append(move(part, ACROSS))
    total = paired[3] + crossed[0].astype(jnp.float32)
    for step in (2, 1, 0):
        arrived = move(total.astype(jnp.bfloat16), ALONG)
        total = paired[step] + crossed[3 - step].astype(jnp.float32) + arrived.astype(jnp.float32)
    return total


def add_tiles(stage, pieces, table_ref, bounds_ref, sources, tile_sets, half, occ, sem):
    rows = sources[0].shape[0]
    for index, source in enumerate(sources):
        pltpu.make_async_copy(source, occ.at[pl.ds(index * rows, rows)], sem).start()
    pltpu.make_async_copy(occ, occ, sem).wait()
    begin, end = bounds_ref[stage], bounds_ref[stage + 1]
    slots, depth, lanes = tile_sets[0].shape
    low = lax.broadcasted_iota(jnp.int32, (depth, lanes), 1) < BLK
    zero = jnp.zeros((depth, lanes), jnp.bfloat16)
    spill = half.shape[0] - BLK
    columns = 2 + pieces
    piece = BLK // pieces

    @pl.loop(0, (end - begin + UNROLL - 1) // UNROLL)
    def _(group):
        products, starts = [], []
        for lane in range(UNROLL):
            entry = begin + group * UNROLL + lane
            tile = table_ref[entry * columns]
            starts.append(jnp.where(entry < end, table_ref[entry * columns + 1], spill))
            spots = [jnp.where(entry < end, table_ref[entry * columns + 2 + cut], 0) for cut in range(pieces)]
            parts = [occ[pl.ds(pl.multiple_of(spot, piece), piece), :] for spot in spots]
            slot = lax.rem(tile, slots)
            pair = jnp.where(tile < slots, tile_sets[0][slot], tile_sets[1][slot])
            left = jnp.concatenate([jnp.where(low, pair, zero), jnp.where(low, zero, pair)], axis=0)
            block = jnp.concatenate(parts * 2, axis=0)
            products.append(jnp.dot(left, block, preferred_element_type=jnp.float32))
        for product, start in zip(products, starts):
            start = pl.multiple_of(start, BLK)
            for odd in range(2):
                span = pl.ds(start + odd, BLK // 2, stride=2)
                half[span, :] += product[odd * (BLK // 2) : (odd + 1) * (BLK // 2)]


def fill_window(half, weights, shard, chips_ref, first, parity, out):
    side_rows = (half.shape[0] - BLK) // 2
    chunk = math.gcd(shard, 256)
    chunks = shard // chunk

    @pl.loop(0, out.shape[0] * chunks)
    def _(turn):
        index, part = turn // chunks, lax.rem(turn, chunks) * chunk
        start = pl.multiple_of((2 * chips_ref[first + index] + parity) * shard + part, 32)
        both = jnp.concatenate(
            [half[pl.ds(side * side_rows + start, chunk), :].astype(jnp.bfloat16) for side in range(2)], axis=1
        )
        product = jnp.dot(both, weights[...], preferred_element_type=jnp.float32)
        out[index, pl.ds(pl.multiple_of(part, 32), chunk), :] = product.astype(out.dtype)


def stage_kernel(stage, count, pieces, table_ref, bounds_ref, *refs):
    sources, tile_sets = refs[:count], refs[count : count + 2]
    half, occ, sem = refs[-3:]
    if stage == 0:

        @pl.loop(0, half.shape[0] // BLK)
        def _(index):
            half[pl.ds(pl.multiple_of(index * BLK, BLK), BLK), :] = jnp.zeros((BLK, LANES), jnp.float32)

    add_tiles(stage, pieces, table_ref, bounds_ref, sources, tile_sets, half, occ, sem)


def window_kernel(stage, count, pieces, shard, first, table_ref, bounds_ref, chips_ref, core_ref, *refs):
    sources, tile_sets = refs[:count], refs[count : count + 2]
    half, weights = refs[count + 3 : count + 5]
    outs = refs[count + 5 : -2]
    occ, sem = refs[-2:]
    add_tiles(stage, pieces, table_ref, bounds_ref, sources, tile_sets, half, occ, sem)
    side_rows = (half.shape[0] - BLK) // 2
    for side in range(2):
        weights[pl.ds(side * LANES, LANES), :] = half[pl.ds(side * side_rows, WIN), :].T.astype(jnp.bfloat16)
    for index, out in enumerate(outs):
        fill_window(half, weights, shard, chips_ref, first + index * out.shape[0], 1 - core_ref[0], out)


def rest_kernel(shard, plan, chips_ref, core_ref, half, weights, *outs):
    for (first, keeps), out in zip(plan, outs):
        parity = core_ref[0] if keeps else 1 - core_ref[0]
        fill_window(half, weights, shard, chips_ref, first, parity, out)


SMEM = pl.BlockSpec(memory_space=pltpu.SMEM)
HBM = pl.BlockSpec(memory_space=pl.ANY)
VMEM = pl.BlockSpec(memory_space=pltpu.VMEM)


def pinned(array):
    return pltpu.with_memory_space_constraint(array, pltpu.VMEM)


def call(kernel, ins, in_specs, outs, scratch, aliases, flops):
    return pl.pallas_call(
        kernel,
        out_shape=outs,
        in_specs=in_specs,
        out_specs=[VMEM] * len(outs),
        scratch_shapes=scratch,
        input_output_aliases=aliases,
        compiler_params=pltpu.CompilerParams(vmem_limit_bytes=SCOPED_BYTES),
        cost_estimate=pl.CostEstimate(flops=flops, bytes_accessed=4 << 20, transcendentals=0),
    )(*ins)


def local(block_values, block_pairs, live_counts, occupied):
    owners = lax.axis_size("aux")
    me = lax.axis_index("aux")
    core, chip = me % 2, me // 2
    shard, width = occupied.shape
    total = owners * shard
    slots = block_values.shape[0]
    piece = math.gcd(BLK, shard)
    pieces = BLK // piece
    chips = owners // 2
    lined = chips == 2 * LINE
    same_core = [[2 * i + k for i in range(chips)] for k in range(2)]
    swap = [(i, i ^ 1) for i in range(owners)]

    mine = lax.dynamic_slice_in_dim(occupied, core * LANES, LANES, 1)
    given = lax.dynamic_slice_in_dim(occupied, (1 - core) * LANES, LANES, 1)
    parts = (mine, move(given, swap))
    tile_sets = [
        values.reshape(slots, BLK * BLK // LANES, LANES) for values in (block_values, move(block_values, swap))
    ]

    slot_ids = jnp.arange(chips, dtype=jnp.int32)
    chip_of_slot = slot_ids
    stage_count = 1
    if lined:
        chip_of_slot = (slot_ids + chip // 2) % LINE * 2 + ((slot_ids // LINE) ^ (chip % 2))
        stage_count = LINE + 1

    tile_ids = jnp.arange(2 * slots, dtype=jnp.int32)
    row_starts = jnp.where(tile_ids[:slots] < live_counts[0], block_pairs[:, 0] * BLK, -1)
    table = jnp.stack([row_starts, block_pairs[:, 1]])
    both = jnp.concatenate([table, move(table, swap)], axis=1)
    first = both[1][:, None] * BLK + jnp.arange(pieces, dtype=jnp.int32) * piece
    owner = first // shard
    part = (owner % 2) ^ core
    owner_chip = owner // 2
    if lined:
        back = (chip // 2 - owner_chip // 2) % LINE
        side = (owner_chip % 2) ^ (chip % 2)
        stage = (back + side)[:, 0]
        slot_of = part + 2 * jnp.where(back + side < LINE, side, 0)
    else:
        stage = jnp.zeros_like(tile_ids)
        slot_of = part * chips + owner_chip
    spots = slot_of * shard + first % shard
    stage = jnp.where(both[0] >= 0, stage, stage_count)
    rows = both[0] + tile_ids // slots * total
    ahead = (stage[None, :] < stage[:, None]) | (
        (stage[None, :] == stage[:, None]) & (tile_ids[None, :] < tile_ids[:, None])
    )
    rank = jnp.sum(ahead.astype(jnp.int32), axis=1)
    entries = jnp.arange(2 * slots + UNROLL, dtype=jnp.int32)
    chosen = rank[None, :] == entries[:, None]
    columns = [tile_ids, rows] + [spots[:, cut] for cut in range(pieces)]
    ordered = jnp.stack(
        [jnp.sum(jnp.where(chosen, column[None, :], 0), axis=1) for column in columns], axis=1
    ).reshape(-1)
    bounds = jnp.sum((stage[None, :] < jnp.arange(stage_count + 1)[:, None]).astype(jnp.int32), axis=1)
    cores = core.astype(jnp.int32).reshape(1)

    half_type = pltpu.VMEM((2 * total + BLK, LANES), jnp.float32)
    work = 4 * slots * BLK * BLK * LANES // stage_count
    halves = []

    def stage_ins(sources):
        scratch = [
            pltpu.VMEM((len(sources) * sources[0].shape[0], LANES), jnp.bfloat16),
            pltpu.SemaphoreType.DMA,
        ]
        return [*sources, *map(pinned, tile_sets)], [HBM] * len(sources) + [VMEM] * 2, scratch

    def add_stage(stage, sources):
        ins, specs, scratch = stage_ins(sources)
        ins, specs = [ordered, bounds] + ins, [SMEM] * 2 + specs
        aliases = {}
        if halves:
            aliases = {len(ins): 0}
            ins, specs = ins + [pinned(halves[-1])], specs + [VMEM]
        halves.extend(
            call(
                functools.partial(stage_kernel, stage, len(sources), pieces),
                ins, specs, [half_type], scratch, aliases, work,
            )
        )

    def meanwhile(step, index, arrived, moved):
        if (step, index) in LAY_AT:
            which = LAY_AT[step, index]
            moved, tile_sets[which] = tie(moved, tile_sets[which])
        if (step, index) in ADD_AT:
            stage = ADD_AT[step, index]
            add_stage(stage, arrived(stage))
            moved, halves[-1] = tie(moved, halves[-1])
        return moved

    if lined:
        stages = spread(parts, meanwhile)
        for stage in range(len(ADD_AT), LINE):
            add_stage(stage, stages[stage])
    else:
        stages = [[lax.all_gather(part, "aux", axis_index_groups=same_core, axis=0, tiled=True) for part in parts]]
        halves.extend(call(clear_kernel, [], [], [half_type], [], {}, 0))

    group = 1 if lined else chips // 2
    far = [group] * (chips // 2 // group)
    ins, specs, scratch = stage_ins(stages[-1])
    ins = [ordered, bounds, chip_of_slot, cores] + ins + [pinned(halves[-1])]
    half, weights, *far_send = call(
        functools.partial(window_kernel, stage_count - 1, len(stages[-1]), pieces, shard, chips // 2),
        ins,
        [SMEM] * 4 + specs + [VMEM],
        [half_type, pltpu.VMEM((2 * LANES, WIN), jnp.bfloat16)]
        + [pltpu.VMEM((size, shard, WIN), jnp.bfloat16) for size in far],
        scratch,
        {len(ins) - 1: 0},
        work + total // 4 * width * WIN * 2,
    )

    def rest(plan):
        return call(
            functools.partial(rest_kernel, shard, plan),
            [chip_of_slot, cores, pinned(half), pinned(weights)],
            [SMEM] * 2 + [VMEM] * 2,
            [pltpu.VMEM((group, shard, WIN), jnp.float32 if keeps else jnp.bfloat16) for _, keeps in plan],
            [],
            {},
            total // 4 * width * WIN * 2,
        )

    far_keep = rest([(chips // 2 + index * group, True) for index in range(len(far))])
    near = rest([(index * group, keeps) for keeps in (False, True) for index in range(len(far))])
    near_send, near_keep = near[: len(far)], near[len(far) :]

    factor = 1.0 / math.sqrt(owners * width)
    keep, send = [*near_keep, *far_keep], [*near_send, *far_send]
    if lined:
        return collect([block[0] for block in keep], [block[0] for block in send], swap) * factor
    keep, send = jnp.concatenate(keep), jnp.concatenate(send)
    pair_sum = (keep + move(send, swap).astype(jnp.float32)).astype(jnp.bfloat16)
    block_sum = lax.psum_scatter(
        pair_sum.reshape(total // 2, WIN), "aux", axis_index_groups=same_core, scatter_dimension=0, tiled=True
    )
    return block_sum.astype(jnp.float32) * factor


def clear_kernel(half):
    @pl.loop(0, half.shape[0] // BLK)
    def _(index):
        half[pl.ds(pl.multiple_of(index * BLK, BLK), BLK), :] = jnp.zeros((BLK, LANES), jnp.float32)


def solution(mesh):
    placed = (
        P(("groups", "aux"), None),
        P(("groups", "aux"), None),
        P(("groups", "aux")),
        P(("groups", "aux"), None),
    )
    return jax.shard_map(
        local, mesh=mesh, in_specs=placed, out_specs=P(("groups", "aux"), None), check_vma=False
    )
```

time: 419 us -> 139 us (0.33)
  waiting for transfers between devices: 289 us -> 62.8 us
  matrix products: 78.2 us -> 0 us
  Pallas kernels: 0 us -> 37.2 us
  starting transfers between devices: 0.04 us -> 22.5 us
  local copies, waits for them, and re-layouts: 33.8 us -> 11.5 us
  between operations: 14.1 us -> 1.14 us
    reduce_scatter x1 -> x0, waiting for transfers between devices: 196 us -> none  [local(): lax.psum_scatter(lax.dot_general(half_rows, window_own, (((1,), (1,)), ((...]
    all_gather x1 -> x0, waiting for transfers between devices: 92.3 us -> none  [local(): occ_whole = lax.all_gather(occupied, 'aux', axis=0, tiled=True)]
    dot_general x7 -> x0, matrix products: 78.2 us -> none  [the longest x2 48.6 us: add_group(): jnp.einsum('gr,gak->rak', row_hot, product, precision=lax.Precision.HIGHE...]
    ppermute x0 -> x32, waiting for transfers between devices: none -> 62.8 us  [move(): return lax.ppermute(array, 'aux', pairs)]
    pallas_call x0 -> x7, Pallas kernels: none -> 37.2 us  [call(): pl.pallas_call(kernel, out_shape=outs, in_specs=in_specs, out_specs=[VMEM...]
    ppermute x0 -> x32, starting transfers between devices: none -> 22.5 us  [move(): return lax.ppermute(array, 'aux', pairs)]
    while x1 -> x0, local copies, waits for them, and re-layouts: 19.6 us -> none  [local(): half_sum = lax.fori_loop(0, turn_total, add_group, start_sum)]
    unnamed x2 -> x28, local copies, waits for them, and re-layouts: 0.01 us -> 10 us
  transfers between devices with their start and end apart: 2 -> 32, of which waited for: 2 -> 13; matrix products, arithmetic and copies ran while one was open for 0% -> 6% of each run, Pallas kernels for 0% -> 22%
where the time goes in v6:
time: 139 us
  waiting for transfers between devices  62.8 us (45%)
  Pallas kernels  37.2 us (27%)
  starting transfers between devices  22.5 us (16%)
  local copies, waits for them, and re-layouts  11.5 us (8%)
  other arithmetic  3.7 us (3%)
    ppermute x32, waiting for transfers between devices, move(): return lax.ppermute(array, 'aux', pairs)  62.8 us
    pallas_call x7, Pallas kernels, call(): pl.pallas_call(kernel, out_shape=outs, in_specs=in_specs, out_specs=[VMEM...  37.2 us
    ppermute x32, starting transfers between devices, move(): return lax.ppermute(array, 'aux', pairs)  22.5 us
    unnamed x28, local copies, waits for them, and re-layouts  10 us
  transfers between devices with their start and end apart: 32, of which 13 were waited for; matrix products, arithmetic and copies ran while one was open for 6% of the time, Pallas kernels for 22%

profile of v6, /device:TPU:0, one launch (start us, length us, event | category | flops | bytes accessed | tf_op | source)
XLA Modules:
  0.0 138.8 jit_solution(7469436302189093794)
XLA Ops:
  0.0 1.1 constant_dynamic-slice_fusion
  1.1 3.1 %collective-permute-start.1 = (bf16[1280,128]{1,0:T(8,128)(2,1)S(1)}, bf16[1280,128]{1,0:T(8,128)(2,1)S(1)}, u32[]{:S(2)}, u32[]{:S(2)}) collective-permute-start(bf16[1280,128]{1,0:T(8,128)(2,1)S(1)} %get-tuple-element.83.refs_0_), channel_id=1, source_target_pairs={{0,4},{1,5},{2,6},{3,7},{4,8},{5,9},{6,10},{7,11},{8,12},{9,13},{1... | collective-permute-start | bytes 983048 | tf_op jit(solution)/shard_map/ppermute | solution.py:34
  4.2 1.5 %collective-permute-start.2 = (bf16[1280,128]{1,0:T(8,128)(2,1)S(1)}, bf16[1280,128]{1,0:T(8,128)(2,1)S(1)}, u32[]{:S(2)}, u32[]{:S(2)}) collective-permute-start(bf16[1280,128]{1,0:T(8,128)(2,1)S(1)} %get-tuple-element.83.refs_0_), channel_id=1, source_target_pairs={{0,2},{1,3},{2,0},{3,1},{4,6},{5,7},{6,4},{7,5},{8,10},{9,11},{10,... | collective-permute-start | bytes 983048 | tf_op jit(solution)/shard_map/ppermute | solution.py:34
  5.7 0.5 collective-permute-start.16
  6.2 0.8 slice_multiply_fusion.1
  7.8 3.4 %copy.11 = bf16[32,8,32,128]{3,2,1,0:T(8,128)(2,1)} copy(bf16[32,8,32,128]{3,1,2,0:T(8,128)(2,1)} %bitcast.87) | data formatting | bytes 4194304
  11.2 0.6 collective-permute-start.10
  11.8 1.6 %collective-permute-start.9 = (bf16[1280,128]{1,0:T(8,128)(2,1)S(1)}, bf16[1280,128]{1,0:T(8,128)(2,1)S(1)}, u32[]{:S(2)}, u32[]{:S(2)}) collective-permute-start(bf16[1280,128]{1,0:T(8,128)(2,1)S(1)} %collective-permute-done.8.refs_1_), channel_id=1, source_target_pairs={{0,4},{1,5},{2,6},{3,7},{4,8},{5,9},{6,10},{7,11},{8,12},{9,13},{1... | collective-permute-start | bytes 983048 | tf_op jit(solution)/shard_map/ppermute | solution.py:34
  13.4 0.7 copy-done.11
  14.2 1.6 %collective-permute-start.3 = (bf16[1280,128]{1,0:T(8,128)(2,1)S(1)}, bf16[1280,128]{1,0:T(8,128)(2,1)S(1)}, u32[]{:S(2)}, u32[]{:S(2)}) collective-permute-start(bf16[1280,128]{1,0:T(8,128)(2,1)S(1)} %collective-permute-done.1.refs_0_), channel_id=1, source_target_pairs={{0,4},{1,5},{2,6},{3,7},{4,8},{5,9},{6,10},{7,11},{8,12},{9,13},{1... | collective-permute-start | bytes 983048 | tf_op jit(solution)/shard_map/ppermute | solution.py:34
  15.9 1.5 %collective-permute-start.4 = (bf16[1280,128]{1,0:T(8,128)(2,1)S(1)}, bf16[1280,128]{1,0:T(8,128)(2,1)S(1)}, u32[]{:S(2)}, u32[]{:S(2)}) collective-permute-start(bf16[1280,128]{1,0:T(8,128)(2,1)S(1)} %collective-permute-done.1.refs_0_), channel_id=1, source_target_pairs={{0,2},{1,3},{2,0},{3,1},{4,6},{5,7},{6,4},{7,5},{8,10},{9,11},{10,... | collective-permute-start | bytes 983048 | tf_op jit(solution)/shard_map/ppermute | solution.py:34
  17.4 4.5 %collective-permute-done.10.refs_3_ = bf16[1280,128]{1,0:T(8,128)(2,1)S(1)} collective-permute-done((bf16[1280,128]{1,0:T(8,128)(2,1)S(1)}, bf16[1280,128]{1,0:T(8,128)(2,1)S(1)}, u32[]{:S(2)}, u32[]{:S(2)}) %collective-permute-start.10) | collective-permute-done | bytes 327712 | tf_op jit(solution)/shard_map/ppermute | solution.py:34
  21.8 2.4 %collective-permute-done.9.refs_1_ = bf16[1280,128]{1,0:T(8,128)(2,1)S(1)} collective-permute-done((bf16[1280,128]{1,0:T(8,128)(2,1)S(1)}, bf16[1280,128]{1,0:T(8,128)(2,1)S(1)}, u32[]{:S(2)}, u32[]{:S(2)}) %collective-permute-start.9) | collective-permute-done | bytes 327712 | tf_op jit(solution)/shard_map/ppermute | solution.py:34
  24.2 1.5 %collective-permute-start.12 = (bf16[1280,128]{1,0:T(8,128)(2,1)S(1)}, bf16[1280,128]{1,0:T(8,128)(2,1)S(1)}, u32[]{:S(2)}, u32[]{:S(2)}) collective-permute-start(bf16[1280,128]{1,0:T(8,128)(2,1)S(1)} %collective-permute-done.9.refs_1_), channel_id=1, source_target_pairs={{0,2},{1,3},{2,0},{3,1},{4,6},{5,7},{6,4},{7,5},{8,10},{9,11},{10,... | collective-permute-start | bytes 983048 | tf_op jit(solution)/shard_map/ppermute | solution.py:34
  25.8 5.5 %collective-permute-done.3.refs_0_ = bf16[1280,128]{1,0:T(8,128)(2,1)S(1)} collective-permute-done((bf16[1280,128]{1,0:T(8,128)(2,1)S(1)}, bf16[1280,128]{1,0:T(8,128)(2,1)S(1)}, u32[]{:S(2)}, u32[]{:S(2)}) %collective-permute-start.3) | collective-permute-done | bytes 327712 | tf_op jit(solution)/shard_map/ppermute | solution.py:34
  31.2 0.7 copy-done.1
  31.9 1.5 %collective-permute-start.6 = (bf16[1280,128]{1,0:T(8,128)(2,1)S(1)}, bf16[1280,128]{1,0:T(8,128)(2,1)S(1)}, u32[]{:S(2)}, u32[]{:S(2)}) collective-permute-start(bf16[1280,128]{1,0:T(8,128)(2,1)S(1)} %collective-permute-done.3.refs_0_), channel_id=1, source_target_pairs={{0,2},{1,3},{2,0},{3,1},{4,6},{5,7},{6,4},{7,5},{8,10},{9,11},{10,... | collective-permute-start | bytes 983048 | tf_op jit(solution)/shard_map/ppermute | solution.py:34
  33.4 4.8 %collective-permute-done.11.refs_1_ = bf16[1280,128]{1,0:T(8,128)(2,1)S(1)} collective-permute-done((bf16[1280,128]{1,0:T(8,128)(2,1)S(1)}, bf16[1280,128]{1,0:T(8,128)(2,1)S(1)}, u32[]{:S(2)}, u32[]{:S(2)}) %collective-permute-start.11) | collective-permute-done | bytes 327712 | tf_op jit(solution)/shard_map/ppermute | solution.py:34
  38.2 0.7 copy-done.5
  39.0 1.5 %collective-permute-start.14 = (bf16[1280,128]{1,0:T(8,128)(2,1)S(1)}, bf16[1280,128]{1,0:T(8,128)(2,1)S(1)}, u32[]{:S(2)}, u32[]{:S(2)}) collective-permute-start(bf16[1280,128]{1,0:T(8,128)(2,1)S(1)} %collective-permute-done.11.refs_1_), channel_id=1, source_target_pairs={{0,2},{1,3},{2,0},{3,1},{4,6},{5,7},{6,4},{7,5},{8,10},{9,11},{10,... | collective-permute-start | bytes 983048 | tf_op jit(solution)/shard_map/ppermute | solution.py:34
  40.5 0.7 copy-done.3
  41.2 0.3 convert_reduce_fusion
  41.5 3.8 %collective-permute-done.5.refs_0_ = bf16[1280,128]{1,0:T(8,128)(2,1)} collective-permute-done((bf16[1280,128]{1,0:T(8,128)(2,1)S(1)}, bf16[1280,128]{1,0:T(8,128)(2,1)}, u32[]{:S(2)}, u32[]{:S(2)}) %collective-permute-start.5) | collective-permute-done | bytes 327712 | tf_op jit(solution)/shard_map/ppermute | solution.py:34
  45.4 0.7 copy-done.7
  46.1 1.5 %collective-permute-start.7 = (bf16[1280,128]{1,0:T(8,128)(2,1)}, bf16[1280,128]{1,0:T(8,128)(2,1)}, u32[]{:S(2)}, u32[]{:S(2)}) collective-permute-start(bf16[1280,128]{1,0:T(8,128)(2,1)} %collective-permute-done.5.refs_0_), channel_id=1, source_target_pairs={{0,2},{1,3},{2,0},{3,1},{4,6},{5,7},{6,4},{7,5},{8,10},{9,11},{10,... | collective-permute-start | bytes 983048 | tf_op jit(solution)/shard_map/ppermute | solution.py:34
  47.6 4.0 %collective-permute-done.13.refs_1_ = bf16[1280,128]{1,0:T(8,128)(2,1)} collective-permute-done((bf16[1280,128]{1,0:T(8,128)(2,1)S(1)}, bf16[1280,128]{1,0:T(8,128)(2,1)}, u32[]{:S(2)}, u32[]{:S(2)}) %collective-permute-start.13) | collective-permute-done | bytes 327712 | tf_op jit(solution)/shard_map/ppermute | solution.py:34
  51.6 0.7 copy-done.9
  52.4 1.5 %collective-permute-start.15 = (bf16[1280,128]{1,0:T(8,128)(2,1)}, bf16[1280,128]{1,0:T(8,128)(2,1)}, u32[]{:S(2)}, u32[]{:S(2)}) collective-permute-start(bf16[1280,128]{1,0:T(8,128)(2,1)} %collective-permute-done.13.refs_1_), channel_id=1, source_target_pairs={{0,2},{1,3},{2,0},{3,1},{4,6},{5,7},{6,4},{7,5},{8,10},{9,11},{10,... | collective-permute-start | bytes 983048 | tf_op jit(solution)/shard_map/ppermute | solution.py:34
  53.9 0.5 select_reduce_fusion.2
  54.5 0.1 copy.10
  54.6 0.2 reshape.224.table_ref
  54.8 0.1 convert_reduce_fusion.1.bounds_ref
  55.0 2.2 %copy.12 = bf16[32,8,32,128]{3,2,1,0:T(8,128)(2,1)S(1)} copy(bf16[32,8,32,128]{3,1,2,0:T(8,128)(2,1)} %bitcast.27) | data formatting | bytes 4194304
  57.2 6.1 %shard_map.46.refs_6_ = f32[41024,128]{1,0:T(8,128)S(1)} custom-call(s32[1560]{0:T(1024)S(1)} %reshape.224.table_ref, s32[6]{0:T(128)S(1)} %convert_reduce_fusion.1.bounds_ref, bf16[1280,128]{1,0:T(8,128)(2,1)S(1)} %get-tuple-element.83.refs_0_, bf16[1280,128]{1,0:T(8,128)(2,1)S(1)} %copy-done.12, bf16[256,32,128]{2,1,0:T(8,128)(2,1)S(1)} %bitcast.69, ...), custom_call_target="tpu_custom_call" | custom-call | flops 107374184 | bytes 4194304 | tf_op jit(solution)/shard_map/pallas_call | solution.py:171
  63.3 4.3 %shard_map.47.refs_6_ = f32[41024,128]{1,0:T(8,128)S(1)} custom-call(s32[1560]{0:T(1024)S(1)} %reshape.224.table_ref, s32[6]{0:T(128)S(1)} %convert_reduce_fusion.1.bounds_ref, bf16[1280,128]{1,0:T(8,128)(2,1)S(1)} %collective-permute-done.1.refs_0_, bf16[1280,128]{1,0:T(8,128)(2,1)S(1)} %collective-permute-done.9.refs_1_, ...), custom_call_target="tpu_custom_call", output_to_operand_aliasing={{}: (8, {})} | custom-call | flops 107374184 | bytes 4194304 | tf_op jit(solution)/shard_map/pallas_call | solution.py:171
  67.7 3.6 %shard_map.48.refs_6_ = f32[41024,128]{1,0:T(8,128)S(1)} custom-call(s32[1560]{0:T(1024)S(1)} %reshape.224.table_ref, s32[6]{0:T(128)S(1)} %convert_reduce_fusion.1.bounds_ref, bf16[1280,128]{1,0:T(8,128)(2,1)S(1)} %collective-permute-done.3.refs_0_, bf16[1280,128]{1,0:T(8,128)(2,1)S(1)} %copy-done.4, ...), custom_call_target="tpu_custom_call", output_to_operand_aliasing={{}: (8, {})} | custom-call | flops 107374184 | bytes 4194304 | tf_op jit(solution)/shard_map/pallas_call | solution.py:171
  71.3 4.9 %shard_map.49.refs_4_ = f32[41024,128]{1,0:T(8,128)S(1)} custom-call(s32[1560]{0:T(1024)S(1)} %reshape.224.table_ref, s32[6]{0:T(128)S(1)} %convert_reduce_fusion.1.bounds_ref, bf16[1280,128]{1,0:T(8,128)(2,1)} %collective-permute-done.5.refs_0_, bf16[1280,128]{1,0:T(8,128)(2,1)} %collective-permute-done.13.refs_1_, ...), custom_call_target="tpu_custom_call", output_to_operand_aliasing={{}: (8, {})} | custom-call | flops 107374184 | bytes 4194304 | tf_op jit(solution)/shard_map/pallas_call | solution.py:171
  76.3 6.6 %shard_map.50 = (f32[41024,128]{1,0:T(8,128)S(1)}, bf16[256,128]{1,0:T(8,128)(2,1)S(1)}, bf16[1,1280,128]{2,1,0:T(8,128)(2,1)S(1)}, bf16[1,1280,128]{2,1,0:T(8,1...) custom-call(s32[1560]{0:T(1024)S(1)} %reshape.224.table_ref, ...), custom_call_target="tpu_custom_call", output_to_operand_aliasing={{0}: (8, {})} | custom-call | flops 442918496 | bytes 4194304 | tf_op jit(solution)/shard_map/pallas_call | solution.py:171
  83.0 0.5 collective-permute-start.18
  83.5 0.1 collective-permute-start.24
  83.5 0.4 collective-permute-start.23
  84.0 7.6 %shard_map.51 = (bf16[1,1280,128]{2,1,0:T(8,128)(2,1)S(1)}, bf16[1,1280,128]{2,1,0:T(8,128)(2,1)S(1)}, bf16[1,1280,128]{2,1,0:T(8,128)(2,1)S(1)}, bf16[1,1280,12...) custom-call(s32[8]{0:T(128)S(1)} %fusion.35.chips_ref, ...), custom_call_target="tpu_custom_call" | custom-call | flops 335544320 | bytes 4194304 | tf_op jit(solution)/shard_map/pallas_call | solution.py:171
  91.6 0.1 collective-permute-start.28
  91.7 4.1 %shard_map.52 = (f32[1,1280,128]{2,1,0:T(8,128)S(1)}, f32[1,1280,128]{2,1,0:T(8,128)S(1)}, f32[1,1280,128]{2,1,0:T(8,128)S(1)}, f32[1,1280,128]{2,1,0:T(8,128)S(1)}) custom-call(s32[8]{0:T(128)S(1)} %fusion.35.chips_ref, s32[1]{0:T(128)} %bitcast.core_ref, f32[41024,128]{1,0:T(8,128)S(1)} %get-tuple-element.51.half, ...), custom_call_target="tpu_custom_call" | custom-call | flops 335544320 | bytes 4194304 | tf_op jit(solution)/shard_map/pallas_call | solution.py:171
  95.8 0.5 collective-permute-start.27
  96.3 0.1 fusion.12
  96.4 0.1 collective-permute-start.22
  96.5 0.1 fusion.7
  96.7 0.1 fusion.8
  96.8 10.0 %collective-permute-done.25 = bf16[1280,128]{1,0:T(8,128)(2,1)S(1)} collective-permute-done((bf16[1280,128]{1,0:T(8,128)(2,1)S(1)}, bf16[1280,128]{1,0:T(8,128)(2,1)S(1)}, u32[]{:S(2)}, u32[]{:S(2)}) %collective-permute-start.25) | collective-permute-done | bytes 327712 | tf_op jit(solution)/shard_map/ppermute | solution.py:34
  106.8 0.3 collective-permute-start.20
  107.0 0.1 fusion.3
  107.2 0.1 fusion.13
  107.3 8.7 %collective-permute-done.20 = bf16[1280,128]{1,0:T(8,128)(2,1)S(1)} collective-permute-done((bf16[1280,128]{1,0:T(8,128)(2,1)S(1)}, bf16[1280,128]{1,0:T(8,128)(2,1)S(1)}, u32[]{:S(2)}, u32[]{:S(2)}) %collective-permute-start.20) | collective-permute-done | bytes 327712 | tf_op jit(solution)/shard_map/ppermute | solution.py:34
  116.0 0.5 collective-permute-start.26
  116.5 1.7 %collective-permute-done.29 = bf16[1280,128]{1,0:T(8,128)(2,1)S(1)} collective-permute-done((bf16[1280,128]{1,0:T(8,128)(2,1)S(1)}, bf16[1280,128]{1,0:T(8,128)(2,1)S(1)}, u32[]{:S(2)}, u32[]{:S(2)}) %collective-permute-start.29) | collective-permute-done | bytes 327712 | tf_op jit(solution)/shard_map/ppermute | solution.py:34
  118.2 0.2 fusion.6
  118.5 1.6 %collective-permute-start.21 = (bf16[1280,128]{1,0:T(8,128)(2,1)S(1)}, bf16[1280,128]{1,0:T(8,128)(2,1)S(1)}, u32[]{:S(2)}, u32[]{:S(2)}) collective-permute-start(bf16[1280,128]{1,0:T(8,128)(2,1)S(1)} %fusion.13), channel_id=1, source_target_pairs={{0,2},{1,3},{2,0},{3,1},{4,6},{5,7},{6,4},{7,5},{8,10},{9,11},{10,... | collective-permute-start | bytes 983048 | tf_op jit(solution)/shard_map/ppermute | solution.py:34
  120.1 6.5 %collective-permute-done.26 = bf16[1280,128]{1,0:T(8,128)(2,1)S(1)} collective-permute-done((bf16[1280,128]{1,0:T(8,128)(2,1)S(1)}, bf16[1280,128]{1,0:T(8,128)(2,1)S(1)}, u32[]{:S(2)}, u32[]{:S(2)}) %collective-permute-start.26) | collective-permute-done | bytes 327712 | tf_op jit(solution)/shard_map/ppermute | solution.py:34
  126.7 1.8 %collective-permute-done.30 = bf16[1280,128]{1,0:T(8,128)(2,1)S(1)} collective-permute-done((bf16[1280,128]{1,0:T(8,128)(2,1)S(1)}, bf16[1280,128]{1,0:T(8,128)(2,1)S(1)}, u32[]{:S(2)}, u32[]{:S(2)}) %collective-permute-start.30) | collective-permute-done | bytes 327712 | tf_op jit(solution)/shard_map/ppermute | solution.py:34
  128.5 0.2 fusion.11
  128.7 2.7 %collective-permute-done.21 = bf16[1280,128]{1,0:T(8,128)(2,1)S(1)} collective-permute-done((bf16[1280,128]{1,0:T(8,128)(2,1)S(1)}, bf16[1280,128]{1,0:T(8,128)(2,1)S(1)}, u32[]{:S(2)}, u32[]{:S(2)}) %collective-permute-start.21) | collective-permute-done | bytes 327712 | tf_op jit(solution)/shard_map/ppermute | solution.py:34
  131.4 6.4 %collective-permute-done.31 = bf16[1280,128]{1,0:T(8,128)(2,1)S(1)} collective-permute-done((bf16[1280,128]{1,0:T(8,128)(2,1)S(1)}, bf16[1280,128]{1,0:T(8,128)(2,1)S(1)}, u32[]{:S(2)}, u32[]{:S(2)}) %collective-permute-start.31) | collective-permute-done | bytes 327712 | tf_op jit(solution)/shard_map/ppermute | solution.py:34
  137.8 1.0 fusion.16
  (64 shorter events, 0.8 us)
Async XLA Ops:
  1.1 13.1 %collective-permute-start.1 = (bf16[1280,128]{1,0:T(8,128)(2,1)S(1)}, bf16[1280,128]{1,0:T(8,128)(2,1)S(1)}, u32[]{:S(2)}, u32[]{:S(2)}) collective-permute-start(bf16[1280,128]{1,0:T(8,128)(2,1)S(1)} %get-tuple-element.83.refs_0_), channel_id=1, source_target_pairs={{0,4},{1,5},{2,6},{3,7},{4,8},{5,9},{6,10},{7,11},{8,12},{9,13},{1... | collective-permute-start | bytes 983048 | tf_op jit(solution)/shard_map/ppermute | solution.py:34
  4.2 10.0 %collective-permute-start.2 = (bf16[1280,128]{1,0:T(8,128)(2,1)S(1)}, bf16[1280,128]{1,0:T(8,128)(2,1)S(1)}, u32[]{:S(2)}, u32[]{:S(2)}) collective-permute-start(bf16[1280,128]{1,0:T(8,128)(2,1)S(1)} %get-tuple-element.83.refs_0_), channel_id=1, source_target_pairs={{0,2},{1,3},{2,0},{3,1},{4,6},{5,7},{6,4},{7,5},{8,10},{9,11},{10,... | collective-permute-start | bytes 983048 | tf_op jit(solution)/shard_map/ppermute | solution.py:34
  5.7 5.5 %collective-permute-start.8 = (bf16[1280,128]{1,0:T(8,128)(2,1)S(1)}, bf16[1280,128]{1,0:T(8,128)(2,1)S(1)}, u32[]{:S(2)}, u32[]{:S(2)}) collective-permute-start(bf16[1280,128]{1,0:T(8,128)(2,1)S(1)} %get-tuple-element.82), channel_id=1, source_target_pairs={{0,1},{1,0},{2,3},{3,2},{4,5},{5,4},{6,7},{7,6},{8,9},{9,8},{10,11... | collective-permute-start | bytes 983048 | tf_op jit(solution)/shard_map/ppermute | solution.py:34
  5.7 49.3 %collective-permute-start.16 = (bf16[256,4096]{1,0:T(8,128)(2,1)}, bf16[256,4096]{1,0:T(8,128)(2,1)}, u32[]{:S(2)}, u32[]{:S(2)}) collective-permute-start(bf16[256,4096]{1,0:T(8,128)(2,1)} %param.4), channel_id=1, source_target_pairs={{0,1},{1,0},{2,3},{3,2},{4,5},{5,4},{6,7},{7,6},{8,9},{9,8},{10,11... | collective-permute-start | bytes 6291464 | tf_op jit(solution)/shard_map/ppermute | solution.py:34
  7.6 3.6 %collective-permute-start = (s32[2,256]{1,0:T(2,128)S(1)}, s32[2,256]{1,0:T(2,128)S(1)}, u32[]{:S(2)}, u32[]{:S(2)}) collective-permute-start(s32[2,256]{1,0:T(2,128)S(1)} %pad_add_fusion.2), channel_id=1, source_target_pairs={{0,1},{1,0},{2,3},{3,2},{4,5},{5,4},{6,7},{7,6},{8,9},{9,8},{10,11... | collective-permute-start | bytes 6152 | tf_op jit(solution)/shard_map/ppermute | solution.py:34
  11.2 10.6 %collective-permute-start.10 = (bf16[1280,128]{1,0:T(8,128)(2,1)S(1)}, bf16[1280,128]{1,0:T(8,128)(2,1)S(1)}, u32[]{:S(2)}, u32[]{:S(2)}) collective-permute-start(bf16[1280,128]{1,0:T(8,128)(2,1)S(1)} %collective-permute-done.8.refs_1_), channel_id=1, source_target_pairs={{0,2},{1,3},{2,0},{3,1},{4,6},{5,7},{6,4},{7,5},{8,10},{9,11},{10,... | collective-permute-start | bytes 983048 | tf_op jit(solution)/shard_map/ppermute | solution.py:34
  11.8 12.3 %collective-permute-start.9 = (bf16[1280,128]{1,0:T(8,128)(2,1)S(1)}, bf16[1280,128]{1,0:T(8,128)(2,1)S(1)}, u32[]{:S(2)}, u32[]{:S(2)}) collective-permute-start(bf16[1280,128]{1,0:T(8,128)(2,1)S(1)} %collective-permute-done.8.refs_1_), channel_id=1, source_target_pairs={{0,4},{1,5},{2,6},{3,7},{4,8},{5,9},{6,10},{7,11},{8,12},{9,13},{1... | collective-permute-start | bytes 983048 | tf_op jit(solution)/shard_map/ppermute | solution.py:34
  13.4 0.7 copy-start.11
  14.2 17.0 %collective-permute-start.3 = (bf16[1280,128]{1,0:T(8,128)(2,1)S(1)}, bf16[1280,128]{1,0:T(8,128)(2,1)S(1)}, u32[]{:S(2)}, u32[]{:S(2)}) collective-permute-start(bf16[1280,128]{1,0:T(8,128)(2,1)S(1)} %collective-permute-done.1.refs_0_), channel_id=1, source_target_pairs={{0,4},{1,5},{2,6},{3,7},{4,8},{5,9},{6,10},{7,11},{8,12},{9,13},{1... | collective-permute-start | bytes 983048 | tf_op jit(solution)/shard_map/ppermute | solution.py:34
  15.9 15.3 %collective-permute-start.4 = (bf16[1280,128]{1,0:T(8,128)(2,1)S(1)}, bf16[1280,128]{1,0:T(8,128)(2,1)S(1)}, u32[]{:S(2)}, u32[]{:S(2)}) collective-permute-start(bf16[1280,128]{1,0:T(8,128)(2,1)S(1)} %collective-permute-done.1.refs_0_), channel_id=1, source_target_pairs={{0,2},{1,3},{2,0},{3,1},{4,6},{5,7},{6,4},{7,5},{8,10},{9,11},{10,... | collective-permute-start | bytes 983048 | tf_op jit(solution)/shard_map/ppermute | solution.py:34
  24.2 14.0 %collective-permute-start.11 = (bf16[1280,128]{1,0:T(8,128)(2,1)S(1)}, bf16[1280,128]{1,0:T(8,128)(2,1)S(1)}, u32[]{:S(2)}, u32[]{:S(2)}) collective-permute-start(bf16[1280,128]{1,0:T(8,128)(2,1)S(1)} %collective-permute-done.9.refs_1_), channel_id=1, source_target_pairs={{0,4},{1,5},{2,6},{3,7},{4,8},{5,9},{6,10},{7,11},{8,12},{9,13},{1... | collective-permute-start | bytes 983048 | tf_op jit(solution)/shard_map/ppermute | solution.py:34
  24.2 14.0 %collective-permute-start.12 = (bf16[1280,128]{1,0:T(8,128)(2,1)S(1)}, bf16[1280,128]{1,0:T(8,128)(2,1)S(1)}, u32[]{:S(2)}, u32[]{:S(2)}) collective-permute-start(bf16[1280,128]{1,0:T(8,128)(2,1)S(1)} %collective-permute-done.9.refs_1_), channel_id=1, source_target_pairs={{0,2},{1,3},{2,0},{3,1},{4,6},{5,7},{6,4},{7,5},{8,10},{9,11},{10,... | collective-permute-start | bytes 983048 | tf_op jit(solution)/shard_map/ppermute | solution.py:34
  31.2 0.7 copy-start.1
  31.9 13.4 %collective-permute-start.5 = (bf16[1280,128]{1,0:T(8,128)(2,1)S(1)}, bf16[1280,128]{1,0:T(8,128)(2,1)}, u32[]{:S(2)}, u32[]{:S(2)}) collective-permute-start(bf16[1280,128]{1,0:T(8,128)(2,1)S(1)} %collective-permute-done.3.refs_0_), channel_id=1, source_target_pairs={{0,4},{1,5},{2,6},{3,7},{4,8},{5,9},{6,10},{7,11},{8,12},{9,13},{1... | collective-permute-start | bytes 983048 | tf_op jit(solution)/shard_map/ppermute | solution.py:34
  31.9 13.4 %collective-permute-start.6 = (bf16[1280,128]{1,0:T(8,128)(2,1)S(1)}, bf16[1280,128]{1,0:T(8,128)(2,1)S(1)}, u32[]{:S(2)}, u32[]{:S(2)}) collective-permute-start(bf16[1280,128]{1,0:T(8,128)(2,1)S(1)} %collective-permute-done.3.refs_0_), channel_id=1, source_target_pairs={{0,2},{1,3},{2,0},{3,1},{4,6},{5,7},{6,4},{7,5},{8,10},{9,11},{10,... | collective-permute-start | bytes 983048 | tf_op jit(solution)/shard_map/ppermute | solution.py:34
  38.2 0.7 copy-start.5
  39.0 12.7 %collective-permute-start.13 = (bf16[1280,128]{1,0:T(8,128)(2,1)S(1)}, bf16[1280,128]{1,0:T(8,128)(2,1)}, u32[]{:S(2)}, u32[]{:S(2)}) collective-permute-start(bf16[1280,128]{1,0:T(8,128)(2,1)S(1)} %collective-permute-done.11.refs_1_), channel_id=1, source_target_pairs={{0,4},{1,5},{2,6},{3,7},{4,8},{5,9},{6,10},{7,11},{8,12},{9,13},{1... | collective-permute-start | bytes 983048 | tf_op jit(solution)/shard_map/ppermute | solution.py:34
  39.0 12.7 %collective-permute-start.14 = (bf16[1280,128]{1,0:T(8,128)(2,1)S(1)}, bf16[1280,128]{1,0:T(8,128)(2,1)S(1)}, u32[]{:S(2)}, u32[]{:S(2)}) collective-permute-start(bf16[1280,128]{1,0:T(8,128)(2,1)S(1)} %collective-permute-done.11.refs_1_), channel_id=1, source_target_pairs={{0,2},{1,3},{2,0},{3,1},{4,6},{5,7},{6,4},{7,5},{8,10},{9,11},{10,... | collective-permute-start | bytes 983048 | tf_op jit(solution)/shard_map/ppermute | solution.py:34
  40.5 0.7 copy-start.3
  45.4 0.7 copy-start.7
  46.1 30.2 %collective-permute-start.7 = (bf16[1280,128]{1,0:T(8,128)(2,1)}, bf16[1280,128]{1,0:T(8,128)(2,1)}, u32[]{:S(2)}, u32[]{:S(2)}) collective-permute-start(bf16[1280,128]{1,0:T(8,128)(2,1)} %collective-permute-done.5.refs_0_), channel_id=1, source_target_pairs={{0,2},{1,3},{2,0},{3,1},{4,6},{5,7},{6,4},{7,5},{8,10},{9,11},{10,... | collective-permute-start | bytes 983048 | tf_op jit(solution)/shard_map/ppermute | solution.py:34
  51.6 0.7 copy-start.9
  52.4 23.9 %collective-permute-start.15 = (bf16[1280,128]{1,0:T(8,128)(2,1)}, bf16[1280,128]{1,0:T(8,128)(2,1)}, u32[]{:S(2)}, u32[]{:S(2)}) collective-permute-start(bf16[1280,128]{1,0:T(8,128)(2,1)} %collective-permute-done.13.refs_1_), channel_id=1, source_target_pairs={{0,2},{1,3},{2,0},{3,1},{4,6},{5,7},{6,4},{7,5},{8,10},{9,11},{10,... | collective-permute-start | bytes 983048 | tf_op jit(solution)/shard_map/ppermute | solution.py:34
  54.9 2.2 %copy-start = (bf16[32,8,32,128]{3,2,1,0:T(8,128)(2,1)S(1)}, bf16[32,8,32,128]{3,2,1,0:T(8,128)(2,1)}, u32[]{:S(2)}) copy-start(bf16[32,8,32,128]{3,2,1,0:T(8,128)(2,1)} %copy.11) | copy-start | bytes 6291460
  55.0 2.2 %copy-start.12 = (bf16[1280,128]{1,0:T(8,128)(2,1)S(1)}, bf16[1280,128]{1,0:T(8,128)(2,1)}, u32[]{:S(2)}) copy-start(bf16[1280,128]{1,0:T(8,128)(2,1)} %copy-done.11) | copy-start | bytes 983044
  63.3 4.3 %copy-start.2 = (bf16[1280,128]{1,0:T(8,128)(2,1)S(1)}, bf16[1280,128]{1,0:T(8,128)(2,1)}, u32[]{:S(2)}) copy-start(bf16[1280,128]{1,0:T(8,128)(2,1)} %copy-done.1) | copy-start | bytes 983044
  63.3 4.3 %copy-start.4 = (bf16[1280,128]{1,0:T(8,128)(2,1)S(1)}, bf16[1280,128]{1,0:T(8,128)(2,1)}, u32[]{:S(2)}) copy-start(bf16[1280,128]{1,0:T(8,128)(2,1)} %copy-done.3) | copy-start | bytes 983044
  63.3 4.3 %copy-start.6 = (bf16[1280,128]{1,0:T(8,128)(2,1)S(1)}, bf16[1280,128]{1,0:T(8,128)(2,1)}, u32[]{:S(2)}) copy-start(bf16[1280,128]{1,0:T(8,128)(2,1)} %copy-done.5) | copy-start | bytes 983044
  67.6 3.7 %copy-start.8 = (bf16[1280,128]{1,0:T(8,128)(2,1)S(1)}, bf16[1280,128]{1,0:T(8,128)(2,1)}, u32[]{:S(2)}) copy-start(bf16[1280,128]{1,0:T(8,128)(2,1)} %copy-done.7) | copy-start | bytes 983044
  67.6 3.7 %copy-start.10 = (bf16[1280,128]{1,0:T(8,128)(2,1)S(1)}, bf16[1280,128]{1,0:T(8,128)(2,1)}, u32[]{:S(2)}) copy-start(bf16[1280,128]{1,0:T(8,128)(2,1)} %copy-done.9) | copy-start | bytes 983044
  82.9 12.9 %collective-permute-start.19 = (bf16[1280,128]{1,0:T(8,128)(2,1)S(1)}, bf16[1280,128]{1,0:T(8,128)(2,1)S(1)}, u32[]{:S(2)}, u32[]{:S(2)}) collective-permute-start(bf16[1280,128]{1,0:T(8,128)(2,1)S(1)} %bitcast.86), channel_id=1, source_target_pairs={{0,1},{1,0},{2,3},{3,2},{4,5},{5,4},{6,7},{7,6},{8,9},{9,8},{10,11... | collective-permute-start | bytes 983048 | tf_op jit(solution)/shard_map/ppermute | solution.py:34
  83.0 24.3 %collective-permute-start.18 = (bf16[1280,128]{1,0:T(8,128)(2,1)S(1)}, bf16[1280,128]{1,0:T(8,128)(2,1)S(1)}, u32[]{:S(2)}, u32[]{:S(2)}) collective-permute-start(bf16[1280,128]{1,0:T(8,128)(2,1)S(1)} %bitcast.81), channel_id=1, source_target_pairs={{0,1},{1,0},{2,3},{3,2},{4,5},{5,4},{6,7},{7,6},{8,9},{9,8},{10,11... | collective-permute-start | bytes 983048 | tf_op jit(solution)/shard_map/ppermute | solution.py:34
  83.5 12.9 %collective-permute-start.24 = (bf16[1280,128]{1,0:T(8,128)(2,1)S(1)}, bf16[1280,128]{1,0:T(8,128)(2,1)S(1)}, u32[]{:S(2)}, u32[]{:S(2)}) collective-permute-start(bf16[1280,128]{1,0:T(8,128)(2,1)S(1)} %bitcast.85), channel_id=1, source_target_pairs={{0,1},{1,0},{2,3},{3,2},{4,5},{5,4},{6,7},{7,6},{8,9},{9,8},{10,11... | collective-permute-start | bytes 983048 | tf_op jit(solution)/shard_map/ppermute | solution.py:34
  83.5 13.1 %collective-permute-start.23 = (bf16[1280,128]{1,0:T(8,128)(2,1)S(1)}, bf16[1280,128]{1,0:T(8,128)(2,1)S(1)}, u32[]{:S(2)}, u32[]{:S(2)}) collective-permute-start(bf16[1280,128]{1,0:T(8,128)(2,1)S(1)} %bitcast.83), channel_id=1, source_target_pairs={{0,1},{1,0},{2,3},{3,2},{4,5},{5,4},{6,7},{7,6},{8,9},{9,8},{10,11... | collective-permute-start | bytes 983048 | tf_op jit(solution)/shard_map/ppermute | solution.py:34
  91.6 15.5 %collective-permute-start.28 = (bf16[1280,128]{1,0:T(8,128)(2,1)S(1)}, bf16[1280,128]{1,0:T(8,128)(2,1)S(1)}, u32[]{:S(2)}, u32[]{:S(2)}) collective-permute-start(bf16[1280,128]{1,0:T(8,128)(2,1)S(1)} %bitcast.84), channel_id=1, source_target_pairs={{0,1},{1,0},{2,3},{3,2},{4,5},{5,4},{6,7},{7,6},{8,9},{9,8},{10,11... | collective-permute-start | bytes 983048 | tf_op jit(solution)/shard_map/ppermute | solution.py:34
  95.8 20.7 %collective-permute-start.27 = (bf16[1280,128]{1,0:T(8,128)(2,1)S(1)}, bf16[1280,128]{1,0:T(8,128)(2,1)S(1)}, u32[]{:S(2)}, u32[]{:S(2)}) collective-permute-start(bf16[1280,128]{1,0:T(8,128)(2,1)S(1)} %bitcast.82), channel_id=1, source_target_pairs={{0,1},{1,0},{2,3},{3,2},{4,5},{5,4},{6,7},{7,6},{8,9},{9,8},{10,11... | collective-permute-start | bytes 983048 | tf_op jit(solution)/shard_map/ppermute | solution.py:34
  96.4 23.7 %collective-permute-start.22 = (bf16[1280,128]{1,0:T(8,128)(2,1)S(1)}, bf16[1280,128]{1,0:T(8,128)(2,1)S(1)}, u32[]{:S(2)}, u32[]{:S(2)}) collective-permute-start(bf16[1280,128]{1,0:T(8,128)(2,1)S(1)} %bitcast.80), channel_id=1, source_target_pairs={{0,1},{1,0},{2,3},{3,2},{4,5},{5,4},{6,7},{7,6},{8,9},{9,8},{10,11... | collective-permute-start | bytes 983048 | tf_op jit(solution)/shard_map/ppermute | solution.py:34
  96.6 10.1 %collective-permute-start.25 = (bf16[1280,128]{1,0:T(8,128)(2,1)S(1)}, bf16[1280,128]{1,0:T(8,128)(2,1)S(1)}, u32[]{:S(2)}, u32[]{:S(2)}) collective-permute-start(bf16[1280,128]{1,0:T(8,128)(2,1)S(1)} %fusion.7), channel_id=1, source_target_pairs={{0,2},{1,3},{2,0},{3,1},{4,6},{5,7},{6,4},{7,5},{8,10},{9,11},{10,... | collective-permute-start | bytes 983048 | tf_op jit(solution)/shard_map/ppermute | solution.py:34
  106.8 9.3 %collective-permute-start.20 = (bf16[1280,128]{1,0:T(8,128)(2,1)S(1)}, bf16[1280,128]{1,0:T(8,128)(2,1)S(1)}, u32[]{:S(2)}, u32[]{:S(2)}) collective-permute-start(bf16[1280,128]{1,0:T(8,128)(2,1)S(1)} %fusion.12), channel_id=1, source_target_pairs={{0,2},{1,3},{2,0},{3,1},{4,6},{5,7},{6,4},{7,5},{8,10},{9,11},{10,... | collective-permute-start | bytes 983048 | tf_op jit(solution)/shard_map/ppermute | solution.py:34
  107.2 11.0 %collective-permute-start.29 = (bf16[1280,128]{1,0:T(8,128)(2,1)S(1)}, bf16[1280,128]{1,0:T(8,128)(2,1)S(1)}, u32[]{:S(2)}, u32[]{:S(2)}) collective-permute-start(bf16[1280,128]{1,0:T(8,128)(2,1)S(1)} %fusion.3), channel_id=1, source_target_pairs={{0,4},{1,5},{2,6},{3,7},{4,8},{5,9},{6,10},{7,11},{8,12},{9,13},{1... | collective-permute-start | bytes 983048 | tf_op jit(solution)/shard_map/ppermute | solution.py:34
  116.0 10.6 %collective-permute-start.26 = (bf16[1280,128]{1,0:T(8,128)(2,1)S(1)}, bf16[1280,128]{1,0:T(8,128)(2,1)S(1)}, u32[]{:S(2)}, u32[]{:S(2)}) collective-permute-start(bf16[1280,128]{1,0:T(8,128)(2,1)S(1)} %fusion.8), channel_id=1, source_target_pairs={{0,2},{1,3},{2,0},{3,1},{4,6},{5,7},{6,4},{7,5},{8,10},{9,11},{10,... | collective-permute-start | bytes 983048 | tf_op jit(solution)/shard_map/ppermute | solution.py:34
  118.4 10.1 %collective-permute-start.30 = (bf16[1280,128]{1,0:T(8,128)(2,1)S(1)}, bf16[1280,128]{1,0:T(8,128)(2,1)S(1)}, u32[]{:S(2)}, u32[]{:S(2)}) collective-permute-start(bf16[1280,128]{1,0:T(8,128)(2,1)S(1)} %fusion.6), channel_id=1, source_target_pairs={{0,4},{1,5},{2,6},{3,7},{4,8},{5,9},{6,10},{7,11},{8,12},{9,13},{1... | collective-permute-start | bytes 983048 | tf_op jit(solution)/shard_map/ppermute | solution.py:34
  118.4 10.3 %collective-permute-start.17 = (bf16[1280,128]{1,0:T(8,128)(2,1)S(1)}, bf16[1280,128]{1,0:T(8,128)(2,1)S(1)}, u32[]{:S(2)}, u32[]{:S(2)}) collective-permute-start(bf16[1280,128]{1,0:T(8,128)(2,1)S(1)} %bitcast.79), channel_id=1, source_target_pairs={{0,1},{1,0},{2,3},{3,2},{4,5},{5,4},{6,7},{7,6},{8,9},{9,8},{10,11... | collective-permute-start | bytes 983048 | tf_op jit(solution)/shard_map/ppermute | solution.py:34
  118.5 12.9 %collective-permute-start.21 = (bf16[1280,128]{1,0:T(8,128)(2,1)S(1)}, bf16[1280,128]{1,0:T(8,128)(2,1)S(1)}, u32[]{:S(2)}, u32[]{:S(2)}) collective-permute-start(bf16[1280,128]{1,0:T(8,128)(2,1)S(1)} %fusion.13), channel_id=1, source_target_pairs={{0,2},{1,3},{2,0},{3,1},{4,6},{5,7},{6,4},{7,5},{8,10},{9,11},{10,... | collective-permute-start | bytes 983048 | tf_op jit(solution)/shard_map/ppermute | solution.py:34
  128.6 9.2 %collective-permute-start.31 = (bf16[1280,128]{1,0:T(8,128)(2,1)S(1)}, bf16[1280,128]{1,0:T(8,128)(2,1)S(1)}, u32[]{:S(2)}, u32[]{:S(2)}) collective-permute-start(bf16[1280,128]{1,0:T(8,128)(2,1)S(1)} %fusion.11), channel_id=1, source_target_pairs={{0,4},{1,5},{2,6},{3,7},{4,8},{5,9},{6,10},{7,11},{8,12},{9,13},{1... | collective-permute-start | bytes 983048 | tf_op jit(solution)/shard_map/ppermute | solution.py:34

commit v7 on v6

--- a/solution.py
+++ b/solution.py
@@ -36,8 +36,8 @@
 
 ALONG = pairs_of(lambda z, x: ((z + 1) % LINE, x))
 ACROSS = pairs_of(lambda z, x: (z, 1 - x))
-ADD_AT = {}
-LAY_AT = {}
+ADD_AT = {(2, 1): 0, (3, 1): 1}
+CLEAR_AT = (1, 1)
 
 
 def spread(parts, meanwhile):
@@ -59,21 +59,25 @@
     return [arrived(stage) for stage in range(LINE + 1)]
 
 
-def collect(keep, send, swap):
-    order = [LINE + 3, LINE + 2, 3, LINE + 1, 2, LINE, 1, 0]
-    paired = {}
-    for slot in order:
-        paired[slot] = keep[slot] + move(send[slot], swap).astype(jnp.float32)
+def collect(far_keep, far_send, near_of, half, swap):
+    def paired(keep, send):
+        return keep + move(send, swap).astype(jnp.float32)
+
+    steps = range(LINE - 1, -1, -1)
+    parts = {step: paired(far_keep[step], far_send[step]).astype(jnp.bfloat16) for step in steps}
+    half, parts[3], parts[2] = tie(half, parts[3], parts[2])
     crossed = []
-    for step in (3, 2, 1, 0):
-        part = paired[LINE + step].astype(jnp.bfloat16)
+    for step in steps:
+        part = parts[step]
         if len(crossed) > 1:
             part, crossed[-2] = tie(part, crossed[-2])
         crossed.append(move(part, ACROSS))
-    total = paired[3] + crossed[0].astype(jnp.float32)
+    near_keep, near_send = near_of(half)
+    total = paired(near_keep[3], near_send[3]) + crossed[0].astype(jnp.float32)
     for step in (2, 1, 0):
         arrived = move(total.astype(jnp.bfloat16), ALONG)
-        total = paired[step] + crossed[3 - step].astype(jnp.float32) + arrived.astype(jnp.float32)
+        total = paired(near_keep[step], near_send[step]) + crossed[3 - step].astype(jnp.float32)
+        total = total + arrived.astype(jnp.float32)
     return total
 
 
@@ -113,29 +117,19 @@
 
 def fill_window(half, weights, shard, chips_ref, first, parity, out):
     side_rows = (half.shape[0] - BLK) // 2
-    chunk = math.gcd(shard, 256)
-    chunks = shard // chunk
-
-    @pl.loop(0, out.shape[0] * chunks)
-    def _(turn):
-        index, part = turn // chunks, lax.rem(turn, chunks) * chunk
-        start = pl.multiple_of((2 * chips_ref[first + index] + parity) * shard + part, 32)
+
+    @pl.loop(0, out.shape[0])
+    def _(index):
+        start = pl.multiple_of((2 * chips_ref[first + index] + parity) * shard, 32)
         both = jnp.concatenate(
-            [half[pl.ds(side * side_rows + start, chunk), :].astype(jnp.bfloat16) for side in range(2)], axis=1
+            [half[pl.ds(side * side_rows + start, shard), :].astype(jnp.bfloat16) for side in range(2)], axis=1
         )
-        product = jnp.dot(both, weights[...], preferred_element_type=jnp.float32)
-        out[index, pl.ds(pl.multiple_of(part, 32), chunk), :] = product.astype(out.dtype)
+        out[index] = jnp.dot(both, weights[...], preferred_element_type=jnp.float32).astype(out.dtype)
 
 
 def stage_kernel(stage, count, pieces, table_ref, bounds_ref, *refs):
     sources, tile_sets = refs[:count], refs[count : count + 2]
     half, occ, sem = refs[-3:]
-    if stage == 0:
-
-        @pl.loop(0, half.shape[0] // BLK)
-        def _(index):
-            half[pl.ds(pl.multiple_of(index * BLK, BLK), BLK), :] = jnp.zeros((BLK, LANES), jnp.float32)
-
     add_tiles(stage, pieces, table_ref, bounds_ref, sources, tile_sets, half, occ, sem)
 
 
@@ -242,7 +236,7 @@
 
     half_type = pltpu.VMEM((2 * total + BLK, LANES), jnp.float32)
     work = 4 * slots * BLK * BLK * LANES // stage_count
-    halves = []
+    halves = list(call(clear_kernel, [], [], [half_type], [], {}, 0))
 
     def stage_ins(sources):
         scratch = [
@@ -253,22 +247,17 @@
 
     def add_stage(stage, sources):
         ins, specs, scratch = stage_ins(sources)
-        ins, specs = [ordered, bounds] + ins, [SMEM] * 2 + specs
-        aliases = {}
-        if halves:
-            aliases = {len(ins): 0}
-            ins, specs = ins + [pinned(halves[-1])], specs + [VMEM]
+        ins = [ordered, bounds] + ins + [pinned(halves[-1])]
         halves.extend(
             call(
                 functools.partial(stage_kernel, stage, len(sources), pieces),
-                ins, specs, [half_type], scratch, aliases, work,
+                ins, [SMEM] * 2 + specs + [VMEM], [half_type], scratch, {len(ins) - 1: 0}, work,
             )
         )
 
     def meanwhile(step, index, arrived, moved):
-        if (step, index) in LAY_AT:
-            which = LAY_AT[step, index]
-            moved, tile_sets[which] = tie(moved, tile_sets[which])
+        if (step, index) == CLEAR_AT:
+            moved, halves[-1] = tie(moved, halves[-1])
         if (step, index) in ADD_AT:
             stage = ADD_AT[step, index]
             add_stage(stage, arrived(stage))
@@ -281,7 +270,6 @@
             add_stage(stage, stages[stage])
     else:
         stages = [[lax.all_gather(part, "aux", axis_index_groups=same_core, axis=0, tiled=True) for part in parts]]
-        halves.extend(call(clear_kernel, [], [], [half_type], [], {}, 0))
 
     group = 1 if lined else chips // 2
     far = [group] * (chips // 2 // group)
@@ -298,7 +286,7 @@
         work + total // 4 * width * WIN * 2,
     )
 
-    def rest(plan):
+    def rest(plan, half):
         return call(
             functools.partial(rest_kernel, shard, plan),
             [chip_of_slot, cores, pinned(half), pinned(weights)],
@@ -309,14 +297,20 @@
             total // 4 * width * WIN * 2,
         )
 
-    far_keep = rest([(chips // 2 + index * group, True) for index in range(len(far))])
-    near = rest([(index * group, keeps) for keeps in (False, True) for index in range(len(far))])
-    near_send, near_keep = near[: len(far)], near[len(far) :]
+    def near_of(half):
+        blocks = rest([(index * group, keeps) for keeps in (True, False) for index in range(len(far))], half)
+        if lined:
+            blocks = [block[0] for block in blocks]
+        return blocks[: len(far)], blocks[len(far) :]
+
+    far_keep = rest([(chips // 2 + index * group, True) for index in range(len(far))], half)
 
     factor = 1.0 / math.sqrt(owners * width)
+    if lined:
+        far_keep, far_send = [block[0] for block in far_keep], [block[0] for block in far_send]
+        return collect(far_keep, far_send, near_of, half, swap) * factor
+    near_keep, near_send = near_of(half)
     keep, send = [*near_keep, *far_keep], [*near_send, *far_send]
-    if lined:
-        return collect([block[0] for block in keep], [block[0] for block in send], swap) * factor
     keep, send = jnp.concatenate(keep), jnp.concatenate(send)
     pair_sum = (keep + move(send, swap).astype(jnp.float32)).astype(jnp.bfloat16)
     block_sum = lax.psum_scatter(

time: 139 us -> 141 us (1.014)
  Pallas kernels: 37.2 us -> 23.9 us
  local copies, waits for them, and re-layouts: 11.5 us -> 21.2 us
  waiting for transfers between devices: 62.8 us -> 65.5 us
  starting transfers between devices: 22.5 us -> 24.9 us
    pallas_call x7 -> x8, Pallas kernels: 37.2 us -> 23.9 us  [call(): pl.pallas_call(kernel, out_shape=outs, in_specs=in_specs, out_specs=[VMEM...]
    unnamed x28 -> x6, local copies, waits for them, and re-layouts: 10 us -> 18.1 us
    ppermute x32, waiting for transfers between devices: 62.8 us -> 65.5 us  [move(): return lax.ppermute(array, 'aux', pairs)]
    ppermute x32, starting transfers between devices: 22.5 us -> 24.9 us  [move(): return lax.ppermute(array, 'aux', pairs)]
  transfers between devices with their start and end apart: 32 -> 32, of which waited for: 13 -> 12; matrix products, arithmetic and copies ran while one was open for 6% -> 7% of each run, Pallas kernels for 22% -> 15%
where the time goes in v7:
time: 141 us; the launch traced here: 140 us
  waiting for transfers between devices  65.5 us (46%)
  starting transfers between devices  24.9 us (18%)
  Pallas kernels  23.9 us (17%)
  local copies, waits for them, and re-layouts  21.2 us (15%)
  other arithmetic  3.73 us (3%)
    ppermute x32, waiting for transfers between devices, move(): return lax.ppermute(array, 'aux', pairs)  65.5 us
    ppermute x32, starting transfers between devices, move(): return lax.ppermute(array, 'aux', pairs)  24.9 us
    pallas_call x8, Pallas kernels, call(): pl.pallas_call(kernel, out_shape=outs, in_specs=in_specs, out_specs=[VMEM...  23.9 us
    unnamed x6, local copies, waits for them, and re-layouts  18.1 us
  transfers between devices with their start and end apart: 32, of which 12 were waited for; matrix products, arithmetic and copies ran while one was open for 7% of the time, Pallas kernels for 15%

profile of v7, /device:TPU:0, one launch (start us, length us, event | category | flops | bytes accessed | tf_op | source)
XLA Modules:
  0.0 140.2 jit_solution(15097050389312418667)
XLA Ops:
  0.0 0.5 collective-permute-start.13
  0.5 0.8 slice_multiply_fusion.1
  1.9 0.1 collective-permute-start
  2.0 1.1 constant_dynamic-slice_fusion
  3.1 3.1 %collective-permute-start.1 = (bf16[1280,128]{1,0:T(8,128)(2,1)S(1)}, bf16[1280,128]{1,0:T(8,128)(2,1)S(1)}, u32[]{:S(2)}, u32[]{:S(2)}) collective-permute-start(bf16[1280,128]{1,0:T(8,128)(2,1)S(1)} %get-tuple-element.101.refs_0_), channel_id=1, source_target_pairs={{0,4},{1,5},{2,6},{3,7},{4,8},{5,9},{6,10},{7,11},{8,12},{9,13},{1... | collective-permute-start | bytes 983048 | tf_op jit(solution)/shard_map/ppermute | solution.py:34
  6.2 1.5 %collective-permute-start.2 = (bf16[1280,128]{1,0:T(8,128)(2,1)S(1)}, bf16[1280,128]{1,0:T(8,128)(2,1)S(1)}, u32[]{:S(2)}, u32[]{:S(2)}) collective-permute-start(bf16[1280,128]{1,0:T(8,128)(2,1)S(1)} %get-tuple-element.101.refs_0_), channel_id=1, source_target_pairs={{0,2},{1,3},{2,0},{3,1},{4,6},{5,7},{6,4},{7,5},{8,10},{9,11},{10,... | collective-permute-start | bytes 983048 | tf_op jit(solution)/shard_map/ppermute | solution.py:34
  7.7 3.4 %shard_map.46.refs_4_ = f32[41024,128]{1,0:T(8,128)S(1)} custom-call(), custom_call_target="tpu_custom_call" | custom-call | bytes 4194304 | tf_op jit(solution)/shard_map/pallas_call | solution.py:165
  11.1 7.0 %copy-done = f32[41024,128]{1,0:T(8,128)} copy-done((f32[41024,128]{1,0:T(8,128)}, f32[41024,128]{1,0:T(8,128)S(1)}, u32[]{:S(2)}) %copy-start) | copy-done | bytes 21004312
  18.1 2.1 %copy.12 = bf16[32,8,32,128]{3,2,1,0:T(8,128)(2,1)S(1)} copy(bf16[32,8,32,128]{3,1,2,0:T(8,128)(2,1)} %bitcast.87) | data formatting | bytes 4194304
  20.4 0.6 collective-permute-start.10
  21.0 1.6 %collective-permute-start.9 = (bf16[1280,128]{1,0:T(8,128)(2,1)}, bf16[1280,128]{1,0:T(8,128)(2,1)}, u32[]{:S(2)}, u32[]{:S(2)}) collective-permute-start(bf16[1280,128]{1,0:T(8,128)(2,1)} %collective-permute-done.8.refs_1_), channel_id=1, source_target_pairs={{0,4},{1,5},{2,6},{3,7},{4,8},{5,9},{6,10},{7,11},{8,12},{9,13},{1... | collective-permute-start | bytes 983048 | tf_op jit(solution)/shard_map/ppermute | solution.py:34
  22.6 0.3 convert_reduce_fusion
  22.9 1.6 %collective-permute-start.3 = (bf16[1280,128]{1,0:T(8,128)(2,1)S(1)}, bf16[1280,128]{1,0:T(8,128)(2,1)}, u32[]{:S(2)}, u32[]{:S(2)}) collective-permute-start(bf16[1280,128]{1,0:T(8,128)(2,1)S(1)} %collective-permute-done.1.refs_0_), channel_id=1, source_target_pairs={{0,4},{1,5},{2,6},{3,7},{4,8},{5,9},{6,10},{7,11},{8,12},{9,13},{1... | collective-permute-start | bytes 983048 | tf_op jit(solution)/shard_map/ppermute | solution.py:34
  24.5 1.5 %collective-permute-start.4 = (bf16[1280,128]{1,0:T(8,128)(2,1)S(1)}, bf16[1280,128]{1,0:T(8,128)(2,1)}, u32[]{:S(2)}, u32[]{:S(2)}) collective-permute-start(bf16[1280,128]{1,0:T(8,128)(2,1)S(1)} %collective-permute-done.1.refs_0_), channel_id=1, source_target_pairs={{0,2},{1,3},{2,0},{3,1},{4,6},{5,7},{6,4},{7,5},{8,10},{9,11},{10,... | collective-permute-start | bytes 983048 | tf_op jit(solution)/shard_map/ppermute | solution.py:34
  26.0 5.1 %collective-permute-done.10.refs_3_ = bf16[1280,128]{1,0:T(8,128)(2,1)S(1)} collective-permute-done((bf16[1280,128]{1,0:T(8,128)(2,1)}, bf16[1280,128]{1,0:T(8,128)(2,1)S(1)}, u32[]{:S(2)}, u32[]{:S(2)}) %collective-permute-start.10) | collective-permute-done | bytes 327712 | tf_op jit(solution)/shard_map/ppermute | solution.py:34
  31.1 2.5 %collective-permute-done.9.refs_1_ = bf16[1280,128]{1,0:T(8,128)(2,1)} collective-permute-done((bf16[1280,128]{1,0:T(8,128)(2,1)}, bf16[1280,128]{1,0:T(8,128)(2,1)}, u32[]{:S(2)}, u32[]{:S(2)}) %collective-permute-start.9) | collective-permute-done | bytes 327712 | tf_op jit(solution)/shard_map/ppermute | solution.py:34
  33.6 1.5 %collective-permute-start.12 = (bf16[1280,128]{1,0:T(8,128)(2,1)}, bf16[1280,128]{1,0:T(8,128)(2,1)}, u32[]{:S(2)}, u32[]{:S(2)}) collective-permute-start(bf16[1280,128]{1,0:T(8,128)(2,1)} %collective-permute-done.9.refs_1_), channel_id=1, source_target_pairs={{0,2},{1,3},{2,0},{3,1},{4,6},{5,7},{6,4},{7,5},{8,10},{9,11},{10,... | collective-permute-start | bytes 983048 | tf_op jit(solution)/shard_map/ppermute | solution.py:34
  35.1 0.5 select_reduce_fusion.2
  35.7 0.9 copy.11
  36.6 1.2 reshape.224.table_ref
  37.7 0.1 convert_reduce_fusion.1.bounds_ref
  37.8 2.8 %collective-permute-done.3.refs_0_ = bf16[1280,128]{1,0:T(8,128)(2,1)} collective-permute-done((bf16[1280,128]{1,0:T(8,128)(2,1)S(1)}, bf16[1280,128]{1,0:T(8,128)(2,1)}, u32[]{:S(2)}, u32[]{:S(2)}) %collective-permute-start.3) | collective-permute-done | bytes 327712 | tf_op jit(solution)/shard_map/ppermute | solution.py:34
  40.6 1.5 %collective-permute-start.6 = (bf16[1280,128]{1,0:T(8,128)(2,1)}, bf16[1280,128]{1,0:T(8,128)(2,1)S(1)}, u32[]{:S(2)}, u32[]{:S(2)}) collective-permute-start(bf16[1280,128]{1,0:T(8,128)(2,1)} %collective-permute-done.3.refs_0_), channel_id=1, source_target_pairs={{0,2},{1,3},{2,0},{3,1},{4,6},{5,7},{6,4},{7,5},{8,10},{9,11},{10,... | collective-permute-start | bytes 983048 | tf_op jit(solution)/shard_map/ppermute | solution.py:34
  42.1 5.5 %collective-permute-done.11.refs_1_ = bf16[1280,128]{1,0:T(8,128)(2,1)} collective-permute-done((bf16[1280,128]{1,0:T(8,128)(2,1)}, bf16[1280,128]{1,0:T(8,128)(2,1)}, u32[]{:S(2)}, u32[]{:S(2)}) %collective-permute-start.11) | collective-permute-done | bytes 327712 | tf_op jit(solution)/shard_map/ppermute | solution.py:34
  47.7 2.1 %copy.13 = bf16[32,8,32,128]{3,2,1,0:T(8,128)(2,1)S(1)} copy(bf16[32,8,32,128]{3,1,2,0:T(8,128)(2,1)} %bitcast.27) | data formatting | bytes 4194304
  49.7 7.0 %copy-done.1 = f32[41024,128]{1,0:T(8,128)S(1)} copy-done((f32[41024,128]{1,0:T(8,128)S(1)}, f32[41024,128]{1,0:T(8,128)}, u32[]{:S(2)}) %copy-start.1) | copy-done | bytes 21004312
  56.7 3.0 %shard_map.47.refs_6_ = f32[41024,128]{1,0:T(8,128)S(1)} custom-call(s32[1560]{0:T(1024)S(1)} %reshape.224.table_ref, s32[6]{0:T(128)S(1)} %convert_reduce_fusion.1.bounds_ref, bf16[1280,128]{1,0:T(8,128)(2,1)S(1)} %get-tuple-element.101.refs_0_, bf16[1280,128]{1,0:T(8,128)(2,1)} %collective-permute-done.8.refs_1_, ...), custom_call_target="tpu_custom_call", output_to_operand_aliasing={{}: (6, {})} | custom-call | flops 107374184 | bytes 4194304 | tf_op jit(solution)/shard_map/pallas_call | solution.py:165
  59.7 0.3 collective-permute-start.14
  60.0 1.3 collective-permute-start.15
  61.3 0.8 collective-permute-start.7
  62.0 3.7 %shard_map.48.refs_6_ = f32[41024,128]{1,0:T(8,128)S(1)} custom-call(s32[1560]{0:T(1024)S(1)} %reshape.224.table_ref, s32[6]{0:T(128)S(1)} %convert_reduce_fusion.1.bounds_ref, bf16[1280,128]{1,0:T(8,128)(2,1)S(1)} %collective-permute-done.1.refs_0_, bf16[1280,128]{1,0:T(8,128)(2,1)} %collective-permute-done.9.refs_1_, ...), custom_call_target="tpu_custom_call", output_to_operand_aliasing={{}: (8, {})} | custom-call | flops 107374184 | bytes 4194304 | tf_op jit(solution)/shard_map/pallas_call | solution.py:165
  65.7 4.4 %collective-permute-done.14.refs_1_ = bf16[1280,128]{1,0:T(8,128)(2,1)S(1)} collective-permute-done((bf16[1280,128]{1,0:T(8,128)(2,1)}, bf16[1280,128]{1,0:T(8,128)(2,1)S(1)}, u32[]{:S(2)}, u32[]{:S(2)}) %collective-permute-start.14) | collective-permute-done | bytes 327712 | tf_op jit(solution)/shard_map/ppermute | solution.py:34
  70.1 0.7 collective-permute-done.15.refs_3_
  70.9 1.3 collective-permute-start.16
  72.1 4.3 %shard_map.49.refs_6_ = f32[41024,128]{1,0:T(8,128)S(1)} custom-call(s32[1560]{0:T(1024)S(1)} %reshape.224.table_ref, s32[6]{0:T(128)S(1)} %convert_reduce_fusion.1.bounds_ref, bf16[1280,128]{1,0:T(8,128)(2,1)} %collective-permute-done.3.refs_0_, bf16[1280,128]{1,0:T(8,128)(2,1)} %collective-permute-done.11.refs_1_, ...), custom_call_target="tpu_custom_call", output_to_operand_aliasing={{}: (8, {})} | custom-call | flops 107374184 | bytes 4194304 | tf_op jit(solution)/shard_map/pallas_call | solution.py:165
  76.4 3.2 %shard_map.50.refs_4_ = f32[41024,128]{1,0:T(8,128)S(1)} custom-call(s32[1560]{0:T(1024)S(1)} %reshape.224.table_ref, s32[6]{0:T(128)S(1)} %convert_reduce_fusion.1.bounds_ref, bf16[1280,128]{1,0:T(8,128)(2,1)S(1)} %collective-permute-done.5.refs_0_, bf16[1280,128]{1,0:T(8,128)(2,1)S(1)} %collective-permute-done.14.refs_1_, ...), custom_call_target="tpu_custom_call", output_to_operand_aliasing={{}: (8, {})} | custom-call | flops 107374184 | bytes 4194304 | tf_op jit(solution)/shard_map/pallas_call | solution.py:165
  79.7 2.8 %collective-permute-done.16.refs_1_ = bf16[1280,128]{1,0:T(8,128)(2,1)S(1)} collective-permute-done((bf16[1280,128]{1,0:T(8,128)(2,1)S(1)}, bf16[1280,128]{1,0:T(8,128)(2,1)S(1)}, u32[]{:S(2)}, u32[]{:S(2)}) %collective-permute-start.16) | collective-permute-done | bytes 327712 | tf_op jit(solution)/shard_map/ppermute | solution.py:34
  82.4 2.9 %shard_map.51 = (f32[41024,128]{1,0:T(8,128)S(1)}, bf16[256,128]{1,0:T(8,128)(2,1)S(1)}, bf16[1,1280,128]{2,1,0:T(8,128)(2,1)S(1)}, bf16[1,1280,128]{2,1,0:T(8,1...) custom-call(s32[1560]{0:T(1024)S(1)} %reshape.224.table_ref, ...), custom_call_target="tpu_custom_call", output_to_operand_aliasing={{0}: (8, {})} | custom-call | flops 442918496 | bytes 4194304 | tf_op jit(solution)/shard_map/pallas_call | solution.py:165
  85.3 0.1 collective-permute-start.18
  85.4 0.5 collective-permute-start.20
  85.9 0.1 collective-permute-start.17
  86.0 0.4 collective-permute-start.24
  86.4 1.4 shard_map.52
  87.9 0.1 collective-permute-done.17
  88.0 0.1 fusion.16
  88.1 0.8 collective-permute-start.21
  88.8 1.3 collective-permute-start.25
  90.2 2.1 %shard_map.53 = (f32[1,1280,128]{2,1,0:T(8,128)S(1)}, f32[1,1280,128]{2,1,0:T(8,128)S(1)}, f32[1,1280,128]{2,1,0:T(8,128)S(1)}, f32[1,1280,128]{2,1,0:T(8,128)S(...) custom-call(s32[8]{0:T(128)S(1)} %fusion.35.chips_ref, ...), custom_call_target="tpu_custom_call" | custom-call | flops 335544320 | bytes 4194304 | tf_op jit(solution)/shard_map/pallas_call | solution.py:165
  92.2 0.1 collective-permute-start.28
  92.3 0.5 collective-permute-start.27
  92.8 0.1 fusion.7
  92.9 12.0 %collective-permute-done.25 = bf16[1280,128]{1,0:T(8,128)(2,1)S(1)} collective-permute-done((bf16[1280,128]{1,0:T(8,128)(2,1)S(1)}, bf16[1280,128]{1,0:T(8,128)(2,1)S(1)}, u32[]{:S(2)}, u32[]{:S(2)}) %collective-permute-start.25) | collective-permute-done | bytes 327712 | tf_op jit(solution)/shard_map/ppermute | solution.py:34
  104.9 0.1 fusion.3
  105.1 1.2 collective-permute-start.29
  106.3 0.1 fusion.11
  106.4 1.8 %collective-permute-start.26 = (bf16[1280,128]{1,0:T(8,128)(2,1)S(1)}, bf16[1280,128]{1,0:T(8,128)(2,1)S(1)}, u32[]{:S(2)}, u32[]{:S(2)}) collective-permute-start(bf16[1280,128]{1,0:T(8,128)(2,1)S(1)} %fusion.7), channel_id=1, source_target_pairs={{0,2},{1,3},{2,0},{3,1},{4,6},{5,7},{6,4},{7,5},{8,10},{9,11},{10,... | collective-permute-start | bytes 983048 | tf_op jit(solution)/shard_map/ppermute | solution.py:34
  108.2 9.0 %collective-permute-done.29 = bf16[1280,128]{1,0:T(8,128)(2,1)S(1)} collective-permute-done((bf16[1280,128]{1,0:T(8,128)(2,1)S(1)}, bf16[1280,128]{1,0:T(8,128)(2,1)S(1)}, u32[]{:S(2)}, u32[]{:S(2)}) %collective-permute-start.29) | collective-permute-done | bytes 327712 | tf_op jit(solution)/shard_map/ppermute | solution.py:34
  117.2 0.2 fusion.6
  117.4 0.1 collective-permute-start.19
  117.5 0.9 collective-permute-start.22
  118.4 10.2 %collective-permute-done.30 = bf16[1280,128]{1,0:T(8,128)(2,1)S(1)} collective-permute-done((bf16[1280,128]{1,0:T(8,128)(2,1)S(1)}, bf16[1280,128]{1,0:T(8,128)(2,1)S(1)}, u32[]{:S(2)}, u32[]{:S(2)}) %collective-permute-start.30) | collective-permute-done | bytes 327712 | tf_op jit(solution)/shard_map/ppermute | solution.py:34
  128.6 0.2 fusion.10
  128.9 10.3 %collective-permute-done.31 = bf16[1280,128]{1,0:T(8,128)(2,1)S(1)} collective-permute-done((bf16[1280,128]{1,0:T(8,128)(2,1)S(1)}, bf16[1280,128]{1,0:T(8,128)(2,1)S(1)}, u32[]{:S(2)}, u32[]{:S(2)}) %collective-permute-start.31) | collective-permute-done | bytes 327712 | tf_op jit(solution)/shard_map/ppermute | solution.py:34
  139.2 1.0 fusion.14
  (43 shorter events, 0.5 us)
Async XLA Ops:
  0.0 47.7 %collective-permute-start.13 = (bf16[256,4096]{1,0:T(8,128)(2,1)}, bf16[256,4096]{1,0:T(8,128)(2,1)}, u32[]{:S(2)}, u32[]{:S(2)}) collective-permute-start(bf16[256,4096]{1,0:T(8,128)(2,1)} %param.4), channel_id=1, source_target_pairs={{0,1},{1,0},{2,3},{3,2},{4,5},{5,4},{6,7},{7,6},{8,9},{9,8},{10,11... | collective-permute-start | bytes 6291464 | tf_op jit(solution)/shard_map/ppermute | solution.py:34
  1.9 18.3 %collective-permute-start = (s32[2,256]{1,0:T(2,128)S(1)}, s32[2,256]{1,0:T(2,128)S(1)}, u32[]{:S(2)}, u32[]{:S(2)}) collective-permute-start(s32[2,256]{1,0:T(2,128)S(1)} %pad_add_fusion.2), channel_id=1, source_target_pairs={{0,1},{1,0},{2,3},{3,2},{4,5},{5,4},{6,7},{7,6},{8,9},{9,8},{10,11... | collective-permute-start | bytes 6152 | tf_op jit(solution)/shard_map/ppermute | solution.py:34
  3.1 19.7 %collective-permute-start.1 = (bf16[1280,128]{1,0:T(8,128)(2,1)S(1)}, bf16[1280,128]{1,0:T(8,128)(2,1)S(1)}, u32[]{:S(2)}, u32[]{:S(2)}) collective-permute-start(bf16[1280,128]{1,0:T(8,128)(2,1)S(1)} %get-tuple-element.101.refs_0_), channel_id=1, source_target_pairs={{0,4},{1,5},{2,6},{3,7},{4,8},{5,9},{6,10},{7,11},{8,12},{9,13},{1... | collective-permute-start | bytes 983048 | tf_op jit(solution)/shard_map/ppermute | solution.py:34
  6.2 16.7 %collective-permute-start.2 = (bf16[1280,128]{1,0:T(8,128)(2,1)S(1)}, bf16[1280,128]{1,0:T(8,128)(2,1)S(1)}, u32[]{:S(2)}, u32[]{:S(2)}) collective-permute-start(bf16[1280,128]{1,0:T(8,128)(2,1)S(1)} %get-tuple-element.101.refs_0_), channel_id=1, source_target_pairs={{0,2},{1,3},{2,0},{3,1},{4,6},{5,7},{6,4},{7,5},{8,10},{9,11},{10,... | collective-permute-start | bytes 983048 | tf_op jit(solution)/shard_map/ppermute | solution.py:34
  7.7 12.6 %collective-permute-start.8 = (bf16[1280,128]{1,0:T(8,128)(2,1)S(1)}, bf16[1280,128]{1,0:T(8,128)(2,1)}, u32[]{:S(2)}, u32[]{:S(2)}) collective-permute-start(bf16[1280,128]{1,0:T(8,128)(2,1)S(1)} %get-tuple-element.100), channel_id=1, source_target_pairs={{0,1},{1,0},{2,3},{3,2},{4,5},{5,4},{6,7},{7,6},{8,9},{9,8},{10,11... | collective-permute-start | bytes 983048 | tf_op jit(solution)/shard_map/ppermute | solution.py:34
  11.1 7.0 %copy-start = (f32[41024,128]{1,0:T(8,128)}, f32[41024,128]{1,0:T(8,128)S(1)}, u32[]{:S(2)}) copy-start(f32[41024,128]{1,0:T(8,128)S(1)} %shard_map.46.refs_4_) | copy-start | bytes 63012868
  20.4 10.8 %collective-permute-start.10 = (bf16[1280,128]{1,0:T(8,128)(2,1)}, bf16[1280,128]{1,0:T(8,128)(2,1)S(1)}, u32[]{:S(2)}, u32[]{:S(2)}) collective-permute-start(bf16[1280,128]{1,0:T(8,128)(2,1)} %collective-permute-done.8.refs_1_), channel_id=1, source_target_pairs={{0,2},{1,3},{2,0},{3,1},{4,6},{5,7},{6,4},{7,5},{8,10},{9,11},{10,... | collective-permute-start | bytes 983048 | tf_op jit(solution)/shard_map/ppermute | solution.py:34
  21.0 12.7 %collective-permute-start.9 = (bf16[1280,128]{1,0:T(8,128)(2,1)}, bf16[1280,128]{1,0:T(8,128)(2,1)}, u32[]{:S(2)}, u32[]{:S(2)}) collective-permute-start(bf16[1280,128]{1,0:T(8,128)(2,1)} %collective-permute-done.8.refs_1_), channel_id=1, source_target_pairs={{0,4},{1,5},{2,6},{3,7},{4,8},{5,9},{6,10},{7,11},{8,12},{9,13},{1... | collective-permute-start | bytes 983048 | tf_op jit(solution)/shard_map/ppermute | solution.py:34
  22.9 17.7 %collective-permute-start.3 = (bf16[1280,128]{1,0:T(8,128)(2,1)S(1)}, bf16[1280,128]{1,0:T(8,128)(2,1)}, u32[]{:S(2)}, u32[]{:S(2)}) collective-permute-start(bf16[1280,128]{1,0:T(8,128)(2,1)S(1)} %collective-permute-done.1.refs_0_), channel_id=1, source_target_pairs={{0,4},{1,5},{2,6},{3,7},{4,8},{5,9},{6,10},{7,11},{8,12},{9,13},{1... | collective-permute-start | bytes 983048 | tf_op jit(solution)/shard_map/ppermute | solution.py:34
  24.5 16.1 %collective-permute-start.4 = (bf16[1280,128]{1,0:T(8,128)(2,1)S(1)}, bf16[1280,128]{1,0:T(8,128)(2,1)}, u32[]{:S(2)}, u32[]{:S(2)}) collective-permute-start(bf16[1280,128]{1,0:T(8,128)(2,1)S(1)} %collective-permute-done.1.refs_0_), channel_id=1, source_target_pairs={{0,2},{1,3},{2,0},{3,1},{4,6},{5,7},{6,4},{7,5},{8,10},{9,11},{10,... | collective-permute-start | bytes 983048 | tf_op jit(solution)/shard_map/ppermute | solution.py:34
  33.6 14.0 %collective-permute-start.11 = (bf16[1280,128]{1,0:T(8,128)(2,1)}, bf16[1280,128]{1,0:T(8,128)(2,1)}, u32[]{:S(2)}, u32[]{:S(2)}) collective-permute-start(bf16[1280,128]{1,0:T(8,128)(2,1)} %collective-permute-done.9.refs_1_), channel_id=1, source_target_pairs={{0,4},{1,5},{2,6},{3,7},{4,8},{5,9},{6,10},{7,11},{8,12},{9,13},{1... | collective-permute-start | bytes 983048 | tf_op jit(solution)/shard_map/ppermute | solution.py:34
  33.6 14.0 %collective-permute-start.12 = (bf16[1280,128]{1,0:T(8,128)(2,1)}, bf16[1280,128]{1,0:T(8,128)(2,1)}, u32[]{:S(2)}, u32[]{:S(2)}) collective-permute-start(bf16[1280,128]{1,0:T(8,128)(2,1)} %collective-permute-done.9.refs_1_), channel_id=1, source_target_pairs={{0,2},{1,3},{2,0},{3,1},{4,6},{5,7},{6,4},{7,5},{8,10},{9,11},{10,... | collective-permute-start | bytes 983048 | tf_op jit(solution)/shard_map/ppermute | solution.py:34
  40.6 20.6 %collective-permute-start.5 = (bf16[1280,128]{1,0:T(8,128)(2,1)}, bf16[1280,128]{1,0:T(8,128)(2,1)S(1)}, u32[]{:S(2)}, u32[]{:S(2)}) collective-permute-start(bf16[1280,128]{1,0:T(8,128)(2,1)} %collective-permute-done.3.refs_0_), channel_id=1, source_target_pairs={{0,4},{1,5},{2,6},{3,7},{4,8},{5,9},{6,10},{7,11},{8,12},{9,13},{1... | collective-permute-start | bytes 983048 | tf_op jit(solution)/shard_map/ppermute | solution.py:34
  40.6 20.6 %collective-permute-start.6 = (bf16[1280,128]{1,0:T(8,128)(2,1)}, bf16[1280,128]{1,0:T(8,128)(2,1)S(1)}, u32[]{:S(2)}, u32[]{:S(2)}) collective-permute-start(bf16[1280,128]{1,0:T(8,128)(2,1)} %collective-permute-done.3.refs_0_), channel_id=1, source_target_pairs={{0,2},{1,3},{2,0},{3,1},{4,6},{5,7},{6,4},{7,5},{8,10},{9,11},{10,... | collective-permute-start | bytes 983048 | tf_op jit(solution)/shard_map/ppermute | solution.py:34
  49.7 7.0 %copy-start.1 = (f32[41024,128]{1,0:T(8,128)S(1)}, f32[41024,128]{1,0:T(8,128)}, u32[]{:S(2)}) copy-start(f32[41024,128]{1,0:T(8,128)} %copy-done) | copy-start | bytes 63012868
  59.7 10.4 %collective-permute-start.14 = (bf16[1280,128]{1,0:T(8,128)(2,1)}, bf16[1280,128]{1,0:T(8,128)(2,1)S(1)}, u32[]{:S(2)}, u32[]{:S(2)}) collective-permute-start(bf16[1280,128]{1,0:T(8,128)(2,1)} %collective-permute-done.11.refs_1_), channel_id=1, source_target_pairs={{0,4},{1,5},{2,6},{3,7},{4,8},{5,9},{6,10},{7,11},{8,12},{9,13},{1... | collective-permute-start | bytes 983048 | tf_op jit(solution)/shard_map/ppermute | solution.py:34
  60.0 10.9 %collective-permute-start.15 = (bf16[1280,128]{1,0:T(8,128)(2,1)}, bf16[1280,128]{1,0:T(8,128)(2,1)S(1)}, u32[]{:S(2)}, u32[]{:S(2)}) collective-permute-start(bf16[1280,128]{1,0:T(8,128)(2,1)} %collective-permute-done.11.refs_1_), channel_id=1, source_target_pairs={{0,2},{1,3},{2,0},{3,1},{4,6},{5,7},{6,4},{7,5},{8,10},{9,11},{10,... | collective-permute-start | bytes 983048 | tf_op jit(solution)/shard_map/ppermute | solution.py:34
  61.3 18.4 %collective-permute-start.7 = (bf16[1280,128]{1,0:T(8,128)(2,1)S(1)}, bf16[1280,128]{1,0:T(8,128)(2,1)S(1)}, u32[]{:S(2)}, u32[]{:S(2)}) collective-permute-start(bf16[1280,128]{1,0:T(8,128)(2,1)S(1)} %collective-permute-done.5.refs_0_), channel_id=1, source_target_pairs={{0,2},{1,3},{2,0},{3,1},{4,6},{5,7},{6,4},{7,5},{8,10},{9,11},{10,... | collective-permute-start | bytes 983048 | tf_op jit(solution)/shard_map/ppermute | solution.py:34
  70.9 11.6 %collective-permute-start.16 = (bf16[1280,128]{1,0:T(8,128)(2,1)S(1)}, bf16[1280,128]{1,0:T(8,128)(2,1)S(1)}, u32[]{:S(2)}, u32[]{:S(2)}) collective-permute-start(bf16[1280,128]{1,0:T(8,128)(2,1)S(1)} %collective-permute-done.14.refs_1_), channel_id=1, source_target_pairs={{0,2},{1,3},{2,0},{3,1},{4,6},{5,7},{6,4},{7,5},{8,10},{9,11},{10,... | collective-permute-start | bytes 983048 | tf_op jit(solution)/shard_map/ppermute | solution.py:34
  85.3 2.5 %collective-permute-start.18 = (bf16[1280,128]{1,0:T(8,128)(2,1)S(1)}, bf16[1280,128]{1,0:T(8,128)(2,1)S(1)}, u32[]{:S(2)}, u32[]{:S(2)}) collective-permute-start(bf16[1280,128]{1,0:T(8,128)(2,1)S(1)} %bitcast.86), channel_id=1, source_target_pairs={{0,1},{1,0},{2,3},{3,2},{4,5},{5,4},{6,7},{7,6},{8,9},{9,8},{10,11... | collective-permute-start | bytes 983048 | tf_op jit(solution)/shard_map/ppermute | solution.py:34
  85.4 20.9 %collective-permute-start.20 = (bf16[1280,128]{1,0:T(8,128)(2,1)S(1)}, bf16[1280,128]{1,0:T(8,128)(2,1)S(1)}, u32[]{:S(2)}, u32[]{:S(2)}) collective-permute-start(bf16[1280,128]{1,0:T(8,128)(2,1)S(1)} %bitcast.80), channel_id=1, source_target_pairs={{0,1},{1,0},{2,3},{3,2},{4,5},{5,4},{6,7},{7,6},{8,9},{9,8},{10,11... | collective-permute-start | bytes 983048 | tf_op jit(solution)/shard_map/ppermute | solution.py:34
  85.9 2.1 %collective-permute-start.17 = (bf16[1280,128]{1,0:T(8,128)(2,1)S(1)}, bf16[1280,128]{1,0:T(8,128)(2,1)S(1)}, u32[]{:S(2)}, u32[]{:S(2)}) collective-permute-start(bf16[1280,128]{1,0:T(8,128)(2,1)S(1)} %bitcast.84), channel_id=1, source_target_pairs={{0,1},{1,0},{2,3},{3,2},{4,5},{5,4},{6,7},{7,6},{8,9},{9,8},{10,11... | collective-permute-start | bytes 983048 | tf_op jit(solution)/shard_map/ppermute | solution.py:34
  86.0 6.3 %collective-permute-start.24 = (bf16[1280,128]{1,0:T(8,128)(2,1)S(1)}, bf16[1280,128]{1,0:T(8,128)(2,1)S(1)}, u32[]{:S(2)}, u32[]{:S(2)}) collective-permute-start(bf16[1280,128]{1,0:T(8,128)(2,1)S(1)} %bitcast.82), channel_id=1, source_target_pairs={{0,1},{1,0},{2,3},{3,2},{4,5},{5,4},{6,7},{7,6},{8,9},{9,8},{10,11... | collective-permute-start | bytes 983048 | tf_op jit(solution)/shard_map/ppermute | solution.py:34
  88.1 18.3 %collective-permute-start.21 = (bf16[1280,128]{1,0:T(8,128)(2,1)S(1)}, bf16[1280,128]{1,0:T(8,128)(2,1)S(1)}, u32[]{:S(2)}, u32[]{:S(2)}) collective-permute-start(bf16[1280,128]{1,0:T(8,128)(2,1)S(1)} %fusion.15), channel_id=1, source_target_pairs={{0,2},{1,3},{2,0},{3,1},{4,6},{5,7},{6,4},{7,5},{8,10},{9,11},{10,... | collective-permute-start | bytes 983048 | tf_op jit(solution)/shard_map/ppermute | solution.py:34
  88.8 16.1 %collective-permute-start.25 = (bf16[1280,128]{1,0:T(8,128)(2,1)S(1)}, bf16[1280,128]{1,0:T(8,128)(2,1)S(1)}, u32[]{:S(2)}, u32[]{:S(2)}) collective-permute-start(bf16[1280,128]{1,0:T(8,128)(2,1)S(1)} %fusion.16), channel_id=1, source_target_pairs={{0,2},{1,3},{2,0},{3,1},{4,6},{5,7},{6,4},{7,5},{8,10},{9,11},{10,... | collective-permute-start | bytes 983048 | tf_op jit(solution)/shard_map/ppermute | solution.py:34
  92.2 12.7 %collective-permute-start.28 = (bf16[1280,128]{1,0:T(8,128)(2,1)S(1)}, bf16[1280,128]{1,0:T(8,128)(2,1)S(1)}, u32[]{:S(2)}, u32[]{:S(2)}) collective-permute-start(bf16[1280,128]{1,0:T(8,128)(2,1)S(1)} %bitcast.85), channel_id=1, source_target_pairs={{0,1},{1,0},{2,3},{3,2},{4,5},{5,4},{6,7},{7,6},{8,9},{9,8},{10,11... | collective-permute-start | bytes 983048 | tf_op jit(solution)/shard_map/ppermute | solution.py:34
  92.3 15.9 %collective-permute-start.27 = (bf16[1280,128]{1,0:T(8,128)(2,1)S(1)}, bf16[1280,128]{1,0:T(8,128)(2,1)S(1)}, u32[]{:S(2)}, u32[]{:S(2)}) collective-permute-start(bf16[1280,128]{1,0:T(8,128)(2,1)S(1)} %bitcast.83), channel_id=1, source_target_pairs={{0,1},{1,0},{2,3},{3,2},{4,5},{5,4},{6,7},{7,6},{8,9},{9,8},{10,11... | collective-permute-start | bytes 983048 | tf_op jit(solution)/shard_map/ppermute | solution.py:34
  104.9 13.5 %collective-permute-start.23 = (bf16[1280,128]{1,0:T(8,128)(2,1)S(1)}, bf16[1280,128]{1,0:T(8,128)(2,1)S(1)}, u32[]{:S(2)}, u32[]{:S(2)}) collective-permute-start(bf16[1280,128]{1,0:T(8,128)(2,1)S(1)} %bitcast.81), channel_id=1, source_target_pairs={{0,1},{1,0},{2,3},{3,2},{4,5},{5,4},{6,7},{7,6},{8,9},{9,8},{10,11... | collective-permute-start | bytes 983048 | tf_op jit(solution)/shard_map/ppermute | solution.py:34
  105.1 12.1 %collective-permute-start.29 = (bf16[1280,128]{1,0:T(8,128)(2,1)S(1)}, bf16[1280,128]{1,0:T(8,128)(2,1)S(1)}, u32[]{:S(2)}, u32[]{:S(2)}) collective-permute-start(bf16[1280,128]{1,0:T(8,128)(2,1)S(1)} %fusion.3), channel_id=1, source_target_pairs={{0,4},{1,5},{2,6},{3,7},{4,8},{5,9},{6,10},{7,11},{8,12},{9,13},{1... | collective-permute-start | bytes 983048 | tf_op jit(solution)/shard_map/ppermute | solution.py:34
  106.4 12.0 %collective-permute-start.26 = (bf16[1280,128]{1,0:T(8,128)(2,1)S(1)}, bf16[1280,128]{1,0:T(8,128)(2,1)S(1)}, u32[]{:S(2)}, u32[]{:S(2)}) collective-permute-start(bf16[1280,128]{1,0:T(8,128)(2,1)S(1)} %fusion.7), channel_id=1, source_target_pairs={{0,2},{1,3},{2,0},{3,1},{4,6},{5,7},{6,4},{7,5},{8,10},{9,11},{10,... | collective-permute-start | bytes 983048 | tf_op jit(solution)/shard_map/ppermute | solution.py:34
  117.4 11.3 %collective-permute-start.30 = (bf16[1280,128]{1,0:T(8,128)(2,1)S(1)}, bf16[1280,128]{1,0:T(8,128)(2,1)S(1)}, u32[]{:S(2)}, u32[]{:S(2)}) collective-permute-start(bf16[1280,128]{1,0:T(8,128)(2,1)S(1)} %fusion.6), channel_id=1, source_target_pairs={{0,4},{1,5},{2,6},{3,7},{4,8},{5,9},{6,10},{7,11},{8,12},{9,13},{1... | collective-permute-start | bytes 983048 | tf_op jit(solution)/shard_map/ppermute | solution.py:34
  117.4 11.4 %collective-permute-start.19 = (bf16[1280,128]{1,0:T(8,128)(2,1)S(1)}, bf16[1280,128]{1,0:T(8,128)(2,1)S(1)}, u32[]{:S(2)}, u32[]{:S(2)}) collective-permute-start(bf16[1280,128]{1,0:T(8,128)(2,1)S(1)} %bitcast.79), channel_id=1, source_target_pairs={{0,1},{1,0},{2,3},{3,2},{4,5},{5,4},{6,7},{7,6},{8,9},{9,8},{10,11... | collective-permute-start | bytes 983048 | tf_op jit(solution)/shard_map/ppermute | solution.py:34
  117.5 11.4 %collective-permute-start.22 = (bf16[1280,128]{1,0:T(8,128)(2,1)S(1)}, bf16[1280,128]{1,0:T(8,128)(2,1)S(1)}, u32[]{:S(2)}, u32[]{:S(2)}) collective-permute-start(bf16[1280,128]{1,0:T(8,128)(2,1)S(1)} %fusion.11), channel_id=1, source_target_pairs={{0,2},{1,3},{2,0},{3,1},{4,6},{5,7},{6,4},{7,5},{8,10},{9,11},{10,... | collective-permute-start | bytes 983048 | tf_op jit(solution)/shard_map/ppermute | solution.py:34
  128.8 10.4 %collective-permute-start.31 = (bf16[1280,128]{1,0:T(8,128)(2,1)S(1)}, bf16[1280,128]{1,0:T(8,128)(2,1)S(1)}, u32[]{:S(2)}, u32[]{:S(2)}) collective-permute-start(bf16[1280,128]{1,0:T(8,128)(2,1)S(1)} %fusion.10), channel_id=1, source_target_pairs={{0,4},{1,5},{2,6},{3,7},{4,8},{5,9},{6,10},{7,11},{8,12},{9,13},{1... | collective-permute-start | bytes 983048 | tf_op jit(solution)/shard_map/ppermute | solution.py:34

commit v8 on v7

--- a/solution.py
+++ b/solution.py
@@ -35,9 +35,10 @@
 
 
 ALONG = pairs_of(lambda z, x: ((z + 1) % LINE, x))
+BACK = pairs_of(lambda z, x: ((z - 1) % LINE, x))
 ACROSS = pairs_of(lambda z, x: (z, 1 - x))
-ADD_AT = {(2, 1): 0, (3, 1): 1}
-CLEAR_AT = (1, 1)
+ADD_AT = {(3, 1): 0}
+LAY_AT = (2, 1)
 
 
 def spread(parts, meanwhile):
@@ -63,22 +64,34 @@
     def paired(keep, send):
         return keep + move(send, swap).astype(jnp.float32)
 
-    steps = range(LINE - 1, -1, -1)
-    parts = {step: paired(far_keep[step], far_send[step]).astype(jnp.bfloat16) for step in steps}
-    half, parts[3], parts[2] = tie(half, parts[3], parts[2])
-    crossed = []
-    for step in steps:
-        part = parts[step]
-        if len(crossed) > 1:
-            part, crossed[-2] = tie(part, crossed[-2])
-        crossed.append(move(part, ACROSS))
+    order = (2, 1, 3, 0)
+    parts = {step: paired(far_keep[step], far_send[step]).astype(jnp.bfloat16) for step in order}
+    half, parts[2] = tie(half, parts[2])
+    crossed = {2: move(parts[2], ACROSS)}
     near_keep, near_send = near_of(half)
-    total = paired(near_keep[3], near_send[3]) + crossed[0].astype(jnp.float32)
-    for step in (2, 1, 0):
-        arrived = move(total.astype(jnp.bfloat16), ALONG)
-        total = paired(near_keep[step], near_send[step]) + crossed[3 - step].astype(jnp.float32)
-        total = total + arrived.astype(jnp.float32)
-    return total
+    total = {step: paired(near_keep[step], near_send[step]) for step in order}
+    parts[1], total[2] = tie(parts[1], total[2])
+    crossed[1] = move(parts[1], ACROSS)
+    parts[3], crossed[2] = tie(parts[3], crossed[2])
+    crossed[3] = move(parts[3], ACROSS)
+    parts[0], crossed[1] = tie(parts[0], crossed[1])
+    crossed[0] = move(parts[0], ACROSS)
+
+    total = {step: total[step] + crossed[step].astype(jnp.float32) for step in order}
+    two_on = move(total[2].astype(jnp.bfloat16), ALONG)
+    one_on = move((total[1] + two_on.astype(jnp.float32)).astype(jnp.bfloat16), ALONG)
+    one_back = move(total[3].astype(jnp.bfloat16), BACK)
+    return total[0] + one_on.astype(jnp.float32) + one_back.astype(jnp.float32)
+
+
+def clear(half):
+    whole = half.shape[0] // (4 * BLK) * (4 * BLK)
+
+    @pl.loop(0, whole // (4 * BLK))
+    def _(index):
+        half[pl.ds(pl.multiple_of(index * 4 * BLK, BLK), 4 * BLK), :] = jnp.zeros((4 * BLK, LANES), jnp.float32)
+
+    half[pl.ds(whole, half.shape[0] - whole), :] = jnp.zeros((half.shape[0] - whole, LANES), jnp.float32)
 
 
 def add_tiles(stage, pieces, table_ref, bounds_ref, sources, tile_sets, half, occ, sem):
@@ -130,14 +143,19 @@
 def stage_kernel(stage, count, pieces, table_ref, bounds_ref, *refs):
     sources, tile_sets = refs[:count], refs[count : count + 2]
     half, occ, sem = refs[-3:]
+    if stage == 0:
+        clear(half)
     add_tiles(stage, pieces, table_ref, bounds_ref, sources, tile_sets, half, occ, sem)
 
 
 def window_kernel(stage, count, pieces, shard, first, table_ref, bounds_ref, chips_ref, core_ref, *refs):
     sources, tile_sets = refs[:count], refs[count : count + 2]
-    half, weights = refs[count + 3 : count + 5]
-    outs = refs[count + 5 : -2]
+    before = 1 if stage else 0
+    half, weights = refs[count + 2 + before : count + 4 + before]
+    outs = refs[count + 4 + before : -2]
     occ, sem = refs[-2:]
+    if stage == 0:
+        clear(half)
     add_tiles(stage, pieces, table_ref, bounds_ref, sources, tile_sets, half, occ, sem)
     side_rows = (half.shape[0] - BLK) // 2
     for side in range(2):
@@ -236,28 +254,32 @@
 
     half_type = pltpu.VMEM((2 * total + BLK, LANES), jnp.float32)
     work = 4 * slots * BLK * BLK * LANES // stage_count
-    halves = list(call(clear_kernel, [], [], [half_type], [], {}, 0))
+    halves = []
 
     def stage_ins(sources):
         scratch = [
             pltpu.VMEM((len(sources) * sources[0].shape[0], LANES), jnp.bfloat16),
             pltpu.SemaphoreType.DMA,
         ]
-        return [*sources, *map(pinned, tile_sets)], [HBM] * len(sources) + [VMEM] * 2, scratch
+        earlier = [pinned(halves[-1])] if halves else []
+        ins = [*sources, *map(pinned, tile_sets), *earlier]
+        return ins, [HBM] * len(sources) + [VMEM] * (2 + len(earlier)), scratch
+
+    def aliases(ahead, ins):
+        return {ahead + len(ins) - 1: 0} if halves else {}
 
     def add_stage(stage, sources):
         ins, specs, scratch = stage_ins(sources)
-        ins = [ordered, bounds] + ins + [pinned(halves[-1])]
         halves.extend(
             call(
                 functools.partial(stage_kernel, stage, len(sources), pieces),
-                ins, [SMEM] * 2 + specs + [VMEM], [half_type], scratch, {len(ins) - 1: 0}, work,
+                [ordered, bounds] + ins, [SMEM] * 2 + specs, [half_type], scratch, aliases(2, ins), work,
             )
         )
 
     def meanwhile(step, index, arrived, moved):
-        if (step, index) == CLEAR_AT:
-            moved, halves[-1] = tie(moved, halves[-1])
+        if (step, index) == LAY_AT:
+            moved, *tile_sets[:] = tie(moved, *tile_sets)
         if (step, index) in ADD_AT:
             stage = ADD_AT[step, index]
             add_stage(stage, arrived(stage))
@@ -274,15 +296,14 @@
     group = 1 if lined else chips // 2
     far = [group] * (chips // 2 // group)
     ins, specs, scratch = stage_ins(stages[-1])
-    ins = [ordered, bounds, chip_of_slot, cores] + ins + [pinned(halves[-1])]
     half, weights, *far_send = call(
         functools.partial(window_kernel, stage_count - 1, len(stages[-1]), pieces, shard, chips // 2),
-        ins,
-        [SMEM] * 4 + specs + [VMEM],
+        [ordered, bounds, chip_of_slot, cores] + ins,
+        [SMEM] * 4 + specs,
         [half_type, pltpu.VMEM((2 * LANES, WIN), jnp.bfloat16)]
         + [pltpu.VMEM((size, shard, WIN), jnp.bfloat16) for size in far],
         scratch,
-        {len(ins) - 1: 0},
+        aliases(4, ins),
         work + total // 4 * width * WIN * 2,
     )
 
@@ -319,12 +340,6 @@
     return block_sum.astype(jnp.float32) * factor
 
 
-def clear_kernel(half):
-    @pl.loop(0, half.shape[0] // BLK)
-    def _(index):
-        half[pl.ds(pl.multiple_of(index * BLK, BLK), BLK), :] = jnp.zeros((BLK, LANES), jnp.float32)
-
-
 def solution(mesh):
     placed = (
         P(("groups", "aux"), None),

time: 141 us -> 117 us (0.83)
  waiting for transfers between devices: 65.5 us -> 36.6 us
  starting transfers between devices: 24.9 us -> 41.4 us
  local copies, waits for them, and re-layouts: 21.2 us -> 15.4 us
  Pallas kernels: 23.9 us -> 18.8 us
    ppermute x32, waiting for transfers between devices: 65.5 us -> 36.6 us  [move(): return lax.ppermute(array, 'aux', pairs)]
    ppermute x32, starting transfers between devices: 24.9 us -> 41.4 us  [move(): return lax.ppermute(array, 'aux', pairs)]
    pallas_call x8 -> x7, Pallas kernels: 23.9 us -> 18.8 us  [call(): pl.pallas_call(kernel, out_shape=outs, in_specs=in_specs, out_specs=[VMEM...]
    unnamed x6 -> x24, local copies, waits for them, and re-layouts: 18.1 us -> 14 us
  transfers between devices with their start and end apart: 32 -> 32, of which waited for: 12 -> 13; matrix products, arithmetic and copies ran while one was open for 7% -> 9% of each run, Pallas kernels for 15% -> 14%
where the time goes in v8:
time: 117 us
  starting transfers between devices  41.4 us (35%)
  waiting for transfers between devices  36.6 us (31%)
  Pallas kernels  18.8 us (16%)
  local copies, waits for them, and re-layouts  15.4 us (13%)
  other arithmetic  3.69 us (3%)
    ppermute x32, starting transfers between devices, move(): return lax.ppermute(array, 'aux', pairs)  41.4 us
    ppermute x32, waiting for transfers between devices, move(): return lax.ppermute(array, 'aux', pairs)  36.6 us
    pallas_call x7, Pallas kernels, call(): pl.pallas_call(kernel, out_shape=outs, in_specs=in_specs, out_specs=[VMEM...  18.8 us
    unnamed x24, local copies, waits for them, and re-layouts  14 us
  transfers between devices with their start and end apart: 32, of which 13 were waited for; matrix products, arithmetic and copies ran while one was open for 9% of the time, Pallas kernels for 14%

profile of v8, /device:TPU:0, one launch (start us, length us, event | category | flops | bytes accessed | tf_op | source)
XLA Modules:
  0.0 116.9 jit_solution(11133001701856906620)
XLA Ops:
  0.0 0.5 collective-permute-start.13
  1.1 0.8 slice_multiply_fusion.1
  2.0 1.1 constant_dynamic-slice_fusion
  3.1 3.1 %collective-permute-start.1 = (bf16[1280,128]{1,0:T(8,128)(2,1)S(1)}, bf16[1280,128]{1,0:T(8,128)(2,1)S(1)}, u32[]{:S(2)}, u32[]{:S(2)}) collective-permute-start(bf16[1280,128]{1,0:T(8,128)(2,1)S(1)} %get-tuple-element.101.refs_0_), channel_id=1, source_target_pairs={{0,4},{1,5},{2,6},{3,7},{4,8},{5,9},{6,10},{7,11},{8,12},{9,13},{1... | collective-permute-start | bytes 983048 | tf_op jit(solution)/shard_map/ppermute | solution.py:34
  6.2 1.5 %collective-permute-start.2 = (bf16[1280,128]{1,0:T(8,128)(2,1)S(1)}, bf16[1280,128]{1,0:T(8,128)(2,1)S(1)}, u32[]{:S(2)}, u32[]{:S(2)}) collective-permute-start(bf16[1280,128]{1,0:T(8,128)(2,1)S(1)} %get-tuple-element.101.refs_0_), channel_id=1, source_target_pairs={{0,2},{1,3},{2,0},{3,1},{4,6},{5,7},{6,4},{7,5},{8,10},{9,11},{10,... | collective-permute-start | bytes 983048 | tf_op jit(solution)/shard_map/ppermute | solution.py:34
  7.7 3.4 %copy.11 = bf16[32,8,32,128]{3,2,1,0:T(8,128)(2,1)} copy(bf16[32,8,32,128]{3,1,2,0:T(8,128)(2,1)} %bitcast.83) | data formatting | bytes 4194304
  11.2 0.6 collective-permute-start.10
  11.8 1.6 %collective-permute-start.9 = (bf16[1280,128]{1,0:T(8,128)(2,1)S(1)}, bf16[1280,128]{1,0:T(8,128)(2,1)S(1)}, u32[]{:S(2)}, u32[]{:S(2)}) collective-permute-start(bf16[1280,128]{1,0:T(8,128)(2,1)S(1)} %collective-permute-done.8.refs_1_), channel_id=1, source_target_pairs={{0,4},{1,5},{2,6},{3,7},{4,8},{5,9},{6,10},{7,11},{8,12},{9,13},{1... | collective-permute-start | bytes 983048 | tf_op jit(solution)/shard_map/ppermute | solution.py:34
  13.4 0.7 copy-done.9
  14.2 2.0 %collective-permute-done.1.refs_0_ = bf16[1280,128]{1,0:T(8,128)(2,1)S(1)} collective-permute-done((bf16[1280,128]{1,0:T(8,128)(2,1)S(1)}, bf16[1280,128]{1,0:T(8,128)(2,1)S(1)}, u32[]{:S(2)}, u32[]{:S(2)}) %collective-permute-start.1) | collective-permute-done | bytes 327712 | tf_op jit(solution)/shard_map/ppermute | solution.py:34
  16.2 0.6 collective-permute-done.2.refs_2_
  16.7 1.6 %collective-permute-start.3 = (bf16[1280,128]{1,0:T(8,128)(2,1)S(1)}, bf16[1280,128]{1,0:T(8,128)(2,1)S(1)}, u32[]{:S(2)}, u32[]{:S(2)}) collective-permute-start(bf16[1280,128]{1,0:T(8,128)(2,1)S(1)} %collective-permute-done.1.refs_0_), channel_id=1, source_target_pairs={{0,4},{1,5},{2,6},{3,7},{4,8},{5,9},{6,10},{7,11},{8,12},{9,13},{1... | collective-permute-start | bytes 983048 | tf_op jit(solution)/shard_map/ppermute | solution.py:34
  18.3 1.6 %collective-permute-start.4 = (bf16[1280,128]{1,0:T(8,128)(2,1)S(1)}, bf16[1280,128]{1,0:T(8,128)(2,1)S(1)}, u32[]{:S(2)}, u32[]{:S(2)}) collective-permute-start(bf16[1280,128]{1,0:T(8,128)(2,1)S(1)} %collective-permute-done.1.refs_0_), channel_id=1, source_target_pairs={{0,2},{1,3},{2,0},{3,1},{4,6},{5,7},{6,4},{7,5},{8,10},{9,11},{10,... | collective-permute-start | bytes 983048 | tf_op jit(solution)/shard_map/ppermute | solution.py:34
  19.9 3.9 %collective-permute-done.10.refs_3_ = bf16[1280,128]{1,0:T(8,128)(2,1)S(1)} collective-permute-done((bf16[1280,128]{1,0:T(8,128)(2,1)S(1)}, bf16[1280,128]{1,0:T(8,128)(2,1)S(1)}, u32[]{:S(2)}, u32[]{:S(2)}) %collective-permute-start.10) | collective-permute-done | bytes 327712 | tf_op jit(solution)/shard_map/ppermute | solution.py:34
  23.7 0.4 collective-permute-done.9.refs_1_
  24.2 1.2 collective-permute-start.11
  25.3 1.6 %collective-permute-start.12 = (bf16[1280,128]{1,0:T(8,128)(2,1)S(1)}, bf16[1280,128]{1,0:T(8,128)(2,1)S(1)}, u32[]{:S(2)}, u32[]{:S(2)}) collective-permute-start(bf16[1280,128]{1,0:T(8,128)(2,1)S(1)} %collective-permute-done.9.refs_1_), channel_id=1, source_target_pairs={{0,2},{1,3},{2,0},{3,1},{4,6},{5,7},{6,4},{7,5},{8,10},{9,11},{10,... | collective-permute-start | bytes 983048 | tf_op jit(solution)/shard_map/ppermute | solution.py:34
  26.9 0.3 convert_reduce_fusion
  27.3 3.9 %collective-permute-done.3.refs_0_ = bf16[1280,128]{1,0:T(8,128)(2,1)S(1)} collective-permute-done((bf16[1280,128]{1,0:T(8,128)(2,1)S(1)}, bf16[1280,128]{1,0:T(8,128)(2,1)S(1)}, u32[]{:S(2)}, u32[]{:S(2)}) %collective-permute-start.3) | collective-permute-done | bytes 327712 | tf_op jit(solution)/shard_map/ppermute | solution.py:34
  31.2 0.7 copy-done.3
  31.9 1.1 collective-permute-start.5
  33.0 1.6 %collective-permute-start.6 = (bf16[1280,128]{1,0:T(8,128)(2,1)S(1)}, bf16[1280,128]{1,0:T(8,128)(2,1)S(1)}, u32[]{:S(2)}, u32[]{:S(2)}) collective-permute-start(bf16[1280,128]{1,0:T(8,128)(2,1)S(1)} %collective-permute-done.3.refs_0_), channel_id=1, source_target_pairs={{0,2},{1,3},{2,0},{3,1},{4,6},{5,7},{6,4},{7,5},{8,10},{9,11},{10,... | collective-permute-start | bytes 983048 | tf_op jit(solution)/shard_map/ppermute | solution.py:34
  34.6 3.7 %collective-permute-done.11.refs_1_ = bf16[1280,128]{1,0:T(8,128)(2,1)} collective-permute-done((bf16[1280,128]{1,0:T(8,128)(2,1)S(1)}, bf16[1280,128]{1,0:T(8,128)(2,1)}, u32[]{:S(2)}, u32[]{:S(2)}) %collective-permute-start.11) | collective-permute-done | bytes 327712 | tf_op jit(solution)/shard_map/ppermute | solution.py:34
  38.3 0.8 copy-done.5
  39.1 3.4 %copy.12 = bf16[32,8,32,128]{3,2,1,0:T(8,128)(2,1)} copy(bf16[32,8,32,128]{3,1,2,0:T(8,128)(2,1)} %bitcast.27) | data formatting | bytes 4194304
  42.5 1.0 collective-permute-start.14
  43.6 1.6 %collective-permute-start.15 = (bf16[1280,128]{1,0:T(8,128)(2,1)}, bf16[1280,128]{1,0:T(8,128)(2,1)}, u32[]{:S(2)}, u32[]{:S(2)}) collective-permute-start(bf16[1280,128]{1,0:T(8,128)(2,1)} %collective-permute-done.11.refs_1_), channel_id=1, source_target_pairs={{0,2},{1,3},{2,0},{3,1},{4,6},{5,7},{6,4},{7,5},{8,10},{9,11},{10,... | collective-permute-start | bytes 983048 | tf_op jit(solution)/shard_map/ppermute | solution.py:34
  45.2 0.5 select_reduce_fusion.2
  45.9 0.2 reshape.224.table_ref
  46.3 0.7 copy-done.7
  47.0 0.4 collective-permute-start.7
  47.4 1.6 %copy-done = bf16[32,8,32,128]{3,2,1,0:T(8,128)(2,1)S(1)} copy-done((bf16[32,8,32,128]{3,2,1,0:T(8,128)(2,1)S(1)}, bf16[32,8,32,128]{3,2,1,0:T(8,128)(2,1)}, u32[]{:S(2)}) %copy-start) | copy-done | bytes 2097176
  49.0 1.6 %copy-done.2 = bf16[32,8,32,128]{3,2,1,0:T(8,128)(2,1)S(1)} copy-done((bf16[32,8,32,128]{3,2,1,0:T(8,128)(2,1)S(1)}, bf16[32,8,32,128]{3,2,1,0:T(8,128)(2,1)}, u32[]{:S(2)}) %copy-start.2) | copy-done | bytes 2097176
  50.6 1.0 copy-done.10
  51.6 3.3 %shard_map.46.refs_6_ = f32[41024,128]{1,0:T(8,128)S(1)} custom-call(s32[1560]{0:T(1024)S(1)} %reshape.224.table_ref, s32[6]{0:T(128)S(1)} %convert_reduce_fusion.1.bounds_ref, bf16[1280,128]{1,0:T(8,128)(2,1)S(1)} %get-tuple-element.101.refs_0_, bf16[1280,128]{1,0:T(8,128)(2,1)S(1)} %copy-done.10, bf16[256,32,128]{2,1,0:T(8,128)(2,1)S(1)} %bitcast.65, ...), custom_call_target="tpu_custom_call" | custom-call | flops 107374184 | bytes 4194304 | tf_op jit(solution)/shard_map/pallas_call | solution.py:183
  54.9 2.1 %collective-permute-start.16 = (bf16[1280,128]{1,0:T(8,128)(2,1)}, bf16[1280,128]{1,0:T(8,128)(2,1)S(1)}, u32[]{:S(2)}, u32[]{:S(2)}) collective-permute-start(bf16[1280,128]{1,0:T(8,128)(2,1)} %collective-permute-done.14.refs_1_), channel_id=1, source_target_pairs={{0,2},{1,3},{2,0},{3,1},{4,6},{5,7},{6,4},{7,5},{8,10},{9,11},{10,... | collective-permute-start | bytes 983048 | tf_op jit(solution)/shard_map/ppermute | solution.py:34
  57.1 2.6 %shard_map.47.refs_6_ = f32[41024,128]{1,0:T(8,128)S(1)} custom-call(s32[1560]{0:T(1024)S(1)} %reshape.224.table_ref, s32[6]{0:T(128)S(1)} %convert_reduce_fusion.1.bounds_ref, bf16[1280,128]{1,0:T(8,128)(2,1)S(1)} %collective-permute-done.1.refs_0_, bf16[1280,128]{1,0:T(8,128)(2,1)S(1)} %collective-permute-done.9.refs_1_, ...), custom_call_target="tpu_custom_call", output_to_operand_aliasing={{}: (8, {})} | custom-call | flops 107374184 | bytes 4194304 | tf_op jit(solution)/shard_map/pallas_call | solution.py:183
  59.7 3.4 %shard_map.48.refs_6_ = f32[41024,128]{1,0:T(8,128)S(1)} custom-call(s32[1560]{0:T(1024)S(1)} %reshape.224.table_ref, s32[6]{0:T(128)S(1)} %convert_reduce_fusion.1.bounds_ref, bf16[1280,128]{1,0:T(8,128)(2,1)S(1)} %collective-permute-done.3.refs_0_, bf16[1280,128]{1,0:T(8,128)(2,1)} %collective-permute-done.11.refs_1_, ...), custom_call_target="tpu_custom_call", output_to_operand_aliasing={{}: (8, {})} | custom-call | flops 107374184 | bytes 4194304 | tf_op jit(solution)/shard_map/pallas_call | solution.py:183
  63.1 3.3 %shard_map.49.refs_4_ = f32[41024,128]{1,0:T(8,128)S(1)} custom-call(s32[1560]{0:T(1024)S(1)} %reshape.224.table_ref, s32[6]{0:T(128)S(1)} %convert_reduce_fusion.1.bounds_ref, bf16[1280,128]{1,0:T(8,128)(2,1)} %collective-permute-done.5.refs_0_, bf16[1280,128]{1,0:T(8,128)(2,1)} %collective-permute-done.14.refs_1_, ...), custom_call_target="tpu_custom_call", output_to_operand_aliasing={{}: (8, {})} | custom-call | flops 107374184 | bytes 4194304 | tf_op jit(solution)/shard_map/pallas_call | solution.py:183
  66.5 2.7 %shard_map.50 = (f32[41024,128]{1,0:T(8,128)S(1)}, bf16[256,128]{1,0:T(8,128)(2,1)S(1)}, bf16[1,1280,128]{2,1,0:T(8,128)(2,1)S(1)}, bf16[1,1280,128]{2,1,0:T(8,1...) custom-call(s32[1560]{0:T(1024)S(1)} %reshape.224.table_ref, ...), custom_call_target="tpu_custom_call", output_to_operand_aliasing={{0}: (8, {})} | custom-call | flops 442918496 | bytes 4194304 | tf_op jit(solution)/shard_map/pallas_call | solution.py:183
  69.3 0.5 collective-permute-start.19
  69.9 0.4 collective-permute-start.25
  70.3 1.4 %shard_map.51 = (f32[1,1280,128]{2,1,0:T(8,128)S(1)}, f32[1,1280,128]{2,1,0:T(8,128)S(1)}, f32[1,1280,128]{2,1,0:T(8,128)S(1)}, f32[1,1280,128]{2,1,0:T(8,128)S(1)}) custom-call(s32[8]{0:T(128)S(1)} %fusion.33.chips_ref, s32[1]{0:T(128)} %bitcast.core_ref, f32[41024,128]{1,0:T(8,128)S(1)} %get-tuple-element.69.half, ...), custom_call_target="tpu_custom_call" | custom-call | flops 335544320 | bytes 4194304 | tf_op jit(solution)/shard_map/pallas_call | solution.py:183
  71.7 2.1 %shard_map.52 = (f32[1,1280,128]{2,1,0:T(8,128)S(1)}, f32[1,1280,128]{2,1,0:T(8,128)S(1)}, f32[1,1280,128]{2,1,0:T(8,128)S(1)}, f32[1,1280,128]{2,1,0:T(8,128)S(...) custom-call(s32[8]{0:T(128)S(1)} %fusion.33.chips_ref, ...), custom_call_target="tpu_custom_call" | custom-call | flops 335544320 | bytes 4194304 | tf_op jit(solution)/shard_map/pallas_call | solution.py:183
  73.8 0.1 collective-permute-start.21
  74.0 3.4 %collective-permute-start.26 = (bf16[1280,128]{1,0:T(8,128)(2,1)S(1)}, bf16[1280,128]{1,0:T(8,128)(2,1)S(1)}, u32[]{:S(2)}, u32[]{:S(2)}) collective-permute-start(bf16[1280,128]{1,0:T(8,128)(2,1)S(1)} %fusion.14), channel_id=1, source_target_pairs={{0,2},{1,3},{2,0},{3,1},{4,6},{5,7},{6,4},{7,5},{8,10},{9,11},{10,... | collective-permute-start | bytes 983048 | tf_op jit(solution)/shard_map/ppermute | solution.py:34
  77.4 0.2 collective-permute-start.24
  77.7 0.4 collective-permute-start.29
  78.2 0.2 collective-permute-start.18
  78.4 7.2 %collective-permute-done.26 = bf16[1280,128]{1,0:T(8,128)(2,1)S(1)} collective-permute-done((bf16[1280,128]{1,0:T(8,128)(2,1)S(1)}, bf16[1280,128]{1,0:T(8,128)(2,1)S(1)}, u32[]{:S(2)}, u32[]{:S(2)}) %collective-permute-start.26) | collective-permute-done | bytes 327712 | tf_op jit(solution)/shard_map/ppermute | solution.py:34
  85.7 1.8 %collective-permute-start.22 = (bf16[1280,128]{1,0:T(8,128)(2,1)S(1)}, bf16[1280,128]{1,0:T(8,128)(2,1)S(1)}, u32[]{:S(2)}, u32[]{:S(2)}) collective-permute-start(bf16[1280,128]{1,0:T(8,128)(2,1)S(1)} %fusion.8), channel_id=1, source_target_pairs={{0,2},{1,3},{2,0},{3,1},{4,6},{5,7},{6,4},{7,5},{8,10},{9,11},{10,... | collective-permute-start | bytes 983048 | tf_op jit(solution)/shard_map/ppermute | solution.py:34
  87.5 4.6 %collective-permute-start.27 = (bf16[1280,128]{1,0:T(8,128)(2,1)S(1)}, bf16[1280,128]{1,0:T(8,128)(2,1)S(1)}, u32[]{:S(2)}, u32[]{:S(2)}) collective-permute-start(bf16[1280,128]{1,0:T(8,128)(2,1)S(1)} %add_convert_fusion), channel_id=1, source_target_pairs={{0,4},{1,5},{2,6},{3,7},{4,8},{5,9},{6,10},{7,11},{8,12},{9,13},{1... | collective-permute-start | bytes 983048 | tf_op jit(solution)/shard_map/ppermute | solution.py:34
  92.2 2.9 %collective-permute-done.22 = bf16[1280,128]{1,0:T(8,128)(2,1)S(1)} collective-permute-done((bf16[1280,128]{1,0:T(8,128)(2,1)S(1)}, bf16[1280,128]{1,0:T(8,128)(2,1)S(1)}, u32[]{:S(2)}, u32[]{:S(2)}) %collective-permute-start.22) | collective-permute-done | bytes 327712 | tf_op jit(solution)/shard_map/ppermute | solution.py:34
  95.2 1.6 %collective-permute-start.30 = (bf16[1280,128]{1,0:T(8,128)(2,1)S(1)}, bf16[1280,128]{1,0:T(8,128)(2,1)S(1)}, u32[]{:S(2)}, u32[]{:S(2)}) collective-permute-start(bf16[1280,128]{1,0:T(8,128)(2,1)S(1)} %fusion.4), channel_id=1, source_target_pairs={{0,2},{1,3},{2,0},{3,1},{4,6},{5,7},{6,4},{7,5},{8,10},{9,11},{10,... | collective-permute-start | bytes 983048 | tf_op jit(solution)/shard_map/ppermute | solution.py:34
  96.7 1.9 %collective-permute-done.27 = bf16[1280,128]{1,0:T(8,128)(2,1)S(1)} collective-permute-done((bf16[1280,128]{1,0:T(8,128)(2,1)S(1)}, bf16[1280,128]{1,0:T(8,128)(2,1)S(1)}, u32[]{:S(2)}, u32[]{:S(2)}) %collective-permute-start.27) | collective-permute-done | bytes 327712 | tf_op jit(solution)/shard_map/ppermute | solution.py:34
  98.6 0.2 fusion.7
  98.8 2.7 %collective-permute-start.28 = (bf16[1280,128]{1,0:T(8,128)(2,1)S(1)}, bf16[1280,128]{1,0:T(8,128)(2,1)S(1)}, u32[]{:S(2)}, u32[]{:S(2)}) collective-permute-start(bf16[1280,128]{1,0:T(8,128)(2,1)S(1)} %fusion.7), channel_id=1, source_target_pairs={{0,4},{1,5},{2,6},{3,7},{4,8},{5,9},{6,10},{7,11},{8,12},{9,13},{1... | collective-permute-start | bytes 983048 | tf_op jit(solution)/shard_map/ppermute | solution.py:34
  101.5 0.7 collective-permute-start.23
  102.2 2.9 %collective-permute-done.30 = bf16[1280,128]{1,0:T(8,128)(2,1)S(1)} collective-permute-done((bf16[1280,128]{1,0:T(8,128)(2,1)S(1)}, bf16[1280,128]{1,0:T(8,128)(2,1)S(1)}, u32[]{:S(2)}, u32[]{:S(2)}) %collective-permute-start.30) | collective-permute-done | bytes 327712 | tf_op jit(solution)/shard_map/ppermute | solution.py:34
  105.3 3.4 %collective-permute-start.31 = (bf16[1280,128]{1,0:T(8,128)(2,1)S(1)}, bf16[1280,128]{1,0:T(8,128)(2,1)S(1)}, u32[]{:S(2)}, u32[]{:S(2)}) collective-permute-start(bf16[1280,128]{1,0:T(8,128)(2,1)S(1)} %fusion.3), channel_id=1, source_target_pairs={{0,12},{1,13},{2,14},{3,15},{4,0},{5,1},{6,2},{7,3},{8,4},{9,5},{1... | collective-permute-start | bytes 983048 | tf_op jit(solution)/shard_map/ppermute | solution.py:34
  108.7 0.9 collective-permute-done.28
  109.7 1.1 collective-permute-done.23
  110.8 5.1 %collective-permute-done.31 = bf16[1280,128]{1,0:T(8,128)(2,1)S(1)} collective-permute-done((bf16[1280,128]{1,0:T(8,128)(2,1)S(1)}, bf16[1280,128]{1,0:T(8,128)(2,1)S(1)}, u32[]{:S(2)}, u32[]{:S(2)}) %collective-permute-start.31) | collective-permute-done | bytes 327712 | tf_op jit(solution)/shard_map/ppermute | solution.py:34
  115.9 1.0 fusion.13
  (61 shorter events, 1.4 us)
Async XLA Ops:
  0.0 39.1 %collective-permute-start.13 = (bf16[256,4096]{1,0:T(8,128)(2,1)}, bf16[256,4096]{1,0:T(8,128)(2,1)}, u32[]{:S(2)}, u32[]{:S(2)}) collective-permute-start(bf16[256,4096]{1,0:T(8,128)(2,1)} %param.4), channel_id=1, source_target_pairs={{0,1},{1,0},{2,3},{3,2},{4,5},{5,4},{6,7},{7,6},{8,9},{9,8},{10,11... | collective-permute-start | bytes 6291464 | tf_op jit(solution)/shard_map/ppermute | solution.py:34
  1.9 9.2 %collective-permute-start = (s32[2,256]{1,0:T(2,128)S(1)}, s32[2,256]{1,0:T(2,128)S(1)}, u32[]{:S(2)}, u32[]{:S(2)}) collective-permute-start(s32[2,256]{1,0:T(2,128)S(1)} %pad_add_fusion.2), channel_id=1, source_target_pairs={{0,1},{1,0},{2,3},{3,2},{4,5},{5,4},{6,7},{7,6},{8,9},{9,8},{10,11... | collective-permute-start | bytes 6152 | tf_op jit(solution)/shard_map/ppermute | solution.py:34
  3.1 13.0 %collective-permute-start.1 = (bf16[1280,128]{1,0:T(8,128)(2,1)S(1)}, bf16[1280,128]{1,0:T(8,128)(2,1)S(1)}, u32[]{:S(2)}, u32[]{:S(2)}) collective-permute-start(bf16[1280,128]{1,0:T(8,128)(2,1)S(1)} %get-tuple-element.101.refs_0_), channel_id=1, source_target_pairs={{0,4},{1,5},{2,6},{3,7},{4,8},{5,9},{6,10},{7,11},{8,12},{9,13},{1... | collective-permute-start | bytes 983048 | tf_op jit(solution)/shard_map/ppermute | solution.py:34
  6.2 10.5 %collective-permute-start.2 = (bf16[1280,128]{1,0:T(8,128)(2,1)S(1)}, bf16[1280,128]{1,0:T(8,128)(2,1)S(1)}, u32[]{:S(2)}, u32[]{:S(2)}) collective-permute-start(bf16[1280,128]{1,0:T(8,128)(2,1)S(1)} %get-tuple-element.101.refs_0_), channel_id=1, source_target_pairs={{0,2},{1,3},{2,0},{3,1},{4,6},{5,7},{6,4},{7,5},{8,10},{9,11},{10,... | collective-permute-start | bytes 983048 | tf_op jit(solution)/shard_map/ppermute | solution.py:34
  7.7 3.5 %collective-permute-start.8 = (bf16[1280,128]{1,0:T(8,128)(2,1)S(1)}, bf16[1280,128]{1,0:T(8,128)(2,1)S(1)}, u32[]{:S(2)}, u32[]{:S(2)}) collective-permute-start(bf16[1280,128]{1,0:T(8,128)(2,1)S(1)} %get-tuple-element.100), channel_id=1, source_target_pairs={{0,1},{1,0},{2,3},{3,2},{4,5},{5,4},{6,7},{7,6},{8,9},{9,8},{10,11... | collective-permute-start | bytes 983048 | tf_op jit(solution)/shard_map/ppermute | solution.py:34
  11.2 12.5 %collective-permute-start.10 = (bf16[1280,128]{1,0:T(8,128)(2,1)S(1)}, bf16[1280,128]{1,0:T(8,128)(2,1)S(1)}, u32[]{:S(2)}, u32[]{:S(2)}) collective-permute-start(bf16[1280,128]{1,0:T(8,128)(2,1)S(1)} %collective-permute-done.8.refs_1_), channel_id=1, source_target_pairs={{0,2},{1,3},{2,0},{3,1},{4,6},{5,7},{6,4},{7,5},{8,10},{9,11},{10,... | collective-permute-start | bytes 983048 | tf_op jit(solution)/shard_map/ppermute | solution.py:34
  11.8 12.3 %collective-permute-start.9 = (bf16[1280,128]{1,0:T(8,128)(2,1)S(1)}, bf16[1280,128]{1,0:T(8,128)(2,1)S(1)}, u32[]{:S(2)}, u32[]{:S(2)}) collective-permute-start(bf16[1280,128]{1,0:T(8,128)(2,1)S(1)} %collective-permute-done.8.refs_1_), channel_id=1, source_target_pairs={{0,4},{1,5},{2,6},{3,7},{4,8},{5,9},{6,10},{7,11},{8,12},{9,13},{1... | collective-permute-start | bytes 983048 | tf_op jit(solution)/shard_map/ppermute | solution.py:34
  13.4 0.7 copy-start.9
  16.7 14.5 %collective-permute-start.3 = (bf16[1280,128]{1,0:T(8,128)(2,1)S(1)}, bf16[1280,128]{1,0:T(8,128)(2,1)S(1)}, u32[]{:S(2)}, u32[]{:S(2)}) collective-permute-start(bf16[1280,128]{1,0:T(8,128)(2,1)S(1)} %collective-permute-done.1.refs_0_), channel_id=1, source_target_pairs={{0,4},{1,5},{2,6},{3,7},{4,8},{5,9},{6,10},{7,11},{8,12},{9,13},{1... | collective-permute-start | bytes 983048 | tf_op jit(solution)/shard_map/ppermute | solution.py:34
  18.3 12.9 %collective-permute-start.4 = (bf16[1280,128]{1,0:T(8,128)(2,1)S(1)}, bf16[1280,128]{1,0:T(8,128)(2,1)S(1)}, u32[]{:S(2)}, u32[]{:S(2)}) collective-permute-start(bf16[1280,128]{1,0:T(8,128)(2,1)S(1)} %collective-permute-done.1.refs_0_), channel_id=1, source_target_pairs={{0,2},{1,3},{2,0},{3,1},{4,6},{5,7},{6,4},{7,5},{8,10},{9,11},{10,... | collective-permute-start | bytes 983048 | tf_op jit(solution)/shard_map/ppermute | solution.py:34
  24.2 14.1 %collective-permute-start.11 = (bf16[1280,128]{1,0:T(8,128)(2,1)S(1)}, bf16[1280,128]{1,0:T(8,128)(2,1)}, u32[]{:S(2)}, u32[]{:S(2)}) collective-permute-start(bf16[1280,128]{1,0:T(8,128)(2,1)S(1)} %collective-permute-done.9.refs_1_), channel_id=1, source_target_pairs={{0,4},{1,5},{2,6},{3,7},{4,8},{5,9},{6,10},{7,11},{8,12},{9,13},{1... | collective-permute-start | bytes 983048 | tf_op jit(solution)/shard_map/ppermute | solution.py:34
  25.3 13.0 %collective-permute-start.12 = (bf16[1280,128]{1,0:T(8,128)(2,1)S(1)}, bf16[1280,128]{1,0:T(8,128)(2,1)S(1)}, u32[]{:S(2)}, u32[]{:S(2)}) collective-permute-start(bf16[1280,128]{1,0:T(8,128)(2,1)S(1)} %collective-permute-done.9.refs_1_), channel_id=1, source_target_pairs={{0,2},{1,3},{2,0},{3,1},{4,6},{5,7},{6,4},{7,5},{8,10},{9,11},{10,... | collective-permute-start | bytes 983048 | tf_op jit(solution)/shard_map/ppermute | solution.py:34
  31.2 0.7 copy-start.3
  31.9 14.4 %collective-permute-start.5 = (bf16[1280,128]{1,0:T(8,128)(2,1)S(1)}, bf16[1280,128]{1,0:T(8,128)(2,1)}, u32[]{:S(2)}, u32[]{:S(2)}) collective-permute-start(bf16[1280,128]{1,0:T(8,128)(2,1)S(1)} %collective-permute-done.3.refs_0_), channel_id=1, source_target_pairs={{0,4},{1,5},{2,6},{3,7},{4,8},{5,9},{6,10},{7,11},{8,12},{9,13},{1... | collective-permute-start | bytes 983048 | tf_op jit(solution)/shard_map/ppermute | solution.py:34
  33.0 13.2 %collective-permute-start.6 = (bf16[1280,128]{1,0:T(8,128)(2,1)S(1)}, bf16[1280,128]{1,0:T(8,128)(2,1)S(1)}, u32[]{:S(2)}, u32[]{:S(2)}) collective-permute-start(bf16[1280,128]{1,0:T(8,128)(2,1)S(1)} %collective-permute-done.3.refs_0_), channel_id=1, source_target_pairs={{0,2},{1,3},{2,0},{3,1},{4,6},{5,7},{6,4},{7,5},{8,10},{9,11},{10,... | collective-permute-start | bytes 983048 | tf_op jit(solution)/shard_map/ppermute | solution.py:34
  38.3 0.8 copy-start.5
  42.5 12.4 %collective-permute-start.14 = (bf16[1280,128]{1,0:T(8,128)(2,1)}, bf16[1280,128]{1,0:T(8,128)(2,1)}, u32[]{:S(2)}, u32[]{:S(2)}) collective-permute-start(bf16[1280,128]{1,0:T(8,128)(2,1)} %collective-permute-done.11.refs_1_), channel_id=1, source_target_pairs={{0,4},{1,5},{2,6},{3,7},{4,8},{5,9},{6,10},{7,11},{8,12},{9,13},{1... | collective-permute-start | bytes 983048 | tf_op jit(solution)/shard_map/ppermute | solution.py:34
  43.6 11.4 %collective-permute-start.15 = (bf16[1280,128]{1,0:T(8,128)(2,1)}, bf16[1280,128]{1,0:T(8,128)(2,1)}, u32[]{:S(2)}, u32[]{:S(2)}) collective-permute-start(bf16[1280,128]{1,0:T(8,128)(2,1)} %collective-permute-done.11.refs_1_), channel_id=1, source_target_pairs={{0,2},{1,3},{2,0},{3,1},{4,6},{5,7},{6,4},{7,5},{8,10},{9,11},{10,... | collective-permute-start | bytes 983048 | tf_op jit(solution)/shard_map/ppermute | solution.py:34
  46.3 0.7 copy-start.7
  47.0 19.5 %collective-permute-start.7 = (bf16[1280,128]{1,0:T(8,128)(2,1)}, bf16[1280,128]{1,0:T(8,128)(2,1)S(1)}, u32[]{:S(2)}, u32[]{:S(2)}) collective-permute-start(bf16[1280,128]{1,0:T(8,128)(2,1)} %collective-permute-done.5.refs_0_), channel_id=1, source_target_pairs={{0,2},{1,3},{2,0},{3,1},{4,6},{5,7},{6,4},{7,5},{8,10},{9,11},{10,... | collective-permute-start | bytes 983048 | tf_op jit(solution)/shard_map/ppermute | solution.py:34
  47.4 1.6 %copy-start = (bf16[32,8,32,128]{3,2,1,0:T(8,128)(2,1)S(1)}, bf16[32,8,32,128]{3,2,1,0:T(8,128)(2,1)}, u32[]{:S(2)}) copy-start(bf16[32,8,32,128]{3,2,1,0:T(8,128)(2,1)} %copy.11) | copy-start | bytes 6291460
  49.0 1.6 %copy-start.2 = (bf16[32,8,32,128]{3,2,1,0:T(8,128)(2,1)S(1)}, bf16[32,8,32,128]{3,2,1,0:T(8,128)(2,1)}, u32[]{:S(2)}) copy-start(bf16[32,8,32,128]{3,2,1,0:T(8,128)(2,1)} %copy.12) | copy-start | bytes 6291460
  50.6 1.0 copy-start.10
  51.6 5.5 %copy-start.1 = (bf16[32,8,32,128]{3,2,1,0:T(8,128)(2,1)S(1)}, bf16[32,8,32,128]{3,2,1,0:T(8,128)(2,1)}, u32[]{:S(2)}) copy-start(bf16[32,8,32,128]{3,2,1,0:T(8,128)(2,1)} %copy.11) | copy-start | bytes 6291460
  54.9 11.5 %collective-permute-start.16 = (bf16[1280,128]{1,0:T(8,128)(2,1)}, bf16[1280,128]{1,0:T(8,128)(2,1)S(1)}, u32[]{:S(2)}, u32[]{:S(2)}) collective-permute-start(bf16[1280,128]{1,0:T(8,128)(2,1)} %collective-permute-done.14.refs_1_), channel_id=1, source_target_pairs={{0,2},{1,3},{2,0},{3,1},{4,6},{5,7},{6,4},{7,5},{8,10},{9,11},{10,... | collective-permute-start | bytes 983048 | tf_op jit(solution)/shard_map/ppermute | solution.py:34
  57.0 2.6 %copy-start.4 = (bf16[1280,128]{1,0:T(8,128)(2,1)S(1)}, bf16[1280,128]{1,0:T(8,128)(2,1)}, u32[]{:S(2)}) copy-start(bf16[1280,128]{1,0:T(8,128)(2,1)} %copy-done.3) | copy-start | bytes 983044
  57.1 2.6 %copy-start.6 = (bf16[1280,128]{1,0:T(8,128)(2,1)S(1)}, bf16[1280,128]{1,0:T(8,128)(2,1)}, u32[]{:S(2)}) copy-start(bf16[1280,128]{1,0:T(8,128)(2,1)} %copy-done.5) | copy-start | bytes 983044
  59.7 3.5 %copy-start.8 = (bf16[1280,128]{1,0:T(8,128)(2,1)S(1)}, bf16[1280,128]{1,0:T(8,128)(2,1)}, u32[]{:S(2)}) copy-start(bf16[1280,128]{1,0:T(8,128)(2,1)} %copy-done.7) | copy-start | bytes 983044
  69.2 2.5 %collective-permute-start.17 = (bf16[1280,128]{1,0:T(8,128)(2,1)S(1)}, bf16[1280,128]{1,0:T(8,128)(2,1)S(1)}, u32[]{:S(2)}, u32[]{:S(2)}) collective-permute-start(bf16[1280,128]{1,0:T(8,128)(2,1)S(1)} %bitcast.82), channel_id=1, source_target_pairs={{0,1},{1,0},{2,3},{3,2},{4,5},{5,4},{6,7},{7,6},{8,9},{9,8},{10,11... | collective-permute-start | bytes 983048 | tf_op jit(solution)/shard_map/ppermute | solution.py:34
  69.3 18.2 %collective-permute-start.19 = (bf16[1280,128]{1,0:T(8,128)(2,1)S(1)}, bf16[1280,128]{1,0:T(8,128)(2,1)S(1)}, u32[]{:S(2)}, u32[]{:S(2)}) collective-permute-start(bf16[1280,128]{1,0:T(8,128)(2,1)S(1)} %bitcast.76), channel_id=1, source_target_pairs={{0,1},{1,0},{2,3},{3,2},{4,5},{5,4},{6,7},{7,6},{8,9},{9,8},{10,11... | collective-permute-start | bytes 983048 | tf_op jit(solution)/shard_map/ppermute | solution.py:34
  69.8 7.6 %collective-permute-start.20 = (bf16[1280,128]{1,0:T(8,128)(2,1)S(1)}, bf16[1280,128]{1,0:T(8,128)(2,1)S(1)}, u32[]{:S(2)}, u32[]{:S(2)}) collective-permute-start(bf16[1280,128]{1,0:T(8,128)(2,1)S(1)} %bitcast.80), channel_id=1, source_target_pairs={{0,1},{1,0},{2,3},{3,2},{4,5},{5,4},{6,7},{7,6},{8,9},{9,8},{10,11... | collective-permute-start | bytes 983048 | tf_op jit(solution)/shard_map/ppermute | solution.py:34
  69.9 7.8 %collective-permute-start.25 = (bf16[1280,128]{1,0:T(8,128)(2,1)S(1)}, bf16[1280,128]{1,0:T(8,128)(2,1)S(1)}, u32[]{:S(2)}, u32[]{:S(2)}) collective-permute-start(bf16[1280,128]{1,0:T(8,128)(2,1)S(1)} %bitcast.79), channel_id=1, source_target_pairs={{0,1},{1,0},{2,3},{3,2},{4,5},{5,4},{6,7},{7,6},{8,9},{9,8},{10,11... | collective-permute-start | bytes 983048 | tf_op jit(solution)/shard_map/ppermute | solution.py:34
  73.8 4.3 %collective-permute-start.21 = (bf16[1280,128]{1,0:T(8,128)(2,1)S(1)}, bf16[1280,128]{1,0:T(8,128)(2,1)S(1)}, u32[]{:S(2)}, u32[]{:S(2)}) collective-permute-start(bf16[1280,128]{1,0:T(8,128)(2,1)S(1)} %bitcast.81), channel_id=1, source_target_pairs={{0,1},{1,0},{2,3},{3,2},{4,5},{5,4},{6,7},{7,6},{8,9},{9,8},{10,11... | collective-permute-start | bytes 983048 | tf_op jit(solution)/shard_map/ppermute | solution.py:34
  74.0 11.7 %collective-permute-start.26 = (bf16[1280,128]{1,0:T(8,128)(2,1)S(1)}, bf16[1280,128]{1,0:T(8,128)(2,1)S(1)}, u32[]{:S(2)}, u32[]{:S(2)}) collective-permute-start(bf16[1280,128]{1,0:T(8,128)(2,1)S(1)} %fusion.14), channel_id=1, source_target_pairs={{0,2},{1,3},{2,0},{3,1},{4,6},{5,7},{6,4},{7,5},{8,10},{9,11},{10,... | collective-permute-start | bytes 983048 | tf_op jit(solution)/shard_map/ppermute | solution.py:34
  77.4 19.3 %collective-permute-start.24 = (bf16[1280,128]{1,0:T(8,128)(2,1)S(1)}, bf16[1280,128]{1,0:T(8,128)(2,1)S(1)}, u32[]{:S(2)}, u32[]{:S(2)}) collective-permute-start(bf16[1280,128]{1,0:T(8,128)(2,1)S(1)} %bitcast.78), channel_id=1, source_target_pairs={{0,1},{1,0},{2,3},{3,2},{4,5},{5,4},{6,7},{7,6},{8,9},{9,8},{10,11... | collective-permute-start | bytes 983048 | tf_op jit(solution)/shard_map/ppermute | solution.py:34
  77.7 24.6 %collective-permute-start.29 = (bf16[1280,128]{1,0:T(8,128)(2,1)S(1)}, bf16[1280,128]{1,0:T(8,128)(2,1)S(1)}, u32[]{:S(2)}, u32[]{:S(2)}) collective-permute-start(bf16[1280,128]{1,0:T(8,128)(2,1)S(1)} %bitcast.77), channel_id=1, source_target_pairs={{0,1},{1,0},{2,3},{3,2},{4,5},{5,4},{6,7},{7,6},{8,9},{9,8},{10,11... | collective-permute-start | bytes 983048 | tf_op jit(solution)/shard_map/ppermute | solution.py:34
  78.2 30.6 %collective-permute-start.18 = (bf16[1280,128]{1,0:T(8,128)(2,1)S(1)}, bf16[1280,128]{1,0:T(8,128)(2,1)S(1)}, u32[]{:S(2)}, u32[]{:S(2)}) collective-permute-start(bf16[1280,128]{1,0:T(8,128)(2,1)S(1)} %bitcast.75), channel_id=1, source_target_pairs={{0,1},{1,0},{2,3},{3,2},{4,5},{5,4},{6,7},{7,6},{8,9},{9,8},{10,11... | collective-permute-start | bytes 983048 | tf_op jit(solution)/shard_map/ppermute | solution.py:34
  85.7 9.5 %collective-permute-start.22 = (bf16[1280,128]{1,0:T(8,128)(2,1)S(1)}, bf16[1280,128]{1,0:T(8,128)(2,1)S(1)}, u32[]{:S(2)}, u32[]{:S(2)}) collective-permute-start(bf16[1280,128]{1,0:T(8,128)(2,1)S(1)} %fusion.8), channel_id=1, source_target_pairs={{0,2},{1,3},{2,0},{3,1},{4,6},{5,7},{6,4},{7,5},{8,10},{9,11},{10,... | collective-permute-start | bytes 983048 | tf_op jit(solution)/shard_map/ppermute | solution.py:34
  87.5 11.1 %collective-permute-start.27 = (bf16[1280,128]{1,0:T(8,128)(2,1)S(1)}, bf16[1280,128]{1,0:T(8,128)(2,1)S(1)}, u32[]{:S(2)}, u32[]{:S(2)}) collective-permute-start(bf16[1280,128]{1,0:T(8,128)(2,1)S(1)} %add_convert_fusion), channel_id=1, source_target_pairs={{0,4},{1,5},{2,6},{3,7},{4,8},{5,9},{6,10},{7,11},{8,12},{9,13},{1... | collective-permute-start | bytes 983048 | tf_op jit(solution)/shard_map/ppermute | solution.py:34
  95.2 10.0 %collective-permute-start.30 = (bf16[1280,128]{1,0:T(8,128)(2,1)S(1)}, bf16[1280,128]{1,0:T(8,128)(2,1)S(1)}, u32[]{:S(2)}, u32[]{:S(2)}) collective-permute-start(bf16[1280,128]{1,0:T(8,128)(2,1)S(1)} %fusion.4), channel_id=1, source_target_pairs={{0,2},{1,3},{2,0},{3,1},{4,6},{5,7},{6,4},{7,5},{8,10},{9,11},{10,... | collective-permute-start | bytes 983048 | tf_op jit(solution)/shard_map/ppermute | solution.py:34
  98.8 10.9 %collective-permute-start.28 = (bf16[1280,128]{1,0:T(8,128)(2,1)S(1)}, bf16[1280,128]{1,0:T(8,128)(2,1)S(1)}, u32[]{:S(2)}, u32[]{:S(2)}) collective-permute-start(bf16[1280,128]{1,0:T(8,128)(2,1)S(1)} %fusion.7), channel_id=1, source_target_pairs={{0,4},{1,5},{2,6},{3,7},{4,8},{5,9},{6,10},{7,11},{8,12},{9,13},{1... | collective-permute-start | bytes 983048 | tf_op jit(solution)/shard_map/ppermute | solution.py:34
  101.5 9.3 %collective-permute-start.23 = (bf16[1280,128]{1,0:T(8,128)(2,1)S(1)}, bf16[1280,128]{1,0:T(8,128)(2,1)S(1)}, u32[]{:S(2)}, u32[]{:S(2)}) collective-permute-start(bf16[1280,128]{1,0:T(8,128)(2,1)S(1)} %fusion.9), channel_id=1, source_target_pairs={{0,2},{1,3},{2,0},{3,1},{4,6},{5,7},{6,4},{7,5},{8,10},{9,11},{10,... | collective-permute-start | bytes 983048 | tf_op jit(solution)/shard_map/ppermute | solution.py:34
  105.3 10.6 %collective-permute-start.31 = (bf16[1280,128]{1,0:T(8,128)(2,1)S(1)}, bf16[1280,128]{1,0:T(8,128)(2,1)S(1)}, u32[]{:S(2)}, u32[]{:S(2)}) collective-permute-start(bf16[1280,128]{1,0:T(8,128)(2,1)S(1)} %fusion.3), channel_id=1, source_target_pairs={{0,12},{1,13},{2,14},{3,15},{4,0},{5,1},{6,2},{7,3},{8,4},{9,5},{1... | collective-permute-start | bytes 983048 | tf_op jit(solution)/shard_map/ppermute | solution.py:34

commit v9 on v8

--- a/solution.py
+++ b/solution.py
@@ -13,7 +13,7 @@
 LANES = 128
 UNROLL = 8
 LINE = 4
-SCOPED_BYTES = 16 * 1024 * 1024
+SCOPED_BYTES = 6 * 1024 * 1024
 
 
 def place(z, x, core):
@@ -37,8 +37,8 @@
 ALONG = pairs_of(lambda z, x: ((z + 1) % LINE, x))
 BACK = pairs_of(lambda z, x: ((z - 1) % LINE, x))
 ACROSS = pairs_of(lambda z, x: (z, 1 - x))
-ADD_AT = {(3, 1): 0}
-LAY_AT = (2, 1)
+ADD_AT = {(2, 1): 0, (3, 0): 1, (3, 1): 2}
+LAY_AT = (1, 1)
 
 
 def spread(parts, meanwhile):
@@ -52,11 +52,13 @@
         for index, (line, other) in enumerate(zip(lines, others)):
             if other:
                 line[-1], other[-1] = tie(line[-1], other[-1])
-            line[-1] = meanwhile(step, index, arrived, line[-1])
-            now = line[-1]
+            turn = step == LINE - 1 and index == 0
+            source = other if turn else line
+            source[-1] = meanwhile(step, index, arrived, source[-1])
+            now = source[-1]
             if step + 1 < LINE:
                 line.append(move(now, ALONG))
-            other.append(move(now, ACROSS))
+            other.append(move(now, ALONG if turn else ACROSS))
     return [arrived(stage) for stage in range(LINE + 1)]
 
 
@@ -64,24 +66,22 @@
     def paired(keep, send):
         return keep + move(send, swap).astype(jnp.float32)
 
-    order = (2, 1, 3, 0)
-    parts = {step: paired(far_keep[step], far_send[step]).astype(jnp.bfloat16) for step in order}
-    half, parts[2] = tie(half, parts[2])
-    crossed = {2: move(parts[2], ACROSS)}
+    order = (1, 2, 3, 0)
+    far = {step: paired(far_keep[step], far_send[step]) for step in order}
+    aside, crossing = far[1].astype(jnp.bfloat16), far[2].astype(jnp.bfloat16)
+    half, aside, crossing = tie(half, aside, crossing)
+    crossed = {2: move(crossing, ACROSS)}
+    joining = move(aside, ALONG)
     near_keep, near_send = near_of(half)
-    total = {step: paired(near_keep[step], near_send[step]) for step in order}
-    parts[1], total[2] = tie(parts[1], total[2])
-    crossed[1] = move(parts[1], ACROSS)
-    parts[3], crossed[2] = tie(parts[3], crossed[2])
-    crossed[3] = move(parts[3], ACROSS)
-    parts[0], crossed[1] = tie(parts[0], crossed[1])
-    crossed[0] = move(parts[0], ACROSS)
-
-    total = {step: total[step] + crossed[step].astype(jnp.float32) for step in order}
-    two_on = move(total[2].astype(jnp.bfloat16), ALONG)
-    one_on = move((total[1] + two_on.astype(jnp.float32)).astype(jnp.bfloat16), ALONG)
-    one_back = move(total[3].astype(jnp.bfloat16), BACK)
-    return total[0] + one_on.astype(jnp.float32) + one_back.astype(jnp.float32)
+    near = {step: paired(near_keep[step], near_send[step]) for step in (2, 1, 3, 0)}
+    crossing, crossed[2] = tie(far[3].astype(jnp.bfloat16), crossed[2])
+    crossed[3] = move(crossing, ACROSS)
+    crossed[0] = move((far[0] + joining.astype(jnp.float32)).astype(jnp.bfloat16), ACROSS)
+
+    two_on = move((near[2] + crossed[2].astype(jnp.float32)).astype(jnp.bfloat16), ALONG)
+    one_on = move((near[1] + two_on.astype(jnp.float32)).astype(jnp.bfloat16), ALONG)
+    one_back = move((near[3] + crossed[3].astype(jnp.float32)).astype(jnp.bfloat16), BACK)
+    return near[0] + crossed[0].astype(jnp.float32) + one_on.astype(jnp.float32) + one_back.astype(jnp.float32)
 
 
 def clear(half):
@@ -94,15 +94,12 @@
     half[pl.ds(whole, half.shape[0] - whole), :] = jnp.zeros((half.shape[0] - whole, LANES), jnp.float32)
 
 
-def add_tiles(stage, pieces, table_ref, bounds_ref, sources, tile_sets, half, occ, sem):
+def add_tiles(stage, pieces, table_ref, bounds_ref, sources, tiles, half, occ, sem):
     rows = sources[0].shape[0]
     for index, source in enumerate(sources):
         pltpu.make_async_copy(source, occ.at[pl.ds(index * rows, rows)], sem).start()
     pltpu.make_async_copy(occ, occ, sem).wait()
     begin, end = bounds_ref[stage], bounds_ref[stage + 1]
-    slots, depth, lanes = tile_sets[0].shape
-    low = lax.broadcasted_iota(jnp.int32, (depth, lanes), 1) < BLK
-    zero = jnp.zeros((depth, lanes), jnp.bfloat16)
     spill = half.shape[0] - BLK
     columns = 2 + pieces
     piece = BLK // pieces
@@ -116,10 +113,9 @@
             starts.append(jnp.where(entry < end, table_ref[entry * columns + 1], spill))
             spots = [jnp.where(entry < end, table_ref[entry * columns + 2 + cut], 0) for cut in range(pieces)]
             parts = [occ[pl.ds(pl.multiple_of(spot, piece), piece), :] for spot in spots]
-            slot = lax.rem(tile, slots)
-            pair = jnp.where(tile < slots, tile_sets[0][slot], tile_sets[1][slot])
-            left = jnp.concatenate([jnp.where(low, pair, zero), jnp.where(low, zero, pair)], axis=0)
-            block = jnp.concatenate(parts * 2, axis=0)
+            pair = tiles[tile]
+            left = jnp.concatenate([pair[:, :BLK], pair[:, BLK:]], axis=0)
+            block = parts[0] if pieces == 1 else jnp.concatenate(parts, axis=0)
             products.append(jnp.dot(left, block, preferred_element_type=jnp.float32))
         for product, start in zip(products, starts):
             start = pl.multiple_of(start, BLK)
@@ -140,23 +136,39 @@
         out[index] = jnp.dot(both, weights[...], preferred_element_type=jnp.float32).astype(out.dtype)
 
 
+def load_tiles(tile_sets, tiles, sems):
+    slots = tile_sets[0].shape[0]
+    copies = [
+        pltpu.make_async_copy(source, tiles.at[pl.ds(index * slots, slots)], sems.at[index])
+        for index, source in enumerate(tile_sets)
+    ]
+    for copy in copies:
+        copy.start()
+    return copies
+
+
+def add_stage(stage, count, pieces, table_ref, bounds_ref, refs):
+    sources = refs[:count]
+    if stage:
+        tiles, _, half, *outs, occ, sems = refs[count:]
+        copies = []
+    else:
+        *tile_sets, half, tiles = refs[count : count + 4]
+        *outs, occ, sems = refs[count + 4 :]
+        copies = load_tiles(tile_sets, tiles, sems)
+        clear(half)
+    for copy in copies:
+        copy.wait()
+    add_tiles(stage, pieces, table_ref, bounds_ref, sources, tiles, half, occ, sems.at[2])
+    return half, outs
+
+
 def stage_kernel(stage, count, pieces, table_ref, bounds_ref, *refs):
-    sources, tile_sets = refs[:count], refs[count : count + 2]
-    half, occ, sem = refs[-3:]
-    if stage == 0:
-        clear(half)
-    add_tiles(stage, pieces, table_ref, bounds_ref, sources, tile_sets, half, occ, sem)
+    add_stage(stage, count, pieces, table_ref, bounds_ref, refs)
 
 
 def window_kernel(stage, count, pieces, shard, first, table_ref, bounds_ref, chips_ref, core_ref, *refs):
-    sources, tile_sets = refs[:count], refs[count : count + 2]
-    before = 1 if stage else 0
-    half, weights = refs[count + 2 + before : count + 4 + before]
-    outs = refs[count + 4 + before : -2]
-    occ, sem = refs[-2:]
-    if stage == 0:
-        clear(half)
-    add_tiles(stage, pieces, table_ref, bounds_ref, sources, tile_sets, half, occ, sem)
+    half, (weights, *outs) = add_stage(stage, count, pieces, table_ref, bounds_ref, refs)
     side_rows = (half.shape[0] - BLK) // 2
     for side in range(2):
         weights[pl.ds(side * LANES, LANES), :] = half[pl.ds(side * side_rows, WIN), :].T.astype(jnp.bfloat16)
@@ -179,7 +191,7 @@
     return pltpu.with_memory_space_constraint(array, pltpu.VMEM)
 
 
-def call(kernel, ins, in_specs, outs, scratch, aliases, flops):
+def call(kernel, ins, in_specs, outs, scratch, aliases, flops, scoped=0):
     return pl.pallas_call(
         kernel,
         out_shape=outs,
@@ -187,7 +199,7 @@
         out_specs=[VMEM] * len(outs),
         scratch_shapes=scratch,
         input_output_aliases=aliases,
-        compiler_params=pltpu.CompilerParams(vmem_limit_bytes=SCOPED_BYTES),
+        compiler_params=pltpu.CompilerParams(vmem_limit_bytes=SCOPED_BYTES + scoped),
         cost_estimate=pl.CostEstimate(flops=flops, bytes_accessed=4 << 20, transcendentals=0),
     )(*ins)
 
@@ -253,59 +265,55 @@
     cores = core.astype(jnp.int32).reshape(1)
 
     half_type = pltpu.VMEM((2 * total + BLK, LANES), jnp.float32)
+    tiles_type = pltpu.VMEM((2 * slots, BLK * BLK // LANES, LANES), jnp.bfloat16)
     work = 4 * slots * BLK * BLK * LANES // stage_count
-    halves = []
-
-    def stage_ins(sources):
-        scratch = [
-            pltpu.VMEM((len(sources) * sources[0].shape[0], LANES), jnp.bfloat16),
-            pltpu.SemaphoreType.DMA,
-        ]
-        earlier = [pinned(halves[-1])] if halves else []
-        ins = [*sources, *map(pinned, tile_sets), *earlier]
-        return ins, [HBM] * len(sources) + [VMEM] * (2 + len(earlier)), scratch
-
-    def aliases(ahead, ins):
-        return {ahead + len(ins) - 1: 0} if halves else {}
-
-    def add_stage(stage, sources):
-        ins, specs, scratch = stage_ins(sources)
-        halves.extend(
-            call(
-                functools.partial(stage_kernel, stage, len(sources), pieces),
-                [ordered, bounds] + ins, [SMEM] * 2 + specs, [half_type], scratch, aliases(2, ins), work,
-            )
-        )
+    state = []
+
+    def run_stage(kernel, sources, tables, outs, flops):
+        rows = len(sources) * sources[0].shape[0]
+        scratch = [pltpu.VMEM((rows, LANES), jnp.bfloat16), pltpu.SemaphoreType.DMA((3,))]
+        ins, specs = [*tables, *sources], [SMEM] * len(tables) + [HBM] * len(sources)
+        made, aliases = [half_type], {}
+        if state:
+            aliases = {len(ins) + 1: 0}
+            ins, specs = ins + [pinned(state[1]), pinned(state[0])], specs + [VMEM] * 2
+        else:
+            ins, specs, made = ins + tile_sets, specs + [HBM] * 2, [half_type, tiles_type]
+        results = call(kernel, ins, specs, made + outs, scratch, aliases, flops, 2 * rows * LANES)
+        state[:] = [results[0], state[1] if state else results[1]]
+        return results[len(made) :]
+
+    def add(stage, sources):
+        kernel = functools.partial(stage_kernel, stage, len(sources), pieces)
+        run_stage(kernel, sources, [ordered, bounds], [], work)
 
     def meanwhile(step, index, arrived, moved):
         if (step, index) == LAY_AT:
             moved, *tile_sets[:] = tie(moved, *tile_sets)
         if (step, index) in ADD_AT:
             stage = ADD_AT[step, index]
-            add_stage(stage, arrived(stage))
-            moved, halves[-1] = tie(moved, halves[-1])
+            add(stage, arrived(stage))
+            moved, state[0] = tie(moved, state[0])
         return moved
 
     if lined:
         stages = spread(parts, meanwhile)
         for stage in range(len(ADD_AT), LINE):
-            add_stage(stage, stages[stage])
+            add(stage, stages[stage])
     else:
         stages = [[lax.all_gather(part, "aux", axis_index_groups=same_core, axis=0, tiled=True) for part in parts]]
 
     group = 1 if lined else chips // 2
     far = [group] * (chips // 2 // group)
-    ins, specs, scratch = stage_ins(stages[-1])
-    half, weights, *far_send = call(
+    weights, *far_send = run_stage(
         functools.partial(window_kernel, stage_count - 1, len(stages[-1]), pieces, shard, chips // 2),
-        [ordered, bounds, chip_of_slot, cores] + ins,
-        [SMEM] * 4 + specs,
-        [half_type, pltpu.VMEM((2 * LANES, WIN), jnp.bfloat16)]
+        stages[-1],
+        [ordered, bounds, chip_of_slot, cores],
+        [pltpu.VMEM((2 * LANES, WIN), jnp.bfloat16)]
         + [pltpu.VMEM((size, shard, WIN), jnp.bfloat16) for size in far],
-        scratch,
-        aliases(4, ins),
         work + total // 4 * width * WIN * 2,
     )
+    half = state[0]
 
     def rest(plan, half):
         return call(

time: 117 us -> 110 us (0.940)
  starting transfers between devices: 41.4 us -> 30.6 us
  Pallas kernels: 18.8 us -> 24.9 us
  local copies, waits for them, and re-layouts: 15.4 us -> 11.7 us
    ppermute x32, starting transfers between devices: 41.4 us -> 30.6 us  [move(): return lax.ppermute(array, 'aux', pairs)]
    pallas_call x7, Pallas kernels: 18.8 us -> 24.9 us  [call(): pl.pallas_call(kernel, out_shape=outs, in_specs=in_specs, out_specs=[VMEM...]
    unnamed x24 -> x12, local copies, waits for them, and re-layouts: 14 us -> 8.51 us
  transfers between devices with their start and end apart: 32 -> 32, of which waited for: 13 -> 9; matrix products, arithmetic and copies ran while one was open for 9% -> 10% of each run, Pallas kernels for 14% -> 20%
where the time goes in v9:
time: 110 us; the launch traced here: 109 us
  waiting for transfers between devices  37.1 us (34%)
  starting transfers between devices  30.6 us (28%)
  Pallas kernels  24.9 us (23%)
  local copies, waits for them, and re-layouts  11.7 us (11%)
  other arithmetic  3.74 us (3%)
    ppermute x32, waiting for transfers between devices, move(): return lax.ppermute(array, 'aux', pairs)  37.1 us
    ppermute x32, starting transfers between devices, move(): return lax.ppermute(array, 'aux', pairs)  30.6 us
    pallas_call x7, Pallas kernels, call(): pl.pallas_call(kernel, out_shape=outs, in_specs=in_specs, out_specs=[VMEM...  24.9 us
    unnamed x12, local copies, waits for them, and re-layouts  8.51 us
  transfers between devices with their start and end apart: 32, of which 9 were waited for; matrix products, arithmetic and copies ran while one was open for 10% of the time, Pallas kernels for 20%

profile of v9, /device:TPU:0, one launch (start us, length us, event | category | flops | bytes accessed | tf_op | source)
XLA Modules:
  0.0 109.0 jit_solution(13027722123494750962)
XLA Ops:
  0.0 0.5 collective-permute-start.10
  1.1 0.8 slice_multiply_fusion.1
  1.9 0.1 collective-permute-start
  2.0 1.1 %constant_dynamic-slice_fusion = (bf16[1280,128]{1,0:T(8,128)(2,1)S(1)}, bf16[1280,128]{1,0:T(8,128)(2,1)S(1)}) fusion(bf16[1280,256]{1,0:T(8,128)(2,1)} %param.7, s32[]{:T(128)S(6)} %select_n.204, s32[]{:T(128)S(6)} %select_n.203), kind=kLoop, calls=%fused_computation.107 | loop fusion | bytes 1310728 | tf_op jit(solution)/shard_map/dynamic_slice | solution.py:222
  3.1 3.1 %collective-permute-start.1 = (bf16[1280,128]{1,0:T(8,128)(2,1)S(1)}, bf16[1280,128]{1,0:T(8,128)(2,1)S(1)}, u32[]{:S(2)}, u32[]{:S(2)}) collective-permute-start(bf16[1280,128]{1,0:T(8,128)(2,1)S(1)} %get-tuple-element.107.refs_0_), channel_id=1, source_target_pairs={{0,4},{1,5},{2,6},{3,7},{4,8},{5,9},{6,10},{7,11},{8,12},{9,13},{1... | collective-permute-start | bytes 983048 | tf_op jit(solution)/shard_map/ppermute | solution.py:34
  6.2 1.5 %collective-permute-start.2 = (bf16[1280,128]{1,0:T(8,128)(2,1)S(1)}, bf16[1280,128]{1,0:T(8,128)(2,1)S(1)}, u32[]{:S(2)}, u32[]{:S(2)}) collective-permute-start(bf16[1280,128]{1,0:T(8,128)(2,1)S(1)} %get-tuple-element.107.refs_0_), channel_id=1, source_target_pairs={{0,2},{1,3},{2,0},{3,1},{4,6},{5,7},{6,4},{7,5},{8,10},{9,11},{10,... | collective-permute-start | bytes 983048 | tf_op jit(solution)/shard_map/ppermute | solution.py:34
  7.7 2.1 %copy.11 = bf16[32,8,32,128]{3,2,1,0:T(8,128)(2,1)S(1)} copy(bf16[32,8,32,128]{3,1,2,0:T(8,128)(2,1)} %bitcast.79) | data formatting | bytes 4194304
  10.0 1.6 %collective-permute-start.8 = (bf16[1280,128]{1,0:T(8,128)(2,1)}, bf16[1280,128]{1,0:T(8,128)(2,1)S(1)}, u32[]{:S(2)}, u32[]{:S(2)}) collective-permute-start(bf16[1280,128]{1,0:T(8,128)(2,1)} %collective-permute-done.7.refs_1_), channel_id=1, source_target_pairs={{0,4},{1,5},{2,6},{3,7},{4,8},{5,9},{6,10},{7,11},{8,12},{9,13},{1... | collective-permute-start | bytes 983048 | tf_op jit(solution)/shard_map/ppermute | solution.py:34
  11.6 0.5 collective-permute-start.9
  12.2 4.6 %collective-permute-done.1.refs_0_ = bf16[1280,128]{1,0:T(8,128)(2,1)S(1)} collective-permute-done((bf16[1280,128]{1,0:T(8,128)(2,1)S(1)}, bf16[1280,128]{1,0:T(8,128)(2,1)S(1)}, u32[]{:S(2)}, u32[]{:S(2)}) %collective-permute-start.1) | collective-permute-done | bytes 327712 | tf_op jit(solution)/shard_map/ppermute | solution.py:34
  16.7 1.3 %collective-permute-start.3 = (bf16[1280,128]{1,0:T(8,128)(2,1)S(1)}, bf16[1280,128]{1,0:T(8,128)(2,1)}, u32[]{:S(2)}, u32[]{:S(2)}) collective-permute-start(bf16[1280,128]{1,0:T(8,128)(2,1)S(1)} %collective-permute-done.1.refs_0_), channel_id=1, source_target_pairs={{0,4},{1,5},{2,6},{3,7},{4,8},{5,9},{6,10},{7,11},{8,12},{9,13},{1... | collective-permute-start | bytes 983048 | tf_op jit(solution)/shard_map/ppermute | solution.py:34
  18.0 1.9 %collective-permute-start.4 = (bf16[1280,128]{1,0:T(8,128)(2,1)S(1)}, bf16[1280,128]{1,0:T(8,128)(2,1)S(1)}, u32[]{:S(2)}, u32[]{:S(2)}) collective-permute-start(bf16[1280,128]{1,0:T(8,128)(2,1)S(1)} %collective-permute-done.1.refs_0_), channel_id=1, source_target_pairs={{0,2},{1,3},{2,0},{3,1},{4,6},{5,7},{6,4},{7,5},{8,10},{9,11},{10,... | collective-permute-start | bytes 983048 | tf_op jit(solution)/shard_map/ppermute | solution.py:34
  19.9 0.3 convert_reduce_fusion
  20.2 3.6 %collective-permute-done.8.refs_1_ = bf16[1280,128]{1,0:T(8,128)(2,1)S(1)} collective-permute-done((bf16[1280,128]{1,0:T(8,128)(2,1)}, bf16[1280,128]{1,0:T(8,128)(2,1)S(1)}, u32[]{:S(2)}, u32[]{:S(2)}) %collective-permute-start.8) | collective-permute-done | bytes 327712 | tf_op jit(solution)/shard_map/ppermute | solution.py:34
  23.8 0.7 copy-done.1
  24.5 3.4 %copy.12 = bf16[32,8,32,128]{3,2,1,0:T(8,128)(2,1)} copy(bf16[32,8,32,128]{3,1,2,0:T(8,128)(2,1)} %bitcast.27) | data formatting | bytes 4194304
  27.9 1.3 %collective-permute-start.11 = (bf16[1280,128]{1,0:T(8,128)(2,1)S(1)}, bf16[1280,128]{1,0:T(8,128)(2,1)}, u32[]{:S(2)}, u32[]{:S(2)}) collective-permute-start(bf16[1280,128]{1,0:T(8,128)(2,1)S(1)} %collective-permute-done.8.refs_1_), channel_id=1, source_target_pairs={{0,4},{1,5},{2,6},{3,7},{4,8},{5,9},{6,10},{7,11},{8,12},{9,13},{1... | collective-permute-start | bytes 983048 | tf_op jit(solution)/shard_map/ppermute | solution.py:34
  29.2 1.9 %collective-permute-start.12 = (bf16[1280,128]{1,0:T(8,128)(2,1)S(1)}, bf16[1280,128]{1,0:T(8,128)(2,1)}, u32[]{:S(2)}, u32[]{:S(2)}) collective-permute-start(bf16[1280,128]{1,0:T(8,128)(2,1)S(1)} %collective-permute-done.8.refs_1_), channel_id=1, source_target_pairs={{0,2},{1,3},{2,0},{3,1},{4,6},{5,7},{6,4},{7,5},{8,10},{9,11},{10,... | collective-permute-start | bytes 983048 | tf_op jit(solution)/shard_map/ppermute | solution.py:34
  31.0 0.5 select_reduce_fusion.2
  31.7 0.7 copy-done.3
  32.4 1.6 %collective-permute-start.5 = (bf16[1280,128]{1,0:T(8,128)(2,1)}, bf16[1280,128]{1,0:T(8,128)(2,1)}, u32[]{:S(2)}, u32[]{:S(2)}) collective-permute-start(bf16[1280,128]{1,0:T(8,128)(2,1)} %collective-permute-done.3.refs_0_), channel_id=1, source_target_pairs={{0,4},{1,5},{2,6},{3,7},{4,8},{5,9},{6,10},{7,11},{8,12},{9,13},{1... | collective-permute-start | bytes 983048 | tf_op jit(solution)/shard_map/ppermute | solution.py:34
  34.0 0.5 collective-permute-start.6
  34.5 0.1 convert_reduce_fusion.1.bounds_ref
  34.6 0.9 copy.10
  35.5 1.2 %reshape.224.table_ref = s32[1560]{0:T(1024)S(1)} reshape(s32[520,3]{1,0:T(8,128)} %copy.10) | data formatting | bytes 12480 | tf_op jit(solution)/shard_map/reshape | solution.py:263
  36.7 1.6 %copy-done = bf16[32,8,32,128]{3,2,1,0:T(8,128)(2,1)S(1)} copy-done((bf16[32,8,32,128]{3,2,1,0:T(8,128)(2,1)S(1)}, bf16[32,8,32,128]{3,2,1,0:T(8,128)(2,1)}, u32[]{:S(2)}) %copy-start) | copy-done | bytes 2097176
  38.2 5.0 %shard_map.46 = (f32[41024,128]{1,0:T(8,128)S(1)}, bf16[512,32,128]{2,1,0:T(8,128)(2,1)S(1)}) custom-call(s32[1560]{0:T(1024)S(1)} %reshape.224.table_ref, s32[6]{0:T(128)S(1)} %convert_reduce_fusion.1.bounds_ref, bf16[1280,128]{1,0:T(8,128)(2,1)S(1)} %get-tuple-element.107.refs_0_, bf16[1280,128]{1,0:T(8,128)(2,1)} %collective-permute-done.7.refs_1_, ...), custom_call_target="tpu_custom_call" | custom-call | flops 107374184 | bytes 4194304 | tf_op jit(solution)/shard_map/pallas_call | solution.py:195
  43.3 1.1 collective-permute-start.14
  44.4 0.8 collective-permute-start.15
  45.1 0.3 collective-permute-done.5.refs_0_
  45.4 4.2 %shard_map.47.refs_5_ = f32[41024,128]{1,0:T(8,128)S(1)} custom-call(s32[1560]{0:T(1024)S(1)} %reshape.224.table_ref, s32[6]{0:T(128)S(1)} %convert_reduce_fusion.1.bounds_ref, bf16[1280,128]{1,0:T(8,128)(2,1)S(1)} %collective-permute-done.1.refs_0_, bf16[1280,128]{1,0:T(8,128)(2,1)S(1)} %collective-permute-done.8.refs_1_, ...), custom_call_target="tpu_custom_call", output_to_operand_aliasing={{}: (7, {})} | custom-call | flops 107374184 | bytes 4194304 | tf_op jit(solution)/shard_map/pallas_call | solution.py:195
  49.6 0.3 collective-permute-start.13
  49.9 4.8 %shard_map.48.refs_5_ = f32[41024,128]{1,0:T(8,128)S(1)} custom-call(s32[1560]{0:T(1024)S(1)} %reshape.224.table_ref, s32[6]{0:T(128)S(1)} %convert_reduce_fusion.1.bounds_ref, bf16[1280,128]{1,0:T(8,128)(2,1)} %collective-permute-done.3.refs_0_, bf16[1280,128]{1,0:T(8,128)(2,1)} %collective-permute-done.11.refs_1_, ...), custom_call_target="tpu_custom_call", output_to_operand_aliasing={{}: (7, {})} | custom-call | flops 107374184 | bytes 4194304 | tf_op jit(solution)/shard_map/pallas_call | solution.py:195
  54.7 2.0 %collective-permute-start.16 = (bf16[1280,128]{1,0:T(8,128)(2,1)S(1)}, bf16[1280,128]{1,0:T(8,128)(2,1)S(1)}, u32[]{:S(2)}, u32[]{:S(2)}) collective-permute-start(bf16[1280,128]{1,0:T(8,128)(2,1)S(1)} %collective-permute-done.14.refs_1_), channel_id=1, source_target_pairs={{0,2},{1,3},{2,0},{3,1},{4,6},{5,7},{6,4},{7,5},{8,10},{9,11},{10,... | collective-permute-start | bytes 983048 | tf_op jit(solution)/shard_map/ppermute | solution.py:34
  56.7 4.2 %shard_map.49.refs_3_ = f32[41024,128]{1,0:T(8,128)S(1)} custom-call(s32[1560]{0:T(1024)S(1)} %reshape.224.table_ref, s32[6]{0:T(128)S(1)} %convert_reduce_fusion.1.bounds_ref, bf16[1280,128]{1,0:T(8,128)(2,1)} %collective-permute-done.5.refs_0_, bf16[1280,128]{1,0:T(8,128)(2,1)S(1)} %collective-permute-done.14.refs_1_, ...), custom_call_target="tpu_custom_call", output_to_operand_aliasing={{}: (7, {})} | custom-call | flops 107374184 | bytes 4194304 | tf_op jit(solution)/shard_map/pallas_call | solution.py:195
  60.9 1.3 %collective-permute-done.16.refs_1_ = bf16[1280,128]{1,0:T(8,128)(2,1)S(1)} collective-permute-done((bf16[1280,128]{1,0:T(8,128)(2,1)S(1)}, bf16[1280,128]{1,0:T(8,128)(2,1)S(1)}, u32[]{:S(2)}, u32[]{:S(2)}) %collective-permute-start.16) | collective-permute-done | bytes 327712 | tf_op jit(solution)/shard_map/ppermute | solution.py:34
  62.2 3.3 %shard_map.50 = (f32[41024,128]{1,0:T(8,128)S(1)}, bf16[256,128]{1,0:T(8,128)(2,1)S(1)}, bf16[1,1280,128]{2,1,0:T(8,128)(2,1)S(1)}, bf16[1,1280,128]{2,1,0:T(8,1...) custom-call(s32[1560]{0:T(1024)S(1)} %reshape.224.table_ref, ...), custom_call_target="tpu_custom_call", output_to_operand_aliasing={{0}: (7, {})} | custom-call | flops 442918496 | bytes 4194304 | tf_op jit(solution)/shard_map/pallas_call | solution.py:195
  65.5 0.1 collective-permute-start.18
  65.6 0.5 collective-permute-start.17
  66.1 0.1 collective-permute-start.20
  66.2 0.4 collective-permute-start.25
  66.6 1.4 %shard_map.51 = (f32[1,1280,128]{2,1,0:T(8,128)S(1)}, f32[1,1280,128]{2,1,0:T(8,128)S(1)}, f32[1,1280,128]{2,1,0:T(8,128)S(1)}, f32[1,1280,128]{2,1,0:T(8,128)S(1)}) custom-call(s32[8]{0:T(128)S(1)} %fusion.35.chips_ref, s32[1]{0:T(128)} %bitcast.core_ref, f32[41024,128]{1,0:T(8,128)S(1)} %get-tuple-element.80.half, ...), custom_call_target="tpu_custom_call" | custom-call | flops 335544320 | bytes 4194304 | tf_op jit(solution)/shard_map/pallas_call | solution.py:195
  68.0 0.1 fusion.15
  68.1 0.1 fusion.16
  68.2 1.9 %collective-permute-start.26 = (bf16[1280,128]{1,0:T(8,128)(2,1)S(1)}, bf16[1280,128]{1,0:T(8,128)(2,1)S(1)}, u32[]{:S(2)}, u32[]{:S(2)}) collective-permute-start(bf16[1280,128]{1,0:T(8,128)(2,1)S(1)} %fusion.15), channel_id=1, source_target_pairs={{0,2},{1,3},{2,0},{3,1},{4,6},{5,7},{6,4},{7,5},{8,10},{9,11},{10,... | collective-permute-start | bytes 983048 | tf_op jit(solution)/shard_map/ppermute | solution.py:34
  70.1 2.1 %shard_map.52 = (f32[1,1280,128]{2,1,0:T(8,128)S(1)}, f32[1,1280,128]{2,1,0:T(8,128)S(1)}, f32[1,1280,128]{2,1,0:T(8,128)S(1)}, f32[1,1280,128]{2,1,0:T(8,128)S(...) custom-call(s32[8]{0:T(128)S(1)} %fusion.35.chips_ref, ...), custom_call_target="tpu_custom_call" | custom-call | flops 335544320 | bytes 4194304 | tf_op jit(solution)/shard_map/pallas_call | solution.py:195
  72.2 0.1 collective-permute-start.24
  72.2 0.5 collective-permute-start.23
  72.8 5.2 %collective-permute-done.26 = bf16[1280,128]{1,0:T(8,128)(2,1)S(1)} collective-permute-done((bf16[1280,128]{1,0:T(8,128)(2,1)S(1)}, bf16[1280,128]{1,0:T(8,128)(2,1)S(1)}, u32[]{:S(2)}, u32[]{:S(2)}) %collective-permute-start.26) | collective-permute-done | bytes 327712 | tf_op jit(solution)/shard_map/ppermute | solution.py:34
  78.1 0.5 collective-permute-start.19
  78.6 0.1 fusion.6
  78.7 2.5 %collective-permute-start.27 = (bf16[1280,128]{1,0:T(8,128)(2,1)S(1)}, bf16[1280,128]{1,0:T(8,128)(2,1)S(1)}, u32[]{:S(2)}, u32[]{:S(2)}) collective-permute-start(bf16[1280,128]{1,0:T(8,128)(2,1)S(1)} %fusion.6), channel_id=1, source_target_pairs={{0,4},{1,5},{2,6},{3,7},{4,8},{5,9},{6,10},{7,11},{8,12},{9,13},{1... | collective-permute-start | bytes 983048 | tf_op jit(solution)/shard_map/ppermute | solution.py:34
  81.2 0.1 fusion.10
  81.3 0.6 collective-permute-start.22
  81.9 1.5 %collective-permute-start.30 = (bf16[1280,128]{1,0:T(8,128)(2,1)S(1)}, bf16[1280,128]{1,0:T(8,128)(2,1)S(1)}, u32[]{:S(2)}, u32[]{:S(2)}) collective-permute-start(bf16[1280,128]{1,0:T(8,128)(2,1)S(1)} %fusion.4), channel_id=1, source_target_pairs={{0,2},{1,3},{2,0},{3,1},{4,6},{5,7},{6,4},{7,5},{8,10},{9,11},{10,... | collective-permute-start | bytes 983048 | tf_op jit(solution)/shard_map/ppermute | solution.py:34
  83.4 6.7 %collective-permute-done.27 = bf16[1280,128]{1,0:T(8,128)(2,1)S(1)} collective-permute-done((bf16[1280,128]{1,0:T(8,128)(2,1)S(1)}, bf16[1280,128]{1,0:T(8,128)(2,1)S(1)}, u32[]{:S(2)}, u32[]{:S(2)}) %collective-permute-start.27) | collective-permute-done | bytes 327712 | tf_op jit(solution)/shard_map/ppermute | solution.py:34
  90.2 0.1 fusion.8
  90.3 0.7 collective-permute-start.28
  91.0 6.8 %collective-permute-done.30 = bf16[1280,128]{1,0:T(8,128)(2,1)S(1)} collective-permute-done((bf16[1280,128]{1,0:T(8,128)(2,1)S(1)}, bf16[1280,128]{1,0:T(8,128)(2,1)S(1)}, u32[]{:S(2)}, u32[]{:S(2)}) %collective-permute-start.30) | collective-permute-done | bytes 327712 | tf_op jit(solution)/shard_map/ppermute | solution.py:34
  97.8 0.1 fusion.3
  97.9 1.4 %collective-permute-start.31 = (bf16[1280,128]{1,0:T(8,128)(2,1)S(1)}, bf16[1280,128]{1,0:T(8,128)(2,1)S(1)}, u32[]{:S(2)}, u32[]{:S(2)}) collective-permute-start(bf16[1280,128]{1,0:T(8,128)(2,1)S(1)} %fusion.3), channel_id=1, source_target_pairs={{0,12},{1,13},{2,14},{3,15},{4,0},{5,1},{6,2},{7,3},{8,4},{9,5},{1... | collective-permute-start | bytes 983048 | tf_op jit(solution)/shard_map/ppermute | solution.py:34
  99.4 2.0 %collective-permute-done.28 = bf16[1280,128]{1,0:T(8,128)(2,1)S(1)} collective-permute-done((bf16[1280,128]{1,0:T(8,128)(2,1)S(1)}, bf16[1280,128]{1,0:T(8,128)(2,1)S(1)}, u32[]{:S(2)}, u32[]{:S(2)}) %collective-permute-start.28) | collective-permute-done | bytes 327712 | tf_op jit(solution)/shard_map/ppermute | solution.py:34
  101.4 6.6 %collective-permute-done.31 = bf16[1280,128]{1,0:T(8,128)(2,1)S(1)} collective-permute-done((bf16[1280,128]{1,0:T(8,128)(2,1)S(1)}, bf16[1280,128]{1,0:T(8,128)(2,1)S(1)}, u32[]{:S(2)}, u32[]{:S(2)}) %collective-permute-start.31) | collective-permute-done | bytes 327712 | tf_op jit(solution)/shard_map/ppermute | solution.py:34
  107.9 1.0 fusion.14
  (48 shorter events, 0.4 us)
Async XLA Ops:
  0.0 24.5 %collective-permute-start.10 = (bf16[256,4096]{1,0:T(8,128)(2,1)}, bf16[256,4096]{1,0:T(8,128)(2,1)}, u32[]{:S(2)}, u32[]{:S(2)}) collective-permute-start(bf16[256,4096]{1,0:T(8,128)(2,1)} %param.4), channel_id=1, source_target_pairs={{0,1},{1,0},{2,3},{3,2},{4,5},{5,4},{6,7},{7,6},{8,9},{9,8},{10,11... | collective-permute-start | bytes 6291464 | tf_op jit(solution)/shard_map/ppermute | solution.py:34
  1.9 7.9 %collective-permute-start = (s32[2,256]{1,0:T(2,128)S(1)}, s32[2,256]{1,0:T(2,128)S(1)}, u32[]{:S(2)}, u32[]{:S(2)}) collective-permute-start(s32[2,256]{1,0:T(2,128)S(1)} %pad_add_fusion.2), channel_id=1, source_target_pairs={{0,1},{1,0},{2,3},{3,2},{4,5},{5,4},{6,7},{7,6},{8,9},{9,8},{10,11... | collective-permute-start | bytes 6152 | tf_op jit(solution)/shard_map/ppermute | solution.py:34
  3.1 13.6 %collective-permute-start.1 = (bf16[1280,128]{1,0:T(8,128)(2,1)S(1)}, bf16[1280,128]{1,0:T(8,128)(2,1)S(1)}, u32[]{:S(2)}, u32[]{:S(2)}) collective-permute-start(bf16[1280,128]{1,0:T(8,128)(2,1)S(1)} %get-tuple-element.107.refs_0_), channel_id=1, source_target_pairs={{0,4},{1,5},{2,6},{3,7},{4,8},{5,9},{6,10},{7,11},{8,12},{9,13},{1... | collective-permute-start | bytes 983048 | tf_op jit(solution)/shard_map/ppermute | solution.py:34
  6.2 10.5 %collective-permute-start.2 = (bf16[1280,128]{1,0:T(8,128)(2,1)S(1)}, bf16[1280,128]{1,0:T(8,128)(2,1)S(1)}, u32[]{:S(2)}, u32[]{:S(2)}) collective-permute-start(bf16[1280,128]{1,0:T(8,128)(2,1)S(1)} %get-tuple-element.107.refs_0_), channel_id=1, source_target_pairs={{0,2},{1,3},{2,0},{3,1},{4,6},{5,7},{6,4},{7,5},{8,10},{9,11},{10,... | collective-permute-start | bytes 983048 | tf_op jit(solution)/shard_map/ppermute | solution.py:34
  7.7 2.3 %collective-permute-start.7 = (bf16[1280,128]{1,0:T(8,128)(2,1)S(1)}, bf16[1280,128]{1,0:T(8,128)(2,1)}, u32[]{:S(2)}, u32[]{:S(2)}) collective-permute-start(bf16[1280,128]{1,0:T(8,128)(2,1)S(1)} %get-tuple-element.106), channel_id=1, source_target_pairs={{0,1},{1,0},{2,3},{3,2},{4,5},{5,4},{6,7},{7,6},{8,9},{9,8},{10,11... | collective-permute-start | bytes 983048 | tf_op jit(solution)/shard_map/ppermute | solution.py:34
  10.0 13.8 %collective-permute-start.8 = (bf16[1280,128]{1,0:T(8,128)(2,1)}, bf16[1280,128]{1,0:T(8,128)(2,1)S(1)}, u32[]{:S(2)}, u32[]{:S(2)}) collective-permute-start(bf16[1280,128]{1,0:T(8,128)(2,1)} %collective-permute-done.7.refs_1_), channel_id=1, source_target_pairs={{0,4},{1,5},{2,6},{3,7},{4,8},{5,9},{6,10},{7,11},{8,12},{9,13},{1... | collective-permute-start | bytes 983048 | tf_op jit(solution)/shard_map/ppermute | solution.py:34
  11.6 12.1 %collective-permute-start.9 = (bf16[1280,128]{1,0:T(8,128)(2,1)}, bf16[1280,128]{1,0:T(8,128)(2,1)S(1)}, u32[]{:S(2)}, u32[]{:S(2)}) collective-permute-start(bf16[1280,128]{1,0:T(8,128)(2,1)} %collective-permute-done.7.refs_1_), channel_id=1, source_target_pairs={{0,2},{1,3},{2,0},{3,1},{4,6},{5,7},{6,4},{7,5},{8,10},{9,11},{10,... | collective-permute-start | bytes 983048 | tf_op jit(solution)/shard_map/ppermute | solution.py:34
  16.7 14.9 %collective-permute-start.3 = (bf16[1280,128]{1,0:T(8,128)(2,1)S(1)}, bf16[1280,128]{1,0:T(8,128)(2,1)}, u32[]{:S(2)}, u32[]{:S(2)}) collective-permute-start(bf16[1280,128]{1,0:T(8,128)(2,1)S(1)} %collective-permute-done.1.refs_0_), channel_id=1, source_target_pairs={{0,4},{1,5},{2,6},{3,7},{4,8},{5,9},{6,10},{7,11},{8,12},{9,13},{1... | collective-permute-start | bytes 983048 | tf_op jit(solution)/shard_map/ppermute | solution.py:34
  18.0 13.6 %collective-permute-start.4 = (bf16[1280,128]{1,0:T(8,128)(2,1)S(1)}, bf16[1280,128]{1,0:T(8,128)(2,1)S(1)}, u32[]{:S(2)}, u32[]{:S(2)}) collective-permute-start(bf16[1280,128]{1,0:T(8,128)(2,1)S(1)} %collective-permute-done.1.refs_0_), channel_id=1, source_target_pairs={{0,2},{1,3},{2,0},{3,1},{4,6},{5,7},{6,4},{7,5},{8,10},{9,11},{10,... | collective-permute-start | bytes 983048 | tf_op jit(solution)/shard_map/ppermute | solution.py:34
  23.8 0.7 copy-start.1
  27.9 15.3 %collective-permute-start.11 = (bf16[1280,128]{1,0:T(8,128)(2,1)S(1)}, bf16[1280,128]{1,0:T(8,128)(2,1)}, u32[]{:S(2)}, u32[]{:S(2)}) collective-permute-start(bf16[1280,128]{1,0:T(8,128)(2,1)S(1)} %collective-permute-done.8.refs_1_), channel_id=1, source_target_pairs={{0,4},{1,5},{2,6},{3,7},{4,8},{5,9},{6,10},{7,11},{8,12},{9,13},{1... | collective-permute-start | bytes 983048 | tf_op jit(solution)/shard_map/ppermute | solution.py:34
  29.2 14.1 %collective-permute-start.12 = (bf16[1280,128]{1,0:T(8,128)(2,1)S(1)}, bf16[1280,128]{1,0:T(8,128)(2,1)}, u32[]{:S(2)}, u32[]{:S(2)}) collective-permute-start(bf16[1280,128]{1,0:T(8,128)(2,1)S(1)} %collective-permute-done.8.refs_1_), channel_id=1, source_target_pairs={{0,2},{1,3},{2,0},{3,1},{4,6},{5,7},{6,4},{7,5},{8,10},{9,11},{10,... | collective-permute-start | bytes 983048 | tf_op jit(solution)/shard_map/ppermute | solution.py:34
  31.7 0.7 copy-start.3
  32.4 13.0 %collective-permute-start.5 = (bf16[1280,128]{1,0:T(8,128)(2,1)}, bf16[1280,128]{1,0:T(8,128)(2,1)}, u32[]{:S(2)}, u32[]{:S(2)}) collective-permute-start(bf16[1280,128]{1,0:T(8,128)(2,1)} %collective-permute-done.3.refs_0_), channel_id=1, source_target_pairs={{0,4},{1,5},{2,6},{3,7},{4,8},{5,9},{6,10},{7,11},{8,12},{9,13},{1... | collective-permute-start | bytes 983048 | tf_op jit(solution)/shard_map/ppermute | solution.py:34
  34.0 11.4 %collective-permute-start.6 = (bf16[1280,128]{1,0:T(8,128)(2,1)}, bf16[1280,128]{1,0:T(8,128)(2,1)}, u32[]{:S(2)}, u32[]{:S(2)}) collective-permute-start(bf16[1280,128]{1,0:T(8,128)(2,1)} %collective-permute-done.3.refs_0_), channel_id=1, source_target_pairs={{0,2},{1,3},{2,0},{3,1},{4,6},{5,7},{6,4},{7,5},{8,10},{9,11},{10,... | collective-permute-start | bytes 983048 | tf_op jit(solution)/shard_map/ppermute | solution.py:34
  36.6 1.6 %copy-start = (bf16[32,8,32,128]{3,2,1,0:T(8,128)(2,1)S(1)}, bf16[32,8,32,128]{3,2,1,0:T(8,128)(2,1)}, u32[]{:S(2)}) copy-start(bf16[32,8,32,128]{3,2,1,0:T(8,128)(2,1)} %copy.12) | copy-start | bytes 6291460
  38.2 7.1 %copy-start.2 = (bf16[1280,128]{1,0:T(8,128)(2,1)S(1)}, bf16[1280,128]{1,0:T(8,128)(2,1)}, u32[]{:S(2)}) copy-start(bf16[1280,128]{1,0:T(8,128)(2,1)} %copy-done.1) | copy-start | bytes 983044
  43.3 11.4 %collective-permute-start.14 = (bf16[1280,128]{1,0:T(8,128)(2,1)}, bf16[1280,128]{1,0:T(8,128)(2,1)S(1)}, u32[]{:S(2)}, u32[]{:S(2)}) collective-permute-start(bf16[1280,128]{1,0:T(8,128)(2,1)} %collective-permute-done.11.refs_1_), channel_id=1, source_target_pairs={{0,4},{1,5},{2,6},{3,7},{4,8},{5,9},{6,10},{7,11},{8,12},{9,13},{1... | collective-permute-start | bytes 983048 | tf_op jit(solution)/shard_map/ppermute | solution.py:34
  44.4 10.4 %collective-permute-start.15 = (bf16[1280,128]{1,0:T(8,128)(2,1)}, bf16[1280,128]{1,0:T(8,128)(2,1)S(1)}, u32[]{:S(2)}, u32[]{:S(2)}) collective-permute-start(bf16[1280,128]{1,0:T(8,128)(2,1)} %collective-permute-done.11.refs_1_), channel_id=1, source_target_pairs={{0,2},{1,3},{2,0},{3,1},{4,6},{5,7},{6,4},{7,5},{8,10},{9,11},{10,... | collective-permute-start | bytes 983048 | tf_op jit(solution)/shard_map/ppermute | solution.py:34
  45.4 4.5 %copy-start.4 = (bf16[1280,128]{1,0:T(8,128)(2,1)S(1)}, bf16[1280,128]{1,0:T(8,128)(2,1)}, u32[]{:S(2)}) copy-start(bf16[1280,128]{1,0:T(8,128)(2,1)} %copy-done.3) | copy-start | bytes 983044
  49.6 11.2 %collective-permute-start.13 = (bf16[1280,128]{1,0:T(8,128)(2,1)}, bf16[1280,128]{1,0:T(8,128)(2,1)S(1)}, u32[]{:S(2)}, u32[]{:S(2)}) collective-permute-start(bf16[1280,128]{1,0:T(8,128)(2,1)} %collective-permute-done.6.refs_2_), channel_id=1, source_target_pairs={{0,4},{1,5},{2,6},{3,7},{4,8},{5,9},{6,10},{7,11},{8,12},{9,13},{1... | collective-permute-start | bytes 983048 | tf_op jit(solution)/shard_map/ppermute | solution.py:34
  54.7 7.5 %collective-permute-start.16 = (bf16[1280,128]{1,0:T(8,128)(2,1)S(1)}, bf16[1280,128]{1,0:T(8,128)(2,1)S(1)}, u32[]{:S(2)}, u32[]{:S(2)}) collective-permute-start(bf16[1280,128]{1,0:T(8,128)(2,1)S(1)} %collective-permute-done.14.refs_1_), channel_id=1, source_target_pairs={{0,2},{1,3},{2,0},{3,1},{4,6},{5,7},{6,4},{7,5},{8,10},{9,11},{10,... | collective-permute-start | bytes 983048 | tf_op jit(solution)/shard_map/ppermute | solution.py:34
  65.5 2.5 %collective-permute-start.18 = (bf16[1280,128]{1,0:T(8,128)(2,1)S(1)}, bf16[1280,128]{1,0:T(8,128)(2,1)S(1)}, u32[]{:S(2)}, u32[]{:S(2)}) collective-permute-start(bf16[1280,128]{1,0:T(8,128)(2,1)S(1)} %bitcast.78), channel_id=1, source_target_pairs={{0,1},{1,0},{2,3},{3,2},{4,5},{5,4},{6,7},{7,6},{8,9},{9,8},{10,11... | collective-permute-start | bytes 983048 | tf_op jit(solution)/shard_map/ppermute | solution.py:34
  65.6 2.5 %collective-permute-start.17 = (bf16[1280,128]{1,0:T(8,128)(2,1)S(1)}, bf16[1280,128]{1,0:T(8,128)(2,1)S(1)}, u32[]{:S(2)}, u32[]{:S(2)}) collective-permute-start(bf16[1280,128]{1,0:T(8,128)(2,1)S(1)} %bitcast.76), channel_id=1, source_target_pairs={{0,1},{1,0},{2,3},{3,2},{4,5},{5,4},{6,7},{7,6},{8,9},{9,8},{10,11... | collective-permute-start | bytes 983048 | tf_op jit(solution)/shard_map/ppermute | solution.py:34
  66.1 12.6 %collective-permute-start.20 = (bf16[1280,128]{1,0:T(8,128)(2,1)S(1)}, bf16[1280,128]{1,0:T(8,128)(2,1)S(1)}, u32[]{:S(2)}, u32[]{:S(2)}) collective-permute-start(bf16[1280,128]{1,0:T(8,128)(2,1)S(1)} %bitcast.71), channel_id=1, source_target_pairs={{0,1},{1,0},{2,3},{3,2},{4,5},{5,4},{6,7},{7,6},{8,9},{9,8},{10,11... | collective-permute-start | bytes 983048 | tf_op jit(solution)/shard_map/ppermute | solution.py:34
  66.2 6.1 %collective-permute-start.25 = (bf16[1280,128]{1,0:T(8,128)(2,1)S(1)}, bf16[1280,128]{1,0:T(8,128)(2,1)S(1)}, u32[]{:S(2)}, u32[]{:S(2)}) collective-permute-start(bf16[1280,128]{1,0:T(8,128)(2,1)S(1)} %bitcast.74), channel_id=1, source_target_pairs={{0,1},{1,0},{2,3},{3,2},{4,5},{5,4},{6,7},{7,6},{8,9},{9,8},{10,11... | collective-permute-start | bytes 983048 | tf_op jit(solution)/shard_map/ppermute | solution.py:34
  68.2 13.0 %collective-permute-start.21 = (bf16[1280,128]{1,0:T(8,128)(2,1)S(1)}, bf16[1280,128]{1,0:T(8,128)(2,1)S(1)}, u32[]{:S(2)}, u32[]{:S(2)}) collective-permute-start(bf16[1280,128]{1,0:T(8,128)(2,1)S(1)} %fusion.16), channel_id=1, source_target_pairs={{0,4},{1,5},{2,6},{3,7},{4,8},{5,9},{6,10},{7,11},{8,12},{9,13},{1... | collective-permute-start | bytes 983048 | tf_op jit(solution)/shard_map/ppermute | solution.py:34
  68.2 9.8 %collective-permute-start.26 = (bf16[1280,128]{1,0:T(8,128)(2,1)S(1)}, bf16[1280,128]{1,0:T(8,128)(2,1)S(1)}, u32[]{:S(2)}, u32[]{:S(2)}) collective-permute-start(bf16[1280,128]{1,0:T(8,128)(2,1)S(1)} %fusion.15), channel_id=1, source_target_pairs={{0,2},{1,3},{2,0},{3,1},{4,6},{5,7},{6,4},{7,5},{8,10},{9,11},{10,... | collective-permute-start | bytes 983048 | tf_op jit(solution)/shard_map/ppermute | solution.py:34
  72.2 5.9 %collective-permute-start.24 = (bf16[1280,128]{1,0:T(8,128)(2,1)S(1)}, bf16[1280,128]{1,0:T(8,128)(2,1)S(1)}, u32[]{:S(2)}, u32[]{:S(2)}) collective-permute-start(bf16[1280,128]{1,0:T(8,128)(2,1)S(1)} %bitcast.77), channel_id=1, source_target_pairs={{0,1},{1,0},{2,3},{3,2},{4,5},{5,4},{6,7},{7,6},{8,9},{9,8},{10,11... | collective-permute-start | bytes 983048 | tf_op jit(solution)/shard_map/ppermute | solution.py:34
  72.2 9.7 %collective-permute-start.23 = (bf16[1280,128]{1,0:T(8,128)(2,1)S(1)}, bf16[1280,128]{1,0:T(8,128)(2,1)S(1)}, u32[]{:S(2)}, u32[]{:S(2)}) collective-permute-start(bf16[1280,128]{1,0:T(8,128)(2,1)S(1)} %bitcast.75), channel_id=1, source_target_pairs={{0,1},{1,0},{2,3},{3,2},{4,5},{5,4},{6,7},{7,6},{8,9},{9,8},{10,11... | collective-permute-start | bytes 983048 | tf_op jit(solution)/shard_map/ppermute | solution.py:34
  78.0 13.0 %collective-permute-start.29 = (bf16[1280,128]{1,0:T(8,128)(2,1)S(1)}, bf16[1280,128]{1,0:T(8,128)(2,1)S(1)}, u32[]{:S(2)}, u32[]{:S(2)}) collective-permute-start(bf16[1280,128]{1,0:T(8,128)(2,1)S(1)} %bitcast.73), channel_id=1, source_target_pairs={{0,1},{1,0},{2,3},{3,2},{4,5},{5,4},{6,7},{7,6},{8,9},{9,8},{10,11... | collective-permute-start | bytes 983048 | tf_op jit(solution)/shard_map/ppermute | solution.py:34
  78.1 21.3 %collective-permute-start.19 = (bf16[1280,128]{1,0:T(8,128)(2,1)S(1)}, bf16[1280,128]{1,0:T(8,128)(2,1)S(1)}, u32[]{:S(2)}, u32[]{:S(2)}) collective-permute-start(bf16[1280,128]{1,0:T(8,128)(2,1)S(1)} %bitcast.72), channel_id=1, source_target_pairs={{0,1},{1,0},{2,3},{3,2},{4,5},{5,4},{6,7},{7,6},{8,9},{9,8},{10,11... | collective-permute-start | bytes 983048 | tf_op jit(solution)/shard_map/ppermute | solution.py:34
  78.7 11.5 %collective-permute-start.27 = (bf16[1280,128]{1,0:T(8,128)(2,1)S(1)}, bf16[1280,128]{1,0:T(8,128)(2,1)S(1)}, u32[]{:S(2)}, u32[]{:S(2)}) collective-permute-start(bf16[1280,128]{1,0:T(8,128)(2,1)S(1)} %fusion.6), channel_id=1, source_target_pairs={{0,4},{1,5},{2,6},{3,7},{4,8},{5,9},{6,10},{7,11},{8,12},{9,13},{1... | collective-permute-start | bytes 983048 | tf_op jit(solution)/shard_map/ppermute | solution.py:34
  81.3 18.0 %collective-permute-start.22 = (bf16[1280,128]{1,0:T(8,128)(2,1)S(1)}, bf16[1280,128]{1,0:T(8,128)(2,1)S(1)}, u32[]{:S(2)}, u32[]{:S(2)}) collective-permute-start(bf16[1280,128]{1,0:T(8,128)(2,1)S(1)} %fusion.10), channel_id=1, source_target_pairs={{0,2},{1,3},{2,0},{3,1},{4,6},{5,7},{6,4},{7,5},{8,10},{9,11},{10,... | collective-permute-start | bytes 983048 | tf_op jit(solution)/shard_map/ppermute | solution.py:34
  81.9 15.8 %collective-permute-start.30 = (bf16[1280,128]{1,0:T(8,128)(2,1)S(1)}, bf16[1280,128]{1,0:T(8,128)(2,1)S(1)}, u32[]{:S(2)}, u32[]{:S(2)}) collective-permute-start(bf16[1280,128]{1,0:T(8,128)(2,1)S(1)} %fusion.4), channel_id=1, source_target_pairs={{0,2},{1,3},{2,0},{3,1},{4,6},{5,7},{6,4},{7,5},{8,10},{9,11},{10,... | collective-permute-start | bytes 983048 | tf_op jit(solution)/shard_map/ppermute | solution.py:34
  90.3 11.0 %collective-permute-start.28 = (bf16[1280,128]{1,0:T(8,128)(2,1)S(1)}, bf16[1280,128]{1,0:T(8,128)(2,1)S(1)}, u32[]{:S(2)}, u32[]{:S(2)}) collective-permute-start(bf16[1280,128]{1,0:T(8,128)(2,1)S(1)} %fusion.8), channel_id=1, source_target_pairs={{0,4},{1,5},{2,6},{3,7},{4,8},{5,9},{6,10},{7,11},{8,12},{9,13},{1... | collective-permute-start | bytes 983048 | tf_op jit(solution)/shard_map/ppermute | solution.py:34
  97.9 10.0 %collective-permute-start.31 = (bf16[1280,128]{1,0:T(8,128)(2,1)S(1)}, bf16[1280,128]{1,0:T(8,128)(2,1)S(1)}, u32[]{:S(2)}, u32[]{:S(2)}) collective-permute-start(bf16[1280,128]{1,0:T(8,128)(2,1)S(1)} %fusion.3), channel_id=1, source_target_pairs={{0,12},{1,13},{2,14},{3,15},{4,0},{5,1},{6,2},{7,3},{8,4},{9,5},{1... | collective-permute-start | bytes 983048 | tf_op jit(solution)/shard_map/ppermute | solution.py:34

commit v10 on v9

--- a/solution.py
+++ b/solution.py
@@ -11,7 +11,7 @@
 BLK = 64
 WIN = 128
 LANES = 128
-UNROLL = 8
+UNROLL = 16
 LINE = 4
 SCOPED_BYTES = 6 * 1024 * 1024
 
@@ -37,29 +37,24 @@
 ALONG = pairs_of(lambda z, x: ((z + 1) % LINE, x))
 BACK = pairs_of(lambda z, x: ((z - 1) % LINE, x))
 ACROSS = pairs_of(lambda z, x: (z, 1 - x))
-ADD_AT = {(2, 1): 0, (3, 0): 1, (3, 1): 2}
-LAY_AT = (1, 1)
-
-
-def spread(parts, meanwhile):
-    lines, others = [[part] for part in parts], [[] for _ in parts]
-
-    def arrived(stage):
-        held = [line[stage] for line in lines] if stage < LINE else []
-        return held + ([other[stage - 1] for other in others] if stage else [])
-
+ADD_AT = {2: (0,), 3: (1, 2)}
+LAY_AT = 1
+
+
+def spread(own, meanwhile):
+    stages = [[own]]
+    line, other = own, None
     for step in range(LINE):
-        for index, (line, other) in enumerate(zip(lines, others)):
-            if other:
-                line[-1], other[-1] = tie(line[-1], other[-1])
-            turn = step == LINE - 1 and index == 0
-            source = other if turn else line
-            source[-1] = meanwhile(step, index, arrived, source[-1])
-            now = source[-1]
-            if step + 1 < LINE:
-                line.append(move(now, ALONG))
-            other.append(move(now, ALONG if turn else ACROSS))
-    return [arrived(stage) for stage in range(LINE + 1)]
+        line = meanwhile(step, stages, line)
+        if other is not None:
+            line, other = tie(line, other)
+            stages[-1][:] = [line, other]
+        if step + 1 < LINE:
+            line, other = move(line, ALONG), move(line, ACROSS)
+            stages.append([line, other])
+    half = own.shape[0] // 2
+    stages.append([move(other[:half], ALONG), move(line[half:], ACROSS)])
+    return stages
 
 
 def collect(far_keep, far_send, near_of, half, swap):
@@ -76,7 +71,8 @@
     near = {step: paired(near_keep[step], near_send[step]) for step in (2, 1, 3, 0)}
     crossing, crossed[2] = tie(far[3].astype(jnp.bfloat16), crossed[2])
     crossed[3] = move(crossing, ACROSS)
-    crossed[0] = move((far[0] + joining.astype(jnp.float32)).astype(jnp.bfloat16), ACROSS)
+    crossing, crossed[3] = tie((far[0] + joining.astype(jnp.float32)).astype(jnp.bfloat16), crossed[3])
+    crossed[0] = move(crossing, ACROSS)
 
     two_on = move((near[2] + crossed[2].astype(jnp.float32)).astype(jnp.bfloat16), ALONG)
     one_on = move((near[1] + two_on.astype(jnp.float32)).astype(jnp.bfloat16), ALONG)
@@ -100,8 +96,10 @@
         pltpu.make_async_copy(source, occ.at[pl.ds(index * rows, rows)], sem).start()
     pltpu.make_async_copy(occ, occ, sem).wait()
     begin, end = bounds_ref[stage], bounds_ref[stage + 1]
+    low = lax.broadcasted_iota(jnp.int32, tiles.shape[1:], 1) < BLK
+    zero = jnp.zeros(tiles.shape[1:], jnp.bfloat16)
     spill = half.shape[0] - BLK
-    columns = 2 + pieces
+    entries = table_ref.shape[0] // (2 + pieces)
     piece = BLK // pieces
 
     @pl.loop(0, (end - begin + UNROLL - 1) // UNROLL)
@@ -109,13 +107,13 @@
         products, starts = [], []
         for lane in range(UNROLL):
             entry = begin + group * UNROLL + lane
-            tile = table_ref[entry * columns]
-            starts.append(jnp.where(entry < end, table_ref[entry * columns + 1], spill))
-            spots = [jnp.where(entry < end, table_ref[entry * columns + 2 + cut], 0) for cut in range(pieces)]
+            tile = table_ref[entry]
+            starts.append(jnp.where(entry < end, table_ref[entries + entry], spill))
+            spots = [jnp.where(entry < end, table_ref[(2 + cut) * entries + entry], 0) for cut in range(pieces)]
             parts = [occ[pl.ds(pl.multiple_of(spot, piece), piece), :] for spot in spots]
             pair = tiles[tile]
-            left = jnp.concatenate([pair[:, :BLK], pair[:, BLK:]], axis=0)
-            block = parts[0] if pieces == 1 else jnp.concatenate(parts, axis=0)
+            left = jnp.concatenate([jnp.where(low, pair, zero), jnp.where(low, zero, pair)], axis=0)
+            block = jnp.concatenate(parts * 2, axis=0)
             products.append(jnp.dot(left, block, preferred_element_type=jnp.float32))
         for product, start in zip(products, starts):
             start = pl.multiple_of(start, BLK)
@@ -221,9 +219,11 @@
     mine = lax.dynamic_slice_in_dim(occupied, core * LANES, LANES, 1)
     given = lax.dynamic_slice_in_dim(occupied, (1 - core) * LANES, LANES, 1)
     parts = (mine, move(given, swap))
-    tile_sets = [
-        values.reshape(slots, BLK * BLK // LANES, LANES) for values in (block_values, move(block_values, swap))
-    ]
+    others = [move(array, swap) for array in (block_values, block_pairs, live_counts)]
+    own, block_values, block_pairs, live_counts = tie(
+        jnp.concatenate(parts, axis=0), block_values, block_pairs, live_counts
+    )
+    tile_sets = [values.reshape(slots, BLK * BLK // LANES, LANES) for values in (block_values, others[0])]
 
     slot_ids = jnp.arange(chips, dtype=jnp.int32)
     chip_of_slot = slot_ids
@@ -233,10 +233,9 @@
         stage_count = LINE + 1
 
     tile_ids = jnp.arange(2 * slots, dtype=jnp.int32)
-    row_starts = jnp.where(tile_ids[:slots] < live_counts[0], block_pairs[:, 0] * BLK, -1)
-    table = jnp.stack([row_starts, block_pairs[:, 1]])
-    both = jnp.concatenate([table, move(table, swap)], axis=1)
-    first = both[1][:, None] * BLK + jnp.arange(pieces, dtype=jnp.int32) * piece
+    pairs = jnp.concatenate([block_pairs, others[1]])
+    live = tile_ids % slots < jnp.where(tile_ids < slots, live_counts[0], others[2][0])
+    first = pairs[:, 1][:, None] * BLK + jnp.arange(pieces, dtype=jnp.int32) * piece
     owner = first // shard
     part = (owner % 2) ^ core
     owner_chip = owner // 2
@@ -247,10 +246,10 @@
         slot_of = part + 2 * jnp.where(back + side < LINE, side, 0)
     else:
         stage = jnp.zeros_like(tile_ids)
-        slot_of = part * chips + owner_chip
+        slot_of = 2 * owner_chip + part
     spots = slot_of * shard + first % shard
-    stage = jnp.where(both[0] >= 0, stage, stage_count)
-    rows = both[0] + tile_ids // slots * total
+    stage = jnp.where(live, stage, stage_count)
+    rows = pairs[:, 0] * BLK + tile_ids // slots * total
     ahead = (stage[None, :] < stage[:, None]) | (
         (stage[None, :] == stage[:, None]) & (tile_ids[None, :] < tile_ids[:, None])
     )
@@ -258,9 +257,7 @@
     entries = jnp.arange(2 * slots + UNROLL, dtype=jnp.int32)
     chosen = rank[None, :] == entries[:, None]
     columns = [tile_ids, rows] + [spots[:, cut] for cut in range(pieces)]
-    ordered = jnp.stack(
-        [jnp.sum(jnp.where(chosen, column[None, :], 0), axis=1) for column in columns], axis=1
-    ).reshape(-1)
+    ordered = jnp.concatenate([jnp.sum(jnp.where(chosen, column[None, :], 0), axis=1) for column in columns])
     bounds = jnp.sum((stage[None, :] < jnp.arange(stage_count + 1)[:, None]).astype(jnp.int32), axis=1)
     cores = core.astype(jnp.int32).reshape(1)
 
@@ -287,21 +284,20 @@
         kernel = functools.partial(stage_kernel, stage, len(sources), pieces)
         run_stage(kernel, sources, [ordered, bounds], [], work)
 
-    def meanwhile(step, index, arrived, moved):
-        if (step, index) == LAY_AT:
+    def meanwhile(step, stages, moved):
+        if step == LAY_AT:
             moved, *tile_sets[:] = tie(moved, *tile_sets)
-        if (step, index) in ADD_AT:
-            stage = ADD_AT[step, index]
-            add(stage, arrived(stage))
+        for stage in ADD_AT.get(step, ()):
+            add(stage, stages[stage])
             moved, state[0] = tie(moved, state[0])
         return moved
 
     if lined:
-        stages = spread(parts, meanwhile)
-        for stage in range(len(ADD_AT), LINE):
+        stages = spread(own, meanwhile)
+        for stage in range(sum(map(len, ADD_AT.values())), LINE):
             add(stage, stages[stage])
     else:
-        stages = [[lax.all_gather(part, "aux", axis_index_groups=same_core, axis=0, tiled=True) for part in parts]]
+        stages = [[lax.all_gather(own, "aux", axis_index_groups=same_core, axis=0, tiled=True)]]
 
     group = 1 if lined else chips // 2
     far = [group] * (chips // 2 // group)

time: 110 us -> 119 us (1.082)
  waiting for transfers between devices: 37.1 us -> 70.3 us
  starting transfers between devices: 30.6 us -> 17.9 us
  Pallas kernels: 24.9 us -> 16.4 us
  local copies, waits for them, and re-layouts: 11.7 us -> 9.13 us
    ppermute x32 -> x27, waiting for transfers between devices: 37.1 us -> 70.3 us  [move(): return lax.ppermute(array, 'aux', pairs)]
    ppermute x32 -> x27, starting transfers between devices: 30.6 us -> 17.9 us  [move(): return lax.ppermute(array, 'aux', pairs)]
    pallas_call x7, Pallas kernels: 24.9 us -> 16.4 us  [call(): pl.pallas_call(kernel, out_shape=outs, in_specs=in_specs, out_specs=[VMEM...]
    select_n x4 -> x2, other arithmetic: 0.07 us -> 1.44 us  [local(): stage = jnp.where(live, stage, stage_count)]
    unnamed x12 -> x11, local copies, waits for them, and re-layouts: 8.51 us -> 7.89 us
  transfers between devices with their start and end apart: 32 -> 27, of which waited for: 9 -> 12; matrix products, arithmetic and copies ran while one was open for 10% -> 8% of each run, Pallas kernels for 20% -> 12%
where the time goes in v10:
time: 119 us
  waiting for transfers between devices  70.3 us (59%)
  starting transfers between devices  17.9 us (15%)
  Pallas kernels  16.4 us (14%)
  local copies, waits for them, and re-layouts  9.13 us (8%)
  other arithmetic  4.26 us (4%)
    ppermute x27, waiting for transfers between devices, move(): return lax.ppermute(array, 'aux', pairs)  70.3 us
    ppermute x27, starting transfers between devices, move(): return lax.ppermute(array, 'aux', pairs)  17.9 us
    pallas_call x7, Pallas kernels, call(): pl.pallas_call(kernel, out_shape=outs, in_specs=in_specs, out_specs=[VMEM...  16.4 us
    unnamed x11, local copies, waits for them, and re-layouts  7.89 us
  transfers between devices with their start and end apart: 27, of which 12 were waited for; matrix products, arithmetic and copies ran while one was open for 8% of the time, Pallas kernels for 12%

profile of v10, /device:TPU:0, one launch (start us, length us, event | category | flops | bytes accessed | tf_op | source)
XLA Modules:
  0.0 119.0 jit_solution(11641533796237613150)
XLA Ops:
  0.0 0.5 collective-permute-start.4
  0.5 1.1 constant_dynamic-slice_fusion.1
  1.6 0.1 collective-permute-start
  1.7 0.5 collective-permute-start.2
  2.2 0.1 collective-permute-start.1
  2.9 1.8 %collective-permute-done = bf16[1280,128]{1,0:T(8,128)(2,1)S(1)} collective-permute-done((bf16[1280,128]{1,0:T(8,128)(2,1)S(1)}, bf16[1280,128]{1,0:T(8,128)(2,1)S(1)}, u32[]{:S(2)}, u32[]{:S(2)}) %collective-permute-start) | collective-permute-done | bytes 327712 | tf_op jit(solution)/shard_map/ppermute | solution.py:34
  4.8 3.0 %collective-permute-start.3 = (bf16[2560,128]{1,0:T(8,128)(2,1)S(1)}, bf16[2560,128]{1,0:T(8,128)(2,1)S(1)}, u32[]{:S(2)}, u32[]{:S(2)}) collective-permute-start(bf16[2560,128]{1,0:T(8,128)(2,1)S(1)} %pad_maximum_fusion.refs_0_), channel_id=1, source_target_pairs={{0,4},{1,5},{2,6},{3,7},{4,8},{5,9},{6,10},{7,11},{8,12},{9,13},{1... | collective-permute-start | bytes 1966088 | tf_op jit(solution)/shard_map/ppermute | solution.py:34
  7.8 1.5 %collective-permute-start.5 = (bf16[2560,128]{1,0:T(8,128)(2,1)S(1)}, bf16[2560,128]{1,0:T(8,128)(2,1)S(1)}, u32[]{:S(2)}, u32[]{:S(2)}) collective-permute-start(bf16[2560,128]{1,0:T(8,128)(2,1)S(1)} %pad_maximum_fusion.refs_0_), channel_id=1, source_target_pairs={{0,2},{1,3},{2,0},{3,1},{4,6},{5,7},{6,4},{7,5},{8,10},{9,11},{10,... | collective-permute-start | bytes 1966088 | tf_op jit(solution)/shard_map/ppermute | solution.py:34
  9.2 2.1 %copy.9 = bf16[32,8,32,128]{3,2,1,0:T(8,128)(2,1)S(1)} copy(bf16[32,8,32,128]{3,1,2,0:T(8,128)(2,1)} %bitcast.77) | data formatting | bytes 4194304
  11.3 0.0 collective-permute-done.2
  11.4 0.7 compare_select_fusion.3
  12.1 0.7 fusion.31
  12.8 0.0 collective-permute-done.4
  12.9 3.4 %copy.10 = bf16[32,8,32,128]{3,2,1,0:T(8,128)(2,1)} copy(bf16[32,8,32,128]{3,1,2,0:T(8,128)(2,1)} %bitcast.25) | data formatting | bytes 4194304
  16.2 8.6 %collective-permute-done.3.refs_0_ = bf16[2560,128]{1,0:T(8,128)(2,1)S(1)} collective-permute-done((bf16[2560,128]{1,0:T(8,128)(2,1)S(1)}, bf16[2560,128]{1,0:T(8,128)(2,1)S(1)}, u32[]{:S(2)}, u32[]{:S(2)}) %collective-permute-start.3) | collective-permute-done | bytes 655392 | tf_op jit(solution)/shard_map/ppermute | solution.py:34
  24.8 0.8 copy-done.1
  25.7 1.0 collective-permute-start.6
  26.7 1.5 %collective-permute-start.7 = (bf16[2560,128]{1,0:T(8,128)(2,1)S(1)}, bf16[2560,128]{1,0:T(8,128)(2,1)}, u32[]{:S(2)}, u32[]{:S(2)}) collective-permute-start(bf16[2560,128]{1,0:T(8,128)(2,1)S(1)} %collective-permute-done.3.refs_0_), channel_id=1, source_target_pairs={{0,2},{1,3},{2,0},{3,1},{4,6},{5,7},{6,4},{7,5},{8,10},{9,11},{10,... | collective-permute-start | bytes 1966088 | tf_op jit(solution)/shard_map/ppermute | solution.py:34
  28.2 0.3 convert_reduce_fusion
  28.5 0.5 select_reduce_fusion
  29.0 0.1 concatenate.11.table_ref
  29.1 0.1 convert_reduce_fusion.1.bounds_ref
  29.2 1.6 %copy-done = bf16[32,8,32,128]{3,2,1,0:T(8,128)(2,1)S(1)} copy-done((bf16[32,8,32,128]{3,2,1,0:T(8,128)(2,1)S(1)}, bf16[32,8,32,128]{3,2,1,0:T(8,128)(2,1)}, u32[]{:S(2)}) %copy-start) | copy-done | bytes 2097176
  30.8 3.3 %shard_map.46 = (f32[41024,128]{1,0:T(8,128)S(1)}, bf16[512,32,128]{2,1,0:T(8,128)(2,1)S(1)}) custom-call(s32[1584]{0:T(1024)S(1)} %concatenate.11.table_ref, s32[6]{0:T(128)S(1)} %convert_reduce_fusion.1.bounds_ref, bf16[2560,128]{1,0:T(8,128)(2,1)S(1)} %pad_maximum_fusion.refs_0_, bf16[256,32,128]{2,1,0:T(8,128)(2,1)S(1)} %bitcast.67, ...), custom_call_target="tpu_custom_call" | custom-call | flops 107374184 | bytes 4194304 | tf_op jit(solution)/shard_map/pallas_call | solution.py:193
  34.1 9.7 %collective-permute-done.6.refs_0_ = bf16[2560,128]{1,0:T(8,128)(2,1)} collective-permute-done((bf16[2560,128]{1,0:T(8,128)(2,1)S(1)}, bf16[2560,128]{1,0:T(8,128)(2,1)}, u32[]{:S(2)}, u32[]{:S(2)}) %collective-permute-start.6) | collective-permute-done | bytes 655392 | tf_op jit(solution)/shard_map/ppermute | solution.py:34
  43.8 0.0 collective-permute-done.7.refs_1_
  43.8 1.3 %collective-permute-start.9 = (bf16[2560,128]{1,0:T(8,128)(2,1)}, bf16[2560,128]{1,0:T(8,128)(2,1)S(1)}, u32[]{:S(2)}, u32[]{:S(2)}) collective-permute-start(bf16[2560,128]{1,0:T(8,128)(2,1)} %collective-permute-done.6.refs_0_), channel_id=1, source_target_pairs={{0,2},{1,3},{2,0},{3,1},{4,6},{5,7},{6,4},{7,5},{8,10},{9,11},{10,... | collective-permute-start | bytes 1966088 | tf_op jit(solution)/shard_map/ppermute | solution.py:34
  45.2 1.9 %shard_map.47.refs_3_ = f32[41024,128]{1,0:T(8,128)S(1)} custom-call(s32[1584]{0:T(1024)S(1)} %concatenate.11.table_ref, s32[6]{0:T(128)S(1)} %convert_reduce_fusion.1.bounds_ref, bf16[2560,128]{1,0:T(8,128)(2,1)S(1)} %collective-permute-done.3.refs_0_, bf16[2560,128]{1,0:T(8,128)(2,1)S(1)} %copy-done.2, ...), custom_call_target="tpu_custom_call", output_to_operand_aliasing={{}: (5, {})} | custom-call | flops 107374184 | bytes 4194304 | tf_op jit(solution)/shard_map/pallas_call | solution.py:193
  47.1 14.1 %collective-permute-done.8.refs_0_ = bf16[2560,128]{1,0:T(8,128)(2,1)S(1)} collective-permute-done((bf16[2560,128]{1,0:T(8,128)(2,1)}, bf16[2560,128]{1,0:T(8,128)(2,1)S(1)}, u32[]{:S(2)}, u32[]{:S(2)}) %collective-permute-start.8) | collective-permute-done | bytes 655392 | tf_op jit(solution)/shard_map/ppermute | solution.py:34
  61.2 3.1 %shard_map.48.refs_3_ = f32[41024,128]{1,0:T(8,128)S(1)} custom-call(s32[1584]{0:T(1024)S(1)} %concatenate.11.table_ref, s32[6]{0:T(128)S(1)} %convert_reduce_fusion.1.bounds_ref, bf16[2560,128]{1,0:T(8,128)(2,1)} %collective-permute-done.6.refs_0_, bf16[2560,128]{1,0:T(8,128)(2,1)} %collective-permute-done.7.refs_1_, ...), custom_call_target="tpu_custom_call", output_to_operand_aliasing={{}: (5, {})} | custom-call | flops 107374184 | bytes 4194304 | tf_op jit(solution)/shard_map/pallas_call | solution.py:193
  64.3 0.1 collective-permute-start.10
  64.4 1.6 %collective-permute-start.11 = (bf16[1280,128]{1,0:T(8,128)(2,1)S(1)}, bf16[1280,128]{1,0:T(8,128)(2,1)S(1)}, u32[]{:S(2)}, u32[]{:S(2)}) collective-permute-start(bf16[1280,128]{1,0:T(8,128)(2,1)S(1)} %slice.15), channel_id=1, source_target_pairs={{0,2},{1,3},{2,0},{3,1},{4,6},{5,7},{6,4},{7,5},{8,10},{9,11},{10,... | collective-permute-start | bytes 983048 | tf_op jit(solution)/shard_map/ppermute | solution.py:34
  66.0 2.2 %shard_map.49.refs_3_ = f32[41024,128]{1,0:T(8,128)S(1)} custom-call(s32[1584]{0:T(1024)S(1)} %concatenate.11.table_ref, s32[6]{0:T(128)S(1)} %convert_reduce_fusion.1.bounds_ref, bf16[2560,128]{1,0:T(8,128)(2,1)S(1)} %collective-permute-done.8.refs_0_, bf16[2560,128]{1,0:T(8,128)(2,1)S(1)} %collective-permute-done.9.refs_1_, ...), custom_call_target="tpu_custom_call", output_to_operand_aliasing={{}: (5, {})} | custom-call | flops 107374184 | bytes 4194304 | tf_op jit(solution)/shard_map/pallas_call | solution.py:193
  68.3 5.3 %collective-permute-done.10.refs_0_ = bf16[1280,128]{1,0:T(8,128)(2,1)S(1)} collective-permute-done((bf16[1280,128]{1,0:T(8,128)(2,1)S(1)}, bf16[1280,128]{1,0:T(8,128)(2,1)S(1)}, u32[]{:S(2)}, u32[]{:S(2)}) %collective-permute-start.10) | collective-permute-done | bytes 327712 | tf_op jit(solution)/shard_map/ppermute | solution.py:34
  73.6 2.4 %shard_map.50 = (f32[41024,128]{1,0:T(8,128)S(1)}, bf16[256,128]{1,0:T(8,128)(2,1)S(1)}, bf16[1,1280,128]{2,1,0:T(8,128)(2,1)S(1)}, bf16[1,1280,128]{2,1,0:T(8,1...) custom-call(s32[1584]{0:T(1024)S(1)} %concatenate.11.table_ref, ...), custom_call_target="tpu_custom_call", output_to_operand_aliasing={{0}: (7, {})} | custom-call | flops 442918496 | bytes 4194304 | tf_op jit(solution)/shard_map/pallas_call | solution.py:193
  76.0 0.1 collective-permute-start.13
  76.1 0.5 collective-permute-start.17
  76.6 0.1 collective-permute-start.12
  76.7 0.4 collective-permute-start.15
  77.1 1.4 %shard_map.51 = (f32[1,1280,128]{2,1,0:T(8,128)S(1)}, f32[1,1280,128]{2,1,0:T(8,128)S(1)}, f32[1,1280,128]{2,1,0:T(8,128)S(1)}, f32[1,1280,128]{2,1,0:T(8,128)S(1)}) custom-call(s32[8]{0:T(128)S(1)} %fusion.34.chips_ref, s32[1]{0:T(128)} %bitcast.core_ref, f32[41024,128]{1,0:T(8,128)S(1)} %get-tuple-element.78.half, ...), custom_call_target="tpu_custom_call" | custom-call | flops 335544320 | bytes 4194304 | tf_op jit(solution)/shard_map/pallas_call | solution.py:193
  78.5 0.1 fusion.15
  78.6 0.1 collective-permute-done.12
  78.7 0.1 fusion.16
  78.8 1.6 %collective-permute-start.18 = (bf16[1280,128]{1,0:T(8,128)(2,1)S(1)}, bf16[1280,128]{1,0:T(8,128)(2,1)S(1)}, u32[]{:S(2)}, u32[]{:S(2)}) collective-permute-start(bf16[1280,128]{1,0:T(8,128)(2,1)S(1)} %fusion.15), channel_id=1, source_target_pairs={{0,2},{1,3},{2,0},{3,1},{4,6},{5,7},{6,4},{7,5},{8,10},{9,11},{10,... | collective-permute-start | bytes 983048 | tf_op jit(solution)/shard_map/ppermute | solution.py:34
  80.3 2.1 %shard_map.52 = (f32[1,1280,128]{2,1,0:T(8,128)S(1)}, f32[1,1280,128]{2,1,0:T(8,128)S(1)}, f32[1,1280,128]{2,1,0:T(8,128)S(1)}, f32[1,1280,128]{2,1,0:T(8,128)S(...) custom-call(s32[8]{0:T(128)S(1)} %fusion.34.chips_ref, ...), custom_call_target="tpu_custom_call" | custom-call | flops 335544320 | bytes 4194304 | tf_op jit(solution)/shard_map/pallas_call | solution.py:193
  82.4 0.1 collective-permute-start.22
  82.5 0.5 collective-permute-start.21
  83.0 0.1 fusion.8
  83.1 5.5 %collective-permute-done.18 = bf16[1280,128]{1,0:T(8,128)(2,1)S(1)} collective-permute-done((bf16[1280,128]{1,0:T(8,128)(2,1)S(1)}, bf16[1280,128]{1,0:T(8,128)(2,1)S(1)}, u32[]{:S(2)}, u32[]{:S(2)}) %collective-permute-start.18) | collective-permute-done | bytes 327712 | tf_op jit(solution)/shard_map/ppermute | solution.py:34
  88.6 0.5 collective-permute-start.14
  89.1 0.1 fusion.5
  89.2 0.1 collective-permute-start.23
  89.3 6.0 %collective-permute-done.16 = bf16[1280,128]{1,0:T(8,128)(2,1)S(1)} collective-permute-done((bf16[1280,128]{1,0:T(8,128)(2,1)S(1)}, bf16[1280,128]{1,0:T(8,128)(2,1)S(1)}, u32[]{:S(2)}, u32[]{:S(2)}) %collective-permute-start.16) | collective-permute-done | bytes 327712 | tf_op jit(solution)/shard_map/ppermute | solution.py:34
  95.2 0.1 fusion.10
  95.4 6.1 %collective-permute-done.23 = bf16[1280,128]{1,0:T(8,128)(2,1)S(1)} collective-permute-done((bf16[1280,128]{1,0:T(8,128)(2,1)S(1)}, bf16[1280,128]{1,0:T(8,128)(2,1)S(1)}, u32[]{:S(2)}, u32[]{:S(2)}) %collective-permute-start.23) | collective-permute-done | bytes 327712 | tf_op jit(solution)/shard_map/ppermute | solution.py:34
  101.5 0.1 fusion.7
  101.6 0.1 collective-permute-start.24
  101.7 1.6 %collective-permute-done.19 = bf16[1280,128]{1,0:T(8,128)(2,1)S(1)} collective-permute-done((bf16[1280,128]{1,0:T(8,128)(2,1)S(1)}, bf16[1280,128]{1,0:T(8,128)(2,1)S(1)}, u32[]{:S(2)}, u32[]{:S(2)}) %collective-permute-start.19) | collective-permute-done | bytes 327712 | tf_op jit(solution)/shard_map/ppermute | solution.py:34
  103.3 0.1 fusion.3
  103.5 2.2 %collective-permute-start.26 = (bf16[1280,128]{1,0:T(8,128)(2,1)S(1)}, bf16[1280,128]{1,0:T(8,128)(2,1)S(1)}, u32[]{:S(2)}, u32[]{:S(2)}) collective-permute-start(bf16[1280,128]{1,0:T(8,128)(2,1)S(1)} %fusion.3), channel_id=1, source_target_pairs={{0,12},{1,13},{2,14},{3,15},{4,0},{5,1},{6,2},{7,3},{8,4},{9,5},{1... | collective-permute-start | bytes 983048 | tf_op jit(solution)/shard_map/ppermute | solution.py:34
  105.7 0.7 collective-permute-start.20
  106.4 7.7 %collective-permute-done.24 = bf16[1280,128]{1,0:T(8,128)(2,1)S(1)} collective-permute-done((bf16[1280,128]{1,0:T(8,128)(2,1)S(1)}, bf16[1280,128]{1,0:T(8,128)(2,1)S(1)}, u32[]{:S(2)}, u32[]{:S(2)}) %collective-permute-start.24) | collective-permute-done | bytes 327712 | tf_op jit(solution)/shard_map/ppermute | solution.py:34
  114.1 3.8 %collective-permute-done.26 = bf16[1280,128]{1,0:T(8,128)(2,1)S(1)} collective-permute-done((bf16[1280,128]{1,0:T(8,128)(2,1)S(1)}, bf16[1280,128]{1,0:T(8,128)(2,1)S(1)}, u32[]{:S(2)}, u32[]{:S(2)}) %collective-permute-start.26) | collective-permute-done | bytes 327712 | tf_op jit(solution)/shard_map/ppermute | solution.py:34
  117.9 1.0 fusion.14
  (30 shorter events, 0.2 us)
Async XLA Ops:
  0.0 1.7 %copy-start.3 = (s32[256,2]{0,1:T(2,128)S(1)}, s32[256,2]{0,1:T(2,128)}, u32[]{:S(2)}) copy-start(s32[256,2]{0,1:T(2,128)} %param.5) | copy-start | bytes 6148
  0.0 12.8 %collective-permute-start.4 = (bf16[256,4096]{1,0:T(8,128)(2,1)}, bf16[256,4096]{1,0:T(8,128)(2,1)}, u32[]{:S(2)}, u32[]{:S(2)}) collective-permute-start(bf16[256,4096]{1,0:T(8,128)(2,1)} %param.4), channel_id=1, source_target_pairs={{0,1},{1,0},{2,3},{3,2},{4,5},{5,4},{6,7},{7,6},{8,9},{9,8},{10,11... | collective-permute-start | bytes 6291464 | tf_op jit(solution)/shard_map/ppermute | solution.py:34
  1.6 3.1 %collective-permute-start = (bf16[1280,128]{1,0:T(8,128)(2,1)S(1)}, bf16[1280,128]{1,0:T(8,128)(2,1)S(1)}, u32[]{:S(2)}, u32[]{:S(2)}) collective-permute-start(bf16[1280,128]{1,0:T(8,128)(2,1)S(1)} %get-tuple-element.105), channel_id=1, source_target_pairs={{0,1},{1,0},{2,3},{3,2},{4,5},{5,4},{6,7},{7,6},{8,9},{9,8},{10,11... | collective-permute-start | bytes 983048 | tf_op jit(solution)/shard_map/ppermute | solution.py:34
  1.7 9.6 %collective-permute-start.2 = (s32[256,2]{0,1:T(2,128)S(1)}, s32[256,2]{0,1:T(2,128)S(1)}, u32[]{:S(2)}, u32[]{:S(2)}) collective-permute-start(s32[256,2]{0,1:T(2,128)S(1)} %copy-done.3), channel_id=1, source_target_pairs={{0,1},{1,0},{2,3},{3,2},{4,5},{5,4},{6,7},{7,6},{8,9},{9,8},{10,11... | collective-permute-start | bytes 6152 | tf_op jit(solution)/shard_map/ppermute | solution.py:34
  2.2 9.2 %collective-permute-start.1 = (s32[1]{0:T(128)}, s32[1]{0:T(128)}, u32[]{:S(2)}, u32[]{:S(2)}) collective-permute-start(s32[1]{0:T(128)} %param.6), channel_id=1, source_target_pairs={{0,1},{1,0},{2,3},{3,2},{4,5},{5,4},{6,7},{7,6},{8,9},{9,8},{10,11... | collective-permute-start | bytes 20 | tf_op jit(solution)/shard_map/ppermute | solution.py:34
  4.8 20.1 %collective-permute-start.3 = (bf16[2560,128]{1,0:T(8,128)(2,1)S(1)}, bf16[2560,128]{1,0:T(8,128)(2,1)S(1)}, u32[]{:S(2)}, u32[]{:S(2)}) collective-permute-start(bf16[2560,128]{1,0:T(8,128)(2,1)S(1)} %pad_maximum_fusion.refs_0_), channel_id=1, source_target_pairs={{0,4},{1,5},{2,6},{3,7},{4,8},{5,9},{6,10},{7,11},{8,12},{9,13},{1... | collective-permute-start | bytes 1966088 | tf_op jit(solution)/shard_map/ppermute | solution.py:34
  7.8 17.1 %collective-permute-start.5 = (bf16[2560,128]{1,0:T(8,128)(2,1)S(1)}, bf16[2560,128]{1,0:T(8,128)(2,1)S(1)}, u32[]{:S(2)}, u32[]{:S(2)}) collective-permute-start(bf16[2560,128]{1,0:T(8,128)(2,1)S(1)} %pad_maximum_fusion.refs_0_), channel_id=1, source_target_pairs={{0,2},{1,3},{2,0},{3,1},{4,6},{5,7},{6,4},{7,5},{8,10},{9,11},{10,... | collective-permute-start | bytes 1966088 | tf_op jit(solution)/shard_map/ppermute | solution.py:34
  24.8 0.8 copy-start.1
  25.7 18.2 %collective-permute-start.6 = (bf16[2560,128]{1,0:T(8,128)(2,1)S(1)}, bf16[2560,128]{1,0:T(8,128)(2,1)}, u32[]{:S(2)}, u32[]{:S(2)}) collective-permute-start(bf16[2560,128]{1,0:T(8,128)(2,1)S(1)} %collective-permute-done.3.refs_0_), channel_id=1, source_target_pairs={{0,4},{1,5},{2,6},{3,7},{4,8},{5,9},{6,10},{7,11},{8,12},{9,13},{1... | collective-permute-start | bytes 1966088 | tf_op jit(solution)/shard_map/ppermute | solution.py:34
  26.7 17.2 %collective-permute-start.7 = (bf16[2560,128]{1,0:T(8,128)(2,1)S(1)}, bf16[2560,128]{1,0:T(8,128)(2,1)}, u32[]{:S(2)}, u32[]{:S(2)}) collective-permute-start(bf16[2560,128]{1,0:T(8,128)(2,1)S(1)} %collective-permute-done.3.refs_0_), channel_id=1, source_target_pairs={{0,2},{1,3},{2,0},{3,1},{4,6},{5,7},{6,4},{7,5},{8,10},{9,11},{10,... | collective-permute-start | bytes 1966088 | tf_op jit(solution)/shard_map/ppermute | solution.py:34
  29.2 1.6 %copy-start = (bf16[32,8,32,128]{3,2,1,0:T(8,128)(2,1)S(1)}, bf16[32,8,32,128]{3,2,1,0:T(8,128)(2,1)}, u32[]{:S(2)}) copy-start(bf16[32,8,32,128]{3,2,1,0:T(8,128)(2,1)} %copy.10) | copy-start | bytes 6291460
  30.8 14.4 %copy-start.2 = (bf16[2560,128]{1,0:T(8,128)(2,1)S(1)}, bf16[2560,128]{1,0:T(8,128)(2,1)}, u32[]{:S(2)}) copy-start(bf16[2560,128]{1,0:T(8,128)(2,1)} %copy-done.1) | copy-start | bytes 1966084
  43.8 17.4 %collective-permute-start.8 = (bf16[2560,128]{1,0:T(8,128)(2,1)}, bf16[2560,128]{1,0:T(8,128)(2,1)S(1)}, u32[]{:S(2)}, u32[]{:S(2)}) collective-permute-start(bf16[2560,128]{1,0:T(8,128)(2,1)} %collective-permute-done.6.refs_0_), channel_id=1, source_target_pairs={{0,4},{1,5},{2,6},{3,7},{4,8},{5,9},{6,10},{7,11},{8,12},{9,13},{1... | collective-permute-start | bytes 1966088 | tf_op jit(solution)/shard_map/ppermute | solution.py:34
  43.8 20.5 %collective-permute-start.9 = (bf16[2560,128]{1,0:T(8,128)(2,1)}, bf16[2560,128]{1,0:T(8,128)(2,1)S(1)}, u32[]{:S(2)}, u32[]{:S(2)}) collective-permute-start(bf16[2560,128]{1,0:T(8,128)(2,1)} %collective-permute-done.6.refs_0_), channel_id=1, source_target_pairs={{0,2},{1,3},{2,0},{3,1},{4,6},{5,7},{6,4},{7,5},{8,10},{9,11},{10,... | collective-permute-start | bytes 1966088 | tf_op jit(solution)/shard_map/ppermute | solution.py:34
  64.3 9.3 %collective-permute-start.10 = (bf16[1280,128]{1,0:T(8,128)(2,1)S(1)}, bf16[1280,128]{1,0:T(8,128)(2,1)S(1)}, u32[]{:S(2)}, u32[]{:S(2)}) collective-permute-start(bf16[1280,128]{1,0:T(8,128)(2,1)S(1)} %slice.14), channel_id=1, source_target_pairs={{0,4},{1,5},{2,6},{3,7},{4,8},{5,9},{6,10},{7,11},{8,12},{9,13},{1... | collective-permute-start | bytes 983048 | tf_op jit(solution)/shard_map/ppermute | solution.py:34
  64.4 9.2 %collective-permute-start.11 = (bf16[1280,128]{1,0:T(8,128)(2,1)S(1)}, bf16[1280,128]{1,0:T(8,128)(2,1)S(1)}, u32[]{:S(2)}, u32[]{:S(2)}) collective-permute-start(bf16[1280,128]{1,0:T(8,128)(2,1)S(1)} %slice.15), channel_id=1, source_target_pairs={{0,2},{1,3},{2,0},{3,1},{4,6},{5,7},{6,4},{7,5},{8,10},{9,11},{10,... | collective-permute-start | bytes 983048 | tf_op jit(solution)/shard_map/ppermute | solution.py:34
  76.0 2.5 %collective-permute-start.13 = (bf16[1280,128]{1,0:T(8,128)(2,1)S(1)}, bf16[1280,128]{1,0:T(8,128)(2,1)S(1)}, u32[]{:S(2)}, u32[]{:S(2)}) collective-permute-start(bf16[1280,128]{1,0:T(8,128)(2,1)S(1)} %bitcast.76), channel_id=1, source_target_pairs={{0,1},{1,0},{2,3},{3,2},{4,5},{5,4},{6,7},{7,6},{8,9},{9,8},{10,11... | collective-permute-start | bytes 983048 | tf_op jit(solution)/shard_map/ppermute | solution.py:34
  76.1 6.9 %collective-permute-start.17 = (bf16[1280,128]{1,0:T(8,128)(2,1)S(1)}, bf16[1280,128]{1,0:T(8,128)(2,1)S(1)}, u32[]{:S(2)}, u32[]{:S(2)}) collective-permute-start(bf16[1280,128]{1,0:T(8,128)(2,1)S(1)} %bitcast.73), channel_id=1, source_target_pairs={{0,1},{1,0},{2,3},{3,2},{4,5},{5,4},{6,7},{7,6},{8,9},{9,8},{10,11... | collective-permute-start | bytes 983048 | tf_op jit(solution)/shard_map/ppermute | solution.py:34
  76.6 2.1 %collective-permute-start.12 = (bf16[1280,128]{1,0:T(8,128)(2,1)S(1)}, bf16[1280,128]{1,0:T(8,128)(2,1)S(1)}, u32[]{:S(2)}, u32[]{:S(2)}) collective-permute-start(bf16[1280,128]{1,0:T(8,128)(2,1)S(1)} %bitcast.74), channel_id=1, source_target_pairs={{0,1},{1,0},{2,3},{3,2},{4,5},{5,4},{6,7},{7,6},{8,9},{9,8},{10,11... | collective-permute-start | bytes 983048 | tf_op jit(solution)/shard_map/ppermute | solution.py:34
  76.7 12.5 %collective-permute-start.15 = (bf16[1280,128]{1,0:T(8,128)(2,1)S(1)}, bf16[1280,128]{1,0:T(8,128)(2,1)S(1)}, u32[]{:S(2)}, u32[]{:S(2)}) collective-permute-start(bf16[1280,128]{1,0:T(8,128)(2,1)S(1)} %bitcast.70), channel_id=1, source_target_pairs={{0,1},{1,0},{2,3},{3,2},{4,5},{5,4},{6,7},{7,6},{8,9},{9,8},{10,11... | collective-permute-start | bytes 983048 | tf_op jit(solution)/shard_map/ppermute | solution.py:34
  78.8 9.8 %collective-permute-start.18 = (bf16[1280,128]{1,0:T(8,128)(2,1)S(1)}, bf16[1280,128]{1,0:T(8,128)(2,1)S(1)}, u32[]{:S(2)}, u32[]{:S(2)}) collective-permute-start(bf16[1280,128]{1,0:T(8,128)(2,1)S(1)} %fusion.15), channel_id=1, source_target_pairs={{0,2},{1,3},{2,0},{3,1},{4,6},{5,7},{6,4},{7,5},{8,10},{9,11},{10,... | collective-permute-start | bytes 983048 | tf_op jit(solution)/shard_map/ppermute | solution.py:34
  82.4 6.2 %collective-permute-start.22 = (bf16[1280,128]{1,0:T(8,128)(2,1)S(1)}, bf16[1280,128]{1,0:T(8,128)(2,1)S(1)}, u32[]{:S(2)}, u32[]{:S(2)}) collective-permute-start(bf16[1280,128]{1,0:T(8,128)(2,1)S(1)} %bitcast.75), channel_id=1, source_target_pairs={{0,1},{1,0},{2,3},{3,2},{4,5},{5,4},{6,7},{7,6},{8,9},{9,8},{10,11... | collective-permute-start | bytes 983048 | tf_op jit(solution)/shard_map/ppermute | solution.py:34
  82.5 12.9 %collective-permute-start.21 = (bf16[1280,128]{1,0:T(8,128)(2,1)S(1)}, bf16[1280,128]{1,0:T(8,128)(2,1)S(1)}, u32[]{:S(2)}, u32[]{:S(2)}) collective-permute-start(bf16[1280,128]{1,0:T(8,128)(2,1)S(1)} %bitcast.72), channel_id=1, source_target_pairs={{0,1},{1,0},{2,3},{3,2},{4,5},{5,4},{6,7},{7,6},{8,9},{9,8},{10,11... | collective-permute-start | bytes 983048 | tf_op jit(solution)/shard_map/ppermute | solution.py:34
  83.0 12.2 %collective-permute-start.16 = (bf16[1280,128]{1,0:T(8,128)(2,1)S(1)}, bf16[1280,128]{1,0:T(8,128)(2,1)S(1)}, u32[]{:S(2)}, u32[]{:S(2)}) collective-permute-start(bf16[1280,128]{1,0:T(8,128)(2,1)S(1)} %fusion.16), channel_id=1, source_target_pairs={{0,4},{1,5},{2,6},{3,7},{4,8},{5,9},{6,10},{7,11},{8,12},{9,13},{1... | collective-permute-start | bytes 983048 | tf_op jit(solution)/shard_map/ppermute | solution.py:34
  88.6 14.8 %collective-permute-start.25 = (bf16[1280,128]{1,0:T(8,128)(2,1)S(1)}, bf16[1280,128]{1,0:T(8,128)(2,1)S(1)}, u32[]{:S(2)}, u32[]{:S(2)}) collective-permute-start(bf16[1280,128]{1,0:T(8,128)(2,1)S(1)} %bitcast.71), channel_id=1, source_target_pairs={{0,1},{1,0},{2,3},{3,2},{4,5},{5,4},{6,7},{7,6},{8,9},{9,8},{10,11... | collective-permute-start | bytes 983048 | tf_op jit(solution)/shard_map/ppermute | solution.py:34
  88.6 17.9 %collective-permute-start.14 = (bf16[1280,128]{1,0:T(8,128)(2,1)S(1)}, bf16[1280,128]{1,0:T(8,128)(2,1)S(1)}, u32[]{:S(2)}, u32[]{:S(2)}) collective-permute-start(bf16[1280,128]{1,0:T(8,128)(2,1)S(1)} %bitcast.69), channel_id=1, source_target_pairs={{0,1},{1,0},{2,3},{3,2},{4,5},{5,4},{6,7},{7,6},{8,9},{9,8},{10,11... | collective-permute-start | bytes 983048 | tf_op jit(solution)/shard_map/ppermute | solution.py:34
  89.2 12.3 %collective-permute-start.23 = (bf16[1280,128]{1,0:T(8,128)(2,1)S(1)}, bf16[1280,128]{1,0:T(8,128)(2,1)S(1)}, u32[]{:S(2)}, u32[]{:S(2)}) collective-permute-start(bf16[1280,128]{1,0:T(8,128)(2,1)S(1)} %fusion.5), channel_id=1, source_target_pairs={{0,4},{1,5},{2,6},{3,7},{4,8},{5,9},{6,10},{7,11},{8,12},{9,13},{1... | collective-permute-start | bytes 983048 | tf_op jit(solution)/shard_map/ppermute | solution.py:34
  95.2 8.1 %collective-permute-start.19 = (bf16[1280,128]{1,0:T(8,128)(2,1)S(1)}, bf16[1280,128]{1,0:T(8,128)(2,1)S(1)}, u32[]{:S(2)}, u32[]{:S(2)}) collective-permute-start(bf16[1280,128]{1,0:T(8,128)(2,1)S(1)} %fusion.8), channel_id=1, source_target_pairs={{0,2},{1,3},{2,0},{3,1},{4,6},{5,7},{6,4},{7,5},{8,10},{9,11},{10,... | collective-permute-start | bytes 983048 | tf_op jit(solution)/shard_map/ppermute | solution.py:34
  101.6 12.5 %collective-permute-start.24 = (bf16[1280,128]{1,0:T(8,128)(2,1)S(1)}, bf16[1280,128]{1,0:T(8,128)(2,1)S(1)}, u32[]{:S(2)}, u32[]{:S(2)}) collective-permute-start(bf16[1280,128]{1,0:T(8,128)(2,1)S(1)} %fusion.7), channel_id=1, source_target_pairs={{0,4},{1,5},{2,6},{3,7},{4,8},{5,9},{6,10},{7,11},{8,12},{9,13},{1... | collective-permute-start | bytes 983048 | tf_op jit(solution)/shard_map/ppermute | solution.py:34
  103.5 14.4 %collective-permute-start.26 = (bf16[1280,128]{1,0:T(8,128)(2,1)S(1)}, bf16[1280,128]{1,0:T(8,128)(2,1)S(1)}, u32[]{:S(2)}, u32[]{:S(2)}) collective-permute-start(bf16[1280,128]{1,0:T(8,128)(2,1)S(1)} %fusion.3), channel_id=1, source_target_pairs={{0,12},{1,13},{2,14},{3,15},{4,0},{5,1},{6,2},{7,3},{8,4},{9,5},{1... | collective-permute-start | bytes 983048 | tf_op jit(solution)/shard_map/ppermute | solution.py:34
  105.7 12.2 %collective-permute-start.20 = (bf16[1280,128]{1,0:T(8,128)(2,1)S(1)}, bf16[1280,128]{1,0:T(8,128)(2,1)S(1)}, u32[]{:S(2)}, u32[]{:S(2)}) collective-permute-start(bf16[1280,128]{1,0:T(8,128)(2,1)S(1)} %fusion.10), channel_id=1, source_target_pairs={{0,2},{1,3},{2,0},{3,1},{4,6},{5,7},{6,4},{7,5},{8,10},{9,11},{10,... | collective-permute-start | bytes 983048 | tf_op jit(solution)/shard_map/ppermute | solution.py:34

commit v11 on v9

--- a/solution.py
+++ b/solution.py
@@ -11,7 +11,7 @@
 BLK = 64
 WIN = 128
 LANES = 128
-UNROLL = 8
+UNROLL = 16
 LINE = 4
 SCOPED_BYTES = 6 * 1024 * 1024
 
@@ -76,7 +76,8 @@
     near = {step: paired(near_keep[step], near_send[step]) for step in (2, 1, 3, 0)}
     crossing, crossed[2] = tie(far[3].astype(jnp.bfloat16), crossed[2])
     crossed[3] = move(crossing, ACROSS)
-    crossed[0] = move((far[0] + joining.astype(jnp.float32)).astype(jnp.bfloat16), ACROSS)
+    crossing, crossed[3] = tie((far[0] + joining.astype(jnp.float32)).astype(jnp.bfloat16), crossed[3])
+    crossed[0] = move(crossing, ACROSS)
 
     two_on = move((near[2] + crossed[2].astype(jnp.float32)).astype(jnp.bfloat16), ALONG)
     one_on = move((near[1] + two_on.astype(jnp.float32)).astype(jnp.bfloat16), ALONG)
@@ -100,8 +101,10 @@
         pltpu.make_async_copy(source, occ.at[pl.ds(index * rows, rows)], sem).start()
     pltpu.make_async_copy(occ, occ, sem).wait()
     begin, end = bounds_ref[stage], bounds_ref[stage + 1]
+    low = lax.broadcasted_iota(jnp.int32, tiles.shape[1:], 1) < BLK
+    zero = jnp.zeros(tiles.shape[1:], jnp.bfloat16)
     spill = half.shape[0] - BLK
-    columns = 2 + pieces
+    entries = table_ref.shape[0] // (2 + pieces)
     piece = BLK // pieces
 
     @pl.loop(0, (end - begin + UNROLL - 1) // UNROLL)
@@ -109,13 +112,13 @@
         products, starts = [], []
         for lane in range(UNROLL):
             entry = begin + group * UNROLL + lane
-            tile = table_ref[entry * columns]
-            starts.append(jnp.where(entry < end, table_ref[entry * columns + 1], spill))
-            spots = [jnp.where(entry < end, table_ref[entry * columns + 2 + cut], 0) for cut in range(pieces)]
+            tile = table_ref[entry]
+            starts.append(jnp.where(entry < end, table_ref[entries + entry], spill))
+            spots = [jnp.where(entry < end, table_ref[(2 + cut) * entries + entry], 0) for cut in range(pieces)]
             parts = [occ[pl.ds(pl.multiple_of(spot, piece), piece), :] for spot in spots]
             pair = tiles[tile]
-            left = jnp.concatenate([pair[:, :BLK], pair[:, BLK:]], axis=0)
-            block = parts[0] if pieces == 1 else jnp.concatenate(parts, axis=0)
+            left = jnp.concatenate([jnp.where(low, pair, zero), jnp.where(low, zero, pair)], axis=0)
+            block = jnp.concatenate(parts * 2, axis=0)
             products.append(jnp.dot(left, block, preferred_element_type=jnp.float32))
         for product, start in zip(products, starts):
             start = pl.multiple_of(start, BLK)
@@ -220,10 +223,10 @@
 
     mine = lax.dynamic_slice_in_dim(occupied, core * LANES, LANES, 1)
     given = lax.dynamic_slice_in_dim(occupied, (1 - core) * LANES, LANES, 1)
-    parts = (mine, move(given, swap))
-    tile_sets = [
-        values.reshape(slots, BLK * BLK // LANES, LANES) for values in (block_values, move(block_values, swap))
-    ]
+    parts = [mine, move(given, swap)]
+    others = [move(array, swap) for array in (block_values, block_pairs, live_counts)]
+    *parts, block_values, block_pairs, live_counts = tie(*parts, block_values, block_pairs, live_counts)
+    tile_sets = [values.reshape(slots, BLK * BLK // LANES, LANES) for values in (block_values, others[0])]
 
     slot_ids = jnp.arange(chips, dtype=jnp.int32)
     chip_of_slot = slot_ids
@@ -233,10 +236,9 @@
         stage_count = LINE + 1
 
     tile_ids = jnp.arange(2 * slots, dtype=jnp.int32)
-    row_starts = jnp.where(tile_ids[:slots] < live_counts[0], block_pairs[:, 0] * BLK, -1)
-    table = jnp.stack([row_starts, block_pairs[:, 1]])
-    both = jnp.concatenate([table, move(table, swap)], axis=1)
-    first = both[1][:, None] * BLK + jnp.arange(pieces, dtype=jnp.int32) * piece
+    pairs = jnp.concatenate([block_pairs, others[1]])
+    live = tile_ids % slots < jnp.where(tile_ids < slots, live_counts[0], others[2][0])
+    first = pairs[:, 1][:, None] * BLK + jnp.arange(pieces, dtype=jnp.int32) * piece
     owner = first // shard
     part = (owner % 2) ^ core
     owner_chip = owner // 2
@@ -249,8 +251,8 @@
         stage = jnp.zeros_like(tile_ids)
         slot_of = part * chips + owner_chip
     spots = slot_of * shard + first % shard
-    stage = jnp.where(both[0] >= 0, stage, stage_count)
-    rows = both[0] + tile_ids // slots * total
+    stage = jnp.where(live, stage, stage_count)
+    rows = pairs[:, 0] * BLK + tile_ids // slots * total
     ahead = (stage[None, :] < stage[:, None]) | (
         (stage[None, :] == stage[:, None]) & (tile_ids[None, :] < tile_ids[:, None])
     )
@@ -258,9 +260,7 @@
     entries = jnp.arange(2 * slots + UNROLL, dtype=jnp.int32)
     chosen = rank[None, :] == entries[:, None]
     columns = [tile_ids, rows] + [spots[:, cut] for cut in range(pieces)]
-    ordered = jnp.stack(
-        [jnp.sum(jnp.where(chosen, column[None, :], 0), axis=1) for column in columns], axis=1
-    ).reshape(-1)
+    ordered = jnp.concatenate([jnp.sum(jnp.where(chosen, column[None, :], 0), axis=1) for column in columns])
     bounds = jnp.sum((stage[None, :] < jnp.arange(stage_count + 1)[:, None]).astype(jnp.int32), axis=1)
     cores = core.astype(jnp.int32).reshape(1)
 

time: 110 us -> 113 us (1.027)
  waiting for transfers between devices: 37.1 us -> 53.5 us
  starting transfers between devices: 30.6 us -> 22.9 us
  Pallas kernels: 24.9 us -> 20.9 us
  local copies, waits for them, and re-layouts: 11.7 us -> 9.67 us
    ppermute x32 -> x33, waiting for transfers between devices: 37.1 us -> 53.5 us  [move(): return lax.ppermute(array, 'aux', pairs)]
    ppermute x32 -> x33, starting transfers between devices: 30.6 us -> 22.9 us  [move(): return lax.ppermute(array, 'aux', pairs)]
    pallas_call x7, Pallas kernels: 24.9 us -> 20.9 us  [call(): pl.pallas_call(kernel, out_shape=outs, in_specs=in_specs, out_specs=[VMEM...]
    select_n x4 -> x2, other arithmetic: 0.07 us -> 1.44 us  [local(): stage = jnp.where(live, stage, stage_count)]
    reshape x1 -> x0, local copies, waits for them, and re-layouts: 1.15 us -> none  [local(): ordered = jnp.stack([jnp.sum(jnp.where(chosen, column[None, :], 0), axis=...]
    unnamed x12 -> x13, local copies, waits for them, and re-layouts: 8.51 us -> 8.47 us
  transfers between devices with their start and end apart: 32 -> 33, of which waited for: 9 -> 13; matrix products, arithmetic and copies ran while one was open for 10% -> 9% of each run, Pallas kernels for 20% -> 16%
where the time goes in v11:
time: 113 us; the launch traced here: 112 us
  waiting for transfers between devices  53.5 us (47%)
  starting transfers between devices  22.9 us (20%)
  Pallas kernels  20.9 us (18%)
  local copies, waits for them, and re-layouts  9.67 us (9%)
  other arithmetic  4.23 us (4%)
    ppermute x33, waiting for transfers between devices, move(): return lax.ppermute(array, 'aux', pairs)  53.5 us
    ppermute x33, starting transfers between devices, move(): return lax.ppermute(array, 'aux', pairs)  22.9 us
    pallas_call x7, Pallas kernels, call(): pl.pallas_call(kernel, out_shape=outs, in_specs=in_specs, out_specs=[VMEM...  20.9 us
    unnamed x13, local copies, waits for them, and re-layouts  8.47 us
  transfers between devices with their start and end apart: 33, of which 13 were waited for; matrix products, arithmetic and copies ran while one was open for 9% of the time, Pallas kernels for 16%

profile of v11, /device:TPU:0, one launch (start us, length us, event | category | flops | bytes accessed | tf_op | source)
XLA Modules:
  0.0 112.1 jit_solution(13831009359621010639)
XLA Ops:
  0.0 0.5 collective-permute-start.11
  0.5 1.1 constant_dynamic-slice_fusion
  1.6 0.1 collective-permute-start
  1.7 0.5 collective-permute-start.2
  2.1 0.1 collective-permute-start.1
  2.9 2.0 %collective-permute-done.refs_1_ = bf16[1280,128]{1,0:T(8,128)(2,1)} collective-permute-done((bf16[1280,128]{1,0:T(8,128)(2,1)S(1)}, bf16[1280,128]{1,0:T(8,128)(2,1)}, u32[]{:S(2)}, u32[]{:S(2)}) %collective-permute-start) | collective-permute-done | bytes 327712 | tf_op jit(solution)/shard_map/ppermute | solution.py:34
  4.8 2.9 %collective-permute-start.10 = (bf16[1280,128]{1,0:T(8,128)(2,1)}, bf16[1280,128]{1,0:T(8,128)(2,1)S(1)}, u32[]{:S(2)}, u32[]{:S(2)}) collective-permute-start(bf16[1280,128]{1,0:T(8,128)(2,1)} %collective-permute-done.refs_1_), channel_id=1, source_target_pairs={{0,2},{1,3},{2,0},{3,1},{4,6},{5,7},{6,4},{7,5},{8,10},{9,11},{10,... | collective-permute-start | bytes 983048 | tf_op jit(solution)/shard_map/ppermute | solution.py:34
  7.7 1.6 %collective-permute-start.9 = (bf16[1280,128]{1,0:T(8,128)(2,1)}, bf16[1280,128]{1,0:T(8,128)(2,1)S(1)}, u32[]{:S(2)}, u32[]{:S(2)}) collective-permute-start(bf16[1280,128]{1,0:T(8,128)(2,1)} %collective-permute-done.refs_1_), channel_id=1, source_target_pairs={{0,4},{1,5},{2,6},{3,7},{4,8},{5,9},{6,10},{7,11},{8,12},{9,13},{1... | collective-permute-start | bytes 983048 | tf_op jit(solution)/shard_map/ppermute | solution.py:34
  9.3 0.7 constant_dynamic-update-slice_fusion.1
  10.0 1.6 %collective-permute-start.3 = (bf16[1280,128]{1,0:T(8,128)(2,1)S(1)}, bf16[1280,128]{1,0:T(8,128)(2,1)S(1)}, u32[]{:S(2)}, u32[]{:S(2)}) collective-permute-start(bf16[1280,128]{1,0:T(8,128)(2,1)S(1)} %get-tuple-element.60.refs_0_), channel_id=1, source_target_pairs={{0,4},{1,5},{2,6},{3,7},{4,8},{5,9},{6,10},{7,11},{8,12},{9,13},{1... | collective-permute-start | bytes 983048 | tf_op jit(solution)/shard_map/ppermute | solution.py:34
  11.6 0.5 collective-permute-start.4
  12.1 0.7 compare_select_fusion.3
  12.9 2.1 %copy.9 = bf16[32,8,32,128]{3,2,1,0:T(8,128)(2,1)S(1)} copy(bf16[32,8,32,128]{3,1,2,0:T(8,128)(2,1)} %bitcast.77) | data formatting | bytes 4194304
  15.0 0.7 fusion.31
  15.7 10.6 %collective-permute-done.3.refs_0_ = bf16[1280,128]{1,0:T(8,128)(2,1)S(1)} collective-permute-done((bf16[1280,128]{1,0:T(8,128)(2,1)S(1)}, bf16[1280,128]{1,0:T(8,128)(2,1)S(1)}, u32[]{:S(2)}, u32[]{:S(2)}) %collective-permute-start.3) | collective-permute-done | bytes 327712 | tf_op jit(solution)/shard_map/ppermute | solution.py:34
  26.3 0.6 collective-permute-start.6
  26.9 3.4 %copy.10 = bf16[32,8,32,128]{3,2,1,0:T(8,128)(2,1)} copy(bf16[32,8,32,128]{3,1,2,0:T(8,128)(2,1)} %bitcast.25) | data formatting | bytes 4194304
  30.3 1.2 %collective-permute-start.12 = (bf16[1280,128]{1,0:T(8,128)(2,1)S(1)}, bf16[1280,128]{1,0:T(8,128)(2,1)}, u32[]{:S(2)}, u32[]{:S(2)}) collective-permute-start(bf16[1280,128]{1,0:T(8,128)(2,1)S(1)} %collective-permute-done.9.refs_1_), channel_id=1, source_target_pairs={{0,4},{1,5},{2,6},{3,7},{4,8},{5,9},{6,10},{7,11},{8,12},{9,13},{1... | collective-permute-start | bytes 983048 | tf_op jit(solution)/shard_map/ppermute | solution.py:34
  31.5 1.5 %collective-permute-start.13 = (bf16[1280,128]{1,0:T(8,128)(2,1)S(1)}, bf16[1280,128]{1,0:T(8,128)(2,1)}, u32[]{:S(2)}, u32[]{:S(2)}) collective-permute-start(bf16[1280,128]{1,0:T(8,128)(2,1)S(1)} %collective-permute-done.9.refs_1_), channel_id=1, source_target_pairs={{0,2},{1,3},{2,0},{3,1},{4,6},{5,7},{6,4},{7,5},{8,10},{9,11},{10,... | collective-permute-start | bytes 983048 | tf_op jit(solution)/shard_map/ppermute | solution.py:34
  33.0 0.3 convert_reduce_fusion
  33.3 0.5 select_reduce_fusion
  33.9 5.0 %collective-permute-done.5.refs_0_ = bf16[1280,128]{1,0:T(8,128)(2,1)} collective-permute-done((bf16[1280,128]{1,0:T(8,128)(2,1)S(1)}, bf16[1280,128]{1,0:T(8,128)(2,1)}, u32[]{:S(2)}, u32[]{:S(2)}) %collective-permute-start.5) | collective-permute-done | bytes 327712 | tf_op jit(solution)/shard_map/ppermute | solution.py:34
  38.9 0.7 copy-done.3
  39.6 0.5 collective-permute-start.8
  40.1 0.1 convert_reduce_fusion.1.bounds_ref
  40.2 0.1 concatenate.7.table_ref
  40.3 1.6 %copy-done = bf16[32,8,32,128]{3,2,1,0:T(8,128)(2,1)S(1)} copy-done((bf16[32,8,32,128]{3,2,1,0:T(8,128)(2,1)S(1)}, bf16[32,8,32,128]{3,2,1,0:T(8,128)(2,1)}, u32[]{:S(2)}) %copy-start) | copy-done | bytes 2097176
  41.9 4.7 %shard_map.46 = (f32[41024,128]{1,0:T(8,128)S(1)}, bf16[512,32,128]{2,1,0:T(8,128)(2,1)S(1)}) custom-call(s32[1584]{0:T(1024)S(1)} %concatenate.7.table_ref, s32[6]{0:T(128)S(1)} %convert_reduce_fusion.1.bounds_ref, bf16[1280,128]{1,0:T(8,128)(2,1)S(1)} %get-tuple-element.60.refs_0_, bf16[1280,128]{1,0:T(8,128)(2,1)} %collective-permute-done.refs_1_, ...), custom_call_target="tpu_custom_call" | custom-call | flops 107374184 | bytes 4194304 | tf_op jit(solution)/shard_map/pallas_call | solution.py:198
  46.7 1.2 %collective-permute-start.16 = (bf16[1280,128]{1,0:T(8,128)(2,1)}, bf16[1280,128]{1,0:T(8,128)(2,1)S(1)}, u32[]{:S(2)}, u32[]{:S(2)}) collective-permute-start(bf16[1280,128]{1,0:T(8,128)(2,1)} %collective-permute-done.12.refs_1_), channel_id=1, source_target_pairs={{0,2},{1,3},{2,0},{3,1},{4,6},{5,7},{6,4},{7,5},{8,10},{9,11},{10,... | collective-permute-start | bytes 983048 | tf_op jit(solution)/shard_map/ppermute | solution.py:34
  47.9 5.0 %collective-permute-done.7.refs_0_ = bf16[1280,128]{1,0:T(8,128)(2,1)} collective-permute-done((bf16[1280,128]{1,0:T(8,128)(2,1)}, bf16[1280,128]{1,0:T(8,128)(2,1)}, u32[]{:S(2)}, u32[]{:S(2)}) %collective-permute-start.7) | collective-permute-done | bytes 327712 | tf_op jit(solution)/shard_map/ppermute | solution.py:34
  52.9 2.5 %shard_map.47.refs_5_ = f32[41024,128]{1,0:T(8,128)S(1)} custom-call(s32[1584]{0:T(1024)S(1)} %concatenate.7.table_ref, s32[6]{0:T(128)S(1)} %convert_reduce_fusion.1.bounds_ref, bf16[1280,128]{1,0:T(8,128)(2,1)S(1)} %collective-permute-done.3.refs_0_, bf16[1280,128]{1,0:T(8,128)(2,1)S(1)} %collective-permute-done.9.refs_1_, ...), custom_call_target="tpu_custom_call", output_to_operand_aliasing={{}: (7, {})} | custom-call | flops 107374184 | bytes 4194304 | tf_op jit(solution)/shard_map/pallas_call | solution.py:198
  55.5 3.8 %shard_map.48.refs_5_ = f32[41024,128]{1,0:T(8,128)S(1)} custom-call(s32[1584]{0:T(1024)S(1)} %concatenate.7.table_ref, s32[6]{0:T(128)S(1)} %convert_reduce_fusion.1.bounds_ref, bf16[1280,128]{1,0:T(8,128)(2,1)} %collective-permute-done.5.refs_0_, bf16[1280,128]{1,0:T(8,128)(2,1)} %collective-permute-done.12.refs_1_, ...), custom_call_target="tpu_custom_call", output_to_operand_aliasing={{}: (7, {})} | custom-call | flops 107374184 | bytes 4194304 | tf_op jit(solution)/shard_map/pallas_call | solution.py:198
  59.4 1.2 %collective-permute-start.17 = (bf16[1280,128]{1,0:T(8,128)(2,1)S(1)}, bf16[1280,128]{1,0:T(8,128)(2,1)S(1)}, u32[]{:S(2)}, u32[]{:S(2)}) collective-permute-start(bf16[1280,128]{1,0:T(8,128)(2,1)S(1)} %collective-permute-done.15.refs_1_), channel_id=1, source_target_pairs={{0,2},{1,3},{2,0},{3,1},{4,6},{5,7},{6,4},{7,5},{8,10},{9,11},{10,... | collective-permute-start | bytes 983048 | tf_op jit(solution)/shard_map/ppermute | solution.py:34
  60.6 3.7 %shard_map.49.refs_3_ = f32[41024,128]{1,0:T(8,128)S(1)} custom-call(s32[1584]{0:T(1024)S(1)} %concatenate.7.table_ref, s32[6]{0:T(128)S(1)} %convert_reduce_fusion.1.bounds_ref, bf16[1280,128]{1,0:T(8,128)(2,1)} %collective-permute-done.7.refs_0_, bf16[1280,128]{1,0:T(8,128)(2,1)S(1)} %collective-permute-done.15.refs_1_, ...), custom_call_target="tpu_custom_call", output_to_operand_aliasing={{}: (7, {})} | custom-call | flops 107374184 | bytes 4194304 | tf_op jit(solution)/shard_map/pallas_call | solution.py:198
  64.3 0.6 collective-permute-done.14.refs_0_
  64.9 1.6 %collective-permute-done.17.refs_1_ = bf16[1280,128]{1,0:T(8,128)(2,1)S(1)} collective-permute-done((bf16[1280,128]{1,0:T(8,128)(2,1)S(1)}, bf16[1280,128]{1,0:T(8,128)(2,1)S(1)}, u32[]{:S(2)}, u32[]{:S(2)}) %collective-permute-start.17) | collective-permute-done | bytes 327712 | tf_op jit(solution)/shard_map/ppermute | solution.py:34
  66.5 2.7 %shard_map.50 = (f32[41024,128]{1,0:T(8,128)S(1)}, bf16[256,128]{1,0:T(8,128)(2,1)S(1)}, bf16[1,1280,128]{2,1,0:T(8,128)(2,1)S(1)}, bf16[1,1280,128]{2,1,0:T(8,1...) custom-call(s32[1584]{0:T(1024)S(1)} %concatenate.7.table_ref, ...), custom_call_target="tpu_custom_call", output_to_operand_aliasing={{0}: (7, {})} | custom-call | flops 442918496 | bytes 4194304 | tf_op jit(solution)/shard_map/pallas_call | solution.py:198
  69.2 0.1 collective-permute-start.19
  69.3 0.5 collective-permute-start.23
  69.8 0.1 collective-permute-start.18
  69.9 0.4 collective-permute-start.21
  70.3 1.4 %shard_map.51 = (f32[1,1280,128]{2,1,0:T(8,128)S(1)}, f32[1,1280,128]{2,1,0:T(8,128)S(1)}, f32[1,1280,128]{2,1,0:T(8,128)S(1)}, f32[1,1280,128]{2,1,0:T(8,128)S(1)}) custom-call(s32[8]{0:T(128)S(1)} %fusion.34.chips_ref, s32[1]{0:T(128)} %bitcast.core_ref, f32[41024,128]{1,0:T(8,128)S(1)} %get-tuple-element.92.half, ...), custom_call_target="tpu_custom_call" | custom-call | flops 335544320 | bytes 4194304 | tf_op jit(solution)/shard_map/pallas_call | solution.py:198
  71.7 0.1 fusion.15
  71.8 0.1 collective-permute-done.18
  71.9 0.1 fusion.16
  71.9 0.9 collective-permute-start.24
  72.8 2.1 %shard_map.52 = (f32[1,1280,128]{2,1,0:T(8,128)S(1)}, f32[1,1280,128]{2,1,0:T(8,128)S(1)}, f32[1,1280,128]{2,1,0:T(8,128)S(1)}, f32[1,1280,128]{2,1,0:T(8,128)S(...) custom-call(s32[8]{0:T(128)S(1)} %fusion.34.chips_ref, ...), custom_call_target="tpu_custom_call" | custom-call | flops 335544320 | bytes 4194304 | tf_op jit(solution)/shard_map/pallas_call | solution.py:198
  74.9 0.1 collective-permute-start.28
  75.0 0.5 collective-permute-start.27
  75.6 6.2 %collective-permute-done.24 = bf16[1280,128]{1,0:T(8,128)(2,1)S(1)} collective-permute-done((bf16[1280,128]{1,0:T(8,128)(2,1)S(1)}, bf16[1280,128]{1,0:T(8,128)(2,1)S(1)}, u32[]{:S(2)}, u32[]{:S(2)}) %collective-permute-start.24) | collective-permute-done | bytes 327712 | tf_op jit(solution)/shard_map/ppermute | solution.py:34
  81.8 0.5 collective-permute-start.20
  82.3 0.1 fusion.5
  82.5 4.5 %collective-permute-done.22 = bf16[1280,128]{1,0:T(8,128)(2,1)S(1)} collective-permute-done((bf16[1280,128]{1,0:T(8,128)(2,1)S(1)}, bf16[1280,128]{1,0:T(8,128)(2,1)S(1)}, u32[]{:S(2)}, u32[]{:S(2)}) %collective-permute-start.22) | collective-permute-done | bytes 327712 | tf_op jit(solution)/shard_map/ppermute | solution.py:34
  87.0 2.0 %collective-permute-start.25 = (bf16[1280,128]{1,0:T(8,128)(2,1)S(1)}, bf16[1280,128]{1,0:T(8,128)(2,1)S(1)}, u32[]{:S(2)}, u32[]{:S(2)}) collective-permute-start(bf16[1280,128]{1,0:T(8,128)(2,1)S(1)} %fusion.8), channel_id=1, source_target_pairs={{0,2},{1,3},{2,0},{3,1},{4,6},{5,7},{6,4},{7,5},{8,10},{9,11},{10,... | collective-permute-start | bytes 983048 | tf_op jit(solution)/shard_map/ppermute | solution.py:34
  89.0 0.1 fusion.10
  89.1 5.0 %collective-permute-done.29 = bf16[1280,128]{1,0:T(8,128)(2,1)S(1)} collective-permute-done((bf16[1280,128]{1,0:T(8,128)(2,1)S(1)}, bf16[1280,128]{1,0:T(8,128)(2,1)S(1)}, u32[]{:S(2)}, u32[]{:S(2)}) %collective-permute-start.29) | collective-permute-done | bytes 327712 | tf_op jit(solution)/shard_map/ppermute | solution.py:34
  94.2 0.1 fusion.7
  94.4 1.5 %collective-permute-done.25 = bf16[1280,128]{1,0:T(8,128)(2,1)S(1)} collective-permute-done((bf16[1280,128]{1,0:T(8,128)(2,1)S(1)}, bf16[1280,128]{1,0:T(8,128)(2,1)S(1)}, u32[]{:S(2)}, u32[]{:S(2)}) %collective-permute-start.25) | collective-permute-done | bytes 327712 | tf_op jit(solution)/shard_map/ppermute | solution.py:34
  95.9 0.1 fusion.3
  96.0 2.4 %collective-permute-start.32 = (bf16[1280,128]{1,0:T(8,128)(2,1)S(1)}, bf16[1280,128]{1,0:T(8,128)(2,1)S(1)}, u32[]{:S(2)}, u32[]{:S(2)}) collective-permute-start(bf16[1280,128]{1,0:T(8,128)(2,1)S(1)} %fusion.3), channel_id=1, source_target_pairs={{0,12},{1,13},{2,14},{3,15},{4,0},{5,1},{6,2},{7,3},{8,4},{9,5},{1... | collective-permute-start | bytes 983048 | tf_op jit(solution)/shard_map/ppermute | solution.py:34
  98.4 1.3 %collective-permute-start.26 = (bf16[1280,128]{1,0:T(8,128)(2,1)S(1)}, bf16[1280,128]{1,0:T(8,128)(2,1)S(1)}, u32[]{:S(2)}, u32[]{:S(2)}) collective-permute-start(bf16[1280,128]{1,0:T(8,128)(2,1)S(1)} %fusion.10), channel_id=1, source_target_pairs={{0,2},{1,3},{2,0},{3,1},{4,6},{5,7},{6,4},{7,5},{8,10},{9,11},{10,... | collective-permute-start | bytes 983048 | tf_op jit(solution)/shard_map/ppermute | solution.py:34
  99.7 7.1 %collective-permute-done.30 = bf16[1280,128]{1,0:T(8,128)(2,1)S(1)} collective-permute-done((bf16[1280,128]{1,0:T(8,128)(2,1)S(1)}, bf16[1280,128]{1,0:T(8,128)(2,1)S(1)}, u32[]{:S(2)}, u32[]{:S(2)}) %collective-permute-start.30) | collective-permute-done | bytes 327712 | tf_op jit(solution)/shard_map/ppermute | solution.py:34
  106.8 4.2 %collective-permute-done.32 = bf16[1280,128]{1,0:T(8,128)(2,1)S(1)} collective-permute-done((bf16[1280,128]{1,0:T(8,128)(2,1)S(1)}, bf16[1280,128]{1,0:T(8,128)(2,1)S(1)}, u32[]{:S(2)}, u32[]{:S(2)}) %collective-permute-start.32) | collective-permute-done | bytes 327712 | tf_op jit(solution)/shard_map/ppermute | solution.py:34
  111.0 1.0 fusion.14
  (41 shorter events, 0.5 us)
Async XLA Ops:
  0.0 26.9 %collective-permute-start.11 = (bf16[256,4096]{1,0:T(8,128)(2,1)}, bf16[256,4096]{1,0:T(8,128)(2,1)}, u32[]{:S(2)}, u32[]{:S(2)}) collective-permute-start(bf16[256,4096]{1,0:T(8,128)(2,1)} %param.4), channel_id=1, source_target_pairs={{0,1},{1,0},{2,3},{3,2},{4,5},{5,4},{6,7},{7,6},{8,9},{9,8},{10,11... | collective-permute-start | bytes 6291464 | tf_op jit(solution)/shard_map/ppermute | solution.py:34
  1.6 3.3 %collective-permute-start = (bf16[1280,128]{1,0:T(8,128)(2,1)S(1)}, bf16[1280,128]{1,0:T(8,128)(2,1)}, u32[]{:S(2)}, u32[]{:S(2)}) collective-permute-start(bf16[1280,128]{1,0:T(8,128)(2,1)S(1)} %get-tuple-element.118), channel_id=1, source_target_pairs={{0,1},{1,0},{2,3},{3,2},{4,5},{5,4},{6,7},{7,6},{8,9},{9,8},{10,11... | collective-permute-start | bytes 983048 | tf_op jit(solution)/shard_map/ppermute | solution.py:34
  1.7 8.3 %collective-permute-start.2 = (s32[256,2]{0,1:T(2,128)}, s32[256,2]{0,1:T(2,128)S(1)}, u32[]{:S(2)}, u32[]{:S(2)}) collective-permute-start(s32[256,2]{0,1:T(2,128)} %param.5), channel_id=1, source_target_pairs={{0,1},{1,0},{2,3},{3,2},{4,5},{5,4},{6,7},{7,6},{8,9},{9,8},{10,11... | collective-permute-start | bytes 6152 | tf_op jit(solution)/shard_map/ppermute | solution.py:34
  2.1 9.4 %collective-permute-start.1 = (s32[1]{0:T(128)}, s32[1]{0:T(128)}, u32[]{:S(2)}, u32[]{:S(2)}) collective-permute-start(s32[1]{0:T(128)} %param.6), channel_id=1, source_target_pairs={{0,1},{1,0},{2,3},{3,2},{4,5},{5,4},{6,7},{7,6},{8,9},{9,8},{10,11... | collective-permute-start | bytes 20 | tf_op jit(solution)/shard_map/ppermute | solution.py:34
  4.8 22.1 %collective-permute-start.10 = (bf16[1280,128]{1,0:T(8,128)(2,1)}, bf16[1280,128]{1,0:T(8,128)(2,1)S(1)}, u32[]{:S(2)}, u32[]{:S(2)}) collective-permute-start(bf16[1280,128]{1,0:T(8,128)(2,1)} %collective-permute-done.refs_1_), channel_id=1, source_target_pairs={{0,2},{1,3},{2,0},{3,1},{4,6},{5,7},{6,4},{7,5},{8,10},{9,11},{10,... | collective-permute-start | bytes 983048 | tf_op jit(solution)/shard_map/ppermute | solution.py:34
  7.7 19.2 %collective-permute-start.9 = (bf16[1280,128]{1,0:T(8,128)(2,1)}, bf16[1280,128]{1,0:T(8,128)(2,1)S(1)}, u32[]{:S(2)}, u32[]{:S(2)}) collective-permute-start(bf16[1280,128]{1,0:T(8,128)(2,1)} %collective-permute-done.refs_1_), channel_id=1, source_target_pairs={{0,4},{1,5},{2,6},{3,7},{4,8},{5,9},{6,10},{7,11},{8,12},{9,13},{1... | collective-permute-start | bytes 983048 | tf_op jit(solution)/shard_map/ppermute | solution.py:34
  10.0 16.3 %collective-permute-start.3 = (bf16[1280,128]{1,0:T(8,128)(2,1)S(1)}, bf16[1280,128]{1,0:T(8,128)(2,1)S(1)}, u32[]{:S(2)}, u32[]{:S(2)}) collective-permute-start(bf16[1280,128]{1,0:T(8,128)(2,1)S(1)} %get-tuple-element.60.refs_0_), channel_id=1, source_target_pairs={{0,4},{1,5},{2,6},{3,7},{4,8},{5,9},{6,10},{7,11},{8,12},{9,13},{1... | collective-permute-start | bytes 983048 | tf_op jit(solution)/shard_map/ppermute | solution.py:34
  11.6 14.7 %collective-permute-start.4 = (bf16[1280,128]{1,0:T(8,128)(2,1)S(1)}, bf16[1280,128]{1,0:T(8,128)(2,1)S(1)}, u32[]{:S(2)}, u32[]{:S(2)}) collective-permute-start(bf16[1280,128]{1,0:T(8,128)(2,1)S(1)} %get-tuple-element.60.refs_0_), channel_id=1, source_target_pairs={{0,2},{1,3},{2,0},{3,1},{4,6},{5,7},{6,4},{7,5},{8,10},{9,11},{10,... | collective-permute-start | bytes 983048 | tf_op jit(solution)/shard_map/ppermute | solution.py:34
  26.3 4.0 %copy-start.1 = (bf16[1280,128]{1,0:T(8,128)(2,1)}, bf16[1280,128]{1,0:T(8,128)(2,1)S(1)}, u32[]{:S(2)}) copy-start(bf16[1280,128]{1,0:T(8,128)(2,1)S(1)} %collective-permute-done.4.refs_2_) | copy-start | bytes 983044
  26.3 12.6 %collective-permute-start.5 = (bf16[1280,128]{1,0:T(8,128)(2,1)S(1)}, bf16[1280,128]{1,0:T(8,128)(2,1)}, u32[]{:S(2)}, u32[]{:S(2)}) collective-permute-start(bf16[1280,128]{1,0:T(8,128)(2,1)S(1)} %collective-permute-done.3.refs_0_), channel_id=1, source_target_pairs={{0,4},{1,5},{2,6},{3,7},{4,8},{5,9},{6,10},{7,11},{8,12},{9,13},{1... | collective-permute-start | bytes 983048 | tf_op jit(solution)/shard_map/ppermute | solution.py:34
  26.3 12.5 %collective-permute-start.6 = (bf16[1280,128]{1,0:T(8,128)(2,1)S(1)}, bf16[1280,128]{1,0:T(8,128)(2,1)S(1)}, u32[]{:S(2)}, u32[]{:S(2)}) collective-permute-start(bf16[1280,128]{1,0:T(8,128)(2,1)S(1)} %collective-permute-done.3.refs_0_), channel_id=1, source_target_pairs={{0,2},{1,3},{2,0},{3,1},{4,6},{5,7},{6,4},{7,5},{8,10},{9,11},{10,... | collective-permute-start | bytes 983048 | tf_op jit(solution)/shard_map/ppermute | solution.py:34
  30.3 16.3 %collective-permute-start.12 = (bf16[1280,128]{1,0:T(8,128)(2,1)S(1)}, bf16[1280,128]{1,0:T(8,128)(2,1)}, u32[]{:S(2)}, u32[]{:S(2)}) collective-permute-start(bf16[1280,128]{1,0:T(8,128)(2,1)S(1)} %collective-permute-done.9.refs_1_), channel_id=1, source_target_pairs={{0,4},{1,5},{2,6},{3,7},{4,8},{5,9},{6,10},{7,11},{8,12},{9,13},{1... | collective-permute-start | bytes 983048 | tf_op jit(solution)/shard_map/ppermute | solution.py:34
  31.5 15.1 %collective-permute-start.13 = (bf16[1280,128]{1,0:T(8,128)(2,1)S(1)}, bf16[1280,128]{1,0:T(8,128)(2,1)}, u32[]{:S(2)}, u32[]{:S(2)}) collective-permute-start(bf16[1280,128]{1,0:T(8,128)(2,1)S(1)} %collective-permute-done.9.refs_1_), channel_id=1, source_target_pairs={{0,2},{1,3},{2,0},{3,1},{4,6},{5,7},{6,4},{7,5},{8,10},{9,11},{10,... | collective-permute-start | bytes 983048 | tf_op jit(solution)/shard_map/ppermute | solution.py:34
  38.9 0.7 copy-start.3
  39.6 13.3 %collective-permute-start.7 = (bf16[1280,128]{1,0:T(8,128)(2,1)}, bf16[1280,128]{1,0:T(8,128)(2,1)}, u32[]{:S(2)}, u32[]{:S(2)}) collective-permute-start(bf16[1280,128]{1,0:T(8,128)(2,1)} %collective-permute-done.5.refs_0_), channel_id=1, source_target_pairs={{0,4},{1,5},{2,6},{3,7},{4,8},{5,9},{6,10},{7,11},{8,12},{9,13},{1... | collective-permute-start | bytes 983048 | tf_op jit(solution)/shard_map/ppermute | solution.py:34
  39.6 13.3 %collective-permute-start.8 = (bf16[1280,128]{1,0:T(8,128)(2,1)}, bf16[1280,128]{1,0:T(8,128)(2,1)}, u32[]{:S(2)}, u32[]{:S(2)}) collective-permute-start(bf16[1280,128]{1,0:T(8,128)(2,1)} %collective-permute-done.5.refs_0_), channel_id=1, source_target_pairs={{0,2},{1,3},{2,0},{3,1},{4,6},{5,7},{6,4},{7,5},{8,10},{9,11},{10,... | collective-permute-start | bytes 983048 | tf_op jit(solution)/shard_map/ppermute | solution.py:34
  40.3 1.6 %copy-start = (bf16[32,8,32,128]{3,2,1,0:T(8,128)(2,1)S(1)}, bf16[32,8,32,128]{3,2,1,0:T(8,128)(2,1)}, u32[]{:S(2)}) copy-start(bf16[32,8,32,128]{3,2,1,0:T(8,128)(2,1)} %copy.10) | copy-start | bytes 6291460
  41.9 11.0 %copy-start.2 = (bf16[1280,128]{1,0:T(8,128)(2,1)S(1)}, bf16[1280,128]{1,0:T(8,128)(2,1)}, u32[]{:S(2)}) copy-start(bf16[1280,128]{1,0:T(8,128)(2,1)} %copy-done.1) | copy-start | bytes 983044
  46.6 12.7 %collective-permute-start.15 = (bf16[1280,128]{1,0:T(8,128)(2,1)}, bf16[1280,128]{1,0:T(8,128)(2,1)S(1)}, u32[]{:S(2)}, u32[]{:S(2)}) collective-permute-start(bf16[1280,128]{1,0:T(8,128)(2,1)} %collective-permute-done.12.refs_1_), channel_id=1, source_target_pairs={{0,4},{1,5},{2,6},{3,7},{4,8},{5,9},{6,10},{7,11},{8,12},{9,13},{1... | collective-permute-start | bytes 983048 | tf_op jit(solution)/shard_map/ppermute | solution.py:34
  46.7 12.7 %collective-permute-start.16 = (bf16[1280,128]{1,0:T(8,128)(2,1)}, bf16[1280,128]{1,0:T(8,128)(2,1)S(1)}, u32[]{:S(2)}, u32[]{:S(2)}) collective-permute-start(bf16[1280,128]{1,0:T(8,128)(2,1)} %collective-permute-done.12.refs_1_), channel_id=1, source_target_pairs={{0,2},{1,3},{2,0},{3,1},{4,6},{5,7},{6,4},{7,5},{8,10},{9,11},{10,... | collective-permute-start | bytes 983048 | tf_op jit(solution)/shard_map/ppermute | solution.py:34
  52.9 2.6 %copy-start.4 = (bf16[1280,128]{1,0:T(8,128)(2,1)S(1)}, bf16[1280,128]{1,0:T(8,128)(2,1)}, u32[]{:S(2)}) copy-start(bf16[1280,128]{1,0:T(8,128)(2,1)} %copy-done.3) | copy-start | bytes 983044
  55.4 9.5 %collective-permute-start.14 = (bf16[1280,128]{1,0:T(8,128)(2,1)}, bf16[1280,128]{1,0:T(8,128)(2,1)S(1)}, u32[]{:S(2)}, u32[]{:S(2)}) collective-permute-start(bf16[1280,128]{1,0:T(8,128)(2,1)} %collective-permute-done.8.refs_2_), channel_id=1, source_target_pairs={{0,4},{1,5},{2,6},{3,7},{4,8},{5,9},{6,10},{7,11},{8,12},{9,13},{1... | collective-permute-start | bytes 983048 | tf_op jit(solution)/shard_map/ppermute | solution.py:34
  59.4 7.1 %collective-permute-start.17 = (bf16[1280,128]{1,0:T(8,128)(2,1)S(1)}, bf16[1280,128]{1,0:T(8,128)(2,1)S(1)}, u32[]{:S(2)}, u32[]{:S(2)}) collective-permute-start(bf16[1280,128]{1,0:T(8,128)(2,1)S(1)} %collective-permute-done.15.refs_1_), channel_id=1, source_target_pairs={{0,2},{1,3},{2,0},{3,1},{4,6},{5,7},{6,4},{7,5},{8,10},{9,11},{10,... | collective-permute-start | bytes 983048 | tf_op jit(solution)/shard_map/ppermute | solution.py:34
  69.2 2.5 %collective-permute-start.19 = (bf16[1280,128]{1,0:T(8,128)(2,1)S(1)}, bf16[1280,128]{1,0:T(8,128)(2,1)S(1)}, u32[]{:S(2)}, u32[]{:S(2)}) collective-permute-start(bf16[1280,128]{1,0:T(8,128)(2,1)S(1)} %bitcast.76), channel_id=1, source_target_pairs={{0,1},{1,0},{2,3},{3,2},{4,5},{5,4},{6,7},{7,6},{8,9},{9,8},{10,11... | collective-permute-start | bytes 983048 | tf_op jit(solution)/shard_map/ppermute | solution.py:34
  69.3 6.2 %collective-permute-start.23 = (bf16[1280,128]{1,0:T(8,128)(2,1)S(1)}, bf16[1280,128]{1,0:T(8,128)(2,1)S(1)}, u32[]{:S(2)}, u32[]{:S(2)}) collective-permute-start(bf16[1280,128]{1,0:T(8,128)(2,1)S(1)} %bitcast.73), channel_id=1, source_target_pairs={{0,1},{1,0},{2,3},{3,2},{4,5},{5,4},{6,7},{7,6},{8,9},{9,8},{10,11... | collective-permute-start | bytes 983048 | tf_op jit(solution)/shard_map/ppermute | solution.py:34
  69.8 2.1 %collective-permute-start.18 = (bf16[1280,128]{1,0:T(8,128)(2,1)S(1)}, bf16[1280,128]{1,0:T(8,128)(2,1)S(1)}, u32[]{:S(2)}, u32[]{:S(2)}) collective-permute-start(bf16[1280,128]{1,0:T(8,128)(2,1)S(1)} %bitcast.74), channel_id=1, source_target_pairs={{0,1},{1,0},{2,3},{3,2},{4,5},{5,4},{6,7},{7,6},{8,9},{9,8},{10,11... | collective-permute-start | bytes 983048 | tf_op jit(solution)/shard_map/ppermute | solution.py:34
  69.9 12.5 %collective-permute-start.21 = (bf16[1280,128]{1,0:T(8,128)(2,1)S(1)}, bf16[1280,128]{1,0:T(8,128)(2,1)S(1)}, u32[]{:S(2)}, u32[]{:S(2)}) collective-permute-start(bf16[1280,128]{1,0:T(8,128)(2,1)S(1)} %bitcast.70), channel_id=1, source_target_pairs={{0,1},{1,0},{2,3},{3,2},{4,5},{5,4},{6,7},{7,6},{8,9},{9,8},{10,11... | collective-permute-start | bytes 983048 | tf_op jit(solution)/shard_map/ppermute | solution.py:34
  71.9 9.8 %collective-permute-start.24 = (bf16[1280,128]{1,0:T(8,128)(2,1)S(1)}, bf16[1280,128]{1,0:T(8,128)(2,1)S(1)}, u32[]{:S(2)}, u32[]{:S(2)}) collective-permute-start(bf16[1280,128]{1,0:T(8,128)(2,1)S(1)} %fusion.15), channel_id=1, source_target_pairs={{0,2},{1,3},{2,0},{3,1},{4,6},{5,7},{6,4},{7,5},{8,10},{9,11},{10,... | collective-permute-start | bytes 983048 | tf_op jit(solution)/shard_map/ppermute | solution.py:34
  74.9 6.9 %collective-permute-start.28 = (bf16[1280,128]{1,0:T(8,128)(2,1)S(1)}, bf16[1280,128]{1,0:T(8,128)(2,1)S(1)}, u32[]{:S(2)}, u32[]{:S(2)}) collective-permute-start(bf16[1280,128]{1,0:T(8,128)(2,1)S(1)} %bitcast.75), channel_id=1, source_target_pairs={{0,1},{1,0},{2,3},{3,2},{4,5},{5,4},{6,7},{7,6},{8,9},{9,8},{10,11... | collective-permute-start | bytes 983048 | tf_op jit(solution)/shard_map/ppermute | solution.py:34
  75.0 14.1 %collective-permute-start.27 = (bf16[1280,128]{1,0:T(8,128)(2,1)S(1)}, bf16[1280,128]{1,0:T(8,128)(2,1)S(1)}, u32[]{:S(2)}, u32[]{:S(2)}) collective-permute-start(bf16[1280,128]{1,0:T(8,128)(2,1)S(1)} %bitcast.72), channel_id=1, source_target_pairs={{0,1},{1,0},{2,3},{3,2},{4,5},{5,4},{6,7},{7,6},{8,9},{9,8},{10,11... | collective-permute-start | bytes 983048 | tf_op jit(solution)/shard_map/ppermute | solution.py:34
  75.5 11.5 %collective-permute-start.22 = (bf16[1280,128]{1,0:T(8,128)(2,1)S(1)}, bf16[1280,128]{1,0:T(8,128)(2,1)S(1)}, u32[]{:S(2)}, u32[]{:S(2)}) collective-permute-start(bf16[1280,128]{1,0:T(8,128)(2,1)S(1)} %fusion.16), channel_id=1, source_target_pairs={{0,4},{1,5},{2,6},{3,7},{4,8},{5,9},{6,10},{7,11},{8,12},{9,13},{1... | collective-permute-start | bytes 983048 | tf_op jit(solution)/shard_map/ppermute | solution.py:34
  81.8 14.1 %collective-permute-start.31 = (bf16[1280,128]{1,0:T(8,128)(2,1)S(1)}, bf16[1280,128]{1,0:T(8,128)(2,1)S(1)}, u32[]{:S(2)}, u32[]{:S(2)}) collective-permute-start(bf16[1280,128]{1,0:T(8,128)(2,1)S(1)} %bitcast.71), channel_id=1, source_target_pairs={{0,1},{1,0},{2,3},{3,2},{4,5},{5,4},{6,7},{7,6},{8,9},{9,8},{10,11... | collective-permute-start | bytes 983048 | tf_op jit(solution)/shard_map/ppermute | solution.py:34
  81.8 17.9 %collective-permute-start.20 = (bf16[1280,128]{1,0:T(8,128)(2,1)S(1)}, bf16[1280,128]{1,0:T(8,128)(2,1)S(1)}, u32[]{:S(2)}, u32[]{:S(2)}) collective-permute-start(bf16[1280,128]{1,0:T(8,128)(2,1)S(1)} %bitcast.69), channel_id=1, source_target_pairs={{0,1},{1,0},{2,3},{3,2},{4,5},{5,4},{6,7},{7,6},{8,9},{9,8},{10,11... | collective-permute-start | bytes 983048 | tf_op jit(solution)/shard_map/ppermute | solution.py:34
  82.4 11.7 %collective-permute-start.29 = (bf16[1280,128]{1,0:T(8,128)(2,1)S(1)}, bf16[1280,128]{1,0:T(8,128)(2,1)S(1)}, u32[]{:S(2)}, u32[]{:S(2)}) collective-permute-start(bf16[1280,128]{1,0:T(8,128)(2,1)S(1)} %fusion.5), channel_id=1, source_target_pairs={{0,4},{1,5},{2,6},{3,7},{4,8},{5,9},{6,10},{7,11},{8,12},{9,13},{1... | collective-permute-start | bytes 983048 | tf_op jit(solution)/shard_map/ppermute | solution.py:34
  87.0 8.9 %collective-permute-start.25 = (bf16[1280,128]{1,0:T(8,128)(2,1)S(1)}, bf16[1280,128]{1,0:T(8,128)(2,1)S(1)}, u32[]{:S(2)}, u32[]{:S(2)}) collective-permute-start(bf16[1280,128]{1,0:T(8,128)(2,1)S(1)} %fusion.8), channel_id=1, source_target_pairs={{0,2},{1,3},{2,0},{3,1},{4,6},{5,7},{6,4},{7,5},{8,10},{9,11},{10,... | collective-permute-start | bytes 983048 | tf_op jit(solution)/shard_map/ppermute | solution.py:34
  94.3 12.5 %collective-permute-start.30 = (bf16[1280,128]{1,0:T(8,128)(2,1)S(1)}, bf16[1280,128]{1,0:T(8,128)(2,1)S(1)}, u32[]{:S(2)}, u32[]{:S(2)}) collective-permute-start(bf16[1280,128]{1,0:T(8,128)(2,1)S(1)} %fusion.7), channel_id=1, source_target_pairs={{0,4},{1,5},{2,6},{3,7},{4,8},{5,9},{6,10},{7,11},{8,12},{9,13},{1... | collective-permute-start | bytes 983048 | tf_op jit(solution)/shard_map/ppermute | solution.py:34
  96.0 15.0 %collective-permute-start.32 = (bf16[1280,128]{1,0:T(8,128)(2,1)S(1)}, bf16[1280,128]{1,0:T(8,128)(2,1)S(1)}, u32[]{:S(2)}, u32[]{:S(2)}) collective-permute-start(bf16[1280,128]{1,0:T(8,128)(2,1)S(1)} %fusion.3), channel_id=1, source_target_pairs={{0,12},{1,13},{2,14},{3,15},{4,0},{5,1},{6,2},{7,3},{8,4},{9,5},{1... | collective-permute-start | bytes 983048 | tf_op jit(solution)/shard_map/ppermute | solution.py:34
  98.4 12.7 %collective-permute-start.26 = (bf16[1280,128]{1,0:T(8,128)(2,1)S(1)}, bf16[1280,128]{1,0:T(8,128)(2,1)S(1)}, u32[]{:S(2)}, u32[]{:S(2)}) collective-permute-start(bf16[1280,128]{1,0:T(8,128)(2,1)S(1)} %fusion.10), channel_id=1, source_target_pairs={{0,2},{1,3},{2,0},{3,1},{4,6},{5,7},{6,4},{7,5},{8,10},{9,11},{10,... | collective-permute-start | bytes 983048 | tf_op jit(solution)/shard_map/ppermute | solution.py:34

commit v12 on v11

--- a/solution.py
+++ b/solution.py
@@ -66,23 +66,33 @@
     def paired(keep, send):
         return keep + move(send, swap).astype(jnp.float32)
 
-    order = (1, 2, 3, 0)
-    far = {step: paired(far_keep[step], far_send[step]) for step in order}
-    aside, crossing = far[1].astype(jnp.bfloat16), far[2].astype(jnp.bfloat16)
-    half, aside, crossing = tie(half, aside, crossing)
-    crossed = {2: move(crossing, ACROSS)}
+    def halves(array):
+        return array[: array.shape[0] // 2], array[array.shape[0] // 2 :]
+
+    def narrow(array):
+        return array.astype(jnp.bfloat16)
+
+    def wide(array):
+        return array.astype(jnp.float32)
+
+    far = {step: paired(far_keep[step], far_send[step]) for step in (2, 1, 3, 0)}
+    half, far[3], far[0], aside, *crossing = tie(half, far[3], far[0], narrow(far[1]), *map(narrow, halves(far[2])))
+    crossed = {2: [move(part, ACROSS) for part in crossing]}
     joining = move(aside, ALONG)
     near_keep, near_send = near_of(half)
     near = {step: paired(near_keep[step], near_send[step]) for step in (2, 1, 3, 0)}
-    crossing, crossed[2] = tie(far[3].astype(jnp.bfloat16), crossed[2])
+    crossing, crossed[2][1] = tie(narrow(far[3]), crossed[2][1])
     crossed[3] = move(crossing, ACROSS)
-    crossing, crossed[3] = tie((far[0] + joining.astype(jnp.float32)).astype(jnp.bfloat16), crossed[3])
+    crossing, crossed[3] = tie(narrow(far[0] + wide(joining)), crossed[3])
     crossed[0] = move(crossing, ACROSS)
 
-    two_on = move((near[2] + crossed[2].astype(jnp.float32)).astype(jnp.bfloat16), ALONG)
-    one_on = move((near[1] + two_on.astype(jnp.float32)).astype(jnp.bfloat16), ALONG)
-    one_back = move((near[3] + crossed[3].astype(jnp.float32)).astype(jnp.bfloat16), BACK)
-    return near[0] + crossed[0].astype(jnp.float32) + one_on.astype(jnp.float32) + one_back.astype(jnp.float32)
+    two_on = [move(narrow(own + wide(part)), ALONG) for own, part in zip(halves(near[2]), crossed[2])]
+    later, two_on[0] = tie(near[1], two_on[0])
+    one_on = [
+        move(narrow(halves(own)[index] + wide(two_on[index])), ALONG) for index, own in enumerate((near[1], later))
+    ]
+    one_back = move(narrow(near[3] + wide(crossed[3])), BACK)
+    return near[0] + wide(crossed[0]) + wide(one_back) + wide(jnp.concatenate(one_on))
 
 
 def clear(half):
@@ -225,7 +235,6 @@
     given = lax.dynamic_slice_in_dim(occupied, (1 - core) * LANES, LANES, 1)
     parts = [mine, move(given, swap)]
     others = [move(array, swap) for array in (block_values, block_pairs, live_counts)]
-    *parts, block_values, block_pairs, live_counts = tie(*parts, block_values, block_pairs, live_counts)
     tile_sets = [values.reshape(slots, BLK * BLK // LANES, LANES) for values in (block_values, others[0])]
 
     slot_ids = jnp.arange(chips, dtype=jnp.int32)

time: 113 us -> 108 us (0.956); the launches traced: 112 us -> 108 us
  waiting for transfers between devices: 53.5 us -> 41.3 us
  starting transfers between devices: 22.9 us -> 30 us
  local copies, waits for them, and re-layouts: 9.67 us -> 11.4 us
    ppermute x33 -> x36, waiting for transfers between devices: 53.5 us -> 41.3 us  [move(): return lax.ppermute(array, 'aux', pairs)]
    ppermute x33 -> x36, starting transfers between devices: 22.9 us -> 30 us  [move(): return lax.ppermute(array, 'aux', pairs)]
    unnamed x13, local copies, waits for them, and re-layouts: 8.47 us -> 10.2 us
  transfers between devices with their start and end apart: 33 -> 36, of which waited for: 13 -> 14; matrix products, arithmetic and copies ran while one was open for 9% -> 10% of each run, Pallas kernels for 16% -> 14%
where the time goes in v12:
time: 108 us
  waiting for transfers between devices  41.3 us (38%)
  starting transfers between devices  30 us (28%)
  Pallas kernels  20.4 us (19%)
  local copies, waits for them, and re-layouts  11.4 us (11%)
  other arithmetic  4.16 us (4%)
    ppermute x36, waiting for transfers between devices, move(): return lax.ppermute(array, 'aux', pairs)  41.3 us
    ppermute x36, starting transfers between devices, move(): return lax.ppermute(array, 'aux', pairs)  30 us
    pallas_call x7, Pallas kernels, call(): pl.pallas_call(kernel, out_shape=outs, in_specs=in_specs, out_specs=[VMEM...  20.4 us
    unnamed x13, local copies, waits for them, and re-layouts  10.2 us
  transfers between devices with their start and end apart: 36, of which 14 were waited for; matrix products, arithmetic and copies ran while one was open for 10% of the time, Pallas kernels for 14%

profile of v12, /device:TPU:0, one launch (start us, length us, event | category | flops | bytes accessed | tf_op | source)
XLA Modules:
  0.0 108.3 jit_solution(4268896666609703966)
XLA Ops:
  0.0 0.5 collective-permute-start.11
  0.5 1.1 %constant_dynamic-slice_fusion.1 = (bf16[1280,128]{1,0:T(8,128)(2,1)S(1)}, bf16[1280,128]{1,0:T(8,128)(2,1)S(1)}) fusion(bf16[1280,256]{1,0:T(8,128)(2,1)} %param.7, s32[]{:T(128)S(6)} %select_n.162, s32[]{:T(128)S(6)} %select_n.161), kind=kLoop, calls=%fused_computation.91 | loop fusion | bytes 1310728 | tf_op jit(solution)/shard_map/dynamic_slice | solution.py:235
  1.6 2.6 %collective-permute-start.2 = (bf16[1280,128]{1,0:T(8,128)(2,1)S(1)}, bf16[1280,128]{1,0:T(8,128)(2,1)S(1)}, u32[]{:S(2)}, u32[]{:S(2)}) collective-permute-start(bf16[1280,128]{1,0:T(8,128)(2,1)S(1)} %get-tuple-element.121.refs_0_), channel_id=1, source_target_pairs={{0,4},{1,5},{2,6},{3,7},{4,8},{5,9},{6,10},{7,11},{8,12},{9,13},{1... | collective-permute-start | bytes 983048 | tf_op jit(solution)/shard_map/ppermute | solution.py:34
  4.2 1.5 %collective-permute-start.3 = (bf16[1280,128]{1,0:T(8,128)(2,1)S(1)}, bf16[1280,128]{1,0:T(8,128)(2,1)S(1)}, u32[]{:S(2)}, u32[]{:S(2)}) collective-permute-start(bf16[1280,128]{1,0:T(8,128)(2,1)S(1)} %get-tuple-element.121.refs_0_), channel_id=1, source_target_pairs={{0,2},{1,3},{2,0},{3,1},{4,6},{5,7},{6,4},{7,5},{8,10},{9,11},{10,... | collective-permute-start | bytes 983048 | tf_op jit(solution)/shard_map/ppermute | solution.py:34
  5.7 0.5 collective-permute-start
  6.2 0.7 constant_dynamic-update-slice_fusion.1
  7.5 2.1 %copy.9 = bf16[32,8,32,128]{3,2,1,0:T(8,128)(2,1)S(1)} copy(bf16[32,8,32,128]{3,1,2,0:T(8,128)(2,1)} %bitcast.63) | data formatting | bytes 4194304
  9.7 0.1 collective-permute-start.8
  9.8 0.7 compare_select_fusion.3
  10.5 0.9 collective-permute-done.8.refs_1_
  11.3 0.5 collective-permute-start.10
  11.9 1.6 %collective-permute-start.9 = (bf16[1280,128]{1,0:T(8,128)(2,1)S(1)}, bf16[1280,128]{1,0:T(8,128)(2,1)}, u32[]{:S(2)}, u32[]{:S(2)}) collective-permute-start(bf16[1280,128]{1,0:T(8,128)(2,1)S(1)} %collective-permute-done.8.refs_1_), channel_id=1, source_target_pairs={{0,4},{1,5},{2,6},{3,7},{4,8},{5,9},{6,10},{7,11},{8,12},{9,13},{1... | collective-permute-start | bytes 983048 | tf_op jit(solution)/shard_map/ppermute | solution.py:34
  13.5 0.7 copy-done.3
  14.2 0.6 fusion.27
  14.9 1.6 %collective-permute-start.4 = (bf16[1280,128]{1,0:T(8,128)(2,1)S(1)}, bf16[1280,128]{1,0:T(8,128)(2,1)}, u32[]{:S(2)}, u32[]{:S(2)}) collective-permute-start(bf16[1280,128]{1,0:T(8,128)(2,1)S(1)} %collective-permute-done.2.refs_0_), channel_id=1, source_target_pairs={{0,4},{1,5},{2,6},{3,7},{4,8},{5,9},{6,10},{7,11},{8,12},{9,13},{1... | collective-permute-start | bytes 983048 | tf_op jit(solution)/shard_map/ppermute | solution.py:34
  16.5 1.5 %collective-permute-start.5 = (bf16[1280,128]{1,0:T(8,128)(2,1)S(1)}, bf16[1280,128]{1,0:T(8,128)(2,1)S(1)}, u32[]{:S(2)}, u32[]{:S(2)}) collective-permute-start(bf16[1280,128]{1,0:T(8,128)(2,1)S(1)} %collective-permute-done.2.refs_0_), channel_id=1, source_target_pairs={{0,2},{1,3},{2,0},{3,1},{4,6},{5,7},{6,4},{7,5},{8,10},{9,11},{10,... | collective-permute-start | bytes 983048 | tf_op jit(solution)/shard_map/ppermute | solution.py:34
  18.0 3.9 %collective-permute-done.10.refs_3_ = bf16[1280,128]{1,0:T(8,128)(2,1)S(1)} collective-permute-done((bf16[1280,128]{1,0:T(8,128)(2,1)S(1)}, bf16[1280,128]{1,0:T(8,128)(2,1)S(1)}, u32[]{:S(2)}, u32[]{:S(2)}) %collective-permute-start.10) | collective-permute-done | bytes 327712 | tf_op jit(solution)/shard_map/ppermute | solution.py:34
  21.9 2.5 %collective-permute-done.9.refs_1_ = bf16[1280,128]{1,0:T(8,128)(2,1)} collective-permute-done((bf16[1280,128]{1,0:T(8,128)(2,1)S(1)}, bf16[1280,128]{1,0:T(8,128)(2,1)}, u32[]{:S(2)}, u32[]{:S(2)}) %collective-permute-start.9) | collective-permute-done | bytes 327712 | tf_op jit(solution)/shard_map/ppermute | solution.py:34
  24.4 3.4 %copy.10 = bf16[32,8,32,128]{3,2,1,0:T(8,128)(2,1)} copy(bf16[32,8,32,128]{3,1,2,0:T(8,128)(2,1)} %bitcast.25) | data formatting | bytes 4194304
  27.8 1.5 %collective-permute-start.13 = (bf16[1280,128]{1,0:T(8,128)(2,1)}, bf16[1280,128]{1,0:T(8,128)(2,1)}, u32[]{:S(2)}, u32[]{:S(2)}) collective-permute-start(bf16[1280,128]{1,0:T(8,128)(2,1)} %collective-permute-done.9.refs_1_), channel_id=1, source_target_pairs={{0,2},{1,3},{2,0},{3,1},{4,6},{5,7},{6,4},{7,5},{8,10},{9,11},{10,... | collective-permute-start | bytes 983048 | tf_op jit(solution)/shard_map/ppermute | solution.py:34
  29.3 0.3 convert_reduce_fusion
  29.6 0.5 select_reduce_fusion
  30.1 0.2 collective-permute-done.4.refs_0_
  30.3 0.7 copy-done.1
  31.0 1.2 %collective-permute-start.6 = (bf16[1280,128]{1,0:T(8,128)(2,1)}, bf16[1280,128]{1,0:T(8,128)(2,1)}, u32[]{:S(2)}, u32[]{:S(2)}) collective-permute-start(bf16[1280,128]{1,0:T(8,128)(2,1)} %collective-permute-done.4.refs_0_), channel_id=1, source_target_pairs={{0,4},{1,5},{2,6},{3,7},{4,8},{5,9},{6,10},{7,11},{8,12},{9,13},{1... | collective-permute-start | bytes 983048 | tf_op jit(solution)/shard_map/ppermute | solution.py:34
  32.2 1.2 %collective-permute-start.7 = (bf16[1280,128]{1,0:T(8,128)(2,1)}, bf16[1280,128]{1,0:T(8,128)(2,1)}, u32[]{:S(2)}, u32[]{:S(2)}) collective-permute-start(bf16[1280,128]{1,0:T(8,128)(2,1)} %collective-permute-done.4.refs_0_), channel_id=1, source_target_pairs={{0,2},{1,3},{2,0},{3,1},{4,6},{5,7},{6,4},{7,5},{8,10},{9,11},{10,... | collective-permute-start | bytes 983048 | tf_op jit(solution)/shard_map/ppermute | solution.py:34
  33.4 0.1 convert_reduce_fusion.1.bounds_ref
  33.5 0.1 concatenate.10.table_ref
  33.6 1.6 %copy-done = bf16[32,8,32,128]{3,2,1,0:T(8,128)(2,1)S(1)} copy-done((bf16[32,8,32,128]{3,2,1,0:T(8,128)(2,1)S(1)}, bf16[32,8,32,128]{3,2,1,0:T(8,128)(2,1)}, u32[]{:S(2)}) %copy-start) | copy-done | bytes 2097176
  35.2 1.0 copy-done.4
  36.2 3.5 %shard_map.46 = (f32[41024,128]{1,0:T(8,128)S(1)}, bf16[512,32,128]{2,1,0:T(8,128)(2,1)S(1)}) custom-call(s32[1584]{0:T(1024)S(1)} %concatenate.10.table_ref, s32[6]{0:T(128)S(1)} %convert_reduce_fusion.1.bounds_ref, bf16[1280,128]{1,0:T(8,128)(2,1)S(1)} %get-tuple-element.121.refs_0_, bf16[1280,128]{1,0:T(8,128)(2,1)S(1)} %copy-done.4, ...), custom_call_target="tpu_custom_call" | custom-call | flops 107374184 | bytes 4194304 | tf_op jit(solution)/shard_map/pallas_call | solution.py:208
  39.7 0.3 collective-permute-done.12.refs_1_
  40.0 1.4 %collective-permute-start.15 = (bf16[1280,128]{1,0:T(8,128)(2,1)}, bf16[1280,128]{1,0:T(8,128)(2,1)S(1)}, u32[]{:S(2)}, u32[]{:S(2)}) collective-permute-start(bf16[1280,128]{1,0:T(8,128)(2,1)} %collective-permute-done.12.refs_1_), channel_id=1, source_target_pairs={{0,4},{1,5},{2,6},{3,7},{4,8},{5,9},{6,10},{7,11},{8,12},{9,13},{1... | collective-permute-start | bytes 983048 | tf_op jit(solution)/shard_map/ppermute | solution.py:34
  41.4 0.8 collective-permute-start.16
  42.2 4.0 %collective-permute-done.6.refs_0_ = bf16[1280,128]{1,0:T(8,128)(2,1)} collective-permute-done((bf16[1280,128]{1,0:T(8,128)(2,1)}, bf16[1280,128]{1,0:T(8,128)(2,1)}, u32[]{:S(2)}, u32[]{:S(2)}) %collective-permute-start.6) | collective-permute-done | bytes 327712 | tf_op jit(solution)/shard_map/ppermute | solution.py:34
  46.1 3.4 %shard_map.47.refs_5_ = f32[41024,128]{1,0:T(8,128)S(1)} custom-call(s32[1584]{0:T(1024)S(1)} %concatenate.10.table_ref, s32[6]{0:T(128)S(1)} %convert_reduce_fusion.1.bounds_ref, bf16[1280,128]{1,0:T(8,128)(2,1)S(1)} %collective-permute-done.2.refs_0_, bf16[1280,128]{1,0:T(8,128)(2,1)} %collective-permute-done.9.refs_1_, ...), custom_call_target="tpu_custom_call", output_to_operand_aliasing={{}: (7, {})} | custom-call | flops 107374184 | bytes 4194304 | tf_op jit(solution)/shard_map/pallas_call | solution.py:208
  49.7 3.6 %shard_map.48.refs_5_ = f32[41024,128]{1,0:T(8,128)S(1)} custom-call(s32[1584]{0:T(1024)S(1)} %concatenate.10.table_ref, s32[6]{0:T(128)S(1)} %convert_reduce_fusion.1.bounds_ref, bf16[1280,128]{1,0:T(8,128)(2,1)} %collective-permute-done.4.refs_0_, bf16[1280,128]{1,0:T(8,128)(2,1)} %collective-permute-done.12.refs_1_, ...), custom_call_target="tpu_custom_call", output_to_operand_aliasing={{}: (7, {})} | custom-call | flops 107374184 | bytes 4194304 | tf_op jit(solution)/shard_map/pallas_call | solution.py:208
  53.3 3.6 %collective-permute-start.17 = (bf16[1280,128]{1,0:T(8,128)(2,1)S(1)}, bf16[1280,128]{1,0:T(8,128)(2,1)S(1)}, u32[]{:S(2)}, u32[]{:S(2)}) collective-permute-start(bf16[1280,128]{1,0:T(8,128)(2,1)S(1)} %collective-permute-done.15.refs_1_), channel_id=1, source_target_pairs={{0,2},{1,3},{2,0},{3,1},{4,6},{5,7},{6,4},{7,5},{8,10},{9,11},{10,... | collective-permute-start | bytes 983048 | tf_op jit(solution)/shard_map/ppermute | solution.py:34
  56.9 3.5 %shard_map.49.refs_3_ = f32[41024,128]{1,0:T(8,128)S(1)} custom-call(s32[1584]{0:T(1024)S(1)} %concatenate.10.table_ref, s32[6]{0:T(128)S(1)} %convert_reduce_fusion.1.bounds_ref, bf16[1280,128]{1,0:T(8,128)(2,1)} %collective-permute-done.6.refs_0_, bf16[1280,128]{1,0:T(8,128)(2,1)S(1)} %collective-permute-done.15.refs_1_, ...), custom_call_target="tpu_custom_call", output_to_operand_aliasing={{}: (7, {})} | custom-call | flops 107374184 | bytes 4194304 | tf_op jit(solution)/shard_map/pallas_call | solution.py:208
  60.3 1.6 %collective-permute-done.17.refs_1_ = bf16[1280,128]{1,0:T(8,128)(2,1)S(1)} collective-permute-done((bf16[1280,128]{1,0:T(8,128)(2,1)S(1)}, bf16[1280,128]{1,0:T(8,128)(2,1)S(1)}, u32[]{:S(2)}, u32[]{:S(2)}) %collective-permute-start.17) | collective-permute-done | bytes 327712 | tf_op jit(solution)/shard_map/ppermute | solution.py:34
  61.9 3.0 %shard_map.50 = (f32[41024,128]{1,0:T(8,128)S(1)}, bf16[256,128]{1,0:T(8,128)(2,1)S(1)}, bf16[1,1280,128]{2,1,0:T(8,128)(2,1)S(1)}, bf16[1,1280,128]{2,1,0:T(8,1...) custom-call(s32[1584]{0:T(1024)S(1)} %concatenate.10.table_ref, ...), custom_call_target="tpu_custom_call", output_to_operand_aliasing={{0}: (7, {})} | custom-call | flops 442918496 | bytes 4194304 | tf_op jit(solution)/shard_map/pallas_call | solution.py:208
  65.0 0.5 collective-permute-start.21
  65.5 0.1 collective-permute-start.20
  65.5 0.4 collective-permute-start.18
  66.0 1.4 %shard_map.51 = (f32[1,1280,128]{2,1,0:T(8,128)S(1)}, f32[1,1280,128]{2,1,0:T(8,128)S(1)}, f32[1,1280,128]{2,1,0:T(8,128)S(1)}, f32[1,1280,128]{2,1,0:T(8,128)S(1)}) custom-call(s32[8]{0:T(128)S(1)} %fusion.30.chips_ref, s32[1]{0:T(128)} %bitcast.core_ref, f32[41024,128]{1,0:T(8,128)S(1)} %get-tuple-element.91.half, ...), custom_call_target="tpu_custom_call" | custom-call | flops 335544320 | bytes 4194304 | tf_op jit(solution)/shard_map/pallas_call | solution.py:208
  67.6 0.4 collective-permute-done.18
  68.1 2.1 %shard_map.52 = (f32[1,1280,128]{2,1,0:T(8,128)S(1)}, f32[1,1280,128]{2,1,0:T(8,128)S(1)}, f32[1,1280,128]{2,1,0:T(8,128)S(1)}, f32[1,1280,128]{2,1,0:T(8,128)S(...) custom-call(s32[8]{0:T(128)S(1)} %fusion.30.chips_ref, ...), custom_call_target="tpu_custom_call" | custom-call | flops 335544320 | bytes 4194304 | tf_op jit(solution)/shard_map/pallas_call | solution.py:208
  70.1 0.2 collective-permute-start.30
  70.3 2.0 %collective-permute-start.24 = (bf16[640,128]{1,0:T(8,128)(2,1)S(1)}, bf16[640,128]{1,0:T(8,128)(2,1)S(1)}, u32[]{:S(2)}, u32[]{:S(2)}) collective-permute-start(bf16[640,128]{1,0:T(8,128)(2,1)S(1)} %get-tuple-element.97), channel_id=1, source_target_pairs={{0,2},{1,3},{2,0},{3,1},{4,6},{5,7},{6,4},{7,5},{8,10},{9,11},{10,... | collective-permute-start | bytes 491528 | tf_op jit(solution)/shard_map/ppermute | solution.py:34
  72.4 0.1 collective-permute-start.29
  72.5 0.3 collective-permute-start.31
  72.7 4.7 %collective-permute-done.24 = bf16[640,128]{1,0:T(8,128)(2,1)S(1)} collective-permute-done((bf16[640,128]{1,0:T(8,128)(2,1)S(1)}, bf16[640,128]{1,0:T(8,128)(2,1)S(1)}, u32[]{:S(2)}, u32[]{:S(2)}) %collective-permute-start.24) | collective-permute-done | bytes 163872 | tf_op jit(solution)/shard_map/ppermute | solution.py:34
  77.4 0.5 collective-permute-start.22
  77.9 0.1 bitcast_add_fusion
  78.0 2.6 %collective-permute-done.31 = bf16[640,128]{1,0:T(8,128)(2,1)S(1)} collective-permute-done((bf16[640,128]{1,0:T(8,128)(2,1)S(1)}, bf16[640,128]{1,0:T(8,128)(2,1)S(1)}, u32[]{:S(2)}, u32[]{:S(2)}) %collective-permute-start.31) | collective-permute-done | bytes 163872 | tf_op jit(solution)/shard_map/ppermute | solution.py:34
  80.6 1.7 %collective-permute-start.25 = (bf16[1280,128]{1,0:T(8,128)(2,1)S(1)}, bf16[1280,128]{1,0:T(8,128)(2,1)S(1)}, u32[]{:S(2)}, u32[]{:S(2)}) collective-permute-start(bf16[1280,128]{1,0:T(8,128)(2,1)S(1)} %bitcast_add_fusion.7), channel_id=1, source_target_pairs={{0,2},{1,3},{2,0},{3,1},{4,6},{5,7},{6,4},{7,5},{8,10},{9,11},{10,... | collective-permute-start | bytes 983048 | tf_op jit(solution)/shard_map/ppermute | solution.py:34
  82.5 0.1 bitcast_add_fusion.1
  82.6 1.7 %collective-permute-done.23 = bf16[1280,128]{1,0:T(8,128)(2,1)S(1)} collective-permute-done((bf16[1280,128]{1,0:T(8,128)(2,1)S(1)}, bf16[1280,128]{1,0:T(8,128)(2,1)S(1)}, u32[]{:S(2)}, u32[]{:S(2)}) %collective-permute-start.23) | collective-permute-done | bytes 327712 | tf_op jit(solution)/shard_map/ppermute | solution.py:34
  84.4 7.0 %collective-permute-done.32 = bf16[640,128]{1,0:T(8,128)(2,1)S(1)} collective-permute-done((bf16[640,128]{1,0:T(8,128)(2,1)S(1)}, bf16[640,128]{1,0:T(8,128)(2,1)S(1)}, u32[]{:S(2)}, u32[]{:S(2)}) %collective-permute-start.32) | collective-permute-done | bytes 163872 | tf_op jit(solution)/shard_map/ppermute | solution.py:34
  91.5 0.1 fusion.3
  91.6 3.8 %collective-permute-start.28 = (bf16[1280,128]{1,0:T(8,128)(2,1)S(1)}, bf16[1280,128]{1,0:T(8,128)(2,1)S(1)}, u32[]{:S(2)}, u32[]{:S(2)}) collective-permute-start(bf16[1280,128]{1,0:T(8,128)(2,1)S(1)} %fusion.3), channel_id=1, source_target_pairs={{0,12},{1,13},{2,14},{3,15},{4,0},{5,1},{6,2},{7,3},{8,4},{9,5},{1... | collective-permute-start | bytes 983048 | tf_op jit(solution)/shard_map/ppermute | solution.py:34
  95.6 4.9 %collective-permute-done.33 = bf16[640,128]{1,0:T(8,128)(2,1)S(1)} collective-permute-done((bf16[640,128]{1,0:T(8,128)(2,1)S(1)}, bf16[640,128]{1,0:T(8,128)(2,1)S(1)}, u32[]{:S(2)}, u32[]{:S(2)}) %collective-permute-start.33) | collective-permute-done | bytes 163872 | tf_op jit(solution)/shard_map/ppermute | solution.py:34
  100.5 6.8 %collective-permute-done.35 = bf16[640,128]{1,0:T(8,128)(2,1)S(1)} collective-permute-done((bf16[640,128]{1,0:T(8,128)(2,1)S(1)}, bf16[640,128]{1,0:T(8,128)(2,1)S(1)}, u32[]{:S(2)}, u32[]{:S(2)}) %collective-permute-start.35) | collective-permute-done | bytes 163872 | tf_op jit(solution)/shard_map/ppermute | solution.py:34
  107.3 1.0 fusion.7
  (52 shorter events, 1.0 us)
Async XLA Ops:
  0.0 24.4 %collective-permute-start.11 = (bf16[256,4096]{1,0:T(8,128)(2,1)}, bf16[256,4096]{1,0:T(8,128)(2,1)}, u32[]{:S(2)}, u32[]{:S(2)}) collective-permute-start(bf16[256,4096]{1,0:T(8,128)(2,1)} %param.4), channel_id=1, source_target_pairs={{0,1},{1,0},{2,3},{3,2},{4,5},{5,4},{6,7},{7,6},{8,9},{9,8},{10,11... | collective-permute-start | bytes 6291464 | tf_op jit(solution)/shard_map/ppermute | solution.py:34
  1.6 13.3 %collective-permute-start.2 = (bf16[1280,128]{1,0:T(8,128)(2,1)S(1)}, bf16[1280,128]{1,0:T(8,128)(2,1)S(1)}, u32[]{:S(2)}, u32[]{:S(2)}) collective-permute-start(bf16[1280,128]{1,0:T(8,128)(2,1)S(1)} %get-tuple-element.121.refs_0_), channel_id=1, source_target_pairs={{0,4},{1,5},{2,6},{3,7},{4,8},{5,9},{6,10},{7,11},{8,12},{9,13},{1... | collective-permute-start | bytes 983048 | tf_op jit(solution)/shard_map/ppermute | solution.py:34
  4.2 10.6 %collective-permute-start.3 = (bf16[1280,128]{1,0:T(8,128)(2,1)S(1)}, bf16[1280,128]{1,0:T(8,128)(2,1)S(1)}, u32[]{:S(2)}, u32[]{:S(2)}) collective-permute-start(bf16[1280,128]{1,0:T(8,128)(2,1)S(1)} %get-tuple-element.121.refs_0_), channel_id=1, source_target_pairs={{0,2},{1,3},{2,0},{3,1},{4,6},{5,7},{6,4},{7,5},{8,10},{9,11},{10,... | collective-permute-start | bytes 983048 | tf_op jit(solution)/shard_map/ppermute | solution.py:34
  5.7 4.0 %collective-permute-start.1 = (s32[256,2]{0,1:T(2,128)}, s32[256,2]{0,1:T(2,128)S(1)}, u32[]{:S(2)}, u32[]{:S(2)}) collective-permute-start(s32[256,2]{0,1:T(2,128)} %param.5), channel_id=1, source_target_pairs={{0,1},{1,0},{2,3},{3,2},{4,5},{5,4},{6,7},{7,6},{8,9},{9,8},{10,11... | collective-permute-start | bytes 6152 | tf_op jit(solution)/shard_map/ppermute | solution.py:34
  5.7 4.1 %collective-permute-start = (s32[1]{0:T(128)}, s32[1]{0:T(128)}, u32[]{:S(2)}, u32[]{:S(2)}) collective-permute-start(s32[1]{0:T(128)} %param.6), channel_id=1, source_target_pairs={{0,1},{1,0},{2,3},{3,2},{4,5},{5,4},{6,7},{7,6},{8,9},{9,8},{10,11... | collective-permute-start | bytes 20 | tf_op jit(solution)/shard_map/ppermute | solution.py:34
  9.7 1.7 %collective-permute-start.8 = (bf16[1280,128]{1,0:T(8,128)(2,1)S(1)}, bf16[1280,128]{1,0:T(8,128)(2,1)S(1)}, u32[]{:S(2)}, u32[]{:S(2)}) collective-permute-start(bf16[1280,128]{1,0:T(8,128)(2,1)S(1)} %get-tuple-element.120), channel_id=1, source_target_pairs={{0,1},{1,0},{2,3},{3,2},{4,5},{5,4},{6,7},{7,6},{8,9},{9,8},{10,11... | collective-permute-start | bytes 983048 | tf_op jit(solution)/shard_map/ppermute | solution.py:34
  11.3 10.6 %collective-permute-start.10 = (bf16[1280,128]{1,0:T(8,128)(2,1)S(1)}, bf16[1280,128]{1,0:T(8,128)(2,1)S(1)}, u32[]{:S(2)}, u32[]{:S(2)}) collective-permute-start(bf16[1280,128]{1,0:T(8,128)(2,1)S(1)} %collective-permute-done.8.refs_1_), channel_id=1, source_target_pairs={{0,2},{1,3},{2,0},{3,1},{4,6},{5,7},{6,4},{7,5},{8,10},{9,11},{10,... | collective-permute-start | bytes 983048 | tf_op jit(solution)/shard_map/ppermute | solution.py:34
  11.9 12.5 %collective-permute-start.9 = (bf16[1280,128]{1,0:T(8,128)(2,1)S(1)}, bf16[1280,128]{1,0:T(8,128)(2,1)}, u32[]{:S(2)}, u32[]{:S(2)}) collective-permute-start(bf16[1280,128]{1,0:T(8,128)(2,1)S(1)} %collective-permute-done.8.refs_1_), channel_id=1, source_target_pairs={{0,4},{1,5},{2,6},{3,7},{4,8},{5,9},{6,10},{7,11},{8,12},{9,13},{1... | collective-permute-start | bytes 983048 | tf_op jit(solution)/shard_map/ppermute | solution.py:34
  13.5 0.7 copy-start.3
  14.9 15.4 %collective-permute-start.4 = (bf16[1280,128]{1,0:T(8,128)(2,1)S(1)}, bf16[1280,128]{1,0:T(8,128)(2,1)}, u32[]{:S(2)}, u32[]{:S(2)}) collective-permute-start(bf16[1280,128]{1,0:T(8,128)(2,1)S(1)} %collective-permute-done.2.refs_0_), channel_id=1, source_target_pairs={{0,4},{1,5},{2,6},{3,7},{4,8},{5,9},{6,10},{7,11},{8,12},{9,13},{1... | collective-permute-start | bytes 983048 | tf_op jit(solution)/shard_map/ppermute | solution.py:34
  16.5 13.8 %collective-permute-start.5 = (bf16[1280,128]{1,0:T(8,128)(2,1)S(1)}, bf16[1280,128]{1,0:T(8,128)(2,1)S(1)}, u32[]{:S(2)}, u32[]{:S(2)}) collective-permute-start(bf16[1280,128]{1,0:T(8,128)(2,1)S(1)} %collective-permute-done.2.refs_0_), channel_id=1, source_target_pairs={{0,2},{1,3},{2,0},{3,1},{4,6},{5,7},{6,4},{7,5},{8,10},{9,11},{10,... | collective-permute-start | bytes 983048 | tf_op jit(solution)/shard_map/ppermute | solution.py:34
  27.8 12.2 %collective-permute-start.12 = (bf16[1280,128]{1,0:T(8,128)(2,1)}, bf16[1280,128]{1,0:T(8,128)(2,1)}, u32[]{:S(2)}, u32[]{:S(2)}) collective-permute-start(bf16[1280,128]{1,0:T(8,128)(2,1)} %collective-permute-done.9.refs_1_), channel_id=1, source_target_pairs={{0,4},{1,5},{2,6},{3,7},{4,8},{5,9},{6,10},{7,11},{8,12},{9,13},{1... | collective-permute-start | bytes 983048 | tf_op jit(solution)/shard_map/ppermute | solution.py:34
  27.8 12.2 %collective-permute-start.13 = (bf16[1280,128]{1,0:T(8,128)(2,1)}, bf16[1280,128]{1,0:T(8,128)(2,1)}, u32[]{:S(2)}, u32[]{:S(2)}) collective-permute-start(bf16[1280,128]{1,0:T(8,128)(2,1)} %collective-permute-done.9.refs_1_), channel_id=1, source_target_pairs={{0,2},{1,3},{2,0},{3,1},{4,6},{5,7},{6,4},{7,5},{8,10},{9,11},{10,... | collective-permute-start | bytes 983048 | tf_op jit(solution)/shard_map/ppermute | solution.py:34
  30.3 0.7 copy-start.1
  31.0 15.1 %collective-permute-start.6 = (bf16[1280,128]{1,0:T(8,128)(2,1)}, bf16[1280,128]{1,0:T(8,128)(2,1)}, u32[]{:S(2)}, u32[]{:S(2)}) collective-permute-start(bf16[1280,128]{1,0:T(8,128)(2,1)} %collective-permute-done.4.refs_0_), channel_id=1, source_target_pairs={{0,4},{1,5},{2,6},{3,7},{4,8},{5,9},{6,10},{7,11},{8,12},{9,13},{1... | collective-permute-start | bytes 983048 | tf_op jit(solution)/shard_map/ppermute | solution.py:34
  32.2 13.9 %collective-permute-start.7 = (bf16[1280,128]{1,0:T(8,128)(2,1)}, bf16[1280,128]{1,0:T(8,128)(2,1)}, u32[]{:S(2)}, u32[]{:S(2)}) collective-permute-start(bf16[1280,128]{1,0:T(8,128)(2,1)} %collective-permute-done.4.refs_0_), channel_id=1, source_target_pairs={{0,2},{1,3},{2,0},{3,1},{4,6},{5,7},{6,4},{7,5},{8,10},{9,11},{10,... | collective-permute-start | bytes 983048 | tf_op jit(solution)/shard_map/ppermute | solution.py:34
  33.6 1.6 %copy-start = (bf16[32,8,32,128]{3,2,1,0:T(8,128)(2,1)S(1)}, bf16[32,8,32,128]{3,2,1,0:T(8,128)(2,1)}, u32[]{:S(2)}) copy-start(bf16[32,8,32,128]{3,2,1,0:T(8,128)(2,1)} %copy.10) | copy-start | bytes 6291460
  35.2 1.0 copy-start.4
  40.0 13.2 %collective-permute-start.15 = (bf16[1280,128]{1,0:T(8,128)(2,1)}, bf16[1280,128]{1,0:T(8,128)(2,1)S(1)}, u32[]{:S(2)}, u32[]{:S(2)}) collective-permute-start(bf16[1280,128]{1,0:T(8,128)(2,1)} %collective-permute-done.12.refs_1_), channel_id=1, source_target_pairs={{0,4},{1,5},{2,6},{3,7},{4,8},{5,9},{6,10},{7,11},{8,12},{9,13},{1... | collective-permute-start | bytes 983048 | tf_op jit(solution)/shard_map/ppermute | solution.py:34
  41.4 11.9 %collective-permute-start.16 = (bf16[1280,128]{1,0:T(8,128)(2,1)}, bf16[1280,128]{1,0:T(8,128)(2,1)S(1)}, u32[]{:S(2)}, u32[]{:S(2)}) collective-permute-start(bf16[1280,128]{1,0:T(8,128)(2,1)} %collective-permute-done.12.refs_1_), channel_id=1, source_target_pairs={{0,2},{1,3},{2,0},{3,1},{4,6},{5,7},{6,4},{7,5},{8,10},{9,11},{10,... | collective-permute-start | bytes 983048 | tf_op jit(solution)/shard_map/ppermute | solution.py:34
  46.1 3.5 %copy-start.2 = (bf16[1280,128]{1,0:T(8,128)(2,1)S(1)}, bf16[1280,128]{1,0:T(8,128)(2,1)}, u32[]{:S(2)}) copy-start(bf16[1280,128]{1,0:T(8,128)(2,1)} %copy-done.1) | copy-start | bytes 983044
  49.6 10.7 %collective-permute-start.14 = (bf16[1280,128]{1,0:T(8,128)(2,1)}, bf16[1280,128]{1,0:T(8,128)(2,1)S(1)}, u32[]{:S(2)}, u32[]{:S(2)}) collective-permute-start(bf16[1280,128]{1,0:T(8,128)(2,1)} %collective-permute-done.7.refs_2_), channel_id=1, source_target_pairs={{0,4},{1,5},{2,6},{3,7},{4,8},{5,9},{6,10},{7,11},{8,12},{9,13},{1... | collective-permute-start | bytes 983048 | tf_op jit(solution)/shard_map/ppermute | solution.py:34
  53.3 8.6 %collective-permute-start.17 = (bf16[1280,128]{1,0:T(8,128)(2,1)S(1)}, bf16[1280,128]{1,0:T(8,128)(2,1)S(1)}, u32[]{:S(2)}, u32[]{:S(2)}) collective-permute-start(bf16[1280,128]{1,0:T(8,128)(2,1)S(1)} %collective-permute-done.15.refs_1_), channel_id=1, source_target_pairs={{0,2},{1,3},{2,0},{3,1},{4,6},{5,7},{6,4},{7,5},{8,10},{9,11},{10,... | collective-permute-start | bytes 983048 | tf_op jit(solution)/shard_map/ppermute | solution.py:34
  64.9 2.5 %collective-permute-start.19 = (bf16[1280,128]{1,0:T(8,128)(2,1)S(1)}, bf16[1280,128]{1,0:T(8,128)(2,1)S(1)}, u32[]{:S(2)}, u32[]{:S(2)}) collective-permute-start(bf16[1280,128]{1,0:T(8,128)(2,1)S(1)} %bitcast.62), channel_id=1, source_target_pairs={{0,1},{1,0},{2,3},{3,2},{4,5},{5,4},{6,7},{7,6},{8,9},{9,8},{10,11... | collective-permute-start | bytes 983048 | tf_op jit(solution)/shard_map/ppermute | solution.py:34
  65.0 2.5 %collective-permute-start.21 = (bf16[1280,128]{1,0:T(8,128)(2,1)S(1)}, bf16[1280,128]{1,0:T(8,128)(2,1)S(1)}, u32[]{:S(2)}, u32[]{:S(2)}) collective-permute-start(bf16[1280,128]{1,0:T(8,128)(2,1)S(1)} %bitcast.61), channel_id=1, source_target_pairs={{0,1},{1,0},{2,3},{3,2},{4,5},{5,4},{6,7},{7,6},{8,9},{9,8},{10,11... | collective-permute-start | bytes 983048 | tf_op jit(solution)/shard_map/ppermute | solution.py:34
  65.5 2.1 %collective-permute-start.20 = (bf16[1280,128]{1,0:T(8,128)(2,1)S(1)}, bf16[1280,128]{1,0:T(8,128)(2,1)S(1)}, u32[]{:S(2)}, u32[]{:S(2)}) collective-permute-start(bf16[1280,128]{1,0:T(8,128)(2,1)S(1)} %bitcast.59), channel_id=1, source_target_pairs={{0,1},{1,0},{2,3},{3,2},{4,5},{5,4},{6,7},{7,6},{8,9},{9,8},{10,11... | collective-permute-start | bytes 983048 | tf_op jit(solution)/shard_map/ppermute | solution.py:34
  65.5 2.4 %collective-permute-start.18 = (bf16[1280,128]{1,0:T(8,128)(2,1)S(1)}, bf16[1280,128]{1,0:T(8,128)(2,1)S(1)}, u32[]{:S(2)}, u32[]{:S(2)}) collective-permute-start(bf16[1280,128]{1,0:T(8,128)(2,1)S(1)} %bitcast.58), channel_id=1, source_target_pairs={{0,1},{1,0},{2,3},{3,2},{4,5},{5,4},{6,7},{7,6},{8,9},{9,8},{10,11... | collective-permute-start | bytes 983048 | tf_op jit(solution)/shard_map/ppermute | solution.py:34
  70.1 7.3 %collective-permute-start.30 = (bf16[1280,128]{1,0:T(8,128)(2,1)S(1)}, bf16[1280,128]{1,0:T(8,128)(2,1)S(1)}, u32[]{:S(2)}, u32[]{:S(2)}) collective-permute-start(bf16[1280,128]{1,0:T(8,128)(2,1)S(1)} %bitcast.60), channel_id=1, source_target_pairs={{0,1},{1,0},{2,3},{3,2},{4,5},{5,4},{6,7},{7,6},{8,9},{9,8},{10,11... | collective-permute-start | bytes 983048 | tf_op jit(solution)/shard_map/ppermute | solution.py:34
  70.3 7.1 %collective-permute-start.24 = (bf16[640,128]{1,0:T(8,128)(2,1)S(1)}, bf16[640,128]{1,0:T(8,128)(2,1)S(1)}, u32[]{:S(2)}, u32[]{:S(2)}) collective-permute-start(bf16[640,128]{1,0:T(8,128)(2,1)S(1)} %get-tuple-element.97), channel_id=1, source_target_pairs={{0,2},{1,3},{2,0},{3,1},{4,6},{5,7},{6,4},{7,5},{8,10},{9,11},{10,... | collective-permute-start | bytes 491528 | tf_op jit(solution)/shard_map/ppermute | solution.py:34
  72.4 10.1 %collective-permute-start.29 = (bf16[1280,128]{1,0:T(8,128)(2,1)S(1)}, bf16[1280,128]{1,0:T(8,128)(2,1)S(1)}, u32[]{:S(2)}, u32[]{:S(2)}) collective-permute-start(bf16[1280,128]{1,0:T(8,128)(2,1)S(1)} %bitcast.57), channel_id=1, source_target_pairs={{0,1},{1,0},{2,3},{3,2},{4,5},{5,4},{6,7},{7,6},{8,9},{9,8},{10,11... | collective-permute-start | bytes 983048 | tf_op jit(solution)/shard_map/ppermute | solution.py:34
  72.5 8.2 %collective-permute-start.31 = (bf16[640,128]{1,0:T(8,128)(2,1)S(1)}, bf16[640,128]{1,0:T(8,128)(2,1)S(1)}, u32[]{:S(2)}, u32[]{:S(2)}) collective-permute-start(bf16[640,128]{1,0:T(8,128)(2,1)S(1)} %get-tuple-element.107), channel_id=1, source_target_pairs={{0,2},{1,3},{2,0},{3,1},{4,6},{5,7},{6,4},{7,5},{8,10},{9,11},{10,... | collective-permute-start | bytes 491528 | tf_op jit(solution)/shard_map/ppermute | solution.py:34
  72.7 11.6 %collective-permute-start.23 = (bf16[1280,128]{1,0:T(8,128)(2,1)S(1)}, bf16[1280,128]{1,0:T(8,128)(2,1)S(1)}, u32[]{:S(2)}, u32[]{:S(2)}) collective-permute-start(bf16[1280,128]{1,0:T(8,128)(2,1)S(1)} %fusion.9), channel_id=1, source_target_pairs={{0,4},{1,5},{2,6},{3,7},{4,8},{5,9},{6,10},{7,11},{8,12},{9,13},{1... | collective-permute-start | bytes 983048 | tf_op jit(solution)/shard_map/ppermute | solution.py:34
  77.4 14.0 %collective-permute-start.27 = (bf16[1280,128]{1,0:T(8,128)(2,1)S(1)}, bf16[1280,128]{1,0:T(8,128)(2,1)S(1)}, u32[]{:S(2)}, u32[]{:S(2)}) collective-permute-start(bf16[1280,128]{1,0:T(8,128)(2,1)S(1)} %bitcast.56), channel_id=1, source_target_pairs={{0,1},{1,0},{2,3},{3,2},{4,5},{5,4},{6,7},{7,6},{8,9},{9,8},{10,11... | collective-permute-start | bytes 983048 | tf_op jit(solution)/shard_map/ppermute | solution.py:34
  77.4 18.1 %collective-permute-start.22 = (bf16[1280,128]{1,0:T(8,128)(2,1)S(1)}, bf16[1280,128]{1,0:T(8,128)(2,1)S(1)}, u32[]{:S(2)}, u32[]{:S(2)}) collective-permute-start(bf16[1280,128]{1,0:T(8,128)(2,1)S(1)} %bitcast.55), channel_id=1, source_target_pairs={{0,1},{1,0},{2,3},{3,2},{4,5},{5,4},{6,7},{7,6},{8,9},{9,8},{10,11... | collective-permute-start | bytes 983048 | tf_op jit(solution)/shard_map/ppermute | solution.py:34
  80.6 10.8 %collective-permute-start.25 = (bf16[1280,128]{1,0:T(8,128)(2,1)S(1)}, bf16[1280,128]{1,0:T(8,128)(2,1)S(1)}, u32[]{:S(2)}, u32[]{:S(2)}) collective-permute-start(bf16[1280,128]{1,0:T(8,128)(2,1)S(1)} %bitcast_add_fusion.7), channel_id=1, source_target_pairs={{0,2},{1,3},{2,0},{3,1},{4,6},{5,7},{6,4},{7,5},{8,10},{9,11},{10,... | collective-permute-start | bytes 983048 | tf_op jit(solution)/shard_map/ppermute | solution.py:34
  82.4 8.9 %collective-permute-start.32 = (bf16[640,128]{1,0:T(8,128)(2,1)S(1)}, bf16[640,128]{1,0:T(8,128)(2,1)S(1)}, u32[]{:S(2)}, u32[]{:S(2)}) collective-permute-start(bf16[640,128]{1,0:T(8,128)(2,1)S(1)} %get-tuple-element.118), channel_id=1, source_target_pairs={{0,4},{1,5},{2,6},{3,7},{4,8},{5,9},{6,10},{7,11},{8,12},{9,13},{1... | collective-permute-start | bytes 491528 | tf_op jit(solution)/shard_map/ppermute | solution.py:34
  84.3 11.2 %collective-permute-start.34 = (bf16[640,128]{1,0:T(8,128)(2,1)S(1)}, bf16[640,128]{1,0:T(8,128)(2,1)S(1)}, u32[]{:S(2)}, u32[]{:S(2)}) collective-permute-start(bf16[640,128]{1,0:T(8,128)(2,1)S(1)} %get-tuple-element.119), channel_id=1, source_target_pairs={{0,4},{1,5},{2,6},{3,7},{4,8},{5,9},{6,10},{7,11},{8,12},{9,13},{1... | collective-permute-start | bytes 491528 | tf_op jit(solution)/shard_map/ppermute | solution.py:34
  91.4 9.1 %collective-permute-start.33 = (bf16[640,128]{1,0:T(8,128)(2,1)S(1)}, bf16[640,128]{1,0:T(8,128)(2,1)S(1)}, u32[]{:S(2)}, u32[]{:S(2)}) collective-permute-start(bf16[640,128]{1,0:T(8,128)(2,1)S(1)} %fusion.12), channel_id=1, source_target_pairs={{0,4},{1,5},{2,6},{3,7},{4,8},{5,9},{6,10},{7,11},{8,12},{9,13},{1... | collective-permute-start | bytes 491528 | tf_op jit(solution)/shard_map/ppermute | solution.py:34
  91.6 15.7 %collective-permute-start.28 = (bf16[1280,128]{1,0:T(8,128)(2,1)S(1)}, bf16[1280,128]{1,0:T(8,128)(2,1)S(1)}, u32[]{:S(2)}, u32[]{:S(2)}) collective-permute-start(bf16[1280,128]{1,0:T(8,128)(2,1)S(1)} %fusion.3), channel_id=1, source_target_pairs={{0,12},{1,13},{2,14},{3,15},{4,0},{5,1},{6,2},{7,3},{8,4},{9,5},{1... | collective-permute-start | bytes 983048 | tf_op jit(solution)/shard_map/ppermute | solution.py:34
  95.4 11.8 %collective-permute-start.26 = (bf16[1280,128]{1,0:T(8,128)(2,1)S(1)}, bf16[1280,128]{1,0:T(8,128)(2,1)S(1)}, u32[]{:S(2)}, u32[]{:S(2)}) collective-permute-start(bf16[1280,128]{1,0:T(8,128)(2,1)S(1)} %add_convert_fusion), channel_id=1, source_target_pairs={{0,2},{1,3},{2,0},{3,1},{4,6},{5,7},{6,4},{7,5},{8,10},{9,11},{10,... | collective-permute-start | bytes 983048 | tf_op jit(solution)/shard_map/ppermute | solution.py:34
  95.5 11.8 %collective-permute-start.35 = (bf16[640,128]{1,0:T(8,128)(2,1)S(1)}, bf16[640,128]{1,0:T(8,128)(2,1)S(1)}, u32[]{:S(2)}, u32[]{:S(2)}) collective-permute-start(bf16[640,128]{1,0:T(8,128)(2,1)S(1)} %add_convert_fusion.1), channel_id=1, source_target_pairs={{0,4},{1,5},{2,6},{3,7},{4,8},{5,9},{6,10},{7,11},{8,12},{9,13},{1... | collective-permute-start | bytes 491528 | tf_op jit(solution)/shard_map/ppermute | solution.py:34

commit v13 on v12

--- a/solution.py
+++ b/solution.py
@@ -37,6 +37,7 @@
 ALONG = pairs_of(lambda z, x: ((z + 1) % LINE, x))
 BACK = pairs_of(lambda z, x: ((z - 1) % LINE, x))
 ACROSS = pairs_of(lambda z, x: (z, 1 - x))
+NEAR0, NEAR1, NEAR2, NEAR3, FAR0, FAR1, FAR2, FAR3 = range(2 * LINE)
 ADD_AT = {(2, 1): 0, (3, 0): 1, (3, 1): 2}
 LAY_AT = (1, 1)
 
@@ -62,10 +63,7 @@
     return [arrived(stage) for stage in range(LINE + 1)]
 
 
-def collect(far_keep, far_send, near_of, half, swap):
-    def paired(keep, send):
-        return keep + move(send, swap).astype(jnp.float32)
-
+def collect(blocks_of, swap):
     def halves(array):
         return array[: array.shape[0] // 2], array[array.shape[0] // 2 :]
 
@@ -75,24 +73,31 @@
     def wide(array):
         return array.astype(jnp.float32)
 
-    far = {step: paired(far_keep[step], far_send[step]) for step in (2, 1, 3, 0)}
-    half, far[3], far[0], aside, *crossing = tie(half, far[3], far[0], narrow(far[1]), *map(narrow, halves(far[2])))
-    crossed = {2: [move(part, ACROSS) for part in crossing]}
+    def paired(send, keep):
+        return keep + wide(move(send, swap))
+
+    first = [FAR2, FAR1, NEAR2]
+    rest = [FAR3, NEAR1, FAR0, NEAR3, NEAR0]
+    sends = blocks_of(first, False)
+    total = {name: paired(*pair) for name, *pair in zip(first, sends, blocks_of(first, True))}
+    crossing, aside = list(map(narrow, halves(total[FAR2]))), narrow(total[FAR1])
+    *crossing, aside = blocks_of.hold(*crossing, aside)
+    two_on = [move(part, ACROSS) for part in crossing]
     joining = move(aside, ALONG)
-    near_keep, near_send = near_of(half)
-    near = {step: paired(near_keep[step], near_send[step]) for step in (2, 1, 3, 0)}
-    crossing, crossed[2][1] = tie(narrow(far[3]), crossed[2][1])
-    crossed[3] = move(crossing, ACROSS)
-    crossing, crossed[3] = tie(narrow(far[0] + wide(joining)), crossed[3])
-    crossed[0] = move(crossing, ACROSS)
-
-    two_on = [move(narrow(own + wide(part)), ALONG) for own, part in zip(halves(near[2]), crossed[2])]
-    later, two_on[0] = tie(near[1], two_on[0])
+    total.update({name: paired(*pair) for name, *pair in zip(rest, blocks_of(rest, False), blocks_of(rest, True))})
+
+    crossing, two_on[1] = tie(narrow(total[FAR3]), two_on[1])
+    three_on = move(crossing, ACROSS)
+    crossing, three_on = tie(narrow(total[FAR0] + wide(joining)), three_on)
+    straight = move(crossing, ACROSS)
+    two_on = [move(narrow(own + wide(part)), ALONG) for own, part in zip(halves(total[NEAR2]), two_on)]
+    later, two_on[0] = tie(total[NEAR1], two_on[0])
     one_on = [
-        move(narrow(halves(own)[index] + wide(two_on[index])), ALONG) for index, own in enumerate((near[1], later))
+        move(narrow(halves(own)[index] + wide(two_on[index])), ALONG)
+        for index, own in enumerate((total[NEAR1], later))
     ]
-    one_back = move(narrow(near[3] + wide(crossed[3])), BACK)
-    return near[0] + wide(crossed[0]) + wide(one_back) + wide(jnp.concatenate(one_on))
+    one_back = move(narrow(total[NEAR3] + wide(three_on)), BACK)
+    return total[NEAR0] + wide(straight) + wide(one_back) + wide(jnp.concatenate(one_on))
 
 
 def clear(half):
@@ -180,19 +185,17 @@
     add_stage(stage, count, pieces, table_ref, bounds_ref, refs)
 
 
-def window_kernel(stage, count, pieces, shard, first, table_ref, bounds_ref, chips_ref, core_ref, *refs):
+def window_kernel(stage, count, pieces, shard, plan, table_ref, bounds_ref, chips_ref, core_ref, *refs):
     half, (weights, *outs) = add_stage(stage, count, pieces, table_ref, bounds_ref, refs)
     side_rows = (half.shape[0] - BLK) // 2
     for side in range(2):
         weights[pl.ds(side * LANES, LANES), :] = half[pl.ds(side * side_rows, WIN), :].T.astype(jnp.bfloat16)
-    for index, out in enumerate(outs):
-        fill_window(half, weights, shard, chips_ref, first + index * out.shape[0], 1 - core_ref[0], out)
-
-
-def rest_kernel(shard, plan, chips_ref, core_ref, half, weights, *outs):
-    for (first, keeps), out in zip(plan, outs):
-        parity = core_ref[0] if keeps else 1 - core_ref[0]
-        fill_window(half, weights, shard, chips_ref, first, parity, out)
+    rest_kernel(shard, plan, False, chips_ref, core_ref, half, weights, *outs)
+
+
+def rest_kernel(shard, plan, keeps, chips_ref, core_ref, half, weights, *outs):
+    for first, out in zip(plan, outs):
+        fill_window(half, weights, shard, chips_ref, first, core_ref[0] if keeps else 1 - core_ref[0], out)
 
 
 SMEM = pl.BlockSpec(memory_space=pltpu.SMEM)
@@ -202,6 +205,10 @@
 
 def pinned(array):
     return pltpu.with_memory_space_constraint(array, pltpu.VMEM)
+
+
+def held(array):
+    return pltpu.with_memory_space_constraint(array, pltpu.HBM)
 
 
 def call(kernel, ins, in_specs, outs, scratch, aliases, flops, scoped=0):
@@ -287,7 +294,8 @@
             aliases = {len(ins) + 1: 0}
             ins, specs = ins + [pinned(state[1]), pinned(state[0])], specs + [VMEM] * 2
         else:
-            ins, specs, made = ins + tile_sets, specs + [HBM] * 2, [half_type, tiles_type]
+            ins, specs = [*tables, *map(held, sources), *map(held, tile_sets)], specs + [HBM] * 2
+            made = [half_type, tiles_type]
         results = call(kernel, ins, specs, made + outs, scratch, aliases, flops, 2 * rows * LANES)
         state[:] = [results[0], state[1] if state else results[1]]
         return results[len(made) :]
@@ -312,44 +320,46 @@
     else:
         stages = [[lax.all_gather(part, "aux", axis_index_groups=same_core, axis=0, tiled=True) for part in parts]]
 
-    group = 1 if lined else chips // 2
-    far = [group] * (chips // 2 // group)
-    weights, *far_send = run_stage(
-        functools.partial(window_kernel, stage_count - 1, len(stages[-1]), pieces, shard, chips // 2),
-        stages[-1],
-        [ordered, bounds, chip_of_slot, cores],
-        [pltpu.VMEM((2 * LANES, WIN), jnp.bfloat16)]
-        + [pltpu.VMEM((size, shard, WIN), jnp.bfloat16) for size in far],
-        work + total // 4 * width * WIN * 2,
-    )
-    half = state[0]
-
-    def rest(plan, half):
-        return call(
-            functools.partial(rest_kernel, shard, plan),
-            [chip_of_slot, cores, pinned(half), pinned(weights)],
-            [SMEM] * 2 + [VMEM] * 2,
-            [pltpu.VMEM((group, shard, WIN), jnp.float32 if keeps else jnp.bfloat16) for _, keeps in plan],
-            [],
-            {},
-            total // 4 * width * WIN * 2,
+    group = 1 if lined else chips
+
+    def window_types(plan, keeps):
+        return [pltpu.VMEM((group, shard, WIN), jnp.float32 if keeps else jnp.bfloat16) for _ in plan]
+
+    def first_sends(plan):
+        weights, *blocks = run_stage(
+            functools.partial(window_kernel, stage_count - 1, len(stages[-1]), pieces, shard, plan),
+            stages[-1],
+            [ordered, bounds, chip_of_slot, cores],
+            [pltpu.VMEM((2 * LANES, WIN), jnp.bfloat16)] + window_types(plan, False),
+            work + len(plan) * group * shard * width * WIN * 2,
         )
-
-    def near_of(half):
-        blocks = rest([(index * group, keeps) for keeps in (True, False) for index in range(len(far))], half)
-        if lined:
-            blocks = [block[0] for block in blocks]
-        return blocks[: len(far)], blocks[len(far) :]
-
-    far_keep = rest([(chips // 2 + index * group, True) for index in range(len(far))], half)
-
+        state.append(weights)
+        return blocks
+
+    def blocks_of(plan, keeps):
+        if len(state) < 3:
+            blocks = first_sends(plan)
+        else:
+            blocks = call(
+                functools.partial(rest_kernel, shard, plan, keeps),
+                [chip_of_slot, cores, pinned(state[0]), pinned(state[2])],
+                [SMEM] * 2 + [VMEM] * 2,
+                window_types(plan, keeps),
+                [],
+                {},
+                len(plan) * group * shard * width * WIN * 2,
+            )
+        return [block[0] for block in blocks] if lined else blocks
+
+    def hold(*arrays):
+        state[0], *arrays = tie(state[0], *arrays)
+        return arrays
+
+    blocks_of.hold = hold
     factor = 1.0 / math.sqrt(owners * width)
     if lined:
-        far_keep, far_send = [block[0] for block in far_keep], [block[0] for block in far_send]
-        return collect(far_keep, far_send, near_of, half, swap) * factor
-    near_keep, near_send = near_of(half)
-    keep, send = [*near_keep, *far_keep], [*near_send, *far_send]
-    keep, send = jnp.concatenate(keep), jnp.concatenate(send)
+        return collect(blocks_of, swap) * factor
+    (send,), (keep,) = blocks_of([0], False), blocks_of([0], True)
     pair_sum = (keep + move(send, swap).astype(jnp.float32)).astype(jnp.bfloat16)
     block_sum = lax.psum_scatter(
         pair_sum.reshape(total // 2, WIN), "aux", axis_index_groups=same_core, scatter_dimension=0, tiled=True

time: 108 us -> 109 us (level)
  waiting for transfers between devices: 41.3 us -> 51.5 us
  Pallas kernels: 20.4 us -> 16.6 us
  starting transfers between devices: 30 us -> 26.8 us
  local copies, waits for them, and re-layouts: 11.4 us -> 8.77 us
    ppermute x36, waiting for transfers between devices: 41.3 us -> 51.5 us  [move(): return lax.ppermute(array, 'aux', pairs)]
    pallas_call x7 -> x8, Pallas kernels: 20.4 us -> 16.6 us  [call(): pl.pallas_call(kernel, out_shape=outs, in_specs=in_specs, out_specs=[VMEM...]
    ppermute x36, starting transfers between devices: 30 us -> 26.8 us  [move(): return lax.ppermute(array, 'aux', pairs)]
    unnamed x13 -> x7, local copies, waits for them, and re-layouts: 10.2 us -> 7.55 us
  transfers between devices with their start and end apart: 36 -> 36, of which waited for: 14 -> 16; matrix products, arithmetic and copies ran while one was open for 10% -> 11% of each run, Pallas kernels for 14% -> 13%
where the time goes in v13:
time: 109 us
  waiting for transfers between devices  51.5 us (47%)
  starting transfers between devices  26.8 us (25%)
  Pallas kernels  16.6 us (15%)
  local copies, waits for them, and re-layouts  8.77 us (8%)
  other arithmetic  4.13 us (4%)
    ppermute x36, waiting for transfers between devices, move(): return lax.ppermute(array, 'aux', pairs)  51.5 us
    ppermute x36, starting transfers between devices, move(): return lax.ppermute(array, 'aux', pairs)  26.8 us
    pallas_call x8, Pallas kernels, call(): pl.pallas_call(kernel, out_shape=outs, in_specs=in_specs, out_specs=[VMEM...  16.6 us
    unnamed x7, local copies, waits for them, and re-layouts  7.55 us
  transfers between devices with their start and end apart: 36, of which 16 were waited for; matrix products, arithmetic and copies ran while one was open for 11% of the time, Pallas kernels for 13%

profile of v13, /device:TPU:0, one launch (start us, length us, event | category | flops | bytes accessed | tf_op | source)
XLA Modules:
  0.0 108.8 jit_solution(3552348770089595690)
XLA Ops:
  0.0 0.5 collective-permute-start.11
  0.5 1.1 %constant_dynamic-slice_fusion.1 = (bf16[1280,128]{1,0:T(8,128)(2,1)S(1)}, bf16[1280,128]{1,0:T(8,128)(2,1)S(1)}) fusion(bf16[1280,256]{1,0:T(8,128)(2,1)} %param.7, s32[]{:T(128)S(6)} %select_n.162, s32[]{:T(128)S(6)} %select_n.161), kind=kLoop, calls=%fused_computation.93 | loop fusion | bytes 1310728 | tf_op jit(solution)/shard_map/dynamic_slice | solution.py:242
  1.6 2.6 %collective-permute-start.2 = (bf16[1280,128]{1,0:T(8,128)(2,1)S(1)}, bf16[1280,128]{1,0:T(8,128)(2,1)S(1)}, u32[]{:S(2)}, u32[]{:S(2)}) collective-permute-start(bf16[1280,128]{1,0:T(8,128)(2,1)S(1)} %get-tuple-element.117.refs_0_), channel_id=1, source_target_pairs={{0,4},{1,5},{2,6},{3,7},{4,8},{5,9},{6,10},{7,11},{8,12},{9,13},{1... | collective-permute-start | bytes 983048 | tf_op jit(solution)/shard_map/ppermute | solution.py:34
  4.2 1.5 %collective-permute-start.3 = (bf16[1280,128]{1,0:T(8,128)(2,1)S(1)}, bf16[1280,128]{1,0:T(8,128)(2,1)S(1)}, u32[]{:S(2)}, u32[]{:S(2)}) collective-permute-start(bf16[1280,128]{1,0:T(8,128)(2,1)S(1)} %get-tuple-element.117.refs_0_), channel_id=1, source_target_pairs={{0,2},{1,3},{2,0},{3,1},{4,6},{5,7},{6,4},{7,5},{8,10},{9,11},{10,... | collective-permute-start | bytes 983048 | tf_op jit(solution)/shard_map/ppermute | solution.py:34
  5.7 0.5 collective-permute-start
  6.2 0.7 constant_dynamic-update-slice_fusion.1
  7.5 3.4 %copy.9 = bf16[32,8,32,128]{3,2,1,0:T(8,128)(2,1)} copy(bf16[32,8,32,128]{3,1,2,0:T(8,128)(2,1)} %bitcast.69) | data formatting | bytes 4194304
  11.0 0.7 compare_select_fusion.3
  11.7 0.9 collective-permute-done.8.refs_1_
  12.6 0.5 collective-permute-start.10
  13.1 1.6 %collective-permute-start.9 = (bf16[1280,128]{1,0:T(8,128)(2,1)S(1)}, bf16[1280,128]{1,0:T(8,128)(2,1)S(1)}, u32[]{:S(2)}, u32[]{:S(2)}) collective-permute-start(bf16[1280,128]{1,0:T(8,128)(2,1)S(1)} %collective-permute-done.8.refs_1_), channel_id=1, source_target_pairs={{0,4},{1,5},{2,6},{3,7},{4,8},{5,9},{6,10},{7,11},{8,12},{9,13},{1... | collective-permute-start | bytes 983048 | tf_op jit(solution)/shard_map/ppermute | solution.py:34
  14.7 0.6 fusion.30
  15.4 1.6 %collective-permute-start.4 = (bf16[1280,128]{1,0:T(8,128)(2,1)S(1)}, bf16[1280,128]{1,0:T(8,128)(2,1)S(1)}, u32[]{:S(2)}, u32[]{:S(2)}) collective-permute-start(bf16[1280,128]{1,0:T(8,128)(2,1)S(1)} %collective-permute-done.2.refs_0_), channel_id=1, source_target_pairs={{0,4},{1,5},{2,6},{3,7},{4,8},{5,9},{6,10},{7,11},{8,12},{9,13},{1... | collective-permute-start | bytes 983048 | tf_op jit(solution)/shard_map/ppermute | solution.py:34
  17.0 1.5 %collective-permute-start.5 = (bf16[1280,128]{1,0:T(8,128)(2,1)S(1)}, bf16[1280,128]{1,0:T(8,128)(2,1)S(1)}, u32[]{:S(2)}, u32[]{:S(2)}) collective-permute-start(bf16[1280,128]{1,0:T(8,128)(2,1)S(1)} %collective-permute-done.2.refs_0_), channel_id=1, source_target_pairs={{0,2},{1,3},{2,0},{3,1},{4,6},{5,7},{6,4},{7,5},{8,10},{9,11},{10,... | collective-permute-start | bytes 983048 | tf_op jit(solution)/shard_map/ppermute | solution.py:34
  18.5 4.7 %collective-permute-done.10.refs_3_ = bf16[1280,128]{1,0:T(8,128)(2,1)S(1)} collective-permute-done((bf16[1280,128]{1,0:T(8,128)(2,1)S(1)}, bf16[1280,128]{1,0:T(8,128)(2,1)S(1)}, u32[]{:S(2)}, u32[]{:S(2)}) %collective-permute-start.10) | collective-permute-done | bytes 327712 | tf_op jit(solution)/shard_map/ppermute | solution.py:34
  23.1 2.4 %collective-permute-done.9.refs_1_ = bf16[1280,128]{1,0:T(8,128)(2,1)S(1)} collective-permute-done((bf16[1280,128]{1,0:T(8,128)(2,1)S(1)}, bf16[1280,128]{1,0:T(8,128)(2,1)S(1)}, u32[]{:S(2)}, u32[]{:S(2)}) %collective-permute-start.9) | collective-permute-done | bytes 327712 | tf_op jit(solution)/shard_map/ppermute | solution.py:34
  25.5 3.4 %copy.10 = bf16[32,8,32,128]{3,2,1,0:T(8,128)(2,1)} copy(bf16[32,8,32,128]{3,1,2,0:T(8,128)(2,1)} %bitcast.25) | data formatting | bytes 4194304
  29.0 1.5 %collective-permute-start.13 = (bf16[1280,128]{1,0:T(8,128)(2,1)S(1)}, bf16[1280,128]{1,0:T(8,128)(2,1)S(1)}, u32[]{:S(2)}, u32[]{:S(2)}) collective-permute-start(bf16[1280,128]{1,0:T(8,128)(2,1)S(1)} %collective-permute-done.9.refs_1_), channel_id=1, source_target_pairs={{0,2},{1,3},{2,0},{3,1},{4,6},{5,7},{6,4},{7,5},{8,10},{9,11},{10,... | collective-permute-start | bytes 983048 | tf_op jit(solution)/shard_map/ppermute | solution.py:34
  30.5 0.3 convert_reduce_fusion
  30.8 0.5 select_reduce_fusion
  31.3 0.2 collective-permute-done.4.refs_0_
  31.5 1.2 %collective-permute-start.6 = (bf16[1280,128]{1,0:T(8,128)(2,1)S(1)}, bf16[1280,128]{1,0:T(8,128)(2,1)S(1)}, u32[]{:S(2)}, u32[]{:S(2)}) collective-permute-start(bf16[1280,128]{1,0:T(8,128)(2,1)S(1)} %collective-permute-done.4.refs_0_), channel_id=1, source_target_pairs={{0,4},{1,5},{2,6},{3,7},{4,8},{5,9},{6,10},{7,11},{8,12},{9,13},{1... | collective-permute-start | bytes 983048 | tf_op jit(solution)/shard_map/ppermute | solution.py:34
  32.7 1.1 collective-permute-start.7
  33.8 0.1 convert_reduce_fusion.1.bounds_ref
  33.9 0.1 concatenate.10.table_ref
  34.0 4.2 %shard_map.46 = (f32[41024,128]{1,0:T(8,128)S(1)}, bf16[512,32,128]{2,1,0:T(8,128)(2,1)S(1)}) custom-call(s32[1584]{0:T(1024)S(1)} %concatenate.10.table_ref, s32[6]{0:T(128)S(1)} %convert_reduce_fusion.1.bounds_ref, bf16[1280,128]{1,0:T(8,128)(2,1)} %copy-done, bf16[1280,128]{1,0:T(8,128)(2,1)} %copy-done.1, bf16[256,32,128]{2,1,0:T(8,128)(2,1)} %bitcast.67, ...), custom_call_target="tpu_custom_call" | custom-call | flops 107374184 | bytes 4194304 | tf_op jit(solution)/shard_map/pallas_call | solution.py:215
  38.3 3.2 %collective-permute-done.12.refs_1_ = bf16[1280,128]{1,0:T(8,128)(2,1)S(1)} collective-permute-done((bf16[1280,128]{1,0:T(8,128)(2,1)S(1)}, bf16[1280,128]{1,0:T(8,128)(2,1)S(1)}, u32[]{:S(2)}, u32[]{:S(2)}) %collective-permute-start.12) | collective-permute-done | bytes 327712 | tf_op jit(solution)/shard_map/ppermute | solution.py:34
  41.4 1.5 %collective-permute-start.16 = (bf16[1280,128]{1,0:T(8,128)(2,1)S(1)}, bf16[1280,128]{1,0:T(8,128)(2,1)S(1)}, u32[]{:S(2)}, u32[]{:S(2)}) collective-permute-start(bf16[1280,128]{1,0:T(8,128)(2,1)S(1)} %collective-permute-done.12.refs_1_), channel_id=1, source_target_pairs={{0,2},{1,3},{2,0},{3,1},{4,6},{5,7},{6,4},{7,5},{8,10},{9,11},{10,... | collective-permute-start | bytes 983048 | tf_op jit(solution)/shard_map/ppermute | solution.py:34
  42.9 5.5 %collective-permute-done.6.refs_0_ = bf16[1280,128]{1,0:T(8,128)(2,1)S(1)} collective-permute-done((bf16[1280,128]{1,0:T(8,128)(2,1)S(1)}, bf16[1280,128]{1,0:T(8,128)(2,1)S(1)}, u32[]{:S(2)}, u32[]{:S(2)}) %collective-permute-start.6) | collective-permute-done | bytes 327712 | tf_op jit(solution)/shard_map/ppermute | solution.py:34
  48.4 1.9 %shard_map.47.refs_5_ = f32[41024,128]{1,0:T(8,128)S(1)} custom-call(s32[1584]{0:T(1024)S(1)} %concatenate.10.table_ref, s32[6]{0:T(128)S(1)} %convert_reduce_fusion.1.bounds_ref, bf16[1280,128]{1,0:T(8,128)(2,1)S(1)} %collective-permute-done.2.refs_0_, bf16[1280,128]{1,0:T(8,128)(2,1)S(1)} %collective-permute-done.9.refs_1_, ...), custom_call_target="tpu_custom_call", output_to_operand_aliasing={{}: (7, {})} | custom-call | flops 107374184 | bytes 4194304 | tf_op jit(solution)/shard_map/pallas_call | solution.py:215
  50.4 0.2 collective-permute-start.14
  50.6 1.9 %shard_map.48.refs_5_ = f32[41024,128]{1,0:T(8,128)S(1)} custom-call(s32[1584]{0:T(1024)S(1)} %concatenate.10.table_ref, s32[6]{0:T(128)S(1)} %convert_reduce_fusion.1.bounds_ref, bf16[1280,128]{1,0:T(8,128)(2,1)S(1)} %collective-permute-done.4.refs_0_, bf16[1280,128]{1,0:T(8,128)(2,1)S(1)} %collective-permute-done.12.refs_1_, ...), custom_call_target="tpu_custom_call", output_to_operand_aliasing={{}: (7, {})} | custom-call | flops 107374184 | bytes 4194304 | tf_op jit(solution)/shard_map/pallas_call | solution.py:215
  52.5 3.0 %collective-permute-done.15.refs_1_ = bf16[1280,128]{1,0:T(8,128)(2,1)S(1)} collective-permute-done((bf16[1280,128]{1,0:T(8,128)(2,1)S(1)}, bf16[1280,128]{1,0:T(8,128)(2,1)S(1)}, u32[]{:S(2)}, u32[]{:S(2)}) %collective-permute-start.15) | collective-permute-done | bytes 327712 | tf_op jit(solution)/shard_map/ppermute | solution.py:34
  55.5 1.1 collective-permute-start.17
  56.6 1.9 %shard_map.49.refs_3_ = f32[41024,128]{1,0:T(8,128)S(1)} custom-call(s32[1584]{0:T(1024)S(1)} %concatenate.10.table_ref, s32[6]{0:T(128)S(1)} %convert_reduce_fusion.1.bounds_ref, bf16[1280,128]{1,0:T(8,128)(2,1)S(1)} %collective-permute-done.6.refs_0_, bf16[1280,128]{1,0:T(8,128)(2,1)S(1)} %collective-permute-done.15.refs_1_, ...), custom_call_target="tpu_custom_call", output_to_operand_aliasing={{}: (7, {})} | custom-call | flops 107374184 | bytes 4194304 | tf_op jit(solution)/shard_map/pallas_call | solution.py:215
  58.5 1.0 collective-permute-done.14.refs_0_
  59.5 3.0 %collective-permute-done.17.refs_1_ = bf16[1280,128]{1,0:T(8,128)(2,1)S(1)} collective-permute-done((bf16[1280,128]{1,0:T(8,128)(2,1)S(1)}, bf16[1280,128]{1,0:T(8,128)(2,1)S(1)}, u32[]{:S(2)}, u32[]{:S(2)}) %collective-permute-start.17) | collective-permute-done | bytes 327712 | tf_op jit(solution)/shard_map/ppermute | solution.py:34
  62.5 2.2 %shard_map.50 = (f32[41024,128]{1,0:T(8,128)S(1)}, bf16[256,128]{1,0:T(8,128)(2,1)S(1)}, bf16[1,1280,128]{2,1,0:T(8,128)(2,1)S(1)}, bf16[1,1280,128]{2,1,0:T(8,128)(2,1)S(1)}, bf16[1,1280,128]{2,1,0:T(8,128)(2,1)S(1)}) custom-call(s32[1584]{0:T(1024)S(1)} %concatenate.10.table_ref, ...), custom_call_target="tpu_custom_call", output_to_operand_aliasing={{0}: (7, {})} | custom-call | flops 359032416 | bytes 4194304 | tf_op jit(solution)/shard_map/pallas_call | solution.py:215
  64.9 0.5 collective-permute-start.19
  65.4 0.1 collective-permute-start.30
  65.5 1.2 %shard_map.51 = (f32[1,1280,128]{2,1,0:T(8,128)S(1)}, f32[1,1280,128]{2,1,0:T(8,128)S(1)}, f32[1,1280,128]{2,1,0:T(8,128)S(1)}) custom-call(s32[8]{0:T(128)S(1)} %fusion.33.chips_ref, s32[1]{0:T(128)} %bitcast.core_ref, f32[41024,128]{1,0:T(8,128)S(1)} %get-tuple-element.85.half, bf16[256,128]{1,0:T(8,128)(2,1)S(1)} %get-tuple-element.80.weights), custom_call_target="tpu_custom_call" | custom-call | flops 251658240 | bytes 4194304 | tf_op jit(solution)/shard_map/pallas_call | solution.py:215
  66.7 0.3 collective-permute-done.19
  67.0 0.1 fusion.11
  67.1 1.6 %shard_map.53 = (bf16[1,1280,128]{2,1,0:T(8,128)(2,1)S(1)}, bf16[1,1280,128]{2,1,0:T(8,128)(2,1)S(1)}, bf16[1,1280,128]{2,1,0:T(8,128)(2,1)S(1)}, bf16[1,1280,12...) custom-call(s32[8]{0:T(128)S(1)} %fusion.33.chips_ref, s32[1]{0:T(128)} %bitcast.core_ref, ...), custom_call_target="tpu_custom_call" | custom-call | flops 419430400 | bytes 4194304 | tf_op jit(solution)/shard_map/pallas_call | solution.py:215
  68.7 0.2 collective-permute-start.29
  68.9 0.3 collective-permute-start.23
  69.3 1.4 %collective-permute-start.24 = (bf16[640,128]{1,0:T(8,128)(2,1)S(1)}, bf16[640,128]{1,0:T(8,128)(2,1)S(1)}, u32[]{:S(2)}, u32[]{:S(2)}) collective-permute-start(bf16[640,128]{1,0:T(8,128)(2,1)S(1)} %get-tuple-element.93), channel_id=1, source_target_pairs={{0,2},{1,3},{2,0},{3,1},{4,6},{5,7},{6,4},{7,5},{8,10},{9,11},{10,... | collective-permute-start | bytes 491528 | tf_op jit(solution)/shard_map/ppermute | solution.py:34
  70.6 0.6 collective-permute-start.31
  71.3 1.5 %shard_map.52 = (f32[1,1280,128]{2,1,0:T(8,128)S(1)}, f32[1,1280,128]{2,1,0:T(8,128)S(1)}, f32[1,1280,128]{2,1,0:T(8,128)S(1)}, f32[1,1280,128]{2,1,0:T(8,128)S(1)}, f32[1,1280,128]{2,1,0:T(8,128)S(1)}) custom-call(s32[8]{0:T(128)S(1)} %fusion.33.chips_ref, s32[1]{0:T(128)} %bitcast.core_ref, f32[41024,128]{1,0:T(8,128)S(1)} %get-tuple-element.85.half, ...), custom_call_target="tpu_custom_call" | custom-call | flops 419430400 | bytes 4194304 | tf_op jit(solution)/shard_map/pallas_call | solution.py:215
  72.9 0.1 bitcast_add_fusion
  73.2 3.1 %collective-permute-done.24 = bf16[640,128]{1,0:T(8,128)(2,1)S(1)} collective-permute-done((bf16[640,128]{1,0:T(8,128)(2,1)S(1)}, bf16[640,128]{1,0:T(8,128)(2,1)S(1)}, u32[]{:S(2)}, u32[]{:S(2)}) %collective-permute-start.24) | collective-permute-done | bytes 163872 | tf_op jit(solution)/shard_map/ppermute | solution.py:34
  76.3 2.7 %collective-permute-done.31 = bf16[640,128]{1,0:T(8,128)(2,1)S(1)} collective-permute-done((bf16[640,128]{1,0:T(8,128)(2,1)S(1)}, bf16[640,128]{1,0:T(8,128)(2,1)S(1)}, u32[]{:S(2)}, u32[]{:S(2)}) %collective-permute-start.31) | collective-permute-done | bytes 163872 | tf_op jit(solution)/shard_map/ppermute | solution.py:34
  79.0 0.1 fusion.14
  79.2 6.2 %collective-permute-done.22 = bf16[1280,128]{1,0:T(8,128)(2,1)S(1)} collective-permute-done((bf16[1280,128]{1,0:T(8,128)(2,1)S(1)}, bf16[1280,128]{1,0:T(8,128)(2,1)S(1)}, u32[]{:S(2)}, u32[]{:S(2)}) %collective-permute-start.22) | collective-permute-done | bytes 327712 | tf_op jit(solution)/shard_map/ppermute | solution.py:34
  85.4 0.1 fusion.6
  85.5 1.4 %collective-permute-start.25 = (bf16[1280,128]{1,0:T(8,128)(2,1)S(1)}, bf16[1280,128]{1,0:T(8,128)(2,1)S(1)}, u32[]{:S(2)}, u32[]{:S(2)}) collective-permute-start(bf16[1280,128]{1,0:T(8,128)(2,1)S(1)} %fusion.4), channel_id=1, source_target_pairs={{0,2},{1,3},{2,0},{3,1},{4,6},{5,7},{6,4},{7,5},{8,10},{9,11},{10,... | collective-permute-start | bytes 983048 | tf_op jit(solution)/shard_map/ppermute | solution.py:34
  87.0 0.1 bitcast_add_fusion.1
  87.0 1.5 %collective-permute-done.32 = bf16[640,128]{1,0:T(8,128)(2,1)S(1)} collective-permute-done((bf16[640,128]{1,0:T(8,128)(2,1)S(1)}, bf16[640,128]{1,0:T(8,128)(2,1)S(1)}, u32[]{:S(2)}, u32[]{:S(2)}) %collective-permute-start.32) | collective-permute-done | bytes 163872 | tf_op jit(solution)/shard_map/ppermute | solution.py:34
  88.6 5.9 %collective-permute-done.25 = bf16[1280,128]{1,0:T(8,128)(2,1)S(1)} collective-permute-done((bf16[1280,128]{1,0:T(8,128)(2,1)S(1)}, bf16[1280,128]{1,0:T(8,128)(2,1)S(1)}, u32[]{:S(2)}, u32[]{:S(2)}) %collective-permute-start.25) | collective-permute-done | bytes 327712 | tf_op jit(solution)/shard_map/ppermute | solution.py:34
  94.5 0.1 fusion.3
  94.6 3.6 %collective-permute-start.28 = (bf16[1280,128]{1,0:T(8,128)(2,1)S(1)}, bf16[1280,128]{1,0:T(8,128)(2,1)S(1)}, u32[]{:S(2)}, u32[]{:S(2)}) collective-permute-start(bf16[1280,128]{1,0:T(8,128)(2,1)S(1)} %fusion.3), channel_id=1, source_target_pairs={{0,12},{1,13},{2,14},{3,15},{4,0},{5,1},{6,2},{7,3},{8,4},{9,5},{1... | collective-permute-start | bytes 983048 | tf_op jit(solution)/shard_map/ppermute | solution.py:34
  98.2 1.4 %collective-permute-start.26 = (bf16[1280,128]{1,0:T(8,128)(2,1)S(1)}, bf16[1280,128]{1,0:T(8,128)(2,1)S(1)}, u32[]{:S(2)}, u32[]{:S(2)}) collective-permute-start(bf16[1280,128]{1,0:T(8,128)(2,1)S(1)} %fusion.6), channel_id=1, source_target_pairs={{0,2},{1,3},{2,0},{3,1},{4,6},{5,7},{6,4},{7,5},{8,10},{9,11},{10,... | collective-permute-start | bytes 983048 | tf_op jit(solution)/shard_map/ppermute | solution.py:34
  99.7 8.0 %collective-permute-done.35 = bf16[640,128]{1,0:T(8,128)(2,1)S(1)} collective-permute-done((bf16[640,128]{1,0:T(8,128)(2,1)S(1)}, bf16[640,128]{1,0:T(8,128)(2,1)S(1)}, u32[]{:S(2)}, u32[]{:S(2)}) %collective-permute-start.35) | collective-permute-done | bytes 163872 | tf_op jit(solution)/shard_map/ppermute | solution.py:34
  107.7 1.0 fusion.10
  (45 shorter events, 0.7 us)
Async XLA Ops:
  0.0 25.5 %collective-permute-start.11 = (bf16[256,4096]{1,0:T(8,128)(2,1)}, bf16[256,4096]{1,0:T(8,128)(2,1)}, u32[]{:S(2)}, u32[]{:S(2)}) collective-permute-start(bf16[256,4096]{1,0:T(8,128)(2,1)} %param.4), channel_id=1, source_target_pairs={{0,1},{1,0},{2,3},{3,2},{4,5},{5,4},{6,7},{7,6},{8,9},{9,8},{10,11... | collective-permute-start | bytes 6291464 | tf_op jit(solution)/shard_map/ppermute | solution.py:34
  1.6 9.4 %copy-start = (bf16[1280,128]{1,0:T(8,128)(2,1)}, bf16[1280,128]{1,0:T(8,128)(2,1)S(1)}, u32[]{:S(2)}) copy-start(bf16[1280,128]{1,0:T(8,128)(2,1)S(1)} %get-tuple-element.117.refs_0_) | copy-start | bytes 983044
  1.6 13.8 %collective-permute-start.2 = (bf16[1280,128]{1,0:T(8,128)(2,1)S(1)}, bf16[1280,128]{1,0:T(8,128)(2,1)S(1)}, u32[]{:S(2)}, u32[]{:S(2)}) collective-permute-start(bf16[1280,128]{1,0:T(8,128)(2,1)S(1)} %get-tuple-element.117.refs_0_), channel_id=1, source_target_pairs={{0,4},{1,5},{2,6},{3,7},{4,8},{5,9},{6,10},{7,11},{8,12},{9,13},{1... | collective-permute-start | bytes 983048 | tf_op jit(solution)/shard_map/ppermute | solution.py:34
  4.2 11.2 %collective-permute-start.3 = (bf16[1280,128]{1,0:T(8,128)(2,1)S(1)}, bf16[1280,128]{1,0:T(8,128)(2,1)S(1)}, u32[]{:S(2)}, u32[]{:S(2)}) collective-permute-start(bf16[1280,128]{1,0:T(8,128)(2,1)S(1)} %get-tuple-element.117.refs_0_), channel_id=1, source_target_pairs={{0,2},{1,3},{2,0},{3,1},{4,6},{5,7},{6,4},{7,5},{8,10},{9,11},{10,... | collective-permute-start | bytes 983048 | tf_op jit(solution)/shard_map/ppermute | solution.py:34
  5.7 5.3 %collective-permute-start.1 = (s32[256,2]{0,1:T(2,128)}, s32[256,2]{0,1:T(2,128)S(1)}, u32[]{:S(2)}, u32[]{:S(2)}) collective-permute-start(s32[256,2]{0,1:T(2,128)} %param.5), channel_id=1, source_target_pairs={{0,1},{1,0},{2,3},{3,2},{4,5},{5,4},{6,7},{7,6},{8,9},{9,8},{10,11... | collective-permute-start | bytes 6152 | tf_op jit(solution)/shard_map/ppermute | solution.py:34
  5.7 5.3 %collective-permute-start = (s32[1]{0:T(128)}, s32[1]{0:T(128)}, u32[]{:S(2)}, u32[]{:S(2)}) collective-permute-start(s32[1]{0:T(128)} %param.6), channel_id=1, source_target_pairs={{0,1},{1,0},{2,3},{3,2},{4,5},{5,4},{6,7},{7,6},{8,9},{9,8},{10,11... | collective-permute-start | bytes 20 | tf_op jit(solution)/shard_map/ppermute | solution.py:34
  11.0 1.6 %collective-permute-start.8 = (bf16[1280,128]{1,0:T(8,128)(2,1)S(1)}, bf16[1280,128]{1,0:T(8,128)(2,1)S(1)}, u32[]{:S(2)}, u32[]{:S(2)}) collective-permute-start(bf16[1280,128]{1,0:T(8,128)(2,1)S(1)} %get-tuple-element.116), channel_id=1, source_target_pairs={{0,1},{1,0},{2,3},{3,2},{4,5},{5,4},{6,7},{7,6},{8,9},{9,8},{10,11... | collective-permute-start | bytes 983048 | tf_op jit(solution)/shard_map/ppermute | solution.py:34
  12.6 12.9 %copy-start.1 = (bf16[1280,128]{1,0:T(8,128)(2,1)}, bf16[1280,128]{1,0:T(8,128)(2,1)S(1)}, u32[]{:S(2)}) copy-start(bf16[1280,128]{1,0:T(8,128)(2,1)S(1)} %collective-permute-done.8.refs_1_) | copy-start | bytes 983044
  12.6 10.6 %collective-permute-start.10 = (bf16[1280,128]{1,0:T(8,128)(2,1)S(1)}, bf16[1280,128]{1,0:T(8,128)(2,1)S(1)}, u32[]{:S(2)}, u32[]{:S(2)}) collective-permute-start(bf16[1280,128]{1,0:T(8,128)(2,1)S(1)} %collective-permute-done.8.refs_1_), channel_id=1, source_target_pairs={{0,2},{1,3},{2,0},{3,1},{4,6},{5,7},{6,4},{7,5},{8,10},{9,11},{10,... | collective-permute-start | bytes 983048 | tf_op jit(solution)/shard_map/ppermute | solution.py:34
  13.1 12.4 %collective-permute-start.9 = (bf16[1280,128]{1,0:T(8,128)(2,1)S(1)}, bf16[1280,128]{1,0:T(8,128)(2,1)S(1)}, u32[]{:S(2)}, u32[]{:S(2)}) collective-permute-start(bf16[1280,128]{1,0:T(8,128)(2,1)S(1)} %collective-permute-done.8.refs_1_), channel_id=1, source_target_pairs={{0,4},{1,5},{2,6},{3,7},{4,8},{5,9},{6,10},{7,11},{8,12},{9,13},{1... | collective-permute-start | bytes 983048 | tf_op jit(solution)/shard_map/ppermute | solution.py:34
  15.4 16.2 %collective-permute-start.4 = (bf16[1280,128]{1,0:T(8,128)(2,1)S(1)}, bf16[1280,128]{1,0:T(8,128)(2,1)S(1)}, u32[]{:S(2)}, u32[]{:S(2)}) collective-permute-start(bf16[1280,128]{1,0:T(8,128)(2,1)S(1)} %collective-permute-done.2.refs_0_), channel_id=1, source_target_pairs={{0,4},{1,5},{2,6},{3,7},{4,8},{5,9},{6,10},{7,11},{8,12},{9,13},{1... | collective-permute-start | bytes 983048 | tf_op jit(solution)/shard_map/ppermute | solution.py:34
  17.0 14.5 %collective-permute-start.5 = (bf16[1280,128]{1,0:T(8,128)(2,1)S(1)}, bf16[1280,128]{1,0:T(8,128)(2,1)S(1)}, u32[]{:S(2)}, u32[]{:S(2)}) collective-permute-start(bf16[1280,128]{1,0:T(8,128)(2,1)S(1)} %collective-permute-done.2.refs_0_), channel_id=1, source_target_pairs={{0,2},{1,3},{2,0},{3,1},{4,6},{5,7},{6,4},{7,5},{8,10},{9,11},{10,... | collective-permute-start | bytes 983048 | tf_op jit(solution)/shard_map/ppermute | solution.py:34
  29.0 12.4 %collective-permute-start.12 = (bf16[1280,128]{1,0:T(8,128)(2,1)S(1)}, bf16[1280,128]{1,0:T(8,128)(2,1)S(1)}, u32[]{:S(2)}, u32[]{:S(2)}) collective-permute-start(bf16[1280,128]{1,0:T(8,128)(2,1)S(1)} %collective-permute-done.9.refs_1_), channel_id=1, source_target_pairs={{0,4},{1,5},{2,6},{3,7},{4,8},{5,9},{6,10},{7,11},{8,12},{9,13},{1... | collective-permute-start | bytes 983048 | tf_op jit(solution)/shard_map/ppermute | solution.py:34
  29.0 12.4 %collective-permute-start.13 = (bf16[1280,128]{1,0:T(8,128)(2,1)S(1)}, bf16[1280,128]{1,0:T(8,128)(2,1)S(1)}, u32[]{:S(2)}, u32[]{:S(2)}) collective-permute-start(bf16[1280,128]{1,0:T(8,128)(2,1)S(1)} %collective-permute-done.9.refs_1_), channel_id=1, source_target_pairs={{0,2},{1,3},{2,0},{3,1},{4,6},{5,7},{6,4},{7,5},{8,10},{9,11},{10,... | collective-permute-start | bytes 983048 | tf_op jit(solution)/shard_map/ppermute | solution.py:34
  31.5 16.9 %collective-permute-start.6 = (bf16[1280,128]{1,0:T(8,128)(2,1)S(1)}, bf16[1280,128]{1,0:T(8,128)(2,1)S(1)}, u32[]{:S(2)}, u32[]{:S(2)}) collective-permute-start(bf16[1280,128]{1,0:T(8,128)(2,1)S(1)} %collective-permute-done.4.refs_0_), channel_id=1, source_target_pairs={{0,4},{1,5},{2,6},{3,7},{4,8},{5,9},{6,10},{7,11},{8,12},{9,13},{1... | collective-permute-start | bytes 983048 | tf_op jit(solution)/shard_map/ppermute | solution.py:34
  32.7 15.7 %collective-permute-start.7 = (bf16[1280,128]{1,0:T(8,128)(2,1)S(1)}, bf16[1280,128]{1,0:T(8,128)(2,1)S(1)}, u32[]{:S(2)}, u32[]{:S(2)}) collective-permute-start(bf16[1280,128]{1,0:T(8,128)(2,1)S(1)} %collective-permute-done.4.refs_0_), channel_id=1, source_target_pairs={{0,2},{1,3},{2,0},{3,1},{4,6},{5,7},{6,4},{7,5},{8,10},{9,11},{10,... | collective-permute-start | bytes 983048 | tf_op jit(solution)/shard_map/ppermute | solution.py:34
  41.4 14.0 %collective-permute-start.15 = (bf16[1280,128]{1,0:T(8,128)(2,1)S(1)}, bf16[1280,128]{1,0:T(8,128)(2,1)S(1)}, u32[]{:S(2)}, u32[]{:S(2)}) collective-permute-start(bf16[1280,128]{1,0:T(8,128)(2,1)S(1)} %collective-permute-done.12.refs_1_), channel_id=1, source_target_pairs={{0,4},{1,5},{2,6},{3,7},{4,8},{5,9},{6,10},{7,11},{8,12},{9,13},{1... | collective-permute-start | bytes 983048 | tf_op jit(solution)/shard_map/ppermute | solution.py:34
  41.4 14.0 %collective-permute-start.16 = (bf16[1280,128]{1,0:T(8,128)(2,1)S(1)}, bf16[1280,128]{1,0:T(8,128)(2,1)S(1)}, u32[]{:S(2)}, u32[]{:S(2)}) collective-permute-start(bf16[1280,128]{1,0:T(8,128)(2,1)S(1)} %collective-permute-done.12.refs_1_), channel_id=1, source_target_pairs={{0,2},{1,3},{2,0},{3,1},{4,6},{5,7},{6,4},{7,5},{8,10},{9,11},{10,... | collective-permute-start | bytes 983048 | tf_op jit(solution)/shard_map/ppermute | solution.py:34
  50.4 9.1 %collective-permute-start.14 = (bf16[1280,128]{1,0:T(8,128)(2,1)S(1)}, bf16[1280,128]{1,0:T(8,128)(2,1)S(1)}, u32[]{:S(2)}, u32[]{:S(2)}) collective-permute-start(bf16[1280,128]{1,0:T(8,128)(2,1)S(1)} %collective-permute-done.7.refs_2_), channel_id=1, source_target_pairs={{0,4},{1,5},{2,6},{3,7},{4,8},{5,9},{6,10},{7,11},{8,12},{9,13},{1... | collective-permute-start | bytes 983048 | tf_op jit(solution)/shard_map/ppermute | solution.py:34
  55.5 7.1 %collective-permute-start.17 = (bf16[1280,128]{1,0:T(8,128)(2,1)S(1)}, bf16[1280,128]{1,0:T(8,128)(2,1)S(1)}, u32[]{:S(2)}, u32[]{:S(2)}) collective-permute-start(bf16[1280,128]{1,0:T(8,128)(2,1)S(1)} %collective-permute-done.15.refs_1_), channel_id=1, source_target_pairs={{0,2},{1,3},{2,0},{3,1},{4,6},{5,7},{6,4},{7,5},{8,10},{9,11},{10,... | collective-permute-start | bytes 983048 | tf_op jit(solution)/shard_map/ppermute | solution.py:34
  64.8 1.9 %collective-permute-start.18 = (bf16[1280,128]{1,0:T(8,128)(2,1)S(1)}, bf16[1280,128]{1,0:T(8,128)(2,1)S(1)}, u32[]{:S(2)}, u32[]{:S(2)}) collective-permute-start(bf16[1280,128]{1,0:T(8,128)(2,1)S(1)} %bitcast.66), channel_id=1, source_target_pairs={{0,1},{1,0},{2,3},{3,2},{4,5},{5,4},{6,7},{7,6},{8,9},{9,8},{10,11... | collective-permute-start | bytes 983048 | tf_op jit(solution)/shard_map/ppermute | solution.py:34
  64.9 2.1 %collective-permute-start.19 = (bf16[1280,128]{1,0:T(8,128)(2,1)S(1)}, bf16[1280,128]{1,0:T(8,128)(2,1)S(1)}, u32[]{:S(2)}, u32[]{:S(2)}) collective-permute-start(bf16[1280,128]{1,0:T(8,128)(2,1)S(1)} %bitcast.65), channel_id=1, source_target_pairs={{0,1},{1,0},{2,3},{3,2},{4,5},{5,4},{6,7},{7,6},{8,9},{9,8},{10,11... | collective-permute-start | bytes 983048 | tf_op jit(solution)/shard_map/ppermute | solution.py:34
  65.4 7.5 %collective-permute-start.30 = (bf16[1280,128]{1,0:T(8,128)(2,1)S(1)}, bf16[1280,128]{1,0:T(8,128)(2,1)S(1)}, u32[]{:S(2)}, u32[]{:S(2)}) collective-permute-start(bf16[1280,128]{1,0:T(8,128)(2,1)S(1)} %bitcast.62), channel_id=1, source_target_pairs={{0,1},{1,0},{2,3},{3,2},{4,5},{5,4},{6,7},{7,6},{8,9},{9,8},{10,11... | collective-permute-start | bytes 983048 | tf_op jit(solution)/shard_map/ppermute | solution.py:34
  68.7 16.8 %collective-permute-start.29 = (bf16[1280,128]{1,0:T(8,128)(2,1)S(1)}, bf16[1280,128]{1,0:T(8,128)(2,1)S(1)}, u32[]{:S(2)}, u32[]{:S(2)}) collective-permute-start(bf16[1280,128]{1,0:T(8,128)(2,1)S(1)} %bitcast.61), channel_id=1, source_target_pairs={{0,1},{1,0},{2,3},{3,2},{4,5},{5,4},{6,7},{7,6},{8,9},{9,8},{10,11... | collective-permute-start | bytes 983048 | tf_op jit(solution)/shard_map/ppermute | solution.py:34
  68.9 4.1 %collective-permute-start.23 = (bf16[1280,128]{1,0:T(8,128)(2,1)S(1)}, bf16[1280,128]{1,0:T(8,128)(2,1)S(1)}, u32[]{:S(2)}, u32[]{:S(2)}) collective-permute-start(bf16[1280,128]{1,0:T(8,128)(2,1)S(1)} %bitcast.64), channel_id=1, source_target_pairs={{0,1},{1,0},{2,3},{3,2},{4,5},{5,4},{6,7},{7,6},{8,9},{9,8},{10,11... | collective-permute-start | bytes 983048 | tf_op jit(solution)/shard_map/ppermute | solution.py:34
  69.3 7.0 %collective-permute-start.24 = (bf16[640,128]{1,0:T(8,128)(2,1)S(1)}, bf16[640,128]{1,0:T(8,128)(2,1)S(1)}, u32[]{:S(2)}, u32[]{:S(2)}) collective-permute-start(bf16[640,128]{1,0:T(8,128)(2,1)S(1)} %get-tuple-element.93), channel_id=1, source_target_pairs={{0,2},{1,3},{2,0},{3,1},{4,6},{5,7},{6,4},{7,5},{8,10},{9,11},{10,... | collective-permute-start | bytes 491528 | tf_op jit(solution)/shard_map/ppermute | solution.py:34
  70.6 8.4 %collective-permute-start.31 = (bf16[640,128]{1,0:T(8,128)(2,1)S(1)}, bf16[640,128]{1,0:T(8,128)(2,1)S(1)}, u32[]{:S(2)}, u32[]{:S(2)}) collective-permute-start(bf16[640,128]{1,0:T(8,128)(2,1)S(1)} %get-tuple-element.103), channel_id=1, source_target_pairs={{0,2},{1,3},{2,0},{3,1},{4,6},{5,7},{6,4},{7,5},{8,10},{9,11},{10,... | collective-permute-start | bytes 491528 | tf_op jit(solution)/shard_map/ppermute | solution.py:34
  72.9 6.3 %collective-permute-start.21 = (bf16[1280,128]{1,0:T(8,128)(2,1)S(1)}, bf16[1280,128]{1,0:T(8,128)(2,1)S(1)}, u32[]{:S(2)}, u32[]{:S(2)}) collective-permute-start(bf16[1280,128]{1,0:T(8,128)(2,1)S(1)} %bitcast.63), channel_id=1, source_target_pairs={{0,1},{1,0},{2,3},{3,2},{4,5},{5,4},{6,7},{7,6},{8,9},{9,8},{10,11... | collective-permute-start | bytes 983048 | tf_op jit(solution)/shard_map/ppermute | solution.py:34
  73.0 12.4 %collective-permute-start.22 = (bf16[1280,128]{1,0:T(8,128)(2,1)S(1)}, bf16[1280,128]{1,0:T(8,128)(2,1)S(1)}, u32[]{:S(2)}, u32[]{:S(2)}) collective-permute-start(bf16[1280,128]{1,0:T(8,128)(2,1)S(1)} %get-tuple-element.90), channel_id=1, source_target_pairs={{0,4},{1,5},{2,6},{3,7},{4,8},{5,9},{6,10},{7,11},{8,12},{9,13},{1... | collective-permute-start | bytes 983048 | tf_op jit(solution)/shard_map/ppermute | solution.py:34
  76.3 18.2 %collective-permute-start.27 = (bf16[1280,128]{1,0:T(8,128)(2,1)S(1)}, bf16[1280,128]{1,0:T(8,128)(2,1)S(1)}, u32[]{:S(2)}, u32[]{:S(2)}) collective-permute-start(bf16[1280,128]{1,0:T(8,128)(2,1)S(1)} %bitcast.60), channel_id=1, source_target_pairs={{0,1},{1,0},{2,3},{3,2},{4,5},{5,4},{6,7},{7,6},{8,9},{9,8},{10,11... | collective-permute-start | bytes 983048 | tf_op jit(solution)/shard_map/ppermute | solution.py:34
  79.0 20.7 %collective-permute-start.20 = (bf16[1280,128]{1,0:T(8,128)(2,1)S(1)}, bf16[1280,128]{1,0:T(8,128)(2,1)S(1)}, u32[]{:S(2)}, u32[]{:S(2)}) collective-permute-start(bf16[1280,128]{1,0:T(8,128)(2,1)S(1)} %bitcast.59), channel_id=1, source_target_pairs={{0,1},{1,0},{2,3},{3,2},{4,5},{5,4},{6,7},{7,6},{8,9},{9,8},{10,11... | collective-permute-start | bytes 983048 | tf_op jit(solution)/shard_map/ppermute | solution.py:34
  79.1 9.4 %collective-permute-start.32 = (bf16[640,128]{1,0:T(8,128)(2,1)S(1)}, bf16[640,128]{1,0:T(8,128)(2,1)S(1)}, u32[]{:S(2)}, u32[]{:S(2)}) collective-permute-start(bf16[640,128]{1,0:T(8,128)(2,1)S(1)} %get-tuple-element.114), channel_id=1, source_target_pairs={{0,4},{1,5},{2,6},{3,7},{4,8},{5,9},{6,10},{7,11},{8,12},{9,13},{1... | collective-permute-start | bytes 491528 | tf_op jit(solution)/shard_map/ppermute | solution.py:34
  85.4 14.2 %collective-permute-start.34 = (bf16[640,128]{1,0:T(8,128)(2,1)S(1)}, bf16[640,128]{1,0:T(8,128)(2,1)S(1)}, u32[]{:S(2)}, u32[]{:S(2)}) collective-permute-start(bf16[640,128]{1,0:T(8,128)(2,1)S(1)} %get-tuple-element.115), channel_id=1, source_target_pairs={{0,4},{1,5},{2,6},{3,7},{4,8},{5,9},{6,10},{7,11},{8,12},{9,13},{1... | collective-permute-start | bytes 491528 | tf_op jit(solution)/shard_map/ppermute | solution.py:34
  85.5 9.0 %collective-permute-start.25 = (bf16[1280,128]{1,0:T(8,128)(2,1)S(1)}, bf16[1280,128]{1,0:T(8,128)(2,1)S(1)}, u32[]{:S(2)}, u32[]{:S(2)}) collective-permute-start(bf16[1280,128]{1,0:T(8,128)(2,1)S(1)} %fusion.4), channel_id=1, source_target_pairs={{0,2},{1,3},{2,0},{3,1},{4,6},{5,7},{6,4},{7,5},{8,10},{9,11},{10,... | collective-permute-start | bytes 983048 | tf_op jit(solution)/shard_map/ppermute | solution.py:34
  88.5 11.2 %collective-permute-start.33 = (bf16[640,128]{1,0:T(8,128)(2,1)S(1)}, bf16[640,128]{1,0:T(8,128)(2,1)S(1)}, u32[]{:S(2)}, u32[]{:S(2)}) collective-permute-start(bf16[640,128]{1,0:T(8,128)(2,1)S(1)} %fusion.15), channel_id=1, source_target_pairs={{0,4},{1,5},{2,6},{3,7},{4,8},{5,9},{6,10},{7,11},{8,12},{9,13},{1... | collective-permute-start | bytes 491528 | tf_op jit(solution)/shard_map/ppermute | solution.py:34
  94.6 13.1 %collective-permute-start.28 = (bf16[1280,128]{1,0:T(8,128)(2,1)S(1)}, bf16[1280,128]{1,0:T(8,128)(2,1)S(1)}, u32[]{:S(2)}, u32[]{:S(2)}) collective-permute-start(bf16[1280,128]{1,0:T(8,128)(2,1)S(1)} %fusion.3), channel_id=1, source_target_pairs={{0,12},{1,13},{2,14},{3,15},{4,0},{5,1},{6,2},{7,3},{8,4},{9,5},{1... | collective-permute-start | bytes 983048 | tf_op jit(solution)/shard_map/ppermute | solution.py:34
  98.2 9.5 %collective-permute-start.26 = (bf16[1280,128]{1,0:T(8,128)(2,1)S(1)}, bf16[1280,128]{1,0:T(8,128)(2,1)S(1)}, u32[]{:S(2)}, u32[]{:S(2)}) collective-permute-start(bf16[1280,128]{1,0:T(8,128)(2,1)S(1)} %fusion.6), channel_id=1, source_target_pairs={{0,2},{1,3},{2,0},{3,1},{4,6},{5,7},{6,4},{7,5},{8,10},{9,11},{10,... | collective-permute-start | bytes 983048 | tf_op jit(solution)/shard_map/ppermute | solution.py:34
  99.7 8.1 %collective-permute-start.35 = (bf16[640,128]{1,0:T(8,128)(2,1)S(1)}, bf16[640,128]{1,0:T(8,128)(2,1)S(1)}, u32[]{:S(2)}, u32[]{:S(2)}) collective-permute-start(bf16[640,128]{1,0:T(8,128)(2,1)S(1)} %add_convert_fusion), channel_id=1, source_target_pairs={{0,4},{1,5},{2,6},{3,7},{4,8},{5,9},{6,10},{7,11},{8,12},{9,13},{1... | collective-permute-start | bytes 491528 | tf_op jit(solution)/shard_map/ppermute | solution.py:34

commit v14 on v13

--- a/solution.py
+++ b/solution.py
@@ -86,18 +86,20 @@
     joining = move(aside, ALONG)
     total.update({name: paired(*pair) for name, *pair in zip(rest, blocks_of(rest, False), blocks_of(rest, True))})
 
-    crossing, two_on[1] = tie(narrow(total[FAR3]), two_on[1])
+    two_on[0], joining = tie(two_on[0], joining)
+    two_on = [move(narrow(own + wide(part)), ALONG) for own, part in zip(halves(total[NEAR2]), two_on)]
+    crossing, two_on[0] = tie(narrow(total[FAR3]), two_on[0])
     three_on = move(crossing, ACROSS)
-    crossing, three_on = tie(narrow(total[FAR0] + wide(joining)), three_on)
-    straight = move(crossing, ACROSS)
-    two_on = [move(narrow(own + wide(part)), ALONG) for own, part in zip(halves(total[NEAR2]), two_on)]
     later, two_on[0] = tie(total[NEAR1], two_on[0])
     one_on = [
         move(narrow(halves(own)[index] + wide(two_on[index])), ALONG)
         for index, own in enumerate((total[NEAR1], later))
     ]
+    crossing, three_on = tie(narrow(total[FAR0] + wide(joining)), three_on)
+    straight = move(crossing, ACROSS)
     one_back = move(narrow(total[NEAR3] + wide(three_on)), BACK)
-    return total[NEAR0] + wide(straight) + wide(one_back) + wide(jnp.concatenate(one_on))
+    (result,) = tie(total[NEAR0] + wide(jnp.concatenate(one_on)))
+    return result + wide(straight) + wide(one_back)
 
 
 def clear(half):

time: 109 us -> 110 us (level)
  Pallas kernels: 16.6 us -> 21.4 us
  waiting for transfers between devices: 51.5 us -> 49.1 us
  starting transfers between devices: 26.8 us -> 25.5 us
    pallas_call x8, Pallas kernels: 16.6 us -> 21.4 us  [call(): pl.pallas_call(kernel, out_shape=outs, in_specs=in_specs, out_specs=[VMEM...]
    ppermute x36, waiting for transfers between devices: 51.5 us -> 49.1 us  [move(): return lax.ppermute(array, 'aux', pairs)]
    ppermute x36, starting transfers between devices: 26.8 us -> 25.5 us  [move(): return lax.ppermute(array, 'aux', pairs)]
  transfers between devices with their start and end apart: 36 -> 36, of which waited for: 16 -> 17; matrix products, arithmetic and copies ran while one was open for 11% -> 11% of each run, Pallas kernels for 13% -> 17%
where the time goes in v14:
time: 110 us
  waiting for transfers between devices  49.1 us (45%)
  starting transfers between devices  25.5 us (23%)
  Pallas kernels  21.4 us (19%)
  local copies, waits for them, and re-layouts  8.77 us (8%)
  other arithmetic  4.14 us (4%)
    ppermute x36, waiting for transfers between devices, move(): return lax.ppermute(array, 'aux', pairs)  49.1 us
    ppermute x36, starting transfers between devices, move(): return lax.ppermute(array, 'aux', pairs)  25.5 us
    pallas_call x8, Pallas kernels, call(): pl.pallas_call(kernel, out_shape=outs, in_specs=in_specs, out_specs=[VMEM...  21.4 us
    unnamed x7, local copies, waits for them, and re-layouts  7.55 us
  transfers between devices with their start and end apart: 36, of which 17 were waited for; matrix products, arithmetic and copies ran while one was open for 11% of the time, Pallas kernels for 17%

profile of v14, /device:TPU:0, one launch (start us, length us, event | category | flops | bytes accessed | tf_op | source)
XLA Modules:
  0.0 109.9 jit_solution(195372590990630433)
XLA Ops:
  0.0 0.5 collective-permute-start.11
  0.5 1.1 %constant_dynamic-slice_fusion.1 = (bf16[1280,128]{1,0:T(8,128)(2,1)S(1)}, bf16[1280,128]{1,0:T(8,128)(2,1)S(1)}) fusion(bf16[1280,256]{1,0:T(8,128)(2,1)} %param.7, s32[]{:T(128)S(6)} %select_n.162, s32[]{:T(128)S(6)} %select_n.161), kind=kLoop, calls=%fused_computation.91 | loop fusion | bytes 1310728 | tf_op jit(solution)/shard_map/dynamic_slice | solution.py:244
  1.6 2.6 %collective-permute-start.2 = (bf16[1280,128]{1,0:T(8,128)(2,1)S(1)}, bf16[1280,128]{1,0:T(8,128)(2,1)S(1)}, u32[]{:S(2)}, u32[]{:S(2)}) collective-permute-start(bf16[1280,128]{1,0:T(8,128)(2,1)S(1)} %get-tuple-element.121.refs_0_), channel_id=1, source_target_pairs={{0,4},{1,5},{2,6},{3,7},{4,8},{5,9},{6,10},{7,11},{8,12},{9,13},{1... | collective-permute-start | bytes 983048 | tf_op jit(solution)/shard_map/ppermute | solution.py:34
  4.2 1.5 %collective-permute-start.3 = (bf16[1280,128]{1,0:T(8,128)(2,1)S(1)}, bf16[1280,128]{1,0:T(8,128)(2,1)S(1)}, u32[]{:S(2)}, u32[]{:S(2)}) collective-permute-start(bf16[1280,128]{1,0:T(8,128)(2,1)S(1)} %get-tuple-element.121.refs_0_), channel_id=1, source_target_pairs={{0,2},{1,3},{2,0},{3,1},{4,6},{5,7},{6,4},{7,5},{8,10},{9,11},{10,... | collective-permute-start | bytes 983048 | tf_op jit(solution)/shard_map/ppermute | solution.py:34
  5.7 0.5 collective-permute-start
  6.2 0.7 constant_dynamic-update-slice_fusion.1
  7.5 3.4 %copy.9 = bf16[32,8,32,128]{3,2,1,0:T(8,128)(2,1)} copy(bf16[32,8,32,128]{3,1,2,0:T(8,128)(2,1)} %bitcast.63) | data formatting | bytes 4194304
  11.0 0.7 compare_select_fusion.3
  11.7 0.9 collective-permute-done.8.refs_1_
  12.6 0.5 collective-permute-start.10
  13.1 1.6 %collective-permute-start.9 = (bf16[1280,128]{1,0:T(8,128)(2,1)S(1)}, bf16[1280,128]{1,0:T(8,128)(2,1)S(1)}, u32[]{:S(2)}, u32[]{:S(2)}) collective-permute-start(bf16[1280,128]{1,0:T(8,128)(2,1)S(1)} %collective-permute-done.8.refs_1_), channel_id=1, source_target_pairs={{0,4},{1,5},{2,6},{3,7},{4,8},{5,9},{6,10},{7,11},{8,12},{9,13},{1... | collective-permute-start | bytes 983048 | tf_op jit(solution)/shard_map/ppermute | solution.py:34
  14.7 0.6 fusion.27
  15.4 1.6 %collective-permute-start.4 = (bf16[1280,128]{1,0:T(8,128)(2,1)S(1)}, bf16[1280,128]{1,0:T(8,128)(2,1)S(1)}, u32[]{:S(2)}, u32[]{:S(2)}) collective-permute-start(bf16[1280,128]{1,0:T(8,128)(2,1)S(1)} %collective-permute-done.2.refs_0_), channel_id=1, source_target_pairs={{0,4},{1,5},{2,6},{3,7},{4,8},{5,9},{6,10},{7,11},{8,12},{9,13},{1... | collective-permute-start | bytes 983048 | tf_op jit(solution)/shard_map/ppermute | solution.py:34
  17.0 1.5 %collective-permute-start.5 = (bf16[1280,128]{1,0:T(8,128)(2,1)S(1)}, bf16[1280,128]{1,0:T(8,128)(2,1)S(1)}, u32[]{:S(2)}, u32[]{:S(2)}) collective-permute-start(bf16[1280,128]{1,0:T(8,128)(2,1)S(1)} %collective-permute-done.2.refs_0_), channel_id=1, source_target_pairs={{0,2},{1,3},{2,0},{3,1},{4,6},{5,7},{6,4},{7,5},{8,10},{9,11},{10,... | collective-permute-start | bytes 983048 | tf_op jit(solution)/shard_map/ppermute | solution.py:34
  18.5 4.7 %collective-permute-done.10.refs_3_ = bf16[1280,128]{1,0:T(8,128)(2,1)S(1)} collective-permute-done((bf16[1280,128]{1,0:T(8,128)(2,1)S(1)}, bf16[1280,128]{1,0:T(8,128)(2,1)S(1)}, u32[]{:S(2)}, u32[]{:S(2)}) %collective-permute-start.10) | collective-permute-done | bytes 327712 | tf_op jit(solution)/shard_map/ppermute | solution.py:34
  23.1 2.4 %collective-permute-done.9.refs_1_ = bf16[1280,128]{1,0:T(8,128)(2,1)S(1)} collective-permute-done((bf16[1280,128]{1,0:T(8,128)(2,1)S(1)}, bf16[1280,128]{1,0:T(8,128)(2,1)S(1)}, u32[]{:S(2)}, u32[]{:S(2)}) %collective-permute-start.9) | collective-permute-done | bytes 327712 | tf_op jit(solution)/shard_map/ppermute | solution.py:34
  25.5 3.4 %copy.10 = bf16[32,8,32,128]{3,2,1,0:T(8,128)(2,1)} copy(bf16[32,8,32,128]{3,1,2,0:T(8,128)(2,1)} %bitcast.25) | data formatting | bytes 4194304
  29.0 1.5 %collective-permute-start.13 = (bf16[1280,128]{1,0:T(8,128)(2,1)S(1)}, bf16[1280,128]{1,0:T(8,128)(2,1)S(1)}, u32[]{:S(2)}, u32[]{:S(2)}) collective-permute-start(bf16[1280,128]{1,0:T(8,128)(2,1)S(1)} %collective-permute-done.9.refs_1_), channel_id=1, source_target_pairs={{0,2},{1,3},{2,0},{3,1},{4,6},{5,7},{6,4},{7,5},{8,10},{9,11},{10,... | collective-permute-start | bytes 983048 | tf_op jit(solution)/shard_map/ppermute | solution.py:34
  30.5 0.3 convert_reduce_fusion
  30.8 0.5 select_reduce_fusion
  31.3 0.2 collective-permute-done.4.refs_0_
  31.5 1.2 %collective-permute-start.6 = (bf16[1280,128]{1,0:T(8,128)(2,1)S(1)}, bf16[1280,128]{1,0:T(8,128)(2,1)S(1)}, u32[]{:S(2)}, u32[]{:S(2)}) collective-permute-start(bf16[1280,128]{1,0:T(8,128)(2,1)S(1)} %collective-permute-done.4.refs_0_), channel_id=1, source_target_pairs={{0,4},{1,5},{2,6},{3,7},{4,8},{5,9},{6,10},{7,11},{8,12},{9,13},{1... | collective-permute-start | bytes 983048 | tf_op jit(solution)/shard_map/ppermute | solution.py:34
  32.7 1.1 collective-permute-start.7
  33.8 0.1 convert_reduce_fusion.1.bounds_ref
  34.0 5.1 %shard_map.46 = (f32[41024,128]{1,0:T(8,128)S(1)}, bf16[512,32,128]{2,1,0:T(8,128)(2,1)S(1)}) custom-call(s32[1584]{0:T(1024)S(1)} %concatenate.10.table_ref, s32[6]{0:T(128)S(1)} %convert_reduce_fusion.1.bounds_ref, bf16[1280,128]{1,0:T(8,128)(2,1)} %copy-done, bf16[1280,128]{1,0:T(8,128)(2,1)} %copy-done.1, bf16[256,32,128]{2,1,0:T(8,128)(2,1)} %bitcast.61, ...), custom_call_target="tpu_custom_call" | custom-call | flops 107374184 | bytes 4194304 | tf_op jit(solution)/shard_map/pallas_call | solution.py:217
  39.1 2.3 %collective-permute-done.12.refs_1_ = bf16[1280,128]{1,0:T(8,128)(2,1)S(1)} collective-permute-done((bf16[1280,128]{1,0:T(8,128)(2,1)S(1)}, bf16[1280,128]{1,0:T(8,128)(2,1)S(1)}, u32[]{:S(2)}, u32[]{:S(2)}) %collective-permute-start.12) | collective-permute-done | bytes 327712 | tf_op jit(solution)/shard_map/ppermute | solution.py:34
  41.4 1.5 %collective-permute-start.16 = (bf16[1280,128]{1,0:T(8,128)(2,1)S(1)}, bf16[1280,128]{1,0:T(8,128)(2,1)S(1)}, u32[]{:S(2)}, u32[]{:S(2)}) collective-permute-start(bf16[1280,128]{1,0:T(8,128)(2,1)S(1)} %collective-permute-done.12.refs_1_), channel_id=1, source_target_pairs={{0,2},{1,3},{2,0},{3,1},{4,6},{5,7},{6,4},{7,5},{8,10},{9,11},{10,... | collective-permute-start | bytes 983048 | tf_op jit(solution)/shard_map/ppermute | solution.py:34
  42.9 5.5 %collective-permute-done.6.refs_0_ = bf16[1280,128]{1,0:T(8,128)(2,1)S(1)} collective-permute-done((bf16[1280,128]{1,0:T(8,128)(2,1)S(1)}, bf16[1280,128]{1,0:T(8,128)(2,1)S(1)}, u32[]{:S(2)}, u32[]{:S(2)}) %collective-permute-start.6) | collective-permute-done | bytes 327712 | tf_op jit(solution)/shard_map/ppermute | solution.py:34
  48.4 2.8 %shard_map.47.refs_5_ = f32[41024,128]{1,0:T(8,128)S(1)} custom-call(s32[1584]{0:T(1024)S(1)} %concatenate.10.table_ref, s32[6]{0:T(128)S(1)} %convert_reduce_fusion.1.bounds_ref, bf16[1280,128]{1,0:T(8,128)(2,1)S(1)} %collective-permute-done.2.refs_0_, bf16[1280,128]{1,0:T(8,128)(2,1)S(1)} %collective-permute-done.9.refs_1_, ...), custom_call_target="tpu_custom_call", output_to_operand_aliasing={{}: (7, {})} | custom-call | flops 107374184 | bytes 4194304 | tf_op jit(solution)/shard_map/pallas_call | solution.py:217
  51.3 3.1 %shard_map.48.refs_5_ = f32[41024,128]{1,0:T(8,128)S(1)} custom-call(s32[1584]{0:T(1024)S(1)} %concatenate.10.table_ref, s32[6]{0:T(128)S(1)} %convert_reduce_fusion.1.bounds_ref, bf16[1280,128]{1,0:T(8,128)(2,1)S(1)} %collective-permute-done.4.refs_0_, bf16[1280,128]{1,0:T(8,128)(2,1)S(1)} %collective-permute-done.12.refs_1_, ...), custom_call_target="tpu_custom_call", output_to_operand_aliasing={{}: (7, {})} | custom-call | flops 107374184 | bytes 4194304 | tf_op jit(solution)/shard_map/pallas_call | solution.py:217
  54.4 0.7 collective-permute-done.15.refs_1_
  55.1 1.8 %collective-permute-start.17 = (bf16[1280,128]{1,0:T(8,128)(2,1)S(1)}, bf16[1280,128]{1,0:T(8,128)(2,1)S(1)}, u32[]{:S(2)}, u32[]{:S(2)}) collective-permute-start(bf16[1280,128]{1,0:T(8,128)(2,1)S(1)} %collective-permute-done.15.refs_1_), channel_id=1, source_target_pairs={{0,2},{1,3},{2,0},{3,1},{4,6},{5,7},{6,4},{7,5},{8,10},{9,11},{10,... | collective-permute-start | bytes 983048 | tf_op jit(solution)/shard_map/ppermute | solution.py:34
  56.9 3.4 %shard_map.49.refs_3_ = f32[41024,128]{1,0:T(8,128)S(1)} custom-call(s32[1584]{0:T(1024)S(1)} %concatenate.10.table_ref, s32[6]{0:T(128)S(1)} %convert_reduce_fusion.1.bounds_ref, bf16[1280,128]{1,0:T(8,128)(2,1)S(1)} %collective-permute-done.6.refs_0_, bf16[1280,128]{1,0:T(8,128)(2,1)S(1)} %collective-permute-done.15.refs_1_, ...), custom_call_target="tpu_custom_call", output_to_operand_aliasing={{}: (7, {})} | custom-call | flops 107374184 | bytes 4194304 | tf_op jit(solution)/shard_map/pallas_call | solution.py:217
  60.2 1.9 %collective-permute-done.17.refs_1_ = bf16[1280,128]{1,0:T(8,128)(2,1)S(1)} collective-permute-done((bf16[1280,128]{1,0:T(8,128)(2,1)S(1)}, bf16[1280,128]{1,0:T(8,128)(2,1)S(1)}, u32[]{:S(2)}, u32[]{:S(2)}) %collective-permute-start.17) | collective-permute-done | bytes 327712 | tf_op jit(solution)/shard_map/ppermute | solution.py:34
  62.1 2.8 %shard_map.50 = (f32[41024,128]{1,0:T(8,128)S(1)}, bf16[256,128]{1,0:T(8,128)(2,1)S(1)}, bf16[1,1280,128]{2,1,0:T(8,128)(2,1)S(1)}, bf16[1,1280,128]{2,1,0:T(8,128)(2,1)S(1)}, bf16[1,1280,128]{2,1,0:T(8,128)(2,1)S(1)}) custom-call(s32[1584]{0:T(1024)S(1)} %concatenate.10.table_ref, ...), custom_call_target="tpu_custom_call", output_to_operand_aliasing={{0}: (7, {})} | custom-call | flops 359032416 | bytes 4194304 | tf_op jit(solution)/shard_map/pallas_call | solution.py:217
  65.0 0.5 collective-permute-start.19
  65.5 0.1 collective-permute-start.23
  65.6 1.2 %shard_map.51 = (f32[1,1280,128]{2,1,0:T(8,128)S(1)}, f32[1,1280,128]{2,1,0:T(8,128)S(1)}, f32[1,1280,128]{2,1,0:T(8,128)S(1)}) custom-call(s32[8]{0:T(128)S(1)} %fusion.30.chips_ref, s32[1]{0:T(128)} %bitcast.core_ref, f32[41024,128]{1,0:T(8,128)S(1)} %get-tuple-element.87.half, bf16[256,128]{1,0:T(8,128)(2,1)S(1)} %get-tuple-element.82.weights), custom_call_target="tpu_custom_call" | custom-call | flops 251658240 | bytes 4194304 | tf_op jit(solution)/shard_map/pallas_call | solution.py:217
  66.8 0.3 collective-permute-done.19
  67.1 0.2 fusion.8
  67.3 1.6 %shard_map.53 = (bf16[1,1280,128]{2,1,0:T(8,128)(2,1)S(1)}, bf16[1,1280,128]{2,1,0:T(8,128)(2,1)S(1)}, bf16[1,1280,128]{2,1,0:T(8,128)(2,1)S(1)}, bf16[1,1280,12...) custom-call(s32[8]{0:T(128)S(1)} %fusion.30.chips_ref, s32[1]{0:T(128)} %bitcast.core_ref, ...), custom_call_target="tpu_custom_call" | custom-call | flops 419430400 | bytes 4194304 | tf_op jit(solution)/shard_map/pallas_call | solution.py:217
  68.9 0.2 collective-permute-start.21
  69.1 1.5 %collective-permute-start.24 = (bf16[640,128]{1,0:T(8,128)(2,1)S(1)}, bf16[640,128]{1,0:T(8,128)(2,1)S(1)}, u32[]{:S(2)}, u32[]{:S(2)}) collective-permute-start(bf16[640,128]{1,0:T(8,128)(2,1)S(1)} %get-tuple-element.96), channel_id=1, source_target_pairs={{0,2},{1,3},{2,0},{3,1},{4,6},{5,7},{6,4},{7,5},{8,10},{9,11},{10,... | collective-permute-start | bytes 491528 | tf_op jit(solution)/shard_map/ppermute | solution.py:34
  70.6 0.5 collective-permute-start.28
  71.2 1.5 %shard_map.52 = (f32[1,1280,128]{2,1,0:T(8,128)S(1)}, f32[1,1280,128]{2,1,0:T(8,128)S(1)}, f32[1,1280,128]{2,1,0:T(8,128)S(1)}, f32[1,1280,128]{2,1,0:T(8,128)S(1)}, f32[1,1280,128]{2,1,0:T(8,128)S(1)}) custom-call(s32[8]{0:T(128)S(1)} %fusion.30.chips_ref, s32[1]{0:T(128)} %bitcast.core_ref, f32[41024,128]{1,0:T(8,128)S(1)} %get-tuple-element.87.half, ...), custom_call_target="tpu_custom_call" | custom-call | flops 419430400 | bytes 4194304 | tf_op jit(solution)/shard_map/pallas_call | solution.py:217
  72.7 3.4 %collective-permute-done.24 = bf16[640,128]{1,0:T(8,128)(2,1)S(1)} collective-permute-done((bf16[640,128]{1,0:T(8,128)(2,1)S(1)}, bf16[640,128]{1,0:T(8,128)(2,1)S(1)}, u32[]{:S(2)}, u32[]{:S(2)}) %collective-permute-start.24) | collective-permute-done | bytes 163872 | tf_op jit(solution)/shard_map/ppermute | solution.py:34
  76.1 4.7 %collective-permute-done.25 = bf16[1280,128]{1,0:T(8,128)(2,1)S(1)} collective-permute-done((bf16[1280,128]{1,0:T(8,128)(2,1)S(1)}, bf16[1280,128]{1,0:T(8,128)(2,1)S(1)}, u32[]{:S(2)}, u32[]{:S(2)}) %collective-permute-start.25) | collective-permute-done | bytes 327712 | tf_op jit(solution)/shard_map/ppermute | solution.py:34
  80.9 0.5 collective-permute-start.34
  81.4 0.1 fusion.10
  81.5 0.1 fusion.5
  81.7 1.0 collective-permute-start.29
  82.6 0.1 bitcast_add_fusion.4
  82.8 7.6 %collective-permute-done.26 = bf16[640,128]{1,0:T(8,128)(2,1)S(1)} collective-permute-done((bf16[640,128]{1,0:T(8,128)(2,1)S(1)}, bf16[640,128]{1,0:T(8,128)(2,1)S(1)}, u32[]{:S(2)}, u32[]{:S(2)}) %collective-permute-start.26) | collective-permute-done | bytes 163872 | tf_op jit(solution)/shard_map/ppermute | solution.py:34
  90.4 1.5 %collective-permute-start.32 = (bf16[1280,128]{1,0:T(8,128)(2,1)S(1)}, bf16[1280,128]{1,0:T(8,128)(2,1)S(1)}, u32[]{:S(2)}, u32[]{:S(2)}) collective-permute-start(bf16[1280,128]{1,0:T(8,128)(2,1)S(1)} %fusion.6), channel_id=1, source_target_pairs={{0,2},{1,3},{2,0},{3,1},{4,6},{5,7},{6,4},{7,5},{8,10},{9,11},{10,... | collective-permute-start | bytes 983048 | tf_op jit(solution)/shard_map/ppermute | solution.py:34
  92.0 0.9 collective-permute-done.29
  93.0 5.1 %collective-permute-done.32 = bf16[1280,128]{1,0:T(8,128)(2,1)S(1)} collective-permute-done((bf16[1280,128]{1,0:T(8,128)(2,1)S(1)}, bf16[1280,128]{1,0:T(8,128)(2,1)S(1)}, u32[]{:S(2)}, u32[]{:S(2)}) %collective-permute-start.32) | collective-permute-done | bytes 327712 | tf_op jit(solution)/shard_map/ppermute | solution.py:34
  98.2 0.1 fusion.3
  98.3 0.6 collective-permute-start.35
  98.9 1.5 %collective-permute-start.33 = (bf16[1280,128]{1,0:T(8,128)(2,1)S(1)}, bf16[1280,128]{1,0:T(8,128)(2,1)S(1)}, u32[]{:S(2)}, u32[]{:S(2)}) collective-permute-start(bf16[1280,128]{1,0:T(8,128)(2,1)S(1)} %fusion.5), channel_id=1, source_target_pairs={{0,2},{1,3},{2,0},{3,1},{4,6},{5,7},{6,4},{7,5},{8,10},{9,11},{10,... | collective-permute-start | bytes 983048 | tf_op jit(solution)/shard_map/ppermute | solution.py:34
  100.4 0.5 collective-permute-done.27
  100.9 3.5 %collective-permute-done.30 = bf16[640,128]{1,0:T(8,128)(2,1)S(1)} collective-permute-done((bf16[640,128]{1,0:T(8,128)(2,1)S(1)}, bf16[640,128]{1,0:T(8,128)(2,1)S(1)}, u32[]{:S(2)}, u32[]{:S(2)}) %collective-permute-start.30) | collective-permute-done | bytes 163872 | tf_op jit(solution)/shard_map/ppermute | solution.py:34
  104.4 0.1 fusion.7
  104.5 4.5 %collective-permute-done.35 = bf16[1280,128]{1,0:T(8,128)(2,1)S(1)} collective-permute-done((bf16[1280,128]{1,0:T(8,128)(2,1)S(1)}, bf16[1280,128]{1,0:T(8,128)(2,1)S(1)}, u32[]{:S(2)}, u32[]{:S(2)}) %collective-permute-start.35) | collective-permute-done | bytes 327712 | tf_op jit(solution)/shard_map/ppermute | solution.py:34
  109.0 0.9 add_multiply_fusion
  (46 shorter events, 0.8 us)
Async XLA Ops:
  0.0 25.5 %collective-permute-start.11 = (bf16[256,4096]{1,0:T(8,128)(2,1)}, bf16[256,4096]{1,0:T(8,128)(2,1)}, u32[]{:S(2)}, u32[]{:S(2)}) collective-permute-start(bf16[256,4096]{1,0:T(8,128)(2,1)} %param.4), channel_id=1, source_target_pairs={{0,1},{1,0},{2,3},{3,2},{4,5},{5,4},{6,7},{7,6},{8,9},{9,8},{10,11... | collective-permute-start | bytes 6291464 | tf_op jit(solution)/shard_map/ppermute | solution.py:34
  1.6 9.4 %copy-start = (bf16[1280,128]{1,0:T(8,128)(2,1)}, bf16[1280,128]{1,0:T(8,128)(2,1)S(1)}, u32[]{:S(2)}) copy-start(bf16[1280,128]{1,0:T(8,128)(2,1)S(1)} %get-tuple-element.121.refs_0_) | copy-start | bytes 983044
  1.6 13.8 %collective-permute-start.2 = (bf16[1280,128]{1,0:T(8,128)(2,1)S(1)}, bf16[1280,128]{1,0:T(8,128)(2,1)S(1)}, u32[]{:S(2)}, u32[]{:S(2)}) collective-permute-start(bf16[1280,128]{1,0:T(8,128)(2,1)S(1)} %get-tuple-element.121.refs_0_), channel_id=1, source_target_pairs={{0,4},{1,5},{2,6},{3,7},{4,8},{5,9},{6,10},{7,11},{8,12},{9,13},{1... | collective-permute-start | bytes 983048 | tf_op jit(solution)/shard_map/ppermute | solution.py:34
  4.2 11.2 %collective-permute-start.3 = (bf16[1280,128]{1,0:T(8,128)(2,1)S(1)}, bf16[1280,128]{1,0:T(8,128)(2,1)S(1)}, u32[]{:S(2)}, u32[]{:S(2)}) collective-permute-start(bf16[1280,128]{1,0:T(8,128)(2,1)S(1)} %get-tuple-element.121.refs_0_), channel_id=1, source_target_pairs={{0,2},{1,3},{2,0},{3,1},{4,6},{5,7},{6,4},{7,5},{8,10},{9,11},{10,... | collective-permute-start | bytes 983048 | tf_op jit(solution)/shard_map/ppermute | solution.py:34
  5.7 5.3 %collective-permute-start.1 = (s32[256,2]{0,1:T(2,128)}, s32[256,2]{0,1:T(2,128)S(1)}, u32[]{:S(2)}, u32[]{:S(2)}) collective-permute-start(s32[256,2]{0,1:T(2,128)} %param.5), channel_id=1, source_target_pairs={{0,1},{1,0},{2,3},{3,2},{4,5},{5,4},{6,7},{7,6},{8,9},{9,8},{10,11... | collective-permute-start | bytes 6152 | tf_op jit(solution)/shard_map/ppermute | solution.py:34
  5.7 5.3 %collective-permute-start = (s32[1]{0:T(128)}, s32[1]{0:T(128)}, u32[]{:S(2)}, u32[]{:S(2)}) collective-permute-start(s32[1]{0:T(128)} %param.6), channel_id=1, source_target_pairs={{0,1},{1,0},{2,3},{3,2},{4,5},{5,4},{6,7},{7,6},{8,9},{9,8},{10,11... | collective-permute-start | bytes 20 | tf_op jit(solution)/shard_map/ppermute | solution.py:34
  11.0 1.6 %collective-permute-start.8 = (bf16[1280,128]{1,0:T(8,128)(2,1)S(1)}, bf16[1280,128]{1,0:T(8,128)(2,1)S(1)}, u32[]{:S(2)}, u32[]{:S(2)}) collective-permute-start(bf16[1280,128]{1,0:T(8,128)(2,1)S(1)} %get-tuple-element.120), channel_id=1, source_target_pairs={{0,1},{1,0},{2,3},{3,2},{4,5},{5,4},{6,7},{7,6},{8,9},{9,8},{10,11... | collective-permute-start | bytes 983048 | tf_op jit(solution)/shard_map/ppermute | solution.py:34
  12.6 12.9 %copy-start.1 = (bf16[1280,128]{1,0:T(8,128)(2,1)}, bf16[1280,128]{1,0:T(8,128)(2,1)S(1)}, u32[]{:S(2)}) copy-start(bf16[1280,128]{1,0:T(8,128)(2,1)S(1)} %collective-permute-done.8.refs_1_) | copy-start | bytes 983044
  12.6 10.6 %collective-permute-start.10 = (bf16[1280,128]{1,0:T(8,128)(2,1)S(1)}, bf16[1280,128]{1,0:T(8,128)(2,1)S(1)}, u32[]{:S(2)}, u32[]{:S(2)}) collective-permute-start(bf16[1280,128]{1,0:T(8,128)(2,1)S(1)} %collective-permute-done.8.refs_1_), channel_id=1, source_target_pairs={{0,2},{1,3},{2,0},{3,1},{4,6},{5,7},{6,4},{7,5},{8,10},{9,11},{10,... | collective-permute-start | bytes 983048 | tf_op jit(solution)/shard_map/ppermute | solution.py:34
  13.1 12.4 %collective-permute-start.9 = (bf16[1280,128]{1,0:T(8,128)(2,1)S(1)}, bf16[1280,128]{1,0:T(8,128)(2,1)S(1)}, u32[]{:S(2)}, u32[]{:S(2)}) collective-permute-start(bf16[1280,128]{1,0:T(8,128)(2,1)S(1)} %collective-permute-done.8.refs_1_), channel_id=1, source_target_pairs={{0,4},{1,5},{2,6},{3,7},{4,8},{5,9},{6,10},{7,11},{8,12},{9,13},{1... | collective-permute-start | bytes 983048 | tf_op jit(solution)/shard_map/ppermute | solution.py:34
  15.4 16.2 %collective-permute-start.4 = (bf16[1280,128]{1,0:T(8,128)(2,1)S(1)}, bf16[1280,128]{1,0:T(8,128)(2,1)S(1)}, u32[]{:S(2)}, u32[]{:S(2)}) collective-permute-start(bf16[1280,128]{1,0:T(8,128)(2,1)S(1)} %collective-permute-done.2.refs_0_), channel_id=1, source_target_pairs={{0,4},{1,5},{2,6},{3,7},{4,8},{5,9},{6,10},{7,11},{8,12},{9,13},{1... | collective-permute-start | bytes 983048 | tf_op jit(solution)/shard_map/ppermute | solution.py:34
  17.0 14.5 %collective-permute-start.5 = (bf16[1280,128]{1,0:T(8,128)(2,1)S(1)}, bf16[1280,128]{1,0:T(8,128)(2,1)S(1)}, u32[]{:S(2)}, u32[]{:S(2)}) collective-permute-start(bf16[1280,128]{1,0:T(8,128)(2,1)S(1)} %collective-permute-done.2.refs_0_), channel_id=1, source_target_pairs={{0,2},{1,3},{2,0},{3,1},{4,6},{5,7},{6,4},{7,5},{8,10},{9,11},{10,... | collective-permute-start | bytes 983048 | tf_op jit(solution)/shard_map/ppermute | solution.py:34
  29.0 12.4 %collective-permute-start.12 = (bf16[1280,128]{1,0:T(8,128)(2,1)S(1)}, bf16[1280,128]{1,0:T(8,128)(2,1)S(1)}, u32[]{:S(2)}, u32[]{:S(2)}) collective-permute-start(bf16[1280,128]{1,0:T(8,128)(2,1)S(1)} %collective-permute-done.9.refs_1_), channel_id=1, source_target_pairs={{0,4},{1,5},{2,6},{3,7},{4,8},{5,9},{6,10},{7,11},{8,12},{9,13},{1... | collective-permute-start | bytes 983048 | tf_op jit(solution)/shard_map/ppermute | solution.py:34
  29.0 12.4 %collective-permute-start.13 = (bf16[1280,128]{1,0:T(8,128)(2,1)S(1)}, bf16[1280,128]{1,0:T(8,128)(2,1)S(1)}, u32[]{:S(2)}, u32[]{:S(2)}) collective-permute-start(bf16[1280,128]{1,0:T(8,128)(2,1)S(1)} %collective-permute-done.9.refs_1_), channel_id=1, source_target_pairs={{0,2},{1,3},{2,0},{3,1},{4,6},{5,7},{6,4},{7,5},{8,10},{9,11},{10,... | collective-permute-start | bytes 983048 | tf_op jit(solution)/shard_map/ppermute | solution.py:34
  31.5 16.9 %collective-permute-start.6 = (bf16[1280,128]{1,0:T(8,128)(2,1)S(1)}, bf16[1280,128]{1,0:T(8,128)(2,1)S(1)}, u32[]{:S(2)}, u32[]{:S(2)}) collective-permute-start(bf16[1280,128]{1,0:T(8,128)(2,1)S(1)} %collective-permute-done.4.refs_0_), channel_id=1, source_target_pairs={{0,4},{1,5},{2,6},{3,7},{4,8},{5,9},{6,10},{7,11},{8,12},{9,13},{1... | collective-permute-start | bytes 983048 | tf_op jit(solution)/shard_map/ppermute | solution.py:34
  32.7 15.7 %collective-permute-start.7 = (bf16[1280,128]{1,0:T(8,128)(2,1)S(1)}, bf16[1280,128]{1,0:T(8,128)(2,1)S(1)}, u32[]{:S(2)}, u32[]{:S(2)}) collective-permute-start(bf16[1280,128]{1,0:T(8,128)(2,1)S(1)} %collective-permute-done.4.refs_0_), channel_id=1, source_target_pairs={{0,2},{1,3},{2,0},{3,1},{4,6},{5,7},{6,4},{7,5},{8,10},{9,11},{10,... | collective-permute-start | bytes 983048 | tf_op jit(solution)/shard_map/ppermute | solution.py:34
  41.4 13.6 %collective-permute-start.15 = (bf16[1280,128]{1,0:T(8,128)(2,1)S(1)}, bf16[1280,128]{1,0:T(8,128)(2,1)S(1)}, u32[]{:S(2)}, u32[]{:S(2)}) collective-permute-start(bf16[1280,128]{1,0:T(8,128)(2,1)S(1)} %collective-permute-done.12.refs_1_), channel_id=1, source_target_pairs={{0,4},{1,5},{2,6},{3,7},{4,8},{5,9},{6,10},{7,11},{8,12},{9,13},{1... | collective-permute-start | bytes 983048 | tf_op jit(solution)/shard_map/ppermute | solution.py:34
  41.4 13.6 %collective-permute-start.16 = (bf16[1280,128]{1,0:T(8,128)(2,1)S(1)}, bf16[1280,128]{1,0:T(8,128)(2,1)S(1)}, u32[]{:S(2)}, u32[]{:S(2)}) collective-permute-start(bf16[1280,128]{1,0:T(8,128)(2,1)S(1)} %collective-permute-done.12.refs_1_), channel_id=1, source_target_pairs={{0,2},{1,3},{2,0},{3,1},{4,6},{5,7},{6,4},{7,5},{8,10},{9,11},{10,... | collective-permute-start | bytes 983048 | tf_op jit(solution)/shard_map/ppermute | solution.py:34
  51.2 9.0 %collective-permute-start.14 = (bf16[1280,128]{1,0:T(8,128)(2,1)S(1)}, bf16[1280,128]{1,0:T(8,128)(2,1)S(1)}, u32[]{:S(2)}, u32[]{:S(2)}) collective-permute-start(bf16[1280,128]{1,0:T(8,128)(2,1)S(1)} %collective-permute-done.7.refs_2_), channel_id=1, source_target_pairs={{0,4},{1,5},{2,6},{3,7},{4,8},{5,9},{6,10},{7,11},{8,12},{9,13},{1... | collective-permute-start | bytes 983048 | tf_op jit(solution)/shard_map/ppermute | solution.py:34
  55.1 7.1 %collective-permute-start.17 = (bf16[1280,128]{1,0:T(8,128)(2,1)S(1)}, bf16[1280,128]{1,0:T(8,128)(2,1)S(1)}, u32[]{:S(2)}, u32[]{:S(2)}) collective-permute-start(bf16[1280,128]{1,0:T(8,128)(2,1)S(1)} %collective-permute-done.15.refs_1_), channel_id=1, source_target_pairs={{0,2},{1,3},{2,0},{3,1},{4,6},{5,7},{6,4},{7,5},{8,10},{9,11},{10,... | collective-permute-start | bytes 983048 | tf_op jit(solution)/shard_map/ppermute | solution.py:34
  65.0 1.9 %collective-permute-start.18 = (bf16[1280,128]{1,0:T(8,128)(2,1)S(1)}, bf16[1280,128]{1,0:T(8,128)(2,1)S(1)}, u32[]{:S(2)}, u32[]{:S(2)}) collective-permute-start(bf16[1280,128]{1,0:T(8,128)(2,1)S(1)} %bitcast.60), channel_id=1, source_target_pairs={{0,1},{1,0},{2,3},{3,2},{4,5},{5,4},{6,7},{7,6},{8,9},{9,8},{10,11... | collective-permute-start | bytes 983048 | tf_op jit(solution)/shard_map/ppermute | solution.py:34
  65.0 2.1 %collective-permute-start.19 = (bf16[1280,128]{1,0:T(8,128)(2,1)S(1)}, bf16[1280,128]{1,0:T(8,128)(2,1)S(1)}, u32[]{:S(2)}, u32[]{:S(2)}) collective-permute-start(bf16[1280,128]{1,0:T(8,128)(2,1)S(1)} %bitcast.59), channel_id=1, source_target_pairs={{0,1},{1,0},{2,3},{3,2},{4,5},{5,4},{6,7},{7,6},{8,9},{9,8},{10,11... | collective-permute-start | bytes 983048 | tf_op jit(solution)/shard_map/ppermute | solution.py:34
  65.5 5.6 %collective-permute-start.23 = (bf16[1280,128]{1,0:T(8,128)(2,1)S(1)}, bf16[1280,128]{1,0:T(8,128)(2,1)S(1)}, u32[]{:S(2)}, u32[]{:S(2)}) collective-permute-start(bf16[1280,128]{1,0:T(8,128)(2,1)S(1)} %bitcast.58), channel_id=1, source_target_pairs={{0,1},{1,0},{2,3},{3,2},{4,5},{5,4},{6,7},{7,6},{8,9},{9,8},{10,11... | collective-permute-start | bytes 983048 | tf_op jit(solution)/shard_map/ppermute | solution.py:34
  68.9 12.8 %collective-permute-start.21 = (bf16[1280,128]{1,0:T(8,128)(2,1)S(1)}, bf16[1280,128]{1,0:T(8,128)(2,1)S(1)}, u32[]{:S(2)}, u32[]{:S(2)}) collective-permute-start(bf16[1280,128]{1,0:T(8,128)(2,1)S(1)} %bitcast.56), channel_id=1, source_target_pairs={{0,1},{1,0},{2,3},{3,2},{4,5},{5,4},{6,7},{7,6},{8,9},{9,8},{10,11... | collective-permute-start | bytes 983048 | tf_op jit(solution)/shard_map/ppermute | solution.py:34
  69.1 11.8 %collective-permute-start.25 = (bf16[1280,128]{1,0:T(8,128)(2,1)S(1)}, bf16[1280,128]{1,0:T(8,128)(2,1)S(1)}, u32[]{:S(2)}, u32[]{:S(2)}) collective-permute-start(bf16[1280,128]{1,0:T(8,128)(2,1)S(1)} %get-tuple-element.97), channel_id=1, source_target_pairs={{0,4},{1,5},{2,6},{3,7},{4,8},{5,9},{6,10},{7,11},{8,12},{9,13},{1... | collective-permute-start | bytes 983048 | tf_op jit(solution)/shard_map/ppermute | solution.py:34
  69.1 7.0 %collective-permute-start.24 = (bf16[640,128]{1,0:T(8,128)(2,1)S(1)}, bf16[640,128]{1,0:T(8,128)(2,1)S(1)}, u32[]{:S(2)}, u32[]{:S(2)}) collective-permute-start(bf16[640,128]{1,0:T(8,128)(2,1)S(1)} %get-tuple-element.96), channel_id=1, source_target_pairs={{0,2},{1,3},{2,0},{3,1},{4,6},{5,7},{6,4},{7,5},{8,10},{9,11},{10,... | collective-permute-start | bytes 491528 | tf_op jit(solution)/shard_map/ppermute | solution.py:34
  70.6 10.3 %collective-permute-start.28 = (bf16[640,128]{1,0:T(8,128)(2,1)S(1)}, bf16[640,128]{1,0:T(8,128)(2,1)S(1)}, u32[]{:S(2)}, u32[]{:S(2)}) collective-permute-start(bf16[640,128]{1,0:T(8,128)(2,1)S(1)} %get-tuple-element.102), channel_id=1, source_target_pairs={{0,2},{1,3},{2,0},{3,1},{4,6},{5,7},{6,4},{7,5},{8,10},{9,11},{10,... | collective-permute-start | bytes 491528 | tf_op jit(solution)/shard_map/ppermute | solution.py:34
  71.1 10.3 %collective-permute-start.31 = (bf16[1280,128]{1,0:T(8,128)(2,1)S(1)}, bf16[1280,128]{1,0:T(8,128)(2,1)S(1)}, u32[]{:S(2)}, u32[]{:S(2)}) collective-permute-start(bf16[1280,128]{1,0:T(8,128)(2,1)S(1)} %bitcast.57), channel_id=1, source_target_pairs={{0,1},{1,0},{2,3},{3,2},{4,5},{5,4},{6,7},{7,6},{8,9},{9,8},{10,11... | collective-permute-start | bytes 983048 | tf_op jit(solution)/shard_map/ppermute | solution.py:34
  76.1 6.6 %collective-permute-start.22 = (bf16[1280,128]{1,0:T(8,128)(2,1)S(1)}, bf16[1280,128]{1,0:T(8,128)(2,1)S(1)}, u32[]{:S(2)}, u32[]{:S(2)}) collective-permute-start(bf16[1280,128]{1,0:T(8,128)(2,1)S(1)} %bitcast.55), channel_id=1, source_target_pairs={{0,1},{1,0},{2,3},{3,2},{4,5},{5,4},{6,7},{7,6},{8,9},{9,8},{10,11... | collective-permute-start | bytes 983048 | tf_op jit(solution)/shard_map/ppermute | solution.py:34
  80.9 19.5 %collective-permute-start.20 = (bf16[1280,128]{1,0:T(8,128)(2,1)S(1)}, bf16[1280,128]{1,0:T(8,128)(2,1)S(1)}, u32[]{:S(2)}, u32[]{:S(2)}) collective-permute-start(bf16[1280,128]{1,0:T(8,128)(2,1)S(1)} %bitcast.53), channel_id=1, source_target_pairs={{0,1},{1,0},{2,3},{3,2},{4,5},{5,4},{6,7},{7,6},{8,9},{9,8},{10,11... | collective-permute-start | bytes 983048 | tf_op jit(solution)/shard_map/ppermute | solution.py:34
  80.9 17.3 %collective-permute-start.34 = (bf16[1280,128]{1,0:T(8,128)(2,1)S(1)}, bf16[1280,128]{1,0:T(8,128)(2,1)S(1)}, u32[]{:S(2)}, u32[]{:S(2)}) collective-permute-start(bf16[1280,128]{1,0:T(8,128)(2,1)S(1)} %bitcast.54), channel_id=1, source_target_pairs={{0,1},{1,0},{2,3},{3,2},{4,5},{5,4},{6,7},{7,6},{8,9},{9,8},{10,11... | collective-permute-start | bytes 983048 | tf_op jit(solution)/shard_map/ppermute | solution.py:34
  81.5 8.9 %collective-permute-start.26 = (bf16[640,128]{1,0:T(8,128)(2,1)S(1)}, bf16[640,128]{1,0:T(8,128)(2,1)S(1)}, u32[]{:S(2)}, u32[]{:S(2)}) collective-permute-start(bf16[640,128]{1,0:T(8,128)(2,1)S(1)} %get-tuple-element.119), channel_id=1, source_target_pairs={{0,4},{1,5},{2,6},{3,7},{4,8},{5,9},{6,10},{7,11},{8,12},{9,13},{1... | collective-permute-start | bytes 491528 | tf_op jit(solution)/shard_map/ppermute | solution.py:34
  81.7 11.3 %collective-permute-start.29 = (bf16[640,128]{1,0:T(8,128)(2,1)S(1)}, bf16[640,128]{1,0:T(8,128)(2,1)S(1)}, u32[]{:S(2)}, u32[]{:S(2)}) collective-permute-start(bf16[640,128]{1,0:T(8,128)(2,1)S(1)} %get-tuple-element.118), channel_id=1, source_target_pairs={{0,4},{1,5},{2,6},{3,7},{4,8},{5,9},{6,10},{7,11},{8,12},{9,13},{1... | collective-permute-start | bytes 491528 | tf_op jit(solution)/shard_map/ppermute | solution.py:34
  90.4 7.8 %collective-permute-start.32 = (bf16[1280,128]{1,0:T(8,128)(2,1)S(1)}, bf16[1280,128]{1,0:T(8,128)(2,1)S(1)}, u32[]{:S(2)}, u32[]{:S(2)}) collective-permute-start(bf16[1280,128]{1,0:T(8,128)(2,1)S(1)} %fusion.6), channel_id=1, source_target_pairs={{0,2},{1,3},{2,0},{3,1},{4,6},{5,7},{6,4},{7,5},{8,10},{9,11},{10,... | collective-permute-start | bytes 983048 | tf_op jit(solution)/shard_map/ppermute | solution.py:34
  91.9 8.9 %collective-permute-start.27 = (bf16[640,128]{1,0:T(8,128)(2,1)S(1)}, bf16[640,128]{1,0:T(8,128)(2,1)S(1)}, u32[]{:S(2)}, u32[]{:S(2)}) collective-permute-start(bf16[640,128]{1,0:T(8,128)(2,1)S(1)} %fusion.12), channel_id=1, source_target_pairs={{0,4},{1,5},{2,6},{3,7},{4,8},{5,9},{6,10},{7,11},{8,12},{9,13},{1... | collective-permute-start | bytes 491528 | tf_op jit(solution)/shard_map/ppermute | solution.py:34
  93.0 11.4 %collective-permute-start.30 = (bf16[640,128]{1,0:T(8,128)(2,1)S(1)}, bf16[640,128]{1,0:T(8,128)(2,1)S(1)}, u32[]{:S(2)}, u32[]{:S(2)}) collective-permute-start(bf16[640,128]{1,0:T(8,128)(2,1)S(1)} %add_convert_fusion), channel_id=1, source_target_pairs={{0,4},{1,5},{2,6},{3,7},{4,8},{5,9},{6,10},{7,11},{8,12},{9,13},{1... | collective-permute-start | bytes 491528 | tf_op jit(solution)/shard_map/ppermute | solution.py:34
  98.3 10.6 %collective-permute-start.35 = (bf16[1280,128]{1,0:T(8,128)(2,1)S(1)}, bf16[1280,128]{1,0:T(8,128)(2,1)S(1)}, u32[]{:S(2)}, u32[]{:S(2)}) collective-permute-start(bf16[1280,128]{1,0:T(8,128)(2,1)S(1)} %fusion.3), channel_id=1, source_target_pairs={{0,12},{1,13},{2,14},{3,15},{4,0},{5,1},{6,2},{7,3},{8,4},{9,5},{1... | collective-permute-start | bytes 983048 | tf_op jit(solution)/shard_map/ppermute | solution.py:34
  98.9 10.1 %collective-permute-start.33 = (bf16[1280,128]{1,0:T(8,128)(2,1)S(1)}, bf16[1280,128]{1,0:T(8,128)(2,1)S(1)}, u32[]{:S(2)}, u32[]{:S(2)}) collective-permute-start(bf16[1280,128]{1,0:T(8,128)(2,1)S(1)} %fusion.5), channel_id=1, source_target_pairs={{0,2},{1,3},{2,0},{3,1},{4,6},{5,7},{6,4},{7,5},{8,10},{9,11},{10,... | collective-permute-start | bytes 983048 | tf_op jit(solution)/shard_map/ppermute | solution.py:34

commit v15 on v13

--- a/solution.py
+++ b/solution.py
@@ -39,7 +39,7 @@
 ACROSS = pairs_of(lambda z, x: (z, 1 - x))
 NEAR0, NEAR1, NEAR2, NEAR3, FAR0, FAR1, FAR2, FAR3 = range(2 * LINE)
 ADD_AT = {(2, 1): 0, (3, 0): 1, (3, 1): 2}
-LAY_AT = (1, 1)
+RAW_AT, LAY_AT = (0, 1), (1, 1)
 
 
 def spread(parts, meanwhile):
@@ -97,7 +97,8 @@
         for index, own in enumerate((total[NEAR1], later))
     ]
     one_back = move(narrow(total[NEAR3] + wide(three_on)), BACK)
-    return total[NEAR0] + wide(straight) + wide(one_back) + wide(jnp.concatenate(one_on))
+    (result,) = tie(total[NEAR0] + wide(jnp.concatenate(one_on)))
+    return result + wide(straight) + wide(one_back)
 
 
 def clear(half):
@@ -207,10 +208,6 @@
     return pltpu.with_memory_space_constraint(array, pltpu.VMEM)
 
 
-def held(array):
-    return pltpu.with_memory_space_constraint(array, pltpu.HBM)
-
-
 def call(kernel, ins, in_specs, outs, scratch, aliases, flops, scoped=0):
     return pl.pallas_call(
         kernel,
@@ -242,7 +239,11 @@
     given = lax.dynamic_slice_in_dim(occupied, (1 - core) * LANES, LANES, 1)
     parts = [mine, move(given, swap)]
     others = [move(array, swap) for array in (block_values, block_pairs, live_counts)]
-    tile_sets = [values.reshape(slots, BLK * BLK // LANES, LANES) for values in (block_values, others[0])]
+    raw_sets = [block_values, others[0]]
+    tile_sets = []
+
+    def lay_tiles():
+        tile_sets[:] = [values.reshape(slots, BLK * BLK // LANES, LANES) for values in raw_sets]
 
     slot_ids = jnp.arange(chips, dtype=jnp.int32)
     chip_of_slot = slot_ids
@@ -294,7 +295,7 @@
             aliases = {len(ins) + 1: 0}
             ins, specs = ins + [pinned(state[1]), pinned(state[0])], specs + [VMEM] * 2
         else:
-            ins, specs = [*tables, *map(held, sources), *map(held, tile_sets)], specs + [HBM] * 2
+            ins, specs = [*tables, *sources, *tile_sets], specs + [HBM] * 2
             made = [half_type, tiles_type]
         results = call(kernel, ins, specs, made + outs, scratch, aliases, flops, 2 * rows * LANES)
         state[:] = [results[0], state[1] if state else results[1]]
@@ -305,6 +306,9 @@
         run_stage(kernel, sources, [ordered, bounds], [], work)
 
     def meanwhile(step, index, arrived, moved):
+        if (step, index) == RAW_AT:
+            moved, *raw_sets[:] = tie(moved, *raw_sets)
+            lay_tiles()
         if (step, index) == LAY_AT:
             moved, *tile_sets[:] = tie(moved, *tile_sets)
         if (step, index) in ADD_AT:
@@ -318,6 +322,7 @@
         for stage in range(len(ADD_AT), LINE):
             add(stage, stages[stage])
     else:
+        lay_tiles()
         stages = [[lax.all_gather(part, "aux", axis_index_groups=same_core, axis=0, tiled=True) for part in parts]]
 
     group = 1 if lined else chips

time: 109 us -> 105 us (0.963)
  waiting for transfers between devices: 51.5 us -> 32.3 us
  starting transfers between devices: 26.8 us -> 36.5 us
  local copies, waits for them, and re-layouts: 8.77 us -> 11.5 us
  Pallas kernels: 16.6 us -> 19.3 us
    ppermute x36, waiting for transfers between devices: 51.5 us -> 32.3 us  [move(): return lax.ppermute(array, 'aux', pairs)]
    ppermute x36, starting transfers between devices: 26.8 us -> 36.5 us  [move(): return lax.ppermute(array, 'aux', pairs)]
    pallas_call x8, Pallas kernels: 16.6 us -> 19.3 us  [call(): pl.pallas_call(kernel, out_shape=outs, in_specs=in_specs, out_specs=[VMEM...]
    unnamed x7 -> x17, local copies, waits for them, and re-layouts: 7.55 us -> 10.2 us
  transfers between devices with their start and end apart: 36 -> 36, of which waited for: 16 -> 15; matrix products, arithmetic and copies ran while one was open for 11% -> 10% of each run, Pallas kernels for 13% -> 16%
where the time goes in v15:
time: 105 us
  starting transfers between devices  36.5 us (35%)
  waiting for transfers between devices  32.3 us (31%)
  Pallas kernels  19.3 us (18%)
  local copies, waits for them, and re-layouts  11.5 us (11%)
  other arithmetic  4.04 us (4%)
    ppermute x36, starting transfers between devices, move(): return lax.ppermute(array, 'aux', pairs)  36.5 us
    ppermute x36, waiting for transfers between devices, move(): return lax.ppermute(array, 'aux', pairs)  32.3 us
    pallas_call x8, Pallas kernels, call(): pl.pallas_call(kernel, out_shape=outs, in_specs=in_specs, out_specs=[VMEM...  19.3 us
    unnamed x17, local copies, waits for them, and re-layouts  10.2 us
  transfers between devices with their start and end apart: 36, of which 15 were waited for; matrix products, arithmetic and copies ran while one was open for 10% of the time, Pallas kernels for 16%

profile of v15, /device:TPU:0, one launch (start us, length us, event | category | flops | bytes accessed | tf_op | source)
XLA Modules:
  0.0 104.6 jit_solution(17784865151762596988)
XLA Ops:
  0.0 0.5 collective-permute-start.9
  0.5 1.1 %constant_dynamic-slice_fusion.1 = (bf16[1280,128]{1,0:T(8,128)(2,1)S(1)}, bf16[1280,128]{1,0:T(8,128)(2,1)S(1)}) fusion(bf16[1280,256]{1,0:T(8,128)(2,1)} %param.7, s32[]{:T(128)S(6)} %select_n.162, s32[]{:T(128)S(6)} %select_n.161), kind=kLoop, calls=%fused_computation.91 | loop fusion | bytes 1310728 | tf_op jit(solution)/shard_map/dynamic_slice | solution.py:239
  1.6 2.6 %collective-permute-start.2 = (bf16[1280,128]{1,0:T(8,128)(2,1)S(1)}, bf16[1280,128]{1,0:T(8,128)(2,1)S(1)}, u32[]{:S(2)}, u32[]{:S(2)}) collective-permute-start(bf16[1280,128]{1,0:T(8,128)(2,1)S(1)} %get-tuple-element.123.refs_0_), channel_id=1, source_target_pairs={{0,4},{1,5},{2,6},{3,7},{4,8},{5,9},{6,10},{7,11},{8,12},{9,13},{1... | collective-permute-start | bytes 983048 | tf_op jit(solution)/shard_map/ppermute | solution.py:34
  4.2 1.5 %collective-permute-start.3 = (bf16[1280,128]{1,0:T(8,128)(2,1)S(1)}, bf16[1280,128]{1,0:T(8,128)(2,1)S(1)}, u32[]{:S(2)}, u32[]{:S(2)}) collective-permute-start(bf16[1280,128]{1,0:T(8,128)(2,1)S(1)} %get-tuple-element.123.refs_0_), channel_id=1, source_target_pairs={{0,2},{1,3},{2,0},{3,1},{4,6},{5,7},{6,4},{7,5},{8,10},{9,11},{10,... | collective-permute-start | bytes 983048 | tf_op jit(solution)/shard_map/ppermute | solution.py:34
  5.7 0.5 collective-permute-start
  6.2 0.7 constant_dynamic-update-slice_fusion.1
  7.7 0.6 compare_select_fusion.3
  8.3 0.9 collective-permute-done.8.refs_1_
  9.3 1.6 %collective-permute-start.10 = (bf16[1280,128]{1,0:T(8,128)(2,1)S(1)}, bf16[1280,128]{1,0:T(8,128)(2,1)S(1)}, u32[]{:S(2)}, u32[]{:S(2)}) collective-permute-start(bf16[1280,128]{1,0:T(8,128)(2,1)S(1)} %collective-permute-done.8.refs_1_), channel_id=1, source_target_pairs={{0,4},{1,5},{2,6},{3,7},{4,8},{5,9},{6,10},{7,11},{8,12},{9,13},{1... | collective-permute-start | bytes 983048 | tf_op jit(solution)/shard_map/ppermute | solution.py:34
  10.8 0.5 collective-permute-start.11
  11.4 0.6 fusion.27
  12.0 2.8 %collective-permute-done.2.refs_0_ = bf16[1280,128]{1,0:T(8,128)(2,1)S(1)} collective-permute-done((bf16[1280,128]{1,0:T(8,128)(2,1)S(1)}, bf16[1280,128]{1,0:T(8,128)(2,1)S(1)}, u32[]{:S(2)}, u32[]{:S(2)}) %collective-permute-start.2) | collective-permute-done | bytes 327712 | tf_op jit(solution)/shard_map/ppermute | solution.py:34
  14.8 1.5 %collective-permute-start.4 = (bf16[1280,128]{1,0:T(8,128)(2,1)S(1)}, bf16[1280,128]{1,0:T(8,128)(2,1)}, u32[]{:S(2)}, u32[]{:S(2)}) collective-permute-start(bf16[1280,128]{1,0:T(8,128)(2,1)S(1)} %collective-permute-done.2.refs_0_), channel_id=1, source_target_pairs={{0,4},{1,5},{2,6},{3,7},{4,8},{5,9},{6,10},{7,11},{8,12},{9,13},{1... | collective-permute-start | bytes 983048 | tf_op jit(solution)/shard_map/ppermute | solution.py:34
  16.3 1.5 %collective-permute-start.5 = (bf16[1280,128]{1,0:T(8,128)(2,1)S(1)}, bf16[1280,128]{1,0:T(8,128)(2,1)S(1)}, u32[]{:S(2)}, u32[]{:S(2)}) collective-permute-start(bf16[1280,128]{1,0:T(8,128)(2,1)S(1)} %collective-permute-done.2.refs_0_), channel_id=1, source_target_pairs={{0,2},{1,3},{2,0},{3,1},{4,6},{5,7},{6,4},{7,5},{8,10},{9,11},{10,... | collective-permute-start | bytes 983048 | tf_op jit(solution)/shard_map/ppermute | solution.py:34
  17.8 2.1 %copy.9 = bf16[32,8,32,128]{3,2,1,0:T(8,128)(2,1)S(1)} copy(bf16[32,8,32,128]{3,1,2,0:T(8,128)(2,1)} %bitcast.63) | data formatting | bytes 4194304
  19.9 3.4 %copy.10 = bf16[32,8,32,128]{3,2,1,0:T(8,128)(2,1)} copy(bf16[32,8,32,128]{3,1,2,0:T(8,128)(2,1)} %bitcast.25) | data formatting | bytes 4194304
  23.3 0.7 copy-done.1
  24.1 1.6 %collective-permute-start.12 = (bf16[1280,128]{1,0:T(8,128)(2,1)S(1)}, bf16[1280,128]{1,0:T(8,128)(2,1)}, u32[]{:S(2)}, u32[]{:S(2)}) collective-permute-start(bf16[1280,128]{1,0:T(8,128)(2,1)S(1)} %collective-permute-done.10.refs_1_), channel_id=1, source_target_pairs={{0,4},{1,5},{2,6},{3,7},{4,8},{5,9},{6,10},{7,11},{8,12},{9,13},{1... | collective-permute-start | bytes 983048 | tf_op jit(solution)/shard_map/ppermute | solution.py:34
  25.6 0.5 collective-permute-start.13
  26.2 0.3 convert_reduce_fusion
  26.5 0.5 select_reduce_fusion
  27.0 1.9 %collective-permute-done.4.refs_0_ = bf16[1280,128]{1,0:T(8,128)(2,1)} collective-permute-done((bf16[1280,128]{1,0:T(8,128)(2,1)S(1)}, bf16[1280,128]{1,0:T(8,128)(2,1)}, u32[]{:S(2)}, u32[]{:S(2)}) %collective-permute-start.4) | collective-permute-done | bytes 327712 | tf_op jit(solution)/shard_map/ppermute | solution.py:34
  28.9 0.7 copy-done.3
  29.7 1.4 %collective-permute-start.6 = (bf16[1280,128]{1,0:T(8,128)(2,1)}, bf16[1280,128]{1,0:T(8,128)(2,1)}, u32[]{:S(2)}, u32[]{:S(2)}) collective-permute-start(bf16[1280,128]{1,0:T(8,128)(2,1)} %collective-permute-done.4.refs_0_), channel_id=1, source_target_pairs={{0,4},{1,5},{2,6},{3,7},{4,8},{5,9},{6,10},{7,11},{8,12},{9,13},{1... | collective-permute-start | bytes 983048 | tf_op jit(solution)/shard_map/ppermute | solution.py:34
  31.1 1.5 %collective-permute-start.7 = (bf16[1280,128]{1,0:T(8,128)(2,1)}, bf16[1280,128]{1,0:T(8,128)(2,1)}, u32[]{:S(2)}, u32[]{:S(2)}) collective-permute-start(bf16[1280,128]{1,0:T(8,128)(2,1)} %collective-permute-done.4.refs_0_), channel_id=1, source_target_pairs={{0,2},{1,3},{2,0},{3,1},{4,6},{5,7},{6,4},{7,5},{8,10},{9,11},{10,... | collective-permute-start | bytes 983048 | tf_op jit(solution)/shard_map/ppermute | solution.py:34
  32.8 1.6 %copy-done = bf16[32,8,32,128]{3,2,1,0:T(8,128)(2,1)S(1)} copy-done((bf16[32,8,32,128]{3,2,1,0:T(8,128)(2,1)S(1)}, bf16[32,8,32,128]{3,2,1,0:T(8,128)(2,1)}, u32[]{:S(2)}) %copy-start) | copy-done | bytes 2097176
  34.4 1.0 copy-done.6
  35.4 3.5 %shard_map.46 = (f32[41024,128]{1,0:T(8,128)S(1)}, bf16[512,32,128]{2,1,0:T(8,128)(2,1)S(1)}) custom-call(s32[1584]{0:T(1024)S(1)} %concatenate.10.table_ref, s32[6]{0:T(128)S(1)} %convert_reduce_fusion.1.bounds_ref, bf16[1280,128]{1,0:T(8,128)(2,1)S(1)} %get-tuple-element.123.refs_0_, bf16[1280,128]{1,0:T(8,128)(2,1)S(1)} %copy-done.6, ...), custom_call_target="tpu_custom_call" | custom-call | flops 107374184 | bytes 4194304 | tf_op jit(solution)/shard_map/pallas_call | solution.py:212
  38.9 2.5 %collective-permute-start.15 = (bf16[1280,128]{1,0:T(8,128)(2,1)}, bf16[1280,128]{1,0:T(8,128)(2,1)S(1)}, u32[]{:S(2)}, u32[]{:S(2)}) collective-permute-start(bf16[1280,128]{1,0:T(8,128)(2,1)} %collective-permute-done.12.refs_1_), channel_id=1, source_target_pairs={{0,4},{1,5},{2,6},{3,7},{4,8},{5,9},{6,10},{7,11},{8,12},{9,13},{1... | collective-permute-start | bytes 983048 | tf_op jit(solution)/shard_map/ppermute | solution.py:34
  41.4 2.2 %collective-permute-done.6.refs_0_ = bf16[1280,128]{1,0:T(8,128)(2,1)} collective-permute-done((bf16[1280,128]{1,0:T(8,128)(2,1)}, bf16[1280,128]{1,0:T(8,128)(2,1)}, u32[]{:S(2)}, u32[]{:S(2)}) %collective-permute-start.6) | collective-permute-done | bytes 327712 | tf_op jit(solution)/shard_map/ppermute | solution.py:34
  43.7 2.5 %shard_map.47.refs_5_ = f32[41024,128]{1,0:T(8,128)S(1)} custom-call(s32[1584]{0:T(1024)S(1)} %concatenate.10.table_ref, s32[6]{0:T(128)S(1)} %convert_reduce_fusion.1.bounds_ref, bf16[1280,128]{1,0:T(8,128)(2,1)S(1)} %collective-permute-done.2.refs_0_, bf16[1280,128]{1,0:T(8,128)(2,1)S(1)} %collective-permute-done.10.refs_1_, ...), custom_call_target="tpu_custom_call", output_to_operand_aliasing={{}: (7, {})} | custom-call | flops 107374184 | bytes 4194304 | tf_op jit(solution)/shard_map/pallas_call | solution.py:212
  46.2 1.5 %collective-permute-start.14 = (bf16[1280,128]{1,0:T(8,128)(2,1)}, bf16[1280,128]{1,0:T(8,128)(2,1)S(1)}, u32[]{:S(2)}, u32[]{:S(2)}) collective-permute-start(bf16[1280,128]{1,0:T(8,128)(2,1)} %collective-permute-done.7.refs_2_), channel_id=1, source_target_pairs={{0,4},{1,5},{2,6},{3,7},{4,8},{5,9},{6,10},{7,11},{8,12},{9,13},{1... | collective-permute-start | bytes 983048 | tf_op jit(solution)/shard_map/ppermute | solution.py:34
  47.7 3.3 %shard_map.48.refs_5_ = f32[41024,128]{1,0:T(8,128)S(1)} custom-call(s32[1584]{0:T(1024)S(1)} %concatenate.10.table_ref, s32[6]{0:T(128)S(1)} %convert_reduce_fusion.1.bounds_ref, bf16[1280,128]{1,0:T(8,128)(2,1)} %collective-permute-done.4.refs_0_, bf16[1280,128]{1,0:T(8,128)(2,1)} %collective-permute-done.12.refs_1_, ...), custom_call_target="tpu_custom_call", output_to_operand_aliasing={{}: (7, {})} | custom-call | flops 107374184 | bytes 4194304 | tf_op jit(solution)/shard_map/pallas_call | solution.py:212
  51.0 1.3 %collective-permute-start.17 = (bf16[1280,128]{1,0:T(8,128)(2,1)S(1)}, bf16[1280,128]{1,0:T(8,128)(2,1)S(1)}, u32[]{:S(2)}, u32[]{:S(2)}) collective-permute-start(bf16[1280,128]{1,0:T(8,128)(2,1)S(1)} %collective-permute-done.15.refs_1_), channel_id=1, source_target_pairs={{0,2},{1,3},{2,0},{3,1},{4,6},{5,7},{6,4},{7,5},{8,10},{9,11},{10,... | collective-permute-start | bytes 983048 | tf_op jit(solution)/shard_map/ppermute | solution.py:34
  52.3 3.2 %shard_map.49.refs_3_ = f32[41024,128]{1,0:T(8,128)S(1)} custom-call(s32[1584]{0:T(1024)S(1)} %concatenate.10.table_ref, s32[6]{0:T(128)S(1)} %convert_reduce_fusion.1.bounds_ref, bf16[1280,128]{1,0:T(8,128)(2,1)} %collective-permute-done.6.refs_0_, bf16[1280,128]{1,0:T(8,128)(2,1)S(1)} %collective-permute-done.15.refs_1_, ...), custom_call_target="tpu_custom_call", output_to_operand_aliasing={{}: (7, {})} | custom-call | flops 107374184 | bytes 4194304 | tf_op jit(solution)/shard_map/pallas_call | solution.py:212
  55.4 1.3 %collective-permute-done.14.refs_0_ = bf16[1280,128]{1,0:T(8,128)(2,1)S(1)} collective-permute-done((bf16[1280,128]{1,0:T(8,128)(2,1)}, bf16[1280,128]{1,0:T(8,128)(2,1)S(1)}, u32[]{:S(2)}, u32[]{:S(2)}) %collective-permute-start.14) | collective-permute-done | bytes 327712 | tf_op jit(solution)/shard_map/ppermute | solution.py:34
  56.7 2.3 %collective-permute-done.17.refs_1_ = bf16[1280,128]{1,0:T(8,128)(2,1)S(1)} collective-permute-done((bf16[1280,128]{1,0:T(8,128)(2,1)S(1)}, bf16[1280,128]{1,0:T(8,128)(2,1)S(1)}, u32[]{:S(2)}, u32[]{:S(2)}) %collective-permute-start.17) | collective-permute-done | bytes 327712 | tf_op jit(solution)/shard_map/ppermute | solution.py:34
  59.1 2.5 %shard_map.50 = (f32[41024,128]{1,0:T(8,128)S(1)}, bf16[256,128]{1,0:T(8,128)(2,1)S(1)}, bf16[1,1280,128]{2,1,0:T(8,128)(2,1)S(1)}, bf16[1,1280,128]{2,1,0:T(8,128)(2,1)S(1)}, bf16[1,1280,128]{2,1,0:T(8,128)(2,1)S(1)}) custom-call(s32[1584]{0:T(1024)S(1)} %concatenate.10.table_ref, ...), custom_call_target="tpu_custom_call", output_to_operand_aliasing={{0}: (7, {})} | custom-call | flops 359032416 | bytes 4194304 | tf_op jit(solution)/shard_map/pallas_call | solution.py:212
  61.7 0.5 collective-permute-start.19
  62.3 1.2 %shard_map.51 = (f32[1,1280,128]{2,1,0:T(8,128)S(1)}, f32[1,1280,128]{2,1,0:T(8,128)S(1)}, f32[1,1280,128]{2,1,0:T(8,128)S(1)}) custom-call(s32[8]{0:T(128)S(1)} %fusion.30.chips_ref, s32[1]{0:T(128)} %bitcast.core_ref, f32[41024,128]{1,0:T(8,128)S(1)} %get-tuple-element.91.half, bf16[256,128]{1,0:T(8,128)(2,1)S(1)} %get-tuple-element.86.weights), custom_call_target="tpu_custom_call" | custom-call | flops 251658240 | bytes 4194304 | tf_op jit(solution)/shard_map/pallas_call | solution.py:212
  63.5 0.3 collective-permute-done.19
  64.0 1.6 %shard_map.53 = (bf16[1,1280,128]{2,1,0:T(8,128)(2,1)S(1)}, bf16[1,1280,128]{2,1,0:T(8,128)(2,1)S(1)}, bf16[1,1280,128]{2,1,0:T(8,128)(2,1)S(1)}, bf16[1,1280,12...) custom-call(s32[8]{0:T(128)S(1)} %fusion.30.chips_ref, s32[1]{0:T(128)} %bitcast.core_ref, ...), custom_call_target="tpu_custom_call" | custom-call | flops 419430400 | bytes 4194304 | tf_op jit(solution)/shard_map/pallas_call | solution.py:212
  65.5 0.2 collective-permute-start.21
  65.7 0.3 collective-permute-start.26
  66.1 1.5 %collective-permute-start.27 = (bf16[640,128]{1,0:T(8,128)(2,1)S(1)}, bf16[640,128]{1,0:T(8,128)(2,1)S(1)}, u32[]{:S(2)}, u32[]{:S(2)}) collective-permute-start(bf16[640,128]{1,0:T(8,128)(2,1)S(1)} %get-tuple-element.103), channel_id=1, source_target_pairs={{0,2},{1,3},{2,0},{3,1},{4,6},{5,7},{6,4},{7,5},{8,10},{9,11},{10,... | collective-permute-start | bytes 491528 | tf_op jit(solution)/shard_map/ppermute | solution.py:34
  67.6 0.6 collective-permute-start.23
  68.1 1.5 %shard_map.52 = (f32[1,1280,128]{2,1,0:T(8,128)S(1)}, f32[1,1280,128]{2,1,0:T(8,128)S(1)}, f32[1,1280,128]{2,1,0:T(8,128)S(1)}, f32[1,1280,128]{2,1,0:T(8,128)S(1)}, f32[1,1280,128]{2,1,0:T(8,128)S(1)}) custom-call(s32[8]{0:T(128)S(1)} %fusion.30.chips_ref, s32[1]{0:T(128)} %bitcast.core_ref, f32[41024,128]{1,0:T(8,128)S(1)} %get-tuple-element.91.half, ...), custom_call_target="tpu_custom_call" | custom-call | flops 419430400 | bytes 4194304 | tf_op jit(solution)/shard_map/pallas_call | solution.py:212
  69.8 2.2 %collective-permute-start.31 = (bf16[1280,128]{1,0:T(8,128)(2,1)S(1)}, bf16[1280,128]{1,0:T(8,128)(2,1)S(1)}, u32[]{:S(2)}, u32[]{:S(2)}) collective-permute-start(bf16[1280,128]{1,0:T(8,128)(2,1)S(1)} %get-tuple-element.107), channel_id=1, source_target_pairs={{0,4},{1,5},{2,6},{3,7},{4,8},{5,9},{6,10},{7,11},{8,12},{9,13},{1... | collective-permute-start | bytes 983048 | tf_op jit(solution)/shard_map/ppermute | solution.py:34
  72.1 1.0 collective-permute-done.27
  73.1 2.7 %collective-permute-done.23 = bf16[640,128]{1,0:T(8,128)(2,1)S(1)} collective-permute-done((bf16[640,128]{1,0:T(8,128)(2,1)S(1)}, bf16[640,128]{1,0:T(8,128)(2,1)S(1)}, u32[]{:S(2)}, u32[]{:S(2)}) %collective-permute-start.23) | collective-permute-done | bytes 163872 | tf_op jit(solution)/shard_map/ppermute | solution.py:34
  76.0 2.2 %collective-permute-start.24 = (bf16[640,128]{1,0:T(8,128)(2,1)S(1)}, bf16[640,128]{1,0:T(8,128)(2,1)S(1)}, u32[]{:S(2)}, u32[]{:S(2)}) collective-permute-start(bf16[640,128]{1,0:T(8,128)(2,1)S(1)} %get-tuple-element.120), channel_id=1, source_target_pairs={{0,4},{1,5},{2,6},{3,7},{4,8},{5,9},{6,10},{7,11},{8,12},{9,13},{1... | collective-permute-start | bytes 491528 | tf_op jit(solution)/shard_map/ppermute | solution.py:34
  78.2 4.0 %collective-permute-done.31 = bf16[1280,128]{1,0:T(8,128)(2,1)S(1)} collective-permute-done((bf16[1280,128]{1,0:T(8,128)(2,1)S(1)}, bf16[1280,128]{1,0:T(8,128)(2,1)S(1)}, u32[]{:S(2)}, u32[]{:S(2)}) %collective-permute-start.31) | collective-permute-done | bytes 327712 | tf_op jit(solution)/shard_map/ppermute | solution.py:34
  82.2 0.3 collective-permute-start.28
  82.7 1.6 %collective-permute-start.32 = (bf16[1280,128]{1,0:T(8,128)(2,1)S(1)}, bf16[1280,128]{1,0:T(8,128)(2,1)S(1)}, u32[]{:S(2)}, u32[]{:S(2)}) collective-permute-start(bf16[1280,128]{1,0:T(8,128)(2,1)S(1)} %fusion.6), channel_id=1, source_target_pairs={{0,2},{1,3},{2,0},{3,1},{4,6},{5,7},{6,4},{7,5},{8,10},{9,11},{10,... | collective-permute-start | bytes 983048 | tf_op jit(solution)/shard_map/ppermute | solution.py:34
  84.3 1.1 %collective-permute-done.24 = bf16[640,128]{1,0:T(8,128)(2,1)S(1)} collective-permute-done((bf16[640,128]{1,0:T(8,128)(2,1)S(1)}, bf16[640,128]{1,0:T(8,128)(2,1)S(1)}, u32[]{:S(2)}, u32[]{:S(2)}) %collective-permute-start.24) | collective-permute-done | bytes 163872 | tf_op jit(solution)/shard_map/ppermute | solution.py:34
  85.4 0.8 collective-permute-start.25
  86.1 3.3 %collective-permute-done.28 = bf16[640,128]{1,0:T(8,128)(2,1)S(1)} collective-permute-done((bf16[640,128]{1,0:T(8,128)(2,1)S(1)}, bf16[640,128]{1,0:T(8,128)(2,1)S(1)}, u32[]{:S(2)}, u32[]{:S(2)}) %collective-permute-start.28) | collective-permute-done | bytes 163872 | tf_op jit(solution)/shard_map/ppermute | solution.py:34
  89.5 0.2 collective-permute-start.29
  89.8 2.0 %collective-permute-done.32 = bf16[1280,128]{1,0:T(8,128)(2,1)S(1)} collective-permute-done((bf16[1280,128]{1,0:T(8,128)(2,1)S(1)}, bf16[1280,128]{1,0:T(8,128)(2,1)S(1)}, u32[]{:S(2)}, u32[]{:S(2)}) %collective-permute-start.32) | collective-permute-done | bytes 327712 | tf_op jit(solution)/shard_map/ppermute | solution.py:34
  92.0 3.6 %collective-permute-start.35 = (bf16[1280,128]{1,0:T(8,128)(2,1)S(1)}, bf16[1280,128]{1,0:T(8,128)(2,1)S(1)}, u32[]{:S(2)}, u32[]{:S(2)}) collective-permute-start(bf16[1280,128]{1,0:T(8,128)(2,1)S(1)} %fusion.3), channel_id=1, source_target_pairs={{0,12},{1,13},{2,14},{3,15},{4,0},{5,1},{6,2},{7,3},{8,4},{9,5},{1... | collective-permute-start | bytes 983048 | tf_op jit(solution)/shard_map/ppermute | solution.py:34
  95.5 1.7 %collective-permute-start.33 = (bf16[1280,128]{1,0:T(8,128)(2,1)S(1)}, bf16[1280,128]{1,0:T(8,128)(2,1)S(1)}, u32[]{:S(2)}, u32[]{:S(2)}) collective-permute-start(bf16[1280,128]{1,0:T(8,128)(2,1)S(1)} %fusion.5), channel_id=1, source_target_pairs={{0,2},{1,3},{2,0},{3,1},{4,6},{5,7},{6,4},{7,5},{8,10},{9,11},{10,... | collective-permute-start | bytes 983048 | tf_op jit(solution)/shard_map/ppermute | solution.py:34
  97.3 1.1 %collective-permute-done.29 = bf16[640,128]{1,0:T(8,128)(2,1)S(1)} collective-permute-done((bf16[640,128]{1,0:T(8,128)(2,1)S(1)}, bf16[640,128]{1,0:T(8,128)(2,1)S(1)}, u32[]{:S(2)}, u32[]{:S(2)}) %collective-permute-start.29) | collective-permute-done | bytes 163872 | tf_op jit(solution)/shard_map/ppermute | solution.py:34
  98.5 5.1 %collective-permute-done.35 = bf16[1280,128]{1,0:T(8,128)(2,1)S(1)} collective-permute-done((bf16[1280,128]{1,0:T(8,128)(2,1)S(1)}, bf16[1280,128]{1,0:T(8,128)(2,1)S(1)}, u32[]{:S(2)}, u32[]{:S(2)}) %collective-permute-start.35) | collective-permute-done | bytes 327712 | tf_op jit(solution)/shard_map/ppermute | solution.py:34
  103.6 0.9 add_multiply_fusion
  (56 shorter events, 1.5 us)
Async XLA Ops:
  0.0 9.3 %collective-permute-start.9 = (bf16[256,4096]{1,0:T(8,128)(2,1)}, bf16[256,4096]{1,0:T(8,128)(2,1)}, u32[]{:S(2)}, u32[]{:S(2)}) collective-permute-start(bf16[256,4096]{1,0:T(8,128)(2,1)} %param.4), channel_id=1, source_target_pairs={{0,1},{1,0},{2,3},{3,2},{4,5},{5,4},{6,7},{7,6},{8,9},{9,8},{10,11... | collective-permute-start | bytes 6291464 | tf_op jit(solution)/shard_map/ppermute | solution.py:34
  1.6 13.2 %collective-permute-start.2 = (bf16[1280,128]{1,0:T(8,128)(2,1)S(1)}, bf16[1280,128]{1,0:T(8,128)(2,1)S(1)}, u32[]{:S(2)}, u32[]{:S(2)}) collective-permute-start(bf16[1280,128]{1,0:T(8,128)(2,1)S(1)} %get-tuple-element.123.refs_0_), channel_id=1, source_target_pairs={{0,4},{1,5},{2,6},{3,7},{4,8},{5,9},{6,10},{7,11},{8,12},{9,13},{1... | collective-permute-start | bytes 983048 | tf_op jit(solution)/shard_map/ppermute | solution.py:34
  4.2 10.6 %collective-permute-start.3 = (bf16[1280,128]{1,0:T(8,128)(2,1)S(1)}, bf16[1280,128]{1,0:T(8,128)(2,1)S(1)}, u32[]{:S(2)}, u32[]{:S(2)}) collective-permute-start(bf16[1280,128]{1,0:T(8,128)(2,1)S(1)} %get-tuple-element.123.refs_0_), channel_id=1, source_target_pairs={{0,2},{1,3},{2,0},{3,1},{4,6},{5,7},{6,4},{7,5},{8,10},{9,11},{10,... | collective-permute-start | bytes 983048 | tf_op jit(solution)/shard_map/ppermute | solution.py:34
  5.7 1.9 %collective-permute-start.1 = (s32[256,2]{0,1:T(2,128)}, s32[256,2]{0,1:T(2,128)S(1)}, u32[]{:S(2)}, u32[]{:S(2)}) collective-permute-start(s32[256,2]{0,1:T(2,128)} %param.5), channel_id=1, source_target_pairs={{0,1},{1,0},{2,3},{3,2},{4,5},{5,4},{6,7},{7,6},{8,9},{9,8},{10,11... | collective-permute-start | bytes 6152 | tf_op jit(solution)/shard_map/ppermute | solution.py:34
  5.7 2.0 %collective-permute-start = (s32[1]{0:T(128)}, s32[1]{0:T(128)}, u32[]{:S(2)}, u32[]{:S(2)}) collective-permute-start(s32[1]{0:T(128)} %param.6), channel_id=1, source_target_pairs={{0,1},{1,0},{2,3},{3,2},{4,5},{5,4},{6,7},{7,6},{8,9},{9,8},{10,11... | collective-permute-start | bytes 20 | tf_op jit(solution)/shard_map/ppermute | solution.py:34
  7.6 1.7 %collective-permute-start.8 = (bf16[1280,128]{1,0:T(8,128)(2,1)S(1)}, bf16[1280,128]{1,0:T(8,128)(2,1)S(1)}, u32[]{:S(2)}, u32[]{:S(2)}) collective-permute-start(bf16[1280,128]{1,0:T(8,128)(2,1)S(1)} %get-tuple-element.122), channel_id=1, source_target_pairs={{0,1},{1,0},{2,3},{3,2},{4,5},{5,4},{6,7},{7,6},{8,9},{9,8},{10,11... | collective-permute-start | bytes 983048 | tf_op jit(solution)/shard_map/ppermute | solution.py:34
  9.3 10.6 %copy-start.5 = (bf16[1280,128]{1,0:T(8,128)(2,1)}, bf16[1280,128]{1,0:T(8,128)(2,1)S(1)}, u32[]{:S(2)}) copy-start(bf16[1280,128]{1,0:T(8,128)(2,1)S(1)} %collective-permute-done.8.refs_1_) | copy-start | bytes 983044
  9.3 14.1 %collective-permute-start.10 = (bf16[1280,128]{1,0:T(8,128)(2,1)S(1)}, bf16[1280,128]{1,0:T(8,128)(2,1)S(1)}, u32[]{:S(2)}, u32[]{:S(2)}) collective-permute-start(bf16[1280,128]{1,0:T(8,128)(2,1)S(1)} %collective-permute-done.8.refs_1_), channel_id=1, source_target_pairs={{0,4},{1,5},{2,6},{3,7},{4,8},{5,9},{6,10},{7,11},{8,12},{9,13},{1... | collective-permute-start | bytes 983048 | tf_op jit(solution)/shard_map/ppermute | solution.py:34
  10.8 12.5 %collective-permute-start.11 = (bf16[1280,128]{1,0:T(8,128)(2,1)S(1)}, bf16[1280,128]{1,0:T(8,128)(2,1)S(1)}, u32[]{:S(2)}, u32[]{:S(2)}) collective-permute-start(bf16[1280,128]{1,0:T(8,128)(2,1)S(1)} %collective-permute-done.8.refs_1_), channel_id=1, source_target_pairs={{0,2},{1,3},{2,0},{3,1},{4,6},{5,7},{6,4},{7,5},{8,10},{9,11},{10,... | collective-permute-start | bytes 983048 | tf_op jit(solution)/shard_map/ppermute | solution.py:34
  14.8 14.1 %collective-permute-start.4 = (bf16[1280,128]{1,0:T(8,128)(2,1)S(1)}, bf16[1280,128]{1,0:T(8,128)(2,1)}, u32[]{:S(2)}, u32[]{:S(2)}) collective-permute-start(bf16[1280,128]{1,0:T(8,128)(2,1)S(1)} %collective-permute-done.2.refs_0_), channel_id=1, source_target_pairs={{0,4},{1,5},{2,6},{3,7},{4,8},{5,9},{6,10},{7,11},{8,12},{9,13},{1... | collective-permute-start | bytes 983048 | tf_op jit(solution)/shard_map/ppermute | solution.py:34
  16.3 12.6 %collective-permute-start.5 = (bf16[1280,128]{1,0:T(8,128)(2,1)S(1)}, bf16[1280,128]{1,0:T(8,128)(2,1)S(1)}, u32[]{:S(2)}, u32[]{:S(2)}) collective-permute-start(bf16[1280,128]{1,0:T(8,128)(2,1)S(1)} %collective-permute-done.2.refs_0_), channel_id=1, source_target_pairs={{0,2},{1,3},{2,0},{3,1},{4,6},{5,7},{6,4},{7,5},{8,10},{9,11},{10,... | collective-permute-start | bytes 983048 | tf_op jit(solution)/shard_map/ppermute | solution.py:34
  23.3 0.8 copy-start.1
  24.1 14.8 %collective-permute-start.12 = (bf16[1280,128]{1,0:T(8,128)(2,1)S(1)}, bf16[1280,128]{1,0:T(8,128)(2,1)}, u32[]{:S(2)}, u32[]{:S(2)}) collective-permute-start(bf16[1280,128]{1,0:T(8,128)(2,1)S(1)} %collective-permute-done.10.refs_1_), channel_id=1, source_target_pairs={{0,4},{1,5},{2,6},{3,7},{4,8},{5,9},{6,10},{7,11},{8,12},{9,13},{1... | collective-permute-start | bytes 983048 | tf_op jit(solution)/shard_map/ppermute | solution.py:34
  25.6 13.3 %collective-permute-start.13 = (bf16[1280,128]{1,0:T(8,128)(2,1)S(1)}, bf16[1280,128]{1,0:T(8,128)(2,1)}, u32[]{:S(2)}, u32[]{:S(2)}) collective-permute-start(bf16[1280,128]{1,0:T(8,128)(2,1)S(1)} %collective-permute-done.10.refs_1_), channel_id=1, source_target_pairs={{0,2},{1,3},{2,0},{3,1},{4,6},{5,7},{6,4},{7,5},{8,10},{9,11},{10,... | collective-permute-start | bytes 983048 | tf_op jit(solution)/shard_map/ppermute | solution.py:34
  28.9 0.7 copy-start.3
  29.7 14.0 %collective-permute-start.6 = (bf16[1280,128]{1,0:T(8,128)(2,1)}, bf16[1280,128]{1,0:T(8,128)(2,1)}, u32[]{:S(2)}, u32[]{:S(2)}) collective-permute-start(bf16[1280,128]{1,0:T(8,128)(2,1)} %collective-permute-done.4.refs_0_), channel_id=1, source_target_pairs={{0,4},{1,5},{2,6},{3,7},{4,8},{5,9},{6,10},{7,11},{8,12},{9,13},{1... | collective-permute-start | bytes 983048 | tf_op jit(solution)/shard_map/ppermute | solution.py:34
  31.1 12.5 %collective-permute-start.7 = (bf16[1280,128]{1,0:T(8,128)(2,1)}, bf16[1280,128]{1,0:T(8,128)(2,1)}, u32[]{:S(2)}, u32[]{:S(2)}) collective-permute-start(bf16[1280,128]{1,0:T(8,128)(2,1)} %collective-permute-done.4.refs_0_), channel_id=1, source_target_pairs={{0,2},{1,3},{2,0},{3,1},{4,6},{5,7},{6,4},{7,5},{8,10},{9,11},{10,... | collective-permute-start | bytes 983048 | tf_op jit(solution)/shard_map/ppermute | solution.py:34
  32.8 1.6 %copy-start = (bf16[32,8,32,128]{3,2,1,0:T(8,128)(2,1)S(1)}, bf16[32,8,32,128]{3,2,1,0:T(8,128)(2,1)}, u32[]{:S(2)}) copy-start(bf16[32,8,32,128]{3,2,1,0:T(8,128)(2,1)} %copy.10) | copy-start | bytes 6291460
  34.4 1.0 copy-start.6
  35.4 8.3 %copy-start.2 = (bf16[1280,128]{1,0:T(8,128)(2,1)S(1)}, bf16[1280,128]{1,0:T(8,128)(2,1)}, u32[]{:S(2)}) copy-start(bf16[1280,128]{1,0:T(8,128)(2,1)} %copy-done.1) | copy-start | bytes 983044
  38.9 12.0 %collective-permute-start.15 = (bf16[1280,128]{1,0:T(8,128)(2,1)}, bf16[1280,128]{1,0:T(8,128)(2,1)S(1)}, u32[]{:S(2)}, u32[]{:S(2)}) collective-permute-start(bf16[1280,128]{1,0:T(8,128)(2,1)} %collective-permute-done.12.refs_1_), channel_id=1, source_target_pairs={{0,4},{1,5},{2,6},{3,7},{4,8},{5,9},{6,10},{7,11},{8,12},{9,13},{1... | collective-permute-start | bytes 983048 | tf_op jit(solution)/shard_map/ppermute | solution.py:34
  41.4 9.5 %collective-permute-start.16 = (bf16[1280,128]{1,0:T(8,128)(2,1)}, bf16[1280,128]{1,0:T(8,128)(2,1)S(1)}, u32[]{:S(2)}, u32[]{:S(2)}) collective-permute-start(bf16[1280,128]{1,0:T(8,128)(2,1)} %collective-permute-done.12.refs_1_), channel_id=1, source_target_pairs={{0,2},{1,3},{2,0},{3,1},{4,6},{5,7},{6,4},{7,5},{8,10},{9,11},{10,... | collective-permute-start | bytes 983048 | tf_op jit(solution)/shard_map/ppermute | solution.py:34
  43.7 4.0 %copy-start.4 = (bf16[1280,128]{1,0:T(8,128)(2,1)S(1)}, bf16[1280,128]{1,0:T(8,128)(2,1)}, u32[]{:S(2)}) copy-start(bf16[1280,128]{1,0:T(8,128)(2,1)} %copy-done.3) | copy-start | bytes 983044
  46.2 10.6 %collective-permute-start.14 = (bf16[1280,128]{1,0:T(8,128)(2,1)}, bf16[1280,128]{1,0:T(8,128)(2,1)S(1)}, u32[]{:S(2)}, u32[]{:S(2)}) collective-permute-start(bf16[1280,128]{1,0:T(8,128)(2,1)} %collective-permute-done.7.refs_2_), channel_id=1, source_target_pairs={{0,4},{1,5},{2,6},{3,7},{4,8},{5,9},{6,10},{7,11},{8,12},{9,13},{1... | collective-permute-start | bytes 983048 | tf_op jit(solution)/shard_map/ppermute | solution.py:34
  51.0 8.1 %collective-permute-start.17 = (bf16[1280,128]{1,0:T(8,128)(2,1)S(1)}, bf16[1280,128]{1,0:T(8,128)(2,1)S(1)}, u32[]{:S(2)}, u32[]{:S(2)}) collective-permute-start(bf16[1280,128]{1,0:T(8,128)(2,1)S(1)} %collective-permute-done.15.refs_1_), channel_id=1, source_target_pairs={{0,2},{1,3},{2,0},{3,1},{4,6},{5,7},{6,4},{7,5},{8,10},{9,11},{10,... | collective-permute-start | bytes 983048 | tf_op jit(solution)/shard_map/ppermute | solution.py:34
  61.6 1.9 %collective-permute-start.18 = (bf16[1280,128]{1,0:T(8,128)(2,1)S(1)}, bf16[1280,128]{1,0:T(8,128)(2,1)S(1)}, u32[]{:S(2)}, u32[]{:S(2)}) collective-permute-start(bf16[1280,128]{1,0:T(8,128)(2,1)S(1)} %bitcast.62), channel_id=1, source_target_pairs={{0,1},{1,0},{2,3},{3,2},{4,5},{5,4},{6,7},{7,6},{8,9},{9,8},{10,11... | collective-permute-start | bytes 983048 | tf_op jit(solution)/shard_map/ppermute | solution.py:34
  61.7 2.1 %collective-permute-start.19 = (bf16[1280,128]{1,0:T(8,128)(2,1)S(1)}, bf16[1280,128]{1,0:T(8,128)(2,1)S(1)}, u32[]{:S(2)}, u32[]{:S(2)}) collective-permute-start(bf16[1280,128]{1,0:T(8,128)(2,1)S(1)} %bitcast.61), channel_id=1, source_target_pairs={{0,1},{1,0},{2,3},{3,2},{4,5},{5,4},{6,7},{7,6},{8,9},{9,8},{10,11... | collective-permute-start | bytes 983048 | tf_op jit(solution)/shard_map/ppermute | solution.py:34
  62.2 7.5 %collective-permute-start.22 = (bf16[1280,128]{1,0:T(8,128)(2,1)S(1)}, bf16[1280,128]{1,0:T(8,128)(2,1)S(1)}, u32[]{:S(2)}, u32[]{:S(2)}) collective-permute-start(bf16[1280,128]{1,0:T(8,128)(2,1)S(1)} %bitcast.58), channel_id=1, source_target_pairs={{0,1},{1,0},{2,3},{3,2},{4,5},{5,4},{6,7},{7,6},{8,9},{9,8},{10,11... | collective-permute-start | bytes 983048 | tf_op jit(solution)/shard_map/ppermute | solution.py:34
  65.5 17.1 %collective-permute-start.21 = (bf16[1280,128]{1,0:T(8,128)(2,1)S(1)}, bf16[1280,128]{1,0:T(8,128)(2,1)S(1)}, u32[]{:S(2)}, u32[]{:S(2)}) collective-permute-start(bf16[1280,128]{1,0:T(8,128)(2,1)S(1)} %bitcast.57), channel_id=1, source_target_pairs={{0,1},{1,0},{2,3},{3,2},{4,5},{5,4},{6,7},{7,6},{8,9},{9,8},{10,11... | collective-permute-start | bytes 983048 | tf_op jit(solution)/shard_map/ppermute | solution.py:34
  65.7 4.1 %collective-permute-start.26 = (bf16[1280,128]{1,0:T(8,128)(2,1)S(1)}, bf16[1280,128]{1,0:T(8,128)(2,1)S(1)}, u32[]{:S(2)}, u32[]{:S(2)}) collective-permute-start(bf16[1280,128]{1,0:T(8,128)(2,1)S(1)} %bitcast.60), channel_id=1, source_target_pairs={{0,1},{1,0},{2,3},{3,2},{4,5},{5,4},{6,7},{7,6},{8,9},{9,8},{10,11... | collective-permute-start | bytes 983048 | tf_op jit(solution)/shard_map/ppermute | solution.py:34
  66.1 7.0 %collective-permute-start.27 = (bf16[640,128]{1,0:T(8,128)(2,1)S(1)}, bf16[640,128]{1,0:T(8,128)(2,1)S(1)}, u32[]{:S(2)}, u32[]{:S(2)}) collective-permute-start(bf16[640,128]{1,0:T(8,128)(2,1)S(1)} %get-tuple-element.103), channel_id=1, source_target_pairs={{0,2},{1,3},{2,0},{3,1},{4,6},{5,7},{6,4},{7,5},{8,10},{9,11},{10,... | collective-permute-start | bytes 491528 | tf_op jit(solution)/shard_map/ppermute | solution.py:34
  67.6 8.3 %collective-permute-start.23 = (bf16[640,128]{1,0:T(8,128)(2,1)S(1)}, bf16[640,128]{1,0:T(8,128)(2,1)S(1)}, u32[]{:S(2)}, u32[]{:S(2)}) collective-permute-start(bf16[640,128]{1,0:T(8,128)(2,1)S(1)} %get-tuple-element.98), channel_id=1, source_target_pairs={{0,2},{1,3},{2,0},{3,1},{4,6},{5,7},{6,4},{7,5},{8,10},{9,11},{10,... | collective-permute-start | bytes 491528 | tf_op jit(solution)/shard_map/ppermute | solution.py:34
  69.7 6.3 %collective-permute-start.30 = (bf16[1280,128]{1,0:T(8,128)(2,1)S(1)}, bf16[1280,128]{1,0:T(8,128)(2,1)S(1)}, u32[]{:S(2)}, u32[]{:S(2)}) collective-permute-start(bf16[1280,128]{1,0:T(8,128)(2,1)S(1)} %bitcast.59), channel_id=1, source_target_pairs={{0,1},{1,0},{2,3},{3,2},{4,5},{5,4},{6,7},{7,6},{8,9},{9,8},{10,11... | collective-permute-start | bytes 983048 | tf_op jit(solution)/shard_map/ppermute | solution.py:34
  69.8 12.4 %collective-permute-start.31 = (bf16[1280,128]{1,0:T(8,128)(2,1)S(1)}, bf16[1280,128]{1,0:T(8,128)(2,1)S(1)}, u32[]{:S(2)}, u32[]{:S(2)}) collective-permute-start(bf16[1280,128]{1,0:T(8,128)(2,1)S(1)} %get-tuple-element.107), channel_id=1, source_target_pairs={{0,4},{1,5},{2,6},{3,7},{4,8},{5,9},{6,10},{7,11},{8,12},{9,13},{1... | collective-permute-start | bytes 983048 | tf_op jit(solution)/shard_map/ppermute | solution.py:34
  73.1 24.2 %collective-permute-start.20 = (bf16[1280,128]{1,0:T(8,128)(2,1)S(1)}, bf16[1280,128]{1,0:T(8,128)(2,1)S(1)}, u32[]{:S(2)}, u32[]{:S(2)}) collective-permute-start(bf16[1280,128]{1,0:T(8,128)(2,1)S(1)} %bitcast.55), channel_id=1, source_target_pairs={{0,1},{1,0},{2,3},{3,2},{4,5},{5,4},{6,7},{7,6},{8,9},{9,8},{10,11... | collective-permute-start | bytes 983048 | tf_op jit(solution)/shard_map/ppermute | solution.py:34
  75.9 15.9 %collective-permute-start.34 = (bf16[1280,128]{1,0:T(8,128)(2,1)S(1)}, bf16[1280,128]{1,0:T(8,128)(2,1)S(1)}, u32[]{:S(2)}, u32[]{:S(2)}) collective-permute-start(bf16[1280,128]{1,0:T(8,128)(2,1)S(1)} %bitcast.56), channel_id=1, source_target_pairs={{0,1},{1,0},{2,3},{3,2},{4,5},{5,4},{6,7},{7,6},{8,9},{9,8},{10,11... | collective-permute-start | bytes 983048 | tf_op jit(solution)/shard_map/ppermute | solution.py:34
  76.0 9.4 %collective-permute-start.24 = (bf16[640,128]{1,0:T(8,128)(2,1)S(1)}, bf16[640,128]{1,0:T(8,128)(2,1)S(1)}, u32[]{:S(2)}, u32[]{:S(2)}) collective-permute-start(bf16[640,128]{1,0:T(8,128)(2,1)S(1)} %get-tuple-element.120), channel_id=1, source_target_pairs={{0,4},{1,5},{2,6},{3,7},{4,8},{5,9},{6,10},{7,11},{8,12},{9,13},{1... | collective-permute-start | bytes 491528 | tf_op jit(solution)/shard_map/ppermute | solution.py:34
  82.2 7.3 %collective-permute-start.28 = (bf16[640,128]{1,0:T(8,128)(2,1)S(1)}, bf16[640,128]{1,0:T(8,128)(2,1)S(1)}, u32[]{:S(2)}, u32[]{:S(2)}) collective-permute-start(bf16[640,128]{1,0:T(8,128)(2,1)S(1)} %get-tuple-element.121), channel_id=1, source_target_pairs={{0,4},{1,5},{2,6},{3,7},{4,8},{5,9},{6,10},{7,11},{8,12},{9,13},{1... | collective-permute-start | bytes 491528 | tf_op jit(solution)/shard_map/ppermute | solution.py:34
  82.7 9.1 %collective-permute-start.32 = (bf16[1280,128]{1,0:T(8,128)(2,1)S(1)}, bf16[1280,128]{1,0:T(8,128)(2,1)S(1)}, u32[]{:S(2)}, u32[]{:S(2)}) collective-permute-start(bf16[1280,128]{1,0:T(8,128)(2,1)S(1)} %fusion.6), channel_id=1, source_target_pairs={{0,2},{1,3},{2,0},{3,1},{4,6},{5,7},{6,4},{7,5},{8,10},{9,11},{10,... | collective-permute-start | bytes 983048 | tf_op jit(solution)/shard_map/ppermute | solution.py:34
  85.4 11.9 %collective-permute-start.25 = (bf16[640,128]{1,0:T(8,128)(2,1)S(1)}, bf16[640,128]{1,0:T(8,128)(2,1)S(1)}, u32[]{:S(2)}, u32[]{:S(2)}) collective-permute-start(bf16[640,128]{1,0:T(8,128)(2,1)S(1)} %fusion.12), channel_id=1, source_target_pairs={{0,4},{1,5},{2,6},{3,7},{4,8},{5,9},{6,10},{7,11},{8,12},{9,13},{1... | collective-permute-start | bytes 491528 | tf_op jit(solution)/shard_map/ppermute | solution.py:34
  89.5 8.9 %collective-permute-start.29 = (bf16[640,128]{1,0:T(8,128)(2,1)S(1)}, bf16[640,128]{1,0:T(8,128)(2,1)S(1)}, u32[]{:S(2)}, u32[]{:S(2)}) collective-permute-start(bf16[640,128]{1,0:T(8,128)(2,1)S(1)} %add_convert_fusion), channel_id=1, source_target_pairs={{0,4},{1,5},{2,6},{3,7},{4,8},{5,9},{6,10},{7,11},{8,12},{9,13},{1... | collective-permute-start | bytes 491528 | tf_op jit(solution)/shard_map/ppermute | solution.py:34
  92.0 11.7 %collective-permute-start.35 = (bf16[1280,128]{1,0:T(8,128)(2,1)S(1)}, bf16[1280,128]{1,0:T(8,128)(2,1)S(1)}, u32[]{:S(2)}, u32[]{:S(2)}) collective-permute-start(bf16[1280,128]{1,0:T(8,128)(2,1)S(1)} %fusion.3), channel_id=1, source_target_pairs={{0,12},{1,13},{2,14},{3,15},{4,0},{5,1},{6,2},{7,3},{8,4},{9,5},{1... | collective-permute-start | bytes 983048 | tf_op jit(solution)/shard_map/ppermute | solution.py:34
  95.5 8.1 %collective-permute-start.33 = (bf16[1280,128]{1,0:T(8,128)(2,1)S(1)}, bf16[1280,128]{1,0:T(8,128)(2,1)S(1)}, u32[]{:S(2)}, u32[]{:S(2)}) collective-permute-start(bf16[1280,128]{1,0:T(8,128)(2,1)S(1)} %fusion.5), channel_id=1, source_target_pairs={{0,2},{1,3},{2,0},{3,1},{4,6},{5,7},{6,4},{7,5},{8,10},{9,11},{10,... | collective-permute-start | bytes 983048 | tf_op jit(solution)/shard_map/ppermute | solution.py:34

commit v16 on v15

--- a/solution.py
+++ b/solution.py
@@ -38,7 +38,7 @@
 BACK = pairs_of(lambda z, x: ((z - 1) % LINE, x))
 ACROSS = pairs_of(lambda z, x: (z, 1 - x))
 NEAR0, NEAR1, NEAR2, NEAR3, FAR0, FAR1, FAR2, FAR3 = range(2 * LINE)
-ADD_AT = {(2, 1): 0, (3, 0): 1, (3, 1): 2}
+ADD_AT = {(2, 1): 0, (3, 0): 1}
 RAW_AT, LAY_AT = (0, 1), (1, 1)
 
 
@@ -111,10 +111,7 @@
     half[pl.ds(whole, half.shape[0] - whole), :] = jnp.zeros((half.shape[0] - whole, LANES), jnp.float32)
 
 
-def add_tiles(stage, pieces, table_ref, bounds_ref, sources, tiles, half, occ, sem):
-    rows = sources[0].shape[0]
-    for index, source in enumerate(sources):
-        pltpu.make_async_copy(source, occ.at[pl.ds(index * rows, rows)], sem).start()
+def add_tiles(stage, pieces, table_ref, bounds_ref, tiles, half, occ, sem):
     pltpu.make_async_copy(occ, occ, sem).wait()
     begin, end = bounds_ref[stage], bounds_ref[stage + 1]
     low = lax.broadcasted_iota(jnp.int32, tiles.shape[1:], 1) < BLK
@@ -168,17 +165,21 @@
 
 def add_stage(stage, count, pieces, table_ref, bounds_ref, refs):
     sources = refs[:count]
+    *_, occ, sems = refs
+    rows = sources[0].shape[0]
+    for index, source in enumerate(sources):
+        pltpu.make_async_copy(source, occ.at[pl.ds(index * rows, rows)], sems.at[2]).start()
     if stage:
-        tiles, _, half, *outs, occ, sems = refs[count:]
+        tiles, _, half, *outs = refs[count:-2]
         copies = []
     else:
         *tile_sets, half, tiles = refs[count : count + 4]
-        *outs, occ, sems = refs[count + 4 :]
+        outs = refs[count + 4 : -2]
         copies = load_tiles(tile_sets, tiles, sems)
         clear(half)
     for copy in copies:
         copy.wait()
-    add_tiles(stage, pieces, table_ref, bounds_ref, sources, tiles, half, occ, sems.at[2])
+    add_tiles(stage, pieces, table_ref, bounds_ref, tiles, half, occ, sems.at[2])
     return half, outs
 
 
@@ -206,6 +207,10 @@
 
 def pinned(array):
     return pltpu.with_memory_space_constraint(array, pltpu.VMEM)
+
+
+def held(array):
+    return pltpu.with_memory_space_constraint(array, pltpu.HBM)
 
 
 def call(kernel, ins, in_specs, outs, scratch, aliases, flops, scoped=0):
@@ -295,7 +300,8 @@
             aliases = {len(ins) + 1: 0}
             ins, specs = ins + [pinned(state[1]), pinned(state[0])], specs + [VMEM] * 2
         else:
-            ins, specs = [*tables, *sources, *tile_sets], specs + [HBM] * 2
+            ins = [*tables, *map(held, sources), tile_sets[0], held(tile_sets[1])]
+            specs = specs + [HBM] * 2
             made = [half_type, tiles_type]
         results = call(kernel, ins, specs, made + outs, scratch, aliases, flops, 2 * rows * LANES)
         state[:] = [results[0], state[1] if state else results[1]]

time: 105 us -> 105 us (level)
  waiting for transfers between devices: 32.3 us -> 39.9 us
  starting transfers between devices: 36.5 us -> 31.7 us
  local copies, waits for them, and re-layouts: 11.5 us -> 8.14 us
    ppermute x36, waiting for transfers between devices: 32.3 us -> 39.9 us  [move(): return lax.ppermute(array, 'aux', pairs)]
    ppermute x36, starting transfers between devices: 36.5 us -> 31.7 us  [move(): return lax.ppermute(array, 'aux', pairs)]
    unnamed x17 -> x11, local copies, waits for them, and re-layouts: 10.2 us -> 6.92 us
  transfers between devices with their start and end apart: 36 -> 36, of which waited for: 15 -> 17; matrix products, arithmetic and copies ran while one was open for 10% -> 10% of each run, Pallas kernels for 16% -> 16%
where the time goes in v16:
time: 105 us; the launch traced here: 104 us
  waiting for transfers between devices  39.9 us (38%)
  starting transfers between devices  31.7 us (30%)
  Pallas kernels  19.4 us (18%)
  local copies, waits for them, and re-layouts  8.14 us (8%)
  other arithmetic  4.21 us (4%)
    ppermute x36, waiting for transfers between devices, move(): return lax.ppermute(array, 'aux', pairs)  39.9 us
    ppermute x36, starting transfers between devices, move(): return lax.ppermute(array, 'aux', pairs)  31.7 us
    pallas_call x8, Pallas kernels, call(): pl.pallas_call(kernel, out_shape=outs, in_specs=in_specs, out_specs=[VMEM...  19.4 us
    unnamed x11, local copies, waits for them, and re-layouts  6.92 us
  transfers between devices with their start and end apart: 36, of which 17 were waited for; matrix products, arithmetic and copies ran while one was open for 10% of the time, Pallas kernels for 16%

profile of v16, /device:TPU:0, one launch (start us, length us, event | category | flops | bytes accessed | tf_op | source)
XLA Modules:
  0.0 104.4 jit_solution(3138409474479686395)
XLA Ops:
  0.0 0.5 collective-permute-start.9
  0.5 1.1 %constant_dynamic-slice_fusion.1 = (bf16[1280,128]{1,0:T(8,128)(2,1)S(1)}, bf16[1280,128]{1,0:T(8,128)(2,1)S(1)}) fusion(bf16[1280,256]{1,0:T(8,128)(2,1)} %param.7, s32[]{:T(128)S(6)} %select_n.162, s32[]{:T(128)S(6)} %select_n.161), kind=kLoop, calls=%fused_computation.91 | loop fusion | bytes 1310728 | tf_op jit(solution)/shard_map/dynamic_slice | solution.py:244
  1.6 2.6 %collective-permute-start.2 = (bf16[1280,128]{1,0:T(8,128)(2,1)S(1)}, bf16[1280,128]{1,0:T(8,128)(2,1)S(1)}, u32[]{:S(2)}, u32[]{:S(2)}) collective-permute-start(bf16[1280,128]{1,0:T(8,128)(2,1)S(1)} %get-tuple-element.119.refs_0_), channel_id=1, source_target_pairs={{0,4},{1,5},{2,6},{3,7},{4,8},{5,9},{6,10},{7,11},{8,12},{9,13},{1... | collective-permute-start | bytes 983048 | tf_op jit(solution)/shard_map/ppermute | solution.py:34
  4.2 1.5 %collective-permute-start.3 = (bf16[1280,128]{1,0:T(8,128)(2,1)S(1)}, bf16[1280,128]{1,0:T(8,128)(2,1)S(1)}, u32[]{:S(2)}, u32[]{:S(2)}) collective-permute-start(bf16[1280,128]{1,0:T(8,128)(2,1)S(1)} %get-tuple-element.119.refs_0_), channel_id=1, source_target_pairs={{0,2},{1,3},{2,0},{3,1},{4,6},{5,7},{6,4},{7,5},{8,10},{9,11},{10,... | collective-permute-start | bytes 983048 | tf_op jit(solution)/shard_map/ppermute | solution.py:34
  5.7 0.5 collective-permute-start
  6.2 0.7 constant_dynamic-update-slice_fusion.1
  7.7 0.7 compare_select_fusion.3
  8.4 0.8 collective-permute-done.8.refs_1_
  9.3 1.6 %collective-permute-start.10 = (bf16[1280,128]{1,0:T(8,128)(2,1)S(1)}, bf16[1280,128]{1,0:T(8,128)(2,1)S(1)}, u32[]{:S(2)}, u32[]{:S(2)}) collective-permute-start(bf16[1280,128]{1,0:T(8,128)(2,1)S(1)} %collective-permute-done.8.refs_1_), channel_id=1, source_target_pairs={{0,4},{1,5},{2,6},{3,7},{4,8},{5,9},{6,10},{7,11},{8,12},{9,13},{1... | collective-permute-start | bytes 983048 | tf_op jit(solution)/shard_map/ppermute | solution.py:34
  10.9 0.5 collective-permute-start.11
  11.4 0.7 fusion.27
  12.1 2.7 %collective-permute-done.2.refs_0_ = bf16[1280,128]{1,0:T(8,128)(2,1)S(1)} collective-permute-done((bf16[1280,128]{1,0:T(8,128)(2,1)S(1)}, bf16[1280,128]{1,0:T(8,128)(2,1)S(1)}, u32[]{:S(2)}, u32[]{:S(2)}) %collective-permute-start.2) | collective-permute-done | bytes 327712 | tf_op jit(solution)/shard_map/ppermute | solution.py:34
  14.8 1.5 %collective-permute-start.4 = (bf16[1280,128]{1,0:T(8,128)(2,1)S(1)}, bf16[1280,128]{1,0:T(8,128)(2,1)S(1)}, u32[]{:S(2)}, u32[]{:S(2)}) collective-permute-start(bf16[1280,128]{1,0:T(8,128)(2,1)S(1)} %collective-permute-done.2.refs_0_), channel_id=1, source_target_pairs={{0,4},{1,5},{2,6},{3,7},{4,8},{5,9},{6,10},{7,11},{8,12},{9,13},{1... | collective-permute-start | bytes 983048 | tf_op jit(solution)/shard_map/ppermute | solution.py:34
  16.3 1.5 %collective-permute-start.5 = (bf16[1280,128]{1,0:T(8,128)(2,1)S(1)}, bf16[1280,128]{1,0:T(8,128)(2,1)}, u32[]{:S(2)}, u32[]{:S(2)}) collective-permute-start(bf16[1280,128]{1,0:T(8,128)(2,1)S(1)} %collective-permute-done.2.refs_0_), channel_id=1, source_target_pairs={{0,2},{1,3},{2,0},{3,1},{4,6},{5,7},{6,4},{7,5},{8,10},{9,11},{10,... | collective-permute-start | bytes 983048 | tf_op jit(solution)/shard_map/ppermute | solution.py:34
  17.8 2.1 %copy.9 = bf16[32,8,32,128]{3,2,1,0:T(8,128)(2,1)S(1)} copy(bf16[32,8,32,128]{3,1,2,0:T(8,128)(2,1)} %bitcast.63) | data formatting | bytes 4194304
  19.9 3.4 %copy.10 = bf16[32,8,32,128]{3,2,1,0:T(8,128)(2,1)} copy(bf16[32,8,32,128]{3,1,2,0:T(8,128)(2,1)} %bitcast.25) | data formatting | bytes 4194304
  23.3 0.7 copy-done
  24.1 1.6 %collective-permute-start.12 = (bf16[1280,128]{1,0:T(8,128)(2,1)S(1)}, bf16[1280,128]{1,0:T(8,128)(2,1)}, u32[]{:S(2)}, u32[]{:S(2)}) collective-permute-start(bf16[1280,128]{1,0:T(8,128)(2,1)S(1)} %collective-permute-done.10.refs_1_), channel_id=1, source_target_pairs={{0,4},{1,5},{2,6},{3,7},{4,8},{5,9},{6,10},{7,11},{8,12},{9,13},{1... | collective-permute-start | bytes 983048 | tf_op jit(solution)/shard_map/ppermute | solution.py:34
  25.7 0.5 collective-permute-start.13
  26.2 0.3 convert_reduce_fusion
  26.5 0.5 select_reduce_fusion
  27.1 0.1 convert_reduce_fusion.1.bounds_ref
  27.2 1.6 %collective-permute-done.4.refs_0_ = bf16[1280,128]{1,0:T(8,128)(2,1)S(1)} collective-permute-done((bf16[1280,128]{1,0:T(8,128)(2,1)S(1)}, bf16[1280,128]{1,0:T(8,128)(2,1)S(1)}, u32[]{:S(2)}, u32[]{:S(2)}) %collective-permute-start.4) | collective-permute-done | bytes 327712 | tf_op jit(solution)/shard_map/ppermute | solution.py:34
  28.9 1.6 %collective-permute-start.6 = (bf16[1280,128]{1,0:T(8,128)(2,1)S(1)}, bf16[1280,128]{1,0:T(8,128)(2,1)S(1)}, u32[]{:S(2)}, u32[]{:S(2)}) collective-permute-start(bf16[1280,128]{1,0:T(8,128)(2,1)S(1)} %collective-permute-done.4.refs_0_), channel_id=1, source_target_pairs={{0,4},{1,5},{2,6},{3,7},{4,8},{5,9},{6,10},{7,11},{8,12},{9,13},{1... | collective-permute-start | bytes 983048 | tf_op jit(solution)/shard_map/ppermute | solution.py:34
  30.5 1.5 %collective-permute-start.7 = (bf16[1280,128]{1,0:T(8,128)(2,1)S(1)}, bf16[1280,128]{1,0:T(8,128)(2,1)S(1)}, u32[]{:S(2)}, u32[]{:S(2)}) collective-permute-start(bf16[1280,128]{1,0:T(8,128)(2,1)S(1)} %collective-permute-done.4.refs_0_), channel_id=1, source_target_pairs={{0,2},{1,3},{2,0},{3,1},{4,6},{5,7},{6,4},{7,5},{8,10},{9,11},{10,... | collective-permute-start | bytes 983048 | tf_op jit(solution)/shard_map/ppermute | solution.py:34
  32.0 3.4 %shard_map.46 = (f32[41024,128]{1,0:T(8,128)S(1)}, bf16[512,32,128]{2,1,0:T(8,128)(2,1)S(1)}) custom-call(s32[1584]{0:T(1024)S(1)} %concatenate.10.table_ref, s32[6]{0:T(128)S(1)} %convert_reduce_fusion.1.bounds_ref, bf16[1280,128]{1,0:T(8,128)(2,1)} %copy-done.2, bf16[1280,128]{1,0:T(8,128)(2,1)} %copy-done.3, bf16[256,32,128]{2,1,0:T(8,128)(2,1)S(1)} %bitcast.53, ...), custom_call_target="tpu_custom_call" | custom-call | flops 107374184 | bytes 4194304 | tf_op jit(solution)/shard_map/pallas_call | solution.py:217
  35.3 1.3 %collective-permute-done.12.refs_1_ = bf16[1280,128]{1,0:T(8,128)(2,1)} collective-permute-done((bf16[1280,128]{1,0:T(8,128)(2,1)S(1)}, bf16[1280,128]{1,0:T(8,128)(2,1)}, u32[]{:S(2)}, u32[]{:S(2)}) %collective-permute-start.12) | collective-permute-done | bytes 327712 | tf_op jit(solution)/shard_map/ppermute | solution.py:34
  36.6 0.9 collective-permute-start.15
  37.5 1.5 %collective-permute-start.16 = (bf16[1280,128]{1,0:T(8,128)(2,1)}, bf16[1280,128]{1,0:T(8,128)(2,1)S(1)}, u32[]{:S(2)}, u32[]{:S(2)}) collective-permute-start(bf16[1280,128]{1,0:T(8,128)(2,1)} %collective-permute-done.12.refs_1_), channel_id=1, source_target_pairs={{0,2},{1,3},{2,0},{3,1},{4,6},{5,7},{6,4},{7,5},{8,10},{9,11},{10,... | collective-permute-start | bytes 983048 | tf_op jit(solution)/shard_map/ppermute | solution.py:34
  39.0 4.5 %collective-permute-done.6.refs_0_ = bf16[1280,128]{1,0:T(8,128)(2,1)S(1)} collective-permute-done((bf16[1280,128]{1,0:T(8,128)(2,1)S(1)}, bf16[1280,128]{1,0:T(8,128)(2,1)S(1)}, u32[]{:S(2)}, u32[]{:S(2)}) %collective-permute-start.6) | collective-permute-done | bytes 327712 | tf_op jit(solution)/shard_map/ppermute | solution.py:34
  43.6 2.8 %shard_map.47.refs_5_ = f32[41024,128]{1,0:T(8,128)S(1)} custom-call(s32[1584]{0:T(1024)S(1)} %concatenate.10.table_ref, s32[6]{0:T(128)S(1)} %convert_reduce_fusion.1.bounds_ref, bf16[1280,128]{1,0:T(8,128)(2,1)S(1)} %collective-permute-done.2.refs_0_, bf16[1280,128]{1,0:T(8,128)(2,1)S(1)} %collective-permute-done.10.refs_1_, ...), custom_call_target="tpu_custom_call", output_to_operand_aliasing={{}: (7, {})} | custom-call | flops 107374184 | bytes 4194304 | tf_op jit(solution)/shard_map/pallas_call | solution.py:217
  46.4 0.6 collective-permute-start.14
  47.0 3.2 %collective-permute-done.15.refs_1_ = bf16[1280,128]{1,0:T(8,128)(2,1)S(1)} collective-permute-done((bf16[1280,128]{1,0:T(8,128)(2,1)}, bf16[1280,128]{1,0:T(8,128)(2,1)S(1)}, u32[]{:S(2)}, u32[]{:S(2)}) %collective-permute-start.15) | collective-permute-done | bytes 327712 | tf_op jit(solution)/shard_map/ppermute | solution.py:34
  50.2 1.4 %collective-permute-start.17 = (bf16[1280,128]{1,0:T(8,128)(2,1)S(1)}, bf16[1280,128]{1,0:T(8,128)(2,1)S(1)}, u32[]{:S(2)}, u32[]{:S(2)}) collective-permute-start(bf16[1280,128]{1,0:T(8,128)(2,1)S(1)} %collective-permute-done.15.refs_1_), channel_id=1, source_target_pairs={{0,2},{1,3},{2,0},{3,1},{4,6},{5,7},{6,4},{7,5},{8,10},{9,11},{10,... | collective-permute-start | bytes 983048 | tf_op jit(solution)/shard_map/ppermute | solution.py:34
  51.5 3.6 %shard_map.48.refs_5_ = f32[41024,128]{1,0:T(8,128)S(1)} custom-call(s32[1584]{0:T(1024)S(1)} %concatenate.10.table_ref, s32[6]{0:T(128)S(1)} %convert_reduce_fusion.1.bounds_ref, bf16[1280,128]{1,0:T(8,128)(2,1)S(1)} %collective-permute-done.4.refs_0_, bf16[1280,128]{1,0:T(8,128)(2,1)} %collective-permute-done.12.refs_1_, ...), custom_call_target="tpu_custom_call", output_to_operand_aliasing={{}: (7, {})} | custom-call | flops 107374184 | bytes 4194304 | tf_op jit(solution)/shard_map/pallas_call | solution.py:217
  55.2 2.8 %shard_map.49.refs_3_ = f32[41024,128]{1,0:T(8,128)S(1)} custom-call(s32[1584]{0:T(1024)S(1)} %concatenate.10.table_ref, s32[6]{0:T(128)S(1)} %convert_reduce_fusion.1.bounds_ref, bf16[1280,128]{1,0:T(8,128)(2,1)S(1)} %collective-permute-done.6.refs_0_, bf16[1280,128]{1,0:T(8,128)(2,1)S(1)} %collective-permute-done.15.refs_1_, ...), custom_call_target="tpu_custom_call", output_to_operand_aliasing={{}: (7, {})} | custom-call | flops 107374184 | bytes 4194304 | tf_op jit(solution)/shard_map/pallas_call | solution.py:217
  58.0 0.9 collective-permute-done.17.refs_1_
  58.9 2.5 %shard_map.50 = (f32[41024,128]{1,0:T(8,128)S(1)}, bf16[256,128]{1,0:T(8,128)(2,1)S(1)}, bf16[1,1280,128]{2,1,0:T(8,128)(2,1)S(1)}, bf16[1,1280,128]{2,1,0:T(8,128)(2,1)S(1)}, bf16[1,1280,128]{2,1,0:T(8,128)(2,1)S(1)}) custom-call(s32[1584]{0:T(1024)S(1)} %concatenate.10.table_ref, ...), custom_call_target="tpu_custom_call", output_to_operand_aliasing={{0}: (7, {})} | custom-call | flops 359032416 | bytes 4194304 | tf_op jit(solution)/shard_map/pallas_call | solution.py:217
  61.5 0.5 collective-permute-start.19
  62.1 1.2 %shard_map.51 = (f32[1,1280,128]{2,1,0:T(8,128)S(1)}, f32[1,1280,128]{2,1,0:T(8,128)S(1)}, f32[1,1280,128]{2,1,0:T(8,128)S(1)}) custom-call(s32[8]{0:T(128)S(1)} %fusion.30.chips_ref, s32[1]{0:T(128)} %bitcast.core_ref, f32[41024,128]{1,0:T(8,128)S(1)} %get-tuple-element.87.half, bf16[256,128]{1,0:T(8,128)(2,1)S(1)} %get-tuple-element.82.weights), custom_call_target="tpu_custom_call" | custom-call | flops 251658240 | bytes 4194304 | tf_op jit(solution)/shard_map/pallas_call | solution.py:217
  63.3 0.3 collective-permute-done.19
  63.6 0.1 fusion.8
  63.8 1.6 %shard_map.53 = (bf16[1,1280,128]{2,1,0:T(8,128)(2,1)S(1)}, bf16[1,1280,128]{2,1,0:T(8,128)(2,1)S(1)}, bf16[1,1280,128]{2,1,0:T(8,128)(2,1)S(1)}, bf16[1,1280,12...) custom-call(s32[8]{0:T(128)S(1)} %fusion.30.chips_ref, s32[1]{0:T(128)} %bitcast.core_ref, ...), custom_call_target="tpu_custom_call" | custom-call | flops 419430400 | bytes 4194304 | tf_op jit(solution)/shard_map/pallas_call | solution.py:217
  65.3 0.2 collective-permute-start.21
  65.6 0.4 collective-permute-start.26
  65.9 1.5 %collective-permute-start.27 = (bf16[640,128]{1,0:T(8,128)(2,1)S(1)}, bf16[640,128]{1,0:T(8,128)(2,1)S(1)}, u32[]{:S(2)}, u32[]{:S(2)}) collective-permute-start(bf16[640,128]{1,0:T(8,128)(2,1)S(1)} %get-tuple-element.99), channel_id=1, source_target_pairs={{0,2},{1,3},{2,0},{3,1},{4,6},{5,7},{6,4},{7,5},{8,10},{9,11},{10,... | collective-permute-start | bytes 491528 | tf_op jit(solution)/shard_map/ppermute | solution.py:34
  67.4 0.6 collective-permute-start.23
  67.9 1.5 %shard_map.52 = (f32[1,1280,128]{2,1,0:T(8,128)S(1)}, f32[1,1280,128]{2,1,0:T(8,128)S(1)}, f32[1,1280,128]{2,1,0:T(8,128)S(1)}, f32[1,1280,128]{2,1,0:T(8,128)S(1)}, f32[1,1280,128]{2,1,0:T(8,128)S(1)}) custom-call(s32[8]{0:T(128)S(1)} %fusion.30.chips_ref, s32[1]{0:T(128)} %bitcast.core_ref, f32[41024,128]{1,0:T(8,128)S(1)} %get-tuple-element.87.half, ...), custom_call_target="tpu_custom_call" | custom-call | flops 419430400 | bytes 4194304 | tf_op jit(solution)/shard_map/pallas_call | solution.py:217
  69.7 0.9 collective-permute-start.31
  70.6 2.3 %collective-permute-done.27 = bf16[640,128]{1,0:T(8,128)(2,1)S(1)} collective-permute-done((bf16[640,128]{1,0:T(8,128)(2,1)S(1)}, bf16[640,128]{1,0:T(8,128)(2,1)S(1)}, u32[]{:S(2)}, u32[]{:S(2)}) %collective-permute-start.27) | collective-permute-done | bytes 163872 | tf_op jit(solution)/shard_map/ppermute | solution.py:34
  73.0 2.7 %collective-permute-done.23 = bf16[640,128]{1,0:T(8,128)(2,1)S(1)} collective-permute-done((bf16[640,128]{1,0:T(8,128)(2,1)S(1)}, bf16[640,128]{1,0:T(8,128)(2,1)S(1)}, u32[]{:S(2)}, u32[]{:S(2)}) %collective-permute-start.23) | collective-permute-done | bytes 163872 | tf_op jit(solution)/shard_map/ppermute | solution.py:34
  75.8 0.9 collective-permute-start.24
  76.7 5.3 %collective-permute-done.31 = bf16[1280,128]{1,0:T(8,128)(2,1)S(1)} collective-permute-done((bf16[1280,128]{1,0:T(8,128)(2,1)S(1)}, bf16[1280,128]{1,0:T(8,128)(2,1)S(1)}, u32[]{:S(2)}, u32[]{:S(2)}) %collective-permute-start.31) | collective-permute-done | bytes 327712 | tf_op jit(solution)/shard_map/ppermute | solution.py:34
  82.0 0.1 fusion.5
  82.2 1.5 %collective-permute-start.32 = (bf16[1280,128]{1,0:T(8,128)(2,1)S(1)}, bf16[1280,128]{1,0:T(8,128)(2,1)S(1)}, u32[]{:S(2)}, u32[]{:S(2)}) collective-permute-start(bf16[1280,128]{1,0:T(8,128)(2,1)S(1)} %fusion.6), channel_id=1, source_target_pairs={{0,2},{1,3},{2,0},{3,1},{4,6},{5,7},{6,4},{7,5},{8,10},{9,11},{10,... | collective-permute-start | bytes 983048 | tf_op jit(solution)/shard_map/ppermute | solution.py:34
  83.7 1.4 %collective-permute-done.24 = bf16[640,128]{1,0:T(8,128)(2,1)S(1)} collective-permute-done((bf16[640,128]{1,0:T(8,128)(2,1)S(1)}, bf16[640,128]{1,0:T(8,128)(2,1)S(1)}, u32[]{:S(2)}, u32[]{:S(2)}) %collective-permute-start.24) | collective-permute-done | bytes 163872 | tf_op jit(solution)/shard_map/ppermute | solution.py:34
  85.2 4.0 %collective-permute-done.28 = bf16[640,128]{1,0:T(8,128)(2,1)S(1)} collective-permute-done((bf16[640,128]{1,0:T(8,128)(2,1)S(1)}, bf16[640,128]{1,0:T(8,128)(2,1)S(1)}, u32[]{:S(2)}, u32[]{:S(2)}) %collective-permute-start.28) | collective-permute-done | bytes 163872 | tf_op jit(solution)/shard_map/ppermute | solution.py:34
  89.3 1.8 %collective-permute-done.32 = bf16[1280,128]{1,0:T(8,128)(2,1)S(1)} collective-permute-done((bf16[1280,128]{1,0:T(8,128)(2,1)S(1)}, bf16[1280,128]{1,0:T(8,128)(2,1)S(1)}, u32[]{:S(2)}, u32[]{:S(2)}) %collective-permute-start.32) | collective-permute-done | bytes 327712 | tf_op jit(solution)/shard_map/ppermute | solution.py:34
  91.1 0.1 fusion.3
  91.3 3.6 %collective-permute-start.35 = (bf16[1280,128]{1,0:T(8,128)(2,1)S(1)}, bf16[1280,128]{1,0:T(8,128)(2,1)S(1)}, u32[]{:S(2)}, u32[]{:S(2)}) collective-permute-start(bf16[1280,128]{1,0:T(8,128)(2,1)S(1)} %fusion.3), channel_id=1, source_target_pairs={{0,12},{1,13},{2,14},{3,15},{4,0},{5,1},{6,2},{7,3},{8,4},{9,5},{1... | collective-permute-start | bytes 983048 | tf_op jit(solution)/shard_map/ppermute | solution.py:34
  94.9 1.5 %collective-permute-start.33 = (bf16[1280,128]{1,0:T(8,128)(2,1)S(1)}, bf16[1280,128]{1,0:T(8,128)(2,1)S(1)}, u32[]{:S(2)}, u32[]{:S(2)}) collective-permute-start(bf16[1280,128]{1,0:T(8,128)(2,1)S(1)} %fusion.5), channel_id=1, source_target_pairs={{0,2},{1,3},{2,0},{3,1},{4,6},{5,7},{6,4},{7,5},{8,10},{9,11},{10,... | collective-permute-start | bytes 983048 | tf_op jit(solution)/shard_map/ppermute | solution.py:34
  96.4 1.9 %collective-permute-done.29 = bf16[640,128]{1,0:T(8,128)(2,1)S(1)} collective-permute-done((bf16[640,128]{1,0:T(8,128)(2,1)S(1)}, bf16[640,128]{1,0:T(8,128)(2,1)S(1)}, u32[]{:S(2)}, u32[]{:S(2)}) %collective-permute-start.29) | collective-permute-done | bytes 163872 | tf_op jit(solution)/shard_map/ppermute | solution.py:34
  98.4 5.0 %collective-permute-done.35 = bf16[1280,128]{1,0:T(8,128)(2,1)S(1)} collective-permute-done((bf16[1280,128]{1,0:T(8,128)(2,1)S(1)}, bf16[1280,128]{1,0:T(8,128)(2,1)S(1)}, u32[]{:S(2)}, u32[]{:S(2)}) %collective-permute-start.35) | collective-permute-done | bytes 327712 | tf_op jit(solution)/shard_map/ppermute | solution.py:34
  103.4 0.9 add_multiply_fusion
  (50 shorter events, 1.2 us)
Async XLA Ops:
  0.0 9.3 %collective-permute-start.9 = (bf16[256,4096]{1,0:T(8,128)(2,1)}, bf16[256,4096]{1,0:T(8,128)(2,1)}, u32[]{:S(2)}, u32[]{:S(2)}) collective-permute-start(bf16[256,4096]{1,0:T(8,128)(2,1)} %param.4), channel_id=1, source_target_pairs={{0,1},{1,0},{2,3},{3,2},{4,5},{5,4},{6,7},{7,6},{8,9},{9,8},{10,11... | collective-permute-start | bytes 6291464 | tf_op jit(solution)/shard_map/ppermute | solution.py:34
  1.6 13.2 %copy-start.2 = (bf16[1280,128]{1,0:T(8,128)(2,1)}, bf16[1280,128]{1,0:T(8,128)(2,1)S(1)}, u32[]{:S(2)}) copy-start(bf16[1280,128]{1,0:T(8,128)(2,1)S(1)} %get-tuple-element.119.refs_0_) | copy-start | bytes 983044
  1.6 13.2 %collective-permute-start.2 = (bf16[1280,128]{1,0:T(8,128)(2,1)S(1)}, bf16[1280,128]{1,0:T(8,128)(2,1)S(1)}, u32[]{:S(2)}, u32[]{:S(2)}) collective-permute-start(bf16[1280,128]{1,0:T(8,128)(2,1)S(1)} %get-tuple-element.119.refs_0_), channel_id=1, source_target_pairs={{0,4},{1,5},{2,6},{3,7},{4,8},{5,9},{6,10},{7,11},{8,12},{9,13},{1... | collective-permute-start | bytes 983048 | tf_op jit(solution)/shard_map/ppermute | solution.py:34
  4.2 10.6 %collective-permute-start.3 = (bf16[1280,128]{1,0:T(8,128)(2,1)S(1)}, bf16[1280,128]{1,0:T(8,128)(2,1)S(1)}, u32[]{:S(2)}, u32[]{:S(2)}) collective-permute-start(bf16[1280,128]{1,0:T(8,128)(2,1)S(1)} %get-tuple-element.119.refs_0_), channel_id=1, source_target_pairs={{0,2},{1,3},{2,0},{3,1},{4,6},{5,7},{6,4},{7,5},{8,10},{9,11},{10,... | collective-permute-start | bytes 983048 | tf_op jit(solution)/shard_map/ppermute | solution.py:34
  5.7 1.9 %collective-permute-start.1 = (s32[256,2]{0,1:T(2,128)}, s32[256,2]{0,1:T(2,128)S(1)}, u32[]{:S(2)}, u32[]{:S(2)}) collective-permute-start(s32[256,2]{0,1:T(2,128)} %param.5), channel_id=1, source_target_pairs={{0,1},{1,0},{2,3},{3,2},{4,5},{5,4},{6,7},{7,6},{8,9},{9,8},{10,11... | collective-permute-start | bytes 6152 | tf_op jit(solution)/shard_map/ppermute | solution.py:34
  5.7 2.0 %collective-permute-start = (s32[1]{0:T(128)}, s32[1]{0:T(128)}, u32[]{:S(2)}, u32[]{:S(2)}) collective-permute-start(s32[1]{0:T(128)} %param.6), channel_id=1, source_target_pairs={{0,1},{1,0},{2,3},{3,2},{4,5},{5,4},{6,7},{7,6},{8,9},{9,8},{10,11... | collective-permute-start | bytes 20 | tf_op jit(solution)/shard_map/ppermute | solution.py:34
  7.6 1.7 %collective-permute-start.8 = (bf16[1280,128]{1,0:T(8,128)(2,1)S(1)}, bf16[1280,128]{1,0:T(8,128)(2,1)S(1)}, u32[]{:S(2)}, u32[]{:S(2)}) collective-permute-start(bf16[1280,128]{1,0:T(8,128)(2,1)S(1)} %get-tuple-element.118), channel_id=1, source_target_pairs={{0,1},{1,0},{2,3},{3,2},{4,5},{5,4},{6,7},{7,6},{8,9},{9,8},{10,11... | collective-permute-start | bytes 983048 | tf_op jit(solution)/shard_map/ppermute | solution.py:34
  9.3 10.6 %copy-start.3 = (bf16[1280,128]{1,0:T(8,128)(2,1)}, bf16[1280,128]{1,0:T(8,128)(2,1)S(1)}, u32[]{:S(2)}) copy-start(bf16[1280,128]{1,0:T(8,128)(2,1)S(1)} %collective-permute-done.8.refs_1_) | copy-start | bytes 983044
  9.3 14.1 %collective-permute-start.10 = (bf16[1280,128]{1,0:T(8,128)(2,1)S(1)}, bf16[1280,128]{1,0:T(8,128)(2,1)S(1)}, u32[]{:S(2)}, u32[]{:S(2)}) collective-permute-start(bf16[1280,128]{1,0:T(8,128)(2,1)S(1)} %collective-permute-done.8.refs_1_), channel_id=1, source_target_pairs={{0,4},{1,5},{2,6},{3,7},{4,8},{5,9},{6,10},{7,11},{8,12},{9,13},{1... | collective-permute-start | bytes 983048 | tf_op jit(solution)/shard_map/ppermute | solution.py:34
  10.9 12.5 %collective-permute-start.11 = (bf16[1280,128]{1,0:T(8,128)(2,1)S(1)}, bf16[1280,128]{1,0:T(8,128)(2,1)S(1)}, u32[]{:S(2)}, u32[]{:S(2)}) collective-permute-start(bf16[1280,128]{1,0:T(8,128)(2,1)S(1)} %collective-permute-done.8.refs_1_), channel_id=1, source_target_pairs={{0,2},{1,3},{2,0},{3,1},{4,6},{5,7},{6,4},{7,5},{8,10},{9,11},{10,... | collective-permute-start | bytes 983048 | tf_op jit(solution)/shard_map/ppermute | solution.py:34
  14.8 14.0 %collective-permute-start.4 = (bf16[1280,128]{1,0:T(8,128)(2,1)S(1)}, bf16[1280,128]{1,0:T(8,128)(2,1)S(1)}, u32[]{:S(2)}, u32[]{:S(2)}) collective-permute-start(bf16[1280,128]{1,0:T(8,128)(2,1)S(1)} %collective-permute-done.2.refs_0_), channel_id=1, source_target_pairs={{0,4},{1,5},{2,6},{3,7},{4,8},{5,9},{6,10},{7,11},{8,12},{9,13},{1... | collective-permute-start | bytes 983048 | tf_op jit(solution)/shard_map/ppermute | solution.py:34
  16.3 12.6 %collective-permute-start.5 = (bf16[1280,128]{1,0:T(8,128)(2,1)S(1)}, bf16[1280,128]{1,0:T(8,128)(2,1)}, u32[]{:S(2)}, u32[]{:S(2)}) collective-permute-start(bf16[1280,128]{1,0:T(8,128)(2,1)S(1)} %collective-permute-done.2.refs_0_), channel_id=1, source_target_pairs={{0,2},{1,3},{2,0},{3,1},{4,6},{5,7},{6,4},{7,5},{8,10},{9,11},{10,... | collective-permute-start | bytes 983048 | tf_op jit(solution)/shard_map/ppermute | solution.py:34
  23.3 0.7 copy-start
  24.1 12.6 %collective-permute-start.12 = (bf16[1280,128]{1,0:T(8,128)(2,1)S(1)}, bf16[1280,128]{1,0:T(8,128)(2,1)}, u32[]{:S(2)}, u32[]{:S(2)}) collective-permute-start(bf16[1280,128]{1,0:T(8,128)(2,1)S(1)} %collective-permute-done.10.refs_1_), channel_id=1, source_target_pairs={{0,4},{1,5},{2,6},{3,7},{4,8},{5,9},{6,10},{7,11},{8,12},{9,13},{1... | collective-permute-start | bytes 983048 | tf_op jit(solution)/shard_map/ppermute | solution.py:34
  25.7 11.0 %collective-permute-start.13 = (bf16[1280,128]{1,0:T(8,128)(2,1)S(1)}, bf16[1280,128]{1,0:T(8,128)(2,1)}, u32[]{:S(2)}, u32[]{:S(2)}) collective-permute-start(bf16[1280,128]{1,0:T(8,128)(2,1)S(1)} %collective-permute-done.10.refs_1_), channel_id=1, source_target_pairs={{0,2},{1,3},{2,0},{3,1},{4,6},{5,7},{6,4},{7,5},{8,10},{9,11},{10,... | collective-permute-start | bytes 983048 | tf_op jit(solution)/shard_map/ppermute | solution.py:34
  27.2 16.3 %copy-start.1 = (bf16[1280,128]{1,0:T(8,128)(2,1)S(1)}, bf16[1280,128]{1,0:T(8,128)(2,1)}, u32[]{:S(2)}) copy-start(bf16[1280,128]{1,0:T(8,128)(2,1)} %copy-done) | copy-start | bytes 983044
  28.9 14.6 %collective-permute-start.6 = (bf16[1280,128]{1,0:T(8,128)(2,1)S(1)}, bf16[1280,128]{1,0:T(8,128)(2,1)S(1)}, u32[]{:S(2)}, u32[]{:S(2)}) collective-permute-start(bf16[1280,128]{1,0:T(8,128)(2,1)S(1)} %collective-permute-done.4.refs_0_), channel_id=1, source_target_pairs={{0,4},{1,5},{2,6},{3,7},{4,8},{5,9},{6,10},{7,11},{8,12},{9,13},{1... | collective-permute-start | bytes 983048 | tf_op jit(solution)/shard_map/ppermute | solution.py:34
  30.5 13.1 %collective-permute-start.7 = (bf16[1280,128]{1,0:T(8,128)(2,1)S(1)}, bf16[1280,128]{1,0:T(8,128)(2,1)S(1)}, u32[]{:S(2)}, u32[]{:S(2)}) collective-permute-start(bf16[1280,128]{1,0:T(8,128)(2,1)S(1)} %collective-permute-done.4.refs_0_), channel_id=1, source_target_pairs={{0,2},{1,3},{2,0},{3,1},{4,6},{5,7},{6,4},{7,5},{8,10},{9,11},{10,... | collective-permute-start | bytes 983048 | tf_op jit(solution)/shard_map/ppermute | solution.py:34
  36.6 13.5 %collective-permute-start.15 = (bf16[1280,128]{1,0:T(8,128)(2,1)}, bf16[1280,128]{1,0:T(8,128)(2,1)S(1)}, u32[]{:S(2)}, u32[]{:S(2)}) collective-permute-start(bf16[1280,128]{1,0:T(8,128)(2,1)} %collective-permute-done.12.refs_1_), channel_id=1, source_target_pairs={{0,4},{1,5},{2,6},{3,7},{4,8},{5,9},{6,10},{7,11},{8,12},{9,13},{1... | collective-permute-start | bytes 983048 | tf_op jit(solution)/shard_map/ppermute | solution.py:34
  37.5 12.7 %collective-permute-start.16 = (bf16[1280,128]{1,0:T(8,128)(2,1)}, bf16[1280,128]{1,0:T(8,128)(2,1)S(1)}, u32[]{:S(2)}, u32[]{:S(2)}) collective-permute-start(bf16[1280,128]{1,0:T(8,128)(2,1)} %collective-permute-done.12.refs_1_), channel_id=1, source_target_pairs={{0,2},{1,3},{2,0},{3,1},{4,6},{5,7},{6,4},{7,5},{8,10},{9,11},{10,... | collective-permute-start | bytes 983048 | tf_op jit(solution)/shard_map/ppermute | solution.py:34
  46.4 11.6 %collective-permute-start.14 = (bf16[1280,128]{1,0:T(8,128)(2,1)S(1)}, bf16[1280,128]{1,0:T(8,128)(2,1)S(1)}, u32[]{:S(2)}, u32[]{:S(2)}) collective-permute-start(bf16[1280,128]{1,0:T(8,128)(2,1)S(1)} %collective-permute-done.7.refs_2_), channel_id=1, source_target_pairs={{0,4},{1,5},{2,6},{3,7},{4,8},{5,9},{6,10},{7,11},{8,12},{9,13},{1... | collective-permute-start | bytes 983048 | tf_op jit(solution)/shard_map/ppermute | solution.py:34
  50.2 8.7 %collective-permute-start.17 = (bf16[1280,128]{1,0:T(8,128)(2,1)S(1)}, bf16[1280,128]{1,0:T(8,128)(2,1)S(1)}, u32[]{:S(2)}, u32[]{:S(2)}) collective-permute-start(bf16[1280,128]{1,0:T(8,128)(2,1)S(1)} %collective-permute-done.15.refs_1_), channel_id=1, source_target_pairs={{0,2},{1,3},{2,0},{3,1},{4,6},{5,7},{6,4},{7,5},{8,10},{9,11},{10,... | collective-permute-start | bytes 983048 | tf_op jit(solution)/shard_map/ppermute | solution.py:34
  61.4 1.9 %collective-permute-start.18 = (bf16[1280,128]{1,0:T(8,128)(2,1)S(1)}, bf16[1280,128]{1,0:T(8,128)(2,1)S(1)}, u32[]{:S(2)}, u32[]{:S(2)}) collective-permute-start(bf16[1280,128]{1,0:T(8,128)(2,1)S(1)} %bitcast.61), channel_id=1, source_target_pairs={{0,1},{1,0},{2,3},{3,2},{4,5},{5,4},{6,7},{7,6},{8,9},{9,8},{10,11... | collective-permute-start | bytes 983048 | tf_op jit(solution)/shard_map/ppermute | solution.py:34
  61.5 2.1 %collective-permute-start.19 = (bf16[1280,128]{1,0:T(8,128)(2,1)S(1)}, bf16[1280,128]{1,0:T(8,128)(2,1)S(1)}, u32[]{:S(2)}, u32[]{:S(2)}) collective-permute-start(bf16[1280,128]{1,0:T(8,128)(2,1)S(1)} %bitcast.60), channel_id=1, source_target_pairs={{0,1},{1,0},{2,3},{3,2},{4,5},{5,4},{6,7},{7,6},{8,9},{9,8},{10,11... | collective-permute-start | bytes 983048 | tf_op jit(solution)/shard_map/ppermute | solution.py:34
  62.0 7.5 %collective-permute-start.22 = (bf16[1280,128]{1,0:T(8,128)(2,1)S(1)}, bf16[1280,128]{1,0:T(8,128)(2,1)S(1)}, u32[]{:S(2)}, u32[]{:S(2)}) collective-permute-start(bf16[1280,128]{1,0:T(8,128)(2,1)S(1)} %bitcast.57), channel_id=1, source_target_pairs={{0,1},{1,0},{2,3},{3,2},{4,5},{5,4},{6,7},{7,6},{8,9},{9,8},{10,11... | collective-permute-start | bytes 983048 | tf_op jit(solution)/shard_map/ppermute | solution.py:34
  65.3 16.8 %collective-permute-start.21 = (bf16[1280,128]{1,0:T(8,128)(2,1)S(1)}, bf16[1280,128]{1,0:T(8,128)(2,1)S(1)}, u32[]{:S(2)}, u32[]{:S(2)}) collective-permute-start(bf16[1280,128]{1,0:T(8,128)(2,1)S(1)} %bitcast.56), channel_id=1, source_target_pairs={{0,1},{1,0},{2,3},{3,2},{4,5},{5,4},{6,7},{7,6},{8,9},{9,8},{10,11... | collective-permute-start | bytes 983048 | tf_op jit(solution)/shard_map/ppermute | solution.py:34
  65.6 4.1 %collective-permute-start.26 = (bf16[1280,128]{1,0:T(8,128)(2,1)S(1)}, bf16[1280,128]{1,0:T(8,128)(2,1)S(1)}, u32[]{:S(2)}, u32[]{:S(2)}) collective-permute-start(bf16[1280,128]{1,0:T(8,128)(2,1)S(1)} %bitcast.59), channel_id=1, source_target_pairs={{0,1},{1,0},{2,3},{3,2},{4,5},{5,4},{6,7},{7,6},{8,9},{9,8},{10,11... | collective-permute-start | bytes 983048 | tf_op jit(solution)/shard_map/ppermute | solution.py:34
  65.9 7.0 %collective-permute-start.27 = (bf16[640,128]{1,0:T(8,128)(2,1)S(1)}, bf16[640,128]{1,0:T(8,128)(2,1)S(1)}, u32[]{:S(2)}, u32[]{:S(2)}) collective-permute-start(bf16[640,128]{1,0:T(8,128)(2,1)S(1)} %get-tuple-element.99), channel_id=1, source_target_pairs={{0,2},{1,3},{2,0},{3,1},{4,6},{5,7},{6,4},{7,5},{8,10},{9,11},{10,... | collective-permute-start | bytes 491528 | tf_op jit(solution)/shard_map/ppermute | solution.py:34
  67.4 8.3 %collective-permute-start.23 = (bf16[640,128]{1,0:T(8,128)(2,1)S(1)}, bf16[640,128]{1,0:T(8,128)(2,1)S(1)}, u32[]{:S(2)}, u32[]{:S(2)}) collective-permute-start(bf16[640,128]{1,0:T(8,128)(2,1)S(1)} %get-tuple-element.94), channel_id=1, source_target_pairs={{0,2},{1,3},{2,0},{3,1},{4,6},{5,7},{6,4},{7,5},{8,10},{9,11},{10,... | collective-permute-start | bytes 491528 | tf_op jit(solution)/shard_map/ppermute | solution.py:34
  69.5 6.3 %collective-permute-start.30 = (bf16[1280,128]{1,0:T(8,128)(2,1)S(1)}, bf16[1280,128]{1,0:T(8,128)(2,1)S(1)}, u32[]{:S(2)}, u32[]{:S(2)}) collective-permute-start(bf16[1280,128]{1,0:T(8,128)(2,1)S(1)} %bitcast.58), channel_id=1, source_target_pairs={{0,1},{1,0},{2,3},{3,2},{4,5},{5,4},{6,7},{7,6},{8,9},{9,8},{10,11... | collective-permute-start | bytes 983048 | tf_op jit(solution)/shard_map/ppermute | solution.py:34
  69.7 12.4 %collective-permute-start.31 = (bf16[1280,128]{1,0:T(8,128)(2,1)S(1)}, bf16[1280,128]{1,0:T(8,128)(2,1)S(1)}, u32[]{:S(2)}, u32[]{:S(2)}) collective-permute-start(bf16[1280,128]{1,0:T(8,128)(2,1)S(1)} %get-tuple-element.103), channel_id=1, source_target_pairs={{0,4},{1,5},{2,6},{3,7},{4,8},{5,9},{6,10},{7,11},{8,12},{9,13},{1... | collective-permute-start | bytes 983048 | tf_op jit(solution)/shard_map/ppermute | solution.py:34
  73.0 23.4 %collective-permute-start.20 = (bf16[1280,128]{1,0:T(8,128)(2,1)S(1)}, bf16[1280,128]{1,0:T(8,128)(2,1)S(1)}, u32[]{:S(2)}, u32[]{:S(2)}) collective-permute-start(bf16[1280,128]{1,0:T(8,128)(2,1)S(1)} %bitcast.54), channel_id=1, source_target_pairs={{0,1},{1,0},{2,3},{3,2},{4,5},{5,4},{6,7},{7,6},{8,9},{9,8},{10,11... | collective-permute-start | bytes 983048 | tf_op jit(solution)/shard_map/ppermute | solution.py:34
  75.7 15.5 %collective-permute-start.34 = (bf16[1280,128]{1,0:T(8,128)(2,1)S(1)}, bf16[1280,128]{1,0:T(8,128)(2,1)S(1)}, u32[]{:S(2)}, u32[]{:S(2)}) collective-permute-start(bf16[1280,128]{1,0:T(8,128)(2,1)S(1)} %bitcast.55), channel_id=1, source_target_pairs={{0,1},{1,0},{2,3},{3,2},{4,5},{5,4},{6,7},{7,6},{8,9},{9,8},{10,11... | collective-permute-start | bytes 983048 | tf_op jit(solution)/shard_map/ppermute | solution.py:34
  75.8 9.3 %collective-permute-start.24 = (bf16[640,128]{1,0:T(8,128)(2,1)S(1)}, bf16[640,128]{1,0:T(8,128)(2,1)S(1)}, u32[]{:S(2)}, u32[]{:S(2)}) collective-permute-start(bf16[640,128]{1,0:T(8,128)(2,1)S(1)} %get-tuple-element.116), channel_id=1, source_target_pairs={{0,4},{1,5},{2,6},{3,7},{4,8},{5,9},{6,10},{7,11},{8,12},{9,13},{1... | collective-permute-start | bytes 491528 | tf_op jit(solution)/shard_map/ppermute | solution.py:34
  82.0 7.2 %collective-permute-start.28 = (bf16[640,128]{1,0:T(8,128)(2,1)S(1)}, bf16[640,128]{1,0:T(8,128)(2,1)S(1)}, u32[]{:S(2)}, u32[]{:S(2)}) collective-permute-start(bf16[640,128]{1,0:T(8,128)(2,1)S(1)} %get-tuple-element.117), channel_id=1, source_target_pairs={{0,4},{1,5},{2,6},{3,7},{4,8},{5,9},{6,10},{7,11},{8,12},{9,13},{1... | collective-permute-start | bytes 491528 | tf_op jit(solution)/shard_map/ppermute | solution.py:34
  82.2 9.0 %collective-permute-start.32 = (bf16[1280,128]{1,0:T(8,128)(2,1)S(1)}, bf16[1280,128]{1,0:T(8,128)(2,1)S(1)}, u32[]{:S(2)}, u32[]{:S(2)}) collective-permute-start(bf16[1280,128]{1,0:T(8,128)(2,1)S(1)} %fusion.6), channel_id=1, source_target_pairs={{0,2},{1,3},{2,0},{3,1},{4,6},{5,7},{6,4},{7,5},{8,10},{9,11},{10,... | collective-permute-start | bytes 983048 | tf_op jit(solution)/shard_map/ppermute | solution.py:34
  85.2 11.2 %collective-permute-start.25 = (bf16[640,128]{1,0:T(8,128)(2,1)S(1)}, bf16[640,128]{1,0:T(8,128)(2,1)S(1)}, u32[]{:S(2)}, u32[]{:S(2)}) collective-permute-start(bf16[640,128]{1,0:T(8,128)(2,1)S(1)} %fusion.12), channel_id=1, source_target_pairs={{0,4},{1,5},{2,6},{3,7},{4,8},{5,9},{6,10},{7,11},{8,12},{9,13},{1... | collective-permute-start | bytes 491528 | tf_op jit(solution)/shard_map/ppermute | solution.py:34
  89.3 9.0 %collective-permute-start.29 = (bf16[640,128]{1,0:T(8,128)(2,1)S(1)}, bf16[640,128]{1,0:T(8,128)(2,1)S(1)}, u32[]{:S(2)}, u32[]{:S(2)}) collective-permute-start(bf16[640,128]{1,0:T(8,128)(2,1)S(1)} %add_convert_fusion), channel_id=1, source_target_pairs={{0,4},{1,5},{2,6},{3,7},{4,8},{5,9},{6,10},{7,11},{8,12},{9,13},{1... | collective-permute-start | bytes 491528 | tf_op jit(solution)/shard_map/ppermute | solution.py:34
  91.3 12.1 %collective-permute-start.35 = (bf16[1280,128]{1,0:T(8,128)(2,1)S(1)}, bf16[1280,128]{1,0:T(8,128)(2,1)S(1)}, u32[]{:S(2)}, u32[]{:S(2)}) collective-permute-start(bf16[1280,128]{1,0:T(8,128)(2,1)S(1)} %fusion.3), channel_id=1, source_target_pairs={{0,12},{1,13},{2,14},{3,15},{4,0},{5,1},{6,2},{7,3},{8,4},{9,5},{1... | collective-permute-start | bytes 983048 | tf_op jit(solution)/shard_map/ppermute | solution.py:34
  94.9 8.5 %collective-permute-start.33 = (bf16[1280,128]{1,0:T(8,128)(2,1)S(1)}, bf16[1280,128]{1,0:T(8,128)(2,1)S(1)}, u32[]{:S(2)}, u32[]{:S(2)}) collective-permute-start(bf16[1280,128]{1,0:T(8,128)(2,1)S(1)} %fusion.5), channel_id=1, source_target_pairs={{0,2},{1,3},{2,0},{3,1},{4,6},{5,7},{6,4},{7,5},{8,10},{9,11},{10,... | collective-permute-start | bytes 983048 | tf_op jit(solution)/shard_map/ppermute | solution.py:34

commit v17 on v16

--- a/solution.py
+++ b/solution.py
@@ -81,9 +81,9 @@
     sends = blocks_of(first, False)
     total = {name: paired(*pair) for name, *pair in zip(first, sends, blocks_of(first, True))}
     crossing, aside = list(map(narrow, halves(total[FAR2]))), narrow(total[FAR1])
-    *crossing, aside = blocks_of.hold(*crossing, aside)
     two_on = [move(part, ACROSS) for part in crossing]
     joining = move(aside, ALONG)
+    (joining,) = blocks_of.hold(joining)
     total.update({name: paired(*pair) for name, *pair in zip(rest, blocks_of(rest, False), blocks_of(rest, True))})
 
     crossing, two_on[1] = tie(narrow(total[FAR3]), two_on[1])

time: 105 us -> 108 us (1.029)
  waiting for transfers between devices: 39.9 us -> 41.8 us
  starting transfers between devices: 31.7 us -> 32.9 us
    ppermute x36, waiting for transfers between devices: 39.9 us -> 41.8 us  [move(): return lax.ppermute(array, 'aux', pairs)]
    ppermute x36, starting transfers between devices: 31.7 us -> 32.9 us  [move(): return lax.ppermute(array, 'aux', pairs)]
  transfers between devices with their start and end apart: 36 -> 36, of which waited for: 17 -> 14; matrix products, arithmetic and copies ran while one was open for 10% -> 10% of each run, Pallas kernels for 16% -> 16%
where the time goes in v17:
time: 108 us
  waiting for transfers between devices  41.8 us (39%)
  starting transfers between devices  32.9 us (30%)
  Pallas kernels  19.7 us (18%)
  local copies, waits for them, and re-layouts  8.13 us (8%)
  other arithmetic  4.11 us (4%)
    ppermute x36, waiting for transfers between devices, move(): return lax.ppermute(array, 'aux', pairs)  41.8 us
    ppermute x36, starting transfers between devices, move(): return lax.ppermute(array, 'aux', pairs)  32.9 us
    pallas_call x8, Pallas kernels, call(): pl.pallas_call(kernel, out_shape=outs, in_specs=in_specs, out_specs=[VMEM...  19.7 us
    unnamed x11, local copies, waits for them, and re-layouts  6.91 us
  transfers between devices with their start and end apart: 36, of which 14 were waited for; matrix products, arithmetic and copies ran while one was open for 10% of the time, Pallas kernels for 16%

profile of v17, /device:TPU:0, one launch (start us, length us, event | category | flops | bytes accessed | tf_op | source)
XLA Modules:
  0.0 107.6 jit_solution(16807792811609286141)
XLA Ops:
  0.0 0.5 collective-permute-start.9
  0.5 1.1 %constant_dynamic-slice_fusion.1 = (bf16[1280,128]{1,0:T(8,128)(2,1)S(1)}, bf16[1280,128]{1,0:T(8,128)(2,1)S(1)}) fusion(bf16[1280,256]{1,0:T(8,128)(2,1)} %param.7, s32[]{:T(128)S(6)} %select_n.162, s32[]{:T(128)S(6)} %select_n.161), kind=kLoop, calls=%fused_computation.91 | loop fusion | bytes 1310728 | tf_op jit(solution)/shard_map/dynamic_slice | solution.py:244
  1.6 2.6 %collective-permute-start.2 = (bf16[1280,128]{1,0:T(8,128)(2,1)S(1)}, bf16[1280,128]{1,0:T(8,128)(2,1)S(1)}, u32[]{:S(2)}, u32[]{:S(2)}) collective-permute-start(bf16[1280,128]{1,0:T(8,128)(2,1)S(1)} %get-tuple-element.115.refs_0_), channel_id=1, source_target_pairs={{0,4},{1,5},{2,6},{3,7},{4,8},{5,9},{6,10},{7,11},{8,12},{9,13},{1... | collective-permute-start | bytes 983048 | tf_op jit(solution)/shard_map/ppermute | solution.py:34
  4.2 1.5 %collective-permute-start.3 = (bf16[1280,128]{1,0:T(8,128)(2,1)S(1)}, bf16[1280,128]{1,0:T(8,128)(2,1)S(1)}, u32[]{:S(2)}, u32[]{:S(2)}) collective-permute-start(bf16[1280,128]{1,0:T(8,128)(2,1)S(1)} %get-tuple-element.115.refs_0_), channel_id=1, source_target_pairs={{0,2},{1,3},{2,0},{3,1},{4,6},{5,7},{6,4},{7,5},{8,10},{9,11},{10,... | collective-permute-start | bytes 983048 | tf_op jit(solution)/shard_map/ppermute | solution.py:34
  5.7 0.5 collective-permute-start
  6.2 0.7 constant_dynamic-update-slice_fusion.1
  7.7 0.7 compare_select_fusion.3
  8.4 0.9 collective-permute-done.8.refs_1_
  9.3 1.6 %collective-permute-start.10 = (bf16[1280,128]{1,0:T(8,128)(2,1)S(1)}, bf16[1280,128]{1,0:T(8,128)(2,1)S(1)}, u32[]{:S(2)}, u32[]{:S(2)}) collective-permute-start(bf16[1280,128]{1,0:T(8,128)(2,1)S(1)} %collective-permute-done.8.refs_1_), channel_id=1, source_target_pairs={{0,4},{1,5},{2,6},{3,7},{4,8},{5,9},{6,10},{7,11},{8,12},{9,13},{1... | collective-permute-start | bytes 983048 | tf_op jit(solution)/shard_map/ppermute | solution.py:34
  10.9 0.5 collective-permute-start.11
  11.4 0.6 fusion.27
  12.0 2.8 %collective-permute-done.2.refs_0_ = bf16[1280,128]{1,0:T(8,128)(2,1)S(1)} collective-permute-done((bf16[1280,128]{1,0:T(8,128)(2,1)S(1)}, bf16[1280,128]{1,0:T(8,128)(2,1)S(1)}, u32[]{:S(2)}, u32[]{:S(2)}) %collective-permute-start.2) | collective-permute-done | bytes 327712 | tf_op jit(solution)/shard_map/ppermute | solution.py:34
  14.8 1.5 %collective-permute-start.4 = (bf16[1280,128]{1,0:T(8,128)(2,1)S(1)}, bf16[1280,128]{1,0:T(8,128)(2,1)S(1)}, u32[]{:S(2)}, u32[]{:S(2)}) collective-permute-start(bf16[1280,128]{1,0:T(8,128)(2,1)S(1)} %collective-permute-done.2.refs_0_), channel_id=1, source_target_pairs={{0,4},{1,5},{2,6},{3,7},{4,8},{5,9},{6,10},{7,11},{8,12},{9,13},{1... | collective-permute-start | bytes 983048 | tf_op jit(solution)/shard_map/ppermute | solution.py:34
  16.3 1.5 %collective-permute-start.5 = (bf16[1280,128]{1,0:T(8,128)(2,1)S(1)}, bf16[1280,128]{1,0:T(8,128)(2,1)}, u32[]{:S(2)}, u32[]{:S(2)}) collective-permute-start(bf16[1280,128]{1,0:T(8,128)(2,1)S(1)} %collective-permute-done.2.refs_0_), channel_id=1, source_target_pairs={{0,2},{1,3},{2,0},{3,1},{4,6},{5,7},{6,4},{7,5},{8,10},{9,11},{10,... | collective-permute-start | bytes 983048 | tf_op jit(solution)/shard_map/ppermute | solution.py:34
  17.8 2.1 %copy.9 = bf16[32,8,32,128]{3,2,1,0:T(8,128)(2,1)S(1)} copy(bf16[32,8,32,128]{3,1,2,0:T(8,128)(2,1)} %bitcast.63) | data formatting | bytes 4194304
  19.9 3.4 %copy.10 = bf16[32,8,32,128]{3,2,1,0:T(8,128)(2,1)} copy(bf16[32,8,32,128]{3,1,2,0:T(8,128)(2,1)} %bitcast.25) | data formatting | bytes 4194304
  23.3 0.7 copy-done
  24.1 1.6 %collective-permute-start.12 = (bf16[1280,128]{1,0:T(8,128)(2,1)S(1)}, bf16[1280,128]{1,0:T(8,128)(2,1)}, u32[]{:S(2)}, u32[]{:S(2)}) collective-permute-start(bf16[1280,128]{1,0:T(8,128)(2,1)S(1)} %collective-permute-done.10.refs_1_), channel_id=1, source_target_pairs={{0,4},{1,5},{2,6},{3,7},{4,8},{5,9},{6,10},{7,11},{8,12},{9,13},{1... | collective-permute-start | bytes 983048 | tf_op jit(solution)/shard_map/ppermute | solution.py:34
  25.6 0.5 collective-permute-start.13
  26.2 0.3 convert_reduce_fusion
  26.5 0.5 select_reduce_fusion
  27.0 0.1 concatenate.10.table_ref
  27.1 0.1 convert_reduce_fusion.1.bounds_ref
  27.2 1.6 %collective-permute-done.4.refs_0_ = bf16[1280,128]{1,0:T(8,128)(2,1)S(1)} collective-permute-done((bf16[1280,128]{1,0:T(8,128)(2,1)S(1)}, bf16[1280,128]{1,0:T(8,128)(2,1)S(1)}, u32[]{:S(2)}, u32[]{:S(2)}) %collective-permute-start.4) | collective-permute-done | bytes 327712 | tf_op jit(solution)/shard_map/ppermute | solution.py:34
  28.9 1.6 %collective-permute-start.6 = (bf16[1280,128]{1,0:T(8,128)(2,1)S(1)}, bf16[1280,128]{1,0:T(8,128)(2,1)S(1)}, u32[]{:S(2)}, u32[]{:S(2)}) collective-permute-start(bf16[1280,128]{1,0:T(8,128)(2,1)S(1)} %collective-permute-done.4.refs_0_), channel_id=1, source_target_pairs={{0,4},{1,5},{2,6},{3,7},{4,8},{5,9},{6,10},{7,11},{8,12},{9,13},{1... | collective-permute-start | bytes 983048 | tf_op jit(solution)/shard_map/ppermute | solution.py:34
  30.5 1.5 %collective-permute-start.7 = (bf16[1280,128]{1,0:T(8,128)(2,1)S(1)}, bf16[1280,128]{1,0:T(8,128)(2,1)S(1)}, u32[]{:S(2)}, u32[]{:S(2)}) collective-permute-start(bf16[1280,128]{1,0:T(8,128)(2,1)S(1)} %collective-permute-done.4.refs_0_), channel_id=1, source_target_pairs={{0,2},{1,3},{2,0},{3,1},{4,6},{5,7},{6,4},{7,5},{8,10},{9,11},{10,... | collective-permute-start | bytes 983048 | tf_op jit(solution)/shard_map/ppermute | solution.py:34
  32.0 3.4 %shard_map.46 = (f32[41024,128]{1,0:T(8,128)S(1)}, bf16[512,32,128]{2,1,0:T(8,128)(2,1)S(1)}) custom-call(s32[1584]{0:T(1024)S(1)} %concatenate.10.table_ref, s32[6]{0:T(128)S(1)} %convert_reduce_fusion.1.bounds_ref, bf16[1280,128]{1,0:T(8,128)(2,1)} %copy-done.2, bf16[1280,128]{1,0:T(8,128)(2,1)} %copy-done.3, bf16[256,32,128]{2,1,0:T(8,128)(2,1)S(1)} %bitcast.53, ...), custom_call_target="tpu_custom_call" | custom-call | flops 107374184 | bytes 4194304 | tf_op jit(solution)/shard_map/pallas_call | solution.py:217
  35.3 1.3 %collective-permute-done.12.refs_1_ = bf16[1280,128]{1,0:T(8,128)(2,1)} collective-permute-done((bf16[1280,128]{1,0:T(8,128)(2,1)S(1)}, bf16[1280,128]{1,0:T(8,128)(2,1)}, u32[]{:S(2)}, u32[]{:S(2)}) %collective-permute-start.12) | collective-permute-done | bytes 327712 | tf_op jit(solution)/shard_map/ppermute | solution.py:34
  36.6 0.9 collective-permute-start.15
  37.5 1.5 %collective-permute-start.16 = (bf16[1280,128]{1,0:T(8,128)(2,1)}, bf16[1280,128]{1,0:T(8,128)(2,1)S(1)}, u32[]{:S(2)}, u32[]{:S(2)}) collective-permute-start(bf16[1280,128]{1,0:T(8,128)(2,1)} %collective-permute-done.12.refs_1_), channel_id=1, source_target_pairs={{0,2},{1,3},{2,0},{3,1},{4,6},{5,7},{6,4},{7,5},{8,10},{9,11},{10,... | collective-permute-start | bytes 983048 | tf_op jit(solution)/shard_map/ppermute | solution.py:34
  39.0 4.5 %collective-permute-done.6.refs_0_ = bf16[1280,128]{1,0:T(8,128)(2,1)S(1)} collective-permute-done((bf16[1280,128]{1,0:T(8,128)(2,1)S(1)}, bf16[1280,128]{1,0:T(8,128)(2,1)S(1)}, u32[]{:S(2)}, u32[]{:S(2)}) %collective-permute-start.6) | collective-permute-done | bytes 327712 | tf_op jit(solution)/shard_map/ppermute | solution.py:34
  43.5 2.8 %shard_map.47.refs_5_ = f32[41024,128]{1,0:T(8,128)S(1)} custom-call(s32[1584]{0:T(1024)S(1)} %concatenate.10.table_ref, s32[6]{0:T(128)S(1)} %convert_reduce_fusion.1.bounds_ref, bf16[1280,128]{1,0:T(8,128)(2,1)S(1)} %collective-permute-done.2.refs_0_, bf16[1280,128]{1,0:T(8,128)(2,1)S(1)} %collective-permute-done.10.refs_1_, ...), custom_call_target="tpu_custom_call", output_to_operand_aliasing={{}: (7, {})} | custom-call | flops 107374184 | bytes 4194304 | tf_op jit(solution)/shard_map/pallas_call | solution.py:217
  46.3 0.9 collective-permute-start.14
  47.3 2.9 %collective-permute-done.15.refs_1_ = bf16[1280,128]{1,0:T(8,128)(2,1)S(1)} collective-permute-done((bf16[1280,128]{1,0:T(8,128)(2,1)}, bf16[1280,128]{1,0:T(8,128)(2,1)S(1)}, u32[]{:S(2)}, u32[]{:S(2)}) %collective-permute-start.15) | collective-permute-done | bytes 327712 | tf_op jit(solution)/shard_map/ppermute | solution.py:34
  50.2 1.3 %collective-permute-start.17 = (bf16[1280,128]{1,0:T(8,128)(2,1)S(1)}, bf16[1280,128]{1,0:T(8,128)(2,1)S(1)}, u32[]{:S(2)}, u32[]{:S(2)}) collective-permute-start(bf16[1280,128]{1,0:T(8,128)(2,1)S(1)} %collective-permute-done.15.refs_1_), channel_id=1, source_target_pairs={{0,2},{1,3},{2,0},{3,1},{4,6},{5,7},{6,4},{7,5},{8,10},{9,11},{10,... | collective-permute-start | bytes 983048 | tf_op jit(solution)/shard_map/ppermute | solution.py:34
  51.4 3.9 %shard_map.48.refs_5_ = f32[41024,128]{1,0:T(8,128)S(1)} custom-call(s32[1584]{0:T(1024)S(1)} %concatenate.10.table_ref, s32[6]{0:T(128)S(1)} %convert_reduce_fusion.1.bounds_ref, bf16[1280,128]{1,0:T(8,128)(2,1)S(1)} %collective-permute-done.4.refs_0_, bf16[1280,128]{1,0:T(8,128)(2,1)} %collective-permute-done.12.refs_1_, ...), custom_call_target="tpu_custom_call", output_to_operand_aliasing={{}: (7, {})} | custom-call | flops 107374184 | bytes 4194304 | tf_op jit(solution)/shard_map/pallas_call | solution.py:217
  55.3 2.8 %shard_map.49.refs_3_ = f32[41024,128]{1,0:T(8,128)S(1)} custom-call(s32[1584]{0:T(1024)S(1)} %concatenate.10.table_ref, s32[6]{0:T(128)S(1)} %convert_reduce_fusion.1.bounds_ref, bf16[1280,128]{1,0:T(8,128)(2,1)S(1)} %collective-permute-done.6.refs_0_, bf16[1280,128]{1,0:T(8,128)(2,1)S(1)} %collective-permute-done.15.refs_1_, ...), custom_call_target="tpu_custom_call", output_to_operand_aliasing={{}: (7, {})} | custom-call | flops 107374184 | bytes 4194304 | tf_op jit(solution)/shard_map/pallas_call | solution.py:217
  58.2 0.7 collective-permute-done.17.refs_1_
  58.9 2.5 %shard_map.50 = (f32[41024,128]{1,0:T(8,128)S(1)}, bf16[256,128]{1,0:T(8,128)(2,1)S(1)}, bf16[1,1280,128]{2,1,0:T(8,128)(2,1)S(1)}, bf16[1,1280,128]{2,1,0:T(8,128)(2,1)S(1)}, bf16[1,1280,128]{2,1,0:T(8,128)(2,1)S(1)}) custom-call(s32[1584]{0:T(1024)S(1)} %concatenate.10.table_ref, ...), custom_call_target="tpu_custom_call", output_to_operand_aliasing={{0}: (7, {})} | custom-call | flops 359032416 | bytes 4194304 | tf_op jit(solution)/shard_map/pallas_call | solution.py:217
  61.5 0.5 collective-permute-start.22
  62.0 0.1 collective-permute-start.23
  62.1 1.2 %shard_map.51 = (f32[1,1280,128]{2,1,0:T(8,128)S(1)}, f32[1,1280,128]{2,1,0:T(8,128)S(1)}, f32[1,1280,128]{2,1,0:T(8,128)S(1)}) custom-call(s32[8]{0:T(128)S(1)} %fusion.30.chips_ref, s32[1]{0:T(128)} %bitcast.core_ref, f32[41024,128]{1,0:T(8,128)S(1)} %get-tuple-element.83.half, bf16[256,128]{1,0:T(8,128)(2,1)S(1)} %get-tuple-element.80.weights), custom_call_target="tpu_custom_call" | custom-call | flops 251658240 | bytes 4194304 | tf_op jit(solution)/shard_map/pallas_call | solution.py:217
  63.4 1.2 %collective-permute-start.19 = (bf16[1280,128]{1,0:T(8,128)(2,1)S(1)}, bf16[1280,128]{1,0:T(8,128)(2,1)S(1)}, u32[]{:S(2)}, u32[]{:S(2)}) collective-permute-start(bf16[1280,128]{1,0:T(8,128)(2,1)S(1)} %fusion.9), channel_id=1, source_target_pairs={{0,4},{1,5},{2,6},{3,7},{4,8},{5,9},{6,10},{7,11},{8,12},{9,13},{1... | collective-permute-start | bytes 983048 | tf_op jit(solution)/shard_map/ppermute | solution.py:34
  64.7 1.3 %collective-permute-start.28 = (bf16[640,128]{1,0:T(8,128)(2,1)S(1)}, bf16[640,128]{1,0:T(8,128)(2,1)S(1)}, u32[]{:S(2)}, u32[]{:S(2)}) collective-permute-start(bf16[640,128]{1,0:T(8,128)(2,1)S(1)} %get-tuple-element.117), channel_id=1, source_target_pairs={{0,2},{1,3},{2,0},{3,1},{4,6},{5,7},{6,4},{7,5},{8,10},{9,11},{10,... | collective-permute-start | bytes 491528 | tf_op jit(solution)/shard_map/ppermute | solution.py:34
  66.0 0.8 collective-permute-start.24
  66.8 8.5 %collective-permute-done.19 = bf16[1280,128]{1,0:T(8,128)(2,1)S(1)} collective-permute-done((bf16[1280,128]{1,0:T(8,128)(2,1)S(1)}, bf16[1280,128]{1,0:T(8,128)(2,1)S(1)}, u32[]{:S(2)}, u32[]{:S(2)}) %collective-permute-start.19) | collective-permute-done | bytes 327712 | tf_op jit(solution)/shard_map/ppermute | solution.py:34
  75.3 1.6 %shard_map.53 = (bf16[1,1280,128]{2,1,0:T(8,128)(2,1)S(1)}, bf16[1,1280,128]{2,1,0:T(8,128)(2,1)S(1)}, bf16[1,1280,128]{2,1,0:T(8,128)(2,1)S(1)}, bf16[1,1280,12...) custom-call(s32[8]{0:T(128)S(1)} %fusion.30.chips_ref, s32[1]{0:T(128)} %bitcast.core_ref, ...), custom_call_target="tpu_custom_call" | custom-call | flops 419430400 | bytes 4194304 | tf_op jit(solution)/shard_map/pallas_call | solution.py:217
  77.0 0.5 collective-permute-start.21
  77.6 0.1 collective-permute-start.20
  77.6 1.5 %shard_map.52 = (f32[1,1280,128]{2,1,0:T(8,128)S(1)}, f32[1,1280,128]{2,1,0:T(8,128)S(1)}, f32[1,1280,128]{2,1,0:T(8,128)S(1)}, f32[1,1280,128]{2,1,0:T(8,128)S(1)}, f32[1,1280,128]{2,1,0:T(8,128)S(1)}) custom-call(s32[8]{0:T(128)S(1)} %fusion.30.chips_ref, s32[1]{0:T(128)} %bitcast.core_ref, f32[41024,128]{1,0:T(8,128)S(1)} %get-tuple-element.83.half, ...), custom_call_target="tpu_custom_call" | custom-call | flops 419430400 | bytes 4194304 | tf_op jit(solution)/shard_map/pallas_call | solution.py:217
  79.2 0.5 collective-permute-start.31
  79.8 0.1 collective-permute-start.34
  80.1 0.9 collective-permute-done.31
  81.0 0.1 fusion.5
  81.1 1.8 %collective-permute-start.32 = (bf16[1280,128]{1,0:T(8,128)(2,1)S(1)}, bf16[1280,128]{1,0:T(8,128)(2,1)S(1)}, u32[]{:S(2)}, u32[]{:S(2)}) collective-permute-start(bf16[1280,128]{1,0:T(8,128)(2,1)S(1)} %fusion.6), channel_id=1, source_target_pairs={{0,2},{1,3},{2,0},{3,1},{4,6},{5,7},{6,4},{7,5},{8,10},{9,11},{10,... | collective-permute-start | bytes 983048 | tf_op jit(solution)/shard_map/ppermute | solution.py:34
  83.0 5.9 %collective-permute-done.25 = bf16[640,128]{1,0:T(8,128)(2,1)S(1)} collective-permute-done((bf16[640,128]{1,0:T(8,128)(2,1)S(1)}, bf16[640,128]{1,0:T(8,128)(2,1)S(1)}, u32[]{:S(2)}, u32[]{:S(2)}) %collective-permute-start.25) | collective-permute-done | bytes 163872 | tf_op jit(solution)/shard_map/ppermute | solution.py:34
  89.0 2.9 %collective-permute-done.29 = bf16[640,128]{1,0:T(8,128)(2,1)S(1)} collective-permute-done((bf16[640,128]{1,0:T(8,128)(2,1)S(1)}, bf16[640,128]{1,0:T(8,128)(2,1)S(1)}, u32[]{:S(2)}, u32[]{:S(2)}) %collective-permute-start.29) | collective-permute-done | bytes 163872 | tf_op jit(solution)/shard_map/ppermute | solution.py:34
  92.0 0.1 fusion.3
  92.2 3.8 %collective-permute-start.35 = (bf16[1280,128]{1,0:T(8,128)(2,1)S(1)}, bf16[1280,128]{1,0:T(8,128)(2,1)S(1)}, u32[]{:S(2)}, u32[]{:S(2)}) collective-permute-start(bf16[1280,128]{1,0:T(8,128)(2,1)S(1)} %fusion.3), channel_id=1, source_target_pairs={{0,12},{1,13},{2,14},{3,15},{4,0},{5,1},{6,2},{7,3},{8,4},{9,5},{1... | collective-permute-start | bytes 983048 | tf_op jit(solution)/shard_map/ppermute | solution.py:34
  96.0 1.7 %collective-permute-start.33 = (bf16[1280,128]{1,0:T(8,128)(2,1)S(1)}, bf16[1280,128]{1,0:T(8,128)(2,1)S(1)}, u32[]{:S(2)}, u32[]{:S(2)}) collective-permute-start(bf16[1280,128]{1,0:T(8,128)(2,1)S(1)} %fusion.5), channel_id=1, source_target_pairs={{0,2},{1,3},{2,0},{3,1},{4,6},{5,7},{6,4},{7,5},{8,10},{9,11},{10,... | collective-permute-start | bytes 983048 | tf_op jit(solution)/shard_map/ppermute | solution.py:34
  97.8 3.2 %collective-permute-done.30 = bf16[640,128]{1,0:T(8,128)(2,1)S(1)} collective-permute-done((bf16[640,128]{1,0:T(8,128)(2,1)S(1)}, bf16[640,128]{1,0:T(8,128)(2,1)S(1)}, u32[]{:S(2)}, u32[]{:S(2)}) %collective-permute-start.30) | collective-permute-done | bytes 163872 | tf_op jit(solution)/shard_map/ppermute | solution.py:34
  100.9 0.1 fusion.8
  101.0 5.6 %collective-permute-done.35 = bf16[1280,128]{1,0:T(8,128)(2,1)S(1)} collective-permute-done((bf16[1280,128]{1,0:T(8,128)(2,1)S(1)}, bf16[1280,128]{1,0:T(8,128)(2,1)S(1)}, u32[]{:S(2)}, u32[]{:S(2)}) %collective-permute-start.35) | collective-permute-done | bytes 327712 | tf_op jit(solution)/shard_map/ppermute | solution.py:34
  106.6 1.0 add_multiply_fusion
  (51 shorter events, 1.1 us)
Async XLA Ops:
  0.0 9.3 %collective-permute-start.9 = (bf16[256,4096]{1,0:T(8,128)(2,1)}, bf16[256,4096]{1,0:T(8,128)(2,1)}, u32[]{:S(2)}, u32[]{:S(2)}) collective-permute-start(bf16[256,4096]{1,0:T(8,128)(2,1)} %param.4), channel_id=1, source_target_pairs={{0,1},{1,0},{2,3},{3,2},{4,5},{5,4},{6,7},{7,6},{8,9},{9,8},{10,11... | collective-permute-start | bytes 6291464 | tf_op jit(solution)/shard_map/ppermute | solution.py:34
  1.6 13.2 %copy-start.2 = (bf16[1280,128]{1,0:T(8,128)(2,1)}, bf16[1280,128]{1,0:T(8,128)(2,1)S(1)}, u32[]{:S(2)}) copy-start(bf16[1280,128]{1,0:T(8,128)(2,1)S(1)} %get-tuple-element.115.refs_0_) | copy-start | bytes 983044
  1.6 13.2 %collective-permute-start.2 = (bf16[1280,128]{1,0:T(8,128)(2,1)S(1)}, bf16[1280,128]{1,0:T(8,128)(2,1)S(1)}, u32[]{:S(2)}, u32[]{:S(2)}) collective-permute-start(bf16[1280,128]{1,0:T(8,128)(2,1)S(1)} %get-tuple-element.115.refs_0_), channel_id=1, source_target_pairs={{0,4},{1,5},{2,6},{3,7},{4,8},{5,9},{6,10},{7,11},{8,12},{9,13},{1... | collective-permute-start | bytes 983048 | tf_op jit(solution)/shard_map/ppermute | solution.py:34
  4.2 10.6 %collective-permute-start.3 = (bf16[1280,128]{1,0:T(8,128)(2,1)S(1)}, bf16[1280,128]{1,0:T(8,128)(2,1)S(1)}, u32[]{:S(2)}, u32[]{:S(2)}) collective-permute-start(bf16[1280,128]{1,0:T(8,128)(2,1)S(1)} %get-tuple-element.115.refs_0_), channel_id=1, source_target_pairs={{0,2},{1,3},{2,0},{3,1},{4,6},{5,7},{6,4},{7,5},{8,10},{9,11},{10,... | collective-permute-start | bytes 983048 | tf_op jit(solution)/shard_map/ppermute | solution.py:34
  5.7 1.9 %collective-permute-start.1 = (s32[256,2]{0,1:T(2,128)}, s32[256,2]{0,1:T(2,128)S(1)}, u32[]{:S(2)}, u32[]{:S(2)}) collective-permute-start(s32[256,2]{0,1:T(2,128)} %param.5), channel_id=1, source_target_pairs={{0,1},{1,0},{2,3},{3,2},{4,5},{5,4},{6,7},{7,6},{8,9},{9,8},{10,11... | collective-permute-start | bytes 6152 | tf_op jit(solution)/shard_map/ppermute | solution.py:34
  5.7 2.0 %collective-permute-start = (s32[1]{0:T(128)}, s32[1]{0:T(128)}, u32[]{:S(2)}, u32[]{:S(2)}) collective-permute-start(s32[1]{0:T(128)} %param.6), channel_id=1, source_target_pairs={{0,1},{1,0},{2,3},{3,2},{4,5},{5,4},{6,7},{7,6},{8,9},{9,8},{10,11... | collective-permute-start | bytes 20 | tf_op jit(solution)/shard_map/ppermute | solution.py:34
  7.6 1.7 %collective-permute-start.8 = (bf16[1280,128]{1,0:T(8,128)(2,1)S(1)}, bf16[1280,128]{1,0:T(8,128)(2,1)S(1)}, u32[]{:S(2)}, u32[]{:S(2)}) collective-permute-start(bf16[1280,128]{1,0:T(8,128)(2,1)S(1)} %get-tuple-element.114), channel_id=1, source_target_pairs={{0,1},{1,0},{2,3},{3,2},{4,5},{5,4},{6,7},{7,6},{8,9},{9,8},{10,11... | collective-permute-start | bytes 983048 | tf_op jit(solution)/shard_map/ppermute | solution.py:34
  9.3 10.6 %copy-start.3 = (bf16[1280,128]{1,0:T(8,128)(2,1)}, bf16[1280,128]{1,0:T(8,128)(2,1)S(1)}, u32[]{:S(2)}) copy-start(bf16[1280,128]{1,0:T(8,128)(2,1)S(1)} %collective-permute-done.8.refs_1_) | copy-start | bytes 983044
  9.3 14.0 %collective-permute-start.10 = (bf16[1280,128]{1,0:T(8,128)(2,1)S(1)}, bf16[1280,128]{1,0:T(8,128)(2,1)S(1)}, u32[]{:S(2)}, u32[]{:S(2)}) collective-permute-start(bf16[1280,128]{1,0:T(8,128)(2,1)S(1)} %collective-permute-done.8.refs_1_), channel_id=1, source_target_pairs={{0,4},{1,5},{2,6},{3,7},{4,8},{5,9},{6,10},{7,11},{8,12},{9,13},{1... | collective-permute-start | bytes 983048 | tf_op jit(solution)/shard_map/ppermute | solution.py:34
  10.9 12.5 %collective-permute-start.11 = (bf16[1280,128]{1,0:T(8,128)(2,1)S(1)}, bf16[1280,128]{1,0:T(8,128)(2,1)S(1)}, u32[]{:S(2)}, u32[]{:S(2)}) collective-permute-start(bf16[1280,128]{1,0:T(8,128)(2,1)S(1)} %collective-permute-done.8.refs_1_), channel_id=1, source_target_pairs={{0,2},{1,3},{2,0},{3,1},{4,6},{5,7},{6,4},{7,5},{8,10},{9,11},{10,... | collective-permute-start | bytes 983048 | tf_op jit(solution)/shard_map/ppermute | solution.py:34
  14.8 14.0 %collective-permute-start.4 = (bf16[1280,128]{1,0:T(8,128)(2,1)S(1)}, bf16[1280,128]{1,0:T(8,128)(2,1)S(1)}, u32[]{:S(2)}, u32[]{:S(2)}) collective-permute-start(bf16[1280,128]{1,0:T(8,128)(2,1)S(1)} %collective-permute-done.2.refs_0_), channel_id=1, source_target_pairs={{0,4},{1,5},{2,6},{3,7},{4,8},{5,9},{6,10},{7,11},{8,12},{9,13},{1... | collective-permute-start | bytes 983048 | tf_op jit(solution)/shard_map/ppermute | solution.py:34
  16.3 12.6 %collective-permute-start.5 = (bf16[1280,128]{1,0:T(8,128)(2,1)S(1)}, bf16[1280,128]{1,0:T(8,128)(2,1)}, u32[]{:S(2)}, u32[]{:S(2)}) collective-permute-start(bf16[1280,128]{1,0:T(8,128)(2,1)S(1)} %collective-permute-done.2.refs_0_), channel_id=1, source_target_pairs={{0,2},{1,3},{2,0},{3,1},{4,6},{5,7},{6,4},{7,5},{8,10},{9,11},{10,... | collective-permute-start | bytes 983048 | tf_op jit(solution)/shard_map/ppermute | solution.py:34
  23.3 0.7 copy-start
  24.1 12.6 %collective-permute-start.12 = (bf16[1280,128]{1,0:T(8,128)(2,1)S(1)}, bf16[1280,128]{1,0:T(8,128)(2,1)}, u32[]{:S(2)}, u32[]{:S(2)}) collective-permute-start(bf16[1280,128]{1,0:T(8,128)(2,1)S(1)} %collective-permute-done.10.refs_1_), channel_id=1, source_target_pairs={{0,4},{1,5},{2,6},{3,7},{4,8},{5,9},{6,10},{7,11},{8,12},{9,13},{1... | collective-permute-start | bytes 983048 | tf_op jit(solution)/shard_map/ppermute | solution.py:34
  25.6 11.0 %collective-permute-start.13 = (bf16[1280,128]{1,0:T(8,128)(2,1)S(1)}, bf16[1280,128]{1,0:T(8,128)(2,1)}, u32[]{:S(2)}, u32[]{:S(2)}) collective-permute-start(bf16[1280,128]{1,0:T(8,128)(2,1)S(1)} %collective-permute-done.10.refs_1_), channel_id=1, source_target_pairs={{0,2},{1,3},{2,0},{3,1},{4,6},{5,7},{6,4},{7,5},{8,10},{9,11},{10,... | collective-permute-start | bytes 983048 | tf_op jit(solution)/shard_map/ppermute | solution.py:34
  27.2 16.3 %copy-start.1 = (bf16[1280,128]{1,0:T(8,128)(2,1)S(1)}, bf16[1280,128]{1,0:T(8,128)(2,1)}, u32[]{:S(2)}) copy-start(bf16[1280,128]{1,0:T(8,128)(2,1)} %copy-done) | copy-start | bytes 983044
  28.9 14.6 %collective-permute-start.6 = (bf16[1280,128]{1,0:T(8,128)(2,1)S(1)}, bf16[1280,128]{1,0:T(8,128)(2,1)S(1)}, u32[]{:S(2)}, u32[]{:S(2)}) collective-permute-start(bf16[1280,128]{1,0:T(8,128)(2,1)S(1)} %collective-permute-done.4.refs_0_), channel_id=1, source_target_pairs={{0,4},{1,5},{2,6},{3,7},{4,8},{5,9},{6,10},{7,11},{8,12},{9,13},{1... | collective-permute-start | bytes 983048 | tf_op jit(solution)/shard_map/ppermute | solution.py:34
  30.5 13.1 %collective-permute-start.7 = (bf16[1280,128]{1,0:T(8,128)(2,1)S(1)}, bf16[1280,128]{1,0:T(8,128)(2,1)S(1)}, u32[]{:S(2)}, u32[]{:S(2)}) collective-permute-start(bf16[1280,128]{1,0:T(8,128)(2,1)S(1)} %collective-permute-done.4.refs_0_), channel_id=1, source_target_pairs={{0,2},{1,3},{2,0},{3,1},{4,6},{5,7},{6,4},{7,5},{8,10},{9,11},{10,... | collective-permute-start | bytes 983048 | tf_op jit(solution)/shard_map/ppermute | solution.py:34
  36.6 13.5 %collective-permute-start.15 = (bf16[1280,128]{1,0:T(8,128)(2,1)}, bf16[1280,128]{1,0:T(8,128)(2,1)S(1)}, u32[]{:S(2)}, u32[]{:S(2)}) collective-permute-start(bf16[1280,128]{1,0:T(8,128)(2,1)} %collective-permute-done.12.refs_1_), channel_id=1, source_target_pairs={{0,4},{1,5},{2,6},{3,7},{4,8},{5,9},{6,10},{7,11},{8,12},{9,13},{1... | collective-permute-start | bytes 983048 | tf_op jit(solution)/shard_map/ppermute | solution.py:34
  37.5 12.6 %collective-permute-start.16 = (bf16[1280,128]{1,0:T(8,128)(2,1)}, bf16[1280,128]{1,0:T(8,128)(2,1)S(1)}, u32[]{:S(2)}, u32[]{:S(2)}) collective-permute-start(bf16[1280,128]{1,0:T(8,128)(2,1)} %collective-permute-done.12.refs_1_), channel_id=1, source_target_pairs={{0,2},{1,3},{2,0},{3,1},{4,6},{5,7},{6,4},{7,5},{8,10},{9,11},{10,... | collective-permute-start | bytes 983048 | tf_op jit(solution)/shard_map/ppermute | solution.py:34
  46.3 11.8 %collective-permute-start.14 = (bf16[1280,128]{1,0:T(8,128)(2,1)S(1)}, bf16[1280,128]{1,0:T(8,128)(2,1)S(1)}, u32[]{:S(2)}, u32[]{:S(2)}) collective-permute-start(bf16[1280,128]{1,0:T(8,128)(2,1)S(1)} %collective-permute-done.7.refs_2_), channel_id=1, source_target_pairs={{0,4},{1,5},{2,6},{3,7},{4,8},{5,9},{6,10},{7,11},{8,12},{9,13},{1... | collective-permute-start | bytes 983048 | tf_op jit(solution)/shard_map/ppermute | solution.py:34
  50.2 8.7 %collective-permute-start.17 = (bf16[1280,128]{1,0:T(8,128)(2,1)S(1)}, bf16[1280,128]{1,0:T(8,128)(2,1)S(1)}, u32[]{:S(2)}, u32[]{:S(2)}) collective-permute-start(bf16[1280,128]{1,0:T(8,128)(2,1)S(1)} %collective-permute-done.15.refs_1_), channel_id=1, source_target_pairs={{0,2},{1,3},{2,0},{3,1},{4,6},{5,7},{6,4},{7,5},{8,10},{9,11},{10,... | collective-permute-start | bytes 983048 | tf_op jit(solution)/shard_map/ppermute | solution.py:34
  61.4 1.9 %collective-permute-start.18 = (bf16[1280,128]{1,0:T(8,128)(2,1)S(1)}, bf16[1280,128]{1,0:T(8,128)(2,1)S(1)}, u32[]{:S(2)}, u32[]{:S(2)}) collective-permute-start(bf16[1280,128]{1,0:T(8,128)(2,1)S(1)} %bitcast.61), channel_id=1, source_target_pairs={{0,1},{1,0},{2,3},{3,2},{4,5},{5,4},{6,7},{7,6},{8,9},{9,8},{10,11... | collective-permute-start | bytes 983048 | tf_op jit(solution)/shard_map/ppermute | solution.py:34
  61.5 15.4 %collective-permute-start.22 = (bf16[1280,128]{1,0:T(8,128)(2,1)S(1)}, bf16[1280,128]{1,0:T(8,128)(2,1)S(1)}, u32[]{:S(2)}, u32[]{:S(2)}) collective-permute-start(bf16[1280,128]{1,0:T(8,128)(2,1)S(1)} %bitcast.57), channel_id=1, source_target_pairs={{0,1},{1,0},{2,3},{3,2},{4,5},{5,4},{6,7},{7,6},{8,9},{9,8},{10,11... | collective-permute-start | bytes 983048 | tf_op jit(solution)/shard_map/ppermute | solution.py:34
  62.0 2.6 %collective-permute-start.23 = (bf16[1280,128]{1,0:T(8,128)(2,1)S(1)}, bf16[1280,128]{1,0:T(8,128)(2,1)S(1)}, u32[]{:S(2)}, u32[]{:S(2)}) collective-permute-start(bf16[1280,128]{1,0:T(8,128)(2,1)S(1)} %bitcast.59), channel_id=1, source_target_pairs={{0,1},{1,0},{2,3},{3,2},{4,5},{5,4},{6,7},{7,6},{8,9},{9,8},{10,11... | collective-permute-start | bytes 983048 | tf_op jit(solution)/shard_map/ppermute | solution.py:34
  63.4 11.9 %collective-permute-start.19 = (bf16[1280,128]{1,0:T(8,128)(2,1)S(1)}, bf16[1280,128]{1,0:T(8,128)(2,1)S(1)}, u32[]{:S(2)}, u32[]{:S(2)}) collective-permute-start(bf16[1280,128]{1,0:T(8,128)(2,1)S(1)} %fusion.9), channel_id=1, source_target_pairs={{0,4},{1,5},{2,6},{3,7},{4,8},{5,9},{6,10},{7,11},{8,12},{9,13},{1... | collective-permute-start | bytes 983048 | tf_op jit(solution)/shard_map/ppermute | solution.py:34
  64.7 15.1 %collective-permute-start.28 = (bf16[640,128]{1,0:T(8,128)(2,1)S(1)}, bf16[640,128]{1,0:T(8,128)(2,1)S(1)}, u32[]{:S(2)}, u32[]{:S(2)}) collective-permute-start(bf16[640,128]{1,0:T(8,128)(2,1)S(1)} %get-tuple-element.117), channel_id=1, source_target_pairs={{0,2},{1,3},{2,0},{3,1},{4,6},{5,7},{6,4},{7,5},{8,10},{9,11},{10,... | collective-permute-start | bytes 491528 | tf_op jit(solution)/shard_map/ppermute | solution.py:34
  66.0 14.0 %collective-permute-start.24 = (bf16[640,128]{1,0:T(8,128)(2,1)S(1)}, bf16[640,128]{1,0:T(8,128)(2,1)S(1)}, u32[]{:S(2)}, u32[]{:S(2)}) collective-permute-start(bf16[640,128]{1,0:T(8,128)(2,1)S(1)} %get-tuple-element.116), channel_id=1, source_target_pairs={{0,2},{1,3},{2,0},{3,1},{4,6},{5,7},{6,4},{7,5},{8,10},{9,11},{10,... | collective-permute-start | bytes 491528 | tf_op jit(solution)/shard_map/ppermute | solution.py:34
  76.9 2.3 %collective-permute-start.27 = (bf16[1280,128]{1,0:T(8,128)(2,1)S(1)}, bf16[1280,128]{1,0:T(8,128)(2,1)S(1)}, u32[]{:S(2)}, u32[]{:S(2)}) collective-permute-start(bf16[1280,128]{1,0:T(8,128)(2,1)S(1)} %bitcast.60), channel_id=1, source_target_pairs={{0,1},{1,0},{2,3},{3,2},{4,5},{5,4},{6,7},{7,6},{8,9},{9,8},{10,11... | collective-permute-start | bytes 983048 | tf_op jit(solution)/shard_map/ppermute | solution.py:34
  77.0 4.1 %collective-permute-start.21 = (bf16[1280,128]{1,0:T(8,128)(2,1)S(1)}, bf16[1280,128]{1,0:T(8,128)(2,1)S(1)}, u32[]{:S(2)}, u32[]{:S(2)}) collective-permute-start(bf16[1280,128]{1,0:T(8,128)(2,1)S(1)} %bitcast.56), channel_id=1, source_target_pairs={{0,1},{1,0},{2,3},{3,2},{4,5},{5,4},{6,7},{7,6},{8,9},{9,8},{10,11... | collective-permute-start | bytes 983048 | tf_op jit(solution)/shard_map/ppermute | solution.py:34
  77.6 20.2 %collective-permute-start.20 = (bf16[1280,128]{1,0:T(8,128)(2,1)S(1)}, bf16[1280,128]{1,0:T(8,128)(2,1)S(1)}, u32[]{:S(2)}, u32[]{:S(2)}) collective-permute-start(bf16[1280,128]{1,0:T(8,128)(2,1)S(1)} %bitcast.54), channel_id=1, source_target_pairs={{0,1},{1,0},{2,3},{3,2},{4,5},{5,4},{6,7},{7,6},{8,9},{9,8},{10,11... | collective-permute-start | bytes 983048 | tf_op jit(solution)/shard_map/ppermute | solution.py:34
  79.2 1.8 %collective-permute-start.31 = (bf16[1280,128]{1,0:T(8,128)(2,1)S(1)}, bf16[1280,128]{1,0:T(8,128)(2,1)S(1)}, u32[]{:S(2)}, u32[]{:S(2)}) collective-permute-start(bf16[1280,128]{1,0:T(8,128)(2,1)S(1)} %bitcast.58), channel_id=1, source_target_pairs={{0,1},{1,0},{2,3},{3,2},{4,5},{5,4},{6,7},{7,6},{8,9},{9,8},{10,11... | collective-permute-start | bytes 983048 | tf_op jit(solution)/shard_map/ppermute | solution.py:34
  79.8 12.2 %collective-permute-start.34 = (bf16[1280,128]{1,0:T(8,128)(2,1)S(1)}, bf16[1280,128]{1,0:T(8,128)(2,1)S(1)}, u32[]{:S(2)}, u32[]{:S(2)}) collective-permute-start(bf16[1280,128]{1,0:T(8,128)(2,1)S(1)} %bitcast.55), channel_id=1, source_target_pairs={{0,1},{1,0},{2,3},{3,2},{4,5},{5,4},{6,7},{7,6},{8,9},{9,8},{10,11... | collective-permute-start | bytes 983048 | tf_op jit(solution)/shard_map/ppermute | solution.py:34
  80.0 8.9 %collective-permute-start.25 = (bf16[640,128]{1,0:T(8,128)(2,1)S(1)}, bf16[640,128]{1,0:T(8,128)(2,1)S(1)}, u32[]{:S(2)}, u32[]{:S(2)}) collective-permute-start(bf16[640,128]{1,0:T(8,128)(2,1)S(1)} %get-tuple-element.112), channel_id=1, source_target_pairs={{0,4},{1,5},{2,6},{3,7},{4,8},{5,9},{6,10},{7,11},{8,12},{9,13},{1... | collective-permute-start | bytes 491528 | tf_op jit(solution)/shard_map/ppermute | solution.py:34
  81.0 10.9 %collective-permute-start.29 = (bf16[640,128]{1,0:T(8,128)(2,1)S(1)}, bf16[640,128]{1,0:T(8,128)(2,1)S(1)}, u32[]{:S(2)}, u32[]{:S(2)}) collective-permute-start(bf16[640,128]{1,0:T(8,128)(2,1)S(1)} %get-tuple-element.113), channel_id=1, source_target_pairs={{0,4},{1,5},{2,6},{3,7},{4,8},{5,9},{6,10},{7,11},{8,12},{9,13},{1... | collective-permute-start | bytes 491528 | tf_op jit(solution)/shard_map/ppermute | solution.py:34
  81.1 10.9 %collective-permute-start.32 = (bf16[1280,128]{1,0:T(8,128)(2,1)S(1)}, bf16[1280,128]{1,0:T(8,128)(2,1)S(1)}, u32[]{:S(2)}, u32[]{:S(2)}) collective-permute-start(bf16[1280,128]{1,0:T(8,128)(2,1)S(1)} %fusion.6), channel_id=1, source_target_pairs={{0,2},{1,3},{2,0},{3,1},{4,6},{5,7},{6,4},{7,5},{8,10},{9,11},{10,... | collective-permute-start | bytes 983048 | tf_op jit(solution)/shard_map/ppermute | solution.py:34
  88.9 8.9 %collective-permute-start.26 = (bf16[640,128]{1,0:T(8,128)(2,1)S(1)}, bf16[640,128]{1,0:T(8,128)(2,1)S(1)}, u32[]{:S(2)}, u32[]{:S(2)}) collective-permute-start(bf16[640,128]{1,0:T(8,128)(2,1)S(1)} %fusion.12), channel_id=1, source_target_pairs={{0,4},{1,5},{2,6},{3,7},{4,8},{5,9},{6,10},{7,11},{8,12},{9,13},{1... | collective-permute-start | bytes 491528 | tf_op jit(solution)/shard_map/ppermute | solution.py:34
  92.0 9.0 %collective-permute-start.30 = (bf16[640,128]{1,0:T(8,128)(2,1)S(1)}, bf16[640,128]{1,0:T(8,128)(2,1)S(1)}, u32[]{:S(2)}, u32[]{:S(2)}) collective-permute-start(bf16[640,128]{1,0:T(8,128)(2,1)S(1)} %add_convert_fusion), channel_id=1, source_target_pairs={{0,4},{1,5},{2,6},{3,7},{4,8},{5,9},{6,10},{7,11},{8,12},{9,13},{1... | collective-permute-start | bytes 491528 | tf_op jit(solution)/shard_map/ppermute | solution.py:34
  92.2 14.5 %collective-permute-start.35 = (bf16[1280,128]{1,0:T(8,128)(2,1)S(1)}, bf16[1280,128]{1,0:T(8,128)(2,1)S(1)}, u32[]{:S(2)}, u32[]{:S(2)}) collective-permute-start(bf16[1280,128]{1,0:T(8,128)(2,1)S(1)} %fusion.3), channel_id=1, source_target_pairs={{0,12},{1,13},{2,14},{3,15},{4,0},{5,1},{6,2},{7,3},{8,4},{9,5},{1... | collective-permute-start | bytes 983048 | tf_op jit(solution)/shard_map/ppermute | solution.py:34
  96.0 10.6 %collective-permute-start.33 = (bf16[1280,128]{1,0:T(8,128)(2,1)S(1)}, bf16[1280,128]{1,0:T(8,128)(2,1)S(1)}, u32[]{:S(2)}, u32[]{:S(2)}) collective-permute-start(bf16[1280,128]{1,0:T(8,128)(2,1)S(1)} %fusion.5), channel_id=1, source_target_pairs={{0,2},{1,3},{2,0},{3,1},{4,6},{5,7},{6,4},{7,5},{8,10},{9,11},{10,... | collective-permute-start | bytes 983048 | tf_op jit(solution)/shard_map/ppermute | solution.py:34

commit v18 on v16

--- a/solution.py
+++ b/solution.py
@@ -86,7 +86,8 @@
     joining = move(aside, ALONG)
     total.update({name: paired(*pair) for name, *pair in zip(rest, blocks_of(rest, False), blocks_of(rest, True))})
 
-    crossing, two_on[1] = tie(narrow(total[FAR3]), two_on[1])
+    two_on[1], joining = tie(two_on[1], joining)
+    crossing, two_on[0] = tie(narrow(total[FAR3]), two_on[0])
     three_on = move(crossing, ACROSS)
     crossing, three_on = tie(narrow(total[FAR0] + wide(joining)), three_on)
     straight = move(crossing, ACROSS)

time: 105 us -> 105 us (level)
  waiting for transfers between devices: 39.9 us -> 42.6 us
  Pallas kernels: 19.4 us -> 17.7 us
    ppermute x36, waiting for transfers between devices: 39.9 us -> 42.6 us  [move(): return lax.ppermute(array, 'aux', pairs)]
    pallas_call x8, Pallas kernels: 19.4 us -> 17.7 us  [call(): pl.pallas_call(kernel, out_shape=outs, in_specs=in_specs, out_specs=[VMEM...]
  transfers between devices with their start and end apart: 36 -> 36, of which waited for: 17 -> 18; matrix products, arithmetic and copies ran while one was open for 10% -> 10% of each run, Pallas kernels for 16% -> 13%
where the time goes in v18:
time: 105 us
  waiting for transfers between devices  42.6 us (41%)
  starting transfers between devices  31.2 us (30%)
  Pallas kernels  17.7 us (17%)
  local copies, waits for them, and re-layouts  8.14 us (8%)
  other arithmetic  4.19 us (4%)
    ppermute x36, waiting for transfers between devices, move(): return lax.ppermute(array, 'aux', pairs)  42.6 us
    ppermute x36, starting transfers between devices, move(): return lax.ppermute(array, 'aux', pairs)  31.2 us
    pallas_call x8, Pallas kernels, call(): pl.pallas_call(kernel, out_shape=outs, in_specs=in_specs, out_specs=[VMEM...  17.7 us
    unnamed x11, local copies, waits for them, and re-layouts  6.92 us
  transfers between devices with their start and end apart: 36, of which 18 were waited for; matrix products, arithmetic and copies ran while one was open for 10% of the time, Pallas kernels for 13%

profile of v18, /device:TPU:0, one launch (start us, length us, event | category | flops | bytes accessed | tf_op | source)
XLA Modules:
  0.0 104.9 jit_solution(12293799395599719240)
XLA Ops:
  0.0 0.5 collective-permute-start.9
  0.5 1.1 %constant_dynamic-slice_fusion.1 = (bf16[1280,128]{1,0:T(8,128)(2,1)S(1)}, bf16[1280,128]{1,0:T(8,128)(2,1)S(1)}) fusion(bf16[1280,256]{1,0:T(8,128)(2,1)} %param.7, s32[]{:T(128)S(6)} %select_n.162, s32[]{:T(128)S(6)} %select_n.161), kind=kLoop, calls=%fused_computation.91 | loop fusion | bytes 1310728 | tf_op jit(solution)/shard_map/dynamic_slice | solution.py:245
  1.6 2.6 %collective-permute-start.2 = (bf16[1280,128]{1,0:T(8,128)(2,1)S(1)}, bf16[1280,128]{1,0:T(8,128)(2,1)S(1)}, u32[]{:S(2)}, u32[]{:S(2)}) collective-permute-start(bf16[1280,128]{1,0:T(8,128)(2,1)S(1)} %get-tuple-element.123.refs_0_), channel_id=1, source_target_pairs={{0,4},{1,5},{2,6},{3,7},{4,8},{5,9},{6,10},{7,11},{8,12},{9,13},{1... | collective-permute-start | bytes 983048 | tf_op jit(solution)/shard_map/ppermute | solution.py:34
  4.2 1.5 %collective-permute-start.3 = (bf16[1280,128]{1,0:T(8,128)(2,1)S(1)}, bf16[1280,128]{1,0:T(8,128)(2,1)S(1)}, u32[]{:S(2)}, u32[]{:S(2)}) collective-permute-start(bf16[1280,128]{1,0:T(8,128)(2,1)S(1)} %get-tuple-element.123.refs_0_), channel_id=1, source_target_pairs={{0,2},{1,3},{2,0},{3,1},{4,6},{5,7},{6,4},{7,5},{8,10},{9,11},{10,... | collective-permute-start | bytes 983048 | tf_op jit(solution)/shard_map/ppermute | solution.py:34
  5.7 0.5 collective-permute-start
  6.2 0.7 constant_dynamic-update-slice_fusion.1
  7.7 0.7 compare_select_fusion.3
  8.4 0.8 collective-permute-done.8.refs_1_
  9.3 1.6 %collective-permute-start.10 = (bf16[1280,128]{1,0:T(8,128)(2,1)S(1)}, bf16[1280,128]{1,0:T(8,128)(2,1)S(1)}, u32[]{:S(2)}, u32[]{:S(2)}) collective-permute-start(bf16[1280,128]{1,0:T(8,128)(2,1)S(1)} %collective-permute-done.8.refs_1_), channel_id=1, source_target_pairs={{0,4},{1,5},{2,6},{3,7},{4,8},{5,9},{6,10},{7,11},{8,12},{9,13},{1... | collective-permute-start | bytes 983048 | tf_op jit(solution)/shard_map/ppermute | solution.py:34
  10.9 0.5 collective-permute-start.11
  11.4 0.7 fusion.27
  12.1 2.7 %collective-permute-done.2.refs_0_ = bf16[1280,128]{1,0:T(8,128)(2,1)S(1)} collective-permute-done((bf16[1280,128]{1,0:T(8,128)(2,1)S(1)}, bf16[1280,128]{1,0:T(8,128)(2,1)S(1)}, u32[]{:S(2)}, u32[]{:S(2)}) %collective-permute-start.2) | collective-permute-done | bytes 327712 | tf_op jit(solution)/shard_map/ppermute | solution.py:34
  14.8 1.5 %collective-permute-start.4 = (bf16[1280,128]{1,0:T(8,128)(2,1)S(1)}, bf16[1280,128]{1,0:T(8,128)(2,1)S(1)}, u32[]{:S(2)}, u32[]{:S(2)}) collective-permute-start(bf16[1280,128]{1,0:T(8,128)(2,1)S(1)} %collective-permute-done.2.refs_0_), channel_id=1, source_target_pairs={{0,4},{1,5},{2,6},{3,7},{4,8},{5,9},{6,10},{7,11},{8,12},{9,13},{1... | collective-permute-start | bytes 983048 | tf_op jit(solution)/shard_map/ppermute | solution.py:34
  16.3 1.5 %collective-permute-start.5 = (bf16[1280,128]{1,0:T(8,128)(2,1)S(1)}, bf16[1280,128]{1,0:T(8,128)(2,1)}, u32[]{:S(2)}, u32[]{:S(2)}) collective-permute-start(bf16[1280,128]{1,0:T(8,128)(2,1)S(1)} %collective-permute-done.2.refs_0_), channel_id=1, source_target_pairs={{0,2},{1,3},{2,0},{3,1},{4,6},{5,7},{6,4},{7,5},{8,10},{9,11},{10,... | collective-permute-start | bytes 983048 | tf_op jit(solution)/shard_map/ppermute | solution.py:34
  17.8 2.1 %copy.9 = bf16[32,8,32,128]{3,2,1,0:T(8,128)(2,1)S(1)} copy(bf16[32,8,32,128]{3,1,2,0:T(8,128)(2,1)} %bitcast.63) | data formatting | bytes 4194304
  19.9 3.4 %copy.10 = bf16[32,8,32,128]{3,2,1,0:T(8,128)(2,1)} copy(bf16[32,8,32,128]{3,1,2,0:T(8,128)(2,1)} %bitcast.25) | data formatting | bytes 4194304
  23.3 0.7 copy-done
  24.1 1.6 %collective-permute-start.12 = (bf16[1280,128]{1,0:T(8,128)(2,1)S(1)}, bf16[1280,128]{1,0:T(8,128)(2,1)}, u32[]{:S(2)}, u32[]{:S(2)}) collective-permute-start(bf16[1280,128]{1,0:T(8,128)(2,1)S(1)} %collective-permute-done.10.refs_1_), channel_id=1, source_target_pairs={{0,4},{1,5},{2,6},{3,7},{4,8},{5,9},{6,10},{7,11},{8,12},{9,13},{1... | collective-permute-start | bytes 983048 | tf_op jit(solution)/shard_map/ppermute | solution.py:34
  25.7 0.5 collective-permute-start.13
  26.2 0.3 convert_reduce_fusion
  26.5 0.5 select_reduce_fusion
  27.1 0.1 convert_reduce_fusion.1.bounds_ref
  27.2 1.6 %collective-permute-done.4.refs_0_ = bf16[1280,128]{1,0:T(8,128)(2,1)S(1)} collective-permute-done((bf16[1280,128]{1,0:T(8,128)(2,1)S(1)}, bf16[1280,128]{1,0:T(8,128)(2,1)S(1)}, u32[]{:S(2)}, u32[]{:S(2)}) %collective-permute-start.4) | collective-permute-done | bytes 327712 | tf_op jit(solution)/shard_map/ppermute | solution.py:34
  28.9 1.6 %collective-permute-start.6 = (bf16[1280,128]{1,0:T(8,128)(2,1)S(1)}, bf16[1280,128]{1,0:T(8,128)(2,1)S(1)}, u32[]{:S(2)}, u32[]{:S(2)}) collective-permute-start(bf16[1280,128]{1,0:T(8,128)(2,1)S(1)} %collective-permute-done.4.refs_0_), channel_id=1, source_target_pairs={{0,4},{1,5},{2,6},{3,7},{4,8},{5,9},{6,10},{7,11},{8,12},{9,13},{1... | collective-permute-start | bytes 983048 | tf_op jit(solution)/shard_map/ppermute | solution.py:34
  30.5 1.5 %collective-permute-start.7 = (bf16[1280,128]{1,0:T(8,128)(2,1)S(1)}, bf16[1280,128]{1,0:T(8,128)(2,1)S(1)}, u32[]{:S(2)}, u32[]{:S(2)}) collective-permute-start(bf16[1280,128]{1,0:T(8,128)(2,1)S(1)} %collective-permute-done.4.refs_0_), channel_id=1, source_target_pairs={{0,2},{1,3},{2,0},{3,1},{4,6},{5,7},{6,4},{7,5},{8,10},{9,11},{10,... | collective-permute-start | bytes 983048 | tf_op jit(solution)/shard_map/ppermute | solution.py:34
  32.0 3.4 %shard_map.46 = (f32[41024,128]{1,0:T(8,128)S(1)}, bf16[512,32,128]{2,1,0:T(8,128)(2,1)S(1)}) custom-call(s32[1584]{0:T(1024)S(1)} %concatenate.10.table_ref, s32[6]{0:T(128)S(1)} %convert_reduce_fusion.1.bounds_ref, bf16[1280,128]{1,0:T(8,128)(2,1)} %copy-done.2, bf16[1280,128]{1,0:T(8,128)(2,1)} %copy-done.3, bf16[256,32,128]{2,1,0:T(8,128)(2,1)S(1)} %bitcast.53, ...), custom_call_target="tpu_custom_call" | custom-call | flops 107374184 | bytes 4194304 | tf_op jit(solution)/shard_map/pallas_call | solution.py:218
  35.3 1.3 %collective-permute-done.12.refs_1_ = bf16[1280,128]{1,0:T(8,128)(2,1)} collective-permute-done((bf16[1280,128]{1,0:T(8,128)(2,1)S(1)}, bf16[1280,128]{1,0:T(8,128)(2,1)}, u32[]{:S(2)}, u32[]{:S(2)}) %collective-permute-start.12) | collective-permute-done | bytes 327712 | tf_op jit(solution)/shard_map/ppermute | solution.py:34
  36.6 0.9 collective-permute-start.15
  37.5 1.5 %collective-permute-start.16 = (bf16[1280,128]{1,0:T(8,128)(2,1)}, bf16[1280,128]{1,0:T(8,128)(2,1)S(1)}, u32[]{:S(2)}, u32[]{:S(2)}) collective-permute-start(bf16[1280,128]{1,0:T(8,128)(2,1)} %collective-permute-done.12.refs_1_), channel_id=1, source_target_pairs={{0,2},{1,3},{2,0},{3,1},{4,6},{5,7},{6,4},{7,5},{8,10},{9,11},{10,... | collective-permute-start | bytes 983048 | tf_op jit(solution)/shard_map/ppermute | solution.py:34
  39.0 4.5 %collective-permute-done.6.refs_0_ = bf16[1280,128]{1,0:T(8,128)(2,1)S(1)} collective-permute-done((bf16[1280,128]{1,0:T(8,128)(2,1)S(1)}, bf16[1280,128]{1,0:T(8,128)(2,1)S(1)}, u32[]{:S(2)}, u32[]{:S(2)}) %collective-permute-start.6) | collective-permute-done | bytes 327712 | tf_op jit(solution)/shard_map/ppermute | solution.py:34
  43.6 2.2 %shard_map.47.refs_5_ = f32[41024,128]{1,0:T(8,128)S(1)} custom-call(s32[1584]{0:T(1024)S(1)} %concatenate.10.table_ref, s32[6]{0:T(128)S(1)} %convert_reduce_fusion.1.bounds_ref, bf16[1280,128]{1,0:T(8,128)(2,1)S(1)} %collective-permute-done.2.refs_0_, bf16[1280,128]{1,0:T(8,128)(2,1)S(1)} %collective-permute-done.10.refs_1_, ...), custom_call_target="tpu_custom_call", output_to_operand_aliasing={{}: (7, {})} | custom-call | flops 107374184 | bytes 4194304 | tf_op jit(solution)/shard_map/pallas_call | solution.py:218
  45.8 2.3 %collective-permute-start.14 = (bf16[1280,128]{1,0:T(8,128)(2,1)S(1)}, bf16[1280,128]{1,0:T(8,128)(2,1)S(1)}, u32[]{:S(2)}, u32[]{:S(2)}) collective-permute-start(bf16[1280,128]{1,0:T(8,128)(2,1)S(1)} %collective-permute-done.7.refs_2_), channel_id=1, source_target_pairs={{0,4},{1,5},{2,6},{3,7},{4,8},{5,9},{6,10},{7,11},{8,12},{9,13},{1... | collective-permute-start | bytes 983048 | tf_op jit(solution)/shard_map/ppermute | solution.py:34
  48.1 2.4 %collective-permute-done.15.refs_1_ = bf16[1280,128]{1,0:T(8,128)(2,1)S(1)} collective-permute-done((bf16[1280,128]{1,0:T(8,128)(2,1)}, bf16[1280,128]{1,0:T(8,128)(2,1)S(1)}, u32[]{:S(2)}, u32[]{:S(2)}) %collective-permute-start.15) | collective-permute-done | bytes 327712 | tf_op jit(solution)/shard_map/ppermute | solution.py:34
  50.6 1.0 collective-permute-start.17
  51.5 3.4 %shard_map.48.refs_5_ = f32[41024,128]{1,0:T(8,128)S(1)} custom-call(s32[1584]{0:T(1024)S(1)} %concatenate.10.table_ref, s32[6]{0:T(128)S(1)} %convert_reduce_fusion.1.bounds_ref, bf16[1280,128]{1,0:T(8,128)(2,1)S(1)} %collective-permute-done.4.refs_0_, bf16[1280,128]{1,0:T(8,128)(2,1)} %collective-permute-done.12.refs_1_, ...), custom_call_target="tpu_custom_call", output_to_operand_aliasing={{}: (7, {})} | custom-call | flops 107374184 | bytes 4194304 | tf_op jit(solution)/shard_map/pallas_call | solution.py:218
  54.9 2.2 %shard_map.49.refs_3_ = f32[41024,128]{1,0:T(8,128)S(1)} custom-call(s32[1584]{0:T(1024)S(1)} %concatenate.10.table_ref, s32[6]{0:T(128)S(1)} %convert_reduce_fusion.1.bounds_ref, bf16[1280,128]{1,0:T(8,128)(2,1)S(1)} %collective-permute-done.6.refs_0_, bf16[1280,128]{1,0:T(8,128)(2,1)S(1)} %collective-permute-done.15.refs_1_, ...), custom_call_target="tpu_custom_call", output_to_operand_aliasing={{}: (7, {})} | custom-call | flops 107374184 | bytes 4194304 | tf_op jit(solution)/shard_map/pallas_call | solution.py:218
  57.2 1.7 %collective-permute-done.17.refs_1_ = bf16[1280,128]{1,0:T(8,128)(2,1)S(1)} collective-permute-done((bf16[1280,128]{1,0:T(8,128)(2,1)S(1)}, bf16[1280,128]{1,0:T(8,128)(2,1)S(1)}, u32[]{:S(2)}, u32[]{:S(2)}) %collective-permute-start.17) | collective-permute-done | bytes 327712 | tf_op jit(solution)/shard_map/ppermute | solution.py:34
  58.9 2.3 %shard_map.50 = (f32[41024,128]{1,0:T(8,128)S(1)}, bf16[256,128]{1,0:T(8,128)(2,1)S(1)}, bf16[1,1280,128]{2,1,0:T(8,128)(2,1)S(1)}, bf16[1,1280,128]{2,1,0:T(8,128)(2,1)S(1)}, bf16[1,1280,128]{2,1,0:T(8,128)(2,1)S(1)}) custom-call(s32[1584]{0:T(1024)S(1)} %concatenate.10.table_ref, ...), custom_call_target="tpu_custom_call", output_to_operand_aliasing={{0}: (7, {})} | custom-call | flops 359032416 | bytes 4194304 | tf_op jit(solution)/shard_map/pallas_call | solution.py:218
  61.2 0.5 collective-permute-start.19
  61.8 1.2 %shard_map.51 = (f32[1,1280,128]{2,1,0:T(8,128)S(1)}, f32[1,1280,128]{2,1,0:T(8,128)S(1)}, f32[1,1280,128]{2,1,0:T(8,128)S(1)}) custom-call(s32[8]{0:T(128)S(1)} %fusion.30.chips_ref, s32[1]{0:T(128)} %bitcast.core_ref, f32[41024,128]{1,0:T(8,128)S(1)} %get-tuple-element.89.half, bf16[256,128]{1,0:T(8,128)(2,1)S(1)} %get-tuple-element.84.weights), custom_call_target="tpu_custom_call" | custom-call | flops 251658240 | bytes 4194304 | tf_op jit(solution)/shard_map/pallas_call | solution.py:218
  63.2 0.2 collective-permute-done.19
  63.3 0.5 collective-permute-done.22
  63.9 1.6 %shard_map.53 = (bf16[1,1280,128]{2,1,0:T(8,128)(2,1)S(1)}, bf16[1,1280,128]{2,1,0:T(8,128)(2,1)S(1)}, bf16[1,1280,128]{2,1,0:T(8,128)(2,1)S(1)}, bf16[1,1280,12...) custom-call(s32[8]{0:T(128)S(1)} %fusion.30.chips_ref, s32[1]{0:T(128)} %bitcast.core_ref, ...), custom_call_target="tpu_custom_call" | custom-call | flops 419430400 | bytes 4194304 | tf_op jit(solution)/shard_map/pallas_call | solution.py:218
  65.5 0.2 collective-permute-start.23
  65.7 0.4 collective-permute-start.21
  66.0 2.0 %collective-permute-start.24 = (bf16[640,128]{1,0:T(8,128)(2,1)S(1)}, bf16[640,128]{1,0:T(8,128)(2,1)S(1)}, u32[]{:S(2)}, u32[]{:S(2)}) collective-permute-start(bf16[640,128]{1,0:T(8,128)(2,1)S(1)} %get-tuple-element.98), channel_id=1, source_target_pairs={{0,2},{1,3},{2,0},{3,1},{4,6},{5,7},{6,4},{7,5},{8,10},{9,11},{10,... | collective-permute-start | bytes 491528 | tf_op jit(solution)/shard_map/ppermute | solution.py:34
  68.1 0.6 collective-permute-start.28
  68.7 0.8 collective-permute-start.27
  69.5 1.5 %shard_map.52 = (f32[1,1280,128]{2,1,0:T(8,128)S(1)}, f32[1,1280,128]{2,1,0:T(8,128)S(1)}, f32[1,1280,128]{2,1,0:T(8,128)S(1)}, f32[1,1280,128]{2,1,0:T(8,128)S(1)}, f32[1,1280,128]{2,1,0:T(8,128)S(1)}) custom-call(s32[8]{0:T(128)S(1)} %fusion.30.chips_ref, s32[1]{0:T(128)} %bitcast.core_ref, f32[41024,128]{1,0:T(8,128)S(1)} %get-tuple-element.89.half, ...), custom_call_target="tpu_custom_call" | custom-call | flops 419430400 | bytes 4194304 | tf_op jit(solution)/shard_map/pallas_call | solution.py:218
  71.2 1.8 %collective-permute-done.24 = bf16[640,128]{1,0:T(8,128)(2,1)S(1)} collective-permute-done((bf16[640,128]{1,0:T(8,128)(2,1)S(1)}, bf16[640,128]{1,0:T(8,128)(2,1)S(1)}, u32[]{:S(2)}, u32[]{:S(2)}) %collective-permute-start.24) | collective-permute-done | bytes 163872 | tf_op jit(solution)/shard_map/ppermute | solution.py:34
  73.1 3.0 %collective-permute-done.27 = bf16[640,128]{1,0:T(8,128)(2,1)S(1)} collective-permute-done((bf16[640,128]{1,0:T(8,128)(2,1)S(1)}, bf16[640,128]{1,0:T(8,128)(2,1)S(1)}, u32[]{:S(2)}, u32[]{:S(2)}) %collective-permute-start.27) | collective-permute-done | bytes 163872 | tf_op jit(solution)/shard_map/ppermute | solution.py:34
  76.1 3.3 %collective-permute-done.28 = bf16[1280,128]{1,0:T(8,128)(2,1)S(1)} collective-permute-done((bf16[1280,128]{1,0:T(8,128)(2,1)S(1)}, bf16[1280,128]{1,0:T(8,128)(2,1)S(1)}, u32[]{:S(2)}, u32[]{:S(2)}) %collective-permute-start.28) | collective-permute-done | bytes 327712 | tf_op jit(solution)/shard_map/ppermute | solution.py:34
  79.5 0.6 collective-permute-start.29
  80.1 0.1 fusion.5
  80.3 0.4 collective-permute-start.32
  80.7 7.4 %collective-permute-done.25 = bf16[640,128]{1,0:T(8,128)(2,1)S(1)} collective-permute-done((bf16[640,128]{1,0:T(8,128)(2,1)S(1)}, bf16[640,128]{1,0:T(8,128)(2,1)S(1)}, u32[]{:S(2)}, u32[]{:S(2)}) %collective-permute-start.25) | collective-permute-done | bytes 163872 | tf_op jit(solution)/shard_map/ppermute | solution.py:34
  88.2 2.5 %collective-permute-done.29 = bf16[640,128]{1,0:T(8,128)(2,1)S(1)} collective-permute-done((bf16[640,128]{1,0:T(8,128)(2,1)S(1)}, bf16[640,128]{1,0:T(8,128)(2,1)S(1)}, u32[]{:S(2)}, u32[]{:S(2)}) %collective-permute-start.29) | collective-permute-done | bytes 163872 | tf_op jit(solution)/shard_map/ppermute | solution.py:34
  90.9 0.1 fusion.3
  91.0 3.8 %collective-permute-start.35 = (bf16[1280,128]{1,0:T(8,128)(2,1)S(1)}, bf16[1280,128]{1,0:T(8,128)(2,1)S(1)}, u32[]{:S(2)}, u32[]{:S(2)}) collective-permute-start(bf16[1280,128]{1,0:T(8,128)(2,1)S(1)} %fusion.3), channel_id=1, source_target_pairs={{0,12},{1,13},{2,14},{3,15},{4,0},{5,1},{6,2},{7,3},{8,4},{9,5},{1... | collective-permute-start | bytes 983048 | tf_op jit(solution)/shard_map/ppermute | solution.py:34
  94.8 0.3 collective-permute-start.33
  95.1 2.0 %collective-permute-done.26 = bf16[640,128]{1,0:T(8,128)(2,1)S(1)} collective-permute-done((bf16[640,128]{1,0:T(8,128)(2,1)S(1)}, bf16[640,128]{1,0:T(8,128)(2,1)S(1)}, u32[]{:S(2)}, u32[]{:S(2)}) %collective-permute-start.26) | collective-permute-done | bytes 163872 | tf_op jit(solution)/shard_map/ppermute | solution.py:34
  97.1 3.5 %collective-permute-done.30 = bf16[640,128]{1,0:T(8,128)(2,1)S(1)} collective-permute-done((bf16[640,128]{1,0:T(8,128)(2,1)S(1)}, bf16[640,128]{1,0:T(8,128)(2,1)S(1)}, u32[]{:S(2)}, u32[]{:S(2)}) %collective-permute-start.30) | collective-permute-done | bytes 163872 | tf_op jit(solution)/shard_map/ppermute | solution.py:34
  100.7 3.2 %collective-permute-done.35 = bf16[1280,128]{1,0:T(8,128)(2,1)S(1)} collective-permute-done((bf16[1280,128]{1,0:T(8,128)(2,1)S(1)}, bf16[1280,128]{1,0:T(8,128)(2,1)S(1)}, u32[]{:S(2)}, u32[]{:S(2)}) %collective-permute-start.35) | collective-permute-done | bytes 327712 | tf_op jit(solution)/shard_map/ppermute | solution.py:34
  103.9 0.9 add_multiply_fusion
  (50 shorter events, 1.3 us)
Async XLA Ops:
  0.0 9.3 %collective-permute-start.9 = (bf16[256,4096]{1,0:T(8,128)(2,1)}, bf16[256,4096]{1,0:T(8,128)(2,1)}, u32[]{:S(2)}, u32[]{:S(2)}) collective-permute-start(bf16[256,4096]{1,0:T(8,128)(2,1)} %param.4), channel_id=1, source_target_pairs={{0,1},{1,0},{2,3},{3,2},{4,5},{5,4},{6,7},{7,6},{8,9},{9,8},{10,11... | collective-permute-start | bytes 6291464 | tf_op jit(solution)/shard_map/ppermute | solution.py:34
  1.6 13.2 %copy-start.2 = (bf16[1280,128]{1,0:T(8,128)(2,1)}, bf16[1280,128]{1,0:T(8,128)(2,1)S(1)}, u32[]{:S(2)}) copy-start(bf16[1280,128]{1,0:T(8,128)(2,1)S(1)} %get-tuple-element.123.refs_0_) | copy-start | bytes 983044
  1.6 13.2 %collective-permute-start.2 = (bf16[1280,128]{1,0:T(8,128)(2,1)S(1)}, bf16[1280,128]{1,0:T(8,128)(2,1)S(1)}, u32[]{:S(2)}, u32[]{:S(2)}) collective-permute-start(bf16[1280,128]{1,0:T(8,128)(2,1)S(1)} %get-tuple-element.123.refs_0_), channel_id=1, source_target_pairs={{0,4},{1,5},{2,6},{3,7},{4,8},{5,9},{6,10},{7,11},{8,12},{9,13},{1... | collective-permute-start | bytes 983048 | tf_op jit(solution)/shard_map/ppermute | solution.py:34
  4.2 10.6 %collective-permute-start.3 = (bf16[1280,128]{1,0:T(8,128)(2,1)S(1)}, bf16[1280,128]{1,0:T(8,128)(2,1)S(1)}, u32[]{:S(2)}, u32[]{:S(2)}) collective-permute-start(bf16[1280,128]{1,0:T(8,128)(2,1)S(1)} %get-tuple-element.123.refs_0_), channel_id=1, source_target_pairs={{0,2},{1,3},{2,0},{3,1},{4,6},{5,7},{6,4},{7,5},{8,10},{9,11},{10,... | collective-permute-start | bytes 983048 | tf_op jit(solution)/shard_map/ppermute | solution.py:34
  5.7 1.9 %collective-permute-start.1 = (s32[256,2]{0,1:T(2,128)}, s32[256,2]{0,1:T(2,128)S(1)}, u32[]{:S(2)}, u32[]{:S(2)}) collective-permute-start(s32[256,2]{0,1:T(2,128)} %param.5), channel_id=1, source_target_pairs={{0,1},{1,0},{2,3},{3,2},{4,5},{5,4},{6,7},{7,6},{8,9},{9,8},{10,11... | collective-permute-start | bytes 6152 | tf_op jit(solution)/shard_map/ppermute | solution.py:34
  5.7 2.0 %collective-permute-start = (s32[1]{0:T(128)}, s32[1]{0:T(128)}, u32[]{:S(2)}, u32[]{:S(2)}) collective-permute-start(s32[1]{0:T(128)} %param.6), channel_id=1, source_target_pairs={{0,1},{1,0},{2,3},{3,2},{4,5},{5,4},{6,7},{7,6},{8,9},{9,8},{10,11... | collective-permute-start | bytes 20 | tf_op jit(solution)/shard_map/ppermute | solution.py:34
  7.6 1.7 %collective-permute-start.8 = (bf16[1280,128]{1,0:T(8,128)(2,1)S(1)}, bf16[1280,128]{1,0:T(8,128)(2,1)S(1)}, u32[]{:S(2)}, u32[]{:S(2)}) collective-permute-start(bf16[1280,128]{1,0:T(8,128)(2,1)S(1)} %get-tuple-element.122), channel_id=1, source_target_pairs={{0,1},{1,0},{2,3},{3,2},{4,5},{5,4},{6,7},{7,6},{8,9},{9,8},{10,11... | collective-permute-start | bytes 983048 | tf_op jit(solution)/shard_map/ppermute | solution.py:34
  9.3 10.6 %copy-start.3 = (bf16[1280,128]{1,0:T(8,128)(2,1)}, bf16[1280,128]{1,0:T(8,128)(2,1)S(1)}, u32[]{:S(2)}) copy-start(bf16[1280,128]{1,0:T(8,128)(2,1)S(1)} %collective-permute-done.8.refs_1_) | copy-start | bytes 983044
  9.3 14.1 %collective-permute-start.10 = (bf16[1280,128]{1,0:T(8,128)(2,1)S(1)}, bf16[1280,128]{1,0:T(8,128)(2,1)S(1)}, u32[]{:S(2)}, u32[]{:S(2)}) collective-permute-start(bf16[1280,128]{1,0:T(8,128)(2,1)S(1)} %collective-permute-done.8.refs_1_), channel_id=1, source_target_pairs={{0,4},{1,5},{2,6},{3,7},{4,8},{5,9},{6,10},{7,11},{8,12},{9,13},{1... | collective-permute-start | bytes 983048 | tf_op jit(solution)/shard_map/ppermute | solution.py:34
  10.9 12.5 %collective-permute-start.11 = (bf16[1280,128]{1,0:T(8,128)(2,1)S(1)}, bf16[1280,128]{1,0:T(8,128)(2,1)S(1)}, u32[]{:S(2)}, u32[]{:S(2)}) collective-permute-start(bf16[1280,128]{1,0:T(8,128)(2,1)S(1)} %collective-permute-done.8.refs_1_), channel_id=1, source_target_pairs={{0,2},{1,3},{2,0},{3,1},{4,6},{5,7},{6,4},{7,5},{8,10},{9,11},{10,... | collective-permute-start | bytes 983048 | tf_op jit(solution)/shard_map/ppermute | solution.py:34
  14.8 14.0 %collective-permute-start.4 = (bf16[1280,128]{1,0:T(8,128)(2,1)S(1)}, bf16[1280,128]{1,0:T(8,128)(2,1)S(1)}, u32[]{:S(2)}, u32[]{:S(2)}) collective-permute-start(bf16[1280,128]{1,0:T(8,128)(2,1)S(1)} %collective-permute-done.2.refs_0_), channel_id=1, source_target_pairs={{0,4},{1,5},{2,6},{3,7},{4,8},{5,9},{6,10},{7,11},{8,12},{9,13},{1... | collective-permute-start | bytes 983048 | tf_op jit(solution)/shard_map/ppermute | solution.py:34
  16.3 12.6 %collective-permute-start.5 = (bf16[1280,128]{1,0:T(8,128)(2,1)S(1)}, bf16[1280,128]{1,0:T(8,128)(2,1)}, u32[]{:S(2)}, u32[]{:S(2)}) collective-permute-start(bf16[1280,128]{1,0:T(8,128)(2,1)S(1)} %collective-permute-done.2.refs_0_), channel_id=1, source_target_pairs={{0,2},{1,3},{2,0},{3,1},{4,6},{5,7},{6,4},{7,5},{8,10},{9,11},{10,... | collective-permute-start | bytes 983048 | tf_op jit(solution)/shard_map/ppermute | solution.py:34
  23.3 0.7 copy-start
  24.1 12.6 %collective-permute-start.12 = (bf16[1280,128]{1,0:T(8,128)(2,1)S(1)}, bf16[1280,128]{1,0:T(8,128)(2,1)}, u32[]{:S(2)}, u32[]{:S(2)}) collective-permute-start(bf16[1280,128]{1,0:T(8,128)(2,1)S(1)} %collective-permute-done.10.refs_1_), channel_id=1, source_target_pairs={{0,4},{1,5},{2,6},{3,7},{4,8},{5,9},{6,10},{7,11},{8,12},{9,13},{1... | collective-permute-start | bytes 983048 | tf_op jit(solution)/shard_map/ppermute | solution.py:34
  25.7 11.0 %collective-permute-start.13 = (bf16[1280,128]{1,0:T(8,128)(2,1)S(1)}, bf16[1280,128]{1,0:T(8,128)(2,1)}, u32[]{:S(2)}, u32[]{:S(2)}) collective-permute-start(bf16[1280,128]{1,0:T(8,128)(2,1)S(1)} %collective-permute-done.10.refs_1_), channel_id=1, source_target_pairs={{0,2},{1,3},{2,0},{3,1},{4,6},{5,7},{6,4},{7,5},{8,10},{9,11},{10,... | collective-permute-start | bytes 983048 | tf_op jit(solution)/shard_map/ppermute | solution.py:34
  27.2 16.3 %copy-start.1 = (bf16[1280,128]{1,0:T(8,128)(2,1)S(1)}, bf16[1280,128]{1,0:T(8,128)(2,1)}, u32[]{:S(2)}) copy-start(bf16[1280,128]{1,0:T(8,128)(2,1)} %copy-done) | copy-start | bytes 983044
  28.9 14.6 %collective-permute-start.6 = (bf16[1280,128]{1,0:T(8,128)(2,1)S(1)}, bf16[1280,128]{1,0:T(8,128)(2,1)S(1)}, u32[]{:S(2)}, u32[]{:S(2)}) collective-permute-start(bf16[1280,128]{1,0:T(8,128)(2,1)S(1)} %collective-permute-done.4.refs_0_), channel_id=1, source_target_pairs={{0,4},{1,5},{2,6},{3,7},{4,8},{5,9},{6,10},{7,11},{8,12},{9,13},{1... | collective-permute-start | bytes 983048 | tf_op jit(solution)/shard_map/ppermute | solution.py:34
  30.5 13.1 %collective-permute-start.7 = (bf16[1280,128]{1,0:T(8,128)(2,1)S(1)}, bf16[1280,128]{1,0:T(8,128)(2,1)S(1)}, u32[]{:S(2)}, u32[]{:S(2)}) collective-permute-start(bf16[1280,128]{1,0:T(8,128)(2,1)S(1)} %collective-permute-done.4.refs_0_), channel_id=1, source_target_pairs={{0,2},{1,3},{2,0},{3,1},{4,6},{5,7},{6,4},{7,5},{8,10},{9,11},{10,... | collective-permute-start | bytes 983048 | tf_op jit(solution)/shard_map/ppermute | solution.py:34
  36.6 13.9 %collective-permute-start.15 = (bf16[1280,128]{1,0:T(8,128)(2,1)}, bf16[1280,128]{1,0:T(8,128)(2,1)S(1)}, u32[]{:S(2)}, u32[]{:S(2)}) collective-permute-start(bf16[1280,128]{1,0:T(8,128)(2,1)} %collective-permute-done.12.refs_1_), channel_id=1, source_target_pairs={{0,4},{1,5},{2,6},{3,7},{4,8},{5,9},{6,10},{7,11},{8,12},{9,13},{1... | collective-permute-start | bytes 983048 | tf_op jit(solution)/shard_map/ppermute | solution.py:34
  37.5 13.1 %collective-permute-start.16 = (bf16[1280,128]{1,0:T(8,128)(2,1)}, bf16[1280,128]{1,0:T(8,128)(2,1)S(1)}, u32[]{:S(2)}, u32[]{:S(2)}) collective-permute-start(bf16[1280,128]{1,0:T(8,128)(2,1)} %collective-permute-done.12.refs_1_), channel_id=1, source_target_pairs={{0,2},{1,3},{2,0},{3,1},{4,6},{5,7},{6,4},{7,5},{8,10},{9,11},{10,... | collective-permute-start | bytes 983048 | tf_op jit(solution)/shard_map/ppermute | solution.py:34
  45.8 11.4 %collective-permute-start.14 = (bf16[1280,128]{1,0:T(8,128)(2,1)S(1)}, bf16[1280,128]{1,0:T(8,128)(2,1)S(1)}, u32[]{:S(2)}, u32[]{:S(2)}) collective-permute-start(bf16[1280,128]{1,0:T(8,128)(2,1)S(1)} %collective-permute-done.7.refs_2_), channel_id=1, source_target_pairs={{0,4},{1,5},{2,6},{3,7},{4,8},{5,9},{6,10},{7,11},{8,12},{9,13},{1... | collective-permute-start | bytes 983048 | tf_op jit(solution)/shard_map/ppermute | solution.py:34
  50.6 8.3 %collective-permute-start.17 = (bf16[1280,128]{1,0:T(8,128)(2,1)S(1)}, bf16[1280,128]{1,0:T(8,128)(2,1)S(1)}, u32[]{:S(2)}, u32[]{:S(2)}) collective-permute-start(bf16[1280,128]{1,0:T(8,128)(2,1)S(1)} %collective-permute-done.15.refs_1_), channel_id=1, source_target_pairs={{0,2},{1,3},{2,0},{3,1},{4,6},{5,7},{6,4},{7,5},{8,10},{9,11},{10,... | collective-permute-start | bytes 983048 | tf_op jit(solution)/shard_map/ppermute | solution.py:34
  61.2 1.9 %collective-permute-start.18 = (bf16[1280,128]{1,0:T(8,128)(2,1)S(1)}, bf16[1280,128]{1,0:T(8,128)(2,1)S(1)}, u32[]{:S(2)}, u32[]{:S(2)}) collective-permute-start(bf16[1280,128]{1,0:T(8,128)(2,1)S(1)} %bitcast.61), channel_id=1, source_target_pairs={{0,1},{1,0},{2,3},{3,2},{4,5},{5,4},{6,7},{7,6},{8,9},{9,8},{10,11... | collective-permute-start | bytes 983048 | tf_op jit(solution)/shard_map/ppermute | solution.py:34
  61.2 2.1 %collective-permute-start.19 = (bf16[1280,128]{1,0:T(8,128)(2,1)S(1)}, bf16[1280,128]{1,0:T(8,128)(2,1)S(1)}, u32[]{:S(2)}, u32[]{:S(2)}) collective-permute-start(bf16[1280,128]{1,0:T(8,128)(2,1)S(1)} %bitcast.59), channel_id=1, source_target_pairs={{0,1},{1,0},{2,3},{3,2},{4,5},{5,4},{6,7},{7,6},{8,9},{9,8},{10,11... | collective-permute-start | bytes 983048 | tf_op jit(solution)/shard_map/ppermute | solution.py:34
  61.7 2.1 %collective-permute-start.22 = (bf16[1280,128]{1,0:T(8,128)(2,1)S(1)}, bf16[1280,128]{1,0:T(8,128)(2,1)S(1)}, u32[]{:S(2)}, u32[]{:S(2)}) collective-permute-start(bf16[1280,128]{1,0:T(8,128)(2,1)S(1)} %bitcast.58), channel_id=1, source_target_pairs={{0,1},{1,0},{2,3},{3,2},{4,5},{5,4},{6,7},{7,6},{8,9},{9,8},{10,11... | collective-permute-start | bytes 983048 | tf_op jit(solution)/shard_map/ppermute | solution.py:34
  65.5 5.6 %collective-permute-start.23 = (bf16[1280,128]{1,0:T(8,128)(2,1)S(1)}, bf16[1280,128]{1,0:T(8,128)(2,1)S(1)}, u32[]{:S(2)}, u32[]{:S(2)}) collective-permute-start(bf16[1280,128]{1,0:T(8,128)(2,1)S(1)} %bitcast.60), channel_id=1, source_target_pairs={{0,1},{1,0},{2,3},{3,2},{4,5},{5,4},{6,7},{7,6},{8,9},{9,8},{10,11... | collective-permute-start | bytes 983048 | tf_op jit(solution)/shard_map/ppermute | solution.py:34
  65.7 14.6 %collective-permute-start.21 = (bf16[1280,128]{1,0:T(8,128)(2,1)S(1)}, bf16[1280,128]{1,0:T(8,128)(2,1)S(1)}, u32[]{:S(2)}, u32[]{:S(2)}) collective-permute-start(bf16[1280,128]{1,0:T(8,128)(2,1)S(1)} %bitcast.56), channel_id=1, source_target_pairs={{0,1},{1,0},{2,3},{3,2},{4,5},{5,4},{6,7},{7,6},{8,9},{9,8},{10,11... | collective-permute-start | bytes 983048 | tf_op jit(solution)/shard_map/ppermute | solution.py:34
  66.0 7.0 %collective-permute-start.24 = (bf16[640,128]{1,0:T(8,128)(2,1)S(1)}, bf16[640,128]{1,0:T(8,128)(2,1)S(1)}, u32[]{:S(2)}, u32[]{:S(2)}) collective-permute-start(bf16[640,128]{1,0:T(8,128)(2,1)S(1)} %get-tuple-element.98), channel_id=1, source_target_pairs={{0,2},{1,3},{2,0},{3,1},{4,6},{5,7},{6,4},{7,5},{8,10},{9,11},{10,... | collective-permute-start | bytes 491528 | tf_op jit(solution)/shard_map/ppermute | solution.py:34
  68.1 11.3 %collective-permute-start.28 = (bf16[1280,128]{1,0:T(8,128)(2,1)S(1)}, bf16[1280,128]{1,0:T(8,128)(2,1)S(1)}, u32[]{:S(2)}, u32[]{:S(2)}) collective-permute-start(bf16[1280,128]{1,0:T(8,128)(2,1)S(1)} %get-tuple-element.103), channel_id=1, source_target_pairs={{0,4},{1,5},{2,6},{3,7},{4,8},{5,9},{6,10},{7,11},{8,12},{9,13},{1... | collective-permute-start | bytes 983048 | tf_op jit(solution)/shard_map/ppermute | solution.py:34
  68.7 7.4 %collective-permute-start.27 = (bf16[640,128]{1,0:T(8,128)(2,1)S(1)}, bf16[640,128]{1,0:T(8,128)(2,1)S(1)}, u32[]{:S(2)}, u32[]{:S(2)}) collective-permute-start(bf16[640,128]{1,0:T(8,128)(2,1)S(1)} %get-tuple-element.102), channel_id=1, source_target_pairs={{0,2},{1,3},{2,0},{3,1},{4,6},{5,7},{6,4},{7,5},{8,10},{9,11},{10,... | collective-permute-start | bytes 491528 | tf_op jit(solution)/shard_map/ppermute | solution.py:34
  71.1 8.4 %collective-permute-start.31 = (bf16[1280,128]{1,0:T(8,128)(2,1)S(1)}, bf16[1280,128]{1,0:T(8,128)(2,1)S(1)}, u32[]{:S(2)}, u32[]{:S(2)}) collective-permute-start(bf16[1280,128]{1,0:T(8,128)(2,1)S(1)} %bitcast.57), channel_id=1, source_target_pairs={{0,1},{1,0},{2,3},{3,2},{4,5},{5,4},{6,7},{7,6},{8,9},{9,8},{10,11... | collective-permute-start | bytes 983048 | tf_op jit(solution)/shard_map/ppermute | solution.py:34
  73.0 22.1 %collective-permute-start.20 = (bf16[1280,128]{1,0:T(8,128)(2,1)S(1)}, bf16[1280,128]{1,0:T(8,128)(2,1)S(1)}, u32[]{:S(2)}, u32[]{:S(2)}) collective-permute-start(bf16[1280,128]{1,0:T(8,128)(2,1)S(1)} %bitcast.54), channel_id=1, source_target_pairs={{0,1},{1,0},{2,3},{3,2},{4,5},{5,4},{6,7},{7,6},{8,9},{9,8},{10,11... | collective-permute-start | bytes 983048 | tf_op jit(solution)/shard_map/ppermute | solution.py:34
  76.1 14.8 %collective-permute-start.34 = (bf16[1280,128]{1,0:T(8,128)(2,1)S(1)}, bf16[1280,128]{1,0:T(8,128)(2,1)S(1)}, u32[]{:S(2)}, u32[]{:S(2)}) collective-permute-start(bf16[1280,128]{1,0:T(8,128)(2,1)S(1)} %bitcast.55), channel_id=1, source_target_pairs={{0,1},{1,0},{2,3},{3,2},{4,5},{5,4},{6,7},{7,6},{8,9},{9,8},{10,11... | collective-permute-start | bytes 983048 | tf_op jit(solution)/shard_map/ppermute | solution.py:34
  79.4 8.7 %collective-permute-start.25 = (bf16[640,128]{1,0:T(8,128)(2,1)S(1)}, bf16[640,128]{1,0:T(8,128)(2,1)S(1)}, u32[]{:S(2)}, u32[]{:S(2)}) collective-permute-start(bf16[640,128]{1,0:T(8,128)(2,1)S(1)} %get-tuple-element.120), channel_id=1, source_target_pairs={{0,4},{1,5},{2,6},{3,7},{4,8},{5,9},{6,10},{7,11},{8,12},{9,13},{1... | collective-permute-start | bytes 491528 | tf_op jit(solution)/shard_map/ppermute | solution.py:34
  79.5 11.3 %collective-permute-start.29 = (bf16[640,128]{1,0:T(8,128)(2,1)S(1)}, bf16[640,128]{1,0:T(8,128)(2,1)S(1)}, u32[]{:S(2)}, u32[]{:S(2)}) collective-permute-start(bf16[640,128]{1,0:T(8,128)(2,1)S(1)} %get-tuple-element.121), channel_id=1, source_target_pairs={{0,4},{1,5},{2,6},{3,7},{4,8},{5,9},{6,10},{7,11},{8,12},{9,13},{1... | collective-permute-start | bytes 491528 | tf_op jit(solution)/shard_map/ppermute | solution.py:34
  80.3 10.6 %collective-permute-start.32 = (bf16[1280,128]{1,0:T(8,128)(2,1)S(1)}, bf16[1280,128]{1,0:T(8,128)(2,1)S(1)}, u32[]{:S(2)}, u32[]{:S(2)}) collective-permute-start(bf16[1280,128]{1,0:T(8,128)(2,1)S(1)} %fusion.6), channel_id=1, source_target_pairs={{0,2},{1,3},{2,0},{3,1},{4,6},{5,7},{6,4},{7,5},{8,10},{9,11},{10,... | collective-permute-start | bytes 983048 | tf_op jit(solution)/shard_map/ppermute | solution.py:34
  88.1 8.9 %collective-permute-start.26 = (bf16[640,128]{1,0:T(8,128)(2,1)S(1)}, bf16[640,128]{1,0:T(8,128)(2,1)S(1)}, u32[]{:S(2)}, u32[]{:S(2)}) collective-permute-start(bf16[640,128]{1,0:T(8,128)(2,1)S(1)} %fusion.12), channel_id=1, source_target_pairs={{0,4},{1,5},{2,6},{3,7},{4,8},{5,9},{6,10},{7,11},{8,12},{9,13},{1... | collective-permute-start | bytes 491528 | tf_op jit(solution)/shard_map/ppermute | solution.py:34
  90.8 9.8 %collective-permute-start.30 = (bf16[640,128]{1,0:T(8,128)(2,1)S(1)}, bf16[640,128]{1,0:T(8,128)(2,1)S(1)}, u32[]{:S(2)}, u32[]{:S(2)}) collective-permute-start(bf16[640,128]{1,0:T(8,128)(2,1)S(1)} %add_convert_fusion), channel_id=1, source_target_pairs={{0,4},{1,5},{2,6},{3,7},{4,8},{5,9},{6,10},{7,11},{8,12},{9,13},{1... | collective-permute-start | bytes 491528 | tf_op jit(solution)/shard_map/ppermute | solution.py:34
  91.0 12.9 %collective-permute-start.35 = (bf16[1280,128]{1,0:T(8,128)(2,1)S(1)}, bf16[1280,128]{1,0:T(8,128)(2,1)S(1)}, u32[]{:S(2)}, u32[]{:S(2)}) collective-permute-start(bf16[1280,128]{1,0:T(8,128)(2,1)S(1)} %fusion.3), channel_id=1, source_target_pairs={{0,12},{1,13},{2,14},{3,15},{4,0},{5,1},{6,2},{7,3},{8,4},{9,5},{1... | collective-permute-start | bytes 983048 | tf_op jit(solution)/shard_map/ppermute | solution.py:34
  94.8 9.1 %collective-permute-start.33 = (bf16[1280,128]{1,0:T(8,128)(2,1)S(1)}, bf16[1280,128]{1,0:T(8,128)(2,1)S(1)}, u32[]{:S(2)}, u32[]{:S(2)}) collective-permute-start(bf16[1280,128]{1,0:T(8,128)(2,1)S(1)} %fusion.5), channel_id=1, source_target_pairs={{0,2},{1,3},{2,0},{3,1},{4,6},{5,7},{6,4},{7,5},{8,10},{9,11},{10,... | collective-permute-start | bytes 983048 | tf_op jit(solution)/shard_map/ppermute | solution.py:34

commit v19 on v18

--- a/solution.py
+++ b/solution.py
@@ -76,8 +76,8 @@
     def paired(send, keep):
         return keep + wide(move(send, swap))
 
-    first = [FAR2, FAR1, NEAR2]
-    rest = [FAR3, NEAR1, FAR0, NEAR3, NEAR0]
+    first = [FAR2, FAR1, FAR3, NEAR2]
+    rest = [NEAR1, FAR0, NEAR3, NEAR0]
     sends = blocks_of(first, False)
     total = {name: paired(*pair) for name, *pair in zip(first, sends, blocks_of(first, True))}
     crossing, aside = list(map(narrow, halves(total[FAR2]))), narrow(total[FAR1])

time: 105 us -> 105 us (level)
  transfers between devices with their start and end apart: 36 -> 36, of which waited for: 18 -> 16; matrix products, arithmetic and copies ran while one was open for 10% -> 10% of each run, Pallas kernels for 13% -> 15%
where the time goes in v19:
time: 105 us
  waiting for transfers between devices  42.2 us (40%)
  starting transfers between devices  31.3 us (30%)
  Pallas kernels  18.5 us (18%)
  local copies, waits for them, and re-layouts  8.14 us (8%)
  other arithmetic  4.15 us (4%)
    ppermute x36, waiting for transfers between devices, move(): return lax.ppermute(array, 'aux', pairs)  42.2 us
    ppermute x36, starting transfers between devices, move(): return lax.ppermute(array, 'aux', pairs)  31.3 us
    pallas_call x8, Pallas kernels, call(): pl.pallas_call(kernel, out_shape=outs, in_specs=in_specs, out_specs=[VMEM...  18.5 us
    unnamed x11, local copies, waits for them, and re-layouts  6.92 us
  transfers between devices with their start and end apart: 36, of which 16 were waited for; matrix products, arithmetic and copies ran while one was open for 10% of the time, Pallas kernels for 15%

profile of v19, /device:TPU:0, one launch (start us, length us, event | category | flops | bytes accessed | tf_op | source)
XLA Modules:
  0.0 105.3 jit_solution(3085556589862756984)
XLA Ops:
  0.0 0.5 collective-permute-start.9
  0.5 1.1 %constant_dynamic-slice_fusion.1 = (bf16[1280,128]{1,0:T(8,128)(2,1)S(1)}, bf16[1280,128]{1,0:T(8,128)(2,1)S(1)}) fusion(bf16[1280,256]{1,0:T(8,128)(2,1)} %param.7, s32[]{:T(128)S(6)} %select_n.162, s32[]{:T(128)S(6)} %select_n.161), kind=kLoop, calls=%fused_computation.91 | loop fusion | bytes 1310728 | tf_op jit(solution)/shard_map/dynamic_slice | solution.py:245
  1.6 2.6 %collective-permute-start.2 = (bf16[1280,128]{1,0:T(8,128)(2,1)S(1)}, bf16[1280,128]{1,0:T(8,128)(2,1)S(1)}, u32[]{:S(2)}, u32[]{:S(2)}) collective-permute-start(bf16[1280,128]{1,0:T(8,128)(2,1)S(1)} %get-tuple-element.123.refs_0_), channel_id=1, source_target_pairs={{0,4},{1,5},{2,6},{3,7},{4,8},{5,9},{6,10},{7,11},{8,12},{9,13},{1... | collective-permute-start | bytes 983048 | tf_op jit(solution)/shard_map/ppermute | solution.py:34
  4.2 1.5 %collective-permute-start.3 = (bf16[1280,128]{1,0:T(8,128)(2,1)S(1)}, bf16[1280,128]{1,0:T(8,128)(2,1)S(1)}, u32[]{:S(2)}, u32[]{:S(2)}) collective-permute-start(bf16[1280,128]{1,0:T(8,128)(2,1)S(1)} %get-tuple-element.123.refs_0_), channel_id=1, source_target_pairs={{0,2},{1,3},{2,0},{3,1},{4,6},{5,7},{6,4},{7,5},{8,10},{9,11},{10,... | collective-permute-start | bytes 983048 | tf_op jit(solution)/shard_map/ppermute | solution.py:34
  5.7 0.5 collective-permute-start
  6.2 0.7 constant_dynamic-update-slice_fusion.1
  7.7 0.7 compare_select_fusion.3
  8.4 0.8 collective-permute-done.8.refs_1_
  9.3 1.6 %collective-permute-start.10 = (bf16[1280,128]{1,0:T(8,128)(2,1)S(1)}, bf16[1280,128]{1,0:T(8,128)(2,1)S(1)}, u32[]{:S(2)}, u32[]{:S(2)}) collective-permute-start(bf16[1280,128]{1,0:T(8,128)(2,1)S(1)} %collective-permute-done.8.refs_1_), channel_id=1, source_target_pairs={{0,4},{1,5},{2,6},{3,7},{4,8},{5,9},{6,10},{7,11},{8,12},{9,13},{1... | collective-permute-start | bytes 983048 | tf_op jit(solution)/shard_map/ppermute | solution.py:34
  10.9 0.5 collective-permute-start.11
  11.4 0.7 fusion.27
  12.1 2.7 %collective-permute-done.2.refs_0_ = bf16[1280,128]{1,0:T(8,128)(2,1)S(1)} collective-permute-done((bf16[1280,128]{1,0:T(8,128)(2,1)S(1)}, bf16[1280,128]{1,0:T(8,128)(2,1)S(1)}, u32[]{:S(2)}, u32[]{:S(2)}) %collective-permute-start.2) | collective-permute-done | bytes 327712 | tf_op jit(solution)/shard_map/ppermute | solution.py:34
  14.8 1.5 %collective-permute-start.4 = (bf16[1280,128]{1,0:T(8,128)(2,1)S(1)}, bf16[1280,128]{1,0:T(8,128)(2,1)S(1)}, u32[]{:S(2)}, u32[]{:S(2)}) collective-permute-start(bf16[1280,128]{1,0:T(8,128)(2,1)S(1)} %collective-permute-done.2.refs_0_), channel_id=1, source_target_pairs={{0,4},{1,5},{2,6},{3,7},{4,8},{5,9},{6,10},{7,11},{8,12},{9,13},{1... | collective-permute-start | bytes 983048 | tf_op jit(solution)/shard_map/ppermute | solution.py:34
  16.3 1.5 %collective-permute-start.5 = (bf16[1280,128]{1,0:T(8,128)(2,1)S(1)}, bf16[1280,128]{1,0:T(8,128)(2,1)}, u32[]{:S(2)}, u32[]{:S(2)}) collective-permute-start(bf16[1280,128]{1,0:T(8,128)(2,1)S(1)} %collective-permute-done.2.refs_0_), channel_id=1, source_target_pairs={{0,2},{1,3},{2,0},{3,1},{4,6},{5,7},{6,4},{7,5},{8,10},{9,11},{10,... | collective-permute-start | bytes 983048 | tf_op jit(solution)/shard_map/ppermute | solution.py:34
  17.8 2.1 %copy.9 = bf16[32,8,32,128]{3,2,1,0:T(8,128)(2,1)S(1)} copy(bf16[32,8,32,128]{3,1,2,0:T(8,128)(2,1)} %bitcast.63) | data formatting | bytes 4194304
  19.9 3.4 %copy.10 = bf16[32,8,32,128]{3,2,1,0:T(8,128)(2,1)} copy(bf16[32,8,32,128]{3,1,2,0:T(8,128)(2,1)} %bitcast.25) | data formatting | bytes 4194304
  23.3 0.7 copy-done
  24.1 1.6 %collective-permute-start.12 = (bf16[1280,128]{1,0:T(8,128)(2,1)S(1)}, bf16[1280,128]{1,0:T(8,128)(2,1)}, u32[]{:S(2)}, u32[]{:S(2)}) collective-permute-start(bf16[1280,128]{1,0:T(8,128)(2,1)S(1)} %collective-permute-done.10.refs_1_), channel_id=1, source_target_pairs={{0,4},{1,5},{2,6},{3,7},{4,8},{5,9},{6,10},{7,11},{8,12},{9,13},{1... | collective-permute-start | bytes 983048 | tf_op jit(solution)/shard_map/ppermute | solution.py:34
  25.7 0.5 collective-permute-start.13
  26.2 0.3 convert_reduce_fusion
  26.5 0.5 select_reduce_fusion
  27.1 0.1 convert_reduce_fusion.1.bounds_ref
  27.2 1.6 %collective-permute-done.4.refs_0_ = bf16[1280,128]{1,0:T(8,128)(2,1)S(1)} collective-permute-done((bf16[1280,128]{1,0:T(8,128)(2,1)S(1)}, bf16[1280,128]{1,0:T(8,128)(2,1)S(1)}, u32[]{:S(2)}, u32[]{:S(2)}) %collective-permute-start.4) | collective-permute-done | bytes 327712 | tf_op jit(solution)/shard_map/ppermute | solution.py:34
  28.9 1.6 %collective-permute-start.6 = (bf16[1280,128]{1,0:T(8,128)(2,1)S(1)}, bf16[1280,128]{1,0:T(8,128)(2,1)S(1)}, u32[]{:S(2)}, u32[]{:S(2)}) collective-permute-start(bf16[1280,128]{1,0:T(8,128)(2,1)S(1)} %collective-permute-done.4.refs_0_), channel_id=1, source_target_pairs={{0,4},{1,5},{2,6},{3,7},{4,8},{5,9},{6,10},{7,11},{8,12},{9,13},{1... | collective-permute-start | bytes 983048 | tf_op jit(solution)/shard_map/ppermute | solution.py:34
  30.5 1.5 %collective-permute-start.7 = (bf16[1280,128]{1,0:T(8,128)(2,1)S(1)}, bf16[1280,128]{1,0:T(8,128)(2,1)S(1)}, u32[]{:S(2)}, u32[]{:S(2)}) collective-permute-start(bf16[1280,128]{1,0:T(8,128)(2,1)S(1)} %collective-permute-done.4.refs_0_), channel_id=1, source_target_pairs={{0,2},{1,3},{2,0},{3,1},{4,6},{5,7},{6,4},{7,5},{8,10},{9,11},{10,... | collective-permute-start | bytes 983048 | tf_op jit(solution)/shard_map/ppermute | solution.py:34
  32.0 3.1 %shard_map.46 = (f32[41024,128]{1,0:T(8,128)S(1)}, bf16[512,32,128]{2,1,0:T(8,128)(2,1)S(1)}) custom-call(s32[1584]{0:T(1024)S(1)} %concatenate.10.table_ref, s32[6]{0:T(128)S(1)} %convert_reduce_fusion.1.bounds_ref, bf16[1280,128]{1,0:T(8,128)(2,1)} %copy-done.2, bf16[1280,128]{1,0:T(8,128)(2,1)} %copy-done.3, bf16[256,32,128]{2,1,0:T(8,128)(2,1)S(1)} %bitcast.53, ...), custom_call_target="tpu_custom_call" | custom-call | flops 107374184 | bytes 4194304 | tf_op jit(solution)/shard_map/pallas_call | solution.py:218
  35.1 1.6 %collective-permute-done.12.refs_1_ = bf16[1280,128]{1,0:T(8,128)(2,1)} collective-permute-done((bf16[1280,128]{1,0:T(8,128)(2,1)S(1)}, bf16[1280,128]{1,0:T(8,128)(2,1)}, u32[]{:S(2)}, u32[]{:S(2)}) %collective-permute-start.12) | collective-permute-done | bytes 327712 | tf_op jit(solution)/shard_map/ppermute | solution.py:34
  36.6 0.9 collective-permute-start.15
  37.5 1.5 %collective-permute-start.16 = (bf16[1280,128]{1,0:T(8,128)(2,1)}, bf16[1280,128]{1,0:T(8,128)(2,1)S(1)}, u32[]{:S(2)}, u32[]{:S(2)}) collective-permute-start(bf16[1280,128]{1,0:T(8,128)(2,1)} %collective-permute-done.12.refs_1_), channel_id=1, source_target_pairs={{0,2},{1,3},{2,0},{3,1},{4,6},{5,7},{6,4},{7,5},{8,10},{9,11},{10,... | collective-permute-start | bytes 983048 | tf_op jit(solution)/shard_map/ppermute | solution.py:34
  39.0 4.5 %collective-permute-done.6.refs_0_ = bf16[1280,128]{1,0:T(8,128)(2,1)S(1)} collective-permute-done((bf16[1280,128]{1,0:T(8,128)(2,1)S(1)}, bf16[1280,128]{1,0:T(8,128)(2,1)S(1)}, u32[]{:S(2)}, u32[]{:S(2)}) %collective-permute-start.6) | collective-permute-done | bytes 327712 | tf_op jit(solution)/shard_map/ppermute | solution.py:34
  43.6 2.8 %shard_map.47.refs_5_ = f32[41024,128]{1,0:T(8,128)S(1)} custom-call(s32[1584]{0:T(1024)S(1)} %concatenate.10.table_ref, s32[6]{0:T(128)S(1)} %convert_reduce_fusion.1.bounds_ref, bf16[1280,128]{1,0:T(8,128)(2,1)S(1)} %collective-permute-done.2.refs_0_, bf16[1280,128]{1,0:T(8,128)(2,1)S(1)} %collective-permute-done.10.refs_1_, ...), custom_call_target="tpu_custom_call", output_to_operand_aliasing={{}: (7, {})} | custom-call | flops 107374184 | bytes 4194304 | tf_op jit(solution)/shard_map/pallas_call | solution.py:218
  46.3 1.2 %collective-permute-start.14 = (bf16[1280,128]{1,0:T(8,128)(2,1)S(1)}, bf16[1280,128]{1,0:T(8,128)(2,1)S(1)}, u32[]{:S(2)}, u32[]{:S(2)}) collective-permute-start(bf16[1280,128]{1,0:T(8,128)(2,1)S(1)} %collective-permute-done.7.refs_2_), channel_id=1, source_target_pairs={{0,4},{1,5},{2,6},{3,7},{4,8},{5,9},{6,10},{7,11},{8,12},{9,13},{1... | collective-permute-start | bytes 983048 | tf_op jit(solution)/shard_map/ppermute | solution.py:34
  47.6 2.6 %collective-permute-done.15.refs_1_ = bf16[1280,128]{1,0:T(8,128)(2,1)S(1)} collective-permute-done((bf16[1280,128]{1,0:T(8,128)(2,1)}, bf16[1280,128]{1,0:T(8,128)(2,1)S(1)}, u32[]{:S(2)}, u32[]{:S(2)}) %collective-permute-start.15) | collective-permute-done | bytes 327712 | tf_op jit(solution)/shard_map/ppermute | solution.py:34
  50.2 1.3 %collective-permute-start.17 = (bf16[1280,128]{1,0:T(8,128)(2,1)S(1)}, bf16[1280,128]{1,0:T(8,128)(2,1)S(1)}, u32[]{:S(2)}, u32[]{:S(2)}) collective-permute-start(bf16[1280,128]{1,0:T(8,128)(2,1)S(1)} %collective-permute-done.15.refs_1_), channel_id=1, source_target_pairs={{0,2},{1,3},{2,0},{3,1},{4,6},{5,7},{6,4},{7,5},{8,10},{9,11},{10,... | collective-permute-start | bytes 983048 | tf_op jit(solution)/shard_map/ppermute | solution.py:34
  51.4 3.6 %shard_map.48.refs_5_ = f32[41024,128]{1,0:T(8,128)S(1)} custom-call(s32[1584]{0:T(1024)S(1)} %concatenate.10.table_ref, s32[6]{0:T(128)S(1)} %convert_reduce_fusion.1.bounds_ref, bf16[1280,128]{1,0:T(8,128)(2,1)S(1)} %collective-permute-done.4.refs_0_, bf16[1280,128]{1,0:T(8,128)(2,1)} %collective-permute-done.12.refs_1_, ...), custom_call_target="tpu_custom_call", output_to_operand_aliasing={{}: (7, {})} | custom-call | flops 107374184 | bytes 4194304 | tf_op jit(solution)/shard_map/pallas_call | solution.py:218
  55.1 2.5 %shard_map.49.refs_3_ = f32[41024,128]{1,0:T(8,128)S(1)} custom-call(s32[1584]{0:T(1024)S(1)} %concatenate.10.table_ref, s32[6]{0:T(128)S(1)} %convert_reduce_fusion.1.bounds_ref, bf16[1280,128]{1,0:T(8,128)(2,1)S(1)} %collective-permute-done.6.refs_0_, bf16[1280,128]{1,0:T(8,128)(2,1)S(1)} %collective-permute-done.15.refs_1_, ...), custom_call_target="tpu_custom_call", output_to_operand_aliasing={{}: (7, {})} | custom-call | flops 107374184 | bytes 4194304 | tf_op jit(solution)/shard_map/pallas_call | solution.py:218
  57.6 1.3 %collective-permute-done.17.refs_1_ = bf16[1280,128]{1,0:T(8,128)(2,1)S(1)} collective-permute-done((bf16[1280,128]{1,0:T(8,128)(2,1)S(1)}, bf16[1280,128]{1,0:T(8,128)(2,1)S(1)}, u32[]{:S(2)}, u32[]{:S(2)}) %collective-permute-start.17) | collective-permute-done | bytes 327712 | tf_op jit(solution)/shard_map/ppermute | solution.py:34
  58.9 2.4 %shard_map.50 = (f32[41024,128]{1,0:T(8,128)S(1)}, bf16[256,128]{1,0:T(8,128)(2,1)S(1)}, bf16[1,1280,128]{2,1,0:T(8,128)(2,1)S(1)}, bf16[1,1280,128]{2,1,0:T(8,1...) custom-call(s32[1584]{0:T(1024)S(1)} %concatenate.10.table_ref, ...), custom_call_target="tpu_custom_call", output_to_operand_aliasing={{0}: (7, {})} | custom-call | flops 442918496 | bytes 4194304 | tf_op jit(solution)/shard_map/pallas_call | solution.py:218
  61.4 0.5 collective-permute-start.22
  62.0 0.4 collective-permute-start.23
  62.4 1.4 %shard_map.51 = (f32[1,1280,128]{2,1,0:T(8,128)S(1)}, f32[1,1280,128]{2,1,0:T(8,128)S(1)}, f32[1,1280,128]{2,1,0:T(8,128)S(1)}, f32[1,1280,128]{2,1,0:T(8,128)S(1)}) custom-call(s32[8]{0:T(128)S(1)} %fusion.30.chips_ref, s32[1]{0:T(128)} %bitcast.core_ref, f32[41024,128]{1,0:T(8,128)S(1)} %get-tuple-element.89.half, ...), custom_call_target="tpu_custom_call" | custom-call | flops 335544320 | bytes 4194304 | tf_op jit(solution)/shard_map/pallas_call | solution.py:218
  63.8 0.1 bitcast_add_fusion.3
  64.1 1.4 %shard_map.53 = (bf16[1,1280,128]{2,1,0:T(8,128)(2,1)S(1)}, bf16[1,1280,128]{2,1,0:T(8,128)(2,1)S(1)}, bf16[1,1280,128]{2,1,0:T(8,128)(2,1)S(1)}, bf16[1,1280,128]{2,1,0:T(8,128)(2,1)S(1)}) custom-call(s32[8]{0:T(128)S(1)} %fusion.30.chips_ref, s32[1]{0:T(128)} %bitcast.core_ref, f32[41024,128]{1,0:T(8,128)S(1)} %get-tuple-element.89.half, ...), custom_call_target="tpu_custom_call" | custom-call | flops 335544320 | bytes 4194304 | tf_op jit(solution)/shard_map/pallas_call | solution.py:218
  65.5 0.2 collective-permute-start.21
  65.6 2.0 %collective-permute-start.24 = (bf16[640,128]{1,0:T(8,128)(2,1)S(1)}, bf16[640,128]{1,0:T(8,128)(2,1)S(1)}, u32[]{:S(2)}, u32[]{:S(2)}) collective-permute-start(bf16[640,128]{1,0:T(8,128)(2,1)S(1)} %get-tuple-element.98), channel_id=1, source_target_pairs={{0,2},{1,3},{2,0},{3,1},{4,6},{5,7},{6,4},{7,5},{8,10},{9,11},{10,... | collective-permute-start | bytes 491528 | tf_op jit(solution)/shard_map/ppermute | solution.py:34
  67.7 0.9 collective-permute-start.28
  68.6 0.5 collective-permute-start.27
  69.2 1.4 %shard_map.52 = (f32[1,1280,128]{2,1,0:T(8,128)S(1)}, f32[1,1280,128]{2,1,0:T(8,128)S(1)}, f32[1,1280,128]{2,1,0:T(8,128)S(1)}, f32[1,1280,128]{2,1,0:T(8,128)S(1)}) custom-call(s32[8]{0:T(128)S(1)} %fusion.30.chips_ref, s32[1]{0:T(128)} %bitcast.core_ref, f32[41024,128]{1,0:T(8,128)S(1)} %get-tuple-element.89.half, ...), custom_call_target="tpu_custom_call" | custom-call | flops 335544320 | bytes 4194304 | tf_op jit(solution)/shard_map/pallas_call | solution.py:218
  70.6 2.2 %collective-permute-done.24 = bf16[640,128]{1,0:T(8,128)(2,1)S(1)} collective-permute-done((bf16[640,128]{1,0:T(8,128)(2,1)S(1)}, bf16[640,128]{1,0:T(8,128)(2,1)S(1)}, u32[]{:S(2)}, u32[]{:S(2)}) %collective-permute-start.24) | collective-permute-done | bytes 163872 | tf_op jit(solution)/shard_map/ppermute | solution.py:34
  72.7 3.2 %collective-permute-done.27 = bf16[640,128]{1,0:T(8,128)(2,1)S(1)} collective-permute-done((bf16[640,128]{1,0:T(8,128)(2,1)S(1)}, bf16[640,128]{1,0:T(8,128)(2,1)S(1)}, u32[]{:S(2)}, u32[]{:S(2)}) %collective-permute-start.27) | collective-permute-done | bytes 163872 | tf_op jit(solution)/shard_map/ppermute | solution.py:34
  75.9 3.3 %collective-permute-done.28 = bf16[1280,128]{1,0:T(8,128)(2,1)S(1)} collective-permute-done((bf16[1280,128]{1,0:T(8,128)(2,1)S(1)}, bf16[1280,128]{1,0:T(8,128)(2,1)S(1)}, u32[]{:S(2)}, u32[]{:S(2)}) %collective-permute-start.28) | collective-permute-done | bytes 327712 | tf_op jit(solution)/shard_map/ppermute | solution.py:34
  79.2 0.3 collective-permute-start.32
  79.6 0.1 fusion.5
  79.7 0.4 collective-permute-start.29
  80.2 8.3 %collective-permute-done.25 = bf16[640,128]{1,0:T(8,128)(2,1)S(1)} collective-permute-done((bf16[640,128]{1,0:T(8,128)(2,1)S(1)}, bf16[640,128]{1,0:T(8,128)(2,1)S(1)}, u32[]{:S(2)}, u32[]{:S(2)}) %collective-permute-start.25) | collective-permute-done | bytes 163872 | tf_op jit(solution)/shard_map/ppermute | solution.py:34
  88.6 2.5 %collective-permute-done.29 = bf16[640,128]{1,0:T(8,128)(2,1)S(1)} collective-permute-done((bf16[640,128]{1,0:T(8,128)(2,1)S(1)}, bf16[640,128]{1,0:T(8,128)(2,1)S(1)}, u32[]{:S(2)}, u32[]{:S(2)}) %collective-permute-start.29) | collective-permute-done | bytes 163872 | tf_op jit(solution)/shard_map/ppermute | solution.py:34
  91.3 0.1 fusion.3
  91.4 3.8 %collective-permute-start.35 = (bf16[1280,128]{1,0:T(8,128)(2,1)S(1)}, bf16[1280,128]{1,0:T(8,128)(2,1)S(1)}, u32[]{:S(2)}, u32[]{:S(2)}) collective-permute-start(bf16[1280,128]{1,0:T(8,128)(2,1)S(1)} %fusion.3), channel_id=1, source_target_pairs={{0,12},{1,13},{2,14},{3,15},{4,0},{5,1},{6,2},{7,3},{8,4},{9,5},{1... | collective-permute-start | bytes 983048 | tf_op jit(solution)/shard_map/ppermute | solution.py:34
  95.3 1.5 %collective-permute-start.33 = (bf16[1280,128]{1,0:T(8,128)(2,1)S(1)}, bf16[1280,128]{1,0:T(8,128)(2,1)S(1)}, u32[]{:S(2)}, u32[]{:S(2)}) collective-permute-start(bf16[1280,128]{1,0:T(8,128)(2,1)S(1)} %fusion.5), channel_id=1, source_target_pairs={{0,2},{1,3},{2,0},{3,1},{4,6},{5,7},{6,4},{7,5},{8,10},{9,11},{10,... | collective-permute-start | bytes 983048 | tf_op jit(solution)/shard_map/ppermute | solution.py:34
  96.8 0.7 collective-permute-done.26
  97.5 3.5 %collective-permute-done.30 = bf16[640,128]{1,0:T(8,128)(2,1)S(1)} collective-permute-done((bf16[640,128]{1,0:T(8,128)(2,1)S(1)}, bf16[640,128]{1,0:T(8,128)(2,1)S(1)}, u32[]{:S(2)}, u32[]{:S(2)}) %collective-permute-start.30) | collective-permute-done | bytes 163872 | tf_op jit(solution)/shard_map/ppermute | solution.py:34
  101.0 0.1 fusion.7
  101.1 3.2 %collective-permute-done.35 = bf16[1280,128]{1,0:T(8,128)(2,1)S(1)} collective-permute-done((bf16[1280,128]{1,0:T(8,128)(2,1)S(1)}, bf16[1280,128]{1,0:T(8,128)(2,1)S(1)}, u32[]{:S(2)}, u32[]{:S(2)}) %collective-permute-start.35) | collective-permute-done | bytes 327712 | tf_op jit(solution)/shard_map/ppermute | solution.py:34
  104.4 0.9 add_multiply_fusion
  (50 shorter events, 1.0 us)
Async XLA Ops:
  0.0 9.3 %collective-permute-start.9 = (bf16[256,4096]{1,0:T(8,128)(2,1)}, bf16[256,4096]{1,0:T(8,128)(2,1)}, u32[]{:S(2)}, u32[]{:S(2)}) collective-permute-start(bf16[256,4096]{1,0:T(8,128)(2,1)} %param.4), channel_id=1, source_target_pairs={{0,1},{1,0},{2,3},{3,2},{4,5},{5,4},{6,7},{7,6},{8,9},{9,8},{10,11... | collective-permute-start | bytes 6291464 | tf_op jit(solution)/shard_map/ppermute | solution.py:34
  1.6 13.2 %copy-start.2 = (bf16[1280,128]{1,0:T(8,128)(2,1)}, bf16[1280,128]{1,0:T(8,128)(2,1)S(1)}, u32[]{:S(2)}) copy-start(bf16[1280,128]{1,0:T(8,128)(2,1)S(1)} %get-tuple-element.123.refs_0_) | copy-start | bytes 983044
  1.6 13.2 %collective-permute-start.2 = (bf16[1280,128]{1,0:T(8,128)(2,1)S(1)}, bf16[1280,128]{1,0:T(8,128)(2,1)S(1)}, u32[]{:S(2)}, u32[]{:S(2)}) collective-permute-start(bf16[1280,128]{1,0:T(8,128)(2,1)S(1)} %get-tuple-element.123.refs_0_), channel_id=1, source_target_pairs={{0,4},{1,5},{2,6},{3,7},{4,8},{5,9},{6,10},{7,11},{8,12},{9,13},{1... | collective-permute-start | bytes 983048 | tf_op jit(solution)/shard_map/ppermute | solution.py:34
  4.2 10.6 %collective-permute-start.3 = (bf16[1280,128]{1,0:T(8,128)(2,1)S(1)}, bf16[1280,128]{1,0:T(8,128)(2,1)S(1)}, u32[]{:S(2)}, u32[]{:S(2)}) collective-permute-start(bf16[1280,128]{1,0:T(8,128)(2,1)S(1)} %get-tuple-element.123.refs_0_), channel_id=1, source_target_pairs={{0,2},{1,3},{2,0},{3,1},{4,6},{5,7},{6,4},{7,5},{8,10},{9,11},{10,... | collective-permute-start | bytes 983048 | tf_op jit(solution)/shard_map/ppermute | solution.py:34
  5.7 1.9 %collective-permute-start.1 = (s32[256,2]{0,1:T(2,128)}, s32[256,2]{0,1:T(2,128)S(1)}, u32[]{:S(2)}, u32[]{:S(2)}) collective-permute-start(s32[256,2]{0,1:T(2,128)} %param.5), channel_id=1, source_target_pairs={{0,1},{1,0},{2,3},{3,2},{4,5},{5,4},{6,7},{7,6},{8,9},{9,8},{10,11... | collective-permute-start | bytes 6152 | tf_op jit(solution)/shard_map/ppermute | solution.py:34
  5.7 2.0 %collective-permute-start = (s32[1]{0:T(128)}, s32[1]{0:T(128)}, u32[]{:S(2)}, u32[]{:S(2)}) collective-permute-start(s32[1]{0:T(128)} %param.6), channel_id=1, source_target_pairs={{0,1},{1,0},{2,3},{3,2},{4,5},{5,4},{6,7},{7,6},{8,9},{9,8},{10,11... | collective-permute-start | bytes 20 | tf_op jit(solution)/shard_map/ppermute | solution.py:34
  7.6 1.7 %collective-permute-start.8 = (bf16[1280,128]{1,0:T(8,128)(2,1)S(1)}, bf16[1280,128]{1,0:T(8,128)(2,1)S(1)}, u32[]{:S(2)}, u32[]{:S(2)}) collective-permute-start(bf16[1280,128]{1,0:T(8,128)(2,1)S(1)} %get-tuple-element.122), channel_id=1, source_target_pairs={{0,1},{1,0},{2,3},{3,2},{4,5},{5,4},{6,7},{7,6},{8,9},{9,8},{10,11... | collective-permute-start | bytes 983048 | tf_op jit(solution)/shard_map/ppermute | solution.py:34
  9.3 10.6 %copy-start.3 = (bf16[1280,128]{1,0:T(8,128)(2,1)}, bf16[1280,128]{1,0:T(8,128)(2,1)S(1)}, u32[]{:S(2)}) copy-start(bf16[1280,128]{1,0:T(8,128)(2,1)S(1)} %collective-permute-done.8.refs_1_) | copy-start | bytes 983044
  9.3 14.1 %collective-permute-start.10 = (bf16[1280,128]{1,0:T(8,128)(2,1)S(1)}, bf16[1280,128]{1,0:T(8,128)(2,1)S(1)}, u32[]{:S(2)}, u32[]{:S(2)}) collective-permute-start(bf16[1280,128]{1,0:T(8,128)(2,1)S(1)} %collective-permute-done.8.refs_1_), channel_id=1, source_target_pairs={{0,4},{1,5},{2,6},{3,7},{4,8},{5,9},{6,10},{7,11},{8,12},{9,13},{1... | collective-permute-start | bytes 983048 | tf_op jit(solution)/shard_map/ppermute | solution.py:34
  10.9 12.5 %collective-permute-start.11 = (bf16[1280,128]{1,0:T(8,128)(2,1)S(1)}, bf16[1280,128]{1,0:T(8,128)(2,1)S(1)}, u32[]{:S(2)}, u32[]{:S(2)}) collective-permute-start(bf16[1280,128]{1,0:T(8,128)(2,1)S(1)} %collective-permute-done.8.refs_1_), channel_id=1, source_target_pairs={{0,2},{1,3},{2,0},{3,1},{4,6},{5,7},{6,4},{7,5},{8,10},{9,11},{10,... | collective-permute-start | bytes 983048 | tf_op jit(solution)/shard_map/ppermute | solution.py:34
  14.8 14.0 %collective-permute-start.4 = (bf16[1280,128]{1,0:T(8,128)(2,1)S(1)}, bf16[1280,128]{1,0:T(8,128)(2,1)S(1)}, u32[]{:S(2)}, u32[]{:S(2)}) collective-permute-start(bf16[1280,128]{1,0:T(8,128)(2,1)S(1)} %collective-permute-done.2.refs_0_), channel_id=1, source_target_pairs={{0,4},{1,5},{2,6},{3,7},{4,8},{5,9},{6,10},{7,11},{8,12},{9,13},{1... | collective-permute-start | bytes 983048 | tf_op jit(solution)/shard_map/ppermute | solution.py:34
  16.3 12.6 %collective-permute-start.5 = (bf16[1280,128]{1,0:T(8,128)(2,1)S(1)}, bf16[1280,128]{1,0:T(8,128)(2,1)}, u32[]{:S(2)}, u32[]{:S(2)}) collective-permute-start(bf16[1280,128]{1,0:T(8,128)(2,1)S(1)} %collective-permute-done.2.refs_0_), channel_id=1, source_target_pairs={{0,2},{1,3},{2,0},{3,1},{4,6},{5,7},{6,4},{7,5},{8,10},{9,11},{10,... | collective-permute-start | bytes 983048 | tf_op jit(solution)/shard_map/ppermute | solution.py:34
  23.3 0.7 copy-start
  24.1 12.6 %collective-permute-start.12 = (bf16[1280,128]{1,0:T(8,128)(2,1)S(1)}, bf16[1280,128]{1,0:T(8,128)(2,1)}, u32[]{:S(2)}, u32[]{:S(2)}) collective-permute-start(bf16[1280,128]{1,0:T(8,128)(2,1)S(1)} %collective-permute-done.10.refs_1_), channel_id=1, source_target_pairs={{0,4},{1,5},{2,6},{3,7},{4,8},{5,9},{6,10},{7,11},{8,12},{9,13},{1... | collective-permute-start | bytes 983048 | tf_op jit(solution)/shard_map/ppermute | solution.py:34
  25.7 11.0 %collective-permute-start.13 = (bf16[1280,128]{1,0:T(8,128)(2,1)S(1)}, bf16[1280,128]{1,0:T(8,128)(2,1)}, u32[]{:S(2)}, u32[]{:S(2)}) collective-permute-start(bf16[1280,128]{1,0:T(8,128)(2,1)S(1)} %collective-permute-done.10.refs_1_), channel_id=1, source_target_pairs={{0,2},{1,3},{2,0},{3,1},{4,6},{5,7},{6,4},{7,5},{8,10},{9,11},{10,... | collective-permute-start | bytes 983048 | tf_op jit(solution)/shard_map/ppermute | solution.py:34
  27.2 16.3 %copy-start.1 = (bf16[1280,128]{1,0:T(8,128)(2,1)S(1)}, bf16[1280,128]{1,0:T(8,128)(2,1)}, u32[]{:S(2)}) copy-start(bf16[1280,128]{1,0:T(8,128)(2,1)} %copy-done) | copy-start | bytes 983044
  28.9 14.6 %collective-permute-start.6 = (bf16[1280,128]{1,0:T(8,128)(2,1)S(1)}, bf16[1280,128]{1,0:T(8,128)(2,1)S(1)}, u32[]{:S(2)}, u32[]{:S(2)}) collective-permute-start(bf16[1280,128]{1,0:T(8,128)(2,1)S(1)} %collective-permute-done.4.refs_0_), channel_id=1, source_target_pairs={{0,4},{1,5},{2,6},{3,7},{4,8},{5,9},{6,10},{7,11},{8,12},{9,13},{1... | collective-permute-start | bytes 983048 | tf_op jit(solution)/shard_map/ppermute | solution.py:34
  30.5 13.1 %collective-permute-start.7 = (bf16[1280,128]{1,0:T(8,128)(2,1)S(1)}, bf16[1280,128]{1,0:T(8,128)(2,1)S(1)}, u32[]{:S(2)}, u32[]{:S(2)}) collective-permute-start(bf16[1280,128]{1,0:T(8,128)(2,1)S(1)} %collective-permute-done.4.refs_0_), channel_id=1, source_target_pairs={{0,2},{1,3},{2,0},{3,1},{4,6},{5,7},{6,4},{7,5},{8,10},{9,11},{10,... | collective-permute-start | bytes 983048 | tf_op jit(solution)/shard_map/ppermute | solution.py:34
  36.6 13.5 %collective-permute-start.15 = (bf16[1280,128]{1,0:T(8,128)(2,1)}, bf16[1280,128]{1,0:T(8,128)(2,1)S(1)}, u32[]{:S(2)}, u32[]{:S(2)}) collective-permute-start(bf16[1280,128]{1,0:T(8,128)(2,1)} %collective-permute-done.12.refs_1_), channel_id=1, source_target_pairs={{0,4},{1,5},{2,6},{3,7},{4,8},{5,9},{6,10},{7,11},{8,12},{9,13},{1... | collective-permute-start | bytes 983048 | tf_op jit(solution)/shard_map/ppermute | solution.py:34
  37.5 12.7 %collective-permute-start.16 = (bf16[1280,128]{1,0:T(8,128)(2,1)}, bf16[1280,128]{1,0:T(8,128)(2,1)S(1)}, u32[]{:S(2)}, u32[]{:S(2)}) collective-permute-start(bf16[1280,128]{1,0:T(8,128)(2,1)} %collective-permute-done.12.refs_1_), channel_id=1, source_target_pairs={{0,2},{1,3},{2,0},{3,1},{4,6},{5,7},{6,4},{7,5},{8,10},{9,11},{10,... | collective-permute-start | bytes 983048 | tf_op jit(solution)/shard_map/ppermute | solution.py:34
  46.3 11.2 %collective-permute-start.14 = (bf16[1280,128]{1,0:T(8,128)(2,1)S(1)}, bf16[1280,128]{1,0:T(8,128)(2,1)S(1)}, u32[]{:S(2)}, u32[]{:S(2)}) collective-permute-start(bf16[1280,128]{1,0:T(8,128)(2,1)S(1)} %collective-permute-done.7.refs_2_), channel_id=1, source_target_pairs={{0,4},{1,5},{2,6},{3,7},{4,8},{5,9},{6,10},{7,11},{8,12},{9,13},{1... | collective-permute-start | bytes 983048 | tf_op jit(solution)/shard_map/ppermute | solution.py:34
  50.2 8.7 %collective-permute-start.17 = (bf16[1280,128]{1,0:T(8,128)(2,1)S(1)}, bf16[1280,128]{1,0:T(8,128)(2,1)S(1)}, u32[]{:S(2)}, u32[]{:S(2)}) collective-permute-start(bf16[1280,128]{1,0:T(8,128)(2,1)S(1)} %collective-permute-done.15.refs_1_), channel_id=1, source_target_pairs={{0,2},{1,3},{2,0},{3,1},{4,6},{5,7},{6,4},{7,5},{8,10},{9,11},{10,... | collective-permute-start | bytes 983048 | tf_op jit(solution)/shard_map/ppermute | solution.py:34
  61.3 2.5 %collective-permute-start.19 = (bf16[1280,128]{1,0:T(8,128)(2,1)S(1)}, bf16[1280,128]{1,0:T(8,128)(2,1)S(1)}, u32[]{:S(2)}, u32[]{:S(2)}) collective-permute-start(bf16[1280,128]{1,0:T(8,128)(2,1)S(1)} %bitcast.61), channel_id=1, source_target_pairs={{0,1},{1,0},{2,3},{3,2},{4,5},{5,4},{6,7},{7,6},{8,9},{9,8},{10,11... | collective-permute-start | bytes 983048 | tf_op jit(solution)/shard_map/ppermute | solution.py:34
  61.4 2.4 %collective-permute-start.22 = (bf16[1280,128]{1,0:T(8,128)(2,1)S(1)}, bf16[1280,128]{1,0:T(8,128)(2,1)S(1)}, u32[]{:S(2)}, u32[]{:S(2)}) collective-permute-start(bf16[1280,128]{1,0:T(8,128)(2,1)S(1)} %bitcast.60), channel_id=1, source_target_pairs={{0,1},{1,0},{2,3},{3,2},{4,5},{5,4},{6,7},{7,6},{8,9},{9,8},{10,11... | collective-permute-start | bytes 983048 | tf_op jit(solution)/shard_map/ppermute | solution.py:34
  61.9 2.1 %collective-permute-start.18 = (bf16[1280,128]{1,0:T(8,128)(2,1)S(1)}, bf16[1280,128]{1,0:T(8,128)(2,1)S(1)}, u32[]{:S(2)}, u32[]{:S(2)}) collective-permute-start(bf16[1280,128]{1,0:T(8,128)(2,1)S(1)} %bitcast.59), channel_id=1, source_target_pairs={{0,1},{1,0},{2,3},{3,2},{4,5},{5,4},{6,7},{7,6},{8,9},{9,8},{10,11... | collective-permute-start | bytes 983048 | tf_op jit(solution)/shard_map/ppermute | solution.py:34
  62.0 7.1 %collective-permute-start.23 = (bf16[1280,128]{1,0:T(8,128)(2,1)S(1)}, bf16[1280,128]{1,0:T(8,128)(2,1)S(1)}, u32[]{:S(2)}, u32[]{:S(2)}) collective-permute-start(bf16[1280,128]{1,0:T(8,128)(2,1)S(1)} %bitcast.57), channel_id=1, source_target_pairs={{0,1},{1,0},{2,3},{3,2},{4,5},{5,4},{6,7},{7,6},{8,9},{9,8},{10,11... | collective-permute-start | bytes 983048 | tf_op jit(solution)/shard_map/ppermute | solution.py:34
  65.5 14.3 %collective-permute-start.21 = (bf16[1280,128]{1,0:T(8,128)(2,1)S(1)}, bf16[1280,128]{1,0:T(8,128)(2,1)S(1)}, u32[]{:S(2)}, u32[]{:S(2)}) collective-permute-start(bf16[1280,128]{1,0:T(8,128)(2,1)S(1)} %bitcast.56), channel_id=1, source_target_pairs={{0,1},{1,0},{2,3},{3,2},{4,5},{5,4},{6,7},{7,6},{8,9},{9,8},{10,11... | collective-permute-start | bytes 983048 | tf_op jit(solution)/shard_map/ppermute | solution.py:34
  65.6 7.1 %collective-permute-start.24 = (bf16[640,128]{1,0:T(8,128)(2,1)S(1)}, bf16[640,128]{1,0:T(8,128)(2,1)S(1)}, u32[]{:S(2)}, u32[]{:S(2)}) collective-permute-start(bf16[640,128]{1,0:T(8,128)(2,1)S(1)} %get-tuple-element.98), channel_id=1, source_target_pairs={{0,2},{1,3},{2,0},{3,1},{4,6},{5,7},{6,4},{7,5},{8,10},{9,11},{10,... | collective-permute-start | bytes 491528 | tf_op jit(solution)/shard_map/ppermute | solution.py:34
  67.7 11.5 %collective-permute-start.28 = (bf16[1280,128]{1,0:T(8,128)(2,1)S(1)}, bf16[1280,128]{1,0:T(8,128)(2,1)S(1)}, u32[]{:S(2)}, u32[]{:S(2)}) collective-permute-start(bf16[1280,128]{1,0:T(8,128)(2,1)S(1)} %get-tuple-element.103), channel_id=1, source_target_pairs={{0,4},{1,5},{2,6},{3,7},{4,8},{5,9},{6,10},{7,11},{8,12},{9,13},{1... | collective-permute-start | bytes 983048 | tf_op jit(solution)/shard_map/ppermute | solution.py:34
  68.6 7.3 %collective-permute-start.27 = (bf16[640,128]{1,0:T(8,128)(2,1)S(1)}, bf16[640,128]{1,0:T(8,128)(2,1)S(1)}, u32[]{:S(2)}, u32[]{:S(2)}) collective-permute-start(bf16[640,128]{1,0:T(8,128)(2,1)S(1)} %get-tuple-element.102), channel_id=1, source_target_pairs={{0,2},{1,3},{2,0},{3,1},{4,6},{5,7},{6,4},{7,5},{8,10},{9,11},{10,... | collective-permute-start | bytes 491528 | tf_op jit(solution)/shard_map/ppermute | solution.py:34
  69.1 10.4 %collective-permute-start.31 = (bf16[1280,128]{1,0:T(8,128)(2,1)S(1)}, bf16[1280,128]{1,0:T(8,128)(2,1)S(1)}, u32[]{:S(2)}, u32[]{:S(2)}) collective-permute-start(bf16[1280,128]{1,0:T(8,128)(2,1)S(1)} %bitcast.58), channel_id=1, source_target_pairs={{0,1},{1,0},{2,3},{3,2},{4,5},{5,4},{6,7},{7,6},{8,9},{9,8},{10,11... | collective-permute-start | bytes 983048 | tf_op jit(solution)/shard_map/ppermute | solution.py:34
  72.7 24.1 %collective-permute-start.20 = (bf16[1280,128]{1,0:T(8,128)(2,1)S(1)}, bf16[1280,128]{1,0:T(8,128)(2,1)S(1)}, u32[]{:S(2)}, u32[]{:S(2)}) collective-permute-start(bf16[1280,128]{1,0:T(8,128)(2,1)S(1)} %bitcast.54), channel_id=1, source_target_pairs={{0,1},{1,0},{2,3},{3,2},{4,5},{5,4},{6,7},{7,6},{8,9},{9,8},{10,11... | collective-permute-start | bytes 983048 | tf_op jit(solution)/shard_map/ppermute | solution.py:34
  75.9 15.4 %collective-permute-start.34 = (bf16[1280,128]{1,0:T(8,128)(2,1)S(1)}, bf16[1280,128]{1,0:T(8,128)(2,1)S(1)}, u32[]{:S(2)}, u32[]{:S(2)}) collective-permute-start(bf16[1280,128]{1,0:T(8,128)(2,1)S(1)} %bitcast.55), channel_id=1, source_target_pairs={{0,1},{1,0},{2,3},{3,2},{4,5},{5,4},{6,7},{7,6},{8,9},{9,8},{10,11... | collective-permute-start | bytes 983048 | tf_op jit(solution)/shard_map/ppermute | solution.py:34
  79.2 12.1 %collective-permute-start.32 = (bf16[1280,128]{1,0:T(8,128)(2,1)S(1)}, bf16[1280,128]{1,0:T(8,128)(2,1)S(1)}, u32[]{:S(2)}, u32[]{:S(2)}) collective-permute-start(bf16[1280,128]{1,0:T(8,128)(2,1)S(1)} %fusion.6), channel_id=1, source_target_pairs={{0,2},{1,3},{2,0},{3,1},{4,6},{5,7},{6,4},{7,5},{8,10},{9,11},{10,... | collective-permute-start | bytes 983048 | tf_op jit(solution)/shard_map/ppermute | solution.py:34
  79.5 9.0 %collective-permute-start.25 = (bf16[640,128]{1,0:T(8,128)(2,1)S(1)}, bf16[640,128]{1,0:T(8,128)(2,1)S(1)}, u32[]{:S(2)}, u32[]{:S(2)}) collective-permute-start(bf16[640,128]{1,0:T(8,128)(2,1)S(1)} %get-tuple-element.120), channel_id=1, source_target_pairs={{0,4},{1,5},{2,6},{3,7},{4,8},{5,9},{6,10},{7,11},{8,12},{9,13},{1... | collective-permute-start | bytes 491528 | tf_op jit(solution)/shard_map/ppermute | solution.py:34
  79.7 11.4 %collective-permute-start.29 = (bf16[640,128]{1,0:T(8,128)(2,1)S(1)}, bf16[640,128]{1,0:T(8,128)(2,1)S(1)}, u32[]{:S(2)}, u32[]{:S(2)}) collective-permute-start(bf16[640,128]{1,0:T(8,128)(2,1)S(1)} %get-tuple-element.121), channel_id=1, source_target_pairs={{0,4},{1,5},{2,6},{3,7},{4,8},{5,9},{6,10},{7,11},{8,12},{9,13},{1... | collective-permute-start | bytes 491528 | tf_op jit(solution)/shard_map/ppermute | solution.py:34
  88.6 8.9 %collective-permute-start.26 = (bf16[640,128]{1,0:T(8,128)(2,1)S(1)}, bf16[640,128]{1,0:T(8,128)(2,1)S(1)}, u32[]{:S(2)}, u32[]{:S(2)}) collective-permute-start(bf16[640,128]{1,0:T(8,128)(2,1)S(1)} %fusion.12), channel_id=1, source_target_pairs={{0,4},{1,5},{2,6},{3,7},{4,8},{5,9},{6,10},{7,11},{8,12},{9,13},{1... | collective-permute-start | bytes 491528 | tf_op jit(solution)/shard_map/ppermute | solution.py:34
  91.2 9.8 %collective-permute-start.30 = (bf16[640,128]{1,0:T(8,128)(2,1)S(1)}, bf16[640,128]{1,0:T(8,128)(2,1)S(1)}, u32[]{:S(2)}, u32[]{:S(2)}) collective-permute-start(bf16[640,128]{1,0:T(8,128)(2,1)S(1)} %add_convert_fusion), channel_id=1, source_target_pairs={{0,4},{1,5},{2,6},{3,7},{4,8},{5,9},{6,10},{7,11},{8,12},{9,13},{1... | collective-permute-start | bytes 491528 | tf_op jit(solution)/shard_map/ppermute | solution.py:34
  91.4 12.9 %collective-permute-start.35 = (bf16[1280,128]{1,0:T(8,128)(2,1)S(1)}, bf16[1280,128]{1,0:T(8,128)(2,1)S(1)}, u32[]{:S(2)}, u32[]{:S(2)}) collective-permute-start(bf16[1280,128]{1,0:T(8,128)(2,1)S(1)} %fusion.3), channel_id=1, source_target_pairs={{0,12},{1,13},{2,14},{3,15},{4,0},{5,1},{6,2},{7,3},{8,4},{9,5},{1... | collective-permute-start | bytes 983048 | tf_op jit(solution)/shard_map/ppermute | solution.py:34
  95.3 9.1 %collective-permute-start.33 = (bf16[1280,128]{1,0:T(8,128)(2,1)S(1)}, bf16[1280,128]{1,0:T(8,128)(2,1)S(1)}, u32[]{:S(2)}, u32[]{:S(2)}) collective-permute-start(bf16[1280,128]{1,0:T(8,128)(2,1)S(1)} %fusion.5), channel_id=1, source_target_pairs={{0,2},{1,3},{2,0},{3,1},{4,6},{5,7},{6,4},{7,5},{8,10},{9,11},{10,... | collective-permute-start | bytes 983048 | tf_op jit(solution)/shard_map/ppermute | solution.py:34

commit v20 on v19

--- a/solution.py
+++ b/solution.py
@@ -80,26 +80,27 @@
     rest = [NEAR1, FAR0, NEAR3, NEAR0]
     sends = blocks_of(first, False)
     total = {name: paired(*pair) for name, *pair in zip(first, sends, blocks_of(first, True))}
-    crossing, aside = list(map(narrow, halves(total[FAR2]))), narrow(total[FAR1])
-    *crossing, aside = blocks_of.hold(*crossing, aside)
-    two_on = [move(part, ACROSS) for part in crossing]
+    aside, beside = map(narrow, halves(total[FAR1]))
+    crossing = narrow(total[FAR2])
+    crossing, aside, beside = blocks_of.hold(crossing, aside, beside)
+    two_on = move(crossing, ACROSS)
     joining = move(aside, ALONG)
     total.update({name: paired(*pair) for name, *pair in zip(rest, blocks_of(rest, False), blocks_of(rest, True))})
 
-    two_on[1], joining = tie(two_on[1], joining)
-    crossing, two_on[0] = tie(narrow(total[FAR3]), two_on[0])
-    three_on = move(crossing, ACROSS)
-    crossing, three_on = tie(narrow(total[FAR0] + wide(joining)), three_on)
+    two_on, joining = tie(two_on, joining)
+    beside, two_on = tie(beside, two_on)
+    beside = move(beside, ACROSS)
+    three_on, two_on = tie(narrow(total[FAR3]), two_on)
+    three_on = move(three_on, ACROSS)
+    two_on = move(narrow(total[NEAR2] + wide(two_on)), ALONG)
+    rows = beside.shape[0]
+    beside, joining = jnp.pad(wide(beside), ((rows, 0), (0, 0))), jnp.pad(wide(joining), ((0, rows), (0, 0)))
+    one_on = move(narrow(total[NEAR1] + wide(two_on) + beside), ALONG)
+    total[FAR0], two_on = tie(total[FAR0], two_on)
+    crossing, three_on = tie(narrow(total[FAR0] + joining), three_on)
     straight = move(crossing, ACROSS)
-    two_on = [move(narrow(own + wide(part)), ALONG) for own, part in zip(halves(total[NEAR2]), two_on)]
-    later, two_on[0] = tie(total[NEAR1], two_on[0])
-    one_on = [
-        move(narrow(halves(own)[index] + wide(two_on[index])), ALONG)
-        for index, own in enumerate((total[NEAR1], later))
-    ]
     one_back = move(narrow(total[NEAR3] + wide(three_on)), BACK)
-    (result,) = tie(total[NEAR0] + wide(jnp.concatenate(one_on)))
-    return result + wide(straight) + wide(one_back)
+    return total[NEAR0] + wide(one_on) + wide(straight) + wide(one_back)
 
 
 def clear(half):

time: 105 us -> 106 us (level); the launches traced: 105 us -> 105 us
  Pallas kernels: 18.5 us -> 15.7 us
  waiting for transfers between devices: 42.2 us -> 44.2 us
    pallas_call x8, Pallas kernels: 18.5 us -> 15.7 us  [call(): pl.pallas_call(kernel, out_shape=outs, in_specs=in_specs, out_specs=[VMEM...]
    ppermute x36 -> x34, waiting for transfers between devices: 42.2 us -> 44.2 us  [move(): return lax.ppermute(array, 'aux', pairs)]
    ppermute x36 -> x34, starting transfers between devices: 31.3 us -> 32.2 us  [move(): return lax.ppermute(array, 'aux', pairs)]
  transfers between devices with their start and end apart: 36 -> 34, of which waited for: 16 -> 17; matrix products, arithmetic and copies ran while one was open for 10% -> 10% of each run, Pallas kernels for 15% -> 13%
where the time goes in v20:
time: 106 us; the launch traced here: 105 us
  waiting for transfers between devices  44.2 us (42%)
  starting transfers between devices  32.2 us (30%)
  Pallas kernels  15.7 us (15%)
  local copies, waits for them, and re-layouts  8.14 us (8%)
  other arithmetic  4.07 us (4%)
    ppermute x34, waiting for transfers between devices, move(): return lax.ppermute(array, 'aux', pairs)  44.2 us
    ppermute x34, starting transfers between devices, move(): return lax.ppermute(array, 'aux', pairs)  32.2 us
    pallas_call x8, Pallas kernels, call(): pl.pallas_call(kernel, out_shape=outs, in_specs=in_specs, out_specs=[VMEM...  15.7 us
    unnamed x11, local copies, waits for them, and re-layouts  6.92 us
  transfers between devices with their start and end apart: 34, of which 17 were waited for; matrix products, arithmetic and copies ran while one was open for 10% of the time, Pallas kernels for 13%

profile of v20, /device:TPU:0, one launch (start us, length us, event | category | flops | bytes accessed | tf_op | source)
XLA Modules:
  0.0 105.2 jit_solution(14927397889943916340)
XLA Ops:
  0.0 0.5 collective-permute-start.9
  0.5 1.1 %constant_dynamic-slice_fusion.1 = (bf16[1280,128]{1,0:T(8,128)(2,1)S(1)}, bf16[1280,128]{1,0:T(8,128)(2,1)S(1)}) fusion(bf16[1280,256]{1,0:T(8,128)(2,1)} %param.7, s32[]{:T(128)S(6)} %select_n.162, s32[]{:T(128)S(6)} %select_n.161), kind=kLoop, calls=%fused_computation.90 | loop fusion | bytes 1310728 | tf_op jit(solution)/shard_map/dynamic_slice | solution.py:246
  1.6 2.6 %collective-permute-start.2 = (bf16[1280,128]{1,0:T(8,128)(2,1)S(1)}, bf16[1280,128]{1,0:T(8,128)(2,1)S(1)}, u32[]{:S(2)}, u32[]{:S(2)}) collective-permute-start(bf16[1280,128]{1,0:T(8,128)(2,1)S(1)} %get-tuple-element.123.refs_0_), channel_id=1, source_target_pairs={{0,4},{1,5},{2,6},{3,7},{4,8},{5,9},{6,10},{7,11},{8,12},{9,13},{1... | collective-permute-start | bytes 983048 | tf_op jit(solution)/shard_map/ppermute | solution.py:34
  4.2 1.5 %collective-permute-start.3 = (bf16[1280,128]{1,0:T(8,128)(2,1)S(1)}, bf16[1280,128]{1,0:T(8,128)(2,1)S(1)}, u32[]{:S(2)}, u32[]{:S(2)}) collective-permute-start(bf16[1280,128]{1,0:T(8,128)(2,1)S(1)} %get-tuple-element.123.refs_0_), channel_id=1, source_target_pairs={{0,2},{1,3},{2,0},{3,1},{4,6},{5,7},{6,4},{7,5},{8,10},{9,11},{10,... | collective-permute-start | bytes 983048 | tf_op jit(solution)/shard_map/ppermute | solution.py:34
  5.7 0.5 collective-permute-start
  6.2 0.7 constant_dynamic-update-slice_fusion.1
  7.7 0.7 compare_select_fusion.3
  8.4 0.9 collective-permute-done.8.refs_1_
  9.3 1.6 %collective-permute-start.10 = (bf16[1280,128]{1,0:T(8,128)(2,1)S(1)}, bf16[1280,128]{1,0:T(8,128)(2,1)S(1)}, u32[]{:S(2)}, u32[]{:S(2)}) collective-permute-start(bf16[1280,128]{1,0:T(8,128)(2,1)S(1)} %collective-permute-done.8.refs_1_), channel_id=1, source_target_pairs={{0,4},{1,5},{2,6},{3,7},{4,8},{5,9},{6,10},{7,11},{8,12},{9,13},{1... | collective-permute-start | bytes 983048 | tf_op jit(solution)/shard_map/ppermute | solution.py:34
  10.9 0.5 collective-permute-start.11
  11.4 0.6 fusion.30
  12.0 2.8 %collective-permute-done.2.refs_0_ = bf16[1280,128]{1,0:T(8,128)(2,1)S(1)} collective-permute-done((bf16[1280,128]{1,0:T(8,128)(2,1)S(1)}, bf16[1280,128]{1,0:T(8,128)(2,1)S(1)}, u32[]{:S(2)}, u32[]{:S(2)}) %collective-permute-start.2) | collective-permute-done | bytes 327712 | tf_op jit(solution)/shard_map/ppermute | solution.py:34
  14.8 1.5 %collective-permute-start.4 = (bf16[1280,128]{1,0:T(8,128)(2,1)S(1)}, bf16[1280,128]{1,0:T(8,128)(2,1)S(1)}, u32[]{:S(2)}, u32[]{:S(2)}) collective-permute-start(bf16[1280,128]{1,0:T(8,128)(2,1)S(1)} %collective-permute-done.2.refs_0_), channel_id=1, source_target_pairs={{0,4},{1,5},{2,6},{3,7},{4,8},{5,9},{6,10},{7,11},{8,12},{9,13},{1... | collective-permute-start | bytes 983048 | tf_op jit(solution)/shard_map/ppermute | solution.py:34
  16.3 1.5 %collective-permute-start.5 = (bf16[1280,128]{1,0:T(8,128)(2,1)S(1)}, bf16[1280,128]{1,0:T(8,128)(2,1)}, u32[]{:S(2)}, u32[]{:S(2)}) collective-permute-start(bf16[1280,128]{1,0:T(8,128)(2,1)S(1)} %collective-permute-done.2.refs_0_), channel_id=1, source_target_pairs={{0,2},{1,3},{2,0},{3,1},{4,6},{5,7},{6,4},{7,5},{8,10},{9,11},{10,... | collective-permute-start | bytes 983048 | tf_op jit(solution)/shard_map/ppermute | solution.py:34
  17.8 2.1 %copy.9 = bf16[32,8,32,128]{3,2,1,0:T(8,128)(2,1)S(1)} copy(bf16[32,8,32,128]{3,1,2,0:T(8,128)(2,1)} %bitcast.75) | data formatting | bytes 4194304
  19.9 3.4 %copy.10 = bf16[32,8,32,128]{3,2,1,0:T(8,128)(2,1)} copy(bf16[32,8,32,128]{3,1,2,0:T(8,128)(2,1)} %bitcast.25) | data formatting | bytes 4194304
  23.3 0.7 copy-done
  24.1 1.6 %collective-permute-start.12 = (bf16[1280,128]{1,0:T(8,128)(2,1)S(1)}, bf16[1280,128]{1,0:T(8,128)(2,1)}, u32[]{:S(2)}, u32[]{:S(2)}) collective-permute-start(bf16[1280,128]{1,0:T(8,128)(2,1)S(1)} %collective-permute-done.10.refs_1_), channel_id=1, source_target_pairs={{0,4},{1,5},{2,6},{3,7},{4,8},{5,9},{6,10},{7,11},{8,12},{9,13},{1... | collective-permute-start | bytes 983048 | tf_op jit(solution)/shard_map/ppermute | solution.py:34
  25.6 0.5 collective-permute-start.13
  26.2 0.3 convert_reduce_fusion
  26.5 0.5 select_reduce_fusion
  27.2 1.6 %collective-permute-done.4.refs_0_ = bf16[1280,128]{1,0:T(8,128)(2,1)S(1)} collective-permute-done((bf16[1280,128]{1,0:T(8,128)(2,1)S(1)}, bf16[1280,128]{1,0:T(8,128)(2,1)S(1)}, u32[]{:S(2)}, u32[]{:S(2)}) %collective-permute-start.4) | collective-permute-done | bytes 327712 | tf_op jit(solution)/shard_map/ppermute | solution.py:34
  28.9 1.6 %collective-permute-start.6 = (bf16[1280,128]{1,0:T(8,128)(2,1)S(1)}, bf16[1280,128]{1,0:T(8,128)(2,1)S(1)}, u32[]{:S(2)}, u32[]{:S(2)}) collective-permute-start(bf16[1280,128]{1,0:T(8,128)(2,1)S(1)} %collective-permute-done.4.refs_0_), channel_id=1, source_target_pairs={{0,4},{1,5},{2,6},{3,7},{4,8},{5,9},{6,10},{7,11},{8,12},{9,13},{1... | collective-permute-start | bytes 983048 | tf_op jit(solution)/shard_map/ppermute | solution.py:34
  30.5 1.5 %collective-permute-start.7 = (bf16[1280,128]{1,0:T(8,128)(2,1)S(1)}, bf16[1280,128]{1,0:T(8,128)(2,1)S(1)}, u32[]{:S(2)}, u32[]{:S(2)}) collective-permute-start(bf16[1280,128]{1,0:T(8,128)(2,1)S(1)} %collective-permute-done.4.refs_0_), channel_id=1, source_target_pairs={{0,2},{1,3},{2,0},{3,1},{4,6},{5,7},{6,4},{7,5},{8,10},{9,11},{10,... | collective-permute-start | bytes 983048 | tf_op jit(solution)/shard_map/ppermute | solution.py:34
  32.0 3.1 %shard_map.46 = (f32[41024,128]{1,0:T(8,128)S(1)}, bf16[512,32,128]{2,1,0:T(8,128)(2,1)S(1)}) custom-call(s32[1584]{0:T(1024)S(1)} %concatenate.7.table_ref, s32[6]{0:T(128)S(1)} %convert_reduce_fusion.1.bounds_ref, bf16[1280,128]{1,0:T(8,128)(2,1)} %copy-done.2, bf16[1280,128]{1,0:T(8,128)(2,1)} %copy-done.3, bf16[256,32,128]{2,1,0:T(8,128)(2,1)S(1)} %bitcast.65, ...), custom_call_target="tpu_custom_call" | custom-call | flops 107374184 | bytes 4194304 | tf_op jit(solution)/shard_map/pallas_call | solution.py:219
  35.1 1.6 %collective-permute-done.12.refs_1_ = bf16[1280,128]{1,0:T(8,128)(2,1)} collective-permute-done((bf16[1280,128]{1,0:T(8,128)(2,1)S(1)}, bf16[1280,128]{1,0:T(8,128)(2,1)}, u32[]{:S(2)}, u32[]{:S(2)}) %collective-permute-start.12) | collective-permute-done | bytes 327712 | tf_op jit(solution)/shard_map/ppermute | solution.py:34
  36.6 0.9 collective-permute-start.15
  37.5 1.5 %collective-permute-start.16 = (bf16[1280,128]{1,0:T(8,128)(2,1)}, bf16[1280,128]{1,0:T(8,128)(2,1)S(1)}, u32[]{:S(2)}, u32[]{:S(2)}) collective-permute-start(bf16[1280,128]{1,0:T(8,128)(2,1)} %collective-permute-done.12.refs_1_), channel_id=1, source_target_pairs={{0,2},{1,3},{2,0},{3,1},{4,6},{5,7},{6,4},{7,5},{8,10},{9,11},{10,... | collective-permute-start | bytes 983048 | tf_op jit(solution)/shard_map/ppermute | solution.py:34
  39.0 4.5 %collective-permute-done.6.refs_0_ = bf16[1280,128]{1,0:T(8,128)(2,1)S(1)} collective-permute-done((bf16[1280,128]{1,0:T(8,128)(2,1)S(1)}, bf16[1280,128]{1,0:T(8,128)(2,1)S(1)}, u32[]{:S(2)}, u32[]{:S(2)}) %collective-permute-start.6) | collective-permute-done | bytes 327712 | tf_op jit(solution)/shard_map/ppermute | solution.py:34
  43.5 1.9 %shard_map.47.refs_5_ = f32[41024,128]{1,0:T(8,128)S(1)} custom-call(s32[1584]{0:T(1024)S(1)} %concatenate.7.table_ref, s32[6]{0:T(128)S(1)} %convert_reduce_fusion.1.bounds_ref, bf16[1280,128]{1,0:T(8,128)(2,1)S(1)} %collective-permute-done.2.refs_0_, bf16[1280,128]{1,0:T(8,128)(2,1)S(1)} %collective-permute-done.10.refs_1_, ...), custom_call_target="tpu_custom_call", output_to_operand_aliasing={{}: (7, {})} | custom-call | flops 107374184 | bytes 4194304 | tf_op jit(solution)/shard_map/pallas_call | solution.py:219
  45.5 2.1 %collective-permute-start.14 = (bf16[1280,128]{1,0:T(8,128)(2,1)S(1)}, bf16[1280,128]{1,0:T(8,128)(2,1)S(1)}, u32[]{:S(2)}, u32[]{:S(2)}) collective-permute-start(bf16[1280,128]{1,0:T(8,128)(2,1)S(1)} %collective-permute-done.7.refs_2_), channel_id=1, source_target_pairs={{0,4},{1,5},{2,6},{3,7},{4,8},{5,9},{6,10},{7,11},{8,12},{9,13},{1... | collective-permute-start | bytes 983048 | tf_op jit(solution)/shard_map/ppermute | solution.py:34
  47.6 3.0 %collective-permute-done.15.refs_1_ = bf16[1280,128]{1,0:T(8,128)(2,1)S(1)} collective-permute-done((bf16[1280,128]{1,0:T(8,128)(2,1)}, bf16[1280,128]{1,0:T(8,128)(2,1)S(1)}, u32[]{:S(2)}, u32[]{:S(2)}) %collective-permute-start.15) | collective-permute-done | bytes 327712 | tf_op jit(solution)/shard_map/ppermute | solution.py:34
  50.6 0.7 collective-permute-start.17
  51.2 2.8 %shard_map.48.refs_5_ = f32[41024,128]{1,0:T(8,128)S(1)} custom-call(s32[1584]{0:T(1024)S(1)} %concatenate.7.table_ref, s32[6]{0:T(128)S(1)} %convert_reduce_fusion.1.bounds_ref, bf16[1280,128]{1,0:T(8,128)(2,1)S(1)} %collective-permute-done.4.refs_0_, bf16[1280,128]{1,0:T(8,128)(2,1)} %collective-permute-done.12.refs_1_, ...), custom_call_target="tpu_custom_call", output_to_operand_aliasing={{}: (7, {})} | custom-call | flops 107374184 | bytes 4194304 | tf_op jit(solution)/shard_map/pallas_call | solution.py:219
  54.0 1.7 %shard_map.49.refs_3_ = f32[41024,128]{1,0:T(8,128)S(1)} custom-call(s32[1584]{0:T(1024)S(1)} %concatenate.7.table_ref, s32[6]{0:T(128)S(1)} %convert_reduce_fusion.1.bounds_ref, bf16[1280,128]{1,0:T(8,128)(2,1)S(1)} %collective-permute-done.6.refs_0_, bf16[1280,128]{1,0:T(8,128)(2,1)S(1)} %collective-permute-done.15.refs_1_, ...), custom_call_target="tpu_custom_call", output_to_operand_aliasing={{}: (7, {})} | custom-call | flops 107374184 | bytes 4194304 | tf_op jit(solution)/shard_map/pallas_call | solution.py:219
  55.7 1.0 collective-permute-done.14.refs_0_
  56.8 2.1 %collective-permute-done.17.refs_1_ = bf16[1280,128]{1,0:T(8,128)(2,1)S(1)} collective-permute-done((bf16[1280,128]{1,0:T(8,128)(2,1)S(1)}, bf16[1280,128]{1,0:T(8,128)(2,1)S(1)}, u32[]{:S(2)}, u32[]{:S(2)}) %collective-permute-start.17) | collective-permute-done | bytes 327712 | tf_op jit(solution)/shard_map/ppermute | solution.py:34
  58.9 2.1 %shard_map.50 = (f32[41024,128]{1,0:T(8,128)S(1)}, bf16[256,128]{1,0:T(8,128)(2,1)S(1)}, bf16[1,1280,128]{2,1,0:T(8,128)(2,1)S(1)}, bf16[1,1280,128]{2,1,0:T(8,1...) custom-call(s32[1584]{0:T(1024)S(1)} %concatenate.7.table_ref, ...), custom_call_target="tpu_custom_call", output_to_operand_aliasing={{0}: (7, {})} | custom-call | flops 442918496 | bytes 4194304 | tf_op jit(solution)/shard_map/pallas_call | solution.py:219
  61.1 0.5 collective-permute-start.23
  61.7 1.4 %shard_map.51 = (f32[1,1280,128]{2,1,0:T(8,128)S(1)}, f32[1,1280,128]{2,1,0:T(8,128)S(1)}, f32[1,1280,128]{2,1,0:T(8,128)S(1)}, f32[1,1280,128]{2,1,0:T(8,128)S(1)}) custom-call(s32[8]{0:T(128)S(1)} %fusion.33.chips_ref, s32[1]{0:T(128)} %bitcast.core_ref, f32[41024,128]{1,0:T(8,128)S(1)} %get-tuple-element.90.half, ...), custom_call_target="tpu_custom_call" | custom-call | flops 335544320 | bytes 4194304 | tf_op jit(solution)/shard_map/pallas_call | solution.py:219
  63.1 0.1 collective-permute-done.23
  63.2 0.1 fusion.4
  63.4 0.3 collective-permute-done.18
  63.8 2.1 %collective-permute-start.24 = (bf16[1280,128]{1,0:T(8,128)(2,1)S(1)}, bf16[1280,128]{1,0:T(8,128)(2,1)S(1)}, u32[]{:S(2)}, u32[]{:S(2)}) collective-permute-start(bf16[1280,128]{1,0:T(8,128)(2,1)S(1)} %fusion.15), channel_id=1, source_target_pairs={{0,2},{1,3},{2,0},{3,1},{4,6},{5,7},{6,4},{7,5},{8,10},{9,11},{10,... | collective-permute-start | bytes 983048 | tf_op jit(solution)/shard_map/ppermute | solution.py:34
  65.8 0.9 collective-permute-start.25
  66.7 1.4 %shard_map.53 = (bf16[1,1280,128]{2,1,0:T(8,128)(2,1)S(1)}, bf16[1,1280,128]{2,1,0:T(8,128)(2,1)S(1)}, bf16[1,1280,128]{2,1,0:T(8,128)(2,1)S(1)}, bf16[1,1280,128]{2,1,0:T(8,128)(2,1)S(1)}) custom-call(s32[8]{0:T(128)S(1)} %fusion.33.chips_ref, s32[1]{0:T(128)} %bitcast.core_ref, f32[41024,128]{1,0:T(8,128)S(1)} %get-tuple-element.90.half, ...), custom_call_target="tpu_custom_call" | custom-call | flops 335544320 | bytes 4194304 | tf_op jit(solution)/shard_map/pallas_call | solution.py:219
  68.1 0.3 collective-permute-start.21
  68.4 0.3 collective-permute-start.29
  68.7 1.4 %shard_map.52 = (f32[1,1280,128]{2,1,0:T(8,128)S(1)}, f32[1,1280,128]{2,1,0:T(8,128)S(1)}, f32[1,1280,128]{2,1,0:T(8,128)S(1)}, f32[1,1280,128]{2,1,0:T(8,128)S(1)}) custom-call(s32[8]{0:T(128)S(1)} %fusion.33.chips_ref, s32[1]{0:T(128)} %bitcast.core_ref, f32[41024,128]{1,0:T(8,128)S(1)} %get-tuple-element.90.half, ...), custom_call_target="tpu_custom_call" | custom-call | flops 335544320 | bytes 4194304 | tf_op jit(solution)/shard_map/pallas_call | solution.py:219
  70.1 4.2 %collective-permute-done.25 = bf16[640,128]{1,0:T(8,128)(2,1)S(1)} collective-permute-done((bf16[640,128]{1,0:T(8,128)(2,1)S(1)}, bf16[640,128]{1,0:T(8,128)(2,1)S(1)}, u32[]{:S(2)}, u32[]{:S(2)}) %collective-permute-start.25) | collective-permute-done | bytes 163872 | tf_op jit(solution)/shard_map/ppermute | solution.py:34
  74.3 0.5 collective-permute-start.20
  74.9 0.3 collective-permute-start.26
  75.2 1.5 %collective-permute-start.27 = (bf16[640,128]{1,0:T(8,128)(2,1)S(1)}, bf16[640,128]{1,0:T(8,128)(2,1)S(1)}, u32[]{:S(2)}, u32[]{:S(2)}) collective-permute-start(bf16[640,128]{1,0:T(8,128)(2,1)S(1)} %get-tuple-element.105), channel_id=1, source_target_pairs={{0,2},{1,3},{2,0},{3,1},{4,6},{5,7},{6,4},{7,5},{8,10},{9,11},{10,... | collective-permute-start | bytes 491528 | tf_op jit(solution)/shard_map/ppermute | solution.py:34
  76.7 0.6 collective-permute-start.30
  77.3 4.9 %collective-permute-done.27 = bf16[640,128]{1,0:T(8,128)(2,1)S(1)} collective-permute-done((bf16[640,128]{1,0:T(8,128)(2,1)S(1)}, bf16[640,128]{1,0:T(8,128)(2,1)S(1)}, u32[]{:S(2)}, u32[]{:S(2)}) %collective-permute-start.27) | collective-permute-done | bytes 163872 | tf_op jit(solution)/shard_map/ppermute | solution.py:34
  82.2 4.2 %collective-permute-done.26 = bf16[1280,128]{1,0:T(8,128)(2,1)S(1)} collective-permute-done((bf16[1280,128]{1,0:T(8,128)(2,1)S(1)}, bf16[1280,128]{1,0:T(8,128)(2,1)S(1)}, u32[]{:S(2)}, u32[]{:S(2)}) %collective-permute-start.26) | collective-permute-done | bytes 327712 | tf_op jit(solution)/shard_map/ppermute | solution.py:34
  86.4 0.1 fusion.9
  86.6 1.9 %collective-permute-done.30 = bf16[1280,128]{1,0:T(8,128)(2,1)S(1)} collective-permute-done((bf16[1280,128]{1,0:T(8,128)(2,1)S(1)}, bf16[1280,128]{1,0:T(8,128)(2,1)S(1)}, u32[]{:S(2)}, u32[]{:S(2)}) %collective-permute-start.30) | collective-permute-done | bytes 327712 | tf_op jit(solution)/shard_map/ppermute | solution.py:34
  88.5 0.1 fusion.3
  88.7 3.1 %collective-permute-start.33 = (bf16[1280,128]{1,0:T(8,128)(2,1)S(1)}, bf16[1280,128]{1,0:T(8,128)(2,1)S(1)}, u32[]{:S(2)}, u32[]{:S(2)}) collective-permute-start(bf16[1280,128]{1,0:T(8,128)(2,1)S(1)} %fusion.3), channel_id=1, source_target_pairs={{0,12},{1,13},{2,14},{3,15},{4,0},{5,1},{6,2},{7,3},{8,4},{9,5},{1... | collective-permute-start | bytes 983048 | tf_op jit(solution)/shard_map/ppermute | solution.py:34
  91.8 1.3 %collective-permute-start.31 = (bf16[1280,128]{1,0:T(8,128)(2,1)S(1)}, bf16[1280,128]{1,0:T(8,128)(2,1)S(1)}, u32[]{:S(2)}, u32[]{:S(2)}) collective-permute-start(bf16[1280,128]{1,0:T(8,128)(2,1)S(1)} %add_convert_fusion), channel_id=1, source_target_pairs={{0,2},{1,3},{2,0},{3,1},{4,6},{5,7},{6,4},{7,5},{8,10},{9,11},{10,... | collective-permute-start | bytes 983048 | tf_op jit(solution)/shard_map/ppermute | solution.py:34
  93.1 5.9 %collective-permute-done.28 = bf16[1280,128]{1,0:T(8,128)(2,1)S(1)} collective-permute-done((bf16[1280,128]{1,0:T(8,128)(2,1)S(1)}, bf16[1280,128]{1,0:T(8,128)(2,1)S(1)}, u32[]{:S(2)}, u32[]{:S(2)}) %collective-permute-start.28) | collective-permute-done | bytes 327712 | tf_op jit(solution)/shard_map/ppermute | solution.py:34
  99.1 5.1 %collective-permute-done.33 = bf16[1280,128]{1,0:T(8,128)(2,1)S(1)} collective-permute-done((bf16[1280,128]{1,0:T(8,128)(2,1)S(1)}, bf16[1280,128]{1,0:T(8,128)(2,1)S(1)}, u32[]{:S(2)}, u32[]{:S(2)}) %collective-permute-start.33) | collective-permute-done | bytes 327712 | tf_op jit(solution)/shard_map/ppermute | solution.py:34
  104.2 1.0 fusion.13
  (43 shorter events, 1.0 us)
Async XLA Ops:
  0.0 9.3 %collective-permute-start.9 = (bf16[256,4096]{1,0:T(8,128)(2,1)}, bf16[256,4096]{1,0:T(8,128)(2,1)}, u32[]{:S(2)}, u32[]{:S(2)}) collective-permute-start(bf16[256,4096]{1,0:T(8,128)(2,1)} %param.4), channel_id=1, source_target_pairs={{0,1},{1,0},{2,3},{3,2},{4,5},{5,4},{6,7},{7,6},{8,9},{9,8},{10,11... | collective-permute-start | bytes 6291464 | tf_op jit(solution)/shard_map/ppermute | solution.py:34
  1.6 13.2 %copy-start.2 = (bf16[1280,128]{1,0:T(8,128)(2,1)}, bf16[1280,128]{1,0:T(8,128)(2,1)S(1)}, u32[]{:S(2)}) copy-start(bf16[1280,128]{1,0:T(8,128)(2,1)S(1)} %get-tuple-element.123.refs_0_) | copy-start | bytes 983044
  1.6 13.2 %collective-permute-start.2 = (bf16[1280,128]{1,0:T(8,128)(2,1)S(1)}, bf16[1280,128]{1,0:T(8,128)(2,1)S(1)}, u32[]{:S(2)}, u32[]{:S(2)}) collective-permute-start(bf16[1280,128]{1,0:T(8,128)(2,1)S(1)} %get-tuple-element.123.refs_0_), channel_id=1, source_target_pairs={{0,4},{1,5},{2,6},{3,7},{4,8},{5,9},{6,10},{7,11},{8,12},{9,13},{1... | collective-permute-start | bytes 983048 | tf_op jit(solution)/shard_map/ppermute | solution.py:34
  4.2 10.6 %collective-permute-start.3 = (bf16[1280,128]{1,0:T(8,128)(2,1)S(1)}, bf16[1280,128]{1,0:T(8,128)(2,1)S(1)}, u32[]{:S(2)}, u32[]{:S(2)}) collective-permute-start(bf16[1280,128]{1,0:T(8,128)(2,1)S(1)} %get-tuple-element.123.refs_0_), channel_id=1, source_target_pairs={{0,2},{1,3},{2,0},{3,1},{4,6},{5,7},{6,4},{7,5},{8,10},{9,11},{10,... | collective-permute-start | bytes 983048 | tf_op jit(solution)/shard_map/ppermute | solution.py:34
  5.7 1.9 %collective-permute-start.1 = (s32[256,2]{0,1:T(2,128)}, s32[256,2]{0,1:T(2,128)S(1)}, u32[]{:S(2)}, u32[]{:S(2)}) collective-permute-start(s32[256,2]{0,1:T(2,128)} %param.5), channel_id=1, source_target_pairs={{0,1},{1,0},{2,3},{3,2},{4,5},{5,4},{6,7},{7,6},{8,9},{9,8},{10,11... | collective-permute-start | bytes 6152 | tf_op jit(solution)/shard_map/ppermute | solution.py:34
  5.7 2.0 %collective-permute-start = (s32[1]{0:T(128)}, s32[1]{0:T(128)}, u32[]{:S(2)}, u32[]{:S(2)}) collective-permute-start(s32[1]{0:T(128)} %param.6), channel_id=1, source_target_pairs={{0,1},{1,0},{2,3},{3,2},{4,5},{5,4},{6,7},{7,6},{8,9},{9,8},{10,11... | collective-permute-start | bytes 20 | tf_op jit(solution)/shard_map/ppermute | solution.py:34
  7.6 1.7 %collective-permute-start.8 = (bf16[1280,128]{1,0:T(8,128)(2,1)S(1)}, bf16[1280,128]{1,0:T(8,128)(2,1)S(1)}, u32[]{:S(2)}, u32[]{:S(2)}) collective-permute-start(bf16[1280,128]{1,0:T(8,128)(2,1)S(1)} %get-tuple-element.122), channel_id=1, source_target_pairs={{0,1},{1,0},{2,3},{3,2},{4,5},{5,4},{6,7},{7,6},{8,9},{9,8},{10,11... | collective-permute-start | bytes 983048 | tf_op jit(solution)/shard_map/ppermute | solution.py:34
  9.3 10.6 %copy-start.3 = (bf16[1280,128]{1,0:T(8,128)(2,1)}, bf16[1280,128]{1,0:T(8,128)(2,1)S(1)}, u32[]{:S(2)}) copy-start(bf16[1280,128]{1,0:T(8,128)(2,1)S(1)} %collective-permute-done.8.refs_1_) | copy-start | bytes 983044
  9.3 14.1 %collective-permute-start.10 = (bf16[1280,128]{1,0:T(8,128)(2,1)S(1)}, bf16[1280,128]{1,0:T(8,128)(2,1)S(1)}, u32[]{:S(2)}, u32[]{:S(2)}) collective-permute-start(bf16[1280,128]{1,0:T(8,128)(2,1)S(1)} %collective-permute-done.8.refs_1_), channel_id=1, source_target_pairs={{0,4},{1,5},{2,6},{3,7},{4,8},{5,9},{6,10},{7,11},{8,12},{9,13},{1... | collective-permute-start | bytes 983048 | tf_op jit(solution)/shard_map/ppermute | solution.py:34
  10.9 12.5 %collective-permute-start.11 = (bf16[1280,128]{1,0:T(8,128)(2,1)S(1)}, bf16[1280,128]{1,0:T(8,128)(2,1)S(1)}, u32[]{:S(2)}, u32[]{:S(2)}) collective-permute-start(bf16[1280,128]{1,0:T(8,128)(2,1)S(1)} %collective-permute-done.8.refs_1_), channel_id=1, source_target_pairs={{0,2},{1,3},{2,0},{3,1},{4,6},{5,7},{6,4},{7,5},{8,10},{9,11},{10,... | collective-permute-start | bytes 983048 | tf_op jit(solution)/shard_map/ppermute | solution.py:34
  14.8 14.0 %collective-permute-start.4 = (bf16[1280,128]{1,0:T(8,128)(2,1)S(1)}, bf16[1280,128]{1,0:T(8,128)(2,1)S(1)}, u32[]{:S(2)}, u32[]{:S(2)}) collective-permute-start(bf16[1280,128]{1,0:T(8,128)(2,1)S(1)} %collective-permute-done.2.refs_0_), channel_id=1, source_target_pairs={{0,4},{1,5},{2,6},{3,7},{4,8},{5,9},{6,10},{7,11},{8,12},{9,13},{1... | collective-permute-start | bytes 983048 | tf_op jit(solution)/shard_map/ppermute | solution.py:34
  16.3 12.6 %collective-permute-start.5 = (bf16[1280,128]{1,0:T(8,128)(2,1)S(1)}, bf16[1280,128]{1,0:T(8,128)(2,1)}, u32[]{:S(2)}, u32[]{:S(2)}) collective-permute-start(bf16[1280,128]{1,0:T(8,128)(2,1)S(1)} %collective-permute-done.2.refs_0_), channel_id=1, source_target_pairs={{0,2},{1,3},{2,0},{3,1},{4,6},{5,7},{6,4},{7,5},{8,10},{9,11},{10,... | collective-permute-start | bytes 983048 | tf_op jit(solution)/shard_map/ppermute | solution.py:34
  23.3 0.7 copy-start
  24.1 12.6 %collective-permute-start.12 = (bf16[1280,128]{1,0:T(8,128)(2,1)S(1)}, bf16[1280,128]{1,0:T(8,128)(2,1)}, u32[]{:S(2)}, u32[]{:S(2)}) collective-permute-start(bf16[1280,128]{1,0:T(8,128)(2,1)S(1)} %collective-permute-done.10.refs_1_), channel_id=1, source_target_pairs={{0,4},{1,5},{2,6},{3,7},{4,8},{5,9},{6,10},{7,11},{8,12},{9,13},{1... | collective-permute-start | bytes 983048 | tf_op jit(solution)/shard_map/ppermute | solution.py:34
  25.6 11.0 %collective-permute-start.13 = (bf16[1280,128]{1,0:T(8,128)(2,1)S(1)}, bf16[1280,128]{1,0:T(8,128)(2,1)}, u32[]{:S(2)}, u32[]{:S(2)}) collective-permute-start(bf16[1280,128]{1,0:T(8,128)(2,1)S(1)} %collective-permute-done.10.refs_1_), channel_id=1, source_target_pairs={{0,2},{1,3},{2,0},{3,1},{4,6},{5,7},{6,4},{7,5},{8,10},{9,11},{10,... | collective-permute-start | bytes 983048 | tf_op jit(solution)/shard_map/ppermute | solution.py:34
  27.2 16.3 %copy-start.1 = (bf16[1280,128]{1,0:T(8,128)(2,1)S(1)}, bf16[1280,128]{1,0:T(8,128)(2,1)}, u32[]{:S(2)}) copy-start(bf16[1280,128]{1,0:T(8,128)(2,1)} %copy-done) | copy-start | bytes 983044
  28.9 14.6 %collective-permute-start.6 = (bf16[1280,128]{1,0:T(8,128)(2,1)S(1)}, bf16[1280,128]{1,0:T(8,128)(2,1)S(1)}, u32[]{:S(2)}, u32[]{:S(2)}) collective-permute-start(bf16[1280,128]{1,0:T(8,128)(2,1)S(1)} %collective-permute-done.4.refs_0_), channel_id=1, source_target_pairs={{0,4},{1,5},{2,6},{3,7},{4,8},{5,9},{6,10},{7,11},{8,12},{9,13},{1... | collective-permute-start | bytes 983048 | tf_op jit(solution)/shard_map/ppermute | solution.py:34
  30.5 13.1 %collective-permute-start.7 = (bf16[1280,128]{1,0:T(8,128)(2,1)S(1)}, bf16[1280,128]{1,0:T(8,128)(2,1)S(1)}, u32[]{:S(2)}, u32[]{:S(2)}) collective-permute-start(bf16[1280,128]{1,0:T(8,128)(2,1)S(1)} %collective-permute-done.4.refs_0_), channel_id=1, source_target_pairs={{0,2},{1,3},{2,0},{3,1},{4,6},{5,7},{6,4},{7,5},{8,10},{9,11},{10,... | collective-permute-start | bytes 983048 | tf_op jit(solution)/shard_map/ppermute | solution.py:34
  36.6 13.9 %collective-permute-start.15 = (bf16[1280,128]{1,0:T(8,128)(2,1)}, bf16[1280,128]{1,0:T(8,128)(2,1)S(1)}, u32[]{:S(2)}, u32[]{:S(2)}) collective-permute-start(bf16[1280,128]{1,0:T(8,128)(2,1)} %collective-permute-done.12.refs_1_), channel_id=1, source_target_pairs={{0,4},{1,5},{2,6},{3,7},{4,8},{5,9},{6,10},{7,11},{8,12},{9,13},{1... | collective-permute-start | bytes 983048 | tf_op jit(solution)/shard_map/ppermute | solution.py:34
  37.5 13.1 %collective-permute-start.16 = (bf16[1280,128]{1,0:T(8,128)(2,1)}, bf16[1280,128]{1,0:T(8,128)(2,1)S(1)}, u32[]{:S(2)}, u32[]{:S(2)}) collective-permute-start(bf16[1280,128]{1,0:T(8,128)(2,1)} %collective-permute-done.12.refs_1_), channel_id=1, source_target_pairs={{0,2},{1,3},{2,0},{3,1},{4,6},{5,7},{6,4},{7,5},{8,10},{9,11},{10,... | collective-permute-start | bytes 983048 | tf_op jit(solution)/shard_map/ppermute | solution.py:34
  45.5 11.2 %collective-permute-start.14 = (bf16[1280,128]{1,0:T(8,128)(2,1)S(1)}, bf16[1280,128]{1,0:T(8,128)(2,1)S(1)}, u32[]{:S(2)}, u32[]{:S(2)}) collective-permute-start(bf16[1280,128]{1,0:T(8,128)(2,1)S(1)} %collective-permute-done.7.refs_2_), channel_id=1, source_target_pairs={{0,4},{1,5},{2,6},{3,7},{4,8},{5,9},{6,10},{7,11},{8,12},{9,13},{1... | collective-permute-start | bytes 983048 | tf_op jit(solution)/shard_map/ppermute | solution.py:34
  50.6 8.3 %collective-permute-start.17 = (bf16[1280,128]{1,0:T(8,128)(2,1)S(1)}, bf16[1280,128]{1,0:T(8,128)(2,1)S(1)}, u32[]{:S(2)}, u32[]{:S(2)}) collective-permute-start(bf16[1280,128]{1,0:T(8,128)(2,1)S(1)} %collective-permute-done.15.refs_1_), channel_id=1, source_target_pairs={{0,2},{1,3},{2,0},{3,1},{4,6},{5,7},{6,4},{7,5},{8,10},{9,11},{10,... | collective-permute-start | bytes 983048 | tf_op jit(solution)/shard_map/ppermute | solution.py:34
  61.0 2.0 %collective-permute-start.19 = (bf16[1280,128]{1,0:T(8,128)(2,1)S(1)}, bf16[1280,128]{1,0:T(8,128)(2,1)S(1)}, u32[]{:S(2)}, u32[]{:S(2)}) collective-permute-start(bf16[1280,128]{1,0:T(8,128)(2,1)S(1)} %bitcast.73), channel_id=1, source_target_pairs={{0,1},{1,0},{2,3},{3,2},{4,5},{5,4},{6,7},{7,6},{8,9},{9,8},{10,11... | collective-permute-start | bytes 983048 | tf_op jit(solution)/shard_map/ppermute | solution.py:34
  61.1 2.1 %collective-permute-start.23 = (bf16[1280,128]{1,0:T(8,128)(2,1)S(1)}, bf16[1280,128]{1,0:T(8,128)(2,1)S(1)}, u32[]{:S(2)}, u32[]{:S(2)}) collective-permute-start(bf16[1280,128]{1,0:T(8,128)(2,1)S(1)} %bitcast.72), channel_id=1, source_target_pairs={{0,1},{1,0},{2,3},{3,2},{4,5},{5,4},{6,7},{7,6},{8,9},{9,8},{10,11... | collective-permute-start | bytes 983048 | tf_op jit(solution)/shard_map/ppermute | solution.py:34
  61.6 2.1 %collective-permute-start.18 = (bf16[1280,128]{1,0:T(8,128)(2,1)S(1)}, bf16[1280,128]{1,0:T(8,128)(2,1)S(1)}, u32[]{:S(2)}, u32[]{:S(2)}) collective-permute-start(bf16[1280,128]{1,0:T(8,128)(2,1)S(1)} %bitcast.71), channel_id=1, source_target_pairs={{0,1},{1,0},{2,3},{3,2},{4,5},{5,4},{6,7},{7,6},{8,9},{9,8},{10,11... | collective-permute-start | bytes 983048 | tf_op jit(solution)/shard_map/ppermute | solution.py:34
  63.8 10.5 %collective-permute-start.24 = (bf16[1280,128]{1,0:T(8,128)(2,1)S(1)}, bf16[1280,128]{1,0:T(8,128)(2,1)S(1)}, u32[]{:S(2)}, u32[]{:S(2)}) collective-permute-start(bf16[1280,128]{1,0:T(8,128)(2,1)S(1)} %fusion.15), channel_id=1, source_target_pairs={{0,2},{1,3},{2,0},{3,1},{4,6},{5,7},{6,4},{7,5},{8,10},{9,11},{10,... | collective-permute-start | bytes 983048 | tf_op jit(solution)/shard_map/ppermute | solution.py:34
  65.8 8.9 %collective-permute-start.22 = (bf16[1280,128]{1,0:T(8,128)(2,1)S(1)}, bf16[1280,128]{1,0:T(8,128)(2,1)S(1)}, u32[]{:S(2)}, u32[]{:S(2)}) collective-permute-start(bf16[1280,128]{1,0:T(8,128)(2,1)S(1)} %bitcast.67), channel_id=1, source_target_pairs={{0,1},{1,0},{2,3},{3,2},{4,5},{5,4},{6,7},{7,6},{8,9},{9,8},{10,11... | collective-permute-start | bytes 983048 | tf_op jit(solution)/shard_map/ppermute | solution.py:34
  65.8 8.4 %collective-permute-start.25 = (bf16[640,128]{1,0:T(8,128)(2,1)S(1)}, bf16[640,128]{1,0:T(8,128)(2,1)S(1)}, u32[]{:S(2)}, u32[]{:S(2)}) collective-permute-start(bf16[640,128]{1,0:T(8,128)(2,1)S(1)} %get-tuple-element.101), channel_id=1, source_target_pairs={{0,4},{1,5},{2,6},{3,7},{4,8},{5,9},{6,10},{7,11},{8,12},{9,13},{1... | collective-permute-start | bytes 491528 | tf_op jit(solution)/shard_map/ppermute | solution.py:34
  68.1 8.6 %collective-permute-start.21 = (bf16[1280,128]{1,0:T(8,128)(2,1)S(1)}, bf16[1280,128]{1,0:T(8,128)(2,1)S(1)}, u32[]{:S(2)}, u32[]{:S(2)}) collective-permute-start(bf16[1280,128]{1,0:T(8,128)(2,1)S(1)} %bitcast.69), channel_id=1, source_target_pairs={{0,1},{1,0},{2,3},{3,2},{4,5},{5,4},{6,7},{7,6},{8,9},{9,8},{10,11... | collective-permute-start | bytes 983048 | tf_op jit(solution)/shard_map/ppermute | solution.py:34
  68.4 6.8 %collective-permute-start.29 = (bf16[1280,128]{1,0:T(8,128)(2,1)S(1)}, bf16[1280,128]{1,0:T(8,128)(2,1)S(1)}, u32[]{:S(2)}, u32[]{:S(2)}) collective-permute-start(bf16[1280,128]{1,0:T(8,128)(2,1)S(1)} %bitcast.70), channel_id=1, source_target_pairs={{0,1},{1,0},{2,3},{3,2},{4,5},{5,4},{6,7},{7,6},{8,9},{9,8},{10,11... | collective-permute-start | bytes 983048 | tf_op jit(solution)/shard_map/ppermute | solution.py:34
  74.3 14.3 %collective-permute-start.32 = (bf16[1280,128]{1,0:T(8,128)(2,1)S(1)}, bf16[1280,128]{1,0:T(8,128)(2,1)S(1)}, u32[]{:S(2)}, u32[]{:S(2)}) collective-permute-start(bf16[1280,128]{1,0:T(8,128)(2,1)S(1)} %bitcast.68), channel_id=1, source_target_pairs={{0,1},{1,0},{2,3},{3,2},{4,5},{5,4},{6,7},{7,6},{8,9},{9,8},{10,11... | collective-permute-start | bytes 983048 | tf_op jit(solution)/shard_map/ppermute | solution.py:34
  74.3 18.9 %collective-permute-start.20 = (bf16[1280,128]{1,0:T(8,128)(2,1)S(1)}, bf16[1280,128]{1,0:T(8,128)(2,1)S(1)}, u32[]{:S(2)}, u32[]{:S(2)}) collective-permute-start(bf16[1280,128]{1,0:T(8,128)(2,1)S(1)} %bitcast.66), channel_id=1, source_target_pairs={{0,1},{1,0},{2,3},{3,2},{4,5},{5,4},{6,7},{7,6},{8,9},{9,8},{10,11... | collective-permute-start | bytes 983048 | tf_op jit(solution)/shard_map/ppermute | solution.py:34
  74.9 11.5 %collective-permute-start.26 = (bf16[1280,128]{1,0:T(8,128)(2,1)S(1)}, bf16[1280,128]{1,0:T(8,128)(2,1)S(1)}, u32[]{:S(2)}, u32[]{:S(2)}) collective-permute-start(bf16[1280,128]{1,0:T(8,128)(2,1)S(1)} %fusion.6), channel_id=1, source_target_pairs={{0,4},{1,5},{2,6},{3,7},{4,8},{5,9},{6,10},{7,11},{8,12},{9,13},{1... | collective-permute-start | bytes 983048 | tf_op jit(solution)/shard_map/ppermute | solution.py:34
  75.2 7.0 %collective-permute-start.27 = (bf16[640,128]{1,0:T(8,128)(2,1)S(1)}, bf16[640,128]{1,0:T(8,128)(2,1)S(1)}, u32[]{:S(2)}, u32[]{:S(2)}) collective-permute-start(bf16[640,128]{1,0:T(8,128)(2,1)S(1)} %get-tuple-element.105), channel_id=1, source_target_pairs={{0,2},{1,3},{2,0},{3,1},{4,6},{5,7},{6,4},{7,5},{8,10},{9,11},{10,... | collective-permute-start | bytes 491528 | tf_op jit(solution)/shard_map/ppermute | solution.py:34
  76.7 11.8 %collective-permute-start.30 = (bf16[1280,128]{1,0:T(8,128)(2,1)S(1)}, bf16[1280,128]{1,0:T(8,128)(2,1)S(1)}, u32[]{:S(2)}, u32[]{:S(2)}) collective-permute-start(bf16[1280,128]{1,0:T(8,128)(2,1)S(1)} %get-tuple-element.110), channel_id=1, source_target_pairs={{0,2},{1,3},{2,0},{3,1},{4,6},{5,7},{6,4},{7,5},{8,10},{9,11},{10,... | collective-permute-start | bytes 983048 | tf_op jit(solution)/shard_map/ppermute | solution.py:34
  86.5 12.5 %collective-permute-start.28 = (bf16[1280,128]{1,0:T(8,128)(2,1)S(1)}, bf16[1280,128]{1,0:T(8,128)(2,1)S(1)}, u32[]{:S(2)}, u32[]{:S(2)}) collective-permute-start(bf16[1280,128]{1,0:T(8,128)(2,1)S(1)} %fusion.9), channel_id=1, source_target_pairs={{0,4},{1,5},{2,6},{3,7},{4,8},{5,9},{6,10},{7,11},{8,12},{9,13},{1... | collective-permute-start | bytes 983048 | tf_op jit(solution)/shard_map/ppermute | solution.py:34
  88.7 15.5 %collective-permute-start.33 = (bf16[1280,128]{1,0:T(8,128)(2,1)S(1)}, bf16[1280,128]{1,0:T(8,128)(2,1)S(1)}, u32[]{:S(2)}, u32[]{:S(2)}) collective-permute-start(bf16[1280,128]{1,0:T(8,128)(2,1)S(1)} %fusion.3), channel_id=1, source_target_pairs={{0,12},{1,13},{2,14},{3,15},{4,0},{5,1},{6,2},{7,3},{8,4},{9,5},{1... | collective-permute-start | bytes 983048 | tf_op jit(solution)/shard_map/ppermute | solution.py:34
  91.8 12.3 %collective-permute-start.31 = (bf16[1280,128]{1,0:T(8,128)(2,1)S(1)}, bf16[1280,128]{1,0:T(8,128)(2,1)S(1)}, u32[]{:S(2)}, u32[]{:S(2)}) collective-permute-start(bf16[1280,128]{1,0:T(8,128)(2,1)S(1)} %add_convert_fusion), channel_id=1, source_target_pairs={{0,2},{1,3},{2,0},{3,1},{4,6},{5,7},{6,4},{7,5},{8,10},{9,11},{10,... | collective-permute-start | bytes 983048 | tf_op jit(solution)/shard_map/ppermute | solution.py:34

commit v21 on v20

--- a/solution.py
+++ b/solution.py
@@ -92,15 +92,19 @@
     beside = move(beside, ACROSS)
     three_on, two_on = tie(narrow(total[FAR3]), two_on)
     three_on = move(three_on, ACROSS)
-    two_on = move(narrow(total[NEAR2] + wide(two_on)), ALONG)
-    rows = beside.shape[0]
-    beside, joining = jnp.pad(wide(beside), ((rows, 0), (0, 0))), jnp.pad(wide(joining), ((0, rows), (0, 0)))
-    one_on = move(narrow(total[NEAR1] + wide(two_on) + beside), ALONG)
-    total[FAR0], two_on = tie(total[FAR0], two_on)
+    two_on = [move(narrow(own + wide(part)), ALONG) for own, part in zip(halves(total[NEAR2]), halves(two_on))]
+    two_on[1], three_on = tie(two_on[1], three_on)
+    later, two_on[0] = tie(total[NEAR1], two_on[0])
+    one_on = [
+        move(narrow(halves(total[NEAR1])[0] + wide(two_on[0])), ALONG),
+        move(narrow(halves(later)[1] + wide(two_on[1]) + wide(beside)), ALONG),
+    ]
+    joining = jnp.pad(wide(joining), ((0, joining.shape[0]), (0, 0)))
+    total[FAR0], two_on[0] = tie(total[FAR0], two_on[0])
     crossing, three_on = tie(narrow(total[FAR0] + joining), three_on)
     straight = move(crossing, ACROSS)
     one_back = move(narrow(total[NEAR3] + wide(three_on)), BACK)
-    return total[NEAR0] + wide(one_on) + wide(straight) + wide(one_back)
+    return total[NEAR0] + wide(jnp.concatenate(one_on)) + wide(straight) + wide(one_back)
 
 
 def clear(half):

time: 106 us -> 105 us (level)
  waiting for transfers between devices: 44.2 us -> 41 us
  starting transfers between devices: 32.2 us -> 33.8 us
  Pallas kernels: 15.7 us -> 17.2 us
    ppermute x34 -> x36, waiting for transfers between devices: 44.2 us -> 41 us  [move(): return lax.ppermute(array, 'aux', pairs)]
    ppermute x34 -> x36, starting transfers between devices: 32.2 us -> 33.8 us  [move(): return lax.ppermute(array, 'aux', pairs)]
    pallas_call x8, Pallas kernels: 15.7 us -> 17.2 us  [call(): pl.pallas_call(kernel, out_shape=outs, in_specs=in_specs, out_specs=[VMEM...]
  transfers between devices with their start and end apart: 34 -> 36, of which waited for: 17 -> 15; matrix products, arithmetic and copies ran while one was open for 10% -> 10% of each run, Pallas kernels for 13% -> 14%
where the time goes in v21:
time: 105 us
  waiting for transfers between devices  41 us (39%)
  starting transfers between devices  33.8 us (32%)
  Pallas kernels  17.2 us (16%)
  local copies, waits for them, and re-layouts  8.14 us (8%)
  other arithmetic  4.06 us (4%)
    ppermute x36, waiting for transfers between devices, move(): return lax.ppermute(array, 'aux', pairs)  41 us
    ppermute x36, starting transfers between devices, move(): return lax.ppermute(array, 'aux', pairs)  33.8 us
    pallas_call x8, Pallas kernels, call(): pl.pallas_call(kernel, out_shape=outs, in_specs=in_specs, out_specs=[VMEM...  17.2 us
    unnamed x11, local copies, waits for them, and re-layouts  6.91 us
  transfers between devices with their start and end apart: 36, of which 15 were waited for; matrix products, arithmetic and copies ran while one was open for 10% of the time, Pallas kernels for 14%

profile of v21, /device:TPU:0, one launch (start us, length us, event | category | flops | bytes accessed | tf_op | source)
XLA Modules:
  0.0 105.1 jit_solution(17214973274067193323)
XLA Ops:
  0.0 0.5 collective-permute-start.9
  0.5 1.1 %constant_dynamic-slice_fusion.1 = (bf16[1280,128]{1,0:T(8,128)(2,1)S(1)}, bf16[1280,128]{1,0:T(8,128)(2,1)S(1)}) fusion(bf16[1280,256]{1,0:T(8,128)(2,1)} %param.7, s32[]{:T(128)S(6)} %select_n.162, s32[]{:T(128)S(6)} %select_n.161), kind=kLoop, calls=%fused_computation.92 | loop fusion | bytes 1310728 | tf_op jit(solution)/shard_map/dynamic_slice | solution.py:250
  1.6 2.6 %collective-permute-start.2 = (bf16[1280,128]{1,0:T(8,128)(2,1)S(1)}, bf16[1280,128]{1,0:T(8,128)(2,1)S(1)}, u32[]{:S(2)}, u32[]{:S(2)}) collective-permute-start(bf16[1280,128]{1,0:T(8,128)(2,1)S(1)} %get-tuple-element.133.refs_0_), channel_id=1, source_target_pairs={{0,4},{1,5},{2,6},{3,7},{4,8},{5,9},{6,10},{7,11},{8,12},{9,13},{1... | collective-permute-start | bytes 983048 | tf_op jit(solution)/shard_map/ppermute | solution.py:34
  4.2 1.5 %collective-permute-start.3 = (bf16[1280,128]{1,0:T(8,128)(2,1)S(1)}, bf16[1280,128]{1,0:T(8,128)(2,1)S(1)}, u32[]{:S(2)}, u32[]{:S(2)}) collective-permute-start(bf16[1280,128]{1,0:T(8,128)(2,1)S(1)} %get-tuple-element.133.refs_0_), channel_id=1, source_target_pairs={{0,2},{1,3},{2,0},{3,1},{4,6},{5,7},{6,4},{7,5},{8,10},{9,11},{10,... | collective-permute-start | bytes 983048 | tf_op jit(solution)/shard_map/ppermute | solution.py:34
  5.7 0.5 collective-permute-start
  6.2 0.7 constant_dynamic-update-slice_fusion.1
  7.7 0.7 compare_select_fusion.3
  8.4 0.9 collective-permute-done.8.refs_1_
  9.3 1.6 %collective-permute-start.10 = (bf16[1280,128]{1,0:T(8,128)(2,1)S(1)}, bf16[1280,128]{1,0:T(8,128)(2,1)S(1)}, u32[]{:S(2)}, u32[]{:S(2)}) collective-permute-start(bf16[1280,128]{1,0:T(8,128)(2,1)S(1)} %collective-permute-done.8.refs_1_), channel_id=1, source_target_pairs={{0,4},{1,5},{2,6},{3,7},{4,8},{5,9},{6,10},{7,11},{8,12},{9,13},{1... | collective-permute-start | bytes 983048 | tf_op jit(solution)/shard_map/ppermute | solution.py:34
  10.9 0.5 collective-permute-start.11
  11.4 0.6 fusion.28
  12.0 2.8 %collective-permute-done.2.refs_0_ = bf16[1280,128]{1,0:T(8,128)(2,1)S(1)} collective-permute-done((bf16[1280,128]{1,0:T(8,128)(2,1)S(1)}, bf16[1280,128]{1,0:T(8,128)(2,1)S(1)}, u32[]{:S(2)}, u32[]{:S(2)}) %collective-permute-start.2) | collective-permute-done | bytes 327712 | tf_op jit(solution)/shard_map/ppermute | solution.py:34
  14.8 1.5 %collective-permute-start.4 = (bf16[1280,128]{1,0:T(8,128)(2,1)S(1)}, bf16[1280,128]{1,0:T(8,128)(2,1)S(1)}, u32[]{:S(2)}, u32[]{:S(2)}) collective-permute-start(bf16[1280,128]{1,0:T(8,128)(2,1)S(1)} %collective-permute-done.2.refs_0_), channel_id=1, source_target_pairs={{0,4},{1,5},{2,6},{3,7},{4,8},{5,9},{6,10},{7,11},{8,12},{9,13},{1... | collective-permute-start | bytes 983048 | tf_op jit(solution)/shard_map/ppermute | solution.py:34
  16.3 1.5 %collective-permute-start.5 = (bf16[1280,128]{1,0:T(8,128)(2,1)S(1)}, bf16[1280,128]{1,0:T(8,128)(2,1)}, u32[]{:S(2)}, u32[]{:S(2)}) collective-permute-start(bf16[1280,128]{1,0:T(8,128)(2,1)S(1)} %collective-permute-done.2.refs_0_), channel_id=1, source_target_pairs={{0,2},{1,3},{2,0},{3,1},{4,6},{5,7},{6,4},{7,5},{8,10},{9,11},{10,... | collective-permute-start | bytes 983048 | tf_op jit(solution)/shard_map/ppermute | solution.py:34
  17.8 2.1 %copy.9 = bf16[32,8,32,128]{3,2,1,0:T(8,128)(2,1)S(1)} copy(bf16[32,8,32,128]{3,1,2,0:T(8,128)(2,1)} %bitcast.65) | data formatting | bytes 4194304
  19.9 3.4 %copy.10 = bf16[32,8,32,128]{3,2,1,0:T(8,128)(2,1)} copy(bf16[32,8,32,128]{3,1,2,0:T(8,128)(2,1)} %bitcast.25) | data formatting | bytes 4194304
  23.3 0.7 copy-done
  24.1 1.6 %collective-permute-start.12 = (bf16[1280,128]{1,0:T(8,128)(2,1)S(1)}, bf16[1280,128]{1,0:T(8,128)(2,1)}, u32[]{:S(2)}, u32[]{:S(2)}) collective-permute-start(bf16[1280,128]{1,0:T(8,128)(2,1)S(1)} %collective-permute-done.10.refs_1_), channel_id=1, source_target_pairs={{0,4},{1,5},{2,6},{3,7},{4,8},{5,9},{6,10},{7,11},{8,12},{9,13},{1... | collective-permute-start | bytes 983048 | tf_op jit(solution)/shard_map/ppermute | solution.py:34
  25.6 0.5 collective-permute-start.13
  26.2 0.3 convert_reduce_fusion
  26.5 0.5 select_reduce_fusion
  27.1 0.1 convert_reduce_fusion.1.bounds_ref
  27.2 1.6 %collective-permute-done.4.refs_0_ = bf16[1280,128]{1,0:T(8,128)(2,1)S(1)} collective-permute-done((bf16[1280,128]{1,0:T(8,128)(2,1)S(1)}, bf16[1280,128]{1,0:T(8,128)(2,1)S(1)}, u32[]{:S(2)}, u32[]{:S(2)}) %collective-permute-start.4) | collective-permute-done | bytes 327712 | tf_op jit(solution)/shard_map/ppermute | solution.py:34
  28.9 1.6 %collective-permute-start.6 = (bf16[1280,128]{1,0:T(8,128)(2,1)S(1)}, bf16[1280,128]{1,0:T(8,128)(2,1)S(1)}, u32[]{:S(2)}, u32[]{:S(2)}) collective-permute-start(bf16[1280,128]{1,0:T(8,128)(2,1)S(1)} %collective-permute-done.4.refs_0_), channel_id=1, source_target_pairs={{0,4},{1,5},{2,6},{3,7},{4,8},{5,9},{6,10},{7,11},{8,12},{9,13},{1... | collective-permute-start | bytes 983048 | tf_op jit(solution)/shard_map/ppermute | solution.py:34
  30.5 1.5 %collective-permute-start.7 = (bf16[1280,128]{1,0:T(8,128)(2,1)S(1)}, bf16[1280,128]{1,0:T(8,128)(2,1)S(1)}, u32[]{:S(2)}, u32[]{:S(2)}) collective-permute-start(bf16[1280,128]{1,0:T(8,128)(2,1)S(1)} %collective-permute-done.4.refs_0_), channel_id=1, source_target_pairs={{0,2},{1,3},{2,0},{3,1},{4,6},{5,7},{6,4},{7,5},{8,10},{9,11},{10,... | collective-permute-start | bytes 983048 | tf_op jit(solution)/shard_map/ppermute | solution.py:34
  32.0 3.1 %shard_map.46 = (f32[41024,128]{1,0:T(8,128)S(1)}, bf16[512,32,128]{2,1,0:T(8,128)(2,1)S(1)}) custom-call(s32[1584]{0:T(1024)S(1)} %concatenate.10.table_ref, s32[6]{0:T(128)S(1)} %convert_reduce_fusion.1.bounds_ref, bf16[1280,128]{1,0:T(8,128)(2,1)} %copy-done.2, bf16[1280,128]{1,0:T(8,128)(2,1)} %copy-done.3, bf16[256,32,128]{2,1,0:T(8,128)(2,1)S(1)} %bitcast.55, ...), custom_call_target="tpu_custom_call" | custom-call | flops 107374184 | bytes 4194304 | tf_op jit(solution)/shard_map/pallas_call | solution.py:223
  35.1 1.6 %collective-permute-done.12.refs_1_ = bf16[1280,128]{1,0:T(8,128)(2,1)} collective-permute-done((bf16[1280,128]{1,0:T(8,128)(2,1)S(1)}, bf16[1280,128]{1,0:T(8,128)(2,1)}, u32[]{:S(2)}, u32[]{:S(2)}) %collective-permute-start.12) | collective-permute-done | bytes 327712 | tf_op jit(solution)/shard_map/ppermute | solution.py:34
  36.6 0.9 collective-permute-start.15
  37.5 1.5 %collective-permute-start.16 = (bf16[1280,128]{1,0:T(8,128)(2,1)}, bf16[1280,128]{1,0:T(8,128)(2,1)S(1)}, u32[]{:S(2)}, u32[]{:S(2)}) collective-permute-start(bf16[1280,128]{1,0:T(8,128)(2,1)} %collective-permute-done.12.refs_1_), channel_id=1, source_target_pairs={{0,2},{1,3},{2,0},{3,1},{4,6},{5,7},{6,4},{7,5},{8,10},{9,11},{10,... | collective-permute-start | bytes 983048 | tf_op jit(solution)/shard_map/ppermute | solution.py:34
  39.0 4.5 %collective-permute-done.6.refs_0_ = bf16[1280,128]{1,0:T(8,128)(2,1)S(1)} collective-permute-done((bf16[1280,128]{1,0:T(8,128)(2,1)S(1)}, bf16[1280,128]{1,0:T(8,128)(2,1)S(1)}, u32[]{:S(2)}, u32[]{:S(2)}) %collective-permute-start.6) | collective-permute-done | bytes 327712 | tf_op jit(solution)/shard_map/ppermute | solution.py:34
  43.5 2.2 %shard_map.47.refs_5_ = f32[41024,128]{1,0:T(8,128)S(1)} custom-call(s32[1584]{0:T(1024)S(1)} %concatenate.10.table_ref, s32[6]{0:T(128)S(1)} %convert_reduce_fusion.1.bounds_ref, bf16[1280,128]{1,0:T(8,128)(2,1)S(1)} %collective-permute-done.2.refs_0_, bf16[1280,128]{1,0:T(8,128)(2,1)S(1)} %collective-permute-done.10.refs_1_, ...), custom_call_target="tpu_custom_call", output_to_operand_aliasing={{}: (7, {})} | custom-call | flops 107374184 | bytes 4194304 | tf_op jit(solution)/shard_map/pallas_call | solution.py:223
  45.8 0.9 collective-permute-start.14
  46.7 3.8 %collective-permute-done.15.refs_1_ = bf16[1280,128]{1,0:T(8,128)(2,1)S(1)} collective-permute-done((bf16[1280,128]{1,0:T(8,128)(2,1)}, bf16[1280,128]{1,0:T(8,128)(2,1)S(1)}, u32[]{:S(2)}, u32[]{:S(2)}) %collective-permute-start.15) | collective-permute-done | bytes 327712 | tf_op jit(solution)/shard_map/ppermute | solution.py:34
  50.6 0.7 collective-permute-start.17
  51.2 3.1 %shard_map.48.refs_5_ = f32[41024,128]{1,0:T(8,128)S(1)} custom-call(s32[1584]{0:T(1024)S(1)} %concatenate.10.table_ref, s32[6]{0:T(128)S(1)} %convert_reduce_fusion.1.bounds_ref, bf16[1280,128]{1,0:T(8,128)(2,1)S(1)} %collective-permute-done.4.refs_0_, bf16[1280,128]{1,0:T(8,128)(2,1)} %collective-permute-done.12.refs_1_, ...), custom_call_target="tpu_custom_call", output_to_operand_aliasing={{}: (7, {})} | custom-call | flops 107374184 | bytes 4194304 | tf_op jit(solution)/shard_map/pallas_call | solution.py:223
  54.3 2.2 %shard_map.49.refs_3_ = f32[41024,128]{1,0:T(8,128)S(1)} custom-call(s32[1584]{0:T(1024)S(1)} %concatenate.10.table_ref, s32[6]{0:T(128)S(1)} %convert_reduce_fusion.1.bounds_ref, bf16[1280,128]{1,0:T(8,128)(2,1)S(1)} %collective-permute-done.6.refs_0_, bf16[1280,128]{1,0:T(8,128)(2,1)S(1)} %collective-permute-done.15.refs_1_, ...), custom_call_target="tpu_custom_call", output_to_operand_aliasing={{}: (7, {})} | custom-call | flops 107374184 | bytes 4194304 | tf_op jit(solution)/shard_map/pallas_call | solution.py:223
  56.6 0.2 collective-permute-done.14.refs_0_
  56.8 2.1 %collective-permute-done.17.refs_1_ = bf16[1280,128]{1,0:T(8,128)(2,1)S(1)} collective-permute-done((bf16[1280,128]{1,0:T(8,128)(2,1)S(1)}, bf16[1280,128]{1,0:T(8,128)(2,1)S(1)}, u32[]{:S(2)}, u32[]{:S(2)}) %collective-permute-start.17) | collective-permute-done | bytes 327712 | tf_op jit(solution)/shard_map/ppermute | solution.py:34
  58.9 2.4 %shard_map.50 = (f32[41024,128]{1,0:T(8,128)S(1)}, bf16[256,128]{1,0:T(8,128)(2,1)S(1)}, bf16[1,1280,128]{2,1,0:T(8,128)(2,1)S(1)}, bf16[1,1280,128]{2,1,0:T(8,1...) custom-call(s32[1584]{0:T(1024)S(1)} %concatenate.10.table_ref, ...), custom_call_target="tpu_custom_call", output_to_operand_aliasing={{0}: (7, {})} | custom-call | flops 442918496 | bytes 4194304 | tf_op jit(solution)/shard_map/pallas_call | solution.py:223
  61.4 0.5 collective-permute-start.19
  62.0 0.4 collective-permute-start.23
  62.4 1.4 %shard_map.51 = (f32[1,1280,128]{2,1,0:T(8,128)S(1)}, f32[1,1280,128]{2,1,0:T(8,128)S(1)}, f32[1,1280,128]{2,1,0:T(8,128)S(1)}, f32[1,1280,128]{2,1,0:T(8,128)S(1)}) custom-call(s32[8]{0:T(128)S(1)} %fusion.31.chips_ref, s32[1]{0:T(128)} %bitcast.core_ref, f32[41024,128]{1,0:T(8,128)S(1)} %get-tuple-element.94.half, ...), custom_call_target="tpu_custom_call" | custom-call | flops 335544320 | bytes 4194304 | tf_op jit(solution)/shard_map/pallas_call | solution.py:223
  63.8 0.1 fusion.9
  64.0 2.4 %collective-permute-start.24 = (bf16[1280,128]{1,0:T(8,128)(2,1)S(1)}, bf16[1280,128]{1,0:T(8,128)(2,1)S(1)}, u32[]{:S(2)}, u32[]{:S(2)}) collective-permute-start(bf16[1280,128]{1,0:T(8,128)(2,1)S(1)} %get-tuple-element.104), channel_id=1, source_target_pairs={{0,2},{1,3},{2,0},{3,1},{4,6},{5,7},{6,4},{7,5},{8,10},{9,11},{10,... | collective-permute-start | bytes 983048 | tf_op jit(solution)/shard_map/ppermute | solution.py:34
  66.4 0.3 collective-permute-start.25
  66.7 1.4 %shard_map.53 = (bf16[1,1280,128]{2,1,0:T(8,128)(2,1)S(1)}, bf16[1,1280,128]{2,1,0:T(8,128)(2,1)S(1)}, bf16[1,1280,128]{2,1,0:T(8,128)(2,1)S(1)}, bf16[1,1280,128]{2,1,0:T(8,128)(2,1)S(1)}) custom-call(s32[8]{0:T(128)S(1)} %fusion.31.chips_ref, s32[1]{0:T(128)} %bitcast.core_ref, f32[41024,128]{1,0:T(8,128)S(1)} %get-tuple-element.94.half, ...), custom_call_target="tpu_custom_call" | custom-call | flops 335544320 | bytes 4194304 | tf_op jit(solution)/shard_map/pallas_call | solution.py:223
  68.2 0.5 collective-permute-start.32
  68.7 0.1 collective-permute-start.34
  68.8 0.1 fusion.4
  68.9 1.4 %shard_map.52 = (f32[1,1280,128]{2,1,0:T(8,128)S(1)}, f32[1,1280,128]{2,1,0:T(8,128)S(1)}, f32[1,1280,128]{2,1,0:T(8,128)S(1)}, f32[1,1280,128]{2,1,0:T(8,128)S(1)}) custom-call(s32[8]{0:T(128)S(1)} %fusion.31.chips_ref, s32[1]{0:T(128)} %bitcast.core_ref, f32[41024,128]{1,0:T(8,128)S(1)} %get-tuple-element.94.half, ...), custom_call_target="tpu_custom_call" | custom-call | flops 335544320 | bytes 4194304 | tf_op jit(solution)/shard_map/pallas_call | solution.py:223
  70.2 3.8 %collective-permute-done.25 = bf16[640,128]{1,0:T(8,128)(2,1)S(1)} collective-permute-done((bf16[640,128]{1,0:T(8,128)(2,1)S(1)}, bf16[640,128]{1,0:T(8,128)(2,1)S(1)}, u32[]{:S(2)}, u32[]{:S(2)}) %collective-permute-start.25) | collective-permute-done | bytes 163872 | tf_op jit(solution)/shard_map/ppermute | solution.py:34
  74.1 0.2 collective-permute-done.24
  74.4 0.4 collective-permute-start.26
  74.8 2.1 %collective-permute-start.28 = (bf16[640,128]{1,0:T(8,128)(2,1)S(1)}, bf16[640,128]{1,0:T(8,128)(2,1)S(1)}, u32[]{:S(2)}, u32[]{:S(2)}) collective-permute-start(bf16[640,128]{1,0:T(8,128)(2,1)S(1)} %get-tuple-element.130), channel_id=1, source_target_pairs={{0,4},{1,5},{2,6},{3,7},{4,8},{5,9},{6,10},{7,11},{8,12},{9,13},{1... | collective-permute-start | bytes 491528 | tf_op jit(solution)/shard_map/ppermute | solution.py:34
  77.0 1.0 collective-permute-start.29
  78.0 5.3 %collective-permute-done.26 = bf16[640,128]{1,0:T(8,128)(2,1)S(1)} collective-permute-done((bf16[640,128]{1,0:T(8,128)(2,1)S(1)}, bf16[640,128]{1,0:T(8,128)(2,1)S(1)}, u32[]{:S(2)}, u32[]{:S(2)}) %collective-permute-start.26) | collective-permute-done | bytes 163872 | tf_op jit(solution)/shard_map/ppermute | solution.py:34
  83.3 1.8 %collective-permute-start.30 = (bf16[640,128]{1,0:T(8,128)(2,1)S(1)}, bf16[640,128]{1,0:T(8,128)(2,1)S(1)}, u32[]{:S(2)}, u32[]{:S(2)}) collective-permute-start(bf16[640,128]{1,0:T(8,128)(2,1)S(1)} %get-tuple-element.113), channel_id=1, source_target_pairs={{0,2},{1,3},{2,0},{3,1},{4,6},{5,7},{6,4},{7,5},{8,10},{9,11},{10,... | collective-permute-start | bytes 491528 | tf_op jit(solution)/shard_map/ppermute | solution.py:34
  85.2 0.9 collective-permute-done.28
  86.1 0.1 fusion.3
  86.3 3.9 %collective-permute-start.35 = (bf16[1280,128]{1,0:T(8,128)(2,1)S(1)}, bf16[1280,128]{1,0:T(8,128)(2,1)S(1)}, u32[]{:S(2)}, u32[]{:S(2)}) collective-permute-start(bf16[1280,128]{1,0:T(8,128)(2,1)S(1)} %fusion.3), channel_id=1, source_target_pairs={{0,12},{1,13},{2,14},{3,15},{4,0},{5,1},{6,2},{7,3},{8,4},{9,5},{1... | collective-permute-start | bytes 983048 | tf_op jit(solution)/shard_map/ppermute | solution.py:34
  90.1 0.7 collective-permute-start.33
  91.0 4.0 %collective-permute-done.27 = bf16[640,128]{1,0:T(8,128)(2,1)S(1)} collective-permute-done((bf16[640,128]{1,0:T(8,128)(2,1)S(1)}, bf16[640,128]{1,0:T(8,128)(2,1)S(1)}, u32[]{:S(2)}, u32[]{:S(2)}) %collective-permute-start.27) | collective-permute-done | bytes 163872 | tf_op jit(solution)/shard_map/ppermute | solution.py:34
  95.0 9.0 %collective-permute-done.31 = bf16[640,128]{1,0:T(8,128)(2,1)S(1)} collective-permute-done((bf16[640,128]{1,0:T(8,128)(2,1)S(1)}, bf16[640,128]{1,0:T(8,128)(2,1)S(1)}, u32[]{:S(2)}, u32[]{:S(2)}) %collective-permute-start.31) | collective-permute-done | bytes 163872 | tf_op jit(solution)/shard_map/ppermute | solution.py:34
  104.0 1.0 fusion.8
  (49 shorter events, 1.0 us)
Async XLA Ops:
  0.0 9.3 %collective-permute-start.9 = (bf16[256,4096]{1,0:T(8,128)(2,1)}, bf16[256,4096]{1,0:T(8,128)(2,1)}, u32[]{:S(2)}, u32[]{:S(2)}) collective-permute-start(bf16[256,4096]{1,0:T(8,128)(2,1)} %param.4), channel_id=1, source_target_pairs={{0,1},{1,0},{2,3},{3,2},{4,5},{5,4},{6,7},{7,6},{8,9},{9,8},{10,11... | collective-permute-start | bytes 6291464 | tf_op jit(solution)/shard_map/ppermute | solution.py:34
  1.6 13.2 %copy-start.2 = (bf16[1280,128]{1,0:T(8,128)(2,1)}, bf16[1280,128]{1,0:T(8,128)(2,1)S(1)}, u32[]{:S(2)}) copy-start(bf16[1280,128]{1,0:T(8,128)(2,1)S(1)} %get-tuple-element.133.refs_0_) | copy-start | bytes 983044
  1.6 13.2 %collective-permute-start.2 = (bf16[1280,128]{1,0:T(8,128)(2,1)S(1)}, bf16[1280,128]{1,0:T(8,128)(2,1)S(1)}, u32[]{:S(2)}, u32[]{:S(2)}) collective-permute-start(bf16[1280,128]{1,0:T(8,128)(2,1)S(1)} %get-tuple-element.133.refs_0_), channel_id=1, source_target_pairs={{0,4},{1,5},{2,6},{3,7},{4,8},{5,9},{6,10},{7,11},{8,12},{9,13},{1... | collective-permute-start | bytes 983048 | tf_op jit(solution)/shard_map/ppermute | solution.py:34
  4.2 10.6 %collective-permute-start.3 = (bf16[1280,128]{1,0:T(8,128)(2,1)S(1)}, bf16[1280,128]{1,0:T(8,128)(2,1)S(1)}, u32[]{:S(2)}, u32[]{:S(2)}) collective-permute-start(bf16[1280,128]{1,0:T(8,128)(2,1)S(1)} %get-tuple-element.133.refs_0_), channel_id=1, source_target_pairs={{0,2},{1,3},{2,0},{3,1},{4,6},{5,7},{6,4},{7,5},{8,10},{9,11},{10,... | collective-permute-start | bytes 983048 | tf_op jit(solution)/shard_map/ppermute | solution.py:34
  5.7 1.9 %collective-permute-start.1 = (s32[256,2]{0,1:T(2,128)}, s32[256,2]{0,1:T(2,128)S(1)}, u32[]{:S(2)}, u32[]{:S(2)}) collective-permute-start(s32[256,2]{0,1:T(2,128)} %param.5), channel_id=1, source_target_pairs={{0,1},{1,0},{2,3},{3,2},{4,5},{5,4},{6,7},{7,6},{8,9},{9,8},{10,11... | collective-permute-start | bytes 6152 | tf_op jit(solution)/shard_map/ppermute | solution.py:34
  5.7 2.0 %collective-permute-start = (s32[1]{0:T(128)}, s32[1]{0:T(128)}, u32[]{:S(2)}, u32[]{:S(2)}) collective-permute-start(s32[1]{0:T(128)} %param.6), channel_id=1, source_target_pairs={{0,1},{1,0},{2,3},{3,2},{4,5},{5,4},{6,7},{7,6},{8,9},{9,8},{10,11... | collective-permute-start | bytes 20 | tf_op jit(solution)/shard_map/ppermute | solution.py:34
  7.6 1.7 %collective-permute-start.8 = (bf16[1280,128]{1,0:T(8,128)(2,1)S(1)}, bf16[1280,128]{1,0:T(8,128)(2,1)S(1)}, u32[]{:S(2)}, u32[]{:S(2)}) collective-permute-start(bf16[1280,128]{1,0:T(8,128)(2,1)S(1)} %get-tuple-element.132), channel_id=1, source_target_pairs={{0,1},{1,0},{2,3},{3,2},{4,5},{5,4},{6,7},{7,6},{8,9},{9,8},{10,11... | collective-permute-start | bytes 983048 | tf_op jit(solution)/shard_map/ppermute | solution.py:34
  9.3 10.6 %copy-start.3 = (bf16[1280,128]{1,0:T(8,128)(2,1)}, bf16[1280,128]{1,0:T(8,128)(2,1)S(1)}, u32[]{:S(2)}) copy-start(bf16[1280,128]{1,0:T(8,128)(2,1)S(1)} %collective-permute-done.8.refs_1_) | copy-start | bytes 983044
  9.3 14.1 %collective-permute-start.10 = (bf16[1280,128]{1,0:T(8,128)(2,1)S(1)}, bf16[1280,128]{1,0:T(8,128)(2,1)S(1)}, u32[]{:S(2)}, u32[]{:S(2)}) collective-permute-start(bf16[1280,128]{1,0:T(8,128)(2,1)S(1)} %collective-permute-done.8.refs_1_), channel_id=1, source_target_pairs={{0,4},{1,5},{2,6},{3,7},{4,8},{5,9},{6,10},{7,11},{8,12},{9,13},{1... | collective-permute-start | bytes 983048 | tf_op jit(solution)/shard_map/ppermute | solution.py:34
  10.9 12.5 %collective-permute-start.11 = (bf16[1280,128]{1,0:T(8,128)(2,1)S(1)}, bf16[1280,128]{1,0:T(8,128)(2,1)S(1)}, u32[]{:S(2)}, u32[]{:S(2)}) collective-permute-start(bf16[1280,128]{1,0:T(8,128)(2,1)S(1)} %collective-permute-done.8.refs_1_), channel_id=1, source_target_pairs={{0,2},{1,3},{2,0},{3,1},{4,6},{5,7},{6,4},{7,5},{8,10},{9,11},{10,... | collective-permute-start | bytes 983048 | tf_op jit(solution)/shard_map/ppermute | solution.py:34
  14.8 14.0 %collective-permute-start.4 = (bf16[1280,128]{1,0:T(8,128)(2,1)S(1)}, bf16[1280,128]{1,0:T(8,128)(2,1)S(1)}, u32[]{:S(2)}, u32[]{:S(2)}) collective-permute-start(bf16[1280,128]{1,0:T(8,128)(2,1)S(1)} %collective-permute-done.2.refs_0_), channel_id=1, source_target_pairs={{0,4},{1,5},{2,6},{3,7},{4,8},{5,9},{6,10},{7,11},{8,12},{9,13},{1... | collective-permute-start | bytes 983048 | tf_op jit(solution)/shard_map/ppermute | solution.py:34
  16.3 12.6 %collective-permute-start.5 = (bf16[1280,128]{1,0:T(8,128)(2,1)S(1)}, bf16[1280,128]{1,0:T(8,128)(2,1)}, u32[]{:S(2)}, u32[]{:S(2)}) collective-permute-start(bf16[1280,128]{1,0:T(8,128)(2,1)S(1)} %collective-permute-done.2.refs_0_), channel_id=1, source_target_pairs={{0,2},{1,3},{2,0},{3,1},{4,6},{5,7},{6,4},{7,5},{8,10},{9,11},{10,... | collective-permute-start | bytes 983048 | tf_op jit(solution)/shard_map/ppermute | solution.py:34
  23.3 0.7 copy-start
  24.1 12.5 %collective-permute-start.12 = (bf16[1280,128]{1,0:T(8,128)(2,1)S(1)}, bf16[1280,128]{1,0:T(8,128)(2,1)}, u32[]{:S(2)}, u32[]{:S(2)}) collective-permute-start(bf16[1280,128]{1,0:T(8,128)(2,1)S(1)} %collective-permute-done.10.refs_1_), channel_id=1, source_target_pairs={{0,4},{1,5},{2,6},{3,7},{4,8},{5,9},{6,10},{7,11},{8,12},{9,13},{1... | collective-permute-start | bytes 983048 | tf_op jit(solution)/shard_map/ppermute | solution.py:34
  25.6 11.0 %collective-permute-start.13 = (bf16[1280,128]{1,0:T(8,128)(2,1)S(1)}, bf16[1280,128]{1,0:T(8,128)(2,1)}, u32[]{:S(2)}, u32[]{:S(2)}) collective-permute-start(bf16[1280,128]{1,0:T(8,128)(2,1)S(1)} %collective-permute-done.10.refs_1_), channel_id=1, source_target_pairs={{0,2},{1,3},{2,0},{3,1},{4,6},{5,7},{6,4},{7,5},{8,10},{9,11},{10,... | collective-permute-start | bytes 983048 | tf_op jit(solution)/shard_map/ppermute | solution.py:34
  27.2 16.3 %copy-start.1 = (bf16[1280,128]{1,0:T(8,128)(2,1)S(1)}, bf16[1280,128]{1,0:T(8,128)(2,1)}, u32[]{:S(2)}) copy-start(bf16[1280,128]{1,0:T(8,128)(2,1)} %copy-done) | copy-start | bytes 983044
  28.9 14.6 %collective-permute-start.6 = (bf16[1280,128]{1,0:T(8,128)(2,1)S(1)}, bf16[1280,128]{1,0:T(8,128)(2,1)S(1)}, u32[]{:S(2)}, u32[]{:S(2)}) collective-permute-start(bf16[1280,128]{1,0:T(8,128)(2,1)S(1)} %collective-permute-done.4.refs_0_), channel_id=1, source_target_pairs={{0,4},{1,5},{2,6},{3,7},{4,8},{5,9},{6,10},{7,11},{8,12},{9,13},{1... | collective-permute-start | bytes 983048 | tf_op jit(solution)/shard_map/ppermute | solution.py:34
  30.5 13.1 %collective-permute-start.7 = (bf16[1280,128]{1,0:T(8,128)(2,1)S(1)}, bf16[1280,128]{1,0:T(8,128)(2,1)S(1)}, u32[]{:S(2)}, u32[]{:S(2)}) collective-permute-start(bf16[1280,128]{1,0:T(8,128)(2,1)S(1)} %collective-permute-done.4.refs_0_), channel_id=1, source_target_pairs={{0,2},{1,3},{2,0},{3,1},{4,6},{5,7},{6,4},{7,5},{8,10},{9,11},{10,... | collective-permute-start | bytes 983048 | tf_op jit(solution)/shard_map/ppermute | solution.py:34
  36.6 13.9 %collective-permute-start.15 = (bf16[1280,128]{1,0:T(8,128)(2,1)}, bf16[1280,128]{1,0:T(8,128)(2,1)S(1)}, u32[]{:S(2)}, u32[]{:S(2)}) collective-permute-start(bf16[1280,128]{1,0:T(8,128)(2,1)} %collective-permute-done.12.refs_1_), channel_id=1, source_target_pairs={{0,4},{1,5},{2,6},{3,7},{4,8},{5,9},{6,10},{7,11},{8,12},{9,13},{1... | collective-permute-start | bytes 983048 | tf_op jit(solution)/shard_map/ppermute | solution.py:34
  37.5 13.1 %collective-permute-start.16 = (bf16[1280,128]{1,0:T(8,128)(2,1)}, bf16[1280,128]{1,0:T(8,128)(2,1)S(1)}, u32[]{:S(2)}, u32[]{:S(2)}) collective-permute-start(bf16[1280,128]{1,0:T(8,128)(2,1)} %collective-permute-done.12.refs_1_), channel_id=1, source_target_pairs={{0,2},{1,3},{2,0},{3,1},{4,6},{5,7},{6,4},{7,5},{8,10},{9,11},{10,... | collective-permute-start | bytes 983048 | tf_op jit(solution)/shard_map/ppermute | solution.py:34
  45.8 11.0 %collective-permute-start.14 = (bf16[1280,128]{1,0:T(8,128)(2,1)S(1)}, bf16[1280,128]{1,0:T(8,128)(2,1)S(1)}, u32[]{:S(2)}, u32[]{:S(2)}) collective-permute-start(bf16[1280,128]{1,0:T(8,128)(2,1)S(1)} %collective-permute-done.7.refs_2_), channel_id=1, source_target_pairs={{0,4},{1,5},{2,6},{3,7},{4,8},{5,9},{6,10},{7,11},{8,12},{9,13},{1... | collective-permute-start | bytes 983048 | tf_op jit(solution)/shard_map/ppermute | solution.py:34
  50.6 8.3 %collective-permute-start.17 = (bf16[1280,128]{1,0:T(8,128)(2,1)S(1)}, bf16[1280,128]{1,0:T(8,128)(2,1)S(1)}, u32[]{:S(2)}, u32[]{:S(2)}) collective-permute-start(bf16[1280,128]{1,0:T(8,128)(2,1)S(1)} %collective-permute-done.15.refs_1_), channel_id=1, source_target_pairs={{0,2},{1,3},{2,0},{3,1},{4,6},{5,7},{6,4},{7,5},{8,10},{9,11},{10,... | collective-permute-start | bytes 983048 | tf_op jit(solution)/shard_map/ppermute | solution.py:34
  61.3 2.5 %collective-permute-start.18 = (bf16[1280,128]{1,0:T(8,128)(2,1)S(1)}, bf16[1280,128]{1,0:T(8,128)(2,1)S(1)}, u32[]{:S(2)}, u32[]{:S(2)}) collective-permute-start(bf16[1280,128]{1,0:T(8,128)(2,1)S(1)} %bitcast.63), channel_id=1, source_target_pairs={{0,1},{1,0},{2,3},{3,2},{4,5},{5,4},{6,7},{7,6},{8,9},{9,8},{10,11... | collective-permute-start | bytes 983048 | tf_op jit(solution)/shard_map/ppermute | solution.py:34
  61.4 2.4 %collective-permute-start.19 = (bf16[1280,128]{1,0:T(8,128)(2,1)S(1)}, bf16[1280,128]{1,0:T(8,128)(2,1)S(1)}, u32[]{:S(2)}, u32[]{:S(2)}) collective-permute-start(bf16[1280,128]{1,0:T(8,128)(2,1)S(1)} %bitcast.62), channel_id=1, source_target_pairs={{0,1},{1,0},{2,3},{3,2},{4,5},{5,4},{6,7},{7,6},{8,9},{9,8},{10,11... | collective-permute-start | bytes 983048 | tf_op jit(solution)/shard_map/ppermute | solution.py:34
  61.9 6.3 %collective-permute-start.22 = (bf16[1280,128]{1,0:T(8,128)(2,1)S(1)}, bf16[1280,128]{1,0:T(8,128)(2,1)S(1)}, u32[]{:S(2)}, u32[]{:S(2)}) collective-permute-start(bf16[1280,128]{1,0:T(8,128)(2,1)S(1)} %bitcast.60), channel_id=1, source_target_pairs={{0,1},{1,0},{2,3},{3,2},{4,5},{5,4},{6,7},{7,6},{8,9},{9,8},{10,11... | collective-permute-start | bytes 983048 | tf_op jit(solution)/shard_map/ppermute | solution.py:34
  62.0 6.7 %collective-permute-start.23 = (bf16[1280,128]{1,0:T(8,128)(2,1)S(1)}, bf16[1280,128]{1,0:T(8,128)(2,1)S(1)}, u32[]{:S(2)}, u32[]{:S(2)}) collective-permute-start(bf16[1280,128]{1,0:T(8,128)(2,1)S(1)} %bitcast.58), channel_id=1, source_target_pairs={{0,1},{1,0},{2,3},{3,2},{4,5},{5,4},{6,7},{7,6},{8,9},{9,8},{10,11... | collective-permute-start | bytes 983048 | tf_op jit(solution)/shard_map/ppermute | solution.py:34
  64.0 10.3 %collective-permute-start.24 = (bf16[1280,128]{1,0:T(8,128)(2,1)S(1)}, bf16[1280,128]{1,0:T(8,128)(2,1)S(1)}, u32[]{:S(2)}, u32[]{:S(2)}) collective-permute-start(bf16[1280,128]{1,0:T(8,128)(2,1)S(1)} %get-tuple-element.104), channel_id=1, source_target_pairs={{0,2},{1,3},{2,0},{3,1},{4,6},{5,7},{6,4},{7,5},{8,10},{9,11},{10,... | collective-permute-start | bytes 983048 | tf_op jit(solution)/shard_map/ppermute | solution.py:34
  66.4 7.7 %collective-permute-start.25 = (bf16[640,128]{1,0:T(8,128)(2,1)S(1)}, bf16[640,128]{1,0:T(8,128)(2,1)S(1)}, u32[]{:S(2)}, u32[]{:S(2)}) collective-permute-start(bf16[640,128]{1,0:T(8,128)(2,1)S(1)} %get-tuple-element.105), channel_id=1, source_target_pairs={{0,4},{1,5},{2,6},{3,7},{4,8},{5,9},{6,10},{7,11},{8,12},{9,13},{1... | collective-permute-start | bytes 491528 | tf_op jit(solution)/shard_map/ppermute | solution.py:34
  68.1 6.7 %collective-permute-start.21 = (bf16[1280,128]{1,0:T(8,128)(2,1)S(1)}, bf16[1280,128]{1,0:T(8,128)(2,1)S(1)}, u32[]{:S(2)}, u32[]{:S(2)}) collective-permute-start(bf16[1280,128]{1,0:T(8,128)(2,1)S(1)} %bitcast.61), channel_id=1, source_target_pairs={{0,1},{1,0},{2,3},{3,2},{4,5},{5,4},{6,7},{7,6},{8,9},{9,8},{10,11... | collective-permute-start | bytes 983048 | tf_op jit(solution)/shard_map/ppermute | solution.py:34
  68.2 8.8 %collective-permute-start.32 = (bf16[1280,128]{1,0:T(8,128)(2,1)S(1)}, bf16[1280,128]{1,0:T(8,128)(2,1)S(1)}, u32[]{:S(2)}, u32[]{:S(2)}) collective-permute-start(bf16[1280,128]{1,0:T(8,128)(2,1)S(1)} %bitcast.59), channel_id=1, source_target_pairs={{0,1},{1,0},{2,3},{3,2},{4,5},{5,4},{6,7},{7,6},{8,9},{9,8},{10,11... | collective-permute-start | bytes 983048 | tf_op jit(solution)/shard_map/ppermute | solution.py:34
  68.7 17.5 %collective-permute-start.34 = (bf16[1280,128]{1,0:T(8,128)(2,1)S(1)}, bf16[1280,128]{1,0:T(8,128)(2,1)S(1)}, u32[]{:S(2)}, u32[]{:S(2)}) collective-permute-start(bf16[1280,128]{1,0:T(8,128)(2,1)S(1)} %bitcast.57), channel_id=1, source_target_pairs={{0,1},{1,0},{2,3},{3,2},{4,5},{5,4},{6,7},{7,6},{8,9},{9,8},{10,11... | collective-permute-start | bytes 983048 | tf_op jit(solution)/shard_map/ppermute | solution.py:34
  74.1 16.9 %collective-permute-start.20 = (bf16[1280,128]{1,0:T(8,128)(2,1)S(1)}, bf16[1280,128]{1,0:T(8,128)(2,1)S(1)}, u32[]{:S(2)}, u32[]{:S(2)}) collective-permute-start(bf16[1280,128]{1,0:T(8,128)(2,1)S(1)} %bitcast.56), channel_id=1, source_target_pairs={{0,1},{1,0},{2,3},{3,2},{4,5},{5,4},{6,7},{7,6},{8,9},{9,8},{10,11... | collective-permute-start | bytes 983048 | tf_op jit(solution)/shard_map/ppermute | solution.py:34
  74.4 8.9 %collective-permute-start.26 = (bf16[640,128]{1,0:T(8,128)(2,1)S(1)}, bf16[640,128]{1,0:T(8,128)(2,1)S(1)}, u32[]{:S(2)}, u32[]{:S(2)}) collective-permute-start(bf16[640,128]{1,0:T(8,128)(2,1)S(1)} %get-tuple-element.131), channel_id=1, source_target_pairs={{0,4},{1,5},{2,6},{3,7},{4,8},{5,9},{6,10},{7,11},{8,12},{9,13},{1... | collective-permute-start | bytes 491528 | tf_op jit(solution)/shard_map/ppermute | solution.py:34
  74.8 11.3 %collective-permute-start.28 = (bf16[640,128]{1,0:T(8,128)(2,1)S(1)}, bf16[640,128]{1,0:T(8,128)(2,1)S(1)}, u32[]{:S(2)}, u32[]{:S(2)}) collective-permute-start(bf16[640,128]{1,0:T(8,128)(2,1)S(1)} %get-tuple-element.130), channel_id=1, source_target_pairs={{0,4},{1,5},{2,6},{3,7},{4,8},{5,9},{6,10},{7,11},{8,12},{9,13},{1... | collective-permute-start | bytes 491528 | tf_op jit(solution)/shard_map/ppermute | solution.py:34
  77.0 9.2 %collective-permute-start.29 = (bf16[1280,128]{1,0:T(8,128)(2,1)S(1)}, bf16[1280,128]{1,0:T(8,128)(2,1)S(1)}, u32[]{:S(2)}, u32[]{:S(2)}) collective-permute-start(bf16[1280,128]{1,0:T(8,128)(2,1)S(1)} %get-tuple-element.111), channel_id=1, source_target_pairs={{0,2},{1,3},{2,0},{3,1},{4,6},{5,7},{6,4},{7,5},{8,10},{9,11},{10,... | collective-permute-start | bytes 983048 | tf_op jit(solution)/shard_map/ppermute | solution.py:34
  83.3 7.6 %collective-permute-start.30 = (bf16[640,128]{1,0:T(8,128)(2,1)S(1)}, bf16[640,128]{1,0:T(8,128)(2,1)S(1)}, u32[]{:S(2)}, u32[]{:S(2)}) collective-permute-start(bf16[640,128]{1,0:T(8,128)(2,1)S(1)} %get-tuple-element.113), channel_id=1, source_target_pairs={{0,2},{1,3},{2,0},{3,1},{4,6},{5,7},{6,4},{7,5},{8,10},{9,11},{10,... | collective-permute-start | bytes 491528 | tf_op jit(solution)/shard_map/ppermute | solution.py:34
  86.1 8.9 %collective-permute-start.27 = (bf16[640,128]{1,0:T(8,128)(2,1)S(1)}, bf16[640,128]{1,0:T(8,128)(2,1)S(1)}, u32[]{:S(2)}, u32[]{:S(2)}) collective-permute-start(bf16[640,128]{1,0:T(8,128)(2,1)S(1)} %fusion.13), channel_id=1, source_target_pairs={{0,4},{1,5},{2,6},{3,7},{4,8},{5,9},{6,10},{7,11},{8,12},{9,13},{1... | collective-permute-start | bytes 491528 | tf_op jit(solution)/shard_map/ppermute | solution.py:34
  86.3 17.8 %collective-permute-start.35 = (bf16[1280,128]{1,0:T(8,128)(2,1)S(1)}, bf16[1280,128]{1,0:T(8,128)(2,1)S(1)}, u32[]{:S(2)}, u32[]{:S(2)}) collective-permute-start(bf16[1280,128]{1,0:T(8,128)(2,1)S(1)} %fusion.3), channel_id=1, source_target_pairs={{0,12},{1,13},{2,14},{3,15},{4,0},{5,1},{6,2},{7,3},{8,4},{9,5},{1... | collective-permute-start | bytes 983048 | tf_op jit(solution)/shard_map/ppermute | solution.py:34
  90.1 13.9 %collective-permute-start.33 = (bf16[1280,128]{1,0:T(8,128)(2,1)S(1)}, bf16[1280,128]{1,0:T(8,128)(2,1)S(1)}, u32[]{:S(2)}, u32[]{:S(2)}) collective-permute-start(bf16[1280,128]{1,0:T(8,128)(2,1)S(1)} %add_convert_fusion), channel_id=1, source_target_pairs={{0,2},{1,3},{2,0},{3,1},{4,6},{5,7},{6,4},{7,5},{8,10},{9,11},{10,... | collective-permute-start | bytes 983048 | tf_op jit(solution)/shard_map/ppermute | solution.py:34
  90.9 13.1 %collective-permute-start.31 = (bf16[640,128]{1,0:T(8,128)(2,1)S(1)}, bf16[640,128]{1,0:T(8,128)(2,1)S(1)}, u32[]{:S(2)}, u32[]{:S(2)}) collective-permute-start(bf16[640,128]{1,0:T(8,128)(2,1)S(1)} %add_convert_fusion.1), channel_id=1, source_target_pairs={{0,4},{1,5},{2,6},{3,7},{4,8},{5,9},{6,10},{7,11},{8,12},{9,13},{1... | collective-permute-start | bytes 491528 | tf_op jit(solution)/shard_map/ppermute | solution.py:34

commit v22 on v20

--- a/solution.py
+++ b/solution.py
@@ -76,8 +76,8 @@
     def paired(send, keep):
         return keep + wide(move(send, swap))
 
-    first = [FAR2, FAR1, FAR3, NEAR2]
-    rest = [NEAR1, FAR0, NEAR3, NEAR0]
+    first = [FAR2, FAR1]
+    rest = [NEAR2, FAR3, NEAR1, FAR0, NEAR3, NEAR0]
     sends = blocks_of(first, False)
     total = {name: paired(*pair) for name, *pair in zip(first, sends, blocks_of(first, True))}
     aside, beside = map(narrow, halves(total[FAR1]))

time: 106 us -> 108 us (1.019)
  Pallas kernels: 15.7 us -> 20.3 us
  starting transfers between devices: 32.2 us -> 29.3 us
    pallas_call x8, Pallas kernels: 15.7 us -> 20.3 us  [call(): pl.pallas_call(kernel, out_shape=outs, in_specs=in_specs, out_specs=[VMEM...]
    ppermute x34, starting transfers between devices: 32.2 us -> 29.3 us  [move(): return lax.ppermute(array, 'aux', pairs)]
  transfers between devices with their start and end apart: 34 -> 34, of which waited for: 17 -> 17; matrix products, arithmetic and copies ran while one was open for 10% -> 10% of each run, Pallas kernels for 13% -> 16%
where the time goes in v22:
time: 108 us
  waiting for transfers between devices  44.9 us (42%)
  starting transfers between devices  29.3 us (27%)
  Pallas kernels  20.3 us (19%)
  local copies, waits for them, and re-layouts  8.14 us (8%)
  other arithmetic  4.11 us (4%)
    ppermute x34, waiting for transfers between devices, move(): return lax.ppermute(array, 'aux', pairs)  44.9 us
    ppermute x34, starting transfers between devices, move(): return lax.ppermute(array, 'aux', pairs)  29.3 us
    pallas_call x8, Pallas kernels, call(): pl.pallas_call(kernel, out_shape=outs, in_specs=in_specs, out_specs=[VMEM...  20.3 us
    unnamed x11, local copies, waits for them, and re-layouts  6.92 us
  transfers between devices with their start and end apart: 34, of which 17 were waited for; matrix products, arithmetic and copies ran while one was open for 10% of the time, Pallas kernels for 16%

profile of v22, /device:TPU:0, one launch (start us, length us, event | category | flops | bytes accessed | tf_op | source)
XLA Modules:
  0.0 107.7 jit_solution(2968634986875817111)
XLA Ops:
  0.0 0.5 collective-permute-start.9
  0.5 1.1 %constant_dynamic-slice_fusion.1 = (bf16[1280,128]{1,0:T(8,128)(2,1)S(1)}, bf16[1280,128]{1,0:T(8,128)(2,1)S(1)}) fusion(bf16[1280,256]{1,0:T(8,128)(2,1)} %param.7, s32[]{:T(128)S(6)} %select_n.162, s32[]{:T(128)S(6)} %select_n.161), kind=kLoop, calls=%fused_computation.90 | loop fusion | bytes 1310728 | tf_op jit(solution)/shard_map/dynamic_slice | solution.py:246
  1.6 2.6 %collective-permute-start.2 = (bf16[1280,128]{1,0:T(8,128)(2,1)S(1)}, bf16[1280,128]{1,0:T(8,128)(2,1)S(1)}, u32[]{:S(2)}, u32[]{:S(2)}) collective-permute-start(bf16[1280,128]{1,0:T(8,128)(2,1)S(1)} %get-tuple-element.123.refs_0_), channel_id=1, source_target_pairs={{0,4},{1,5},{2,6},{3,7},{4,8},{5,9},{6,10},{7,11},{8,12},{9,13},{1... | collective-permute-start | bytes 983048 | tf_op jit(solution)/shard_map/ppermute | solution.py:34
  4.2 1.5 %collective-permute-start.3 = (bf16[1280,128]{1,0:T(8,128)(2,1)S(1)}, bf16[1280,128]{1,0:T(8,128)(2,1)S(1)}, u32[]{:S(2)}, u32[]{:S(2)}) collective-permute-start(bf16[1280,128]{1,0:T(8,128)(2,1)S(1)} %get-tuple-element.123.refs_0_), channel_id=1, source_target_pairs={{0,2},{1,3},{2,0},{3,1},{4,6},{5,7},{6,4},{7,5},{8,10},{9,11},{10,... | collective-permute-start | bytes 983048 | tf_op jit(solution)/shard_map/ppermute | solution.py:34
  5.7 0.5 collective-permute-start
  6.2 0.7 constant_dynamic-update-slice_fusion.1
  7.7 0.7 compare_select_fusion.3
  8.4 0.9 collective-permute-done.8.refs_1_
  9.3 1.6 %collective-permute-start.10 = (bf16[1280,128]{1,0:T(8,128)(2,1)S(1)}, bf16[1280,128]{1,0:T(8,128)(2,1)S(1)}, u32[]{:S(2)}, u32[]{:S(2)}) collective-permute-start(bf16[1280,128]{1,0:T(8,128)(2,1)S(1)} %collective-permute-done.8.refs_1_), channel_id=1, source_target_pairs={{0,4},{1,5},{2,6},{3,7},{4,8},{5,9},{6,10},{7,11},{8,12},{9,13},{1... | collective-permute-start | bytes 983048 | tf_op jit(solution)/shard_map/ppermute | solution.py:34
  10.9 0.5 collective-permute-start.11
  11.4 0.6 fusion.30
  12.0 2.8 %collective-permute-done.2.refs_0_ = bf16[1280,128]{1,0:T(8,128)(2,1)S(1)} collective-permute-done((bf16[1280,128]{1,0:T(8,128)(2,1)S(1)}, bf16[1280,128]{1,0:T(8,128)(2,1)S(1)}, u32[]{:S(2)}, u32[]{:S(2)}) %collective-permute-start.2) | collective-permute-done | bytes 327712 | tf_op jit(solution)/shard_map/ppermute | solution.py:34
  14.8 1.5 %collective-permute-start.4 = (bf16[1280,128]{1,0:T(8,128)(2,1)S(1)}, bf16[1280,128]{1,0:T(8,128)(2,1)S(1)}, u32[]{:S(2)}, u32[]{:S(2)}) collective-permute-start(bf16[1280,128]{1,0:T(8,128)(2,1)S(1)} %collective-permute-done.2.refs_0_), channel_id=1, source_target_pairs={{0,4},{1,5},{2,6},{3,7},{4,8},{5,9},{6,10},{7,11},{8,12},{9,13},{1... | collective-permute-start | bytes 983048 | tf_op jit(solution)/shard_map/ppermute | solution.py:34
  16.3 1.5 %collective-permute-start.5 = (bf16[1280,128]{1,0:T(8,128)(2,1)S(1)}, bf16[1280,128]{1,0:T(8,128)(2,1)}, u32[]{:S(2)}, u32[]{:S(2)}) collective-permute-start(bf16[1280,128]{1,0:T(8,128)(2,1)S(1)} %collective-permute-done.2.refs_0_), channel_id=1, source_target_pairs={{0,2},{1,3},{2,0},{3,1},{4,6},{5,7},{6,4},{7,5},{8,10},{9,11},{10,... | collective-permute-start | bytes 983048 | tf_op jit(solution)/shard_map/ppermute | solution.py:34
  17.8 2.1 %copy.9 = bf16[32,8,32,128]{3,2,1,0:T(8,128)(2,1)S(1)} copy(bf16[32,8,32,128]{3,1,2,0:T(8,128)(2,1)} %bitcast.75) | data formatting | bytes 4194304
  19.9 3.4 %copy.10 = bf16[32,8,32,128]{3,2,1,0:T(8,128)(2,1)} copy(bf16[32,8,32,128]{3,1,2,0:T(8,128)(2,1)} %bitcast.25) | data formatting | bytes 4194304
  23.3 0.7 copy-done
  24.1 1.6 %collective-permute-start.12 = (bf16[1280,128]{1,0:T(8,128)(2,1)S(1)}, bf16[1280,128]{1,0:T(8,128)(2,1)}, u32[]{:S(2)}, u32[]{:S(2)}) collective-permute-start(bf16[1280,128]{1,0:T(8,128)(2,1)S(1)} %collective-permute-done.10.refs_1_), channel_id=1, source_target_pairs={{0,4},{1,5},{2,6},{3,7},{4,8},{5,9},{6,10},{7,11},{8,12},{9,13},{1... | collective-permute-start | bytes 983048 | tf_op jit(solution)/shard_map/ppermute | solution.py:34
  25.6 0.5 collective-permute-start.13
  26.2 0.3 convert_reduce_fusion
  26.5 0.5 select_reduce_fusion
  27.1 0.1 convert_reduce_fusion.1.bounds_ref
  27.2 1.6 %collective-permute-done.4.refs_0_ = bf16[1280,128]{1,0:T(8,128)(2,1)S(1)} collective-permute-done((bf16[1280,128]{1,0:T(8,128)(2,1)S(1)}, bf16[1280,128]{1,0:T(8,128)(2,1)S(1)}, u32[]{:S(2)}, u32[]{:S(2)}) %collective-permute-start.4) | collective-permute-done | bytes 327712 | tf_op jit(solution)/shard_map/ppermute | solution.py:34
  28.9 1.6 %collective-permute-start.6 = (bf16[1280,128]{1,0:T(8,128)(2,1)S(1)}, bf16[1280,128]{1,0:T(8,128)(2,1)S(1)}, u32[]{:S(2)}, u32[]{:S(2)}) collective-permute-start(bf16[1280,128]{1,0:T(8,128)(2,1)S(1)} %collective-permute-done.4.refs_0_), channel_id=1, source_target_pairs={{0,4},{1,5},{2,6},{3,7},{4,8},{5,9},{6,10},{7,11},{8,12},{9,13},{1... | collective-permute-start | bytes 983048 | tf_op jit(solution)/shard_map/ppermute | solution.py:34
  30.5 1.5 %collective-permute-start.7 = (bf16[1280,128]{1,0:T(8,128)(2,1)S(1)}, bf16[1280,128]{1,0:T(8,128)(2,1)S(1)}, u32[]{:S(2)}, u32[]{:S(2)}) collective-permute-start(bf16[1280,128]{1,0:T(8,128)(2,1)S(1)} %collective-permute-done.4.refs_0_), channel_id=1, source_target_pairs={{0,2},{1,3},{2,0},{3,1},{4,6},{5,7},{6,4},{7,5},{8,10},{9,11},{10,... | collective-permute-start | bytes 983048 | tf_op jit(solution)/shard_map/ppermute | solution.py:34
  32.0 3.6 %shard_map.46 = (f32[41024,128]{1,0:T(8,128)S(1)}, bf16[512,32,128]{2,1,0:T(8,128)(2,1)S(1)}) custom-call(s32[1584]{0:T(1024)S(1)} %concatenate.7.table_ref, s32[6]{0:T(128)S(1)} %convert_reduce_fusion.1.bounds_ref, bf16[1280,128]{1,0:T(8,128)(2,1)} %copy-done.2, bf16[1280,128]{1,0:T(8,128)(2,1)} %copy-done.3, bf16[256,32,128]{2,1,0:T(8,128)(2,1)S(1)} %bitcast.65, ...), custom_call_target="tpu_custom_call" | custom-call | flops 107374184 | bytes 4194304 | tf_op jit(solution)/shard_map/pallas_call | solution.py:219
  35.6 1.0 collective-permute-done.12.refs_1_
  36.6 0.9 collective-permute-start.15
  37.5 1.5 %collective-permute-start.16 = (bf16[1280,128]{1,0:T(8,128)(2,1)}, bf16[1280,128]{1,0:T(8,128)(2,1)S(1)}, u32[]{:S(2)}, u32[]{:S(2)}) collective-permute-start(bf16[1280,128]{1,0:T(8,128)(2,1)} %collective-permute-done.12.refs_1_), channel_id=1, source_target_pairs={{0,2},{1,3},{2,0},{3,1},{4,6},{5,7},{6,4},{7,5},{8,10},{9,11},{10,... | collective-permute-start | bytes 983048 | tf_op jit(solution)/shard_map/ppermute | solution.py:34
  39.0 4.5 %collective-permute-done.6.refs_0_ = bf16[1280,128]{1,0:T(8,128)(2,1)S(1)} collective-permute-done((bf16[1280,128]{1,0:T(8,128)(2,1)S(1)}, bf16[1280,128]{1,0:T(8,128)(2,1)S(1)}, u32[]{:S(2)}, u32[]{:S(2)}) %collective-permute-start.6) | collective-permute-done | bytes 327712 | tf_op jit(solution)/shard_map/ppermute | solution.py:34
  43.5 2.8 %shard_map.47.refs_5_ = f32[41024,128]{1,0:T(8,128)S(1)} custom-call(s32[1584]{0:T(1024)S(1)} %concatenate.7.table_ref, s32[6]{0:T(128)S(1)} %convert_reduce_fusion.1.bounds_ref, bf16[1280,128]{1,0:T(8,128)(2,1)S(1)} %collective-permute-done.2.refs_0_, bf16[1280,128]{1,0:T(8,128)(2,1)S(1)} %collective-permute-done.10.refs_1_, ...), custom_call_target="tpu_custom_call", output_to_operand_aliasing={{}: (7, {})} | custom-call | flops 107374184 | bytes 4194304 | tf_op jit(solution)/shard_map/pallas_call | solution.py:219
  46.4 0.9 collective-permute-start.14
  47.3 2.9 %collective-permute-done.15.refs_1_ = bf16[1280,128]{1,0:T(8,128)(2,1)S(1)} collective-permute-done((bf16[1280,128]{1,0:T(8,128)(2,1)}, bf16[1280,128]{1,0:T(8,128)(2,1)S(1)}, u32[]{:S(2)}, u32[]{:S(2)}) %collective-permute-start.15) | collective-permute-done | bytes 327712 | tf_op jit(solution)/shard_map/ppermute | solution.py:34
  50.2 1.1 collective-permute-start.17
  51.2 3.9 %shard_map.48.refs_5_ = f32[41024,128]{1,0:T(8,128)S(1)} custom-call(s32[1584]{0:T(1024)S(1)} %concatenate.7.table_ref, s32[6]{0:T(128)S(1)} %convert_reduce_fusion.1.bounds_ref, bf16[1280,128]{1,0:T(8,128)(2,1)S(1)} %collective-permute-done.4.refs_0_, bf16[1280,128]{1,0:T(8,128)(2,1)} %collective-permute-done.12.refs_1_, ...), custom_call_target="tpu_custom_call", output_to_operand_aliasing={{}: (7, {})} | custom-call | flops 107374184 | bytes 4194304 | tf_op jit(solution)/shard_map/pallas_call | solution.py:219
  55.2 2.8 %shard_map.49.refs_3_ = f32[41024,128]{1,0:T(8,128)S(1)} custom-call(s32[1584]{0:T(1024)S(1)} %concatenate.7.table_ref, s32[6]{0:T(128)S(1)} %convert_reduce_fusion.1.bounds_ref, bf16[1280,128]{1,0:T(8,128)(2,1)S(1)} %collective-permute-done.6.refs_0_, bf16[1280,128]{1,0:T(8,128)(2,1)S(1)} %collective-permute-done.15.refs_1_, ...), custom_call_target="tpu_custom_call", output_to_operand_aliasing={{}: (7, {})} | custom-call | flops 107374184 | bytes 4194304 | tf_op jit(solution)/shard_map/pallas_call | solution.py:219
  58.0 0.9 collective-permute-done.17.refs_1_
  58.9 2.6 %shard_map.50 = (f32[41024,128]{1,0:T(8,128)S(1)}, bf16[256,128]{1,0:T(8,128)(2,1)S(1)}, bf16[1,1280,128]{2,1,0:T(8,128)(2,1)S(1)}, bf16[1,1280,128]{2,1,0:T(8,128)(2,1)S(1)}) custom-call(s32[1584]{0:T(1024)S(1)} %concatenate.7.table_ref, s32[6]{0:T(128)S(1)} %convert_reduce_fusion.1.bounds_ref, ...), custom_call_target="tpu_custom_call", output_to_operand_aliasing={{0}: (7, {})} | custom-call | flops 275146336 | bytes 4194304 | tf_op jit(solution)/shard_map/pallas_call | solution.py:219
  61.6 0.5 collective-permute-start.19
  62.1 1.0 shard_map.51
  63.3 0.5 collective-permute-done.19
  63.7 0.1 fusion.14
  63.9 1.5 %collective-permute-start.24 = (bf16[1280,128]{1,0:T(8,128)(2,1)S(1)}, bf16[1280,128]{1,0:T(8,128)(2,1)S(1)}, u32[]{:S(2)}, u32[]{:S(2)}) collective-permute-start(bf16[1280,128]{1,0:T(8,128)(2,1)S(1)} %get-tuple-element.100), channel_id=1, source_target_pairs={{0,2},{1,3},{2,0},{3,1},{4,6},{5,7},{6,4},{7,5},{8,10},{9,11},{10,... | collective-permute-start | bytes 983048 | tf_op jit(solution)/shard_map/ppermute | solution.py:34
  65.4 1.7 %shard_map.53 = (bf16[1,1280,128]{2,1,0:T(8,128)(2,1)S(1)}, bf16[1,1280,128]{2,1,0:T(8,128)(2,1)S(1)}, bf16[1,1280,128]{2,1,0:T(8,128)(2,1)S(1)}, bf16[1,1280,12...) custom-call(s32[8]{0:T(128)S(1)} %fusion.33.chips_ref, s32[1]{0:T(128)} %bitcast.core_ref, ...), custom_call_target="tpu_custom_call" | custom-call | flops 503316480 | bytes 4194304 | tf_op jit(solution)/shard_map/pallas_call | solution.py:219
  67.2 0.4 collective-permute-start.25
  67.6 0.2 collective-permute-start.22
  67.8 0.3 collective-permute-start.21
  68.1 1.7 %shard_map.52 = (f32[1,1280,128]{2,1,0:T(8,128)S(1)}, f32[1,1280,128]{2,1,0:T(8,128)S(1)}, f32[1,1280,128]{2,1,0:T(8,128)S(1)}, f32[1,1280,128]{2,1,0:T(8,128)S(...) custom-call(s32[8]{0:T(128)S(1)} %fusion.33.chips_ref, s32[1]{0:T(128)} %bitcast.core_ref, ...), custom_call_target="tpu_custom_call" | custom-call | flops 503316480 | bytes 4194304 | tf_op jit(solution)/shard_map/pallas_call | solution.py:219
  69.8 5.8 %collective-permute-done.25 = bf16[640,128]{1,0:T(8,128)(2,1)S(1)} collective-permute-done((bf16[640,128]{1,0:T(8,128)(2,1)S(1)}, bf16[640,128]{1,0:T(8,128)(2,1)S(1)}, u32[]{:S(2)}, u32[]{:S(2)}) %collective-permute-start.25) | collective-permute-done | bytes 163872 | tf_op jit(solution)/shard_map/ppermute | solution.py:34
  75.6 0.5 collective-permute-start.32
  76.3 0.1 fusion.6
  76.5 0.8 collective-permute-done.29
  77.2 0.6 collective-permute-start.27
  77.9 1.5 %collective-permute-start.30 = (bf16[1280,128]{1,0:T(8,128)(2,1)S(1)}, bf16[1280,128]{1,0:T(8,128)(2,1)S(1)}, u32[]{:S(2)}, u32[]{:S(2)}) collective-permute-start(bf16[1280,128]{1,0:T(8,128)(2,1)S(1)} %fusion.4), channel_id=1, source_target_pairs={{0,2},{1,3},{2,0},{3,1},{4,6},{5,7},{6,4},{7,5},{8,10},{9,11},{10,... | collective-permute-start | bytes 983048 | tf_op jit(solution)/shard_map/ppermute | solution.py:34
  79.4 4.9 %collective-permute-done.27 = bf16[640,128]{1,0:T(8,128)(2,1)S(1)} collective-permute-done((bf16[640,128]{1,0:T(8,128)(2,1)S(1)}, bf16[640,128]{1,0:T(8,128)(2,1)S(1)}, u32[]{:S(2)}, u32[]{:S(2)}) %collective-permute-start.27) | collective-permute-done | bytes 163872 | tf_op jit(solution)/shard_map/ppermute | solution.py:34
  84.3 4.0 %collective-permute-done.26 = bf16[1280,128]{1,0:T(8,128)(2,1)S(1)} collective-permute-done((bf16[1280,128]{1,0:T(8,128)(2,1)S(1)}, bf16[1280,128]{1,0:T(8,128)(2,1)S(1)}, u32[]{:S(2)}, u32[]{:S(2)}) %collective-permute-start.26) | collective-permute-done | bytes 327712 | tf_op jit(solution)/shard_map/ppermute | solution.py:34
  88.3 0.1 fusion.9
  88.6 1.9 %collective-permute-done.30 = bf16[1280,128]{1,0:T(8,128)(2,1)S(1)} collective-permute-done((bf16[1280,128]{1,0:T(8,128)(2,1)S(1)}, bf16[1280,128]{1,0:T(8,128)(2,1)S(1)}, u32[]{:S(2)}, u32[]{:S(2)}) %collective-permute-start.30) | collective-permute-done | bytes 327712 | tf_op jit(solution)/shard_map/ppermute | solution.py:34
  90.5 0.1 fusion.3
  90.7 3.1 %collective-permute-start.33 = (bf16[1280,128]{1,0:T(8,128)(2,1)S(1)}, bf16[1280,128]{1,0:T(8,128)(2,1)S(1)}, u32[]{:S(2)}, u32[]{:S(2)}) collective-permute-start(bf16[1280,128]{1,0:T(8,128)(2,1)S(1)} %fusion.3), channel_id=1, source_target_pairs={{0,12},{1,13},{2,14},{3,15},{4,0},{5,1},{6,2},{7,3},{8,4},{9,5},{1... | collective-permute-start | bytes 983048 | tf_op jit(solution)/shard_map/ppermute | solution.py:34
  93.8 0.6 collective-permute-start.31
  94.4 6.6 %collective-permute-done.28 = bf16[1280,128]{1,0:T(8,128)(2,1)S(1)} collective-permute-done((bf16[1280,128]{1,0:T(8,128)(2,1)S(1)}, bf16[1280,128]{1,0:T(8,128)(2,1)S(1)}, u32[]{:S(2)}, u32[]{:S(2)}) %collective-permute-start.28) | collective-permute-done | bytes 327712 | tf_op jit(solution)/shard_map/ppermute | solution.py:34
  101.0 5.7 %collective-permute-done.33 = bf16[1280,128]{1,0:T(8,128)(2,1)S(1)} collective-permute-done((bf16[1280,128]{1,0:T(8,128)(2,1)S(1)}, bf16[1280,128]{1,0:T(8,128)(2,1)S(1)}, u32[]{:S(2)}, u32[]{:S(2)}) %collective-permute-start.33) | collective-permute-done | bytes 327712 | tf_op jit(solution)/shard_map/ppermute | solution.py:34
  106.7 1.0 fusion.13
  (43 shorter events, 1.0 us)
Async XLA Ops:
  0.0 9.3 %collective-permute-start.9 = (bf16[256,4096]{1,0:T(8,128)(2,1)}, bf16[256,4096]{1,0:T(8,128)(2,1)}, u32[]{:S(2)}, u32[]{:S(2)}) collective-permute-start(bf16[256,4096]{1,0:T(8,128)(2,1)} %param.4), channel_id=1, source_target_pairs={{0,1},{1,0},{2,3},{3,2},{4,5},{5,4},{6,7},{7,6},{8,9},{9,8},{10,11... | collective-permute-start | bytes 6291464 | tf_op jit(solution)/shard_map/ppermute | solution.py:34
  1.6 13.2 %copy-start.2 = (bf16[1280,128]{1,0:T(8,128)(2,1)}, bf16[1280,128]{1,0:T(8,128)(2,1)S(1)}, u32[]{:S(2)}) copy-start(bf16[1280,128]{1,0:T(8,128)(2,1)S(1)} %get-tuple-element.123.refs_0_) | copy-start | bytes 983044
  1.6 13.2 %collective-permute-start.2 = (bf16[1280,128]{1,0:T(8,128)(2,1)S(1)}, bf16[1280,128]{1,0:T(8,128)(2,1)S(1)}, u32[]{:S(2)}, u32[]{:S(2)}) collective-permute-start(bf16[1280,128]{1,0:T(8,128)(2,1)S(1)} %get-tuple-element.123.refs_0_), channel_id=1, source_target_pairs={{0,4},{1,5},{2,6},{3,7},{4,8},{5,9},{6,10},{7,11},{8,12},{9,13},{1... | collective-permute-start | bytes 983048 | tf_op jit(solution)/shard_map/ppermute | solution.py:34
  4.2 10.6 %collective-permute-start.3 = (bf16[1280,128]{1,0:T(8,128)(2,1)S(1)}, bf16[1280,128]{1,0:T(8,128)(2,1)S(1)}, u32[]{:S(2)}, u32[]{:S(2)}) collective-permute-start(bf16[1280,128]{1,0:T(8,128)(2,1)S(1)} %get-tuple-element.123.refs_0_), channel_id=1, source_target_pairs={{0,2},{1,3},{2,0},{3,1},{4,6},{5,7},{6,4},{7,5},{8,10},{9,11},{10,... | collective-permute-start | bytes 983048 | tf_op jit(solution)/shard_map/ppermute | solution.py:34
  5.7 1.9 %collective-permute-start.1 = (s32[256,2]{0,1:T(2,128)}, s32[256,2]{0,1:T(2,128)S(1)}, u32[]{:S(2)}, u32[]{:S(2)}) collective-permute-start(s32[256,2]{0,1:T(2,128)} %param.5), channel_id=1, source_target_pairs={{0,1},{1,0},{2,3},{3,2},{4,5},{5,4},{6,7},{7,6},{8,9},{9,8},{10,11... | collective-permute-start | bytes 6152 | tf_op jit(solution)/shard_map/ppermute | solution.py:34
  5.7 2.0 %collective-permute-start = (s32[1]{0:T(128)}, s32[1]{0:T(128)}, u32[]{:S(2)}, u32[]{:S(2)}) collective-permute-start(s32[1]{0:T(128)} %param.6), channel_id=1, source_target_pairs={{0,1},{1,0},{2,3},{3,2},{4,5},{5,4},{6,7},{7,6},{8,9},{9,8},{10,11... | collective-permute-start | bytes 20 | tf_op jit(solution)/shard_map/ppermute | solution.py:34
  7.6 1.7 %collective-permute-start.8 = (bf16[1280,128]{1,0:T(8,128)(2,1)S(1)}, bf16[1280,128]{1,0:T(8,128)(2,1)S(1)}, u32[]{:S(2)}, u32[]{:S(2)}) collective-permute-start(bf16[1280,128]{1,0:T(8,128)(2,1)S(1)} %get-tuple-element.122), channel_id=1, source_target_pairs={{0,1},{1,0},{2,3},{3,2},{4,5},{5,4},{6,7},{7,6},{8,9},{9,8},{10,11... | collective-permute-start | bytes 983048 | tf_op jit(solution)/shard_map/ppermute | solution.py:34
  9.3 10.6 %copy-start.3 = (bf16[1280,128]{1,0:T(8,128)(2,1)}, bf16[1280,128]{1,0:T(8,128)(2,1)S(1)}, u32[]{:S(2)}) copy-start(bf16[1280,128]{1,0:T(8,128)(2,1)S(1)} %collective-permute-done.8.refs_1_) | copy-start | bytes 983044
  9.3 14.1 %collective-permute-start.10 = (bf16[1280,128]{1,0:T(8,128)(2,1)S(1)}, bf16[1280,128]{1,0:T(8,128)(2,1)S(1)}, u32[]{:S(2)}, u32[]{:S(2)}) collective-permute-start(bf16[1280,128]{1,0:T(8,128)(2,1)S(1)} %collective-permute-done.8.refs_1_), channel_id=1, source_target_pairs={{0,4},{1,5},{2,6},{3,7},{4,8},{5,9},{6,10},{7,11},{8,12},{9,13},{1... | collective-permute-start | bytes 983048 | tf_op jit(solution)/shard_map/ppermute | solution.py:34
  10.9 12.5 %collective-permute-start.11 = (bf16[1280,128]{1,0:T(8,128)(2,1)S(1)}, bf16[1280,128]{1,0:T(8,128)(2,1)S(1)}, u32[]{:S(2)}, u32[]{:S(2)}) collective-permute-start(bf16[1280,128]{1,0:T(8,128)(2,1)S(1)} %collective-permute-done.8.refs_1_), channel_id=1, source_target_pairs={{0,2},{1,3},{2,0},{3,1},{4,6},{5,7},{6,4},{7,5},{8,10},{9,11},{10,... | collective-permute-start | bytes 983048 | tf_op jit(solution)/shard_map/ppermute | solution.py:34
  14.8 14.0 %collective-permute-start.4 = (bf16[1280,128]{1,0:T(8,128)(2,1)S(1)}, bf16[1280,128]{1,0:T(8,128)(2,1)S(1)}, u32[]{:S(2)}, u32[]{:S(2)}) collective-permute-start(bf16[1280,128]{1,0:T(8,128)(2,1)S(1)} %collective-permute-done.2.refs_0_), channel_id=1, source_target_pairs={{0,4},{1,5},{2,6},{3,7},{4,8},{5,9},{6,10},{7,11},{8,12},{9,13},{1... | collective-permute-start | bytes 983048 | tf_op jit(solution)/shard_map/ppermute | solution.py:34
  16.3 12.6 %collective-permute-start.5 = (bf16[1280,128]{1,0:T(8,128)(2,1)S(1)}, bf16[1280,128]{1,0:T(8,128)(2,1)}, u32[]{:S(2)}, u32[]{:S(2)}) collective-permute-start(bf16[1280,128]{1,0:T(8,128)(2,1)S(1)} %collective-permute-done.2.refs_0_), channel_id=1, source_target_pairs={{0,2},{1,3},{2,0},{3,1},{4,6},{5,7},{6,4},{7,5},{8,10},{9,11},{10,... | collective-permute-start | bytes 983048 | tf_op jit(solution)/shard_map/ppermute | solution.py:34
  23.3 0.7 copy-start
  24.1 12.6 %collective-permute-start.12 = (bf16[1280,128]{1,0:T(8,128)(2,1)S(1)}, bf16[1280,128]{1,0:T(8,128)(2,1)}, u32[]{:S(2)}, u32[]{:S(2)}) collective-permute-start(bf16[1280,128]{1,0:T(8,128)(2,1)S(1)} %collective-permute-done.10.refs_1_), channel_id=1, source_target_pairs={{0,4},{1,5},{2,6},{3,7},{4,8},{5,9},{6,10},{7,11},{8,12},{9,13},{1... | collective-permute-start | bytes 983048 | tf_op jit(solution)/shard_map/ppermute | solution.py:34
  25.6 11.0 %collective-permute-start.13 = (bf16[1280,128]{1,0:T(8,128)(2,1)S(1)}, bf16[1280,128]{1,0:T(8,128)(2,1)}, u32[]{:S(2)}, u32[]{:S(2)}) collective-permute-start(bf16[1280,128]{1,0:T(8,128)(2,1)S(1)} %collective-permute-done.10.refs_1_), channel_id=1, source_target_pairs={{0,2},{1,3},{2,0},{3,1},{4,6},{5,7},{6,4},{7,5},{8,10},{9,11},{10,... | collective-permute-start | bytes 983048 | tf_op jit(solution)/shard_map/ppermute | solution.py:34
  27.2 16.3 %copy-start.1 = (bf16[1280,128]{1,0:T(8,128)(2,1)S(1)}, bf16[1280,128]{1,0:T(8,128)(2,1)}, u32[]{:S(2)}) copy-start(bf16[1280,128]{1,0:T(8,128)(2,1)} %copy-done) | copy-start | bytes 983044
  28.9 14.6 %collective-permute-start.6 = (bf16[1280,128]{1,0:T(8,128)(2,1)S(1)}, bf16[1280,128]{1,0:T(8,128)(2,1)S(1)}, u32[]{:S(2)}, u32[]{:S(2)}) collective-permute-start(bf16[1280,128]{1,0:T(8,128)(2,1)S(1)} %collective-permute-done.4.refs_0_), channel_id=1, source_target_pairs={{0,4},{1,5},{2,6},{3,7},{4,8},{5,9},{6,10},{7,11},{8,12},{9,13},{1... | collective-permute-start | bytes 983048 | tf_op jit(solution)/shard_map/ppermute | solution.py:34
  30.5 13.1 %collective-permute-start.7 = (bf16[1280,128]{1,0:T(8,128)(2,1)S(1)}, bf16[1280,128]{1,0:T(8,128)(2,1)S(1)}, u32[]{:S(2)}, u32[]{:S(2)}) collective-permute-start(bf16[1280,128]{1,0:T(8,128)(2,1)S(1)} %collective-permute-done.4.refs_0_), channel_id=1, source_target_pairs={{0,2},{1,3},{2,0},{3,1},{4,6},{5,7},{6,4},{7,5},{8,10},{9,11},{10,... | collective-permute-start | bytes 983048 | tf_op jit(solution)/shard_map/ppermute | solution.py:34
  36.6 13.5 %collective-permute-start.15 = (bf16[1280,128]{1,0:T(8,128)(2,1)}, bf16[1280,128]{1,0:T(8,128)(2,1)S(1)}, u32[]{:S(2)}, u32[]{:S(2)}) collective-permute-start(bf16[1280,128]{1,0:T(8,128)(2,1)} %collective-permute-done.12.refs_1_), channel_id=1, source_target_pairs={{0,4},{1,5},{2,6},{3,7},{4,8},{5,9},{6,10},{7,11},{8,12},{9,13},{1... | collective-permute-start | bytes 983048 | tf_op jit(solution)/shard_map/ppermute | solution.py:34
  37.5 12.7 %collective-permute-start.16 = (bf16[1280,128]{1,0:T(8,128)(2,1)}, bf16[1280,128]{1,0:T(8,128)(2,1)S(1)}, u32[]{:S(2)}, u32[]{:S(2)}) collective-permute-start(bf16[1280,128]{1,0:T(8,128)(2,1)} %collective-permute-done.12.refs_1_), channel_id=1, source_target_pairs={{0,2},{1,3},{2,0},{3,1},{4,6},{5,7},{6,4},{7,5},{8,10},{9,11},{10,... | collective-permute-start | bytes 983048 | tf_op jit(solution)/shard_map/ppermute | solution.py:34
  46.4 11.6 %collective-permute-start.14 = (bf16[1280,128]{1,0:T(8,128)(2,1)S(1)}, bf16[1280,128]{1,0:T(8,128)(2,1)S(1)}, u32[]{:S(2)}, u32[]{:S(2)}) collective-permute-start(bf16[1280,128]{1,0:T(8,128)(2,1)S(1)} %collective-permute-done.7.refs_2_), channel_id=1, source_target_pairs={{0,4},{1,5},{2,6},{3,7},{4,8},{5,9},{6,10},{7,11},{8,12},{9,13},{1... | collective-permute-start | bytes 983048 | tf_op jit(solution)/shard_map/ppermute | solution.py:34
  50.2 8.7 %collective-permute-start.17 = (bf16[1280,128]{1,0:T(8,128)(2,1)S(1)}, bf16[1280,128]{1,0:T(8,128)(2,1)S(1)}, u32[]{:S(2)}, u32[]{:S(2)}) collective-permute-start(bf16[1280,128]{1,0:T(8,128)(2,1)S(1)} %collective-permute-done.15.refs_1_), channel_id=1, source_target_pairs={{0,2},{1,3},{2,0},{3,1},{4,6},{5,7},{6,4},{7,5},{8,10},{9,11},{10,... | collective-permute-start | bytes 983048 | tf_op jit(solution)/shard_map/ppermute | solution.py:34
  61.6 1.7 %collective-permute-start.18 = (bf16[1280,128]{1,0:T(8,128)(2,1)S(1)}, bf16[1280,128]{1,0:T(8,128)(2,1)S(1)}, u32[]{:S(2)}, u32[]{:S(2)}) collective-permute-start(bf16[1280,128]{1,0:T(8,128)(2,1)S(1)} %bitcast.73), channel_id=1, source_target_pairs={{0,1},{1,0},{2,3},{3,2},{4,5},{5,4},{6,7},{7,6},{8,9},{9,8},{10,11... | collective-permute-start | bytes 983048 | tf_op jit(solution)/shard_map/ppermute | solution.py:34
  61.6 2.1 %collective-permute-start.19 = (bf16[1280,128]{1,0:T(8,128)(2,1)S(1)}, bf16[1280,128]{1,0:T(8,128)(2,1)S(1)}, u32[]{:S(2)}, u32[]{:S(2)}) collective-permute-start(bf16[1280,128]{1,0:T(8,128)(2,1)S(1)} %bitcast.72), channel_id=1, source_target_pairs={{0,1},{1,0},{2,3},{3,2},{4,5},{5,4},{6,7},{7,6},{8,9},{9,8},{10,11... | collective-permute-start | bytes 983048 | tf_op jit(solution)/shard_map/ppermute | solution.py:34
  63.9 11.7 %collective-permute-start.24 = (bf16[1280,128]{1,0:T(8,128)(2,1)S(1)}, bf16[1280,128]{1,0:T(8,128)(2,1)S(1)}, u32[]{:S(2)}, u32[]{:S(2)}) collective-permute-start(bf16[1280,128]{1,0:T(8,128)(2,1)S(1)} %get-tuple-element.100), channel_id=1, source_target_pairs={{0,2},{1,3},{2,0},{3,1},{4,6},{5,7},{6,4},{7,5},{8,10},{9,11},{10,... | collective-permute-start | bytes 983048 | tf_op jit(solution)/shard_map/ppermute | solution.py:34
  67.1 9.0 %collective-permute-start.23 = (bf16[1280,128]{1,0:T(8,128)(2,1)S(1)}, bf16[1280,128]{1,0:T(8,128)(2,1)S(1)}, u32[]{:S(2)}, u32[]{:S(2)}) collective-permute-start(bf16[1280,128]{1,0:T(8,128)(2,1)S(1)} %bitcast.71), channel_id=1, source_target_pairs={{0,1},{1,0},{2,3},{3,2},{4,5},{5,4},{6,7},{7,6},{8,9},{9,8},{10,11... | collective-permute-start | bytes 983048 | tf_op jit(solution)/shard_map/ppermute | solution.py:34
  67.2 8.4 %collective-permute-start.25 = (bf16[640,128]{1,0:T(8,128)(2,1)S(1)}, bf16[640,128]{1,0:T(8,128)(2,1)S(1)}, u32[]{:S(2)}, u32[]{:S(2)}) collective-permute-start(bf16[640,128]{1,0:T(8,128)(2,1)S(1)} %get-tuple-element.101), channel_id=1, source_target_pairs={{0,4},{1,5},{2,6},{3,7},{4,8},{5,9},{6,10},{7,11},{8,12},{9,13},{1... | collective-permute-start | bytes 491528 | tf_op jit(solution)/shard_map/ppermute | solution.py:34
  67.6 8.7 %collective-permute-start.22 = (bf16[1280,128]{1,0:T(8,128)(2,1)S(1)}, bf16[1280,128]{1,0:T(8,128)(2,1)S(1)}, u32[]{:S(2)}, u32[]{:S(2)}) collective-permute-start(bf16[1280,128]{1,0:T(8,128)(2,1)S(1)} %bitcast.70), channel_id=1, source_target_pairs={{0,1},{1,0},{2,3},{3,2},{4,5},{5,4},{6,7},{7,6},{8,9},{9,8},{10,11... | collective-permute-start | bytes 983048 | tf_op jit(solution)/shard_map/ppermute | solution.py:34
  67.8 10.1 %collective-permute-start.21 = (bf16[1280,128]{1,0:T(8,128)(2,1)S(1)}, bf16[1280,128]{1,0:T(8,128)(2,1)S(1)}, u32[]{:S(2)}, u32[]{:S(2)}) collective-permute-start(bf16[1280,128]{1,0:T(8,128)(2,1)S(1)} %bitcast.68), channel_id=1, source_target_pairs={{0,1},{1,0},{2,3},{3,2},{4,5},{5,4},{6,7},{7,6},{8,9},{9,8},{10,11... | collective-permute-start | bytes 983048 | tf_op jit(solution)/shard_map/ppermute | solution.py:34
  75.6 1.6 %collective-permute-start.29 = (bf16[1280,128]{1,0:T(8,128)(2,1)S(1)}, bf16[1280,128]{1,0:T(8,128)(2,1)S(1)}, u32[]{:S(2)}, u32[]{:S(2)}) collective-permute-start(bf16[1280,128]{1,0:T(8,128)(2,1)S(1)} %bitcast.69), channel_id=1, source_target_pairs={{0,1},{1,0},{2,3},{3,2},{4,5},{5,4},{6,7},{7,6},{8,9},{9,8},{10,11... | collective-permute-start | bytes 983048 | tf_op jit(solution)/shard_map/ppermute | solution.py:34
  75.6 14.9 %collective-permute-start.32 = (bf16[1280,128]{1,0:T(8,128)(2,1)S(1)}, bf16[1280,128]{1,0:T(8,128)(2,1)S(1)}, u32[]{:S(2)}, u32[]{:S(2)}) collective-permute-start(bf16[1280,128]{1,0:T(8,128)(2,1)S(1)} %bitcast.67), channel_id=1, source_target_pairs={{0,1},{1,0},{2,3},{3,2},{4,5},{5,4},{6,7},{7,6},{8,9},{9,8},{10,11... | collective-permute-start | bytes 983048 | tf_op jit(solution)/shard_map/ppermute | solution.py:34
  76.1 18.2 %collective-permute-start.20 = (bf16[1280,128]{1,0:T(8,128)(2,1)S(1)}, bf16[1280,128]{1,0:T(8,128)(2,1)S(1)}, u32[]{:S(2)}, u32[]{:S(2)}) collective-permute-start(bf16[1280,128]{1,0:T(8,128)(2,1)S(1)} %bitcast.66), channel_id=1, source_target_pairs={{0,1},{1,0},{2,3},{3,2},{4,5},{5,4},{6,7},{7,6},{8,9},{9,8},{10,11... | collective-permute-start | bytes 983048 | tf_op jit(solution)/shard_map/ppermute | solution.py:34
  76.4 11.9 %collective-permute-start.26 = (bf16[1280,128]{1,0:T(8,128)(2,1)S(1)}, bf16[1280,128]{1,0:T(8,128)(2,1)S(1)}, u32[]{:S(2)}, u32[]{:S(2)}) collective-permute-start(bf16[1280,128]{1,0:T(8,128)(2,1)S(1)} %fusion.6), channel_id=1, source_target_pairs={{0,4},{1,5},{2,6},{3,7},{4,8},{5,9},{6,10},{7,11},{8,12},{9,13},{1... | collective-permute-start | bytes 983048 | tf_op jit(solution)/shard_map/ppermute | solution.py:34
  77.2 7.0 %collective-permute-start.27 = (bf16[640,128]{1,0:T(8,128)(2,1)S(1)}, bf16[640,128]{1,0:T(8,128)(2,1)S(1)}, u32[]{:S(2)}, u32[]{:S(2)}) collective-permute-start(bf16[640,128]{1,0:T(8,128)(2,1)S(1)} %get-tuple-element.105), channel_id=1, source_target_pairs={{0,2},{1,3},{2,0},{3,1},{4,6},{5,7},{6,4},{7,5},{8,10},{9,11},{10,... | collective-permute-start | bytes 491528 | tf_op jit(solution)/shard_map/ppermute | solution.py:34
  77.9 12.6 %collective-permute-start.30 = (bf16[1280,128]{1,0:T(8,128)(2,1)S(1)}, bf16[1280,128]{1,0:T(8,128)(2,1)S(1)}, u32[]{:S(2)}, u32[]{:S(2)}) collective-permute-start(bf16[1280,128]{1,0:T(8,128)(2,1)S(1)} %fusion.4), channel_id=1, source_target_pairs={{0,2},{1,3},{2,0},{3,1},{4,6},{5,7},{6,4},{7,5},{8,10},{9,11},{10,... | collective-permute-start | bytes 983048 | tf_op jit(solution)/shard_map/ppermute | solution.py:34
  88.5 12.5 %collective-permute-start.28 = (bf16[1280,128]{1,0:T(8,128)(2,1)S(1)}, bf16[1280,128]{1,0:T(8,128)(2,1)S(1)}, u32[]{:S(2)}, u32[]{:S(2)}) collective-permute-start(bf16[1280,128]{1,0:T(8,128)(2,1)S(1)} %fusion.9), channel_id=1, source_target_pairs={{0,4},{1,5},{2,6},{3,7},{4,8},{5,9},{6,10},{7,11},{8,12},{9,13},{1... | collective-permute-start | bytes 983048 | tf_op jit(solution)/shard_map/ppermute | solution.py:34
  90.7 16.0 %collective-permute-start.33 = (bf16[1280,128]{1,0:T(8,128)(2,1)S(1)}, bf16[1280,128]{1,0:T(8,128)(2,1)S(1)}, u32[]{:S(2)}, u32[]{:S(2)}) collective-permute-start(bf16[1280,128]{1,0:T(8,128)(2,1)S(1)} %fusion.3), channel_id=1, source_target_pairs={{0,12},{1,13},{2,14},{3,15},{4,0},{5,1},{6,2},{7,3},{8,4},{9,5},{1... | collective-permute-start | bytes 983048 | tf_op jit(solution)/shard_map/ppermute | solution.py:34
  93.8 12.9 %collective-permute-start.31 = (bf16[1280,128]{1,0:T(8,128)(2,1)S(1)}, bf16[1280,128]{1,0:T(8,128)(2,1)S(1)}, u32[]{:S(2)}, u32[]{:S(2)}) collective-permute-start(bf16[1280,128]{1,0:T(8,128)(2,1)S(1)} %add_convert_fusion), channel_id=1, source_target_pairs={{0,2},{1,3},{2,0},{3,1},{4,6},{5,7},{6,4},{7,5},{8,10},{9,11},{10,... | collective-permute-start | bytes 983048 | tf_op jit(solution)/shard_map/ppermute | solution.py:34

commit v23 on v16

--- a/solution.py
+++ b/solution.py
@@ -12,6 +12,7 @@
 WIN = 128
 LANES = 128
 UNROLL = 16
+TAIL = 2 * BLK
 LINE = 4
 SCOPED_BYTES = 6 * 1024 * 1024
 
@@ -116,7 +117,7 @@
     begin, end = bounds_ref[stage], bounds_ref[stage + 1]
     low = lax.broadcasted_iota(jnp.int32, tiles.shape[1:], 1) < BLK
     zero = jnp.zeros(tiles.shape[1:], jnp.bfloat16)
-    spill = half.shape[0] - BLK
+    spill = half.shape[0] - TAIL
     entries = table_ref.shape[0] // (2 + pieces)
     piece = BLK // pieces
 
@@ -141,7 +142,7 @@
 
 
 def fill_window(half, weights, shard, chips_ref, first, parity, out):
-    side_rows = (half.shape[0] - BLK) // 2
+    side_rows = (half.shape[0] - TAIL) // 2
 
     @pl.loop(0, out.shape[0])
     def _(index):
@@ -189,7 +190,7 @@
 
 def window_kernel(stage, count, pieces, shard, plan, table_ref, bounds_ref, chips_ref, core_ref, *refs):
     half, (weights, *outs) = add_stage(stage, count, pieces, table_ref, bounds_ref, refs)
-    side_rows = (half.shape[0] - BLK) // 2
+    side_rows = (half.shape[0] - TAIL) // 2
     for side in range(2):
         weights[pl.ds(side * LANES, LANES), :] = half[pl.ds(side * side_rows, WIN), :].T.astype(jnp.bfloat16)
     rest_kernel(shard, plan, False, chips_ref, core_ref, half, weights, *outs)
@@ -286,7 +287,7 @@
     bounds = jnp.sum((stage[None, :] < jnp.arange(stage_count + 1)[:, None]).astype(jnp.int32), axis=1)
     cores = core.astype(jnp.int32).reshape(1)
 
-    half_type = pltpu.VMEM((2 * total + BLK, LANES), jnp.float32)
+    half_type = pltpu.VMEM((2 * total + TAIL, LANES), jnp.float32)
     tiles_type = pltpu.VMEM((2 * slots, BLK * BLK // LANES, LANES), jnp.bfloat16)
     work = 4 * slots * BLK * BLK * LANES // stage_count
     state = []

time: 105 us -> 105 us (level)
  Pallas kernels: 19.4 us -> 20.5 us
    pallas_call x8, Pallas kernels: 19.4 us -> 20.5 us  [call(): pl.pallas_call(kernel, out_shape=outs, in_specs=in_specs, out_specs=[VMEM...]
  transfers between devices with their start and end apart: 36 -> 36, of which waited for: 17 -> 17; matrix products, arithmetic and copies ran while one was open for 10% -> 10% of each run, Pallas kernels for 16% -> 17%
where the time goes in v23:
time: 105 us
  waiting for transfers between devices  39.6 us (38%)
  starting transfers between devices  31.1 us (30%)
  Pallas kernels  20.5 us (20%)
  local copies, waits for them, and re-layouts  8.14 us (8%)
  other arithmetic  4.21 us (4%)
    ppermute x36, waiting for transfers between devices, move(): return lax.ppermute(array, 'aux', pairs)  39.6 us
    ppermute x36, starting transfers between devices, move(): return lax.ppermute(array, 'aux', pairs)  31.1 us
    pallas_call x8, Pallas kernels, call(): pl.pallas_call(kernel, out_shape=outs, in_specs=in_specs, out_specs=[VMEM...  20.5 us
    unnamed x11, local copies, waits for them, and re-layouts  6.92 us
  transfers between devices with their start and end apart: 36, of which 17 were waited for; matrix products, arithmetic and copies ran while one was open for 10% of the time, Pallas kernels for 17%

profile of v23, /device:TPU:0, one launch (start us, length us, event | category | flops | bytes accessed | tf_op | source)
XLA Modules:
  0.0 104.6 jit_solution(12443572320079147498)
XLA Ops:
  0.0 0.5 collective-permute-start.9
  0.5 1.1 %constant_dynamic-slice_fusion.1 = (bf16[1280,128]{1,0:T(8,128)(2,1)S(1)}, bf16[1280,128]{1,0:T(8,128)(2,1)S(1)}) fusion(bf16[1280,256]{1,0:T(8,128)(2,1)} %param.7, s32[]{:T(128)S(6)} %select_n.162, s32[]{:T(128)S(6)} %select_n.161), kind=kLoop, calls=%fused_computation.91 | loop fusion | bytes 1310728 | tf_op jit(solution)/shard_map/dynamic_slice | solution.py:245
  1.6 2.6 %collective-permute-start.2 = (bf16[1280,128]{1,0:T(8,128)(2,1)S(1)}, bf16[1280,128]{1,0:T(8,128)(2,1)S(1)}, u32[]{:S(2)}, u32[]{:S(2)}) collective-permute-start(bf16[1280,128]{1,0:T(8,128)(2,1)S(1)} %get-tuple-element.119.refs_0_), channel_id=1, source_target_pairs={{0,4},{1,5},{2,6},{3,7},{4,8},{5,9},{6,10},{7,11},{8,12},{9,13},{1... | collective-permute-start | bytes 983048 | tf_op jit(solution)/shard_map/ppermute | solution.py:35
  4.2 1.5 %collective-permute-start.3 = (bf16[1280,128]{1,0:T(8,128)(2,1)S(1)}, bf16[1280,128]{1,0:T(8,128)(2,1)S(1)}, u32[]{:S(2)}, u32[]{:S(2)}) collective-permute-start(bf16[1280,128]{1,0:T(8,128)(2,1)S(1)} %get-tuple-element.119.refs_0_), channel_id=1, source_target_pairs={{0,2},{1,3},{2,0},{3,1},{4,6},{5,7},{6,4},{7,5},{8,10},{9,11},{10,... | collective-permute-start | bytes 983048 | tf_op jit(solution)/shard_map/ppermute | solution.py:35
  5.7 0.5 collective-permute-start
  6.2 0.7 constant_dynamic-update-slice_fusion.1
  7.7 0.7 compare_select_fusion.3
  8.4 0.8 collective-permute-done.8.refs_1_
  9.3 1.6 %collective-permute-start.10 = (bf16[1280,128]{1,0:T(8,128)(2,1)S(1)}, bf16[1280,128]{1,0:T(8,128)(2,1)S(1)}, u32[]{:S(2)}, u32[]{:S(2)}) collective-permute-start(bf16[1280,128]{1,0:T(8,128)(2,1)S(1)} %collective-permute-done.8.refs_1_), channel_id=1, source_target_pairs={{0,4},{1,5},{2,6},{3,7},{4,8},{5,9},{6,10},{7,11},{8,12},{9,13},{1... | collective-permute-start | bytes 983048 | tf_op jit(solution)/shard_map/ppermute | solution.py:35
  10.9 0.5 collective-permute-start.11
  11.4 0.7 fusion.27
  12.1 2.7 %collective-permute-done.2.refs_0_ = bf16[1280,128]{1,0:T(8,128)(2,1)S(1)} collective-permute-done((bf16[1280,128]{1,0:T(8,128)(2,1)S(1)}, bf16[1280,128]{1,0:T(8,128)(2,1)S(1)}, u32[]{:S(2)}, u32[]{:S(2)}) %collective-permute-start.2) | collective-permute-done | bytes 327712 | tf_op jit(solution)/shard_map/ppermute | solution.py:35
  14.8 1.5 %collective-permute-start.4 = (bf16[1280,128]{1,0:T(8,128)(2,1)S(1)}, bf16[1280,128]{1,0:T(8,128)(2,1)S(1)}, u32[]{:S(2)}, u32[]{:S(2)}) collective-permute-start(bf16[1280,128]{1,0:T(8,128)(2,1)S(1)} %collective-permute-done.2.refs_0_), channel_id=1, source_target_pairs={{0,4},{1,5},{2,6},{3,7},{4,8},{5,9},{6,10},{7,11},{8,12},{9,13},{1... | collective-permute-start | bytes 983048 | tf_op jit(solution)/shard_map/ppermute | solution.py:35
  16.3 1.5 %collective-permute-start.5 = (bf16[1280,128]{1,0:T(8,128)(2,1)S(1)}, bf16[1280,128]{1,0:T(8,128)(2,1)}, u32[]{:S(2)}, u32[]{:S(2)}) collective-permute-start(bf16[1280,128]{1,0:T(8,128)(2,1)S(1)} %collective-permute-done.2.refs_0_), channel_id=1, source_target_pairs={{0,2},{1,3},{2,0},{3,1},{4,6},{5,7},{6,4},{7,5},{8,10},{9,11},{10,... | collective-permute-start | bytes 983048 | tf_op jit(solution)/shard_map/ppermute | solution.py:35
  17.8 2.1 %copy.9 = bf16[32,8,32,128]{3,2,1,0:T(8,128)(2,1)S(1)} copy(bf16[32,8,32,128]{3,1,2,0:T(8,128)(2,1)} %bitcast.63) | data formatting | bytes 4194304
  19.9 3.4 %copy.10 = bf16[32,8,32,128]{3,2,1,0:T(8,128)(2,1)} copy(bf16[32,8,32,128]{3,1,2,0:T(8,128)(2,1)} %bitcast.25) | data formatting | bytes 4194304
  23.3 0.7 copy-done
  24.1 1.6 %collective-permute-start.12 = (bf16[1280,128]{1,0:T(8,128)(2,1)S(1)}, bf16[1280,128]{1,0:T(8,128)(2,1)}, u32[]{:S(2)}, u32[]{:S(2)}) collective-permute-start(bf16[1280,128]{1,0:T(8,128)(2,1)S(1)} %collective-permute-done.10.refs_1_), channel_id=1, source_target_pairs={{0,4},{1,5},{2,6},{3,7},{4,8},{5,9},{6,10},{7,11},{8,12},{9,13},{1... | collective-permute-start | bytes 983048 | tf_op jit(solution)/shard_map/ppermute | solution.py:35
  25.7 0.5 collective-permute-start.13
  26.2 0.3 convert_reduce_fusion
  26.5 0.5 select_reduce_fusion
  27.1 0.1 convert_reduce_fusion.1.bounds_ref
  27.2 1.6 %collective-permute-done.4.refs_0_ = bf16[1280,128]{1,0:T(8,128)(2,1)S(1)} collective-permute-done((bf16[1280,128]{1,0:T(8,128)(2,1)S(1)}, bf16[1280,128]{1,0:T(8,128)(2,1)S(1)}, u32[]{:S(2)}, u32[]{:S(2)}) %collective-permute-start.4) | collective-permute-done | bytes 327712 | tf_op jit(solution)/shard_map/ppermute | solution.py:35
  28.9 1.6 %collective-permute-start.6 = (bf16[1280,128]{1,0:T(8,128)(2,1)S(1)}, bf16[1280,128]{1,0:T(8,128)(2,1)S(1)}, u32[]{:S(2)}, u32[]{:S(2)}) collective-permute-start(bf16[1280,128]{1,0:T(8,128)(2,1)S(1)} %collective-permute-done.4.refs_0_), channel_id=1, source_target_pairs={{0,4},{1,5},{2,6},{3,7},{4,8},{5,9},{6,10},{7,11},{8,12},{9,13},{1... | collective-permute-start | bytes 983048 | tf_op jit(solution)/shard_map/ppermute | solution.py:35
  30.5 1.5 %collective-permute-start.7 = (bf16[1280,128]{1,0:T(8,128)(2,1)S(1)}, bf16[1280,128]{1,0:T(8,128)(2,1)S(1)}, u32[]{:S(2)}, u32[]{:S(2)}) collective-permute-start(bf16[1280,128]{1,0:T(8,128)(2,1)S(1)} %collective-permute-done.4.refs_0_), channel_id=1, source_target_pairs={{0,2},{1,3},{2,0},{3,1},{4,6},{5,7},{6,4},{7,5},{8,10},{9,11},{10,... | collective-permute-start | bytes 983048 | tf_op jit(solution)/shard_map/ppermute | solution.py:35
  32.0 3.4 %shard_map.46 = (f32[41088,128]{1,0:T(8,128)S(1)}, bf16[512,32,128]{2,1,0:T(8,128)(2,1)S(1)}) custom-call(s32[1584]{0:T(1024)S(1)} %concatenate.10.table_ref, s32[6]{0:T(128)S(1)} %convert_reduce_fusion.1.bounds_ref, bf16[1280,128]{1,0:T(8,128)(2,1)} %copy-done.2, bf16[1280,128]{1,0:T(8,128)(2,1)} %copy-done.3, bf16[256,32,128]{2,1,0:T(8,128)(2,1)S(1)} %bitcast.53, ...), custom_call_target="tpu_custom_call" | custom-call | flops 107374184 | bytes 4194304 | tf_op jit(solution)/shard_map/pallas_call | solution.py:218
  35.3 1.3 %collective-permute-done.12.refs_1_ = bf16[1280,128]{1,0:T(8,128)(2,1)} collective-permute-done((bf16[1280,128]{1,0:T(8,128)(2,1)S(1)}, bf16[1280,128]{1,0:T(8,128)(2,1)}, u32[]{:S(2)}, u32[]{:S(2)}) %collective-permute-start.12) | collective-permute-done | bytes 327712 | tf_op jit(solution)/shard_map/ppermute | solution.py:35
  36.6 0.9 collective-permute-start.15
  37.5 1.5 %collective-permute-start.16 = (bf16[1280,128]{1,0:T(8,128)(2,1)}, bf16[1280,128]{1,0:T(8,128)(2,1)S(1)}, u32[]{:S(2)}, u32[]{:S(2)}) collective-permute-start(bf16[1280,128]{1,0:T(8,128)(2,1)} %collective-permute-done.12.refs_1_), channel_id=1, source_target_pairs={{0,2},{1,3},{2,0},{3,1},{4,6},{5,7},{6,4},{7,5},{8,10},{9,11},{10,... | collective-permute-start | bytes 983048 | tf_op jit(solution)/shard_map/ppermute | solution.py:35
  39.0 4.5 %collective-permute-done.6.refs_0_ = bf16[1280,128]{1,0:T(8,128)(2,1)S(1)} collective-permute-done((bf16[1280,128]{1,0:T(8,128)(2,1)S(1)}, bf16[1280,128]{1,0:T(8,128)(2,1)S(1)}, u32[]{:S(2)}, u32[]{:S(2)}) %collective-permute-start.6) | collective-permute-done | bytes 327712 | tf_op jit(solution)/shard_map/ppermute | solution.py:35
  43.6 2.8 %shard_map.47.refs_5_ = f32[41088,128]{1,0:T(8,128)S(1)} custom-call(s32[1584]{0:T(1024)S(1)} %concatenate.10.table_ref, s32[6]{0:T(128)S(1)} %convert_reduce_fusion.1.bounds_ref, bf16[1280,128]{1,0:T(8,128)(2,1)S(1)} %collective-permute-done.2.refs_0_, bf16[1280,128]{1,0:T(8,128)(2,1)S(1)} %collective-permute-done.10.refs_1_, ...), custom_call_target="tpu_custom_call", output_to_operand_aliasing={{}: (7, {})} | custom-call | flops 107374184 | bytes 4194304 | tf_op jit(solution)/shard_map/pallas_call | solution.py:218
  46.4 0.4 collective-permute-start.14
  46.7 3.5 %collective-permute-done.15.refs_1_ = bf16[1280,128]{1,0:T(8,128)(2,1)S(1)} collective-permute-done((bf16[1280,128]{1,0:T(8,128)(2,1)}, bf16[1280,128]{1,0:T(8,128)(2,1)S(1)}, u32[]{:S(2)}, u32[]{:S(2)}) %collective-permute-start.15) | collective-permute-done | bytes 327712 | tf_op jit(solution)/shard_map/ppermute | solution.py:35
  50.2 1.1 %collective-permute-start.17 = (bf16[1280,128]{1,0:T(8,128)(2,1)S(1)}, bf16[1280,128]{1,0:T(8,128)(2,1)S(1)}, u32[]{:S(2)}, u32[]{:S(2)}) collective-permute-start(bf16[1280,128]{1,0:T(8,128)(2,1)S(1)} %collective-permute-done.15.refs_1_), channel_id=1, source_target_pairs={{0,2},{1,3},{2,0},{3,1},{4,6},{5,7},{6,4},{7,5},{8,10},{9,11},{10,... | collective-permute-start | bytes 983048 | tf_op jit(solution)/shard_map/ppermute | solution.py:35
  51.2 4.2 %shard_map.48.refs_5_ = f32[41088,128]{1,0:T(8,128)S(1)} custom-call(s32[1584]{0:T(1024)S(1)} %concatenate.10.table_ref, s32[6]{0:T(128)S(1)} %convert_reduce_fusion.1.bounds_ref, bf16[1280,128]{1,0:T(8,128)(2,1)S(1)} %collective-permute-done.4.refs_0_, bf16[1280,128]{1,0:T(8,128)(2,1)} %collective-permute-done.12.refs_1_, ...), custom_call_target="tpu_custom_call", output_to_operand_aliasing={{}: (7, {})} | custom-call | flops 107374184 | bytes 4194304 | tf_op jit(solution)/shard_map/pallas_call | solution.py:218
  55.5 3.1 %shard_map.49.refs_3_ = f32[41088,128]{1,0:T(8,128)S(1)} custom-call(s32[1584]{0:T(1024)S(1)} %concatenate.10.table_ref, s32[6]{0:T(128)S(1)} %convert_reduce_fusion.1.bounds_ref, bf16[1280,128]{1,0:T(8,128)(2,1)S(1)} %collective-permute-done.6.refs_0_, bf16[1280,128]{1,0:T(8,128)(2,1)S(1)} %collective-permute-done.15.refs_1_, ...), custom_call_target="tpu_custom_call", output_to_operand_aliasing={{}: (7, {})} | custom-call | flops 107374184 | bytes 4194304 | tf_op jit(solution)/shard_map/pallas_call | solution.py:218
  58.5 0.4 collective-permute-done.17.refs_1_
  58.9 2.8 %shard_map.50 = (f32[41088,128]{1,0:T(8,128)S(1)}, bf16[256,128]{1,0:T(8,128)(2,1)S(1)}, bf16[1,1280,128]{2,1,0:T(8,128)(2,1)S(1)}, bf16[1,1280,128]{2,1,0:T(8,128)(2,1)S(1)}, bf16[1,1280,128]{2,1,0:T(8,128)(2,1)S(1)}) custom-call(s32[1584]{0:T(1024)S(1)} %concatenate.10.table_ref, ...), custom_call_target="tpu_custom_call", output_to_operand_aliasing={{0}: (7, {})} | custom-call | flops 359032416 | bytes 4194304 | tf_op jit(solution)/shard_map/pallas_call | solution.py:218
  61.8 0.5 collective-permute-start.19
  62.4 1.2 %shard_map.51 = (f32[1,1280,128]{2,1,0:T(8,128)S(1)}, f32[1,1280,128]{2,1,0:T(8,128)S(1)}, f32[1,1280,128]{2,1,0:T(8,128)S(1)}) custom-call(s32[8]{0:T(128)S(1)} %fusion.30.chips_ref, s32[1]{0:T(128)} %bitcast.core_ref, f32[41088,128]{1,0:T(8,128)S(1)} %get-tuple-element.87.half, bf16[256,128]{1,0:T(8,128)(2,1)S(1)} %get-tuple-element.82.weights), custom_call_target="tpu_custom_call" | custom-call | flops 251658240 | bytes 4194304 | tf_op jit(solution)/shard_map/pallas_call | solution.py:218
  63.6 0.3 collective-permute-done.19
  63.9 0.1 fusion.8
  64.1 1.6 %shard_map.53 = (bf16[1,1280,128]{2,1,0:T(8,128)(2,1)S(1)}, bf16[1,1280,128]{2,1,0:T(8,128)(2,1)S(1)}, bf16[1,1280,128]{2,1,0:T(8,128)(2,1)S(1)}, bf16[1,1280,12...) custom-call(s32[8]{0:T(128)S(1)} %fusion.30.chips_ref, s32[1]{0:T(128)} %bitcast.core_ref, ...), custom_call_target="tpu_custom_call" | custom-call | flops 419430400 | bytes 4194304 | tf_op jit(solution)/shard_map/pallas_call | solution.py:218
  65.6 0.2 collective-permute-start.21
  65.8 0.4 collective-permute-start.26
  66.2 1.7 %collective-permute-start.27 = (bf16[640,128]{1,0:T(8,128)(2,1)S(1)}, bf16[640,128]{1,0:T(8,128)(2,1)S(1)}, u32[]{:S(2)}, u32[]{:S(2)}) collective-permute-start(bf16[640,128]{1,0:T(8,128)(2,1)S(1)} %get-tuple-element.99), channel_id=1, source_target_pairs={{0,2},{1,3},{2,0},{3,1},{4,6},{5,7},{6,4},{7,5},{8,10},{9,11},{10,... | collective-permute-start | bytes 491528 | tf_op jit(solution)/shard_map/ppermute | solution.py:35
  67.9 0.3 collective-permute-start.23
  68.2 1.5 %shard_map.52 = (f32[1,1280,128]{2,1,0:T(8,128)S(1)}, f32[1,1280,128]{2,1,0:T(8,128)S(1)}, f32[1,1280,128]{2,1,0:T(8,128)S(1)}, f32[1,1280,128]{2,1,0:T(8,128)S(1)}, f32[1,1280,128]{2,1,0:T(8,128)S(1)}) custom-call(s32[8]{0:T(128)S(1)} %fusion.30.chips_ref, s32[1]{0:T(128)} %bitcast.core_ref, f32[41088,128]{1,0:T(8,128)S(1)} %get-tuple-element.87.half, ...), custom_call_target="tpu_custom_call" | custom-call | flops 419430400 | bytes 4194304 | tf_op jit(solution)/shard_map/pallas_call | solution.py:218
  69.9 0.6 collective-permute-start.31
  70.6 2.6 %collective-permute-done.27 = bf16[640,128]{1,0:T(8,128)(2,1)S(1)} collective-permute-done((bf16[640,128]{1,0:T(8,128)(2,1)S(1)}, bf16[640,128]{1,0:T(8,128)(2,1)S(1)}, u32[]{:S(2)}, u32[]{:S(2)}) %collective-permute-start.27) | collective-permute-done | bytes 163872 | tf_op jit(solution)/shard_map/ppermute | solution.py:35
  73.2 2.7 %collective-permute-done.23 = bf16[640,128]{1,0:T(8,128)(2,1)S(1)} collective-permute-done((bf16[640,128]{1,0:T(8,128)(2,1)S(1)}, bf16[640,128]{1,0:T(8,128)(2,1)S(1)}, u32[]{:S(2)}, u32[]{:S(2)}) %collective-permute-start.23) | collective-permute-done | bytes 163872 | tf_op jit(solution)/shard_map/ppermute | solution.py:35
  76.1 0.6 collective-permute-start.24
  76.7 5.6 %collective-permute-done.31 = bf16[1280,128]{1,0:T(8,128)(2,1)S(1)} collective-permute-done((bf16[1280,128]{1,0:T(8,128)(2,1)S(1)}, bf16[1280,128]{1,0:T(8,128)(2,1)S(1)}, u32[]{:S(2)}, u32[]{:S(2)}) %collective-permute-start.31) | collective-permute-done | bytes 327712 | tf_op jit(solution)/shard_map/ppermute | solution.py:35
  82.3 0.1 fusion.5
  82.4 1.8 %collective-permute-start.32 = (bf16[1280,128]{1,0:T(8,128)(2,1)S(1)}, bf16[1280,128]{1,0:T(8,128)(2,1)S(1)}, u32[]{:S(2)}, u32[]{:S(2)}) collective-permute-start(bf16[1280,128]{1,0:T(8,128)(2,1)S(1)} %fusion.6), channel_id=1, source_target_pairs={{0,2},{1,3},{2,0},{3,1},{4,6},{5,7},{6,4},{7,5},{8,10},{9,11},{10,... | collective-permute-start | bytes 983048 | tf_op jit(solution)/shard_map/ppermute | solution.py:35
  84.3 1.1 %collective-permute-done.24 = bf16[640,128]{1,0:T(8,128)(2,1)S(1)} collective-permute-done((bf16[640,128]{1,0:T(8,128)(2,1)S(1)}, bf16[640,128]{1,0:T(8,128)(2,1)S(1)}, u32[]{:S(2)}, u32[]{:S(2)}) %collective-permute-start.24) | collective-permute-done | bytes 163872 | tf_op jit(solution)/shard_map/ppermute | solution.py:35
  85.5 4.0 %collective-permute-done.28 = bf16[640,128]{1,0:T(8,128)(2,1)S(1)} collective-permute-done((bf16[640,128]{1,0:T(8,128)(2,1)S(1)}, bf16[640,128]{1,0:T(8,128)(2,1)S(1)}, u32[]{:S(2)}, u32[]{:S(2)}) %collective-permute-start.28) | collective-permute-done | bytes 163872 | tf_op jit(solution)/shard_map/ppermute | solution.py:35
  89.6 1.8 %collective-permute-done.32 = bf16[1280,128]{1,0:T(8,128)(2,1)S(1)} collective-permute-done((bf16[1280,128]{1,0:T(8,128)(2,1)S(1)}, bf16[1280,128]{1,0:T(8,128)(2,1)S(1)}, u32[]{:S(2)}, u32[]{:S(2)}) %collective-permute-start.32) | collective-permute-done | bytes 327712 | tf_op jit(solution)/shard_map/ppermute | solution.py:35
  91.4 0.1 fusion.3
  91.6 3.6 %collective-permute-start.35 = (bf16[1280,128]{1,0:T(8,128)(2,1)S(1)}, bf16[1280,128]{1,0:T(8,128)(2,1)S(1)}, u32[]{:S(2)}, u32[]{:S(2)}) collective-permute-start(bf16[1280,128]{1,0:T(8,128)(2,1)S(1)} %fusion.3), channel_id=1, source_target_pairs={{0,12},{1,13},{2,14},{3,15},{4,0},{5,1},{6,2},{7,3},{8,4},{9,5},{1... | collective-permute-start | bytes 983048 | tf_op jit(solution)/shard_map/ppermute | solution.py:35
  95.2 1.7 %collective-permute-start.33 = (bf16[1280,128]{1,0:T(8,128)(2,1)S(1)}, bf16[1280,128]{1,0:T(8,128)(2,1)S(1)}, u32[]{:S(2)}, u32[]{:S(2)}) collective-permute-start(bf16[1280,128]{1,0:T(8,128)(2,1)S(1)} %fusion.5), channel_id=1, source_target_pairs={{0,2},{1,3},{2,0},{3,1},{4,6},{5,7},{6,4},{7,5},{8,10},{9,11},{10,... | collective-permute-start | bytes 983048 | tf_op jit(solution)/shard_map/ppermute | solution.py:35
  96.9 1.6 %collective-permute-done.29 = bf16[640,128]{1,0:T(8,128)(2,1)S(1)} collective-permute-done((bf16[640,128]{1,0:T(8,128)(2,1)S(1)}, bf16[640,128]{1,0:T(8,128)(2,1)S(1)}, u32[]{:S(2)}, u32[]{:S(2)}) %collective-permute-start.29) | collective-permute-done | bytes 163872 | tf_op jit(solution)/shard_map/ppermute | solution.py:35
  98.7 5.0 %collective-permute-done.35 = bf16[1280,128]{1,0:T(8,128)(2,1)S(1)} collective-permute-done((bf16[1280,128]{1,0:T(8,128)(2,1)S(1)}, bf16[1280,128]{1,0:T(8,128)(2,1)S(1)}, u32[]{:S(2)}, u32[]{:S(2)}) %collective-permute-start.35) | collective-permute-done | bytes 327712 | tf_op jit(solution)/shard_map/ppermute | solution.py:35
  103.7 0.9 add_multiply_fusion
  (50 shorter events, 1.2 us)
Async XLA Ops:
  0.0 9.3 %collective-permute-start.9 = (bf16[256,4096]{1,0:T(8,128)(2,1)}, bf16[256,4096]{1,0:T(8,128)(2,1)}, u32[]{:S(2)}, u32[]{:S(2)}) collective-permute-start(bf16[256,4096]{1,0:T(8,128)(2,1)} %param.4), channel_id=1, source_target_pairs={{0,1},{1,0},{2,3},{3,2},{4,5},{5,4},{6,7},{7,6},{8,9},{9,8},{10,11... | collective-permute-start | bytes 6291464 | tf_op jit(solution)/shard_map/ppermute | solution.py:35
  1.6 13.2 %copy-start.2 = (bf16[1280,128]{1,0:T(8,128)(2,1)}, bf16[1280,128]{1,0:T(8,128)(2,1)S(1)}, u32[]{:S(2)}) copy-start(bf16[1280,128]{1,0:T(8,128)(2,1)S(1)} %get-tuple-element.119.refs_0_) | copy-start | bytes 983044
  1.6 13.2 %collective-permute-start.2 = (bf16[1280,128]{1,0:T(8,128)(2,1)S(1)}, bf16[1280,128]{1,0:T(8,128)(2,1)S(1)}, u32[]{:S(2)}, u32[]{:S(2)}) collective-permute-start(bf16[1280,128]{1,0:T(8,128)(2,1)S(1)} %get-tuple-element.119.refs_0_), channel_id=1, source_target_pairs={{0,4},{1,5},{2,6},{3,7},{4,8},{5,9},{6,10},{7,11},{8,12},{9,13},{1... | collective-permute-start | bytes 983048 | tf_op jit(solution)/shard_map/ppermute | solution.py:35
  4.2 10.6 %collective-permute-start.3 = (bf16[1280,128]{1,0:T(8,128)(2,1)S(1)}, bf16[1280,128]{1,0:T(8,128)(2,1)S(1)}, u32[]{:S(2)}, u32[]{:S(2)}) collective-permute-start(bf16[1280,128]{1,0:T(8,128)(2,1)S(1)} %get-tuple-element.119.refs_0_), channel_id=1, source_target_pairs={{0,2},{1,3},{2,0},{3,1},{4,6},{5,7},{6,4},{7,5},{8,10},{9,11},{10,... | collective-permute-start | bytes 983048 | tf_op jit(solution)/shard_map/ppermute | solution.py:35
  5.7 1.9 %collective-permute-start.1 = (s32[256,2]{0,1:T(2,128)}, s32[256,2]{0,1:T(2,128)S(1)}, u32[]{:S(2)}, u32[]{:S(2)}) collective-permute-start(s32[256,2]{0,1:T(2,128)} %param.5), channel_id=1, source_target_pairs={{0,1},{1,0},{2,3},{3,2},{4,5},{5,4},{6,7},{7,6},{8,9},{9,8},{10,11... | collective-permute-start | bytes 6152 | tf_op jit(solution)/shard_map/ppermute | solution.py:35
  5.7 2.0 %collective-permute-start = (s32[1]{0:T(128)}, s32[1]{0:T(128)}, u32[]{:S(2)}, u32[]{:S(2)}) collective-permute-start(s32[1]{0:T(128)} %param.6), channel_id=1, source_target_pairs={{0,1},{1,0},{2,3},{3,2},{4,5},{5,4},{6,7},{7,6},{8,9},{9,8},{10,11... | collective-permute-start | bytes 20 | tf_op jit(solution)/shard_map/ppermute | solution.py:35
  7.6 1.7 %collective-permute-start.8 = (bf16[1280,128]{1,0:T(8,128)(2,1)S(1)}, bf16[1280,128]{1,0:T(8,128)(2,1)S(1)}, u32[]{:S(2)}, u32[]{:S(2)}) collective-permute-start(bf16[1280,128]{1,0:T(8,128)(2,1)S(1)} %get-tuple-element.118), channel_id=1, source_target_pairs={{0,1},{1,0},{2,3},{3,2},{4,5},{5,4},{6,7},{7,6},{8,9},{9,8},{10,11... | collective-permute-start | bytes 983048 | tf_op jit(solution)/shard_map/ppermute | solution.py:35
  9.3 10.6 %copy-start.3 = (bf16[1280,128]{1,0:T(8,128)(2,1)}, bf16[1280,128]{1,0:T(8,128)(2,1)S(1)}, u32[]{:S(2)}) copy-start(bf16[1280,128]{1,0:T(8,128)(2,1)S(1)} %collective-permute-done.8.refs_1_) | copy-start | bytes 983044
  9.3 14.1 %collective-permute-start.10 = (bf16[1280,128]{1,0:T(8,128)(2,1)S(1)}, bf16[1280,128]{1,0:T(8,128)(2,1)S(1)}, u32[]{:S(2)}, u32[]{:S(2)}) collective-permute-start(bf16[1280,128]{1,0:T(8,128)(2,1)S(1)} %collective-permute-done.8.refs_1_), channel_id=1, source_target_pairs={{0,4},{1,5},{2,6},{3,7},{4,8},{5,9},{6,10},{7,11},{8,12},{9,13},{1... | collective-permute-start | bytes 983048 | tf_op jit(solution)/shard_map/ppermute | solution.py:35
  10.9 12.5 %collective-permute-start.11 = (bf16[1280,128]{1,0:T(8,128)(2,1)S(1)}, bf16[1280,128]{1,0:T(8,128)(2,1)S(1)}, u32[]{:S(2)}, u32[]{:S(2)}) collective-permute-start(bf16[1280,128]{1,0:T(8,128)(2,1)S(1)} %collective-permute-done.8.refs_1_), channel_id=1, source_target_pairs={{0,2},{1,3},{2,0},{3,1},{4,6},{5,7},{6,4},{7,5},{8,10},{9,11},{10,... | collective-permute-start | bytes 983048 | tf_op jit(solution)/shard_map/ppermute | solution.py:35
  14.8 14.0 %collective-permute-start.4 = (bf16[1280,128]{1,0:T(8,128)(2,1)S(1)}, bf16[1280,128]{1,0:T(8,128)(2,1)S(1)}, u32[]{:S(2)}, u32[]{:S(2)}) collective-permute-start(bf16[1280,128]{1,0:T(8,128)(2,1)S(1)} %collective-permute-done.2.refs_0_), channel_id=1, source_target_pairs={{0,4},{1,5},{2,6},{3,7},{4,8},{5,9},{6,10},{7,11},{8,12},{9,13},{1... | collective-permute-start | bytes 983048 | tf_op jit(solution)/shard_map/ppermute | solution.py:35
  16.3 12.6 %collective-permute-start.5 = (bf16[1280,128]{1,0:T(8,128)(2,1)S(1)}, bf16[1280,128]{1,0:T(8,128)(2,1)}, u32[]{:S(2)}, u32[]{:S(2)}) collective-permute-start(bf16[1280,128]{1,0:T(8,128)(2,1)S(1)} %collective-permute-done.2.refs_0_), channel_id=1, source_target_pairs={{0,2},{1,3},{2,0},{3,1},{4,6},{5,7},{6,4},{7,5},{8,10},{9,11},{10,... | collective-permute-start | bytes 983048 | tf_op jit(solution)/shard_map/ppermute | solution.py:35
  23.3 0.7 copy-start
  24.1 12.6 %collective-permute-start.12 = (bf16[1280,128]{1,0:T(8,128)(2,1)S(1)}, bf16[1280,128]{1,0:T(8,128)(2,1)}, u32[]{:S(2)}, u32[]{:S(2)}) collective-permute-start(bf16[1280,128]{1,0:T(8,128)(2,1)S(1)} %collective-permute-done.10.refs_1_), channel_id=1, source_target_pairs={{0,4},{1,5},{2,6},{3,7},{4,8},{5,9},{6,10},{7,11},{8,12},{9,13},{1... | collective-permute-start | bytes 983048 | tf_op jit(solution)/shard_map/ppermute | solution.py:35
  25.7 11.0 %collective-permute-start.13 = (bf16[1280,128]{1,0:T(8,128)(2,1)S(1)}, bf16[1280,128]{1,0:T(8,128)(2,1)}, u32[]{:S(2)}, u32[]{:S(2)}) collective-permute-start(bf16[1280,128]{1,0:T(8,128)(2,1)S(1)} %collective-permute-done.10.refs_1_), channel_id=1, source_target_pairs={{0,2},{1,3},{2,0},{3,1},{4,6},{5,7},{6,4},{7,5},{8,10},{9,11},{10,... | collective-permute-start | bytes 983048 | tf_op jit(solution)/shard_map/ppermute | solution.py:35
  27.2 16.3 %copy-start.1 = (bf16[1280,128]{1,0:T(8,128)(2,1)S(1)}, bf16[1280,128]{1,0:T(8,128)(2,1)}, u32[]{:S(2)}) copy-start(bf16[1280,128]{1,0:T(8,128)(2,1)} %copy-done) | copy-start | bytes 983044
  28.9 14.6 %collective-permute-start.6 = (bf16[1280,128]{1,0:T(8,128)(2,1)S(1)}, bf16[1280,128]{1,0:T(8,128)(2,1)S(1)}, u32[]{:S(2)}, u32[]{:S(2)}) collective-permute-start(bf16[1280,128]{1,0:T(8,128)(2,1)S(1)} %collective-permute-done.4.refs_0_), channel_id=1, source_target_pairs={{0,4},{1,5},{2,6},{3,7},{4,8},{5,9},{6,10},{7,11},{8,12},{9,13},{1... | collective-permute-start | bytes 983048 | tf_op jit(solution)/shard_map/ppermute | solution.py:35
  30.5 13.1 %collective-permute-start.7 = (bf16[1280,128]{1,0:T(8,128)(2,1)S(1)}, bf16[1280,128]{1,0:T(8,128)(2,1)S(1)}, u32[]{:S(2)}, u32[]{:S(2)}) collective-permute-start(bf16[1280,128]{1,0:T(8,128)(2,1)S(1)} %collective-permute-done.4.refs_0_), channel_id=1, source_target_pairs={{0,2},{1,3},{2,0},{3,1},{4,6},{5,7},{6,4},{7,5},{8,10},{9,11},{10,... | collective-permute-start | bytes 983048 | tf_op jit(solution)/shard_map/ppermute | solution.py:35
  36.6 13.5 %collective-permute-start.15 = (bf16[1280,128]{1,0:T(8,128)(2,1)}, bf16[1280,128]{1,0:T(8,128)(2,1)S(1)}, u32[]{:S(2)}, u32[]{:S(2)}) collective-permute-start(bf16[1280,128]{1,0:T(8,128)(2,1)} %collective-permute-done.12.refs_1_), channel_id=1, source_target_pairs={{0,4},{1,5},{2,6},{3,7},{4,8},{5,9},{6,10},{7,11},{8,12},{9,13},{1... | collective-permute-start | bytes 983048 | tf_op jit(solution)/shard_map/ppermute | solution.py:35
  37.5 12.7 %collective-permute-start.16 = (bf16[1280,128]{1,0:T(8,128)(2,1)}, bf16[1280,128]{1,0:T(8,128)(2,1)S(1)}, u32[]{:S(2)}, u32[]{:S(2)}) collective-permute-start(bf16[1280,128]{1,0:T(8,128)(2,1)} %collective-permute-done.12.refs_1_), channel_id=1, source_target_pairs={{0,2},{1,3},{2,0},{3,1},{4,6},{5,7},{6,4},{7,5},{8,10},{9,11},{10,... | collective-permute-start | bytes 983048 | tf_op jit(solution)/shard_map/ppermute | solution.py:35
  46.4 12.2 %collective-permute-start.14 = (bf16[1280,128]{1,0:T(8,128)(2,1)S(1)}, bf16[1280,128]{1,0:T(8,128)(2,1)S(1)}, u32[]{:S(2)}, u32[]{:S(2)}) collective-permute-start(bf16[1280,128]{1,0:T(8,128)(2,1)S(1)} %collective-permute-done.7.refs_2_), channel_id=1, source_target_pairs={{0,4},{1,5},{2,6},{3,7},{4,8},{5,9},{6,10},{7,11},{8,12},{9,13},{1... | collective-permute-start | bytes 983048 | tf_op jit(solution)/shard_map/ppermute | solution.py:35
  50.2 8.7 %collective-permute-start.17 = (bf16[1280,128]{1,0:T(8,128)(2,1)S(1)}, bf16[1280,128]{1,0:T(8,128)(2,1)S(1)}, u32[]{:S(2)}, u32[]{:S(2)}) collective-permute-start(bf16[1280,128]{1,0:T(8,128)(2,1)S(1)} %collective-permute-done.15.refs_1_), channel_id=1, source_target_pairs={{0,2},{1,3},{2,0},{3,1},{4,6},{5,7},{6,4},{7,5},{8,10},{9,11},{10,... | collective-permute-start | bytes 983048 | tf_op jit(solution)/shard_map/ppermute | solution.py:35
  61.7 1.9 %collective-permute-start.18 = (bf16[1280,128]{1,0:T(8,128)(2,1)S(1)}, bf16[1280,128]{1,0:T(8,128)(2,1)S(1)}, u32[]{:S(2)}, u32[]{:S(2)}) collective-permute-start(bf16[1280,128]{1,0:T(8,128)(2,1)S(1)} %bitcast.61), channel_id=1, source_target_pairs={{0,1},{1,0},{2,3},{3,2},{4,5},{5,4},{6,7},{7,6},{8,9},{9,8},{10,11... | collective-permute-start | bytes 983048 | tf_op jit(solution)/shard_map/ppermute | solution.py:35
  61.8 2.1 %collective-permute-start.19 = (bf16[1280,128]{1,0:T(8,128)(2,1)S(1)}, bf16[1280,128]{1,0:T(8,128)(2,1)S(1)}, u32[]{:S(2)}, u32[]{:S(2)}) collective-permute-start(bf16[1280,128]{1,0:T(8,128)(2,1)S(1)} %bitcast.60), channel_id=1, source_target_pairs={{0,1},{1,0},{2,3},{3,2},{4,5},{5,4},{6,7},{7,6},{8,9},{9,8},{10,11... | collective-permute-start | bytes 983048 | tf_op jit(solution)/shard_map/ppermute | solution.py:35
  62.3 7.5 %collective-permute-start.22 = (bf16[1280,128]{1,0:T(8,128)(2,1)S(1)}, bf16[1280,128]{1,0:T(8,128)(2,1)S(1)}, u32[]{:S(2)}, u32[]{:S(2)}) collective-permute-start(bf16[1280,128]{1,0:T(8,128)(2,1)S(1)} %bitcast.57), channel_id=1, source_target_pairs={{0,1},{1,0},{2,3},{3,2},{4,5},{5,4},{6,7},{7,6},{8,9},{9,8},{10,11... | collective-permute-start | bytes 983048 | tf_op jit(solution)/shard_map/ppermute | solution.py:35
  65.6 16.8 %collective-permute-start.21 = (bf16[1280,128]{1,0:T(8,128)(2,1)S(1)}, bf16[1280,128]{1,0:T(8,128)(2,1)S(1)}, u32[]{:S(2)}, u32[]{:S(2)}) collective-permute-start(bf16[1280,128]{1,0:T(8,128)(2,1)S(1)} %bitcast.56), channel_id=1, source_target_pairs={{0,1},{1,0},{2,3},{3,2},{4,5},{5,4},{6,7},{7,6},{8,9},{9,8},{10,11... | collective-permute-start | bytes 983048 | tf_op jit(solution)/shard_map/ppermute | solution.py:35
  65.8 4.1 %collective-permute-start.26 = (bf16[1280,128]{1,0:T(8,128)(2,1)S(1)}, bf16[1280,128]{1,0:T(8,128)(2,1)S(1)}, u32[]{:S(2)}, u32[]{:S(2)}) collective-permute-start(bf16[1280,128]{1,0:T(8,128)(2,1)S(1)} %bitcast.59), channel_id=1, source_target_pairs={{0,1},{1,0},{2,3},{3,2},{4,5},{5,4},{6,7},{7,6},{8,9},{9,8},{10,11... | collective-permute-start | bytes 983048 | tf_op jit(solution)/shard_map/ppermute | solution.py:35
  66.2 7.0 %collective-permute-start.27 = (bf16[640,128]{1,0:T(8,128)(2,1)S(1)}, bf16[640,128]{1,0:T(8,128)(2,1)S(1)}, u32[]{:S(2)}, u32[]{:S(2)}) collective-permute-start(bf16[640,128]{1,0:T(8,128)(2,1)S(1)} %get-tuple-element.99), channel_id=1, source_target_pairs={{0,2},{1,3},{2,0},{3,1},{4,6},{5,7},{6,4},{7,5},{8,10},{9,11},{10,... | collective-permute-start | bytes 491528 | tf_op jit(solution)/shard_map/ppermute | solution.py:35
  67.9 8.0 %collective-permute-start.23 = (bf16[640,128]{1,0:T(8,128)(2,1)S(1)}, bf16[640,128]{1,0:T(8,128)(2,1)S(1)}, u32[]{:S(2)}, u32[]{:S(2)}) collective-permute-start(bf16[640,128]{1,0:T(8,128)(2,1)S(1)} %get-tuple-element.94), channel_id=1, source_target_pairs={{0,2},{1,3},{2,0},{3,1},{4,6},{5,7},{6,4},{7,5},{8,10},{9,11},{10,... | collective-permute-start | bytes 491528 | tf_op jit(solution)/shard_map/ppermute | solution.py:35
  69.8 6.3 %collective-permute-start.30 = (bf16[1280,128]{1,0:T(8,128)(2,1)S(1)}, bf16[1280,128]{1,0:T(8,128)(2,1)S(1)}, u32[]{:S(2)}, u32[]{:S(2)}) collective-permute-start(bf16[1280,128]{1,0:T(8,128)(2,1)S(1)} %bitcast.58), channel_id=1, source_target_pairs={{0,1},{1,0},{2,3},{3,2},{4,5},{5,4},{6,7},{7,6},{8,9},{9,8},{10,11... | collective-permute-start | bytes 983048 | tf_op jit(solution)/shard_map/ppermute | solution.py:35
  69.9 12.4 %collective-permute-start.31 = (bf16[1280,128]{1,0:T(8,128)(2,1)S(1)}, bf16[1280,128]{1,0:T(8,128)(2,1)S(1)}, u32[]{:S(2)}, u32[]{:S(2)}) collective-permute-start(bf16[1280,128]{1,0:T(8,128)(2,1)S(1)} %get-tuple-element.103), channel_id=1, source_target_pairs={{0,4},{1,5},{2,6},{3,7},{4,8},{5,9},{6,10},{7,11},{8,12},{9,13},{1... | collective-permute-start | bytes 983048 | tf_op jit(solution)/shard_map/ppermute | solution.py:35
  73.2 23.7 %collective-permute-start.20 = (bf16[1280,128]{1,0:T(8,128)(2,1)S(1)}, bf16[1280,128]{1,0:T(8,128)(2,1)S(1)}, u32[]{:S(2)}, u32[]{:S(2)}) collective-permute-start(bf16[1280,128]{1,0:T(8,128)(2,1)S(1)} %bitcast.54), channel_id=1, source_target_pairs={{0,1},{1,0},{2,3},{3,2},{4,5},{5,4},{6,7},{7,6},{8,9},{9,8},{10,11... | collective-permute-start | bytes 983048 | tf_op jit(solution)/shard_map/ppermute | solution.py:35
  76.0 15.5 %collective-permute-start.34 = (bf16[1280,128]{1,0:T(8,128)(2,1)S(1)}, bf16[1280,128]{1,0:T(8,128)(2,1)S(1)}, u32[]{:S(2)}, u32[]{:S(2)}) collective-permute-start(bf16[1280,128]{1,0:T(8,128)(2,1)S(1)} %bitcast.55), channel_id=1, source_target_pairs={{0,1},{1,0},{2,3},{3,2},{4,5},{5,4},{6,7},{7,6},{8,9},{9,8},{10,11... | collective-permute-start | bytes 983048 | tf_op jit(solution)/shard_map/ppermute | solution.py:35
  76.1 9.3 %collective-permute-start.24 = (bf16[640,128]{1,0:T(8,128)(2,1)S(1)}, bf16[640,128]{1,0:T(8,128)(2,1)S(1)}, u32[]{:S(2)}, u32[]{:S(2)}) collective-permute-start(bf16[640,128]{1,0:T(8,128)(2,1)S(1)} %get-tuple-element.116), channel_id=1, source_target_pairs={{0,4},{1,5},{2,6},{3,7},{4,8},{5,9},{6,10},{7,11},{8,12},{9,13},{1... | collective-permute-start | bytes 491528 | tf_op jit(solution)/shard_map/ppermute | solution.py:35
  82.3 7.2 %collective-permute-start.28 = (bf16[640,128]{1,0:T(8,128)(2,1)S(1)}, bf16[640,128]{1,0:T(8,128)(2,1)S(1)}, u32[]{:S(2)}, u32[]{:S(2)}) collective-permute-start(bf16[640,128]{1,0:T(8,128)(2,1)S(1)} %get-tuple-element.117), channel_id=1, source_target_pairs={{0,4},{1,5},{2,6},{3,7},{4,8},{5,9},{6,10},{7,11},{8,12},{9,13},{1... | collective-permute-start | bytes 491528 | tf_op jit(solution)/shard_map/ppermute | solution.py:35
  82.4 9.0 %collective-permute-start.32 = (bf16[1280,128]{1,0:T(8,128)(2,1)S(1)}, bf16[1280,128]{1,0:T(8,128)(2,1)S(1)}, u32[]{:S(2)}, u32[]{:S(2)}) collective-permute-start(bf16[1280,128]{1,0:T(8,128)(2,1)S(1)} %fusion.6), channel_id=1, source_target_pairs={{0,2},{1,3},{2,0},{3,1},{4,6},{5,7},{6,4},{7,5},{8,10},{9,11},{10,... | collective-permute-start | bytes 983048 | tf_op jit(solution)/shard_map/ppermute | solution.py:35
  85.5 11.5 %collective-permute-start.25 = (bf16[640,128]{1,0:T(8,128)(2,1)S(1)}, bf16[640,128]{1,0:T(8,128)(2,1)S(1)}, u32[]{:S(2)}, u32[]{:S(2)}) collective-permute-start(bf16[640,128]{1,0:T(8,128)(2,1)S(1)} %fusion.12), channel_id=1, source_target_pairs={{0,4},{1,5},{2,6},{3,7},{4,8},{5,9},{6,10},{7,11},{8,12},{9,13},{1... | collective-permute-start | bytes 491528 | tf_op jit(solution)/shard_map/ppermute | solution.py:35
  89.6 9.0 %collective-permute-start.29 = (bf16[640,128]{1,0:T(8,128)(2,1)S(1)}, bf16[640,128]{1,0:T(8,128)(2,1)S(1)}, u32[]{:S(2)}, u32[]{:S(2)}) collective-permute-start(bf16[640,128]{1,0:T(8,128)(2,1)S(1)} %add_convert_fusion), channel_id=1, source_target_pairs={{0,4},{1,5},{2,6},{3,7},{4,8},{5,9},{6,10},{7,11},{8,12},{9,13},{1... | collective-permute-start | bytes 491528 | tf_op jit(solution)/shard_map/ppermute | solution.py:35
  91.6 12.1 %collective-permute-start.35 = (bf16[1280,128]{1,0:T(8,128)(2,1)S(1)}, bf16[1280,128]{1,0:T(8,128)(2,1)S(1)}, u32[]{:S(2)}, u32[]{:S(2)}) collective-permute-start(bf16[1280,128]{1,0:T(8,128)(2,1)S(1)} %fusion.3), channel_id=1, source_target_pairs={{0,12},{1,13},{2,14},{3,15},{4,0},{5,1},{6,2},{7,3},{8,4},{9,5},{1... | collective-permute-start | bytes 983048 | tf_op jit(solution)/shard_map/ppermute | solution.py:35
  95.2 8.5 %collective-permute-start.33 = (bf16[1280,128]{1,0:T(8,128)(2,1)S(1)}, bf16[1280,128]{1,0:T(8,128)(2,1)S(1)}, u32[]{:S(2)}, u32[]{:S(2)}) collective-permute-start(bf16[1280,128]{1,0:T(8,128)(2,1)S(1)} %fusion.5), channel_id=1, source_target_pairs={{0,2},{1,3},{2,0},{3,1},{4,6},{5,7},{6,4},{7,5},{8,10},{9,11},{10,... | collective-permute-start | bytes 983048 | tf_op jit(solution)/shard_map/ppermute | solution.py:35

commit v24 on v23

--- a/solution.py
+++ b/solution.py
@@ -11,7 +11,7 @@
 BLK = 64
 WIN = 128
 LANES = 128
-UNROLL = 16
+UNROLL = 24
 TAIL = 2 * BLK
 LINE = 4
 SCOPED_BYTES = 6 * 1024 * 1024

time: 105 us -> 105 us (level)
  no operation moved by 1% of the time
where the time goes in v24:
time: 105 us
  waiting for transfers between devices  39.8 us (38%)
  starting transfers between devices  31.4 us (30%)
  Pallas kernels  20.1 us (19%)
  local copies, waits for them, and re-layouts  8.14 us (8%)
  other arithmetic  4.22 us (4%)
    ppermute x36, waiting for transfers between devices, move(): return lax.ppermute(array, 'aux', pairs)  39.8 us
    ppermute x36, starting transfers between devices, move(): return lax.ppermute(array, 'aux', pairs)  31.4 us
    pallas_call x8, Pallas kernels, call(): pl.pallas_call(kernel, out_shape=outs, in_specs=in_specs, out_specs=[VMEM...  20.1 us
    unnamed x11, local copies, waits for them, and re-layouts  6.92 us
  transfers between devices with their start and end apart: 36, of which 17 were waited for; matrix products, arithmetic and copies ran while one was open for 10% of the time, Pallas kernels for 17%

profile of v24, /device:TPU:0, one launch (start us, length us, event | category | flops | bytes accessed | tf_op | source)
XLA Modules:
  0.0 104.6 jit_solution(13866812276266184722)
XLA Ops:
  0.0 0.5 collective-permute-start.9
  0.5 1.1 %constant_dynamic-slice_fusion.1 = (bf16[1280,128]{1,0:T(8,128)(2,1)S(1)}, bf16[1280,128]{1,0:T(8,128)(2,1)S(1)}) fusion(bf16[1280,256]{1,0:T(8,128)(2,1)} %param.7, s32[]{:T(128)S(6)} %select_n.162, s32[]{:T(128)S(6)} %select_n.161), kind=kLoop, calls=%fused_computation.91 | loop fusion | bytes 1310728 | tf_op jit(solution)/shard_map/dynamic_slice | solution.py:245
  1.6 2.6 %collective-permute-start.2 = (bf16[1280,128]{1,0:T(8,128)(2,1)S(1)}, bf16[1280,128]{1,0:T(8,128)(2,1)S(1)}, u32[]{:S(2)}, u32[]{:S(2)}) collective-permute-start(bf16[1280,128]{1,0:T(8,128)(2,1)S(1)} %get-tuple-element.119.refs_0_), channel_id=1, source_target_pairs={{0,4},{1,5},{2,6},{3,7},{4,8},{5,9},{6,10},{7,11},{8,12},{9,13},{1... | collective-permute-start | bytes 983048 | tf_op jit(solution)/shard_map/ppermute | solution.py:35
  4.2 1.5 %collective-permute-start.3 = (bf16[1280,128]{1,0:T(8,128)(2,1)S(1)}, bf16[1280,128]{1,0:T(8,128)(2,1)S(1)}, u32[]{:S(2)}, u32[]{:S(2)}) collective-permute-start(bf16[1280,128]{1,0:T(8,128)(2,1)S(1)} %get-tuple-element.119.refs_0_), channel_id=1, source_target_pairs={{0,2},{1,3},{2,0},{3,1},{4,6},{5,7},{6,4},{7,5},{8,10},{9,11},{10,... | collective-permute-start | bytes 983048 | tf_op jit(solution)/shard_map/ppermute | solution.py:35
  5.7 0.5 collective-permute-start
  6.2 0.7 constant_dynamic-update-slice_fusion.1
  7.7 0.7 compare_select_fusion.3
  8.4 0.8 collective-permute-done.8.refs_1_
  9.3 1.6 %collective-permute-start.10 = (bf16[1280,128]{1,0:T(8,128)(2,1)S(1)}, bf16[1280,128]{1,0:T(8,128)(2,1)S(1)}, u32[]{:S(2)}, u32[]{:S(2)}) collective-permute-start(bf16[1280,128]{1,0:T(8,128)(2,1)S(1)} %collective-permute-done.8.refs_1_), channel_id=1, source_target_pairs={{0,4},{1,5},{2,6},{3,7},{4,8},{5,9},{6,10},{7,11},{8,12},{9,13},{1... | collective-permute-start | bytes 983048 | tf_op jit(solution)/shard_map/ppermute | solution.py:35
  10.9 0.5 collective-permute-start.11
  11.4 0.7 fusion.27
  12.1 2.7 %collective-permute-done.2.refs_0_ = bf16[1280,128]{1,0:T(8,128)(2,1)S(1)} collective-permute-done((bf16[1280,128]{1,0:T(8,128)(2,1)S(1)}, bf16[1280,128]{1,0:T(8,128)(2,1)S(1)}, u32[]{:S(2)}, u32[]{:S(2)}) %collective-permute-start.2) | collective-permute-done | bytes 327712 | tf_op jit(solution)/shard_map/ppermute | solution.py:35
  14.8 1.5 %collective-permute-start.4 = (bf16[1280,128]{1,0:T(8,128)(2,1)S(1)}, bf16[1280,128]{1,0:T(8,128)(2,1)S(1)}, u32[]{:S(2)}, u32[]{:S(2)}) collective-permute-start(bf16[1280,128]{1,0:T(8,128)(2,1)S(1)} %collective-permute-done.2.refs_0_), channel_id=1, source_target_pairs={{0,4},{1,5},{2,6},{3,7},{4,8},{5,9},{6,10},{7,11},{8,12},{9,13},{1... | collective-permute-start | bytes 983048 | tf_op jit(solution)/shard_map/ppermute | solution.py:35
  16.3 1.5 %collective-permute-start.5 = (bf16[1280,128]{1,0:T(8,128)(2,1)S(1)}, bf16[1280,128]{1,0:T(8,128)(2,1)}, u32[]{:S(2)}, u32[]{:S(2)}) collective-permute-start(bf16[1280,128]{1,0:T(8,128)(2,1)S(1)} %collective-permute-done.2.refs_0_), channel_id=1, source_target_pairs={{0,2},{1,3},{2,0},{3,1},{4,6},{5,7},{6,4},{7,5},{8,10},{9,11},{10,... | collective-permute-start | bytes 983048 | tf_op jit(solution)/shard_map/ppermute | solution.py:35
  17.8 2.1 %copy.9 = bf16[32,8,32,128]{3,2,1,0:T(8,128)(2,1)S(1)} copy(bf16[32,8,32,128]{3,1,2,0:T(8,128)(2,1)} %bitcast.63) | data formatting | bytes 4194304
  19.9 3.4 %copy.10 = bf16[32,8,32,128]{3,2,1,0:T(8,128)(2,1)} copy(bf16[32,8,32,128]{3,1,2,0:T(8,128)(2,1)} %bitcast.25) | data formatting | bytes 4194304
  23.3 0.7 copy-done
  24.1 1.6 %collective-permute-start.12 = (bf16[1280,128]{1,0:T(8,128)(2,1)S(1)}, bf16[1280,128]{1,0:T(8,128)(2,1)}, u32[]{:S(2)}, u32[]{:S(2)}) collective-permute-start(bf16[1280,128]{1,0:T(8,128)(2,1)S(1)} %collective-permute-done.10.refs_1_), channel_id=1, source_target_pairs={{0,4},{1,5},{2,6},{3,7},{4,8},{5,9},{6,10},{7,11},{8,12},{9,13},{1... | collective-permute-start | bytes 983048 | tf_op jit(solution)/shard_map/ppermute | solution.py:35
  25.7 0.5 collective-permute-start.13
  26.2 0.3 convert_reduce_fusion
  26.5 0.5 select_reduce_fusion
  27.1 0.1 convert_reduce_fusion.1.bounds_ref
  27.3 1.6 %collective-permute-done.4.refs_0_ = bf16[1280,128]{1,0:T(8,128)(2,1)S(1)} collective-permute-done((bf16[1280,128]{1,0:T(8,128)(2,1)S(1)}, bf16[1280,128]{1,0:T(8,128)(2,1)S(1)}, u32[]{:S(2)}, u32[]{:S(2)}) %collective-permute-start.4) | collective-permute-done | bytes 327712 | tf_op jit(solution)/shard_map/ppermute | solution.py:35
  28.9 1.6 %collective-permute-start.6 = (bf16[1280,128]{1,0:T(8,128)(2,1)S(1)}, bf16[1280,128]{1,0:T(8,128)(2,1)S(1)}, u32[]{:S(2)}, u32[]{:S(2)}) collective-permute-start(bf16[1280,128]{1,0:T(8,128)(2,1)S(1)} %collective-permute-done.4.refs_0_), channel_id=1, source_target_pairs={{0,4},{1,5},{2,6},{3,7},{4,8},{5,9},{6,10},{7,11},{8,12},{9,13},{1... | collective-permute-start | bytes 983048 | tf_op jit(solution)/shard_map/ppermute | solution.py:35
  30.5 1.5 %collective-permute-start.7 = (bf16[1280,128]{1,0:T(8,128)(2,1)S(1)}, bf16[1280,128]{1,0:T(8,128)(2,1)S(1)}, u32[]{:S(2)}, u32[]{:S(2)}) collective-permute-start(bf16[1280,128]{1,0:T(8,128)(2,1)S(1)} %collective-permute-done.4.refs_0_), channel_id=1, source_target_pairs={{0,2},{1,3},{2,0},{3,1},{4,6},{5,7},{6,4},{7,5},{8,10},{9,11},{10,... | collective-permute-start | bytes 983048 | tf_op jit(solution)/shard_map/ppermute | solution.py:35
  32.0 3.6 %shard_map.46 = (f32[41088,128]{1,0:T(8,128)S(1)}, bf16[512,32,128]{2,1,0:T(8,128)(2,1)S(1)}) custom-call(s32[1608]{0:T(1024)S(1)} %concatenate.10.table_ref, s32[6]{0:T(128)S(1)} %convert_reduce_fusion.1.bounds_ref, bf16[1280,128]{1,0:T(8,128)(2,1)} %copy-done.2, bf16[1280,128]{1,0:T(8,128)(2,1)} %copy-done.3, bf16[256,32,128]{2,1,0:T(8,128)(2,1)S(1)} %bitcast.53, ...), custom_call_target="tpu_custom_call" | custom-call | flops 107374184 | bytes 4194304 | tf_op jit(solution)/shard_map/pallas_call | solution.py:218
  35.6 1.1 %collective-permute-done.12.refs_1_ = bf16[1280,128]{1,0:T(8,128)(2,1)} collective-permute-done((bf16[1280,128]{1,0:T(8,128)(2,1)S(1)}, bf16[1280,128]{1,0:T(8,128)(2,1)}, u32[]{:S(2)}, u32[]{:S(2)}) %collective-permute-start.12) | collective-permute-done | bytes 327712 | tf_op jit(solution)/shard_map/ppermute | solution.py:35
  36.6 0.9 collective-permute-start.15
  37.5 1.5 %collective-permute-start.16 = (bf16[1280,128]{1,0:T(8,128)(2,1)}, bf16[1280,128]{1,0:T(8,128)(2,1)S(1)}, u32[]{:S(2)}, u32[]{:S(2)}) collective-permute-start(bf16[1280,128]{1,0:T(8,128)(2,1)} %collective-permute-done.12.refs_1_), channel_id=1, source_target_pairs={{0,2},{1,3},{2,0},{3,1},{4,6},{5,7},{6,4},{7,5},{8,10},{9,11},{10,... | collective-permute-start | bytes 983048 | tf_op jit(solution)/shard_map/ppermute | solution.py:35
  39.0 4.5 %collective-permute-done.6.refs_0_ = bf16[1280,128]{1,0:T(8,128)(2,1)S(1)} collective-permute-done((bf16[1280,128]{1,0:T(8,128)(2,1)S(1)}, bf16[1280,128]{1,0:T(8,128)(2,1)S(1)}, u32[]{:S(2)}, u32[]{:S(2)}) %collective-permute-start.6) | collective-permute-done | bytes 327712 | tf_op jit(solution)/shard_map/ppermute | solution.py:35
  43.6 2.9 %shard_map.47.refs_5_ = f32[41088,128]{1,0:T(8,128)S(1)} custom-call(s32[1608]{0:T(1024)S(1)} %concatenate.10.table_ref, s32[6]{0:T(128)S(1)} %convert_reduce_fusion.1.bounds_ref, bf16[1280,128]{1,0:T(8,128)(2,1)S(1)} %collective-permute-done.2.refs_0_, bf16[1280,128]{1,0:T(8,128)(2,1)S(1)} %collective-permute-done.10.refs_1_, ...), custom_call_target="tpu_custom_call", output_to_operand_aliasing={{}: (7, {})} | custom-call | flops 107374184 | bytes 4194304 | tf_op jit(solution)/shard_map/pallas_call | solution.py:218
  46.4 0.6 collective-permute-start.14
  47.0 3.1 %collective-permute-done.15.refs_1_ = bf16[1280,128]{1,0:T(8,128)(2,1)S(1)} collective-permute-done((bf16[1280,128]{1,0:T(8,128)(2,1)}, bf16[1280,128]{1,0:T(8,128)(2,1)S(1)}, u32[]{:S(2)}, u32[]{:S(2)}) %collective-permute-start.15) | collective-permute-done | bytes 327712 | tf_op jit(solution)/shard_map/ppermute | solution.py:35
  50.1 1.3 %collective-permute-start.17 = (bf16[1280,128]{1,0:T(8,128)(2,1)S(1)}, bf16[1280,128]{1,0:T(8,128)(2,1)S(1)}, u32[]{:S(2)}, u32[]{:S(2)}) collective-permute-start(bf16[1280,128]{1,0:T(8,128)(2,1)S(1)} %collective-permute-done.15.refs_1_), channel_id=1, source_target_pairs={{0,2},{1,3},{2,0},{3,1},{4,6},{5,7},{6,4},{7,5},{8,10},{9,11},{10,... | collective-permute-start | bytes 983048 | tf_op jit(solution)/shard_map/ppermute | solution.py:35
  51.4 3.7 %shard_map.48.refs_5_ = f32[41088,128]{1,0:T(8,128)S(1)} custom-call(s32[1608]{0:T(1024)S(1)} %concatenate.10.table_ref, s32[6]{0:T(128)S(1)} %convert_reduce_fusion.1.bounds_ref, bf16[1280,128]{1,0:T(8,128)(2,1)S(1)} %collective-permute-done.4.refs_0_, bf16[1280,128]{1,0:T(8,128)(2,1)} %collective-permute-done.12.refs_1_, ...), custom_call_target="tpu_custom_call", output_to_operand_aliasing={{}: (7, {})} | custom-call | flops 107374184 | bytes 4194304 | tf_op jit(solution)/shard_map/pallas_call | solution.py:218
  55.1 2.9 %shard_map.49.refs_3_ = f32[41088,128]{1,0:T(8,128)S(1)} custom-call(s32[1608]{0:T(1024)S(1)} %concatenate.10.table_ref, s32[6]{0:T(128)S(1)} %convert_reduce_fusion.1.bounds_ref, bf16[1280,128]{1,0:T(8,128)(2,1)S(1)} %collective-permute-done.6.refs_0_, bf16[1280,128]{1,0:T(8,128)(2,1)S(1)} %collective-permute-done.15.refs_1_, ...), custom_call_target="tpu_custom_call", output_to_operand_aliasing={{}: (7, {})} | custom-call | flops 107374184 | bytes 4194304 | tf_op jit(solution)/shard_map/pallas_call | solution.py:218
  58.0 0.9 collective-permute-done.17.refs_1_
  58.9 2.7 %shard_map.50 = (f32[41088,128]{1,0:T(8,128)S(1)}, bf16[256,128]{1,0:T(8,128)(2,1)S(1)}, bf16[1,1280,128]{2,1,0:T(8,128)(2,1)S(1)}, bf16[1,1280,128]{2,1,0:T(8,128)(2,1)S(1)}, bf16[1,1280,128]{2,1,0:T(8,128)(2,1)S(1)}) custom-call(s32[1608]{0:T(1024)S(1)} %concatenate.10.table_ref, ...), custom_call_target="tpu_custom_call", output_to_operand_aliasing={{0}: (7, {})} | custom-call | flops 359032416 | bytes 4194304 | tf_op jit(solution)/shard_map/pallas_call | solution.py:218
  61.7 0.5 collective-permute-start.19
  62.3 1.2 %shard_map.51 = (f32[1,1280,128]{2,1,0:T(8,128)S(1)}, f32[1,1280,128]{2,1,0:T(8,128)S(1)}, f32[1,1280,128]{2,1,0:T(8,128)S(1)}) custom-call(s32[8]{0:T(128)S(1)} %fusion.30.chips_ref, s32[1]{0:T(128)} %bitcast.core_ref, f32[41088,128]{1,0:T(8,128)S(1)} %get-tuple-element.87.half, bf16[256,128]{1,0:T(8,128)(2,1)S(1)} %get-tuple-element.82.weights), custom_call_target="tpu_custom_call" | custom-call | flops 251658240 | bytes 4194304 | tf_op jit(solution)/shard_map/pallas_call | solution.py:218
  63.5 0.3 collective-permute-done.19
  63.8 0.1 fusion.8
  64.0 1.6 %shard_map.53 = (bf16[1,1280,128]{2,1,0:T(8,128)(2,1)S(1)}, bf16[1,1280,128]{2,1,0:T(8,128)(2,1)S(1)}, bf16[1,1280,128]{2,1,0:T(8,128)(2,1)S(1)}, bf16[1,1280,12...) custom-call(s32[8]{0:T(128)S(1)} %fusion.30.chips_ref, s32[1]{0:T(128)} %bitcast.core_ref, ...), custom_call_target="tpu_custom_call" | custom-call | flops 419430400 | bytes 4194304 | tf_op jit(solution)/shard_map/pallas_call | solution.py:218
  65.6 0.2 collective-permute-start.21
  65.8 0.4 collective-permute-start.26
  66.1 1.7 %collective-permute-start.27 = (bf16[640,128]{1,0:T(8,128)(2,1)S(1)}, bf16[640,128]{1,0:T(8,128)(2,1)S(1)}, u32[]{:S(2)}, u32[]{:S(2)}) collective-permute-start(bf16[640,128]{1,0:T(8,128)(2,1)S(1)} %get-tuple-element.99), channel_id=1, source_target_pairs={{0,2},{1,3},{2,0},{3,1},{4,6},{5,7},{6,4},{7,5},{8,10},{9,11},{10,... | collective-permute-start | bytes 491528 | tf_op jit(solution)/shard_map/ppermute | solution.py:35
  67.9 0.3 collective-permute-start.23
  68.2 1.6 %shard_map.52 = (f32[1,1280,128]{2,1,0:T(8,128)S(1)}, f32[1,1280,128]{2,1,0:T(8,128)S(1)}, f32[1,1280,128]{2,1,0:T(8,128)S(1)}, f32[1,1280,128]{2,1,0:T(8,128)S(1)}, f32[1,1280,128]{2,1,0:T(8,128)S(1)}) custom-call(s32[8]{0:T(128)S(1)} %fusion.30.chips_ref, s32[1]{0:T(128)} %bitcast.core_ref, f32[41088,128]{1,0:T(8,128)S(1)} %get-tuple-element.87.half, ...), custom_call_target="tpu_custom_call" | custom-call | flops 419430400 | bytes 4194304 | tf_op jit(solution)/shard_map/pallas_call | solution.py:218
  69.9 0.6 collective-permute-start.31
  70.5 2.7 %collective-permute-done.27 = bf16[640,128]{1,0:T(8,128)(2,1)S(1)} collective-permute-done((bf16[640,128]{1,0:T(8,128)(2,1)S(1)}, bf16[640,128]{1,0:T(8,128)(2,1)S(1)}, u32[]{:S(2)}, u32[]{:S(2)}) %collective-permute-start.27) | collective-permute-done | bytes 163872 | tf_op jit(solution)/shard_map/ppermute | solution.py:35
  73.2 2.7 %collective-permute-done.23 = bf16[640,128]{1,0:T(8,128)(2,1)S(1)} collective-permute-done((bf16[640,128]{1,0:T(8,128)(2,1)S(1)}, bf16[640,128]{1,0:T(8,128)(2,1)S(1)}, u32[]{:S(2)}, u32[]{:S(2)}) %collective-permute-start.23) | collective-permute-done | bytes 163872 | tf_op jit(solution)/shard_map/ppermute | solution.py:35
  76.0 0.6 collective-permute-start.24
  76.6 5.7 %collective-permute-done.31 = bf16[1280,128]{1,0:T(8,128)(2,1)S(1)} collective-permute-done((bf16[1280,128]{1,0:T(8,128)(2,1)S(1)}, bf16[1280,128]{1,0:T(8,128)(2,1)S(1)}, u32[]{:S(2)}, u32[]{:S(2)}) %collective-permute-start.31) | collective-permute-done | bytes 327712 | tf_op jit(solution)/shard_map/ppermute | solution.py:35
  82.2 0.1 fusion.5
  82.4 1.8 %collective-permute-start.32 = (bf16[1280,128]{1,0:T(8,128)(2,1)S(1)}, bf16[1280,128]{1,0:T(8,128)(2,1)S(1)}, u32[]{:S(2)}, u32[]{:S(2)}) collective-permute-start(bf16[1280,128]{1,0:T(8,128)(2,1)S(1)} %fusion.6), channel_id=1, source_target_pairs={{0,2},{1,3},{2,0},{3,1},{4,6},{5,7},{6,4},{7,5},{8,10},{9,11},{10,... | collective-permute-start | bytes 983048 | tf_op jit(solution)/shard_map/ppermute | solution.py:35
  84.2 1.1 %collective-permute-done.24 = bf16[640,128]{1,0:T(8,128)(2,1)S(1)} collective-permute-done((bf16[640,128]{1,0:T(8,128)(2,1)S(1)}, bf16[640,128]{1,0:T(8,128)(2,1)S(1)}, u32[]{:S(2)}, u32[]{:S(2)}) %collective-permute-start.24) | collective-permute-done | bytes 163872 | tf_op jit(solution)/shard_map/ppermute | solution.py:35
  85.5 4.0 %collective-permute-done.28 = bf16[640,128]{1,0:T(8,128)(2,1)S(1)} collective-permute-done((bf16[640,128]{1,0:T(8,128)(2,1)S(1)}, bf16[640,128]{1,0:T(8,128)(2,1)S(1)}, u32[]{:S(2)}, u32[]{:S(2)}) %collective-permute-start.28) | collective-permute-done | bytes 163872 | tf_op jit(solution)/shard_map/ppermute | solution.py:35
  89.6 1.8 %collective-permute-done.32 = bf16[1280,128]{1,0:T(8,128)(2,1)S(1)} collective-permute-done((bf16[1280,128]{1,0:T(8,128)(2,1)S(1)}, bf16[1280,128]{1,0:T(8,128)(2,1)S(1)}, u32[]{:S(2)}, u32[]{:S(2)}) %collective-permute-start.32) | collective-permute-done | bytes 327712 | tf_op jit(solution)/shard_map/ppermute | solution.py:35
  91.4 0.1 fusion.3
  91.5 3.6 %collective-permute-start.35 = (bf16[1280,128]{1,0:T(8,128)(2,1)S(1)}, bf16[1280,128]{1,0:T(8,128)(2,1)S(1)}, u32[]{:S(2)}, u32[]{:S(2)}) collective-permute-start(bf16[1280,128]{1,0:T(8,128)(2,1)S(1)} %fusion.3), channel_id=1, source_target_pairs={{0,12},{1,13},{2,14},{3,15},{4,0},{5,1},{6,2},{7,3},{8,4},{9,5},{1... | collective-permute-start | bytes 983048 | tf_op jit(solution)/shard_map/ppermute | solution.py:35
  95.1 1.7 %collective-permute-start.33 = (bf16[1280,128]{1,0:T(8,128)(2,1)S(1)}, bf16[1280,128]{1,0:T(8,128)(2,1)S(1)}, u32[]{:S(2)}, u32[]{:S(2)}) collective-permute-start(bf16[1280,128]{1,0:T(8,128)(2,1)S(1)} %fusion.5), channel_id=1, source_target_pairs={{0,2},{1,3},{2,0},{3,1},{4,6},{5,7},{6,4},{7,5},{8,10},{9,11},{10,... | collective-permute-start | bytes 983048 | tf_op jit(solution)/shard_map/ppermute | solution.py:35
  96.9 1.6 %collective-permute-done.29 = bf16[640,128]{1,0:T(8,128)(2,1)S(1)} collective-permute-done((bf16[640,128]{1,0:T(8,128)(2,1)S(1)}, bf16[640,128]{1,0:T(8,128)(2,1)S(1)}, u32[]{:S(2)}, u32[]{:S(2)}) %collective-permute-start.29) | collective-permute-done | bytes 163872 | tf_op jit(solution)/shard_map/ppermute | solution.py:35
  98.6 5.1 %collective-permute-done.35 = bf16[1280,128]{1,0:T(8,128)(2,1)S(1)} collective-permute-done((bf16[1280,128]{1,0:T(8,128)(2,1)S(1)}, bf16[1280,128]{1,0:T(8,128)(2,1)S(1)}, u32[]{:S(2)}, u32[]{:S(2)}) %collective-permute-start.35) | collective-permute-done | bytes 327712 | tf_op jit(solution)/shard_map/ppermute | solution.py:35
  103.7 0.9 add_multiply_fusion
  (50 shorter events, 1.2 us)
Async XLA Ops:
  0.0 9.3 %collective-permute-start.9 = (bf16[256,4096]{1,0:T(8,128)(2,1)}, bf16[256,4096]{1,0:T(8,128)(2,1)}, u32[]{:S(2)}, u32[]{:S(2)}) collective-permute-start(bf16[256,4096]{1,0:T(8,128)(2,1)} %param.4), channel_id=1, source_target_pairs={{0,1},{1,0},{2,3},{3,2},{4,5},{5,4},{6,7},{7,6},{8,9},{9,8},{10,11... | collective-permute-start | bytes 6291464 | tf_op jit(solution)/shard_map/ppermute | solution.py:35
  1.6 13.2 %copy-start.2 = (bf16[1280,128]{1,0:T(8,128)(2,1)}, bf16[1280,128]{1,0:T(8,128)(2,1)S(1)}, u32[]{:S(2)}) copy-start(bf16[1280,128]{1,0:T(8,128)(2,1)S(1)} %get-tuple-element.119.refs_0_) | copy-start | bytes 983044
  1.6 13.2 %collective-permute-start.2 = (bf16[1280,128]{1,0:T(8,128)(2,1)S(1)}, bf16[1280,128]{1,0:T(8,128)(2,1)S(1)}, u32[]{:S(2)}, u32[]{:S(2)}) collective-permute-start(bf16[1280,128]{1,0:T(8,128)(2,1)S(1)} %get-tuple-element.119.refs_0_), channel_id=1, source_target_pairs={{0,4},{1,5},{2,6},{3,7},{4,8},{5,9},{6,10},{7,11},{8,12},{9,13},{1... | collective-permute-start | bytes 983048 | tf_op jit(solution)/shard_map/ppermute | solution.py:35
  4.2 10.6 %collective-permute-start.3 = (bf16[1280,128]{1,0:T(8,128)(2,1)S(1)}, bf16[1280,128]{1,0:T(8,128)(2,1)S(1)}, u32[]{:S(2)}, u32[]{:S(2)}) collective-permute-start(bf16[1280,128]{1,0:T(8,128)(2,1)S(1)} %get-tuple-element.119.refs_0_), channel_id=1, source_target_pairs={{0,2},{1,3},{2,0},{3,1},{4,6},{5,7},{6,4},{7,5},{8,10},{9,11},{10,... | collective-permute-start | bytes 983048 | tf_op jit(solution)/shard_map/ppermute | solution.py:35
  5.7 1.9 %collective-permute-start.1 = (s32[256,2]{0,1:T(2,128)}, s32[256,2]{0,1:T(2,128)S(1)}, u32[]{:S(2)}, u32[]{:S(2)}) collective-permute-start(s32[256,2]{0,1:T(2,128)} %param.5), channel_id=1, source_target_pairs={{0,1},{1,0},{2,3},{3,2},{4,5},{5,4},{6,7},{7,6},{8,9},{9,8},{10,11... | collective-permute-start | bytes 6152 | tf_op jit(solution)/shard_map/ppermute | solution.py:35
  5.7 2.0 %collective-permute-start = (s32[1]{0:T(128)}, s32[1]{0:T(128)}, u32[]{:S(2)}, u32[]{:S(2)}) collective-permute-start(s32[1]{0:T(128)} %param.6), channel_id=1, source_target_pairs={{0,1},{1,0},{2,3},{3,2},{4,5},{5,4},{6,7},{7,6},{8,9},{9,8},{10,11... | collective-permute-start | bytes 20 | tf_op jit(solution)/shard_map/ppermute | solution.py:35
  7.6 1.7 %collective-permute-start.8 = (bf16[1280,128]{1,0:T(8,128)(2,1)S(1)}, bf16[1280,128]{1,0:T(8,128)(2,1)S(1)}, u32[]{:S(2)}, u32[]{:S(2)}) collective-permute-start(bf16[1280,128]{1,0:T(8,128)(2,1)S(1)} %get-tuple-element.118), channel_id=1, source_target_pairs={{0,1},{1,0},{2,3},{3,2},{4,5},{5,4},{6,7},{7,6},{8,9},{9,8},{10,11... | collective-permute-start | bytes 983048 | tf_op jit(solution)/shard_map/ppermute | solution.py:35
  9.3 10.6 %copy-start.3 = (bf16[1280,128]{1,0:T(8,128)(2,1)}, bf16[1280,128]{1,0:T(8,128)(2,1)S(1)}, u32[]{:S(2)}) copy-start(bf16[1280,128]{1,0:T(8,128)(2,1)S(1)} %collective-permute-done.8.refs_1_) | copy-start | bytes 983044
  9.3 14.1 %collective-permute-start.10 = (bf16[1280,128]{1,0:T(8,128)(2,1)S(1)}, bf16[1280,128]{1,0:T(8,128)(2,1)S(1)}, u32[]{:S(2)}, u32[]{:S(2)}) collective-permute-start(bf16[1280,128]{1,0:T(8,128)(2,1)S(1)} %collective-permute-done.8.refs_1_), channel_id=1, source_target_pairs={{0,4},{1,5},{2,6},{3,7},{4,8},{5,9},{6,10},{7,11},{8,12},{9,13},{1... | collective-permute-start | bytes 983048 | tf_op jit(solution)/shard_map/ppermute | solution.py:35
  10.9 12.5 %collective-permute-start.11 = (bf16[1280,128]{1,0:T(8,128)(2,1)S(1)}, bf16[1280,128]{1,0:T(8,128)(2,1)S(1)}, u32[]{:S(2)}, u32[]{:S(2)}) collective-permute-start(bf16[1280,128]{1,0:T(8,128)(2,1)S(1)} %collective-permute-done.8.refs_1_), channel_id=1, source_target_pairs={{0,2},{1,3},{2,0},{3,1},{4,6},{5,7},{6,4},{7,5},{8,10},{9,11},{10,... | collective-permute-start | bytes 983048 | tf_op jit(solution)/shard_map/ppermute | solution.py:35
  14.8 14.0 %collective-permute-start.4 = (bf16[1280,128]{1,0:T(8,128)(2,1)S(1)}, bf16[1280,128]{1,0:T(8,128)(2,1)S(1)}, u32[]{:S(2)}, u32[]{:S(2)}) collective-permute-start(bf16[1280,128]{1,0:T(8,128)(2,1)S(1)} %collective-permute-done.2.refs_0_), channel_id=1, source_target_pairs={{0,4},{1,5},{2,6},{3,7},{4,8},{5,9},{6,10},{7,11},{8,12},{9,13},{1... | collective-permute-start | bytes 983048 | tf_op jit(solution)/shard_map/ppermute | solution.py:35
  16.3 12.6 %collective-permute-start.5 = (bf16[1280,128]{1,0:T(8,128)(2,1)S(1)}, bf16[1280,128]{1,0:T(8,128)(2,1)}, u32[]{:S(2)}, u32[]{:S(2)}) collective-permute-start(bf16[1280,128]{1,0:T(8,128)(2,1)S(1)} %collective-permute-done.2.refs_0_), channel_id=1, source_target_pairs={{0,2},{1,3},{2,0},{3,1},{4,6},{5,7},{6,4},{7,5},{8,10},{9,11},{10,... | collective-permute-start | bytes 983048 | tf_op jit(solution)/shard_map/ppermute | solution.py:35
  23.3 0.7 copy-start
  24.1 12.6 %collective-permute-start.12 = (bf16[1280,128]{1,0:T(8,128)(2,1)S(1)}, bf16[1280,128]{1,0:T(8,128)(2,1)}, u32[]{:S(2)}, u32[]{:S(2)}) collective-permute-start(bf16[1280,128]{1,0:T(8,128)(2,1)S(1)} %collective-permute-done.10.refs_1_), channel_id=1, source_target_pairs={{0,4},{1,5},{2,6},{3,7},{4,8},{5,9},{6,10},{7,11},{8,12},{9,13},{1... | collective-permute-start | bytes 983048 | tf_op jit(solution)/shard_map/ppermute | solution.py:35
  25.7 11.0 %collective-permute-start.13 = (bf16[1280,128]{1,0:T(8,128)(2,1)S(1)}, bf16[1280,128]{1,0:T(8,128)(2,1)}, u32[]{:S(2)}, u32[]{:S(2)}) collective-permute-start(bf16[1280,128]{1,0:T(8,128)(2,1)S(1)} %collective-permute-done.10.refs_1_), channel_id=1, source_target_pairs={{0,2},{1,3},{2,0},{3,1},{4,6},{5,7},{6,4},{7,5},{8,10},{9,11},{10,... | collective-permute-start | bytes 983048 | tf_op jit(solution)/shard_map/ppermute | solution.py:35
  27.2 16.3 %copy-start.1 = (bf16[1280,128]{1,0:T(8,128)(2,1)S(1)}, bf16[1280,128]{1,0:T(8,128)(2,1)}, u32[]{:S(2)}) copy-start(bf16[1280,128]{1,0:T(8,128)(2,1)} %copy-done) | copy-start | bytes 983044
  28.9 14.6 %collective-permute-start.6 = (bf16[1280,128]{1,0:T(8,128)(2,1)S(1)}, bf16[1280,128]{1,0:T(8,128)(2,1)S(1)}, u32[]{:S(2)}, u32[]{:S(2)}) collective-permute-start(bf16[1280,128]{1,0:T(8,128)(2,1)S(1)} %collective-permute-done.4.refs_0_), channel_id=1, source_target_pairs={{0,4},{1,5},{2,6},{3,7},{4,8},{5,9},{6,10},{7,11},{8,12},{9,13},{1... | collective-permute-start | bytes 983048 | tf_op jit(solution)/shard_map/ppermute | solution.py:35
  30.5 13.1 %collective-permute-start.7 = (bf16[1280,128]{1,0:T(8,128)(2,1)S(1)}, bf16[1280,128]{1,0:T(8,128)(2,1)S(1)}, u32[]{:S(2)}, u32[]{:S(2)}) collective-permute-start(bf16[1280,128]{1,0:T(8,128)(2,1)S(1)} %collective-permute-done.4.refs_0_), channel_id=1, source_target_pairs={{0,2},{1,3},{2,0},{3,1},{4,6},{5,7},{6,4},{7,5},{8,10},{9,11},{10,... | collective-permute-start | bytes 983048 | tf_op jit(solution)/shard_map/ppermute | solution.py:35
  36.6 13.5 %collective-permute-start.15 = (bf16[1280,128]{1,0:T(8,128)(2,1)}, bf16[1280,128]{1,0:T(8,128)(2,1)S(1)}, u32[]{:S(2)}, u32[]{:S(2)}) collective-permute-start(bf16[1280,128]{1,0:T(8,128)(2,1)} %collective-permute-done.12.refs_1_), channel_id=1, source_target_pairs={{0,4},{1,5},{2,6},{3,7},{4,8},{5,9},{6,10},{7,11},{8,12},{9,13},{1... | collective-permute-start | bytes 983048 | tf_op jit(solution)/shard_map/ppermute | solution.py:35
  37.5 12.6 %collective-permute-start.16 = (bf16[1280,128]{1,0:T(8,128)(2,1)}, bf16[1280,128]{1,0:T(8,128)(2,1)S(1)}, u32[]{:S(2)}, u32[]{:S(2)}) collective-permute-start(bf16[1280,128]{1,0:T(8,128)(2,1)} %collective-permute-done.12.refs_1_), channel_id=1, source_target_pairs={{0,2},{1,3},{2,0},{3,1},{4,6},{5,7},{6,4},{7,5},{8,10},{9,11},{10,... | collective-permute-start | bytes 983048 | tf_op jit(solution)/shard_map/ppermute | solution.py:35
  46.4 11.6 %collective-permute-start.14 = (bf16[1280,128]{1,0:T(8,128)(2,1)S(1)}, bf16[1280,128]{1,0:T(8,128)(2,1)S(1)}, u32[]{:S(2)}, u32[]{:S(2)}) collective-permute-start(bf16[1280,128]{1,0:T(8,128)(2,1)S(1)} %collective-permute-done.7.refs_2_), channel_id=1, source_target_pairs={{0,4},{1,5},{2,6},{3,7},{4,8},{5,9},{6,10},{7,11},{8,12},{9,13},{1... | collective-permute-start | bytes 983048 | tf_op jit(solution)/shard_map/ppermute | solution.py:35
  50.1 8.8 %collective-permute-start.17 = (bf16[1280,128]{1,0:T(8,128)(2,1)S(1)}, bf16[1280,128]{1,0:T(8,128)(2,1)S(1)}, u32[]{:S(2)}, u32[]{:S(2)}) collective-permute-start(bf16[1280,128]{1,0:T(8,128)(2,1)S(1)} %collective-permute-done.15.refs_1_), channel_id=1, source_target_pairs={{0,2},{1,3},{2,0},{3,1},{4,6},{5,7},{6,4},{7,5},{8,10},{9,11},{10,... | collective-permute-start | bytes 983048 | tf_op jit(solution)/shard_map/ppermute | solution.py:35
  61.7 1.9 %collective-permute-start.18 = (bf16[1280,128]{1,0:T(8,128)(2,1)S(1)}, bf16[1280,128]{1,0:T(8,128)(2,1)S(1)}, u32[]{:S(2)}, u32[]{:S(2)}) collective-permute-start(bf16[1280,128]{1,0:T(8,128)(2,1)S(1)} %bitcast.61), channel_id=1, source_target_pairs={{0,1},{1,0},{2,3},{3,2},{4,5},{5,4},{6,7},{7,6},{8,9},{9,8},{10,11... | collective-permute-start | bytes 983048 | tf_op jit(solution)/shard_map/ppermute | solution.py:35
  61.7 2.1 %collective-permute-start.19 = (bf16[1280,128]{1,0:T(8,128)(2,1)S(1)}, bf16[1280,128]{1,0:T(8,128)(2,1)S(1)}, u32[]{:S(2)}, u32[]{:S(2)}) collective-permute-start(bf16[1280,128]{1,0:T(8,128)(2,1)S(1)} %bitcast.60), channel_id=1, source_target_pairs={{0,1},{1,0},{2,3},{3,2},{4,5},{5,4},{6,7},{7,6},{8,9},{9,8},{10,11... | collective-permute-start | bytes 983048 | tf_op jit(solution)/shard_map/ppermute | solution.py:35
  62.2 7.5 %collective-permute-start.22 = (bf16[1280,128]{1,0:T(8,128)(2,1)S(1)}, bf16[1280,128]{1,0:T(8,128)(2,1)S(1)}, u32[]{:S(2)}, u32[]{:S(2)}) collective-permute-start(bf16[1280,128]{1,0:T(8,128)(2,1)S(1)} %bitcast.57), channel_id=1, source_target_pairs={{0,1},{1,0},{2,3},{3,2},{4,5},{5,4},{6,7},{7,6},{8,9},{9,8},{10,11... | collective-permute-start | bytes 983048 | tf_op jit(solution)/shard_map/ppermute | solution.py:35
  65.6 16.8 %collective-permute-start.21 = (bf16[1280,128]{1,0:T(8,128)(2,1)S(1)}, bf16[1280,128]{1,0:T(8,128)(2,1)S(1)}, u32[]{:S(2)}, u32[]{:S(2)}) collective-permute-start(bf16[1280,128]{1,0:T(8,128)(2,1)S(1)} %bitcast.56), channel_id=1, source_target_pairs={{0,1},{1,0},{2,3},{3,2},{4,5},{5,4},{6,7},{7,6},{8,9},{9,8},{10,11... | collective-permute-start | bytes 983048 | tf_op jit(solution)/shard_map/ppermute | solution.py:35
  65.8 4.1 %collective-permute-start.26 = (bf16[1280,128]{1,0:T(8,128)(2,1)S(1)}, bf16[1280,128]{1,0:T(8,128)(2,1)S(1)}, u32[]{:S(2)}, u32[]{:S(2)}) collective-permute-start(bf16[1280,128]{1,0:T(8,128)(2,1)S(1)} %bitcast.59), channel_id=1, source_target_pairs={{0,1},{1,0},{2,3},{3,2},{4,5},{5,4},{6,7},{7,6},{8,9},{9,8},{10,11... | collective-permute-start | bytes 983048 | tf_op jit(solution)/shard_map/ppermute | solution.py:35
  66.1 7.0 %collective-permute-start.27 = (bf16[640,128]{1,0:T(8,128)(2,1)S(1)}, bf16[640,128]{1,0:T(8,128)(2,1)S(1)}, u32[]{:S(2)}, u32[]{:S(2)}) collective-permute-start(bf16[640,128]{1,0:T(8,128)(2,1)S(1)} %get-tuple-element.99), channel_id=1, source_target_pairs={{0,2},{1,3},{2,0},{3,1},{4,6},{5,7},{6,4},{7,5},{8,10},{9,11},{10,... | collective-permute-start | bytes 491528 | tf_op jit(solution)/shard_map/ppermute | solution.py:35
  67.9 8.0 %collective-permute-start.23 = (bf16[640,128]{1,0:T(8,128)(2,1)S(1)}, bf16[640,128]{1,0:T(8,128)(2,1)S(1)}, u32[]{:S(2)}, u32[]{:S(2)}) collective-permute-start(bf16[640,128]{1,0:T(8,128)(2,1)S(1)} %get-tuple-element.94), channel_id=1, source_target_pairs={{0,2},{1,3},{2,0},{3,1},{4,6},{5,7},{6,4},{7,5},{8,10},{9,11},{10,... | collective-permute-start | bytes 491528 | tf_op jit(solution)/shard_map/ppermute | solution.py:35
  69.7 6.3 %collective-permute-start.30 = (bf16[1280,128]{1,0:T(8,128)(2,1)S(1)}, bf16[1280,128]{1,0:T(8,128)(2,1)S(1)}, u32[]{:S(2)}, u32[]{:S(2)}) collective-permute-start(bf16[1280,128]{1,0:T(8,128)(2,1)S(1)} %bitcast.58), channel_id=1, source_target_pairs={{0,1},{1,0},{2,3},{3,2},{4,5},{5,4},{6,7},{7,6},{8,9},{9,8},{10,11... | collective-permute-start | bytes 983048 | tf_op jit(solution)/shard_map/ppermute | solution.py:35
  69.9 12.4 %collective-permute-start.31 = (bf16[1280,128]{1,0:T(8,128)(2,1)S(1)}, bf16[1280,128]{1,0:T(8,128)(2,1)S(1)}, u32[]{:S(2)}, u32[]{:S(2)}) collective-permute-start(bf16[1280,128]{1,0:T(8,128)(2,1)S(1)} %get-tuple-element.103), channel_id=1, source_target_pairs={{0,4},{1,5},{2,6},{3,7},{4,8},{5,9},{6,10},{7,11},{8,12},{9,13},{1... | collective-permute-start | bytes 983048 | tf_op jit(solution)/shard_map/ppermute | solution.py:35
  73.2 23.7 %collective-permute-start.20 = (bf16[1280,128]{1,0:T(8,128)(2,1)S(1)}, bf16[1280,128]{1,0:T(8,128)(2,1)S(1)}, u32[]{:S(2)}, u32[]{:S(2)}) collective-permute-start(bf16[1280,128]{1,0:T(8,128)(2,1)S(1)} %bitcast.54), channel_id=1, source_target_pairs={{0,1},{1,0},{2,3},{3,2},{4,5},{5,4},{6,7},{7,6},{8,9},{9,8},{10,11... | collective-permute-start | bytes 983048 | tf_op jit(solution)/shard_map/ppermute | solution.py:35
  75.9 15.5 %collective-permute-start.34 = (bf16[1280,128]{1,0:T(8,128)(2,1)S(1)}, bf16[1280,128]{1,0:T(8,128)(2,1)S(1)}, u32[]{:S(2)}, u32[]{:S(2)}) collective-permute-start(bf16[1280,128]{1,0:T(8,128)(2,1)S(1)} %bitcast.55), channel_id=1, source_target_pairs={{0,1},{1,0},{2,3},{3,2},{4,5},{5,4},{6,7},{7,6},{8,9},{9,8},{10,11... | collective-permute-start | bytes 983048 | tf_op jit(solution)/shard_map/ppermute | solution.py:35
  76.0 9.3 %collective-permute-start.24 = (bf16[640,128]{1,0:T(8,128)(2,1)S(1)}, bf16[640,128]{1,0:T(8,128)(2,1)S(1)}, u32[]{:S(2)}, u32[]{:S(2)}) collective-permute-start(bf16[640,128]{1,0:T(8,128)(2,1)S(1)} %get-tuple-element.116), channel_id=1, source_target_pairs={{0,4},{1,5},{2,6},{3,7},{4,8},{5,9},{6,10},{7,11},{8,12},{9,13},{1... | collective-permute-start | bytes 491528 | tf_op jit(solution)/shard_map/ppermute | solution.py:35
  82.2 7.2 %collective-permute-start.28 = (bf16[640,128]{1,0:T(8,128)(2,1)S(1)}, bf16[640,128]{1,0:T(8,128)(2,1)S(1)}, u32[]{:S(2)}, u32[]{:S(2)}) collective-permute-start(bf16[640,128]{1,0:T(8,128)(2,1)S(1)} %get-tuple-element.117), channel_id=1, source_target_pairs={{0,4},{1,5},{2,6},{3,7},{4,8},{5,9},{6,10},{7,11},{8,12},{9,13},{1... | collective-permute-start | bytes 491528 | tf_op jit(solution)/shard_map/ppermute | solution.py:35
  82.4 9.0 %collective-permute-start.32 = (bf16[1280,128]{1,0:T(8,128)(2,1)S(1)}, bf16[1280,128]{1,0:T(8,128)(2,1)S(1)}, u32[]{:S(2)}, u32[]{:S(2)}) collective-permute-start(bf16[1280,128]{1,0:T(8,128)(2,1)S(1)} %fusion.6), channel_id=1, source_target_pairs={{0,2},{1,3},{2,0},{3,1},{4,6},{5,7},{6,4},{7,5},{8,10},{9,11},{10,... | collective-permute-start | bytes 983048 | tf_op jit(solution)/shard_map/ppermute | solution.py:35
  85.4 11.5 %collective-permute-start.25 = (bf16[640,128]{1,0:T(8,128)(2,1)S(1)}, bf16[640,128]{1,0:T(8,128)(2,1)S(1)}, u32[]{:S(2)}, u32[]{:S(2)}) collective-permute-start(bf16[640,128]{1,0:T(8,128)(2,1)S(1)} %fusion.12), channel_id=1, source_target_pairs={{0,4},{1,5},{2,6},{3,7},{4,8},{5,9},{6,10},{7,11},{8,12},{9,13},{1... | collective-permute-start | bytes 491528 | tf_op jit(solution)/shard_map/ppermute | solution.py:35
  89.5 9.0 %collective-permute-start.29 = (bf16[640,128]{1,0:T(8,128)(2,1)S(1)}, bf16[640,128]{1,0:T(8,128)(2,1)S(1)}, u32[]{:S(2)}, u32[]{:S(2)}) collective-permute-start(bf16[640,128]{1,0:T(8,128)(2,1)S(1)} %add_convert_fusion), channel_id=1, source_target_pairs={{0,4},{1,5},{2,6},{3,7},{4,8},{5,9},{6,10},{7,11},{8,12},{9,13},{1... | collective-permute-start | bytes 491528 | tf_op jit(solution)/shard_map/ppermute | solution.py:35
  91.5 12.2 %collective-permute-start.35 = (bf16[1280,128]{1,0:T(8,128)(2,1)S(1)}, bf16[1280,128]{1,0:T(8,128)(2,1)S(1)}, u32[]{:S(2)}, u32[]{:S(2)}) collective-permute-start(bf16[1280,128]{1,0:T(8,128)(2,1)S(1)} %fusion.3), channel_id=1, source_target_pairs={{0,12},{1,13},{2,14},{3,15},{4,0},{5,1},{6,2},{7,3},{8,4},{9,5},{1... | collective-permute-start | bytes 983048 | tf_op jit(solution)/shard_map/ppermute | solution.py:35
  95.1 8.6 %collective-permute-start.33 = (bf16[1280,128]{1,0:T(8,128)(2,1)S(1)}, bf16[1280,128]{1,0:T(8,128)(2,1)S(1)}, u32[]{:S(2)}, u32[]{:S(2)}) collective-permute-start(bf16[1280,128]{1,0:T(8,128)(2,1)S(1)} %fusion.5), channel_id=1, source_target_pairs={{0,2},{1,3},{2,0},{3,1},{4,6},{5,7},{6,4},{7,5},{8,10},{9,11},{10,... | collective-permute-start | bytes 983048 | tf_op jit(solution)/shard_map/ppermute | solution.py:35
